TPU v7x, 32 devices: a whole 2x2x4 slice. The times are simulated.
32 devices in a mesh: groups: 2 (over y), dp: 8 (over z, x), tensor: 2 (over core).
Axes of the slice: x: 2, y: 2, z: 4, core: 2. Of those that a mesh axis runs over, the one named last changes fastest.
Arguments:
- inputs: bfloat16 [2048, 4096], P(('groups', 'dp', 'tensor')), parts along dimension 0, may hold values from -6 to 6
- output_gradient: bfloat16 [2048, 512], P(('groups', 'dp')), parts along dimension 0, may hold values from -6 to 6
- frozen_weight: bfloat16 [4096, 512], P('tensor'), may hold values from -0.25 to 0.25
- down_maps: bfloat16 [8192, 128], P(('groups', 'dp')), parts along dimension 0, may hold values from -0.09375 to 0.09375
- up_maps: bfloat16 [256, 512], P(('groups', 'dp')), parts along dimension 0, may hold values from -0.25 to 0.25
- segment_start: int32 [16, 2], P('groups'), parts along dimension 0, may hold values from 0 to 96, as said below
- segment_adapter: int32 [16, 2], P('groups'), parts along dimension 0, may hold values from 0 to 7
- adapter_slot: int32 [16], P('groups'), parts along dimension 0, may hold values from 0 to 7, each once
- token_count: int32 [16], P('groups'), parts along dimension 0, may hold values from 64 to 128, as said below
Outputs:
- grad_x: bfloat16 [2048, 4096], P(('groups', 'dp'), 'tensor'), parts along dimension 0
- grad_a: float32 [8192, 128], P(('groups', 'dp')), parts along dimension 0
- up_map_gradient: float32 [256, 512], P(('groups', 'dp'), 'tensor'), parts along dimension 0
There are 2 independent parts, one for each index of `groups`. A program takes and returns all parts, laid end to end along the dimension named above; an argument that names none is the same for every part. Nothing has to cross between parts.
Inputs may be any that keep to these rules, and one draw needn't show every extreme that they name: `segment_start`: column 0 is 0; the second start lies between 32 and 96, the latter on some rank. `token_count`: rows at or past a rank's count are padding; some rank is full.
All inputs are finite; a program needn't handle non-finite values.
Results may differ from a plain program's by a relative error of at most 0.0034.
Values may be sent and summed in bfloat16 or wider, within the bound.
No kernel may reach another device: no remote copies, remote signals or barrier semaphores. Data moves between devices by JAX's collectives and lax.ppermute only.
A program may use at most 64 MiB of HBM per device.

v0:
```python
import jax
import jax.numpy as jnp
from jax import lax
from jax.sharding import PartitionSpec as P

ADAPTER_RANK = 16


adapter_scale = 2.0


def segment_of(starts, tok_rows):
    position = jnp.arange(tok_rows, dtype=jnp.int32)
    return jnp.sum((starts[None, :] <= position[:, None]).astype(jnp.int32), axis=1) - 1


def slot_lookup(chosen, table):
    adapter_ids = jnp.arange(table.shape[0], dtype=jnp.int32)
    matched = chosen[..., None] == adapter_ids
    return jnp.sum(jnp.where(matched, table, 0), axis=-1)


def spread_blocks(values, segment, segs):
    matched = segment[..., None] == jnp.arange(segs, dtype=jnp.int32)
    placed = jnp.where(matched[..., None], values[..., None, :], jnp.zeros((), values.dtype))
    return placed.reshape(segment.shape + (segs * values.shape[-1],))


def pick_block(full, segment, segs):
    matched = segment[..., None] == jnp.arange(segs, dtype=jnp.int32)
    shaped = full.reshape(segment.shape + (segs, full.shape[-1] // segs))
    return jnp.sum(jnp.where(matched[..., None], shaped, 0.0), axis=-2)


def place_slots(received, slot_table, adapter_list):
    ranks, column_total, width = received.shape
    segs = slot_table.shape[1]
    onehot = (
        slot_table[:, :, None] == jnp.arange(adapter_list, dtype=jnp.int32)[None, None, :]
    ).astype(jnp.float32)
    parts = received.reshape(ranks, column_total, segs, width // segs)
    placed = jnp.einsum("pckr,pks->csr", parts, onehot, precision=lax.Precision.HIGHEST)
    return placed.reshape(column_total, adapter_list * (width // segs))


def local(
    inputs,
    output_gradient,
    frozen_weight,
    down_maps,
    up_maps,
    segment_start,
    segment_adapter,
    adapter_slot,
    token_count,
):
    tok_half = inputs.shape[0]
    tok_rows = output_gradient.shape[0]
    out_width = output_gradient.shape[1]
    column_total = down_maps.shape[0]
    adapter_list = adapter_slot.shape[0]
    segs = segment_start.shape[1]
    dp_size = lax.axis_size("dp")
    tp_size = lax.axis_size("tensor")
    my_rank = lax.axis_index("dp")
    core_idx = lax.axis_index("tensor")
    every_seg = jax.vmap(lambda row_starts: segment_of(row_starts, tok_rows))(segment_start)
    slot_table = slot_lookup(segment_adapter, adapter_slot)
    my_seg = lax.dynamic_index_in_dim(every_seg, my_rank, 0, keepdims=False)
    my_slots = lax.dynamic_index_in_dim(slot_table, my_rank, 0, keepdims=False)
    live_count = lax.dynamic_index_in_dim(token_count, my_rank, 0, keepdims=False)
    seg_ids = jnp.arange(segs, dtype=jnp.int32)
    row_slot_index = jnp.sum(
        jnp.where(my_seg[:, None] == seg_ids[None, :], my_slots[None, :], 0), axis=1
    )
    live_mask = jnp.arange(tok_rows, dtype=jnp.int32) < live_count
    grads_out = jnp.where(live_mask[:, None], output_gradient, jnp.zeros_like(output_gradient))
    first_row = core_idx * tok_half
    down_stack = down_maps.reshape(column_total, adapter_list, ADAPTER_RANK)
    a_sel = jnp.take(down_stack, slot_table.reshape(-1), axis=1).reshape(
        column_total, dp_size, segs * ADAPTER_RANK
    )
    row_portion = lax.all_gather(up_maps, "dp", axis=0, tiled=True)
    product = lax.dot_general(
        grads_out, row_portion, (((1,), (1,)), ((), ())), preferred_element_type=jnp.float32
    )
    col_index = jnp.arange(row_portion.shape[0], dtype=jnp.int32)
    keep_mask = (col_index // ADAPTER_RANK)[None, :] == row_slot_index[:, None]
    product = jnp.where(keep_mask, product, 0.0)
    spread = (
        (col_index % ADAPTER_RANK)[:, None] == jnp.arange(ADAPTER_RANK, dtype=jnp.int32)[None, :]
    ).astype(jnp.float32)
    folded_rows = jnp.dot(product, spread, precision=lax.Precision.HIGHEST)
    low_gradient = (adapter_scale * folded_rows).astype(jnp.bfloat16)
    x_cols = lax.all_to_all(inputs, "dp", split_axis=1, concat_axis=0, tiled=True)
    x_ranks = x_cols.reshape(dp_size, tok_half, column_total)
    seg_cols = lax.dynamic_slice_in_dim(every_seg, first_row, tok_half, 1)
    low_full = jnp.einsum("ptc,cpq->ptq", x_ranks, a_sel, preferred_element_type=jnp.float32)
    low_part = pick_block(low_full, seg_cols, segs).reshape(dp_size * tok_half, ADAPTER_RANK)
    low_half = lax.psum_scatter(low_part, "dp", scatter_dimension=0, tiled=True).astype(
        jnp.bfloat16
    )
    low_rows = lax.all_gather(low_half, "tensor", axis=0, tiled=True)
    dlow_small = lax.dynamic_slice_in_dim(low_gradient, first_row, tok_half, 0)
    dlow_cols = lax.all_gather(dlow_small, "dp", axis=0, tiled=True).reshape(
        dp_size, tok_half, ADAPTER_RANK
    )
    dlow_seg_cols = spread_blocks(dlow_cols, seg_cols, segs)
    dx_cols = jnp.einsum("ptq,cpq->ptc", dlow_seg_cols, a_sel, preferred_element_type=jnp.float32)
    contrib = jnp.einsum("ptc,ptq->pcq", x_ranks, dlow_seg_cols, preferred_element_type=jnp.float32)
    grad_part = place_slots(contrib, slot_table, adapter_list)
    grad_a = lax.psum(grad_part, "tensor")
    dx_rows = lax.all_to_all(
        dx_cols.reshape(dp_size * tok_half, column_total),
        "dp",
        split_axis=0,
        concat_axis=1,
        tiled=True,
    )
    dx_adapter = lax.all_to_all(dx_rows, "tensor", split_axis=1, concat_axis=0, tiled=True)
    base_grad = lax.dot_general(
        grads_out, frozen_weight, (((1,), (1,)), ((), ())), preferred_element_type=jnp.float32
    )
    grad_x = (base_grad + dx_adapter).astype(jnp.bfloat16)
    onehot_local = (
        row_slot_index[:, None] == jnp.arange(adapter_list, dtype=jnp.int32)[None, :]
    ).astype(jnp.bfloat16)
    low_wide = (onehot_local[:, :, None] * low_rows[:, None, :]).reshape(
        tok_rows, adapter_list * ADAPTER_RANK
    )
    piece_out = out_width // tp_size
    grads_piece = lax.dynamic_slice_in_dim(grads_out, core_idx * piece_out, piece_out, 1)
    up_map_gradient = lax.psum_scatter(
        adapter_scale
        * lax.dot_general(
            low_wide, grads_piece, (((0,), (0,)), ((), ())), preferred_element_type=jnp.float32
        ),
        "dp",
        scatter_dimension=0,
        tiled=True,
    )
    return (grad_x, grad_a, up_map_gradient)


def solution(mesh):
    in_specs = (
        P(("groups", "dp", "tensor"), None),
        P(("groups", "dp"), None),
        P("tensor", None),
        P(("groups", "dp"), None),
        P(("groups", "dp"), None),
        P("groups", None),
        P("groups", None),
        P("groups"),
        P("groups"),
    )
    out_specs = (
        P(("groups", "dp"), "tensor"),
        P(("groups", "dp"), None),
        P(("groups", "dp"), "tensor"),
    )
    return jax.shard_map(local, mesh=mesh, in_specs=in_specs, out_specs=out_specs, check_vma=False)
```

profile of v0, /device:TPU:0, one launch (start us, length us, event | category | flops | bytes accessed | tf_op | source)
XLA Modules:
  0.0 231.7 jit_solution(13630514103030339747)
XLA Ops:
  8.0 0.0 copy-start
  8.0 0.0 copy-start.6
  8.0 0.0 copy-start.5
  8.0 0.0 copy-start.7
  8.0 0.0 copy-start.4
  8.1 0.0 copy-start.1
  8.1 0.0 copy-start.3
  8.1 0.0 copy-start.2
  8.1 2.0 copy.102
  10.1 7.3 %all-to-all-start.2 = ((bf16[64,8,512]{2,0,1:T(8,128)(2,1)}), bf16[64,8,512]{2,0,1:T(8,128)(2,1)S(1)}, u32[]{:S(2)}, u32[]{:S(2)}) async-start(bf16[64,8,512]{2,0,1:T(8,128)(2,1)} %bitcast.55), calls=%async_computation.2 | async-start | bytes 1048576 | tf_op jit(solution)/shard_map/all_to_all | solution.py:95
  17.4 0.0 copy-done.6
  17.4 0.0 copy-done.5
  17.4 0.2 select_reduce_fusion.1
  17.6 0.1 copy.84
  17.7 0.2 fusion.19
  17.9 0.0 copy-done.7
  17.9 0.6 dynamic_slice.21
  18.5 0.6 iota_compare_fusion.7
  19.1 0.1 copy.82
  19.2 0.1 broadcast_in_dim.119
  19.3 0.1 broadcast_in_dim.120
  19.4 0.1 reshape.145
  19.5 0.0 copy-done.4
  19.5 0.1 convert_reduce_fusion
  19.6 0.1 copy.83
  19.7 35.0 %all_gather.9 = bf16[128,512]{1,0:T(8,128)(2,1)S(1)} all-gather(bf16[16,512]{1,0:T(8,128)(2,1)S(1)} %copy-done.3), channel_id=1, replica_groups=mesh['groups'=2,'dp'=8,'tensor'=2] {'dp'}, dimensions={0}, use_global_device_ids=true | all-gather | bytes 147456 | tf_op jit(solution)/shard_map/all_gather | solution.py:83
  54.8 0.1 fusion.20
  54.8 0.0 copy-done.2
  54.8 0.1 broadcast_select_fusion.3
  54.9 0.6 gather_fusion
  55.5 0.2 convolution_select_fusion
  55.7 0.3 fusion.10
  56.0 0.1 fusion.15
  56.0 30.6 %all-gather = bf16[8,64,16]{1,2,0:T(8,128)(2,1)S(1)} all-gather(bf16[1,64,16]{1,2,0:T(8,128)(2,1)S(1)} %fusion.15), channel_id=1, replica_groups=mesh['groups'=2,'dp'=8,'tensor'=2] {'dp'}, dimensions={0}, use_global_device_ids=true | all-gather | bytes 18432 | tf_op jit(solution)/shard_map/all_gather | solution.py:105
  86.7 0.1 constant_dynamic-slice_fusion.2
  86.8 1.4 fusion.6
  88.2 0.0 all-to-all-done.2
  88.2 4.2 %all-to-all-start = ((f32[8,64,512]{2,1,0:T(8,128)}), f32[8,64,512]{2,1,0:T(8,128)}, u32[]{:S(2)}, u32[]{:S(2)}) async-start(f32[8,64,512]{2,1,0:T(8,128)} %fusion.6), calls=%async_computation | async-start | bytes 2097152 | tf_op jit(solution)/shard_map/all_to_all | solution.py:113
  92.5 0.0 reduce-scatter.7.cloned.1.call-start
  92.5 0.3 fusion.1
  92.9 0.8 copy.96
  93.7 0.0 reduce-scatter.7.cloned.1.call-update
  93.7 0.0 all-reduce.2.cloned.1.call-start
  93.8 0.2 fusion.3
  94.0 0.6 convolution_bitcast_fusion
  94.6 0.9 copy.89
  95.5 0.0 all-reduce.2.cloned.1.call-update
  95.5 0.0 reduce-scatter.5.cloned.1.call-start
  95.5 64.6 %reduce-scatter.7.cloned.1.call-done = f32[64,16]{1,0:T(8,128)} async-done(((f32[512,16]{1,0:T(8,128)}), f32[64,16]{1,0:T(8,128)}) %reduce-scatter.7.cloned.1.call-update) | async-done | bytes 4112
  160.1 0.8 copy.95
  160.9 1.8 all-gather.1
  162.7 0.1 reshape.161
  162.8 0.8 convolution_multiply_fusion
  163.6 0.0 reduce-scatter.5.cloned.1.call-update
  163.7 0.0 all-reduce.2.cloned.1.call-done
  163.7 1.8 copy.92
  165.5 0.0 all-to-all-done
  165.5 2.9 %copy.85 = f32[64,8,512]{2,1,0:T(8,128)} copy(f32[64,8,512]{2,0,1:T(8,128)} %bitcast.8) | data formatting | bytes 2097152 | tf_op jit(solution)/shard_map/all_to_all | solution.py:113
  168.4 3.0 %all_to_all.38 = f32[64,2,2048]{2,1,0:T(2,128)} reshape(f32[64,8,512]{2,1,0:T(8,128)} %copy.85) | data formatting | bytes 2097152 | tf_op jit(solution)/shard_map/all_to_all | solution.py:120
  171.4 1.8 copy.86
  173.2 4.6 %all_to_all.48 = f32[64,2,2048]{2,0,1:T(8,128)S(1)} all-to-all(f32[64,2,2048]{2,0,1:T(8,128)S(1)} %copy.86), channel_id=1, replica_groups=mesh['groups'=2,'dp'=8,'tensor'=2] {'tensor'}, dimensions={1} | all-to-all | bytes 2097152 | tf_op jit(solution)/shard_map/all_to_all | solution.py:120
  177.8 0.0 copy-done
  177.8 1.6 fusion
  179.4 44.9 %reduce-scatter.5.cloned.1.call-done = f32[16,256]{1,0:T(8,128)} async-done(((f32[128,256]{1,0:T(8,128)}), f32[16,256]{1,0:T(8,128)}) %reduce-scatter.5.cloned.1.call-update) | async-done | bytes 16400 | tf_op jit(solution)/shard_map/reduce_scatter | solution.py:133
  (14 shorter events, 0.1 us)
Async XLA Ops:
  8.0 169.8 %copy-start = (bf16[2048,512]{1,0:T(8,128)(2,1)S(1)}, bf16[2048,512]{1,0:T(8,128)(2,1)}, u32[]{:S(2)}) copy-start(bf16[2048,512]{1,0:T(8,128)(2,1)} %param.11) | copy-start | bytes 6291460
  8.0 9.4 %copy-start.6 = (s32[8]{0:T(128)S(1)}, s32[8]{0:T(128)}, u32[]{:S(2)}) copy-start(s32[8]{0:T(128)} %param.16) | copy-start | bytes 100
  8.0 9.4 %copy-start.5 = (s32[8,2]{0,1:T(2,128)S(1)}, s32[8,2]{0,1:T(2,128)}, u32[]{:S(2)}) copy-start(s32[8,2]{0,1:T(2,128)} %param.15) | copy-start | bytes 196
  8.0 9.9 %copy-start.7 = (s32[8]{0:T(128)S(1)}, s32[8]{0:T(128)}, u32[]{:S(2)}) copy-start(s32[8]{0:T(128)} %param.17) | copy-start | bytes 100
  8.0 11.5 %copy-start.4 = (s32[8,2]{0,1:T(2,128)S(1)}, s32[8,2]{0,1:T(2,128)}, u32[]{:S(2)}) copy-start(s32[8,2]{0,1:T(2,128)} %param.14) | copy-start | bytes 196
  8.1 11.5 %copy-start.1 = (bf16[512,128]{1,0:T(8,128)(2,1)S(1)}, bf16[512,128]{1,0:T(8,128)(2,1)}, u32[]{:S(2)}) copy-start(bf16[512,128]{1,0:T(8,128)(2,1)} %param.12) | copy-start | bytes 393220
  8.1 11.7 %copy-start.3 = (bf16[16,512]{1,0:T(8,128)(2,1)S(1)}, bf16[16,512]{1,0:T(8,128)(2,1)}, u32[]{:S(2)}) copy-start(bf16[16,512]{1,0:T(8,128)(2,1)} %param.13) | copy-start | bytes 49156
  8.1 46.8 %copy-start.2 = (bf16[128,512]{1,0:T(8,128)(2,1)S(1)}, bf16[128,512]{1,0:T(8,128)(2,1)}, u32[]{:S(2)}) copy-start(bf16[128,512]{1,0:T(8,128)(2,1)} %param.10) | copy-start | bytes 393220
  10.1 78.1 %all-to-all-start.2 = ((bf16[64,8,512]{2,0,1:T(8,128)(2,1)}), bf16[64,8,512]{2,0,1:T(8,128)(2,1)S(1)}, u32[]{:S(2)}, u32[]{:S(2)}) async-start(bf16[64,8,512]{2,0,1:T(8,128)(2,1)} %bitcast.55), calls=%async_computation.2 | async-start | bytes 1048576 | tf_op jit(solution)/shard_map/all_to_all | solution.py:95
  88.2 77.3 %all-to-all-start = ((f32[8,64,512]{2,1,0:T(8,128)}), f32[8,64,512]{2,1,0:T(8,128)}, u32[]{:S(2)}, u32[]{:S(2)}) async-start(f32[8,64,512]{2,1,0:T(8,128)} %fusion.6), calls=%async_computation | async-start | bytes 2097152 | tf_op jit(solution)/shard_map/all_to_all | solution.py:113
  92.5 67.7 %reduce-scatter.7.cloned.1.call-start = ((), (), s32[]{:S(2)}) async-start(), calls=%async_computation.7 | async-start | bytes 294912
  93.7 69.9 %all-reduce.2.cloned.1.call-start = ((), (), s32[]{:S(2)}) async-start(), calls=%async_computation.5 | async-start | bytes 524288 | tf_op jit(solution)/shard_map/psum | solution.py:112
  95.5 128.8 %reduce-scatter.5.cloned.1.call-start = ((), (), s32[]{:S(2)}) async-start(), calls=%async_computation.6 | async-start | bytes 147456 | tf_op jit(solution)/shard_map/reduce_scatter | solution.py:133
Sparse Core Ops, SparseCore 0:
  97.6 62.5 reduce-scatter.6
  164.4 59.8 reduce-scatter.4
Sparse Core Ops, SparseCore 1:
  97.1 19.2 all-reduce.1
where the time goes:
time: 232 us
  waiting for transfers between devices  110 us (47%)
  blocking collectives  72 us (31%)
  local copies, waits for them, and re-layouts  16.2 us (7%)
  between operations  15.7 us (7%)
  starting transfers between devices  11.6 us (5%)
  matrix products  5.39 us (2%)
    unnamed x4, waiting for transfers between devices  64.6 us
    reduce_scatter x1, waiting for transfers between devices, local(): lax.psum_scatter(adapter_scale * lax.dot_general(low_wide, grads_piece, (...  44.9 us
    all_gather x1, blocking collectives, local(): row_portion = lax.all_gather(up_maps, 'dp', axis=0, tiled=True)  35 us
    all_gather x1, blocking collectives, local(): lax.all_gather(dlow_small, 'dp', axis=0, tiled=True)  30.6 us
    all_to_all x1, starting transfers between devices, local(): lax.all_to_all(inputs, 'dp', split_axis=1, concat_axis=0, tiled=True)  7.25 us
    all_to_all x2, local copies, waits for them, and re-layouts, local(): lax.all_to_all(dx_rows, 'tensor', split_axis=1, concat_axis=0, tiled=True)  4.87 us
  transfers between devices with their start and end apart: 5, of which 2 were waited for; matrix products, arithmetic and copies ran while one was open for 8% of the time, Pallas kernels for 0%

commit v1 on v0

v1 whole, which is shorter than its diff:
```python
import jax
import jax.numpy as jnp
from jax import lax
from jax.sharding import PartitionSpec as P

ADAPTER_RANK = 16
adapter_scale = 2.0


def dot(a, b, ca, cb):
    return lax.dot_general(a, b, (((ca,), (cb,)), ((), ())), preferred_element_type=jnp.float32)


def local(
    inputs,
    output_gradient,
    frozen_weight,
    down_maps,
    up_maps,
    segment_start,
    segment_adapter,
    adapter_slot,
    token_count,
):
    bf16, f32, i32 = jnp.bfloat16, jnp.float32, jnp.int32
    tok_half = inputs.shape[0]
    tok_rows, out_width = output_gradient.shape
    column_total = down_maps.shape[0]
    adapter_list = adapter_slot.shape[0]
    segs = segment_start.shape[1]
    dp_size = lax.axis_size("dp")
    tp_size = lax.axis_size("tensor")
    my_rank = lax.axis_index("dp")
    core_idx = lax.axis_index("tensor")
    picked = segs * ADAPTER_RANK
    piece_out = out_width // tp_size
    half = frozen_weight.shape[0]

    x_other = lax.ppermute(inputs, "tensor", [(0, 1), (1, 0)])

    adapter_ids = jnp.arange(adapter_list, dtype=i32)
    slot_table = jnp.sum(
        jnp.where(segment_adapter[..., None] == adapter_ids, adapter_slot, 0), axis=-1
    )
    column = slot_table[:, :, None] * ADAPTER_RANK + jnp.arange(ADAPTER_RANK, dtype=i32)
    onehot = (
        column.reshape(-1)[:, None] == jnp.arange(adapter_list * ADAPTER_RANK, dtype=i32)
    ).astype(bf16)

    a_send = dot(onehot, down_maps, 1, 1).astype(bf16).reshape(dp_size, picked, column_total)
    b_send = jnp.broadcast_to(up_maps[None], (dp_size,) + up_maps.shape)
    if column_total == out_width:
        got = lax.all_to_all(jnp.concatenate([a_send, b_send], axis=1), "dp", 0, 0, tiled=True)
        a_got, b_got = got[:, :picked], got[:, picked:]
    else:
        a_got = lax.all_to_all(a_send, "dp", 0, 0, tiled=True)
        b_got = lax.all_to_all(b_send, "dp", 0, 0, tiled=True)

    position = jnp.arange(tok_rows, dtype=i32)
    starts = lax.dynamic_index_in_dim(segment_start, my_rank, 0, keepdims=False)
    live = position < lax.dynamic_index_in_dim(token_count, my_rank, 0, keepdims=False)
    my_seg = jnp.sum((starts[None, :] <= position[:, None]).astype(i32), axis=1) - 1
    in_seg = my_seg[:, None] == (jnp.arange(picked, dtype=i32) // ADAPTER_RANK)[None, :]
    my_onehot = lax.dynamic_slice_in_dim(onehot, my_rank * picked, picked, 0)
    g = jnp.where(live[:, None], output_gradient, jnp.zeros_like(output_gradient))
    base = dot(g, frozen_weight, 1, 1)

    b_sel = dot(my_onehot, b_got.reshape(-1, out_width), 1, 0).astype(bf16)
    dlow = (adapter_scale * dot(g, b_sel, 1, 1)).astype(bf16)
    dlow = jnp.where(in_seg, dlow, jnp.zeros_like(dlow))
    a_sel = jnp.moveaxis(a_got, 0, 1).reshape(picked, -1)
    first = core_idx == 0
    x = jnp.concatenate(
        [jnp.where(first, inputs, x_other), jnp.where(first, x_other, inputs)], axis=0
    )
    low = dot(x, a_sel, 1, 1).astype(bf16)
    low = jnp.where(in_seg, low, jnp.zeros_like(low))
    low_wide = dot(low, my_onehot, 1, 0).astype(bf16)

    ga_send = dot(dlow, x, 0, 0).astype(bf16).reshape(picked, dp_size, column_total)
    ga_send = jnp.moveaxis(ga_send, 1, 0)
    g_piece = lax.dynamic_slice_in_dim(g, core_idx * piece_out, piece_out, 1)
    up_send = (adapter_scale * dot(low_wide, g_piece, 0, 0)).astype(bf16)
    up_send = up_send.reshape(dp_size, -1, piece_out)
    if column_total % piece_out == 0:
        parts = column_total // piece_out
        folded = [ga_send[:, :, k * piece_out : (k + 1) * piece_out] for k in range(parts)]
        got = lax.all_to_all(jnp.concatenate(folded + [up_send], axis=1), "dp", 0, 0, tiled=True)
        ga_got = jnp.concatenate(
            [got[:, k * picked : (k + 1) * picked] for k in range(parts)], axis=2
        )
        up_got = got[:, parts * picked :]
    else:
        ga_got = lax.all_to_all(ga_send, "dp", 0, 0, tiled=True)
        up_got = lax.all_to_all(up_send, "dp", 0, 0, tiled=True)

    a_half = lax.dynamic_slice_in_dim(a_sel, core_idx * half, half, 1)
    grad_x = (base + dot(dlow, a_half, 1, 0)).astype(bf16)

    grad_a = dot(ga_got.reshape(dp_size * picked, column_total), onehot, 0, 0)
    up_map_gradient = jnp.sum(up_got.astype(f32), axis=0)
    return grad_x, grad_a, up_map_gradient


def solution(mesh):
    in_specs = (
        P(("groups", "dp", "tensor"), None),
        P(("groups", "dp"), None),
        P("tensor", None),
        P(("groups", "dp"), None),
        P(("groups", "dp"), None),
        P("groups", None),
        P("groups", None),
        P("groups"),
        P("groups"),
    )
    out_specs = (
        P(("groups", "dp"), "tensor"),
        P(("groups", "dp"), None),
        P(("groups", "dp"), "tensor"),
    )
    return jax.shard_map(local, mesh=mesh, in_specs=in_specs, out_specs=out_specs, check_vma=False)
```

time: 232 us -> 44.3 us (0.19)
  waiting for transfers between devices: 110 us -> 16 us
  blocking collectives: 72 us -> 0 us
  between operations: 15.7 us -> 0.84 us
  local copies, waits for them, and re-layouts: 16.2 us -> 1.81 us
  other arithmetic: 1.29 us -> 6.3 us
  matrix products: 5.39 us -> 7.89 us
    all_gather x3 -> x0, blocking collectives: 67.5 us -> none  [the longest x1 35 us: local(): row_portion = lax.all_gather(up_maps, 'dp', axis=0, tiled=True)]
    unnamed x4 -> x0, waiting for transfers between devices: 64.6 us -> none
    reduce_scatter x1 -> x0, waiting for transfers between devices: 44.9 us -> none  [local(): lax.psum_scatter(adapter_scale * lax.dot_general(low_wide, grads_piece, (...]
    all_to_all x2, waiting for transfers between devices: 0.01 us -> 15.7 us  [the longest x1 8.23 us: local(): lax.all_to_all(jnp.concatenate(folded + [up_send], axis=1), 'dp', 0, 0, t...]
    all_to_all x4 -> x0, local copies, waits for them, and re-layouts: 9.77 us -> none  [the longest x2 4.87 us: local(): lax.all_to_all(dx_rows, 'tensor', split_axis=1, concat_axis=0, tiled=True)]
    all_to_all x1 -> x0, blocking collectives: 4.58 us -> none  [local(): lax.all_to_all(dx_rows, 'tensor', split_axis=1, concat_axis=0, tiled=True)]
    unnamed x21 -> x11, local copies, waits for them, and re-layouts: 3.68 us -> 0.04 us
    dot_general x8, matrix products: 5.39 us -> 7.89 us  [dot(): lax.dot_general(a, b, (((ca,), (cb,)), ((), ())), preferred_element_type=...]
  transfers between devices with their start and end apart: 5 -> 3, of which waited for: 2 -> 3; matrix products, arithmetic and copies ran while one was open for 8% -> 13% of each run, Pallas kernels for 0% -> 0%
where the time goes in v1:
time: 44.3 us; the launch traced here: 43.8 us
  waiting for transfers between devices  16 us (36%)
  starting transfers between devices  11 us (25%)
  matrix products  7.89 us (18%)
  other arithmetic  6.3 us (14%)
  local copies, waits for them, and re-layouts  1.81 us (4%)
  between operations  0.84 us (2%)
    all_to_all x1, waiting for transfers between devices, local(): lax.all_to_all(jnp.concatenate(folded + [up_send], axis=1), 'dp', 0, 0, t...  8.23 us
    dot_general x8, matrix products, dot(): lax.dot_general(a, b, (((ca,), (cb,)), ((), ())), preferred_element_type=...  7.89 us
    all_to_all x1, waiting for transfers between devices, local(): lax.all_to_all(jnp.concatenate([a_send, b_send], axis=1), 'dp', 0, 0, til...  7.51 us
    all_to_all x1, starting transfers between devices, local(): lax.all_to_all(jnp.concatenate([a_send, b_send], axis=1), 'dp', 0, 0, til...  7.25 us
    all_to_all x1, starting transfers between devices, local(): lax.all_to_all(jnp.concatenate(folded + [up_send], axis=1), 'dp', 0, 0, t...  3.63 us
    select_n x1, other arithmetic, local(): jnp.where(first, inputs, x_other)  2.06 us
    reduce_sum x1, other arithmetic, local(): jnp.sum(jnp.where(segment_adapter[..., None] == adapter_ids, adapter_slot...  1.05 us
  transfers between devices with their start and end apart: 3, of which 3 were waited for; matrix products, arithmetic and copies ran while one was open for 13% of the time, Pallas kernels for 0%

profile of v1, /device:TPU:0, one launch (start us, length us, event | category | flops | bytes accessed | tf_op | source)
XLA Modules:
  0.0 43.8 jit_solution(11695788787897445587)
XLA Ops:
  0.6 0.0 copy-start
  0.6 0.0 copy-start.1
  0.7 0.0 copy-start.4
  0.7 0.0 copy-start.3
  0.7 0.0 copy-start.2
  0.7 1.1 %select_reduce_fusion = s32[8,2]{0,1:T(2,128)S(1)} fusion(s32[8]{0:T(128)} %param.16, s32[8,2]{0,1:T(2,128)} %param.15), kind=kLoop, calls=%fused_computation.33 | loop fusion | flops 368 | bytes 160 | tf_op jit(solution)/shard_map/reduce_sum | solution.py:42
  1.8 0.1 copy.20
  1.8 0.1 iota_add_fusion
  1.9 0.1 add.52
  2.0 1.2 %convolution_convert_fusion.1 = bf16[256,512]{1,0:T(8,128)(2,1)S(1)} fusion(bf16[512,128]{1,0:T(8,128)(2,1)} %param.12, s32[256]{0:T(256)S(1)} %add.52), kind=kOutput, calls=%fused_computation.3 | convolution fusion | flops 33718272 | bytes 394240 | tf_op jit(solution)/shard_map/dot_general | solution.py:11
  3.2 0.7 %broadcast_in_dim.21 = bf16[8,16,512]{2,1,0:T(8,128)(2,1)S(1)} broadcast(bf16[16,512]{1,0:T(8,128)(2,1)} %param.13), dimensions={1,2} | broadcast | bytes 147456 | tf_op jit(solution)/shard_map/broadcast_in_dim | solution.py:51
  3.9 0.8 %pad_maximum_fusion.3 = bf16[8,48,512]{2,1,0:T(8,128)(2,1)} fusion(bf16[8,16,512]{2,1,0:T(8,128)(2,1)S(1)} %broadcast_in_dim.21, bf16[8,32,512]{2,1,0:T(8,128)(2,1)S(1)} %bitcast.26), kind=kLoop, calls=%fused_computation.17 | loop fusion | flops 786432 | bytes 786432 | tf_op jit(solution)/shard_map/concatenate | solution.py:53
  4.7 7.3 %all-to-all-start = ((bf16[8,48,512]{2,1,0:T(8,128)(2,1)}), bf16[8,48,512]{2,1,0:T(8,128)(2,1)S(1)}, u32[]{:S(2)}, u32[]{:S(2)}) async-start(bf16[8,48,512]{2,1,0:T(8,128)(2,1)} %pad_maximum_fusion.3), calls=%async_computation | async-start | bytes 786432 | tf_op jit(solution)/shard_map/all_to_all | solution.py:53
  12.0 0.0 copy-done.1
  12.0 0.1 collective-permute-start
  12.1 0.0 copy-done.4
  12.1 0.6 %dynamic_slice.17 = s32[1]{0:T(128)} dynamic-slice(s32[8]{0:T(128)S(1)} %copy-done.4, s32[]{:T(128)S(6)} %select_n.51), dynamic_slice_sizes={1} | dynamic-slice | bytes 12 | tf_op jit(solution)/shard_map/jit(dynamic_index_in_dim)/dynamic_slice | solution.py:61
  12.7 0.0 copy-done.3
  12.7 0.2 dynamic-slice_reduce_fusion
  12.8 0.1 fusion.16
  12.9 0.7 %iota_compare_fusion.4 = pred[128]{0:T(512)(128)(4,1)S(1)} fusion(s32[]{:T(128)} %bitcast), kind=kLoop, calls=%fused_computation.46 | loop fusion | flops 128 | bytes 132 | tf_op jit(solution)/shard_map/lt | solution.py:61
  13.6 0.1 iota_compare_fusion
  13.7 0.0 copy-done.2
  13.7 0.1 broadcast_select_fusion.2
  13.8 0.3 collective-permute-done
  14.1 2.1 %broadcast_select_fusion.1 = (bf16[64,4096]{1,0:T(8,128)(2,1)}, bf16[64,4096]{1,0:T(8,128)(2,1)}) fusion(bf16[64,4096]{1,0:T(8,128)(2,1)S(1)} %copy-done.1, bf16[64,4096]{1,0:T(8,128)(2,1)} %collective-permute-done, pred[]{:T(512)S(6)} %eq.51), kind=kLoop, calls=%fused_computation.16 | loop fusion | flops 524288 | bytes 2097153 | tf_op jit(solution)/shard_map/jit(_where)/select_n | solution.py:74
  16.1 7.5 %all-to-all-done = bf16[8,48,512]{2,1,0:T(8,128)(2,1)S(1)} async-done(((bf16[8,48,512]{2,1,0:T(8,128)(2,1)}), bf16[8,48,512]{2,1,0:T(8,128)(2,1)S(1)}, u32[]{:S(2)}, u32[]{:S(2)}) %all-to-all-start) | async-done | bytes 393248 | tf_op jit(solution)/shard_map/all_to_all | solution.py:53
  23.7 1.7 %fusion.5 = bf16[128,32]{0,1:T(8,128)(2,1)S(1)} fusion(bf16[32,4096]{1,0:T(8,128)(2,1)S(1)} %bitcast.29, bf16[64,4096]{1,0:T(8,128)(2,1)} %get-tuple-element.4, bf16[64,4096]{1,0:T(8,128)(2,1)} %get-tuple-element.3, s32[128]{0:T(128)S(1)} %broadcast_add_fusion, s32[32]{0:T(128)S(1)} %and_select_fusion), kind=kOutput, calls=%fused_computation.12 | convolution fusion | flops 35663872 | bytes 1319552 | tf_op jit(solution)/shard_map/dot_general | solution.py:11
  25.4 0.2 fusion.6
  25.6 1.5 %convolution_convert_fusion = bf16[32,4096]{1,0:T(8,128)(2,1)S(1)} fusion(bf16[128,32]{0,1:T(8,128)(2,1)S(1)} %fusion.6, bf16[64,4096]{1,0:T(8,128)(2,1)} %get-tuple-element.4, bf16[64,4096]{1,0:T(8,128)(2,1)} %get-tuple-element.3), kind=kOutput, calls=%fused_computation | convolution fusion | flops 35782656 | bytes 1318912 | tf_op jit(solution)/shard_map/dot_general | solution.py:11
  27.2 0.4 fusion.1
  27.5 0.7 %pad_maximum_fusion.4 = bf16[8,80,256]{2,1,0:T(8,128)(2,1)} fusion(bf16[8,16,256]{2,1,0:T(8,128)(2,1)S(1)} %bitcast.31, bf16[8,32,256]{2,1,0:T(8,128)(2,1)S(1)} %get-tuple-element.8, bf16[8,32,256]{2,1,0:T(8,128)(2,1)S(1)} %get-tuple-element.7), kind=kLoop, calls=%fused_computation.18 | loop fusion | flops 983040 | bytes 655360 | tf_op jit(solution)/shard_map/concatenate | solution.py:88
  28.3 3.6 %all-to-all-start.1 = ((bf16[8,80,256]{2,1,0:T(8,128)(2,1)}), bf16[8,80,256]{2,1,0:T(8,128)(2,1)S(1)}, u32[]{:S(2)}, u32[]{:S(2)}) async-start(bf16[8,80,256]{2,1,0:T(8,128)(2,1)} %pad_maximum_fusion.4), calls=%async_computation.1 | async-start | bytes 655360 | tf_op jit(solution)/shard_map/all_to_all | solution.py:88
  31.9 0.0 copy-done
  31.9 0.8 %fusion.26 = f32[128,2048]{1,0:T(8,128)S(1)} fusion(bf16[128,512]{1,0:T(8,128)(2,1)S(1)} %broadcast_select_fusion.2, bf16[2048,512]{1,0:T(8,128)(2,1)S(1)} %copy-done), kind=kOutput, calls=%fused_computation.52 | convolution fusion | flops 268435456 | bytes 3276800 | tf_op jit(solution)/shard_map/dot_general | solution.py:11
  32.7 1.1 %fusion = bf16[128,2048]{1,0:T(8,128)(2,1)} fusion(f32[128,2048]{1,0:T(8,128)S(1)} %fusion.26, bf16[128,32]{0,1:T(8,128)(2,1)S(1)} %fusion.6, bf16[32,4096]{1,0:T(8,128)(2,1)S(1)} %bitcast.30, s32[]{:T(128)S(6)} %select_n.57), kind=kOutput, calls=%fused_computation.2 | convolution fusion | flops 17301504 | bytes 1712132 | tf_op jit(solution)/shard_map/dot_general | solution.py:11
  33.9 8.2 %all-to-all-done.1 = bf16[8,80,256]{2,1,0:T(8,128)(2,1)S(1)} async-done(((bf16[8,80,256]{2,1,0:T(8,128)(2,1)}), bf16[8,80,256]{2,1,0:T(8,128)(2,1)S(1)}, u32[]{:S(2)}, u32[]{:S(2)}) %all-to-all-start.1) | async-done | bytes 327712 | tf_op jit(solution)/shard_map/all_to_all | solution.py:88
  42.1 1.0 %fusion.8 = f32[512,128]{1,0:T(8,128)} fusion(bf16[256,512]{1,0:T(8,128)(2,1)S(1)} %bitcast.28, s32[256]{0:T(256)S(1)} %add.52), kind=kOutput, calls=%fused_computation.26 | convolution fusion | flops 33587200 | bytes 525312 | tf_op jit(solution)/shard_map/dot_general | solution.py:11
  43.2 0.6 %convert_reduce_fusion = f32[16,256]{1,0:T(8,128)} fusion(bf16[8,80,256]{2,1,0:T(8,128)(2,1)S(1)} %all-to-all-done.1), kind=kLoop, calls=%fused_computation.22 | loop fusion | flops 61440 | bytes 81920 | tf_op jit(solution)/shard_map/reduce_sum | solution.py:101
  (10 shorter events, 0.1 us)
Async XLA Ops:
  0.6 31.3 %copy-start = (bf16[2048,512]{1,0:T(8,128)(2,1)S(1)}, bf16[2048,512]{1,0:T(8,128)(2,1)}, u32[]{:S(2)}) copy-start(bf16[2048,512]{1,0:T(8,128)(2,1)} %param.11) | copy-start | bytes 6291460
  0.6 11.3 %copy-start.1 = (bf16[64,4096]{1,0:T(8,128)(2,1)S(1)}, bf16[64,4096]{1,0:T(8,128)(2,1)}, u32[]{:S(2)}) copy-start(bf16[64,4096]{1,0:T(8,128)(2,1)} %param.9) | copy-start | bytes 1572868
  0.7 11.4 %copy-start.4 = (s32[8]{0:T(128)S(1)}, s32[8]{0:T(128)}, u32[]{:S(2)}) copy-start(s32[8]{0:T(128)} %param.17) | copy-start | bytes 100
  0.7 12.0 %copy-start.3 = (s32[8,2]{0,1:T(2,128)S(1)}, s32[8,2]{0,1:T(2,128)}, u32[]{:S(2)}) copy-start(s32[8,2]{0,1:T(2,128)} %param.14) | copy-start | bytes 196
  0.7 13.0 %copy-start.2 = (bf16[128,512]{1,0:T(8,128)(2,1)S(1)}, bf16[128,512]{1,0:T(8,128)(2,1)}, u32[]{:S(2)}) copy-start(bf16[128,512]{1,0:T(8,128)(2,1)} %param.10) | copy-start | bytes 393220
  4.7 18.9 %all-to-all-start = ((bf16[8,48,512]{2,1,0:T(8,128)(2,1)}), bf16[8,48,512]{2,1,0:T(8,128)(2,1)S(1)}, u32[]{:S(2)}, u32[]{:S(2)}) async-start(bf16[8,48,512]{2,1,0:T(8,128)(2,1)} %pad_maximum_fusion.3), calls=%async_computation | async-start | bytes 786432 | tf_op jit(solution)/shard_map/all_to_all | solution.py:53
  12.0 2.1 %collective-permute-start = (bf16[64,4096]{1,0:T(8,128)(2,1)S(1)}, bf16[64,4096]{1,0:T(8,128)(2,1)}, u32[]{:S(2)}, u32[]{:S(2)}) collective-permute-start(bf16[64,4096]{1,0:T(8,128)(2,1)S(1)} %copy-done.1), channel_id=1, source_target_pairs={{0,1},{1,0},{2,3},{3,2},{4,5},{5,4},{6,7},{7,6},{8,9},{9,8},{10,11... | collective-permute-start | bytes 1572872 | tf_op jit(solution)/shard_map/ppermute | solution.py:39
  28.3 13.8 %all-to-all-start.1 = ((bf16[8,80,256]{2,1,0:T(8,128)(2,1)}), bf16[8,80,256]{2,1,0:T(8,128)(2,1)S(1)}, u32[]{:S(2)}, u32[]{:S(2)}) async-start(bf16[8,80,256]{2,1,0:T(8,128)(2,1)} %pad_maximum_fusion.4), calls=%async_computation.1 | async-start | bytes 655360 | tf_op jit(solution)/shard_map/all_to_all | solution.py:88

commit v2 on v1

--- a/solution.py
+++ b/solution.py
@@ -1,17 +1,137 @@
+import functools
+
 import jax
 import jax.numpy as jnp
 from jax import lax
+from jax.experimental import pallas as pl
+from jax.experimental.pallas import tpu as pltpu
 from jax.sharding import PartitionSpec as P
 
 ADAPTER_RANK = 16
 adapter_scale = 2.0
 
+bf16, f32, i32 = jnp.bfloat16, jnp.float32, jnp.int32
+
+SMEM = pl.BlockSpec(memory_space=pltpu.SMEM)
+VMEM = pl.BlockSpec(memory_space=pltpu.VMEM)
+
 
 def dot(a, b, ca, cb):
-    return lax.dot_general(a, b, (((ca,), (cb,)), ((), ())), preferred_element_type=jnp.float32)
-
-
-def local(
+    return lax.dot_general(a, b, (((ca,), (cb,)), ((), ())), preferred_element_type=f32)
+
+
+def params(mib):
+    return pltpu.CompilerParams(vmem_limit_bytes=mib << 20)
+
+
+def slot_rows(chosen_ref, slot_ref, ranks, width):
+    segs = chosen_ref.shape[1]
+    lane = lax.broadcasted_iota(i32, (ADAPTER_RANK, width), 1)
+    row = lax.broadcasted_iota(i32, (ADAPTER_RANK, width), 0)
+    rows = []
+    for rank in ranks:
+        for k in range(segs):
+            first = slot_ref[chosen_ref[rank, k]] * ADAPTER_RANK
+            rows.append(jnp.where(lane == row + first, 1.0, 0.0))
+    return jnp.concatenate(rows, axis=0).astype(bf16)
+
+
+def others(me, n, sign):
+    return [lax.rem(me + (sign * d) % n, n) for d in range(n)]
+
+
+def pack_kernel(n, chosen_ref, slot_ref, down_ref, up_ref, *send):
+    me = lax.axis_index("dp")
+    onehot = slot_rows(chosen_ref, slot_ref, others(me, n, 1), down_ref.shape[1])
+    picked = onehot.shape[0] // n
+    columns = dot(onehot, down_ref[...], 1, 1).astype(bf16)
+    for d in range(n):
+        send[d][:picked, :] = columns[d * picked : (d + 1) * picked]
+        send[d][picked:, :] = up_ref[...]
+
+
+def middle_kernel(n, piece, start_ref, chosen_ref, slot_ref, count_ref, x_mine, x_other, g_ref, *refs):
+    got, (dlow_ref, a_ref), send = refs[:n], refs[n : n + 2], refs[n + 2 : 2 * n + 2]
+    x_ref, b_ref, up_ref = refs[2 * n + 2 :]
+    me, core = lax.axis_index("dp"), lax.axis_index("tensor")
+    segs = start_ref.shape[1]
+    picked = segs * ADAPTER_RANK
+    half, rows, width = x_mine.shape[0], g_ref.shape[0], got[0].shape[1]
+
+    x_ref[pl.ds(pl.multiple_of(core * half, half), half), :] = x_mine[...]
+    x_ref[pl.ds(pl.multiple_of((1 - core) * half, half), half), :] = x_other[...]
+    sources = others(me, n, -1)
+    for d in range(n):
+        a_ref[sources[d]] = got[d][:picked, :]
+        b_ref[sources[d]] = got[d][picked:, :]
+
+    position = lax.broadcasted_iota(i32, (rows, picked), 0)
+    group = lax.broadcasted_iota(i32, (rows, picked), 1) // ADAPTER_RANK
+    segment = jnp.full((rows, picked), -1, i32)
+    for k in range(segs):
+        segment += jnp.where(position >= start_ref[me, k], 1, 0)
+    in_seg = segment == group
+    live = lax.broadcasted_iota(i32, g_ref.shape, 0) < count_ref[me]
+    g = jnp.where(live, g_ref[...], jnp.zeros(g_ref.shape, bf16))
+
+    b_sel = jnp.concatenate([b_ref[slot_ref[chosen_ref[me, k]]] for k in range(segs)], axis=0)
+    dlow = jnp.where(in_seg, adapter_scale * dot(g, b_sel, 1, 1), 0.0).astype(bf16)
+    dlow_ref[...] = dlow
+    targets = others(me, n, 1)
+    for d in range(n):
+        at = pl.multiple_of(targets[d] * width, width)
+        part = dot(dlow, x_ref[:, pl.ds(at, width)], 0, 0).astype(bf16)
+        for k in range(width // piece):
+            send[d][k * picked : (k + 1) * picked, :] = part[:, k * piece : (k + 1) * piece]
+
+    low = jnp.zeros((rows, picked), f32)
+    for q in range(n):
+        low += dot(x_ref[:, q * width : (q + 1) * width], a_ref[q], 1, 1)
+    low = jnp.where(in_seg, low, 0.0).astype(bf16)
+    onehot = slot_rows(chosen_ref, slot_ref, [me], n * ADAPTER_RANK)
+    low_wide = dot(low, onehot, 1, 0).astype(bf16)
+    g_piece = g_ref[:, pl.ds(pl.multiple_of(core * piece, piece), piece)]
+    g_piece = jnp.where(live[:, :piece], g_piece, jnp.zeros(g_piece.shape, bf16))
+    up = (adapter_scale * dot(low_wide, g_piece, 0, 0)).astype(bf16)
+    for s in range(n):
+        up_ref[s] = up[s * ADAPTER_RANK : (s + 1) * ADAPTER_RANK]
+    for d in range(n):
+        send[d][width // piece * picked :, :] = up_ref[targets[d]]
+
+
+def grad_x_kernel(count_ref, g_ref, w_ref, dlow_ref, a_ref, out_ref):
+    me, core = lax.axis_index("dp"), lax.axis_index("tensor")
+    live = lax.broadcasted_iota(i32, g_ref.shape, 0) < count_ref[me]
+    g = jnp.where(live, g_ref[...], jnp.zeros(g_ref.shape, bf16))
+    block = core * pl.num_programs(0) + pl.program_id(0)
+    total = dot(g, w_ref[...], 1, 1) + dot(dlow_ref[...], a_ref[block], 1, 0)
+    out_ref[...] = total.astype(bf16)
+
+
+def final_kernel(n, chosen_ref, slot_ref, *refs):
+    got, (a_ref, up_ref) = refs[:n], refs[n:]
+    me = lax.axis_index("dp")
+    onehot = slot_rows(chosen_ref, slot_ref, others(me, n, -1), a_ref.shape[1])
+    picked = onehot.shape[0] // n
+    piece = got[0].shape[1]
+    parts = a_ref.shape[0] // piece
+    for k in range(parts):
+        rows = jnp.concatenate([r[k * picked : (k + 1) * picked, :] for r in got], axis=0)
+        a_ref[k * piece : (k + 1) * piece, :] = dot(rows, onehot, 0, 0)
+    up = got[0][parts * picked :, :].astype(f32)
+    for r in got[1:]:
+        up += r[parts * picked :, :].astype(f32)
+    up_ref[...] = up
+
+
+def exchange(messages):
+    n = len(messages)
+    return [messages[0]] + [
+        lax.ppermute(messages[d], "dp", [(i, (i + d) % n) for i in range(n)]) for d in range(1, n)
+    ]
+
+
+def local_kernels(
     inputs,
     output_gradient,
     frozen_weight,
@@ -22,22 +142,107 @@
     adapter_slot,
     token_count,
 ):
-    bf16, f32, i32 = jnp.bfloat16, jnp.float32, jnp.int32
-    tok_half = inputs.shape[0]
+    tok_half, model_width = inputs.shape
+    tok_rows, out_width = output_gradient.shape
+    column_total, slot_width = down_maps.shape
+    half = frozen_weight.shape[0]
+    n = lax.axis_size("dp")
+    piece = out_width // lax.axis_size("tensor")
+    picked = segment_start.shape[1] * ADAPTER_RANK
+    shape = jax.ShapeDtypeStruct
+
+    x_other = lax.ppermute(inputs, "tensor", [(0, 1), (1, 0)])
+
+    sent = pl.pallas_call(
+        functools.partial(pack_kernel, n),
+        out_shape=[shape((picked + ADAPTER_RANK, column_total), bf16)] * n,
+        in_specs=[SMEM, SMEM, VMEM, VMEM],
+        out_specs=[VMEM] * n,
+        compiler_params=params(8),
+    )(segment_adapter, adapter_slot, down_maps, up_maps)
+    got = exchange(sent)
+
+    rows = column_total // piece * picked + ADAPTER_RANK
+    dlow, a_all, *sent = pl.pallas_call(
+        functools.partial(middle_kernel, n, piece),
+        out_shape=[
+            shape((tok_rows, picked), bf16),
+            shape((n, picked, column_total), bf16),
+        ]
+        + [shape((rows, piece), bf16)] * n,
+        in_specs=[SMEM] * 4 + [VMEM] * (3 + n),
+        out_specs=[VMEM] * (2 + n),
+        scratch_shapes=[
+            pltpu.VMEM((tok_rows, model_width), bf16),
+            pltpu.VMEM((n, ADAPTER_RANK, out_width), bf16),
+            pltpu.VMEM((n, ADAPTER_RANK, piece), bf16),
+        ],
+        compiler_params=params(16),
+    )(
+        segment_start,
+        segment_adapter,
+        adapter_slot,
+        token_count,
+        inputs,
+        x_other,
+        output_gradient,
+        *got,
+    )
+    got = exchange(sent)
+
+    grad_x = pl.pallas_call(
+        grad_x_kernel,
+        out_shape=shape((tok_rows, half), bf16),
+        grid=(half // column_total,),
+        in_specs=[
+            SMEM,
+            pl.BlockSpec((tok_rows, out_width), lambda j: (0, 0)),
+            pl.BlockSpec((column_total, out_width), lambda j: (j, 0)),
+            pl.BlockSpec((tok_rows, picked), lambda j: (0, 0)),
+            pl.BlockSpec((n, picked, column_total), lambda j: (0, 0, 0)),
+        ],
+        out_specs=pl.BlockSpec((tok_rows, column_total), lambda j: (0, j)),
+        compiler_params=params(16),
+        cost_estimate=pl.CostEstimate(
+            flops=2 * tok_rows * half * (out_width + picked),
+            bytes_accessed=2 * half * (out_width + tok_rows),
+            transcendentals=0,
+        ),
+    )(token_count, output_gradient, frozen_weight, dlow, a_all)
+
+    grad_a, up_map_gradient = pl.pallas_call(
+        functools.partial(final_kernel, n),
+        out_shape=[shape((column_total, slot_width), f32), shape((ADAPTER_RANK, piece), f32)],
+        in_specs=[SMEM, SMEM] + [VMEM] * n,
+        out_specs=[VMEM, VMEM],
+        compiler_params=params(8),
+    )(segment_adapter, adapter_slot, *got)
+    return grad_x, grad_a, up_map_gradient
+
+
+def local_plain(
+    inputs,
+    output_gradient,
+    frozen_weight,
+    down_maps,
+    up_maps,
+    segment_start,
+    segment_adapter,
+    adapter_slot,
+    token_count,
+):
     tok_rows, out_width = output_gradient.shape
     column_total = down_maps.shape[0]
     adapter_list = adapter_slot.shape[0]
     segs = segment_start.shape[1]
     dp_size = lax.axis_size("dp")
-    tp_size = lax.axis_size("tensor")
     my_rank = lax.axis_index("dp")
     core_idx = lax.axis_index("tensor")
     picked = segs * ADAPTER_RANK
-    piece_out = out_width // tp_size
+    piece_out = out_width // lax.axis_size("tensor")
     half = frozen_weight.shape[0]
 
     x_other = lax.ppermute(inputs, "tensor", [(0, 1), (1, 0)])
-
     adapter_ids = jnp.arange(adapter_list, dtype=i32)
     slot_table = jnp.sum(
         jnp.where(segment_adapter[..., None] == adapter_ids, adapter_slot, 0), axis=-1
@@ -49,12 +254,8 @@
 
     a_send = dot(onehot, down_maps, 1, 1).astype(bf16).reshape(dp_size, picked, column_total)
     b_send = jnp.broadcast_to(up_maps[None], (dp_size,) + up_maps.shape)
-    if column_total == out_width:
-        got = lax.all_to_all(jnp.concatenate([a_send, b_send], axis=1), "dp", 0, 0, tiled=True)
-        a_got, b_got = got[:, :picked], got[:, picked:]
-    else:
-        a_got = lax.all_to_all(a_send, "dp", 0, 0, tiled=True)
-        b_got = lax.all_to_all(b_send, "dp", 0, 0, tiled=True)
+    a_got = lax.all_to_all(a_send, "dp", 0, 0, tiled=True)
+    b_got = lax.all_to_all(b_send, "dp", 0, 0, tiled=True)
 
     position = jnp.arange(tok_rows, dtype=i32)
     starts = lax.dynamic_index_in_dim(segment_start, my_rank, 0, keepdims=False)
@@ -78,28 +279,30 @@
     low_wide = dot(low, my_onehot, 1, 0).astype(bf16)
 
     ga_send = dot(dlow, x, 0, 0).astype(bf16).reshape(picked, dp_size, column_total)
-    ga_send = jnp.moveaxis(ga_send, 1, 0)
+    ga_got = lax.all_to_all(jnp.moveaxis(ga_send, 1, 0), "dp", 0, 0, tiled=True)
     g_piece = lax.dynamic_slice_in_dim(g, core_idx * piece_out, piece_out, 1)
     up_send = (adapter_scale * dot(low_wide, g_piece, 0, 0)).astype(bf16)
-    up_send = up_send.reshape(dp_size, -1, piece_out)
-    if column_total % piece_out == 0:
-        parts = column_total // piece_out
-        folded = [ga_send[:, :, k * piece_out : (k + 1) * piece_out] for k in range(parts)]
-        got = lax.all_to_all(jnp.concatenate(folded + [up_send], axis=1), "dp", 0, 0, tiled=True)
-        ga_got = jnp.concatenate(
-            [got[:, k * picked : (k + 1) * picked] for k in range(parts)], axis=2
-        )
-        up_got = got[:, parts * picked :]
-    else:
-        ga_got = lax.all_to_all(ga_send, "dp", 0, 0, tiled=True)
-        up_got = lax.all_to_all(up_send, "dp", 0, 0, tiled=True)
+    up_got = lax.all_to_all(up_send.reshape(dp_size, -1, piece_out), "dp", 0, 0, tiled=True)
 
     a_half = lax.dynamic_slice_in_dim(a_sel, core_idx * half, half, 1)
     grad_x = (base + dot(dlow, a_half, 1, 0)).astype(bf16)
-
     grad_a = dot(ga_got.reshape(dp_size * picked, column_total), onehot, 0, 0)
     up_map_gradient = jnp.sum(up_got.astype(f32), axis=0)
     return grad_x, grad_a, up_map_gradient
+
+
+def local(*args):
+    down_maps, up_maps = args[3], args[4]
+    n, tp = lax.axis_size("dp"), lax.axis_size("tensor")
+    out_width = up_maps.shape[1]
+    kernels_fit = (
+        n <= 16
+        and tp == 2
+        and down_maps.shape[0] == out_width
+        and down_maps.shape[1] == n * up_maps.shape[0]
+        and out_width % (128 * tp) == 0
+    )
+    return (local_kernels if kernels_fit else local_plain)(*args)
 
 
 def solution(mesh):

time: 44.3 us -> 44.8 us (1.011)
  waiting for transfers between devices: 16 us -> 3.14 us
  starting transfers between devices: 11 us -> 23.3 us
  local copies, waits for them, and re-layouts: 1.81 us -> 10.2 us
  matrix products: 7.89 us -> 0 us
  Pallas kernels: 0 us -> 7.11 us
  other arithmetic: 6.3 us -> 0 us
    ppermute x1 -> x15, starting transfers between devices: 0.07 us -> 23.3 us  [the longest x14 22.8 us: exchange(): lax.ppermute(messages[d], 'dp', [(i, (i + d) % n) for i in range(n)])]
    all_to_all x2 -> x0, waiting for transfers between devices: 15.7 us -> none  [the longest x1 8.23 us: local(): lax.all_to_all(jnp.concatenate(folded + [up_send], axis=1), 'dp', 0, 0, t...]
    all_to_all x2 -> x0, starting transfers between devices: 10.9 us -> none  [the longest x1 7.25 us: local(): lax.all_to_all(jnp.concatenate([a_send, b_send], axis=1), 'dp', 0, 0, til...]
    unnamed x11 -> x24, local copies, waits for them, and re-layouts: 0.04 us -> 10.2 us
    dot_general x8 -> x0, matrix products: 7.89 us -> none  [dot(): lax.dot_general(a, b, (((ca,), (cb,)), ((), ())), preferred_element_type=...]
    pallas_call x0 -> x4, Pallas kernels: none -> 7.11 us  [the longest x1 2.89 us: local_kernels(): pl.pallas_call(grad_x_kernel, out_shape=shape((tok_rows, half), bf16), gr...]
    ppermute x1 -> x15, waiting for transfers between devices: 0.26 us -> 3.14 us  [the longest x14 3.13 us: exchange(): lax.ppermute(messages[d], 'dp', [(i, (i + d) % n) for i in range(n)])]
    select_n x3 -> x0, other arithmetic: 2.15 us -> none  [the longest x1 2.06 us: local(): jnp.where(first, inputs, x_other)]
  transfers between devices with their start and end apart: 3 -> 15, of which waited for: 3 -> 5; matrix products, arithmetic and copies ran while one was open for 13% -> 3% of each run, Pallas kernels for 0% -> 8%
where the time goes in v2:
time: 44.8 us; the launch traced here: 44.4 us
  starting transfers between devices  23.3 us (52%)
  local copies, waits for them, and re-layouts  10.2 us (23%)
  Pallas kernels  7.11 us (16%)
  waiting for transfers between devices  3.14 us (7%)
  between operations  0.7 us (2%)
    ppermute x14, starting transfers between devices, exchange(): lax.ppermute(messages[d], 'dp', [(i, (i + d) % n) for i in range(n)])  22.8 us
    unnamed x24, local copies, waits for them, and re-layouts  10.2 us
    ppermute x14, waiting for transfers between devices, exchange(): lax.ppermute(messages[d], 'dp', [(i, (i + d) % n) for i in range(n)])  3.13 us
    pallas_call x1, Pallas kernels, local_kernels(): pl.pallas_call(grad_x_kernel, out_shape=shape((tok_rows, half), bf16), gr...  2.89 us
    pallas_call x1, Pallas kernels, local_kernels(): pl.pallas_call(functools.partial(middle_kernel, n, piece), out_shape=[sha...  1.8 us
    pallas_call x1, Pallas kernels, local_kernels(): pl.pallas_call(functools.partial(final_kernel, n), out_shape=[shape((colu...  1.59 us
  transfers between devices with their start and end apart: 15, of which 5 were waited for; matrix products, arithmetic and copies ran while one was open for 3% of the time, Pallas kernels for 8%

profile of v2, /device:TPU:0, one launch (start us, length us, event | category | flops | bytes accessed | tf_op | source)
XLA Modules:
  0.0 44.4 jit_solution(4388456040117259362)
XLA Ops:
  0.6 0.5 %collective-permute-start = (bf16[64,4096]{1,0:T(8,128)(2,1)}, bf16[64,4096]{1,0:T(8,128)(2,1)S(1)}, u32[]{:S(2)}, u32[]{:S(2)}) collective-permute-start(bf16[64,4096]{1,0:T(8,128)(2,1)} %x_mine.1), channel_id=1, source_target_pairs={{0,1},{1,0},{2,3},{3,2},{4,5},{5,4},{6,7},{7,6},{8,9},{9,8},{10,11... | collective-permute-start | bytes 1572872 | tf_op jit(solution)/shard_map/ppermute | solution.py:154
  1.1 0.8 %copy.14.chosen_ref = s32[8,2]{1,0:T(8,128)S(1)} copy(s32[8,2]{0,1:T(2,128)} %param.15) | data formatting | bytes 128 | tf_op args[6]
  1.9 0.0 copy-start.4
  1.9 0.9 %copy-done.4 = bf16[512,128]{1,0:T(8,128)(2,1)S(1)} copy-done((bf16[512,128]{1,0:T(8,128)(2,1)S(1)}, bf16[512,128]{1,0:T(8,128)(2,1)}, u32[]{:S(2)}) %copy-start.4) | copy-done | bytes 131096
  2.8 0.0 copy-start.5
  2.8 0.7 %copy-done.5 = bf16[16,512]{1,0:T(8,128)(2,1)S(1)} copy-done((bf16[16,512]{1,0:T(8,128)(2,1)S(1)}, bf16[16,512]{1,0:T(8,128)(2,1)}, u32[]{:S(2)}) %copy-start.5) | copy-done | bytes 16408
  3.5 0.0 copy-start.6
  3.5 0.7 %copy-done.6 = s32[8]{0:T(128)S(1)} copy-done((s32[8]{0:T(128)S(1)}, s32[8]{0:T(128)}, u32[]{:S(2)}) %copy-start.6) | copy-done | bytes 56
  4.2 0.8 %shard_map.112 = (bf16[48,512]{1,0:T(8,128)(2,1)S(1)}, bf16[48,512]{1,0:T(8,128)(2,1)S(1)}, bf16[48,512]{1,0:T(8,128)(2,1)S(1)}, bf16[48,512]{1,0:T(8,128)(2,1)S...) custom-call(s32[8,2]{1,0:T(8,128)S(1)} %copy.14.chosen_ref, ...), custom_call_target="tpu_custom_call" | custom-call | tf_op jit(solution)/shard_map/pallas_call | solution.py:156
  5.0 2.6 %collective-permute-start.1 = (bf16[48,512]{1,0:T(8,128)(2,1)S(1)}, bf16[48,512]{1,0:T(8,128)(2,1)S(1)}, u32[]{:S(2)}, u32[]{:S(2)}) collective-permute-start(bf16[48,512]{1,0:T(8,128)(2,1)S(1)} %get-tuple-element.24), channel_id=1, source_target_pairs={{0,2},{2,4},{4,6},{6,8},{8,10},{10,12},{12,14},{14,0},{1,3},{3,5},... | collective-permute-start | bytes 147464 | tf_op jit(solution)/shard_map/ppermute | solution.py:130
  7.6 1.6 %collective-permute-start.2 = (bf16[48,512]{1,0:T(8,128)(2,1)S(1)}, bf16[48,512]{1,0:T(8,128)(2,1)S(1)}, u32[]{:S(2)}, u32[]{:S(2)}) collective-permute-start(bf16[48,512]{1,0:T(8,128)(2,1)S(1)} %get-tuple-element.25), channel_id=1, source_target_pairs={{0,4},{2,6},{4,8},{6,10},{8,12},{10,14},{12,0},{14,2},{1,5},{3,7},... | collective-permute-start | bytes 147464 | tf_op jit(solution)/shard_map/ppermute | solution.py:130
  9.2 2.6 %collective-permute-start.3 = (bf16[48,512]{1,0:T(8,128)(2,1)S(1)}, bf16[48,512]{1,0:T(8,128)(2,1)S(1)}, u32[]{:S(2)}, u32[]{:S(2)}) collective-permute-start(bf16[48,512]{1,0:T(8,128)(2,1)S(1)} %get-tuple-element.26), channel_id=1, source_target_pairs={{0,6},{2,8},{4,10},{6,12},{8,14},{10,0},{12,2},{14,4},{1,7},{3,9},... | collective-permute-start | bytes 147464 | tf_op jit(solution)/shard_map/ppermute | solution.py:130
  11.7 1.2 %collective-permute-start.4 = (bf16[48,512]{1,0:T(8,128)(2,1)S(1)}, bf16[48,512]{1,0:T(8,128)(2,1)S(1)}, u32[]{:S(2)}, u32[]{:S(2)}) collective-permute-start(bf16[48,512]{1,0:T(8,128)(2,1)S(1)} %get-tuple-element.27), channel_id=1, source_target_pairs={{0,8},{2,10},{4,12},{6,14},{8,0},{10,2},{12,4},{14,6},{1,9},{3,11}... | collective-permute-start | bytes 147464 | tf_op jit(solution)/shard_map/ppermute | solution.py:130
  12.9 0.1 collective-permute-done.1.refs_1_
  13.0 2.6 %collective-permute-start.5 = (bf16[48,512]{1,0:T(8,128)(2,1)S(1)}, bf16[48,512]{1,0:T(8,128)(2,1)S(1)}, u32[]{:S(2)}, u32[]{:S(2)}) collective-permute-start(bf16[48,512]{1,0:T(8,128)(2,1)S(1)} %get-tuple-element.28), channel_id=1, source_target_pairs={{0,10},{2,12},{4,14},{6,0},{8,2},{10,4},{12,6},{14,8},{1,11},{3,13... | collective-permute-start | bytes 147464 | tf_op jit(solution)/shard_map/ppermute | solution.py:130
  15.6 0.0 collective-permute-done.2.refs_2_
  15.6 1.3 %collective-permute-start.6 = (bf16[48,512]{1,0:T(8,128)(2,1)S(1)}, bf16[48,512]{1,0:T(8,128)(2,1)S(1)}, u32[]{:S(2)}, u32[]{:S(2)}) collective-permute-start(bf16[48,512]{1,0:T(8,128)(2,1)S(1)} %get-tuple-element.29), channel_id=1, source_target_pairs={{0,12},{2,14},{4,0},{6,2},{8,4},{10,6},{12,8},{14,10},{1,13},{3,15... | collective-permute-start | bytes 147464 | tf_op jit(solution)/shard_map/ppermute | solution.py:130
  16.9 0.6 %collective-permute-done.3.refs_3_ = bf16[48,512]{1,0:T(8,128)(2,1)S(1)} collective-permute-done((bf16[48,512]{1,0:T(8,128)(2,1)S(1)}, bf16[48,512]{1,0:T(8,128)(2,1)S(1)}, u32[]{:S(2)}, u32[]{:S(2)}) %collective-permute-start.3) | collective-permute-done | bytes 49184 | tf_op jit(solution)/shard_map/ppermute | solution.py:130
  17.5 0.9 %collective-permute-start.7 = (bf16[48,512]{1,0:T(8,128)(2,1)S(1)}, bf16[48,512]{1,0:T(8,128)(2,1)S(1)}, u32[]{:S(2)}, u32[]{:S(2)}) collective-permute-start(bf16[48,512]{1,0:T(8,128)(2,1)S(1)} %get-tuple-element.30), channel_id=1, source_target_pairs={{0,14},{2,0},{4,2},{6,4},{8,6},{10,8},{12,10},{14,12},{1,15},{3,1}... | collective-permute-start | bytes 147464 | tf_op jit(solution)/shard_map/ppermute | solution.py:130
  18.4 0.8 %copy.13.start_ref = s32[8,2]{1,0:T(8,128)S(1)} copy(s32[8,2]{0,1:T(2,128)} %param.14) | data formatting | bytes 128 | tf_op args[5]
  19.1 0.0 collective-permute-done.4.refs_4_
  19.1 0.2 collective-permute-done.5.refs_5_
  19.3 1.3 %collective-permute-done.6.refs_6_ = bf16[48,512]{1,0:T(8,128)(2,1)S(1)} collective-permute-done((bf16[48,512]{1,0:T(8,128)(2,1)S(1)}, bf16[48,512]{1,0:T(8,128)(2,1)S(1)}, u32[]{:S(2)}, u32[]{:S(2)}) %collective-permute-start.6) | collective-permute-done | bytes 49184 | tf_op jit(solution)/shard_map/ppermute | solution.py:130
  20.6 0.9 %collective-permute-done.7.refs_7_ = bf16[48,512]{1,0:T(8,128)(2,1)S(1)} collective-permute-done((bf16[48,512]{1,0:T(8,128)(2,1)S(1)}, bf16[48,512]{1,0:T(8,128)(2,1)S(1)}, u32[]{:S(2)}, u32[]{:S(2)}) %collective-permute-start.7) | collective-permute-done | bytes 49184 | tf_op jit(solution)/shard_map/ppermute | solution.py:130
  21.6 0.0 collective-permute-done.x_other
  21.6 0.0 copy-start.1
  21.6 1.0 %copy-done.1 = bf16[64,4096]{1,0:T(8,128)(2,1)S(1)} copy-done((bf16[64,4096]{1,0:T(8,128)(2,1)S(1)}, bf16[64,4096]{1,0:T(8,128)(2,1)}, u32[]{:S(2)}) %copy-start.1) | copy-done | bytes 524312
  22.6 0.0 copy-start.2
  22.6 0.9 %copy-done.2 = bf16[128,512]{1,0:T(8,128)(2,1)S(1)} copy-done((bf16[128,512]{1,0:T(8,128)(2,1)S(1)}, bf16[128,512]{1,0:T(8,128)(2,1)}, u32[]{:S(2)}) %copy-start.2) | copy-done | bytes 131096
  23.5 0.0 copy-start.7
  23.5 0.7 %copy-done.7 = s32[8]{0:T(128)S(1)} copy-done((s32[8]{0:T(128)S(1)}, s32[8]{0:T(128)}, u32[]{:S(2)}) %copy-start.7) | copy-done | bytes 56
  24.2 0.0 copy-start.9
  24.2 0.7 %copy-done.9 = s32[8]{0:T(128)S(1)} copy-done((s32[8]{0:T(128)S(1)}, s32[8]{0:T(128)}, u32[]{:S(2)}) %copy-start.9) | copy-done | bytes 56
  24.8 0.0 copy-start.8
  24.9 1.8 %shard_map.113 = (bf16[128,32]{1,0:T(8,128)(2,1)S(1)}, bf16[8,32,512]{2,1,0:T(8,128)(2,1)S(1)}, bf16[80,256]{1,0:T(8,128)(2,1)S(1)}, bf16[80,256]{1,0:T(8,128)(2...) custom-call(s32[8,2]{1,0:T(8,128)S(1)} %copy.13.start_ref, ...), custom_call_target="tpu_custom_call" | custom-call | tf_op jit(solution)/shard_map/pallas_call | solution.py:166
  26.7 1.1 %collective-permute-start.8 = (bf16[80,256]{1,0:T(8,128)(2,1)S(1)}, bf16[80,256]{1,0:T(8,128)(2,1)S(1)}, u32[]{:S(2)}, u32[]{:S(2)}) collective-permute-start(bf16[80,256]{1,0:T(8,128)(2,1)S(1)} %get-tuple-element.34), channel_id=1, source_target_pairs={{0,2},{2,4},{4,6},{6,8},{8,10},{10,12},{12,14},{14,0},{1,3},{3,5},... | collective-permute-start | bytes 122888 | tf_op jit(solution)/shard_map/ppermute | solution.py:130
  27.8 1.3 %collective-permute-start.9 = (bf16[80,256]{1,0:T(8,128)(2,1)S(1)}, bf16[80,256]{1,0:T(8,128)(2,1)S(1)}, u32[]{:S(2)}, u32[]{:S(2)}) collective-permute-start(bf16[80,256]{1,0:T(8,128)(2,1)S(1)} %get-tuple-element.35), channel_id=1, source_target_pairs={{0,4},{2,6},{4,8},{6,10},{8,12},{10,14},{12,0},{14,2},{1,5},{3,7},... | collective-permute-start | bytes 122888 | tf_op jit(solution)/shard_map/ppermute | solution.py:130
  29.0 1.8 %collective-permute-start.10 = (bf16[80,256]{1,0:T(8,128)(2,1)S(1)}, bf16[80,256]{1,0:T(8,128)(2,1)S(1)}, u32[]{:S(2)}, u32[]{:S(2)}) collective-permute-start(bf16[80,256]{1,0:T(8,128)(2,1)S(1)} %get-tuple-element.36), channel_id=1, source_target_pairs={{0,6},{2,8},{4,10},{6,12},{8,14},{10,0},{12,2},{14,4},{1,7},{3,9},... | collective-permute-start | bytes 122888 | tf_op jit(solution)/shard_map/ppermute | solution.py:130
  30.9 1.2 %collective-permute-start.11 = (bf16[80,256]{1,0:T(8,128)(2,1)S(1)}, bf16[80,256]{1,0:T(8,128)(2,1)S(1)}, u32[]{:S(2)}, u32[]{:S(2)}) collective-permute-start(bf16[80,256]{1,0:T(8,128)(2,1)S(1)} %get-tuple-element.37), channel_id=1, source_target_pairs={{0,8},{2,10},{4,12},{6,14},{8,0},{10,2},{12,4},{14,6},{1,9},{3,11}... | collective-permute-start | bytes 122888 | tf_op jit(solution)/shard_map/ppermute | solution.py:130
  32.1 3.1 %collective-permute-start.12 = (bf16[80,256]{1,0:T(8,128)(2,1)S(1)}, bf16[80,256]{1,0:T(8,128)(2,1)S(1)}, u32[]{:S(2)}, u32[]{:S(2)}) collective-permute-start(bf16[80,256]{1,0:T(8,128)(2,1)S(1)} %get-tuple-element.38), channel_id=1, source_target_pairs={{0,10},{2,12},{4,14},{6,0},{8,2},{10,4},{12,6},{14,8},{1,11},{3,13... | collective-permute-start | bytes 122888 | tf_op jit(solution)/shard_map/ppermute | solution.py:130
  35.2 0.0 collective-permute-done.8.refs_1_
  35.2 0.4 collective-permute-start.13
  35.6 0.0 collective-permute-done.9.refs_2_
  35.6 1.2 %collective-permute-start.14 = (bf16[80,256]{1,0:T(8,128)(2,1)S(1)}, bf16[80,256]{1,0:T(8,128)(2,1)S(1)}, u32[]{:S(2)}, u32[]{:S(2)}) collective-permute-start(bf16[80,256]{1,0:T(8,128)(2,1)S(1)} %get-tuple-element.40), channel_id=1, source_target_pairs={{0,14},{2,0},{4,2},{6,4},{8,6},{10,8},{12,10},{14,12},{1,15},{3,1}... | collective-permute-start | bytes 122888 | tf_op jit(solution)/shard_map/ppermute | solution.py:130
  36.8 0.0 copy-start
  36.8 1.6 %copy-done = bf16[2048,512]{1,0:T(8,128)(2,1)S(1)} copy-done((bf16[2048,512]{1,0:T(8,128)(2,1)S(1)}, bf16[2048,512]{1,0:T(8,128)(2,1)}, u32[]{:S(2)}) %copy-start) | copy-done | bytes 2097176
  38.3 0.0 copy-start.3
  38.3 0.9 %copy-done.3 = bf16[128,512]{1,0:T(8,128)(2,1)S(1)} copy-done((bf16[128,512]{1,0:T(8,128)(2,1)S(1)}, bf16[128,512]{1,0:T(8,128)(2,1)}, u32[]{:S(2)}) %copy-start.3) | copy-done | bytes 131096
  39.3 0.0 copy-start.10
  39.3 0.7 %copy-done.10 = s32[8]{0:T(128)S(1)} copy-done((s32[8]{0:T(128)S(1)}, s32[8]{0:T(128)}, u32[]{:S(2)}) %copy-start.10) | copy-done | bytes 56
  39.9 2.9 %shard_map.114 = bf16[128,2048]{1,0:T(8,128)(2,1)} custom-call(s32[8]{0:T(128)S(1)} %copy-done.10, bf16[128,512]{1,0:T(8,128)(2,1)S(1)} %copy-done.3, bf16[2048,512]{1,0:T(8,128)(2,1)S(1)} %copy-done, bf16[128,32]{1,0:T(8,128)(2,1)S(1)} %get-tuple-element.31.dlow_ref, bf16[8,32,512]{2,1,0:T(8,128)(2,1)S(1)} %get-tuple-element.32.a_ref), custom_call_target="tpu_custom_call" | custom-call | flops 285212672 | bytes 2621440 | tf_op jit(solution)/shard_map/pallas_call | solution.py:193
  42.8 0.0 collective-permute-done.10.refs_3_
  42.8 0.0 collective-permute-done.11.refs_4_
  42.8 0.0 collective-permute-done.12.refs_5_
  42.8 0.0 collective-permute-done.13.refs_6_
  42.8 0.0 collective-permute-done.14.refs_7_
  42.8 0.0 copy-done.8
  42.8 1.6 %shard_map.115 = (f32[512,128]{1,0:T(8,128)}, f32[16,256]{1,0:T(8,128)}) custom-call(s32[8,2]{1,0:T(8,128)S(1)} %copy.14.chosen_ref, s32[8]{0:T(128)S(1)} %copy-done.8, bf16[80,256]{1,0:T(8,128)(2,1)S(1)} %get-tuple-element.33.refs_0_, bf16[80,256]{1,0:T(8,128)(2,1)S(1)} %collective-permute-done.8.refs_1_, ...), custom_call_target="tpu_custom_call" | custom-call | tf_op jit(solution)/shard_map/pallas_call | solution.py:213
Async XLA Ops:
  0.6 21.0 %collective-permute-start = (bf16[64,4096]{1,0:T(8,128)(2,1)}, bf16[64,4096]{1,0:T(8,128)(2,1)S(1)}, u32[]{:S(2)}, u32[]{:S(2)}) collective-permute-start(bf16[64,4096]{1,0:T(8,128)(2,1)} %x_mine.1), channel_id=1, source_target_pairs={{0,1},{1,0},{2,3},{3,2},{4,5},{5,4},{6,7},{7,6},{8,9},{9,8},{10,11... | collective-permute-start | bytes 1572872 | tf_op jit(solution)/shard_map/ppermute | solution.py:154
  1.9 0.9 %copy-start.4 = (bf16[512,128]{1,0:T(8,128)(2,1)S(1)}, bf16[512,128]{1,0:T(8,128)(2,1)}, u32[]{:S(2)}) copy-start(bf16[512,128]{1,0:T(8,128)(2,1)} %down_ref.1) | copy-start | bytes 393220
  2.8 0.7 %copy-start.5 = (bf16[16,512]{1,0:T(8,128)(2,1)S(1)}, bf16[16,512]{1,0:T(8,128)(2,1)}, u32[]{:S(2)}) copy-start(bf16[16,512]{1,0:T(8,128)(2,1)} %up_ref.1) | copy-start | bytes 49156
  3.5 0.7 %copy-start.6 = (s32[8]{0:T(128)S(1)}, s32[8]{0:T(128)}, u32[]{:S(2)}) copy-start(s32[8]{0:T(128)} %slot_ref.5) | copy-start | bytes 100
  5.0 8.0 %collective-permute-start.1 = (bf16[48,512]{1,0:T(8,128)(2,1)S(1)}, bf16[48,512]{1,0:T(8,128)(2,1)S(1)}, u32[]{:S(2)}, u32[]{:S(2)}) collective-permute-start(bf16[48,512]{1,0:T(8,128)(2,1)S(1)} %get-tuple-element.24), channel_id=1, source_target_pairs={{0,2},{2,4},{4,6},{6,8},{8,10},{10,12},{12,14},{14,0},{1,3},{3,5},... | collective-permute-start | bytes 147464 | tf_op jit(solution)/shard_map/ppermute | solution.py:130
  7.6 8.0 %collective-permute-start.2 = (bf16[48,512]{1,0:T(8,128)(2,1)S(1)}, bf16[48,512]{1,0:T(8,128)(2,1)S(1)}, u32[]{:S(2)}, u32[]{:S(2)}) collective-permute-start(bf16[48,512]{1,0:T(8,128)(2,1)S(1)} %get-tuple-element.25), channel_id=1, source_target_pairs={{0,4},{2,6},{4,8},{6,10},{8,12},{10,14},{12,0},{14,2},{1,5},{3,7},... | collective-permute-start | bytes 147464 | tf_op jit(solution)/shard_map/ppermute | solution.py:130
  9.2 8.3 %collective-permute-start.3 = (bf16[48,512]{1,0:T(8,128)(2,1)S(1)}, bf16[48,512]{1,0:T(8,128)(2,1)S(1)}, u32[]{:S(2)}, u32[]{:S(2)}) collective-permute-start(bf16[48,512]{1,0:T(8,128)(2,1)S(1)} %get-tuple-element.26), channel_id=1, source_target_pairs={{0,6},{2,8},{4,10},{6,12},{8,14},{10,0},{12,2},{14,4},{1,7},{3,9},... | collective-permute-start | bytes 147464 | tf_op jit(solution)/shard_map/ppermute | solution.py:130
  11.7 7.4 %collective-permute-start.4 = (bf16[48,512]{1,0:T(8,128)(2,1)S(1)}, bf16[48,512]{1,0:T(8,128)(2,1)S(1)}, u32[]{:S(2)}, u32[]{:S(2)}) collective-permute-start(bf16[48,512]{1,0:T(8,128)(2,1)S(1)} %get-tuple-element.27), channel_id=1, source_target_pairs={{0,8},{2,10},{4,12},{6,14},{8,0},{10,2},{12,4},{14,6},{1,9},{3,11}... | collective-permute-start | bytes 147464 | tf_op jit(solution)/shard_map/ppermute | solution.py:130
  13.0 6.3 %collective-permute-start.5 = (bf16[48,512]{1,0:T(8,128)(2,1)S(1)}, bf16[48,512]{1,0:T(8,128)(2,1)S(1)}, u32[]{:S(2)}, u32[]{:S(2)}) collective-permute-start(bf16[48,512]{1,0:T(8,128)(2,1)S(1)} %get-tuple-element.28), channel_id=1, source_target_pairs={{0,10},{2,12},{4,14},{6,0},{8,2},{10,4},{12,6},{14,8},{1,11},{3,13... | collective-permute-start | bytes 147464 | tf_op jit(solution)/shard_map/ppermute | solution.py:130
  15.6 5.1 %collective-permute-start.6 = (bf16[48,512]{1,0:T(8,128)(2,1)S(1)}, bf16[48,512]{1,0:T(8,128)(2,1)S(1)}, u32[]{:S(2)}, u32[]{:S(2)}) collective-permute-start(bf16[48,512]{1,0:T(8,128)(2,1)S(1)} %get-tuple-element.29), channel_id=1, source_target_pairs={{0,12},{2,14},{4,0},{6,2},{8,4},{10,6},{12,8},{14,10},{1,13},{3,15... | collective-permute-start | bytes 147464 | tf_op jit(solution)/shard_map/ppermute | solution.py:130
  17.5 4.1 %collective-permute-start.7 = (bf16[48,512]{1,0:T(8,128)(2,1)S(1)}, bf16[48,512]{1,0:T(8,128)(2,1)S(1)}, u32[]{:S(2)}, u32[]{:S(2)}) collective-permute-start(bf16[48,512]{1,0:T(8,128)(2,1)S(1)} %get-tuple-element.30), channel_id=1, source_target_pairs={{0,14},{2,0},{4,2},{6,4},{8,6},{10,8},{12,10},{14,12},{1,15},{3,1}... | collective-permute-start | bytes 147464 | tf_op jit(solution)/shard_map/ppermute | solution.py:130
  21.6 1.0 %copy-start.1 = (bf16[64,4096]{1,0:T(8,128)(2,1)S(1)}, bf16[64,4096]{1,0:T(8,128)(2,1)}, u32[]{:S(2)}) copy-start(bf16[64,4096]{1,0:T(8,128)(2,1)} %x_mine.1) | copy-start | bytes 1572868
  22.6 0.9 %copy-start.2 = (bf16[128,512]{1,0:T(8,128)(2,1)S(1)}, bf16[128,512]{1,0:T(8,128)(2,1)}, u32[]{:S(2)}) copy-start(bf16[128,512]{1,0:T(8,128)(2,1)} %g_ref.3) | copy-start | bytes 393220
  23.5 0.7 %copy-start.7 = (s32[8]{0:T(128)S(1)}, s32[8]{0:T(128)}, u32[]{:S(2)}) copy-start(s32[8]{0:T(128)} %slot_ref.5) | copy-start | bytes 100
  24.2 0.7 %copy-start.9 = (s32[8]{0:T(128)S(1)}, s32[8]{0:T(128)}, u32[]{:S(2)}) copy-start(s32[8]{0:T(128)} %count_ref.3) | copy-start | bytes 100
  24.8 18.0 %copy-start.8 = (s32[8]{0:T(128)S(1)}, s32[8]{0:T(128)}, u32[]{:S(2)}) copy-start(s32[8]{0:T(128)} %slot_ref.5) | copy-start | bytes 100
  26.7 8.6 %collective-permute-start.8 = (bf16[80,256]{1,0:T(8,128)(2,1)S(1)}, bf16[80,256]{1,0:T(8,128)(2,1)S(1)}, u32[]{:S(2)}, u32[]{:S(2)}) collective-permute-start(bf16[80,256]{1,0:T(8,128)(2,1)S(1)} %get-tuple-element.34), channel_id=1, source_target_pairs={{0,2},{2,4},{4,6},{6,8},{8,10},{10,12},{12,14},{14,0},{1,3},{3,5},... | collective-permute-start | bytes 122888 | tf_op jit(solution)/shard_map/ppermute | solution.py:130
  27.8 7.8 %collective-permute-start.9 = (bf16[80,256]{1,0:T(8,128)(2,1)S(1)}, bf16[80,256]{1,0:T(8,128)(2,1)S(1)}, u32[]{:S(2)}, u32[]{:S(2)}) collective-permute-start(bf16[80,256]{1,0:T(8,128)(2,1)S(1)} %get-tuple-element.35), channel_id=1, source_target_pairs={{0,4},{2,6},{4,8},{6,10},{8,12},{10,14},{12,0},{14,2},{1,5},{3,7},... | collective-permute-start | bytes 122888 | tf_op jit(solution)/shard_map/ppermute | solution.py:130
  29.0 13.8 %collective-permute-start.10 = (bf16[80,256]{1,0:T(8,128)(2,1)S(1)}, bf16[80,256]{1,0:T(8,128)(2,1)S(1)}, u32[]{:S(2)}, u32[]{:S(2)}) collective-permute-start(bf16[80,256]{1,0:T(8,128)(2,1)S(1)} %get-tuple-element.36), channel_id=1, source_target_pairs={{0,6},{2,8},{4,10},{6,12},{8,14},{10,0},{12,2},{14,4},{1,7},{3,9},... | collective-permute-start | bytes 122888 | tf_op jit(solution)/shard_map/ppermute | solution.py:130
  30.9 11.9 %collective-permute-start.11 = (bf16[80,256]{1,0:T(8,128)(2,1)S(1)}, bf16[80,256]{1,0:T(8,128)(2,1)S(1)}, u32[]{:S(2)}, u32[]{:S(2)}) collective-permute-start(bf16[80,256]{1,0:T(8,128)(2,1)S(1)} %get-tuple-element.37), channel_id=1, source_target_pairs={{0,8},{2,10},{4,12},{6,14},{8,0},{10,2},{12,4},{14,6},{1,9},{3,11}... | collective-permute-start | bytes 122888 | tf_op jit(solution)/shard_map/ppermute | solution.py:130
  32.1 10.7 %collective-permute-start.12 = (bf16[80,256]{1,0:T(8,128)(2,1)S(1)}, bf16[80,256]{1,0:T(8,128)(2,1)S(1)}, u32[]{:S(2)}, u32[]{:S(2)}) collective-permute-start(bf16[80,256]{1,0:T(8,128)(2,1)S(1)} %get-tuple-element.38), channel_id=1, source_target_pairs={{0,10},{2,12},{4,14},{6,0},{8,2},{10,4},{12,6},{14,8},{1,11},{3,13... | collective-permute-start | bytes 122888 | tf_op jit(solution)/shard_map/ppermute | solution.py:130
  35.2 7.6 %collective-permute-start.13 = (bf16[80,256]{1,0:T(8,128)(2,1)S(1)}, bf16[80,256]{1,0:T(8,128)(2,1)S(1)}, u32[]{:S(2)}, u32[]{:S(2)}) collective-permute-start(bf16[80,256]{1,0:T(8,128)(2,1)S(1)} %get-tuple-element.39), channel_id=1, source_target_pairs={{0,12},{2,14},{4,0},{6,2},{8,4},{10,6},{12,8},{14,10},{1,13},{3,15... | collective-permute-start | bytes 122888 | tf_op jit(solution)/shard_map/ppermute | solution.py:130
  35.6 7.2 %collective-permute-start.14 = (bf16[80,256]{1,0:T(8,128)(2,1)S(1)}, bf16[80,256]{1,0:T(8,128)(2,1)S(1)}, u32[]{:S(2)}, u32[]{:S(2)}) collective-permute-start(bf16[80,256]{1,0:T(8,128)(2,1)S(1)} %get-tuple-element.40), channel_id=1, source_target_pairs={{0,14},{2,0},{4,2},{6,4},{8,6},{10,8},{12,10},{14,12},{1,15},{3,1}... | collective-permute-start | bytes 122888 | tf_op jit(solution)/shard_map/ppermute | solution.py:130
  36.8 1.6 %copy-start = (bf16[2048,512]{1,0:T(8,128)(2,1)S(1)}, bf16[2048,512]{1,0:T(8,128)(2,1)}, u32[]{:S(2)}) copy-start(bf16[2048,512]{1,0:T(8,128)(2,1)} %w_ref.1) | copy-start | bytes 6291460
  38.3 0.9 %copy-start.3 = (bf16[128,512]{1,0:T(8,128)(2,1)S(1)}, bf16[128,512]{1,0:T(8,128)(2,1)}, u32[]{:S(2)}) copy-start(bf16[128,512]{1,0:T(8,128)(2,1)} %g_ref.3) | copy-start | bytes 393220
  39.3 0.7 %copy-start.10 = (s32[8]{0:T(128)S(1)}, s32[8]{0:T(128)}, u32[]{:S(2)}) copy-start(s32[8]{0:T(128)} %count_ref.3) | copy-start | bytes 100

commit v3 on v2

v3 whole, which is shorter than its diff:
```python
import functools

import jax
import jax.numpy as jnp
from jax import lax
from jax.experimental import pallas as pl
from jax.experimental.pallas import tpu as pltpu
from jax.sharding import PartitionSpec as P

ADAPTER_RANK = 16
adapter_scale = 2.0

bf16, f32, i32 = jnp.bfloat16, jnp.float32, jnp.int32

HBM = pl.BlockSpec(memory_space=pltpu.HBM)
VMEM = pl.BlockSpec(memory_space=pltpu.VMEM)


def dot(a, b, ca, cb):
    return lax.dot_general(a, b, (((ca,), (cb,)), ((), ())), preferred_element_type=f32)


def params(mib):
    return pltpu.CompilerParams(vmem_limit_bytes=mib << 20)


def slot_rows(chosen_ref, slot_ref, ranks, width):
    lane = lax.broadcasted_iota(i32, (ADAPTER_RANK, width), 1)
    row = lax.broadcasted_iota(i32, (ADAPTER_RANK, width), 0)
    rows = []
    for rank in ranks:
        for k in range(chosen_ref.shape[0]):
            first = slot_ref[chosen_ref[k, rank]] * ADAPTER_RANK
            rows.append(jnp.where(lane == row + first, 1.0, 0.0))
    return jnp.concatenate(rows, axis=0).astype(bf16)


def fetch(sources, targets, sems):
    copies = [
        pltpu.make_async_copy(source, target, sems.at[k])
        for k, (source, target) in enumerate(zip(sources, targets))
    ]
    for copy in copies:
        copy.start()
    for copy in copies:
        copy.wait()


def pairs(n, core):
    return [n - 1 - 2 * j - core for j in range(n // 2 - 1)]


def partners(n, me, core):
    steps = [jnp.where(core == 0, a, b) for a, b in zip(pairs(n, 0), pairs(n, 1))]
    return [me] + [me ^ d for d in steps] + [me ^ 1]


def senders(n, me, core):
    return partners(n, me, core) + partners(n, me, 1 - core)[1:-1]


def pack_kernel(n, chosen_hbm, slot_hbm, down_hbm, up_hbm, *refs):
    count = n // 2 + 1
    send, (chosen_ref, slot_ref, down_ref, up_ref, sems) = refs[:count], refs[count:]
    fetch([chosen_hbm, slot_hbm, down_hbm, up_hbm], [chosen_ref, slot_ref, down_ref, up_ref], sems)
    ranks = partners(n, lax.axis_index("dp"), lax.axis_index("tensor"))
    onehot = slot_rows(chosen_ref, slot_ref, ranks, down_ref.shape[1])
    picked = onehot.shape[0] // count
    columns = dot(onehot, down_ref[...], 1, 1).astype(bf16)
    for k in range(count):
        send[k][:picked, :] = columns[k * picked : (k + 1) * picked]
        send[k][picked:, :] = up_ref[...]


def stage_kernel(
    n, start_hbm, chosen_hbm, slot_hbm, count_hbm, g_hbm, x_mine, x_other,
    x_ref, g_ref, seg_ref, own_ref, all_ref,
    start_ref, chosen_ref, slot_ref, count_ref, sems,
):
    me, core = lax.axis_index("dp"), lax.axis_index("tensor")
    half = x_mine.shape[0]
    rows, picked = seg_ref.shape
    mine = pl.ds(pl.multiple_of(core * half, half), half)
    other = pl.ds(pl.multiple_of((1 - core) * half, half), half)
    fetch(
        [start_hbm, chosen_hbm, slot_hbm, count_hbm, g_hbm, x_mine, x_other],
        [start_ref, chosen_ref, slot_ref, count_ref, g_ref, x_ref.at[mine], x_ref.at[other]],
        sems,
    )
    position = lax.broadcasted_iota(i32, (rows, picked), 0)
    group = lax.broadcasted_iota(i32, (rows, picked), 1) // ADAPTER_RANK
    segment = jnp.full((rows, picked), -1, i32)
    for k in range(start_ref.shape[0]):
        segment += jnp.where(position >= start_ref[k, me], 1, 0)
    seg_ref[...] = jnp.where(segment == group, 1.0, 0.0)
    live = lax.broadcasted_iota(i32, g_ref.shape, 0) < count_ref[me]
    g_ref[...] = jnp.where(live, g_ref[...], jnp.zeros(g_ref.shape, bf16))
    own_ref[...] = slot_rows(chosen_ref, slot_ref, [me], own_ref.shape[1])
    all_ref[...] = slot_rows(chosen_ref, slot_ref, range(n), all_ref.shape[1])


def middle_kernel(n, x_ref, g_ref, seg_ref, own_ref, *refs):
    got, (dlow_ref, a_ref), send = refs[:n], refs[n : n + 2], refs[n + 2 : n + 3 + n // 2]
    b_ref, up_ref = refs[n + 3 + n // 2 :]
    me, core = lax.axis_index("dp"), lax.axis_index("tensor")
    rows, picked = seg_ref.shape
    width = got[0].shape[1]
    for sender, message in zip(senders(n, me, core), got):
        a_ref[sender] = message[:picked, :]
        b_ref[sender] = message[picked:, :]

    in_seg = seg_ref[...] > 0.0
    b_sel = dot(own_ref[...], b_ref[...].reshape(-1, width), 1, 0).astype(bf16)
    dlow = jnp.where(in_seg, adapter_scale * dot(g_ref[...], b_sel, 1, 1), 0.0).astype(bf16)
    dlow_ref[...] = dlow
    targets = partners(n, me, core)
    for target, message in zip(targets, send):
        at = pl.ds(pl.multiple_of(target * width, width), width)
        message[:picked, :] = dot(dlow, x_ref[:, at], 0, 0).astype(bf16)

    low = jnp.zeros((rows, picked), f32)
    for q in range(n):
        low += dot(x_ref[:, q * width : (q + 1) * width], a_ref[q], 1, 1)
    low = jnp.where(in_seg, low, 0.0).astype(bf16)
    low_wide = dot(low, own_ref[...], 1, 0).astype(bf16)
    up = (adapter_scale * dot(low_wide, g_ref[...], 0, 0)).astype(bf16)
    up_ref[...] = up.reshape(up_ref.shape)
    for target, message in zip(targets, send):
        message[picked:, :] = up_ref[target]


def grad_x_kernel(g_ref, w_ref, dlow_ref, a_ref, out_ref):
    block = lax.axis_index("tensor") * pl.num_programs(0) + pl.program_id(0)
    total = dot(g_ref[...], w_ref[...], 1, 1) + dot(dlow_ref[...], a_ref[block], 1, 0)
    out_ref[...] = total.astype(bf16)


def final_kernel(n, all_ref, *refs):
    got, (a_ref, up_ref, rows_ref) = refs[:n], refs[n:]
    me, core = lax.axis_index("dp"), lax.axis_index("tensor")
    piece = up_ref.shape[1]
    picked = all_ref.shape[0] // n
    for sender, message in zip(senders(n, me, core), got):
        rows_ref[sender] = message[...]
    rows = rows_ref[:, :picked, :].reshape(n * picked, rows_ref.shape[2])
    a_ref[...] = dot(rows, all_ref[...], 0, 0)
    at = pl.ds(pl.multiple_of(core * piece, piece), piece)
    up_ref[...] = jnp.sum(rows_ref[:, picked:, at].astype(f32), axis=0)


def exchange(messages):
    n = 2 * (len(messages) - 1)
    steps = list(zip(pairs(n, 0), pairs(n, 1))) + [(1, 1)]
    got = [
        lax.ppermute(
            message,
            ("dp", "tensor"),
            [(2 * i + c, 2 * (i ^ step[c]) + c) for i in range(n) for c in range(2)],
        )
        for message, step in zip(messages[1:], steps)
    ]
    passed = [lax.ppermute(message, "tensor", [(0, 1), (1, 0)]) for message in got[:-1]]
    return [messages[0]] + got + passed


def local_kernels(
    inputs,
    output_gradient,
    frozen_weight,
    down_maps,
    up_maps,
    segment_start,
    segment_adapter,
    adapter_slot,
    token_count,
):
    model_width = inputs.shape[1]
    tok_rows, out_width = output_gradient.shape
    column_total, slot_width = down_maps.shape
    half = frozen_weight.shape[0]
    n = lax.axis_size("dp")
    piece = out_width // lax.axis_size("tensor")
    segs = segment_start.shape[1]
    picked = segs * ADAPTER_RANK
    shape = jax.ShapeDtypeStruct
    message = shape((picked + ADAPTER_RANK, column_total), bf16)
    count = n // 2 + 1
    starts, chosen = segment_start.T, segment_adapter.T

    sent = pl.pallas_call(
        functools.partial(pack_kernel, n),
        out_shape=[message] * count,
        in_specs=[HBM] * 4,
        out_specs=[VMEM] * count,
        scratch_shapes=[
            pltpu.SMEM(chosen.shape, i32),
            pltpu.SMEM(adapter_slot.shape, i32),
            pltpu.VMEM(down_maps.shape, bf16),
            pltpu.VMEM(up_maps.shape, bf16),
            pltpu.SemaphoreType.DMA((4,)),
        ],
        compiler_params=params(8),
    )(chosen, adapter_slot, down_maps, up_maps)
    x_other = lax.ppermute(inputs, "tensor", [(0, 1), (1, 0)])
    got = exchange(sent)

    x, g, in_seg, own_rows, all_rows = pl.pallas_call(
        functools.partial(stage_kernel, n),
        out_shape=[
            shape((tok_rows, model_width), bf16),
            shape((tok_rows, out_width), bf16),
            shape((tok_rows, picked), f32),
            shape((picked, slot_width), bf16),
            shape((n * picked, slot_width), bf16),
        ],
        in_specs=[HBM] * 6 + [pl.BlockSpec(memory_space=pl.ANY)],
        out_specs=[VMEM] * 5,
        scratch_shapes=[
            pltpu.SMEM(starts.shape, i32),
            pltpu.SMEM(chosen.shape, i32),
            pltpu.SMEM(adapter_slot.shape, i32),
            pltpu.SMEM(token_count.shape, i32),
            pltpu.SemaphoreType.DMA((7,)),
        ],
        compiler_params=params(8),
        cost_estimate=pl.CostEstimate(flops=0, bytes_accessed=1 << 22, transcendentals=0),
    )(starts, chosen, adapter_slot, token_count, output_gradient, inputs, x_other)

    dlow, a_all, *sent = pl.pallas_call(
        functools.partial(middle_kernel, n),
        out_shape=[shape((tok_rows, picked), bf16), shape((n, picked, column_total), bf16)]
        + [message] * count,
        in_specs=[VMEM] * (4 + n),
        out_specs=[VMEM] * (2 + count),
        scratch_shapes=[
            pltpu.VMEM((n, ADAPTER_RANK, out_width), bf16),
            pltpu.VMEM((n, ADAPTER_RANK, out_width), bf16),
        ],
        compiler_params=params(8),
    )(x, g, in_seg, own_rows, *got)
    got = exchange(sent)

    grad_x = pl.pallas_call(
        grad_x_kernel,
        out_shape=shape((tok_rows, half), bf16),
        grid=(half // column_total,),
        in_specs=[
            pl.BlockSpec((tok_rows, out_width), lambda j: (0, 0)),
            pl.BlockSpec((column_total, out_width), lambda j: (j, 0)),
            pl.BlockSpec((tok_rows, picked), lambda j: (0, 0)),
            pl.BlockSpec((n, picked, column_total), lambda j: (0, 0, 0)),
        ],
        out_specs=pl.BlockSpec((tok_rows, column_total), lambda j: (0, j)),
        compiler_params=params(8),
        cost_estimate=pl.CostEstimate(
            flops=2 * tok_rows * half * (out_width + picked),
            bytes_accessed=2 * half * (out_width + tok_rows),
            transcendentals=0,
        ),
    )(g, frozen_weight, dlow, a_all)

    grad_a, up_map_gradient = pl.pallas_call(
        functools.partial(final_kernel, n),
        out_shape=[shape((column_total, slot_width), f32), shape((ADAPTER_RANK, piece), f32)],
        in_specs=[VMEM] * (1 + n),
        out_specs=[VMEM, VMEM],
        scratch_shapes=[pltpu.VMEM((n,) + message.shape, bf16)],
        compiler_params=params(8),
    )(all_rows, *got)
    return grad_x, grad_a, up_map_gradient


def local_plain(
    inputs,
    output_gradient,
    frozen_weight,
    down_maps,
    up_maps,
    segment_start,
    segment_adapter,
    adapter_slot,
    token_count,
):
    tok_rows, out_width = output_gradient.shape
    column_total = down_maps.shape[0]
    adapter_list = adapter_slot.shape[0]
    segs = segment_start.shape[1]
    dp_size = lax.axis_size("dp")
    my_rank = lax.axis_index("dp")
    core_idx = lax.axis_index("tensor")
    picked = segs * ADAPTER_RANK
    piece_out = out_width // lax.axis_size("tensor")
    half = frozen_weight.shape[0]

    x_other = lax.ppermute(inputs, "tensor", [(0, 1), (1, 0)])
    adapter_ids = jnp.arange(adapter_list, dtype=i32)
    slot_table = jnp.sum(
        jnp.where(segment_adapter[..., None] == adapter_ids, adapter_slot, 0), axis=-1
    )
    column = slot_table[:, :, None] * ADAPTER_RANK + jnp.arange(ADAPTER_RANK, dtype=i32)
    onehot = (
        column.reshape(-1)[:, None] == jnp.arange(adapter_list * ADAPTER_RANK, dtype=i32)
    ).astype(bf16)

    a_send = dot(onehot, down_maps, 1, 1).astype(bf16).reshape(dp_size, picked, column_total)
    b_send = jnp.broadcast_to(up_maps[None], (dp_size,) + up_maps.shape)
    a_got = lax.all_to_all(a_send, "dp", 0, 0, tiled=True)
    b_got = lax.all_to_all(b_send, "dp", 0, 0, tiled=True)

    position = jnp.arange(tok_rows, dtype=i32)
    starts = lax.dynamic_index_in_dim(segment_start, my_rank, 0, keepdims=False)
    live = position < lax.dynamic_index_in_dim(token_count, my_rank, 0, keepdims=False)
    my_seg = jnp.sum((starts[None, :] <= position[:, None]).astype(i32), axis=1) - 1
    in_seg = my_seg[:, None] == (jnp.arange(picked, dtype=i32) // ADAPTER_RANK)[None, :]
    my_onehot = lax.dynamic_slice_in_dim(onehot, my_rank * picked, picked, 0)
    g = jnp.where(live[:, None], output_gradient, jnp.zeros_like(output_gradient))
    base = dot(g, frozen_weight, 1, 1)

    b_sel = dot(my_onehot, b_got.reshape(-1, out_width), 1, 0).astype(bf16)
    dlow = (adapter_scale * dot(g, b_sel, 1, 1)).astype(bf16)
    dlow = jnp.where(in_seg, dlow, jnp.zeros_like(dlow))
    a_sel = jnp.moveaxis(a_got, 0, 1).reshape(picked, -1)
    first = core_idx == 0
    x = jnp.concatenate(
        [jnp.where(first, inputs, x_other), jnp.where(first, x_other, inputs)], axis=0
    )
    low = dot(x, a_sel, 1, 1).astype(bf16)
    low = jnp.where(in_seg, low, jnp.zeros_like(low))
    low_wide = dot(low, my_onehot, 1, 0).astype(bf16)

    ga_send = dot(dlow, x, 0, 0).astype(bf16).reshape(picked, dp_size, column_total)
    ga_got = lax.all_to_all(jnp.moveaxis(ga_send, 1, 0), "dp", 0, 0, tiled=True)
    g_piece = lax.dynamic_slice_in_dim(g, core_idx * piece_out, piece_out, 1)
    up_send = (adapter_scale * dot(low_wide, g_piece, 0, 0)).astype(bf16)
    up_got = lax.all_to_all(up_send.reshape(dp_size, -1, piece_out), "dp", 0, 0, tiled=True)

    a_half = lax.dynamic_slice_in_dim(a_sel, core_idx * half, half, 1)
    grad_x = (base + dot(dlow, a_half, 1, 0)).astype(bf16)
    grad_a = dot(ga_got.reshape(dp_size * picked, column_total), onehot, 0, 0)
    up_map_gradient = jnp.sum(up_got.astype(f32), axis=0)
    return grad_x, grad_a, up_map_gradient


def local(*args):
    down_maps, up_maps = args[3], args[4]
    n, tp = lax.axis_size("dp"), lax.axis_size("tensor")
    out_width = up_maps.shape[1]
    kernels_fit = (
        n in (4, 8, 16)
        and tp == 2
        and down_maps.shape[0] == out_width
        and down_maps.shape[1] == n * up_maps.shape[0]
        and out_width % (128 * tp) == 0
    )
    return (local_kernels if kernels_fit else local_plain)(*args)


def solution(mesh):
    in_specs = (
        P(("groups", "dp", "tensor"), None),
        P(("groups", "dp"), None),
        P("tensor", None),
        P(("groups", "dp"), None),
        P(("groups", "dp"), None),
        P("groups", None),
        P("groups", None),
        P("groups"),
        P("groups"),
    )
    out_specs = (
        P(("groups", "dp"), "tensor"),
        P(("groups", "dp"), None),
        P(("groups", "dp"), "tensor"),
    )
    return jax.shard_map(local, mesh=mesh, in_specs=in_specs, out_specs=out_specs, check_vma=False)
```

time: 44.8 us -> 35.9 us (0.80)
  starting transfers between devices: 23.3 us -> 15.8 us
  local copies, waits for them, and re-layouts: 10.2 us -> 7.67 us
  waiting for transfers between devices: 3.14 us -> 5.31 us
  Pallas kernels: 7.11 us -> 6.05 us
    ppermute x14, starting transfers between devices: 22.8 us -> 15.3 us  [the longest x8 14.6 us: exchange(): lax.ppermute(message, ('dp', 'tensor'), [(2 * i + c, 2 * (i ^ step[c]) +...]
    unnamed x24 -> x22, local copies, waits for them, and re-layouts: 10.2 us -> 7.67 us
    ppermute x14, waiting for transfers between devices: 3.13 us -> 5.31 us  [the longest x8 5.29 us: exchange(): lax.ppermute(message, ('dp', 'tensor'), [(2 * i + c, 2 * (i ^ step[c]) +...]
    pallas_call x1, Pallas kernels: 2.89 us -> 2.31 us  [local_kernels(): pl.pallas_call(grad_x_kernel, out_shape=shape((tok_rows, half), bf16), gr...]
    pallas_call x1, Pallas kernels: 1.59 us -> 1.02 us  [local_kernels(): pl.pallas_call(functools.partial(final_kernel, n), out_shape=[shape((colu...]
    pallas_call x2 -> x3, Pallas kernels: 2.63 us -> 2.73 us  [the longest x1 1.25 us: local_kernels(): pl.pallas_call(functools.partial(middle_kernel, n), out_shape=[shape((tok...]
  transfers between devices with their start and end apart: 15 -> 15, of which waited for: 5 -> 5; matrix products, arithmetic and copies ran while one was open for 3% -> 0% of each run, Pallas kernels for 8% -> 11%
where the time goes in v3:
time: 35.9 us; the launch traced here: 35.6 us
  starting transfers between devices  15.8 us (44%)
  local copies, waits for them, and re-layouts  7.67 us (21%)
  Pallas kernels  6.05 us (17%)
  waiting for transfers between devices  5.31 us (15%)
  between operations  0.73 us (2%)
    ppermute x8, starting transfers between devices, exchange(): lax.ppermute(message, ('dp', 'tensor'), [(2 * i + c, 2 * (i ^ step[c]) +...  14.6 us
    unnamed x22, local copies, waits for them, and re-layouts  7.67 us
    ppermute x8, waiting for transfers between devices, exchange(): lax.ppermute(message, ('dp', 'tensor'), [(2 * i + c, 2 * (i ^ step[c]) +...  5.29 us
    pallas_call x1, Pallas kernels, local_kernels(): pl.pallas_call(grad_x_kernel, out_shape=shape((tok_rows, half), bf16), gr...  2.31 us
    pallas_call x1, Pallas kernels, local_kernels(): pl.pallas_call(functools.partial(middle_kernel, n), out_shape=[shape((tok...  1.25 us
    pallas_call x1, Pallas kernels, local_kernels(): pl.pallas_call(functools.partial(final_kernel, n), out_shape=[shape((colu...  1.02 us
    pallas_call x1, Pallas kernels, local_kernels(): pl.pallas_call(functools.partial(pack_kernel, n), out_shape=[message] * c...  0.79 us
    ppermute x6, starting transfers between devices, exchange(): lax.ppermute(message, 'tensor', [(0, 1), (1, 0)])  0.72 us
  transfers between devices with their start and end apart: 15, of which 5 were waited for; matrix products, arithmetic and copies ran while one was open for 0% of the time, Pallas kernels for 11%

profile of v3, /device:TPU:0, one launch (start us, length us, event | category | flops | bytes accessed | tf_op | source)
XLA Modules:
  0.0 35.6 jit_solution(14467906997923832037)
XLA Ops:
  0.6 0.0 copy-start
  0.6 0.5 %collective-permute-start = (bf16[64,4096]{1,0:T(8,128)(2,1)}, bf16[64,4096]{1,0:T(8,128)(2,1)S(1)}, u32[]{:S(2)}, u32[]{:S(2)}) collective-permute-start(bf16[64,4096]{1,0:T(8,128)(2,1)} %x_mine.1), channel_id=1, source_target_pairs={{0,1},{1,0},{2,3},{3,2},{4,5},{5,4},{6,7},{7,6},{8,9},{9,8},{10,11... | collective-permute-start | bytes 1572872 | tf_op jit(solution)/shard_map/ppermute | solution.py:204
  1.2 0.0 copy-start.2
  1.2 1.0 %copy-done.2 = bf16[512,128]{1,0:T(8,128)(2,1)S(1)} copy-done((bf16[512,128]{1,0:T(8,128)(2,1)S(1)}, bf16[512,128]{1,0:T(8,128)(2,1)}, u32[]{:S(2)}) %copy-start.2) | copy-done | bytes 131096
  2.2 0.0 copy-start.4
  2.2 0.7 %copy-done.4 = bf16[16,512]{1,0:T(8,128)(2,1)S(1)} copy-done((bf16[16,512]{1,0:T(8,128)(2,1)S(1)}, bf16[16,512]{1,0:T(8,128)(2,1)}, u32[]{:S(2)}) %copy-start.4) | copy-done | bytes 16408
  2.9 0.0 copy-start.5
  2.9 0.7 %copy-done.5 = s32[8,2]{0,1:T(2,128)S(1)} copy-done((s32[8,2]{0,1:T(2,128)S(1)}, s32[8,2]{0,1:T(2,128)}, u32[]{:S(2)}) %copy-start.5) | copy-done | bytes 88
  3.6 0.0 copy-start.7
  3.6 0.7 %copy-done.7 = s32[8]{0:T(128)S(1)} copy-done((s32[8]{0:T(128)S(1)}, s32[8]{0:T(128)}, u32[]{:S(2)}) %copy-start.7) | copy-done | bytes 56
  4.2 0.8 %shard_map.113 = (bf16[48,512]{1,0:T(8,128)(2,1)S(1)}, bf16[48,512]{1,0:T(8,128)(2,1)S(1)}, bf16[48,512]{1,0:T(8,128)(2,1)S(1)}, bf16[48,512]{1,0:T(8,128)(2,1)S(1)}, bf16[48,512]{1,0:T(8,128)(2,1)S(1)}) custom-call(s32[2,8]{1,0:T(2,128)S(1)} %bitcast.2, s32[8]{0:T(128)S(1)} %copy-done.7, bf16[512,128]{1,0:T(8,128)(2,1)S(1)} %copy-done.2, ...), custom_call_target="tpu_custom_call" | custom-call | tf_op jit(solution)/shard_map/pallas_call | solution.py:190
  5.0 5.6 %collective-permute-start.1 = (bf16[48,512]{1,0:T(8,128)(2,1)S(1)}, bf16[48,512]{1,0:T(8,128)(2,1)S(1)}, u32[]{:S(2)}, u32[]{:S(2)}) collective-permute-start(bf16[48,512]{1,0:T(8,128)(2,1)S(1)} %get-tuple-element.27), channel_id=1, source_target_pairs={{0,14},{1,13},{2,12},{3,15},{4,10},{5,9},{6,8},{7,11},{8,6},{9,5},... | collective-permute-start | bytes 147464 | tf_op jit(solution)/shard_map/ppermute | solution.py:155
  10.7 0.0 collective-permute-start.2
  10.7 1.7 %collective-permute-start.3 = (bf16[48,512]{1,0:T(8,128)(2,1)S(1)}, bf16[48,512]{1,0:T(8,128)(2,1)S(1)}, u32[]{:S(2)}, u32[]{:S(2)}) collective-permute-start(bf16[48,512]{1,0:T(8,128)(2,1)S(1)} %get-tuple-element.29), channel_id=1, source_target_pairs={{0,6},{1,5},{2,4},{3,7},{4,2},{5,1},{6,0},{7,3},{8,14},{9,13},{10,... | collective-permute-start | bytes 147464 | tf_op jit(solution)/shard_map/ppermute | solution.py:155
  12.3 0.4 %collective-permute-start.4 = (bf16[48,512]{1,0:T(8,128)(2,1)S(1)}, bf16[48,512]{1,0:T(8,128)(2,1)S(1)}, u32[]{:S(2)}, u32[]{:S(2)}) collective-permute-start(bf16[48,512]{1,0:T(8,128)(2,1)S(1)} %get-tuple-element.30), channel_id=1, source_target_pairs={{0,2},{1,3},{2,0},{3,1},{4,6},{5,7},{6,4},{7,5},{8,10},{9,11},{10,... | collective-permute-start | bytes 147464 | tf_op jit(solution)/shard_map/ppermute | solution.py:155
  12.8 0.3 collective-permute-done.1.refs_1_
  13.1 0.0 collective-permute-start.5
  13.1 3.6 %collective-permute-done.2.refs_2_ = bf16[48,512]{1,0:T(8,128)(2,1)S(1)} collective-permute-done((bf16[48,512]{1,0:T(8,128)(2,1)S(1)}, bf16[48,512]{1,0:T(8,128)(2,1)S(1)}, u32[]{:S(2)}, u32[]{:S(2)}) %collective-permute-start.2) | collective-permute-done | bytes 49184 | tf_op jit(solution)/shard_map/ppermute | solution.py:155
  16.7 0.0 collective-permute-start.6
  16.7 0.0 collective-permute-done.3.refs_3_
  16.7 0.5 %collective-permute-start.7 = (bf16[48,512]{1,0:T(8,128)(2,1)S(1)}, bf16[48,512]{1,0:T(8,128)(2,1)S(1)}, u32[]{:S(2)}, u32[]{:S(2)}) collective-permute-start(bf16[48,512]{1,0:T(8,128)(2,1)S(1)} %collective-permute-done.3.refs_3_), channel_id=1, source_target_pairs={{0,1},{1,0},{2,3},{3,2},{4,5},{5,4},{6,7},{7,6},{8,9},{9,8},{10,11... | collective-permute-start | bytes 147464 | tf_op jit(solution)/shard_map/ppermute | solution.py:162
  17.2 0.0 collective-permute-done.x_other
  17.2 0.0 copy-start.1
  17.2 1.0 %copy-done.1 = bf16[64,4096]{1,0:T(8,128)(2,1)S(1)} copy-done((bf16[64,4096]{1,0:T(8,128)(2,1)S(1)}, bf16[64,4096]{1,0:T(8,128)(2,1)}, u32[]{:S(2)}) %copy-start.1) | copy-done | bytes 524312
  18.2 0.0 copy-start.3
  18.2 0.9 %copy-done.3 = bf16[128,512]{1,0:T(8,128)(2,1)S(1)} copy-done((bf16[128,512]{1,0:T(8,128)(2,1)S(1)}, bf16[128,512]{1,0:T(8,128)(2,1)}, u32[]{:S(2)}) %copy-start.3) | copy-done | bytes 131096
  19.1 0.0 copy-start.6
  19.1 0.7 %copy-done.6 = s32[8,2]{0,1:T(2,128)S(1)} copy-done((s32[8,2]{0,1:T(2,128)S(1)}, s32[8,2]{0,1:T(2,128)}, u32[]{:S(2)}) %copy-start.6) | copy-done | bytes 88
  19.8 0.0 copy-start.8
  19.8 0.7 %copy-done.8 = s32[8]{0:T(128)S(1)} copy-done((s32[8]{0:T(128)S(1)}, s32[8]{0:T(128)}, u32[]{:S(2)}) %copy-start.8) | copy-done | bytes 56
  20.5 0.0 copy-start.9
  20.5 0.7 %copy-done.9 = s32[8,2]{0,1:T(2,128)S(1)} copy-done((s32[8,2]{0,1:T(2,128)S(1)}, s32[8,2]{0,1:T(2,128)}, u32[]{:S(2)}) %copy-start.9) | copy-done | bytes 88
  21.1 0.0 copy-start.10
  21.1 0.7 %copy-done.10 = s32[8]{0:T(128)S(1)} copy-done((s32[8]{0:T(128)S(1)}, s32[8]{0:T(128)}, u32[]{:S(2)}) %copy-start.10) | copy-done | bytes 56
  21.8 0.7 %shard_map.112 = (bf16[128,4096]{1,0:T(8,128)(2,1)S(1)}, bf16[128,512]{1,0:T(8,128)(2,1)S(1)}, f32[128,32]{1,0:T(8,128)S(1)}, bf16[32,128]{1,0:T(8,128)(2,1)S(1)}, bf16[256,128]{1,0:T(8,128)(2,1)S(1)}) custom-call(s32[2,8]{1,0:T(2,128)S(1)} %bitcast.4, s32[2,8]{1,0:T(2,128)S(1)} %bitcast.3, s32[8]{0:T(128)S(1)} %copy-done.8, s32[8]{0:T(128)S(1)} %copy-done.10, ...), custom_call_target="tpu_custom_call" | custom-call | bytes 4194304 | tf_op jit(solution)/shard_map/pallas_call | solution.py:207
  22.5 0.0 collective-permute-done.4.refs_4_
  22.5 0.0 collective-permute-done.5.refs_5_
  22.5 0.0 collective-permute-done.6.refs_6_
  22.5 0.0 collective-permute-done.7.refs_7_
  22.5 1.2 %shard_map.114 = (bf16[128,32]{1,0:T(8,128)(2,1)S(1)}, bf16[8,32,512]{2,1,0:T(8,128)(2,1)S(1)}, bf16[48,512]{1,0:T(8,128)(2,1)S(1)}, bf16[48,512]{1,0:T(8,128)(2...) custom-call(bf16[128,4096]{1,0:T(8,128)(2,1)S(1)} %get-tuple-element.23.x_ref, ...), custom_call_target="tpu_custom_call" | custom-call | tf_op jit(solution)/shard_map/pallas_call | solution.py:229
  23.8 1.8 %collective-permute-start.8 = (bf16[48,512]{1,0:T(8,128)(2,1)S(1)}, bf16[48,512]{1,0:T(8,128)(2,1)S(1)}, u32[]{:S(2)}, u32[]{:S(2)}) collective-permute-start(bf16[48,512]{1,0:T(8,128)(2,1)S(1)} %get-tuple-element.35), channel_id=1, source_target_pairs={{0,14},{1,13},{2,12},{3,15},{4,10},{5,9},{6,8},{7,11},{8,6},{9,5},... | collective-permute-start | bytes 147464 | tf_op jit(solution)/shard_map/ppermute | solution.py:155
  25.6 0.6 %collective-permute-start.9 = (bf16[48,512]{1,0:T(8,128)(2,1)S(1)}, bf16[48,512]{1,0:T(8,128)(2,1)S(1)}, u32[]{:S(2)}, u32[]{:S(2)}) collective-permute-start(bf16[48,512]{1,0:T(8,128)(2,1)S(1)} %get-tuple-element.36), channel_id=1, source_target_pairs={{0,10},{1,9},{2,8},{3,11},{4,14},{5,13},{6,12},{7,15},{8,2},{9,1},... | collective-permute-start | bytes 147464 | tf_op jit(solution)/shard_map/ppermute | solution.py:155
  26.2 2.8 %collective-permute-start.10 = (bf16[48,512]{1,0:T(8,128)(2,1)S(1)}, bf16[48,512]{1,0:T(8,128)(2,1)S(1)}, u32[]{:S(2)}, u32[]{:S(2)}) collective-permute-start(bf16[48,512]{1,0:T(8,128)(2,1)S(1)} %get-tuple-element.37), channel_id=1, source_target_pairs={{0,6},{1,5},{2,4},{3,7},{4,2},{5,1},{6,0},{7,3},{8,14},{9,13},{10,... | collective-permute-start | bytes 147464 | tf_op jit(solution)/shard_map/ppermute | solution.py:155
  29.1 1.5 %collective-permute-start.11 = (bf16[48,512]{1,0:T(8,128)(2,1)S(1)}, bf16[48,512]{1,0:T(8,128)(2,1)S(1)}, u32[]{:S(2)}, u32[]{:S(2)}) collective-permute-start(bf16[48,512]{1,0:T(8,128)(2,1)S(1)} %get-tuple-element.38), channel_id=1, source_target_pairs={{0,2},{1,3},{2,0},{3,1},{4,6},{5,7},{6,4},{7,5},{8,10},{9,11},{10,... | collective-permute-start | bytes 147464 | tf_op jit(solution)/shard_map/ppermute | solution.py:155
  30.6 0.7 %collective-permute-done.8.refs_1_ = bf16[48,512]{1,0:T(8,128)(2,1)S(1)} collective-permute-done((bf16[48,512]{1,0:T(8,128)(2,1)S(1)}, bf16[48,512]{1,0:T(8,128)(2,1)S(1)}, u32[]{:S(2)}, u32[]{:S(2)}) %collective-permute-start.8) | collective-permute-done | bytes 49184 | tf_op jit(solution)/shard_map/ppermute | solution.py:155
  31.3 0.0 collective-permute-start.12
  31.3 0.4 %collective-permute-done.9.refs_2_ = bf16[48,512]{1,0:T(8,128)(2,1)S(1)} collective-permute-done((bf16[48,512]{1,0:T(8,128)(2,1)S(1)}, bf16[48,512]{1,0:T(8,128)(2,1)S(1)}, u32[]{:S(2)}, u32[]{:S(2)}) %collective-permute-start.9) | collective-permute-done | bytes 49184 | tf_op jit(solution)/shard_map/ppermute | solution.py:155
  31.7 0.1 collective-permute-start.13
  31.8 0.3 collective-permute-done.10.refs_3_
  32.1 0.1 collective-permute-start.14
  32.2 0.0 copy-done
  32.2 2.3 %shard_map.115 = bf16[128,2048]{1,0:T(8,128)(2,1)} custom-call(bf16[128,512]{1,0:T(8,128)(2,1)S(1)} %get-tuple-element.22.g_ref, bf16[2048,512]{1,0:T(8,128)(2,1)S(1)} %copy-done, bf16[128,32]{1,0:T(8,128)(2,1)S(1)} %get-tuple-element.31.dlow_ref, bf16[8,32,512]{2,1,0:T(8,128)(2,1)S(1)} %get-tuple-element.32.a_ref), custom_call_target="tpu_custom_call" | custom-call | flops 285212672 | bytes 2621440 | tf_op jit(solution)/shard_map/pallas_call | solution.py:243
  34.5 0.0 collective-permute-done.11.refs_4_
  34.5 0.0 collective-permute-done.12.refs_5_
  34.5 0.0 collective-permute-done.13.refs_6_
  34.5 0.0 collective-permute-done.14.refs_7_
  34.5 1.0 %shard_map.116 = (f32[512,128]{1,0:T(8,128)}, f32[16,256]{1,0:T(8,128)}) custom-call(bf16[256,128]{1,0:T(8,128)(2,1)S(1)} %get-tuple-element.33.all_ref, bf16[48,512]{1,0:T(8,128)(2,1)S(1)} %get-tuple-element.34.refs_0_, bf16[48,512]{1,0:T(8,128)(2,1)S(1)} %collective-permute-done.8.refs_1_, bf16[48,512]{1,0:T(8,128)(2,1)S(1)} %collective-permute-done.9.refs_2_, ...), custom_call_target="tpu_custom_call" | custom-call | tf_op jit(solution)/shard_map/pallas_call | solution.py:262
Async XLA Ops:
  0.6 31.6 %copy-start = (bf16[2048,512]{1,0:T(8,128)(2,1)S(1)}, bf16[2048,512]{1,0:T(8,128)(2,1)}, u32[]{:S(2)}) copy-start(bf16[2048,512]{1,0:T(8,128)(2,1)} %w_ref.1) | copy-start | bytes 6291460
  0.6 16.5 %collective-permute-start = (bf16[64,4096]{1,0:T(8,128)(2,1)}, bf16[64,4096]{1,0:T(8,128)(2,1)S(1)}, u32[]{:S(2)}, u32[]{:S(2)}) collective-permute-start(bf16[64,4096]{1,0:T(8,128)(2,1)} %x_mine.1), channel_id=1, source_target_pairs={{0,1},{1,0},{2,3},{3,2},{4,5},{5,4},{6,7},{7,6},{8,9},{9,8},{10,11... | collective-permute-start | bytes 1572872 | tf_op jit(solution)/shard_map/ppermute | solution.py:204
  1.2 1.0 %copy-start.2 = (bf16[512,128]{1,0:T(8,128)(2,1)S(1)}, bf16[512,128]{1,0:T(8,128)(2,1)}, u32[]{:S(2)}) copy-start(bf16[512,128]{1,0:T(8,128)(2,1)} %down_hbm.1) | copy-start | bytes 393220
  2.2 0.7 %copy-start.4 = (bf16[16,512]{1,0:T(8,128)(2,1)S(1)}, bf16[16,512]{1,0:T(8,128)(2,1)}, u32[]{:S(2)}) copy-start(bf16[16,512]{1,0:T(8,128)(2,1)} %up_hbm.1) | copy-start | bytes 49156
  2.9 0.7 %copy-start.5 = (s32[8,2]{0,1:T(2,128)S(1)}, s32[8,2]{0,1:T(2,128)}, u32[]{:S(2)}) copy-start(s32[8,2]{0,1:T(2,128)} %param.15) | copy-start | bytes 196
  3.6 0.7 %copy-start.7 = (s32[8]{0:T(128)S(1)}, s32[8]{0:T(128)}, u32[]{:S(2)}) copy-start(s32[8]{0:T(128)} %slot_hbm.3) | copy-start | bytes 100
  5.0 8.0 %collective-permute-start.1 = (bf16[48,512]{1,0:T(8,128)(2,1)S(1)}, bf16[48,512]{1,0:T(8,128)(2,1)S(1)}, u32[]{:S(2)}, u32[]{:S(2)}) collective-permute-start(bf16[48,512]{1,0:T(8,128)(2,1)S(1)} %get-tuple-element.27), channel_id=1, source_target_pairs={{0,14},{1,13},{2,12},{3,15},{4,10},{5,9},{6,8},{7,11},{8,6},{9,5},... | collective-permute-start | bytes 147464 | tf_op jit(solution)/shard_map/ppermute | solution.py:155
  10.7 6.0 %collective-permute-start.2 = (bf16[48,512]{1,0:T(8,128)(2,1)S(1)}, bf16[48,512]{1,0:T(8,128)(2,1)S(1)}, u32[]{:S(2)}, u32[]{:S(2)}) collective-permute-start(bf16[48,512]{1,0:T(8,128)(2,1)S(1)} %get-tuple-element.28), channel_id=1, source_target_pairs={{0,10},{1,9},{2,8},{3,11},{4,14},{5,13},{6,12},{7,15},{8,2},{9,1},... | collective-permute-start | bytes 147464 | tf_op jit(solution)/shard_map/ppermute | solution.py:155
  10.7 6.0 %collective-permute-start.3 = (bf16[48,512]{1,0:T(8,128)(2,1)S(1)}, bf16[48,512]{1,0:T(8,128)(2,1)S(1)}, u32[]{:S(2)}, u32[]{:S(2)}) collective-permute-start(bf16[48,512]{1,0:T(8,128)(2,1)S(1)} %get-tuple-element.29), channel_id=1, source_target_pairs={{0,6},{1,5},{2,4},{3,7},{4,2},{5,1},{6,0},{7,3},{8,14},{9,13},{10,... | collective-permute-start | bytes 147464 | tf_op jit(solution)/shard_map/ppermute | solution.py:155
  12.3 10.2 %collective-permute-start.4 = (bf16[48,512]{1,0:T(8,128)(2,1)S(1)}, bf16[48,512]{1,0:T(8,128)(2,1)S(1)}, u32[]{:S(2)}, u32[]{:S(2)}) collective-permute-start(bf16[48,512]{1,0:T(8,128)(2,1)S(1)} %get-tuple-element.30), channel_id=1, source_target_pairs={{0,2},{1,3},{2,0},{3,1},{4,6},{5,7},{6,4},{7,5},{8,10},{9,11},{10,... | collective-permute-start | bytes 147464 | tf_op jit(solution)/shard_map/ppermute | solution.py:155
  13.1 9.5 %collective-permute-start.5 = (bf16[48,512]{1,0:T(8,128)(2,1)S(1)}, bf16[48,512]{1,0:T(8,128)(2,1)S(1)}, u32[]{:S(2)}, u32[]{:S(2)}) collective-permute-start(bf16[48,512]{1,0:T(8,128)(2,1)S(1)} %collective-permute-done.1.refs_1_), channel_id=1, source_target_pairs={{0,1},{1,0},{2,3},{3,2},{4,5},{5,4},{6,7},{7,6},{8,9},{9,8},{10,11... | collective-permute-start | bytes 147464 | tf_op jit(solution)/shard_map/ppermute | solution.py:162
  16.7 5.9 %collective-permute-start.6 = (bf16[48,512]{1,0:T(8,128)(2,1)S(1)}, bf16[48,512]{1,0:T(8,128)(2,1)S(1)}, u32[]{:S(2)}, u32[]{:S(2)}) collective-permute-start(bf16[48,512]{1,0:T(8,128)(2,1)S(1)} %collective-permute-done.2.refs_2_), channel_id=1, source_target_pairs={{0,1},{1,0},{2,3},{3,2},{4,5},{5,4},{6,7},{7,6},{8,9},{9,8},{10,11... | collective-permute-start | bytes 147464 | tf_op jit(solution)/shard_map/ppermute | solution.py:162
  16.7 5.9 %collective-permute-start.7 = (bf16[48,512]{1,0:T(8,128)(2,1)S(1)}, bf16[48,512]{1,0:T(8,128)(2,1)S(1)}, u32[]{:S(2)}, u32[]{:S(2)}) collective-permute-start(bf16[48,512]{1,0:T(8,128)(2,1)S(1)} %collective-permute-done.3.refs_3_), channel_id=1, source_target_pairs={{0,1},{1,0},{2,3},{3,2},{4,5},{5,4},{6,7},{7,6},{8,9},{9,8},{10,11... | collective-permute-start | bytes 147464 | tf_op jit(solution)/shard_map/ppermute | solution.py:162
  17.2 1.0 %copy-start.1 = (bf16[64,4096]{1,0:T(8,128)(2,1)S(1)}, bf16[64,4096]{1,0:T(8,128)(2,1)}, u32[]{:S(2)}) copy-start(bf16[64,4096]{1,0:T(8,128)(2,1)} %x_mine.1) | copy-start | bytes 1572868
  18.2 0.9 %copy-start.3 = (bf16[128,512]{1,0:T(8,128)(2,1)S(1)}, bf16[128,512]{1,0:T(8,128)(2,1)}, u32[]{:S(2)}) copy-start(bf16[128,512]{1,0:T(8,128)(2,1)} %g_hbm.1) | copy-start | bytes 393220
  19.1 0.7 %copy-start.6 = (s32[8,2]{0,1:T(2,128)S(1)}, s32[8,2]{0,1:T(2,128)}, u32[]{:S(2)}) copy-start(s32[8,2]{0,1:T(2,128)} %param.15) | copy-start | bytes 196
  19.8 0.7 %copy-start.8 = (s32[8]{0:T(128)S(1)}, s32[8]{0:T(128)}, u32[]{:S(2)}) copy-start(s32[8]{0:T(128)} %slot_hbm.3) | copy-start | bytes 100
  20.5 0.7 %copy-start.9 = (s32[8,2]{0,1:T(2,128)S(1)}, s32[8,2]{0,1:T(2,128)}, u32[]{:S(2)}) copy-start(s32[8,2]{0,1:T(2,128)} %param.14) | copy-start | bytes 196
  21.1 0.7 %copy-start.10 = (s32[8]{0:T(128)S(1)}, s32[8]{0:T(128)}, u32[]{:S(2)}) copy-start(s32[8]{0:T(128)} %count_hbm.1) | copy-start | bytes 100
  23.8 7.5 %collective-permute-start.8 = (bf16[48,512]{1,0:T(8,128)(2,1)S(1)}, bf16[48,512]{1,0:T(8,128)(2,1)S(1)}, u32[]{:S(2)}, u32[]{:S(2)}) collective-permute-start(bf16[48,512]{1,0:T(8,128)(2,1)S(1)} %get-tuple-element.35), channel_id=1, source_target_pairs={{0,14},{1,13},{2,12},{3,15},{4,10},{5,9},{6,8},{7,11},{8,6},{9,5},... | collective-permute-start | bytes 147464 | tf_op jit(solution)/shard_map/ppermute | solution.py:155
  25.6 6.1 %collective-permute-start.9 = (bf16[48,512]{1,0:T(8,128)(2,1)S(1)}, bf16[48,512]{1,0:T(8,128)(2,1)S(1)}, u32[]{:S(2)}, u32[]{:S(2)}) collective-permute-start(bf16[48,512]{1,0:T(8,128)(2,1)S(1)} %get-tuple-element.36), channel_id=1, source_target_pairs={{0,10},{1,9},{2,8},{3,11},{4,14},{5,13},{6,12},{7,15},{8,2},{9,1},... | collective-permute-start | bytes 147464 | tf_op jit(solution)/shard_map/ppermute | solution.py:155
  26.2 5.9 %collective-permute-start.10 = (bf16[48,512]{1,0:T(8,128)(2,1)S(1)}, bf16[48,512]{1,0:T(8,128)(2,1)S(1)}, u32[]{:S(2)}, u32[]{:S(2)}) collective-permute-start(bf16[48,512]{1,0:T(8,128)(2,1)S(1)} %get-tuple-element.37), channel_id=1, source_target_pairs={{0,6},{1,5},{2,4},{3,7},{4,2},{5,1},{6,0},{7,3},{8,14},{9,13},{10,... | collective-permute-start | bytes 147464 | tf_op jit(solution)/shard_map/ppermute | solution.py:155
  29.1 5.5 %collective-permute-start.11 = (bf16[48,512]{1,0:T(8,128)(2,1)S(1)}, bf16[48,512]{1,0:T(8,128)(2,1)S(1)}, u32[]{:S(2)}, u32[]{:S(2)}) collective-permute-start(bf16[48,512]{1,0:T(8,128)(2,1)S(1)} %get-tuple-element.38), channel_id=1, source_target_pairs={{0,2},{1,3},{2,0},{3,1},{4,6},{5,7},{6,4},{7,5},{8,10},{9,11},{10,... | collective-permute-start | bytes 147464 | tf_op jit(solution)/shard_map/ppermute | solution.py:155
  31.3 3.3 %collective-permute-start.12 = (bf16[48,512]{1,0:T(8,128)(2,1)S(1)}, bf16[48,512]{1,0:T(8,128)(2,1)S(1)}, u32[]{:S(2)}, u32[]{:S(2)}) collective-permute-start(bf16[48,512]{1,0:T(8,128)(2,1)S(1)} %collective-permute-done.8.refs_1_), channel_id=1, source_target_pairs={{0,1},{1,0},{2,3},{3,2},{4,5},{5,4},{6,7},{7,6},{8,9},{9,8},{10,11... | collective-permute-start | bytes 147464 | tf_op jit(solution)/shard_map/ppermute | solution.py:162
  31.7 2.8 %collective-permute-start.13 = (bf16[48,512]{1,0:T(8,128)(2,1)S(1)}, bf16[48,512]{1,0:T(8,128)(2,1)S(1)}, u32[]{:S(2)}, u32[]{:S(2)}) collective-permute-start(bf16[48,512]{1,0:T(8,128)(2,1)S(1)} %collective-permute-done.9.refs_2_), channel_id=1, source_target_pairs={{0,1},{1,0},{2,3},{3,2},{4,5},{5,4},{6,7},{7,6},{8,9},{9,8},{10,11... | collective-permute-start | bytes 147464 | tf_op jit(solution)/shard_map/ppermute | solution.py:162
  32.1 2.4 %collective-permute-start.14 = (bf16[48,512]{1,0:T(8,128)(2,1)S(1)}, bf16[48,512]{1,0:T(8,128)(2,1)S(1)}, u32[]{:S(2)}, u32[]{:S(2)}) collective-permute-start(bf16[48,512]{1,0:T(8,128)(2,1)S(1)} %collective-permute-done.10.refs_3_), channel_id=1, source_target_pairs={{0,1},{1,0},{2,3},{3,2},{4,5},{5,4},{6,7},{7,6},{8,9},{9,8},{10,11... | collective-permute-start | bytes 147464 | tf_op jit(solution)/shard_map/ppermute | solution.py:162

commit v4 on v3

v4 whole, which is shorter than its diff:
```python
import functools

import jax
import jax.numpy as jnp
from jax import lax
from jax.experimental import pallas as pl
from jax.experimental.pallas import tpu as pltpu
from jax.sharding import PartitionSpec as P

ADAPTER_RANK = 16
adapter_scale = 2.0

bf16, f32, i32 = jnp.bfloat16, jnp.float32, jnp.int32

HBM = pl.BlockSpec(memory_space=pltpu.HBM)
VMEM = pl.BlockSpec(memory_space=pltpu.VMEM)


def dot(a, b, ca, cb):
    return lax.dot_general(a, b, (((ca,), (cb,)), ((), ())), preferred_element_type=f32)


def params(mib):
    return pltpu.CompilerParams(vmem_limit_bytes=mib << 20)


def slot_rows(chosen_ref, slot_ref, ranks, width):
    lane = lax.broadcasted_iota(i32, (ADAPTER_RANK, width), 1)
    row = lax.broadcasted_iota(i32, (ADAPTER_RANK, width), 0)
    rows = []
    for rank in ranks:
        for k in range(chosen_ref.shape[0]):
            first = slot_ref[chosen_ref[k, rank]] * ADAPTER_RANK
            rows.append(jnp.where(lane == row + first, 1.0, 0.0))
    return jnp.concatenate(rows, axis=0).astype(bf16)


def start_all(sources, targets, sems, first=0):
    copies = [
        pltpu.make_async_copy(source, target, sems.at[first + k])
        for k, (source, target) in enumerate(zip(sources, targets))
    ]
    for copy in copies:
        copy.start()
    return copies


def wait_all(copies):
    for copy in copies:
        copy.wait()


def pairs(n, core):
    return [n - 1 - 2 * j - core for j in range(n // 2 - 1)]


def partners(n, me, core):
    steps = [jnp.where(core == 0, a, b) for a, b in zip(pairs(n, 0), pairs(n, 1))]
    return [me] + [me ^ d for d in steps] + [me ^ 1]


def senders(n, me, core):
    return partners(n, me, core) + partners(n, me, 1 - core)[1:-1]


class Staged:
    def __init__(self, n, half, rows, picked, width, slots):
        self.n, self.half, self.rows, self.picked, self.slots = n, half, rows, picked, slots
        self.g = n * half
        self.mask = self.g + rows
        self.message = self.mask + rows
        self.shape = (self.message + picked + ADAPTER_RANK, width)

    def x(self, q):
        return pl.ds(q * self.half, self.half)

    def own_rows(self, ref):
        return ref[self.mask : self.mask + self.picked, self.slots : 2 * self.slots]

    def all_rows(self, kept):
        parts = self.n * self.picked // self.rows
        at = [pl.ds((2 + k) * self.slots, self.slots) for k in range(parts)]
        return jnp.concatenate([kept[self.rows :, k] for k in at], axis=0)


def pack_kernel(n, lay, start_hbm, chosen_hbm, slot_hbm, count_hbm, g_hbm, x_hbm, down_hbm, up_hbm, *refs):
    count = n // 2 + 1
    send, stage = refs[: count - 1], refs[count - 1]
    start_ref, chosen_ref, slot_ref, count_ref, down_ref, up_ref, out_ref, extra_ref, sems = refs[count:]
    width = down_hbm.shape[0]
    rows, picked, slots = lay.rows, lay.picked, lay.slots
    tables = start_all(
        [chosen_hbm, slot_hbm, start_hbm, count_hbm], [chosen_ref, slot_ref, start_ref, count_ref], sems
    )
    maps = start_all([down_hbm, up_hbm], [down_ref, up_ref], sems, 4)
    gradient = start_all([g_hbm], [extra_ref.at[pl.ds(0, rows)]], sems, 6)
    tokens = start_all(
        [x_hbm.at[:, pl.ds(q * width, width)] for q in range(n)],
        [stage.at[lay.x(q)] for q in range(n)],
        sems,
        7,
    )
    me = lax.axis_index("dp")
    ranks = partners(n, me, lax.axis_index("tensor"))
    wait_all(tables)
    onehot = slot_rows(chosen_ref, slot_ref, ranks, slots)
    wait_all(maps)
    columns = dot(onehot, down_ref[...], 1, 1).astype(bf16)
    for k in range(count):
        out_ref[k, :picked, :] = columns[k * picked : (k + 1) * picked]
        out_ref[k, picked:, :] = up_ref[...]
    done = start_all([out_ref.at[k] for k in range(1, count)], send, sems, 7 + n)
    own = stage.at[pl.ds(lay.message, picked + ADAPTER_RANK)]
    done += start_all([out_ref.at[0]], [own], sems, 6 + n + count)

    position = lax.broadcasted_iota(i32, (rows, slots), 0)
    group = lax.broadcasted_iota(i32, (rows, slots), 1) // ADAPTER_RANK
    segment = jnp.full((rows, slots), -1, i32)
    for k in range(start_ref.shape[0]):
        segment += jnp.where(position >= start_ref[k, me], 1, 0)
    extra_ref[rows:, :slots] = jnp.where(segment == group, 1.0, 0.0).astype(bf16)
    extra_ref[rows : rows + picked, slots : 2 * slots] = onehot[:picked]
    every = slot_rows(chosen_ref, slot_ref, range(n), slots)
    for k in range(n * picked // rows):
        extra_ref[rows:, (2 + k) * slots : (3 + k) * slots] = every[k * rows : (k + 1) * rows]
    wait_all(gradient)
    live = lax.broadcasted_iota(i32, (rows, width), 0) < count_ref[me]
    g = extra_ref[:rows, :]
    extra_ref[:rows, :] = jnp.where(live, g, jnp.zeros_like(g))
    done += start_all([extra_ref], [stage.at[pl.ds(lay.g, 2 * rows)]], sems, 7 + n + count)
    wait_all(tokens + done)


def middle_kernel(n, lay, stage, x_other, *refs):
    count = n // 2 + 1
    got, (dlow_ref, a_ref, kept_ref) = refs[: n - 1], refs[n - 1 : n + 2]
    send, (x_ref, got_ref, up_ref) = refs[n + 2 : n + 2 + count], refs[n + 2 + count :]
    me, core = lax.axis_index("dp"), lax.axis_index("tensor")
    half, rows, picked = lay.half, lay.rows, lay.picked
    width = stage.shape[1]
    mine = pl.ds(pl.multiple_of(core * half, half), half)
    other = pl.ds(pl.multiple_of((1 - core) * half, half), half)
    for q in range(n):
        x_ref[mine, q * width : (q + 1) * width] = stage[lay.x(q), :]
    x_ref[other, :] = x_other[...]
    ranks = senders(n, me, core)
    got_ref[me] = stage[lay.message :, :]
    for sender, message in zip(ranks[1:], got):
        got_ref[sender] = message[...]

    in_seg = stage[lay.mask : lay.mask + rows, :picked].astype(f32) > 0.0
    g = stage[lay.g : lay.g + rows, :]
    onehot = lay.own_rows(stage)
    up_maps = got_ref[:, picked:, :].reshape(-1, width)
    b_sel = dot(onehot, up_maps, 1, 0).astype(bf16)
    dlow = jnp.where(in_seg, adapter_scale * dot(g, b_sel, 1, 1), 0.0).astype(bf16)
    dlow_ref[...] = dlow
    parts = n // 2
    a_ref[...] = got_ref[pl.ds(pl.multiple_of(core * parts, parts), parts), :picked, :]
    kept_ref[...] = stage[lay.g : lay.message, :]
    targets = partners(n, me, core)
    for target, message in zip(targets, send):
        at = pl.ds(pl.multiple_of(target * width, width), width)
        message[:picked, :] = dot(dlow, x_ref[:, at], 0, 0).astype(bf16)

    low = jnp.zeros((rows, picked), f32)
    for q in range(n):
        low += dot(x_ref[:, q * width : (q + 1) * width], got_ref[q, :picked, :], 1, 1)
    low = jnp.where(in_seg, low, 0.0).astype(bf16)
    low_wide = dot(low, onehot, 1, 0).astype(bf16)
    up = (adapter_scale * dot(low_wide, g, 0, 0)).astype(bf16)
    up_ref[...] = up.reshape(up_ref.shape)
    for target, message in zip(targets, send):
        message[picked:, :] = up_ref[target]


def grad_x_kernel(kept_ref, w_hbm, dlow_ref, a_ref, out_hbm, w_ref, out_ref, sems):
    steps, picked, width = a_ref.shape
    blocks = [pl.ds(j * width, width) for j in range(steps)]
    weights = start_all([w_hbm.at[k] for k in blocks], [w_ref.at[k] for k in blocks], sems)
    g = kept_ref[: out_ref.shape[0], :]
    done = []
    for j, at in enumerate(blocks):
        total = dot(dlow_ref[...], a_ref[j], 1, 0)
        weights[j].wait()
        total += dot(g, w_ref[at, :], 1, 1)
        out_ref[:, at] = total.astype(bf16)
        done += start_all([out_ref.at[:, at]], [out_hbm.at[:, at]], sems, steps + j)
    wait_all(done)


def final_kernel(n, lay, kept_ref, *refs):
    got, (a_ref, up_ref, rows_ref) = refs[:n], refs[n:]
    me, core = lax.axis_index("dp"), lax.axis_index("tensor")
    piece, picked = up_ref.shape[1], lay.picked
    for sender, message in zip(senders(n, me, core), got):
        rows_ref[sender] = message[...]
    rows = rows_ref[:, :picked, :].reshape(n * picked, rows_ref.shape[2])
    a_ref[...] = dot(rows, lay.all_rows(kept_ref), 0, 0)
    at = pl.ds(pl.multiple_of(core * piece, piece), piece)
    up_ref[...] = jnp.sum(rows_ref[:, picked:, at].astype(f32), axis=0)


def exchange(messages):
    n = 2 * len(messages)
    steps = list(zip(pairs(n, 0), pairs(n, 1))) + [(1, 1)]
    got = [
        lax.ppermute(
            message,
            ("dp", "tensor"),
            [(2 * i + c, 2 * (i ^ step[c]) + c) for i in range(n) for c in range(2)],
        )
        for message, step in zip(messages, steps)
    ]
    passed = [lax.ppermute(message, "tensor", [(0, 1), (1, 0)]) for message in got[:-1]]
    return got + passed


def local_kernels(
    inputs,
    output_gradient,
    frozen_weight,
    down_maps,
    up_maps,
    segment_start,
    segment_adapter,
    adapter_slot,
    token_count,
):
    tok_half, model_width = inputs.shape
    tok_rows, out_width = output_gradient.shape
    column_total, slot_width = down_maps.shape
    half = frozen_weight.shape[0]
    n = lax.axis_size("dp")
    piece = out_width // lax.axis_size("tensor")
    segs = segment_start.shape[1]
    picked = segs * ADAPTER_RANK
    shape = jax.ShapeDtypeStruct
    message = shape((picked + ADAPTER_RANK, column_total), bf16)
    count = n // 2 + 1
    starts, chosen = segment_start.T, segment_adapter.T

    tables = [
        pltpu.SMEM(starts.shape, i32),
        pltpu.SMEM(chosen.shape, i32),
        pltpu.SMEM(adapter_slot.shape, i32),
        pltpu.SMEM(token_count.shape, i32),
    ]
    dma = pltpu.SemaphoreType.DMA

    lay = Staged(n, tok_half, tok_rows, picked, column_total, slot_width)
    *sent, stage = pl.pallas_call(
        functools.partial(pack_kernel, n, lay),
        out_shape=[message] * (count - 1) + [shape(lay.shape, bf16)],
        in_specs=[HBM] * 8,
        out_specs=[HBM] * count,
        scratch_shapes=tables
        + [
            pltpu.VMEM(down_maps.shape, bf16),
            pltpu.VMEM(up_maps.shape, bf16),
            pltpu.VMEM((count,) + message.shape, bf16),
            pltpu.VMEM((2 * tok_rows, out_width), bf16),
            dma((8 + n + count,)),
        ],
        compiler_params=params(56),
    )(
        starts,
        chosen,
        adapter_slot,
        token_count,
        output_gradient,
        inputs,
        down_maps,
        up_maps,
    )
    sent, x_late = lax.optimization_barrier((sent, inputs))
    got = exchange(sent)
    x_other = lax.ppermute(x_late, "tensor", [(0, 1), (1, 0)])

    dlow, a_half, kept, own, *sent = pl.pallas_call(
        functools.partial(middle_kernel, n, lay),
        out_shape=[
            shape((tok_rows, picked), bf16),
            shape((n // 2, picked, column_total), bf16),
            shape((2 * tok_rows, out_width), bf16),
        ]
        + [message] * count,
        in_specs=[VMEM] * (1 + n),
        out_specs=[VMEM] * (3 + count),
        scratch_shapes=[
            pltpu.VMEM((tok_rows, model_width), bf16),
            pltpu.VMEM((n,) + message.shape, bf16),
            pltpu.VMEM((n, ADAPTER_RANK, out_width), bf16),
        ],
        compiler_params=params(8),
    )(stage, x_other, *got)
    got = exchange(sent)

    grad_x = pl.pallas_call(
        grad_x_kernel,
        out_shape=shape((tok_rows, half), bf16),
        in_specs=[VMEM, HBM, VMEM, VMEM],
        out_specs=HBM,
        scratch_shapes=[
            pltpu.VMEM(frozen_weight.shape, bf16),
            pltpu.VMEM((tok_rows, half), bf16),
            dma((n,)),
        ],
        compiler_params=params(52),
        cost_estimate=pl.CostEstimate(
            flops=2 * tok_rows * half * (out_width + picked),
            bytes_accessed=2 * half * (out_width + tok_rows),
            transcendentals=0,
        ),
    )(kept, frozen_weight, dlow, a_half)

    grad_a, up_map_gradient = pl.pallas_call(
        functools.partial(final_kernel, n, lay),
        out_shape=[shape((column_total, slot_width), f32), shape((ADAPTER_RANK, piece), f32)],
        in_specs=[VMEM] * (1 + n),
        out_specs=[VMEM, VMEM],
        scratch_shapes=[pltpu.VMEM((n,) + message.shape, bf16)],
        compiler_params=params(8),
    )(kept, own, *got)
    return grad_x, grad_a, up_map_gradient


def local_plain(
    inputs,
    output_gradient,
    frozen_weight,
    down_maps,
    up_maps,
    segment_start,
    segment_adapter,
    adapter_slot,
    token_count,
):
    tok_rows, out_width = output_gradient.shape
    column_total = down_maps.shape[0]
    adapter_list = adapter_slot.shape[0]
    segs = segment_start.shape[1]
    dp_size = lax.axis_size("dp")
    my_rank = lax.axis_index("dp")
    core_idx = lax.axis_index("tensor")
    picked = segs * ADAPTER_RANK
    piece_out = out_width // lax.axis_size("tensor")
    half = frozen_weight.shape[0]

    x_other = lax.ppermute(inputs, "tensor", [(0, 1), (1, 0)])
    adapter_ids = jnp.arange(adapter_list, dtype=i32)
    slot_table = jnp.sum(
        jnp.where(segment_adapter[..., None] == adapter_ids, adapter_slot, 0), axis=-1
    )
    column = slot_table[:, :, None] * ADAPTER_RANK + jnp.arange(ADAPTER_RANK, dtype=i32)
    onehot = (
        column.reshape(-1)[:, None] == jnp.arange(adapter_list * ADAPTER_RANK, dtype=i32)
    ).astype(bf16)

    a_send = dot(onehot, down_maps, 1, 1).astype(bf16).reshape(dp_size, picked, column_total)
    b_send = jnp.broadcast_to(up_maps[None], (dp_size,) + up_maps.shape)
    a_got = lax.all_to_all(a_send, "dp", 0, 0, tiled=True)
    b_got = lax.all_to_all(b_send, "dp", 0, 0, tiled=True)

    position = jnp.arange(tok_rows, dtype=i32)
    starts = lax.dynamic_index_in_dim(segment_start, my_rank, 0, keepdims=False)
    live = position < lax.dynamic_index_in_dim(token_count, my_rank, 0, keepdims=False)
    my_seg = jnp.sum((starts[None, :] <= position[:, None]).astype(i32), axis=1) - 1
    in_seg = my_seg[:, None] == (jnp.arange(picked, dtype=i32) // ADAPTER_RANK)[None, :]
    my_onehot = lax.dynamic_slice_in_dim(onehot, my_rank * picked, picked, 0)
    g = jnp.where(live[:, None], output_gradient, jnp.zeros_like(output_gradient))
    base = dot(g, frozen_weight, 1, 1)

    b_sel = dot(my_onehot, b_got.reshape(-1, out_width), 1, 0).astype(bf16)
    dlow = (adapter_scale * dot(g, b_sel, 1, 1)).astype(bf16)
    dlow = jnp.where(in_seg, dlow, jnp.zeros_like(dlow))
    a_sel = jnp.moveaxis(a_got, 0, 1).reshape(picked, -1)
    first = core_idx == 0
    x = jnp.concatenate(
        [jnp.where(first, inputs, x_other), jnp.where(first, x_other, inputs)], axis=0
    )
    low = dot(x, a_sel, 1, 1).astype(bf16)
    low = jnp.where(in_seg, low, jnp.zeros_like(low))
    low_wide = dot(low, my_onehot, 1, 0).astype(bf16)

    ga_send = dot(dlow, x, 0, 0).astype(bf16).reshape(picked, dp_size, column_total)
    ga_got = lax.all_to_all(jnp.moveaxis(ga_send, 1, 0), "dp", 0, 0, tiled=True)
    g_piece = lax.dynamic_slice_in_dim(g, core_idx * piece_out, piece_out, 1)
    up_send = (adapter_scale * dot(low_wide, g_piece, 0, 0)).astype(bf16)
    up_got = lax.all_to_all(up_send.reshape(dp_size, -1, piece_out), "dp", 0, 0, tiled=True)

    a_half = lax.dynamic_slice_in_dim(a_sel, core_idx * half, half, 1)
    grad_x = (base + dot(dlow, a_half, 1, 0)).astype(bf16)
    grad_a = dot(ga_got.reshape(dp_size * picked, column_total), onehot, 0, 0)
    up_map_gradient = jnp.sum(up_got.astype(f32), axis=0)
    return grad_x, grad_a, up_map_gradient


def local(*args):
    down_maps, up_maps = args[3], args[4]
    n, tp = lax.axis_size("dp"), lax.axis_size("tensor")
    out_width = up_maps.shape[1]
    kernels_fit = (
        n == 8
        and tp == 2
        and down_maps.shape[0] == out_width
        and down_maps.shape[1] == n * up_maps.shape[0]
        and out_width % (128 * tp) == 0
        and out_width >= 4 * down_maps.shape[1]
        and args[1].shape[0] == 2 * args[0].shape[0] == down_maps.shape[1]
        and args[5].shape[1] * ADAPTER_RANK * n == 2 * down_maps.shape[1]
    )
    return (local_kernels if kernels_fit else local_plain)(*args)


def solution(mesh):
    in_specs = (
        P(("groups", "dp", "tensor"), None),
        P(("groups", "dp"), None),
        P("tensor", None),
        P(("groups", "dp"), None),
        P(("groups", "dp"), None),
        P("groups", None),
        P("groups", None),
        P("groups"),
        P("groups"),
    )
    out_specs = (
        P(("groups", "dp"), "tensor"),
        P(("groups", "dp"), None),
        P(("groups", "dp"), "tensor"),
    )
    return jax.shard_map(local, mesh=mesh, in_specs=in_specs, out_specs=out_specs, check_vma=False)
```

time: 35.9 us -> 47 us (1.31)
  Pallas kernels: 6.05 us -> 22.6 us
  local copies, waits for them, and re-layouts: 7.67 us -> 1.15 us
  waiting for transfers between devices: 5.31 us -> 6.65 us
    pallas_call x5 -> x4, Pallas kernels: 6.05 us -> 22.6 us  [the longest x1 17.2 us: local_kernels(): pl.pallas_call(functools.partial(pack_kernel, n, lay), out_shape=[message...]
    unnamed x22 -> x2, local copies, waits for them, and re-layouts: 7.67 us -> 1.15 us
    ppermute x6, waiting for transfers between devices: 0.02 us -> 0.88 us  [exchange(): lax.ppermute(message, 'tensor', [(0, 1), (1, 0)])]
  transfers between devices with their start and end apart: 15 -> 15, of which waited for: 5 -> 7; matrix products, arithmetic and copies ran while one was open for 0% -> 0% of each run, Pallas kernels for 11% -> 7%
where the time goes in v4:
time: 47 us; the launch traced here: 46.8 us
  Pallas kernels  22.6 us (48%)
  starting transfers between devices  15.6 us (33%)
  waiting for transfers between devices  6.65 us (14%)
  local copies, waits for them, and re-layouts  1.15 us (2%)
  between operations  0.7 us (1%)
    pallas_call x1, Pallas kernels, local_kernels(): pl.pallas_call(functools.partial(pack_kernel, n, lay), out_shape=[message...  17.2 us
    ppermute x8, starting transfers between devices, exchange(): lax.ppermute(message, ('dp', 'tensor'), [(2 * i + c, 2 * (i ^ step[c]) +...  14.5 us
    ppermute x8, waiting for transfers between devices, exchange(): lax.ppermute(message, ('dp', 'tensor'), [(2 * i + c, 2 * (i ^ step[c]) +...  5.76 us
    pallas_call x1, Pallas kernels, local_kernels(): pl.pallas_call(grad_x_kernel, out_shape=shape((tok_rows, half), bf16), in...  3.18 us
    pallas_call x1, Pallas kernels, local_kernels(): pl.pallas_call(functools.partial(middle_kernel, n, lay), out_shape=[shape...  1.26 us
    unnamed x2, local copies, waits for them, and re-layouts  1.15 us
    pallas_call x1, Pallas kernels, local_kernels(): pl.pallas_call(functools.partial(final_kernel, n, lay), out_shape=[shape(...  1.02 us
  transfers between devices with their start and end apart: 15, of which 7 were waited for; matrix products, arithmetic and copies ran while one was open for 0% of the time, Pallas kernels for 7%

profile of v4, /device:TPU:0, one launch (start us, length us, event | category | flops | bytes accessed | tf_op | source)
XLA Modules:
  0.0 46.8 jit_solution(11616750085290463072)
XLA Ops:
  0.6 17.2 %shard_map.112 = (bf16[48,512]{1,0:T(8,128)(2,1)}, bf16[48,512]{1,0:T(8,128)(2,1)}, bf16[48,512]{1,0:T(8,128)(2,1)}, bf16[48,512]{1,0:T(8,128)(2,1)}, bf16[816,512]{1,0:T(8,128)(2,1)}) custom-call(s32[2,8]{1,0:T(2,128)} %bitcast.2, s32[2,8]{1,0:T(2,128)} %bitcast.3, s32[8]{0:T(128)} %slot_hbm.1, s32[8]{0:T(128)} %count_hbm.1, bf16[128,512]{1,0:T(8,128)(2,1)} %g_hbm.1, ...), custom_call_target="tpu_custom_call" | custom-call | tf_op jit(solution)/shard_map/pallas_call | solution.py:252
  17.8 0.5 %collective-permute-start = (bf16[64,4096]{1,0:T(8,128)(2,1)}, bf16[64,4096]{1,0:T(8,128)(2,1)S(1)}, u32[]{:S(2)}, u32[]{:S(2)}) collective-permute-start(bf16[64,4096]{1,0:T(8,128)(2,1)} %x_hbm.1), channel_id=1, source_target_pairs={{0,1},{1,0},{2,3},{3,2},{4,5},{5,4},{6,7},{7,6},{8,9},{9,8},{10,11... | collective-permute-start | bytes 1572872 | tf_op jit(solution)/shard_map/ppermute | solution.py:278
  18.3 5.6 %collective-permute-start.1 = (bf16[48,512]{1,0:T(8,128)(2,1)}, bf16[48,512]{1,0:T(8,128)(2,1)S(1)}, u32[]{:S(2)}, u32[]{:S(2)}) collective-permute-start(bf16[48,512]{1,0:T(8,128)(2,1)} %get-tuple-element.29), channel_id=1, source_target_pairs={{0,14},{1,13},{2,12},{3,15},{4,10},{5,9},{6,8},{7,11},{8,6},{9,5},... | collective-permute-start | bytes 147464 | tf_op jit(solution)/shard_map/ppermute | solution.py:208
  24.0 0.0 collective-permute-start.2
  24.0 1.7 %collective-permute-start.3 = (bf16[48,512]{1,0:T(8,128)(2,1)}, bf16[48,512]{1,0:T(8,128)(2,1)S(1)}, u32[]{:S(2)}, u32[]{:S(2)}) collective-permute-start(bf16[48,512]{1,0:T(8,128)(2,1)} %get-tuple-element.31), channel_id=1, source_target_pairs={{0,6},{1,5},{2,4},{3,7},{4,2},{5,1},{6,0},{7,3},{8,14},{9,13},{10,... | collective-permute-start | bytes 147464 | tf_op jit(solution)/shard_map/ppermute | solution.py:208
  25.6 0.4 collective-permute-start.4
  26.1 0.6 %collective-permute-done.1.refs_0_ = bf16[48,512]{1,0:T(8,128)(2,1)S(1)} collective-permute-done((bf16[48,512]{1,0:T(8,128)(2,1)}, bf16[48,512]{1,0:T(8,128)(2,1)S(1)}, u32[]{:S(2)}, u32[]{:S(2)}) %collective-permute-start.1) | collective-permute-done | bytes 49184 | tf_op jit(solution)/shard_map/ppermute | solution.py:208
  26.7 0.0 collective-permute-start.5
  26.7 3.4 %collective-permute-done.2.refs_1_ = bf16[48,512]{1,0:T(8,128)(2,1)S(1)} collective-permute-done((bf16[48,512]{1,0:T(8,128)(2,1)}, bf16[48,512]{1,0:T(8,128)(2,1)S(1)}, u32[]{:S(2)}, u32[]{:S(2)}) %collective-permute-start.2) | collective-permute-done | bytes 49184 | tf_op jit(solution)/shard_map/ppermute | solution.py:208
  30.2 0.0 collective-permute-start.6
  30.2 0.0 collective-permute-done.3.refs_2_
  30.2 0.5 %collective-permute-start.7 = (bf16[48,512]{1,0:T(8,128)(2,1)S(1)}, bf16[48,512]{1,0:T(8,128)(2,1)S(1)}, u32[]{:S(2)}, u32[]{:S(2)}) collective-permute-start(bf16[48,512]{1,0:T(8,128)(2,1)S(1)} %collective-permute-done.3.refs_2_), channel_id=1, source_target_pairs={{0,1},{1,0},{2,3},{3,2},{4,5},{5,4},{6,7},{7,6},{8,9},{9,8},{10,11... | collective-permute-start | bytes 147464 | tf_op jit(solution)/shard_map/ppermute | solution.py:215
  30.7 0.0 collective-permute-done.4.refs_3_
  30.7 0.0 collective-permute-done.5.refs_4_
  30.7 0.7 %collective-permute-done.6.refs_5_ = bf16[48,512]{1,0:T(8,128)(2,1)S(1)} collective-permute-done((bf16[48,512]{1,0:T(8,128)(2,1)S(1)}, bf16[48,512]{1,0:T(8,128)(2,1)S(1)}, u32[]{:S(2)}, u32[]{:S(2)}) %collective-permute-start.6) | collective-permute-done | bytes 49184 | tf_op jit(solution)/shard_map/ppermute | solution.py:215
  31.4 0.2 collective-permute-done.7.refs_6_
  31.6 0.0 collective-permute-done.x_other
  31.6 0.0 copy-start
  31.6 1.1 %copy-done = bf16[816,512]{1,0:T(8,128)(2,1)S(1)} copy-done((bf16[816,512]{1,0:T(8,128)(2,1)S(1)}, bf16[816,512]{1,0:T(8,128)(2,1)}, u32[]{:S(2)}) %copy-start) | copy-done | bytes 835608
  32.7 1.3 %shard_map.113 = (bf16[128,32]{1,0:T(8,128)(2,1)S(1)}, bf16[4,32,512]{2,1,0:T(8,128)(2,1)S(1)}, bf16[256,512]{1,0:T(8,128)(2,1)S(1)}, bf16[48,512]{1,0:T(8,128)(...) custom-call(bf16[816,512]{1,0:T(8,128)(2,1)S(1)} %copy-done, ...), custom_call_target="tpu_custom_call" | custom-call | tf_op jit(solution)/shard_map/pallas_call | solution.py:280
  34.0 2.0 %collective-permute-start.8 = (bf16[48,512]{1,0:T(8,128)(2,1)S(1)}, bf16[48,512]{1,0:T(8,128)(2,1)S(1)}, u32[]{:S(2)}, u32[]{:S(2)}) collective-permute-start(bf16[48,512]{1,0:T(8,128)(2,1)S(1)} %get-tuple-element.37), channel_id=1, source_target_pairs={{0,14},{1,13},{2,12},{3,15},{4,10},{5,9},{6,8},{7,11},{8,6},{9,5},... | collective-permute-start | bytes 147464 | tf_op jit(solution)/shard_map/ppermute | solution.py:208
  36.0 0.8 %collective-permute-start.9 = (bf16[48,512]{1,0:T(8,128)(2,1)S(1)}, bf16[48,512]{1,0:T(8,128)(2,1)S(1)}, u32[]{:S(2)}, u32[]{:S(2)}) collective-permute-start(bf16[48,512]{1,0:T(8,128)(2,1)S(1)} %get-tuple-element.38), channel_id=1, source_target_pairs={{0,10},{1,9},{2,8},{3,11},{4,14},{5,13},{6,12},{7,15},{8,2},{9,1},... | collective-permute-start | bytes 147464 | tf_op jit(solution)/shard_map/ppermute | solution.py:208
  36.8 2.5 %collective-permute-start.10 = (bf16[48,512]{1,0:T(8,128)(2,1)S(1)}, bf16[48,512]{1,0:T(8,128)(2,1)S(1)}, u32[]{:S(2)}, u32[]{:S(2)}) collective-permute-start(bf16[48,512]{1,0:T(8,128)(2,1)S(1)} %get-tuple-element.39), channel_id=1, source_target_pairs={{0,6},{1,5},{2,4},{3,7},{4,2},{5,1},{6,0},{7,3},{8,14},{9,13},{10,... | collective-permute-start | bytes 147464 | tf_op jit(solution)/shard_map/ppermute | solution.py:208
  39.3 1.5 %collective-permute-start.11 = (bf16[48,512]{1,0:T(8,128)(2,1)S(1)}, bf16[48,512]{1,0:T(8,128)(2,1)S(1)}, u32[]{:S(2)}, u32[]{:S(2)}) collective-permute-start(bf16[48,512]{1,0:T(8,128)(2,1)S(1)} %get-tuple-element.40), channel_id=1, source_target_pairs={{0,2},{1,3},{2,0},{3,1},{4,6},{5,7},{6,4},{7,5},{8,10},{9,11},{10,... | collective-permute-start | bytes 147464 | tf_op jit(solution)/shard_map/ppermute | solution.py:208
  40.8 0.7 %collective-permute-done.8.refs_1_ = bf16[48,512]{1,0:T(8,128)(2,1)S(1)} collective-permute-done((bf16[48,512]{1,0:T(8,128)(2,1)S(1)}, bf16[48,512]{1,0:T(8,128)(2,1)S(1)}, u32[]{:S(2)}, u32[]{:S(2)}) %collective-permute-start.8) | collective-permute-done | bytes 49184 | tf_op jit(solution)/shard_map/ppermute | solution.py:208
  41.4 0.0 collective-permute-start.12
  41.5 0.6 %collective-permute-done.9.refs_2_ = bf16[48,512]{1,0:T(8,128)(2,1)S(1)} collective-permute-done((bf16[48,512]{1,0:T(8,128)(2,1)S(1)}, bf16[48,512]{1,0:T(8,128)(2,1)S(1)}, u32[]{:S(2)}, u32[]{:S(2)}) %collective-permute-start.9) | collective-permute-done | bytes 49184 | tf_op jit(solution)/shard_map/ppermute | solution.py:208
  42.0 0.0 collective-permute-start.13
  42.0 0.4 collective-permute-done.10.refs_3_
  42.4 0.1 collective-permute-start.14
  42.5 3.2 %shard_map.114 = bf16[128,2048]{1,0:T(8,128)(2,1)} custom-call(bf16[256,512]{1,0:T(8,128)(2,1)S(1)} %get-tuple-element.33.kept_ref, bf16[2048,512]{1,0:T(8,128)(2,1)} %w_hbm.1, bf16[128,32]{1,0:T(8,128)(2,1)S(1)} %get-tuple-element.34.dlow_ref, bf16[4,32,512]{2,1,0:T(8,128)(2,1)S(1)} %get-tuple-element.35.a_ref), custom_call_target="tpu_custom_call" | custom-call | flops 285212672 | bytes 2621440 | tf_op jit(solution)/shard_map/pallas_call | solution.py:299
  45.7 0.0 collective-permute-done.11.refs_4_
  45.7 0.0 collective-permute-done.12.refs_5_
  45.7 0.0 collective-permute-done.13.refs_6_
  45.7 0.0 collective-permute-done.14.refs_7_
  45.7 1.0 %shard_map.115 = (f32[512,128]{1,0:T(8,128)}, f32[16,256]{1,0:T(8,128)}) custom-call(bf16[256,512]{1,0:T(8,128)(2,1)S(1)} %get-tuple-element.33.kept_ref, bf16[48,512]{1,0:T(8,128)(2,1)S(1)} %get-tuple-element.36.refs_0_, bf16[48,512]{1,0:T(8,128)(2,1)S(1)} %collective-permute-done.8.refs_1_, bf16[48,512]{1,0:T(8,128)(2,1)S(1)} %collective-permute-done.9.refs_2_, ...), custom_call_target="tpu_custom_call" | custom-call | tf_op jit(solution)/shard_map/pallas_call | solution.py:317
Async XLA Ops:
  17.8 13.7 %collective-permute-start = (bf16[64,4096]{1,0:T(8,128)(2,1)}, bf16[64,4096]{1,0:T(8,128)(2,1)S(1)}, u32[]{:S(2)}, u32[]{:S(2)}) collective-permute-start(bf16[64,4096]{1,0:T(8,128)(2,1)} %x_hbm.1), channel_id=1, source_target_pairs={{0,1},{1,0},{2,3},{3,2},{4,5},{5,4},{6,7},{7,6},{8,9},{9,8},{10,11... | collective-permute-start | bytes 1572872 | tf_op jit(solution)/shard_map/ppermute | solution.py:278
  18.3 8.4 %collective-permute-start.1 = (bf16[48,512]{1,0:T(8,128)(2,1)}, bf16[48,512]{1,0:T(8,128)(2,1)S(1)}, u32[]{:S(2)}, u32[]{:S(2)}) collective-permute-start(bf16[48,512]{1,0:T(8,128)(2,1)} %get-tuple-element.29), channel_id=1, source_target_pairs={{0,14},{1,13},{2,12},{3,15},{4,10},{5,9},{6,8},{7,11},{8,6},{9,5},... | collective-permute-start | bytes 147464 | tf_op jit(solution)/shard_map/ppermute | solution.py:208
  24.0 6.2 %collective-permute-start.2 = (bf16[48,512]{1,0:T(8,128)(2,1)}, bf16[48,512]{1,0:T(8,128)(2,1)S(1)}, u32[]{:S(2)}, u32[]{:S(2)}) collective-permute-start(bf16[48,512]{1,0:T(8,128)(2,1)} %get-tuple-element.30), channel_id=1, source_target_pairs={{0,10},{1,9},{2,8},{3,11},{4,14},{5,13},{6,12},{7,15},{8,2},{9,1},... | collective-permute-start | bytes 147464 | tf_op jit(solution)/shard_map/ppermute | solution.py:208
  24.0 6.2 %collective-permute-start.3 = (bf16[48,512]{1,0:T(8,128)(2,1)}, bf16[48,512]{1,0:T(8,128)(2,1)S(1)}, u32[]{:S(2)}, u32[]{:S(2)}) collective-permute-start(bf16[48,512]{1,0:T(8,128)(2,1)} %get-tuple-element.31), channel_id=1, source_target_pairs={{0,6},{1,5},{2,4},{3,7},{4,2},{5,1},{6,0},{7,3},{8,14},{9,13},{10,... | collective-permute-start | bytes 147464 | tf_op jit(solution)/shard_map/ppermute | solution.py:208
  25.6 5.0 %collective-permute-start.4 = (bf16[48,512]{1,0:T(8,128)(2,1)}, bf16[48,512]{1,0:T(8,128)(2,1)S(1)}, u32[]{:S(2)}, u32[]{:S(2)}) collective-permute-start(bf16[48,512]{1,0:T(8,128)(2,1)} %get-tuple-element.32), channel_id=1, source_target_pairs={{0,2},{1,3},{2,0},{3,1},{4,6},{5,7},{6,4},{7,5},{8,10},{9,11},{10,... | collective-permute-start | bytes 147464 | tf_op jit(solution)/shard_map/ppermute | solution.py:208
  26.7 4.0 %collective-permute-start.5 = (bf16[48,512]{1,0:T(8,128)(2,1)S(1)}, bf16[48,512]{1,0:T(8,128)(2,1)S(1)}, u32[]{:S(2)}, u32[]{:S(2)}) collective-permute-start(bf16[48,512]{1,0:T(8,128)(2,1)S(1)} %collective-permute-done.1.refs_0_), channel_id=1, source_target_pairs={{0,1},{1,0},{2,3},{3,2},{4,5},{5,4},{6,7},{7,6},{8,9},{9,8},{10,11... | collective-permute-start | bytes 147464 | tf_op jit(solution)/shard_map/ppermute | solution.py:215
  30.2 1.2 %collective-permute-start.6 = (bf16[48,512]{1,0:T(8,128)(2,1)S(1)}, bf16[48,512]{1,0:T(8,128)(2,1)S(1)}, u32[]{:S(2)}, u32[]{:S(2)}) collective-permute-start(bf16[48,512]{1,0:T(8,128)(2,1)S(1)} %collective-permute-done.2.refs_1_), channel_id=1, source_target_pairs={{0,1},{1,0},{2,3},{3,2},{4,5},{5,4},{6,7},{7,6},{8,9},{9,8},{10,11... | collective-permute-start | bytes 147464 | tf_op jit(solution)/shard_map/ppermute | solution.py:215
  30.2 1.4 %collective-permute-start.7 = (bf16[48,512]{1,0:T(8,128)(2,1)S(1)}, bf16[48,512]{1,0:T(8,128)(2,1)S(1)}, u32[]{:S(2)}, u32[]{:S(2)}) collective-permute-start(bf16[48,512]{1,0:T(8,128)(2,1)S(1)} %collective-permute-done.3.refs_2_), channel_id=1, source_target_pairs={{0,1},{1,0},{2,3},{3,2},{4,5},{5,4},{6,7},{7,6},{8,9},{9,8},{10,11... | collective-permute-start | bytes 147464 | tf_op jit(solution)/shard_map/ppermute | solution.py:215
  31.6 1.2 %copy-start = (bf16[816,512]{1,0:T(8,128)(2,1)S(1)}, bf16[816,512]{1,0:T(8,128)(2,1)}, u32[]{:S(2)}) copy-start(bf16[816,512]{1,0:T(8,128)(2,1)} %get-tuple-element.23.stage) | copy-start | bytes 2506756
  34.0 7.5 %collective-permute-start.8 = (bf16[48,512]{1,0:T(8,128)(2,1)S(1)}, bf16[48,512]{1,0:T(8,128)(2,1)S(1)}, u32[]{:S(2)}, u32[]{:S(2)}) collective-permute-start(bf16[48,512]{1,0:T(8,128)(2,1)S(1)} %get-tuple-element.37), channel_id=1, source_target_pairs={{0,14},{1,13},{2,12},{3,15},{4,10},{5,9},{6,8},{7,11},{8,6},{9,5},... | collective-permute-start | bytes 147464 | tf_op jit(solution)/shard_map/ppermute | solution.py:208
  36.0 6.0 %collective-permute-start.9 = (bf16[48,512]{1,0:T(8,128)(2,1)S(1)}, bf16[48,512]{1,0:T(8,128)(2,1)S(1)}, u32[]{:S(2)}, u32[]{:S(2)}) collective-permute-start(bf16[48,512]{1,0:T(8,128)(2,1)S(1)} %get-tuple-element.38), channel_id=1, source_target_pairs={{0,10},{1,9},{2,8},{3,11},{4,14},{5,13},{6,12},{7,15},{8,2},{9,1},... | collective-permute-start | bytes 147464 | tf_op jit(solution)/shard_map/ppermute | solution.py:208
  36.8 5.7 %collective-permute-start.10 = (bf16[48,512]{1,0:T(8,128)(2,1)S(1)}, bf16[48,512]{1,0:T(8,128)(2,1)S(1)}, u32[]{:S(2)}, u32[]{:S(2)}) collective-permute-start(bf16[48,512]{1,0:T(8,128)(2,1)S(1)} %get-tuple-element.39), channel_id=1, source_target_pairs={{0,6},{1,5},{2,4},{3,7},{4,2},{5,1},{6,0},{7,3},{8,14},{9,13},{10,... | collective-permute-start | bytes 147464 | tf_op jit(solution)/shard_map/ppermute | solution.py:208
  39.3 6.4 %collective-permute-start.11 = (bf16[48,512]{1,0:T(8,128)(2,1)S(1)}, bf16[48,512]{1,0:T(8,128)(2,1)S(1)}, u32[]{:S(2)}, u32[]{:S(2)}) collective-permute-start(bf16[48,512]{1,0:T(8,128)(2,1)S(1)} %get-tuple-element.40), channel_id=1, source_target_pairs={{0,2},{1,3},{2,0},{3,1},{4,6},{5,7},{6,4},{7,5},{8,10},{9,11},{10,... | collective-permute-start | bytes 147464 | tf_op jit(solution)/shard_map/ppermute | solution.py:208
  41.4 4.3 %collective-permute-start.12 = (bf16[48,512]{1,0:T(8,128)(2,1)S(1)}, bf16[48,512]{1,0:T(8,128)(2,1)S(1)}, u32[]{:S(2)}, u32[]{:S(2)}) collective-permute-start(bf16[48,512]{1,0:T(8,128)(2,1)S(1)} %collective-permute-done.8.refs_1_), channel_id=1, source_target_pairs={{0,1},{1,0},{2,3},{3,2},{4,5},{5,4},{6,7},{7,6},{8,9},{9,8},{10,11... | collective-permute-start | bytes 147464 | tf_op jit(solution)/shard_map/ppermute | solution.py:215
  42.0 3.7 %collective-permute-start.13 = (bf16[48,512]{1,0:T(8,128)(2,1)S(1)}, bf16[48,512]{1,0:T(8,128)(2,1)S(1)}, u32[]{:S(2)}, u32[]{:S(2)}) collective-permute-start(bf16[48,512]{1,0:T(8,128)(2,1)S(1)} %collective-permute-done.9.refs_2_), channel_id=1, source_target_pairs={{0,1},{1,0},{2,3},{3,2},{4,5},{5,4},{6,7},{7,6},{8,9},{9,8},{10,11... | collective-permute-start | bytes 147464 | tf_op jit(solution)/shard_map/ppermute | solution.py:215
  42.4 3.3 %collective-permute-start.14 = (bf16[48,512]{1,0:T(8,128)(2,1)S(1)}, bf16[48,512]{1,0:T(8,128)(2,1)S(1)}, u32[]{:S(2)}, u32[]{:S(2)}) collective-permute-start(bf16[48,512]{1,0:T(8,128)(2,1)S(1)} %collective-permute-done.10.refs_3_), channel_id=1, source_target_pairs={{0,1},{1,0},{2,3},{3,2},{4,5},{5,4},{6,7},{7,6},{8,9},{9,8},{10,11... | collective-permute-start | bytes 147464 | tf_op jit(solution)/shard_map/ppermute | solution.py:215

commit v5 on v4

--- a/solution.py
+++ b/solution.py
@@ -85,15 +85,15 @@
 
 def pack_kernel(n, lay, start_hbm, chosen_hbm, slot_hbm, count_hbm, g_hbm, x_hbm, down_hbm, up_hbm, *refs):
     count = n // 2 + 1
-    send, stage = refs[: count - 1], refs[count - 1]
-    start_ref, chosen_ref, slot_ref, count_ref, down_ref, up_ref, out_ref, extra_ref, sems = refs[count:]
+    send, stage_hbm = refs[: count - 1], refs[count - 1]
+    start_ref, chosen_ref, slot_ref, count_ref, down_ref, up_ref, out_ref, stage, sems = refs[count:]
     width = down_hbm.shape[0]
     rows, picked, slots = lay.rows, lay.picked, lay.slots
     tables = start_all(
         [chosen_hbm, slot_hbm, start_hbm, count_hbm], [chosen_ref, slot_ref, start_ref, count_ref], sems
     )
     maps = start_all([down_hbm, up_hbm], [down_ref, up_ref], sems, 4)
-    gradient = start_all([g_hbm], [extra_ref.at[pl.ds(0, rows)]], sems, 6)
+    gradient = start_all([g_hbm], [stage.at[pl.ds(lay.g, rows)]], sems, 6)
     tokens = start_all(
         [x_hbm.at[:, pl.ds(q * width, width)] for q in range(n)],
         [stage.at[lay.x(q)] for q in range(n)],
@@ -106,29 +106,37 @@
     onehot = slot_rows(chosen_ref, slot_ref, ranks, slots)
     wait_all(maps)
     columns = dot(onehot, down_ref[...], 1, 1).astype(bf16)
-    for k in range(count):
-        out_ref[k, :picked, :] = columns[k * picked : (k + 1) * picked]
-        out_ref[k, picked:, :] = up_ref[...]
-    done = start_all([out_ref.at[k] for k in range(1, count)], send, sems, 7 + n)
-    own = stage.at[pl.ds(lay.message, picked + ADAPTER_RANK)]
-    done += start_all([out_ref.at[0]], [own], sems, 6 + n + count)
+    for k in range(1, count):
+        out_ref[k - 1, :picked, :] = columns[k * picked : (k + 1) * picked]
+        out_ref[k - 1, picked:, :] = up_ref[...]
+    done = start_all([out_ref.at[k] for k in range(count - 1)], send, sems, 7 + n)
+    stage[lay.message : lay.message + picked, :] = columns[:picked]
+    stage[lay.message + picked :, :] = up_ref[...]
 
     position = lax.broadcasted_iota(i32, (rows, slots), 0)
     group = lax.broadcasted_iota(i32, (rows, slots), 1) // ADAPTER_RANK
     segment = jnp.full((rows, slots), -1, i32)
-    for k in range(start_ref.shape[0]):
+    segs = start_ref.shape[0]
+    for k in range(segs):
         segment += jnp.where(position >= start_ref[k, me], 1, 0)
-    extra_ref[rows:, :slots] = jnp.where(segment == group, 1.0, 0.0).astype(bf16)
-    extra_ref[rows : rows + picked, slots : 2 * slots] = onehot[:picked]
+    flag = (segment == group) | ((group == segs) & (position < count_ref[me]))
+    stage[lay.mask : lay.mask + rows, :slots] = jnp.where(flag, 1.0, 0.0).astype(bf16)
+    stage[lay.mask : lay.mask + picked, slots : 2 * slots] = onehot[:picked]
     every = slot_rows(chosen_ref, slot_ref, range(n), slots)
     for k in range(n * picked // rows):
-        extra_ref[rows:, (2 + k) * slots : (3 + k) * slots] = every[k * rows : (k + 1) * rows]
+        at = pl.ds((2 + k) * slots, slots)
+        stage[lay.mask : lay.mask + rows, at] = every[k * rows : (k + 1) * rows]
     wait_all(gradient)
     live = lax.broadcasted_iota(i32, (rows, width), 0) < count_ref[me]
-    g = extra_ref[:rows, :]
-    extra_ref[:rows, :] = jnp.where(live, g, jnp.zeros_like(g))
-    done += start_all([extra_ref], [stage.at[pl.ds(lay.g, 2 * rows)]], sems, 7 + n + count)
-    wait_all(tokens + done)
+    g = stage[lay.g : lay.g + rows, :]
+    stage[lay.g : lay.g + rows, :] = jnp.where(live, g, jnp.zeros_like(g))
+    wait_all(tokens)
+    done += start_all([stage], [stage_hbm], sems, 6 + n + count)
+    wait_all(done)
+
+
+def hand_on_kernel(stage, out_ref):
+    out_ref[...] = stage[...]
 
 
 def middle_kernel(n, lay, stage, x_other, *refs):
@@ -174,18 +182,16 @@
         message[picked:, :] = up_ref[target]
 
 
-def grad_x_kernel(kept_ref, w_hbm, dlow_ref, a_ref, out_hbm, w_ref, out_ref, sems):
+def grad_x_kernel(kept_ref, base_ref, dlow_ref, a_ref, out_hbm, out_ref, sems):
     steps, picked, width = a_ref.shape
-    blocks = [pl.ds(j * width, width) for j in range(steps)]
-    weights = start_all([w_hbm.at[k] for k in blocks], [w_ref.at[k] for k in blocks], sems)
-    g = kept_ref[: out_ref.shape[0], :]
+    rows = out_ref.shape[0]
+    live = kept_ref[rows:, picked : picked + 1].astype(f32) > 0.0
     done = []
-    for j, at in enumerate(blocks):
-        total = dot(dlow_ref[...], a_ref[j], 1, 0)
-        weights[j].wait()
-        total += dot(g, w_ref[at, :], 1, 1)
+    for j in range(steps):
+        at = pl.ds(j * width, width)
+        total = jnp.where(live, base_ref[:, at], 0.0) + dot(dlow_ref[...], a_ref[j], 1, 0)
         out_ref[:, at] = total.astype(bf16)
-        done += start_all([out_ref.at[:, at]], [out_hbm.at[:, at]], sems, steps + j)
+        done += start_all([out_ref.at[:, at]], [out_hbm.at[:, at]], sems, j)
     wait_all(done)
 
 
@@ -258,9 +264,9 @@
         + [
             pltpu.VMEM(down_maps.shape, bf16),
             pltpu.VMEM(up_maps.shape, bf16),
-            pltpu.VMEM((count,) + message.shape, bf16),
-            pltpu.VMEM((2 * tok_rows, out_width), bf16),
-            dma((8 + n + count,)),
+            pltpu.VMEM((count - 1,) + message.shape, bf16),
+            pltpu.VMEM(lay.shape, bf16),
+            dma((7 + n + count,)),
         ],
         compiler_params=params(56),
     )(
@@ -276,6 +282,15 @@
     sent, x_late = lax.optimization_barrier((sent, inputs))
     got = exchange(sent)
     x_other = lax.ppermute(x_late, "tensor", [(0, 1), (1, 0)])
+    stage = pl.pallas_call(
+        hand_on_kernel,
+        out_shape=shape(lay.shape, bf16),
+        in_specs=[VMEM],
+        out_specs=VMEM,
+        compiler_params=params(8),
+        cost_estimate=pl.CostEstimate(flops=0, bytes_accessed=1 << 21, transcendentals=0),
+    )(stage)
+    base = dot(output_gradient, frozen_weight, 1, 1)
 
     dlow, a_half, kept, own, *sent = pl.pallas_call(
         functools.partial(middle_kernel, n, lay),
@@ -299,20 +314,16 @@
     grad_x = pl.pallas_call(
         grad_x_kernel,
         out_shape=shape((tok_rows, half), bf16),
-        in_specs=[VMEM, HBM, VMEM, VMEM],
+        in_specs=[VMEM] * 4,
         out_specs=HBM,
-        scratch_shapes=[
-            pltpu.VMEM(frozen_weight.shape, bf16),
-            pltpu.VMEM((tok_rows, half), bf16),
-            dma((n,)),
-        ],
-        compiler_params=params(52),
+        scratch_shapes=[pltpu.VMEM((tok_rows, half), bf16), dma((n // 2,))],
+        compiler_params=params(8),
         cost_estimate=pl.CostEstimate(
-            flops=2 * tok_rows * half * (out_width + picked),
-            bytes_accessed=2 * half * (out_width + tok_rows),
+            flops=2 * tok_rows * half * picked,
+            bytes_accessed=6 * half * tok_rows,
             transcendentals=0,
         ),
-    )(kept, frozen_weight, dlow, a_half)
+    )(kept, base, dlow, a_half)
 
     grad_a, up_map_gradient = pl.pallas_call(
         functools.partial(final_kernel, n, lay),

time: 47 us -> 30 us (0.64)
  Pallas kernels: 22.6 us -> 5.75 us
  waiting for transfers between devices: 6.65 us -> 5.52 us
  matrix products: 0 us -> 0.8 us
    pallas_call x1, Pallas kernels: 17.2 us -> 2.42 us  [local_kernels(): pl.pallas_call(functools.partial(pack_kernel, n, lay), out_shape=[message...]
    pallas_call x1, Pallas kernels: 3.18 us -> 0.99 us  [local_kernels(): pl.pallas_call(grad_x_kernel, out_shape=shape((tok_rows, half), bf16), in...]
    ppermute x6, waiting for transfers between devices: 0.88 us -> 0.02 us  [exchange(): lax.ppermute(message, 'tensor', [(0, 1), (1, 0)])]
    dot_general x0 -> x1, matrix products: none -> 0.8 us  [dot(): lax.dot_general(a, b, (((ca,), (cb,)), ((), ())), preferred_element_type=...]
    unnamed x2 -> x6, local copies, waits for them, and re-layouts: 1.15 us -> 1.16 us
  transfers between devices with their start and end apart: 15 -> 15, of which waited for: 7 -> 5; matrix products, arithmetic and copies ran while one was open for 0% -> 3% of each run, Pallas kernels for 7% -> 3%
where the time goes in v5:
time: 30 us; the launch traced here: 29.8 us
  starting transfers between devices  15.8 us (53%)
  Pallas kernels  5.75 us (19%)
  waiting for transfers between devices  5.52 us (18%)
  local copies, waits for them, and re-layouts  1.16 us (4%)
  matrix products  0.8 us (3%)
  between operations  0.77 us (3%)
    ppermute x8, starting transfers between devices, exchange(): lax.ppermute(message, ('dp', 'tensor'), [(2 * i + c, 2 * (i ^ step[c]) +...  14.5 us
    ppermute x8, waiting for transfers between devices, exchange(): lax.ppermute(message, ('dp', 'tensor'), [(2 * i + c, 2 * (i ^ step[c]) +...  5.5 us
    pallas_call x1, Pallas kernels, local_kernels(): pl.pallas_call(functools.partial(pack_kernel, n, lay), out_shape=[message...  2.42 us
    pallas_call x1, Pallas kernels, local_kernels(): pl.pallas_call(functools.partial(middle_kernel, n, lay), out_shape=[shape...  1.26 us
    unnamed x6, local copies, waits for them, and re-layouts  1.16 us
    pallas_call x1, Pallas kernels, local_kernels(): pl.pallas_call(functools.partial(final_kernel, n, lay), out_shape=[shape(...  1.02 us
    pallas_call x1, Pallas kernels, local_kernels(): pl.pallas_call(grad_x_kernel, out_shape=shape((tok_rows, half), bf16), in...  0.99 us
    dot_general x1, matrix products, dot(): lax.dot_general(a, b, (((ca,), (cb,)), ((), ())), preferred_element_type=...  0.8 us
  transfers between devices with their start and end apart: 15, of which 5 were waited for; matrix products, arithmetic and copies ran while one was open for 3% of the time, Pallas kernels for 3%

profile of v5, /device:TPU:0, one launch (start us, length us, event | category | flops | bytes accessed | tf_op | source)
XLA Modules:
  0.0 29.8 jit_solution(12362173723571438907)
XLA Ops:
  0.6 0.0 copy-start
  0.6 0.0 copy-start.2
  0.7 2.4 %shard_map.112 = (bf16[48,512]{1,0:T(8,128)(2,1)}, bf16[48,512]{1,0:T(8,128)(2,1)}, bf16[48,512]{1,0:T(8,128)(2,1)}, bf16[48,512]{1,0:T(8,128)(2,1)}, bf16[816,512]{1,0:T(8,128)(2,1)}) custom-call(s32[2,8]{1,0:T(2,128)} %bitcast.4, s32[2,8]{1,0:T(2,128)} %bitcast.5, s32[8]{0:T(128)} %slot_hbm.1, s32[8]{0:T(128)} %count_hbm.1, bf16[128,512]{1,0:T(8,128)(2,1)} %g_hbm.1, ...), custom_call_target="tpu_custom_call" | custom-call | tf_op jit(solution)/shard_map/pallas_call | solution.py:258
  3.1 0.5 %collective-permute-start = (bf16[64,4096]{1,0:T(8,128)(2,1)}, bf16[64,4096]{1,0:T(8,128)(2,1)S(1)}, u32[]{:S(2)}, u32[]{:S(2)}) collective-permute-start(bf16[64,4096]{1,0:T(8,128)(2,1)} %x_hbm.1), channel_id=1, source_target_pairs={{0,1},{1,0},{2,3},{3,2},{4,5},{5,4},{6,7},{7,6},{8,9},{9,8},{10,11... | collective-permute-start | bytes 1572872 | tf_op jit(solution)/shard_map/ppermute | solution.py:284
  3.6 5.6 %collective-permute-start.1 = (bf16[48,512]{1,0:T(8,128)(2,1)}, bf16[48,512]{1,0:T(8,128)(2,1)S(1)}, u32[]{:S(2)}, u32[]{:S(2)}) collective-permute-start(bf16[48,512]{1,0:T(8,128)(2,1)} %get-tuple-element.29), channel_id=1, source_target_pairs={{0,14},{1,13},{2,12},{3,15},{4,10},{5,9},{6,8},{7,11},{8,6},{9,5},... | collective-permute-start | bytes 147464 | tf_op jit(solution)/shard_map/ppermute | solution.py:214
  9.2 0.0 collective-permute-start.2
  9.2 1.7 %collective-permute-start.3 = (bf16[48,512]{1,0:T(8,128)(2,1)}, bf16[48,512]{1,0:T(8,128)(2,1)S(1)}, u32[]{:S(2)}, u32[]{:S(2)}) collective-permute-start(bf16[48,512]{1,0:T(8,128)(2,1)} %get-tuple-element.31), channel_id=1, source_target_pairs={{0,6},{1,5},{2,4},{3,7},{4,2},{5,1},{6,0},{7,3},{8,14},{9,13},{10,... | collective-permute-start | bytes 147464 | tf_op jit(solution)/shard_map/ppermute | solution.py:214
  10.9 0.4 %collective-permute-start.4 = (bf16[48,512]{1,0:T(8,128)(2,1)}, bf16[48,512]{1,0:T(8,128)(2,1)S(1)}, u32[]{:S(2)}, u32[]{:S(2)}) collective-permute-start(bf16[48,512]{1,0:T(8,128)(2,1)} %get-tuple-element.32), channel_id=1, source_target_pairs={{0,2},{1,3},{2,0},{3,1},{4,6},{5,7},{6,4},{7,5},{8,10},{9,11},{10,... | collective-permute-start | bytes 147464 | tf_op jit(solution)/shard_map/ppermute | solution.py:214
  11.3 0.7 %collective-permute-done.1.refs_0_ = bf16[48,512]{1,0:T(8,128)(2,1)S(1)} collective-permute-done((bf16[48,512]{1,0:T(8,128)(2,1)}, bf16[48,512]{1,0:T(8,128)(2,1)S(1)}, u32[]{:S(2)}, u32[]{:S(2)}) %collective-permute-start.1) | collective-permute-done | bytes 49184 | tf_op jit(solution)/shard_map/ppermute | solution.py:214
  12.0 0.0 collective-permute-start.5
  12.0 3.4 %collective-permute-done.2.refs_1_ = bf16[48,512]{1,0:T(8,128)(2,1)S(1)} collective-permute-done((bf16[48,512]{1,0:T(8,128)(2,1)}, bf16[48,512]{1,0:T(8,128)(2,1)S(1)}, u32[]{:S(2)}, u32[]{:S(2)}) %collective-permute-start.2) | collective-permute-done | bytes 49184 | tf_op jit(solution)/shard_map/ppermute | solution.py:214
  15.4 0.0 collective-permute-start.6
  15.4 0.0 collective-permute-done.3.refs_2_
  15.4 0.5 %collective-permute-start.7 = (bf16[48,512]{1,0:T(8,128)(2,1)S(1)}, bf16[48,512]{1,0:T(8,128)(2,1)S(1)}, u32[]{:S(2)}, u32[]{:S(2)}) collective-permute-start(bf16[48,512]{1,0:T(8,128)(2,1)S(1)} %collective-permute-done.3.refs_2_), channel_id=1, source_target_pairs={{0,1},{1,0},{2,3},{3,2},{4,5},{5,4},{6,7},{7,6},{8,9},{9,8},{10,11... | collective-permute-start | bytes 147464 | tf_op jit(solution)/shard_map/ppermute | solution.py:221
  15.9 0.0 copy-start.1
  15.9 1.1 %copy-done.1 = bf16[816,512]{1,0:T(8,128)(2,1)S(1)} copy-done((bf16[816,512]{1,0:T(8,128)(2,1)S(1)}, bf16[816,512]{1,0:T(8,128)(2,1)}, u32[]{:S(2)}) %copy-start.1) | copy-done | bytes 835608
  17.1 0.1 shard_map.113.stage
  17.1 0.0 collective-permute-done.4.refs_3_
  17.2 0.0 collective-permute-done.5.refs_4_
  17.2 0.0 collective-permute-done.6.refs_5_
  17.2 0.0 collective-permute-done.7.refs_6_
  17.2 0.0 collective-permute-done.x_other
  17.2 1.3 %shard_map.114 = (bf16[128,32]{1,0:T(8,128)(2,1)S(1)}, bf16[4,32,512]{2,1,0:T(8,128)(2,1)S(1)}, bf16[256,512]{1,0:T(8,128)(2,1)S(1)}, bf16[48,512]{1,0:T(8,128)(...) custom-call(bf16[816,512]{1,0:T(8,128)(2,1)S(1)} %shard_map.113.stag, ...), custom_call_target="tpu_custom_call" | custom-call | tf_op jit(solution)/shard_map/pallas_call | solution.py:295
  18.5 1.8 %collective-permute-start.8 = (bf16[48,512]{1,0:T(8,128)(2,1)S(1)}, bf16[48,512]{1,0:T(8,128)(2,1)S(1)}, u32[]{:S(2)}, u32[]{:S(2)}) collective-permute-start(bf16[48,512]{1,0:T(8,128)(2,1)S(1)} %get-tuple-element.37), channel_id=1, source_target_pairs={{0,14},{1,13},{2,12},{3,15},{4,10},{5,9},{6,8},{7,11},{8,6},{9,5},... | collective-permute-start | bytes 147464 | tf_op jit(solution)/shard_map/ppermute | solution.py:214
  20.3 0.6 %collective-permute-start.9 = (bf16[48,512]{1,0:T(8,128)(2,1)S(1)}, bf16[48,512]{1,0:T(8,128)(2,1)S(1)}, u32[]{:S(2)}, u32[]{:S(2)}) collective-permute-start(bf16[48,512]{1,0:T(8,128)(2,1)S(1)} %get-tuple-element.38), channel_id=1, source_target_pairs={{0,10},{1,9},{2,8},{3,11},{4,14},{5,13},{6,12},{7,15},{8,2},{9,1},... | collective-permute-start | bytes 147464 | tf_op jit(solution)/shard_map/ppermute | solution.py:214
  20.9 2.8 %collective-permute-start.10 = (bf16[48,512]{1,0:T(8,128)(2,1)S(1)}, bf16[48,512]{1,0:T(8,128)(2,1)S(1)}, u32[]{:S(2)}, u32[]{:S(2)}) collective-permute-start(bf16[48,512]{1,0:T(8,128)(2,1)S(1)} %get-tuple-element.39), channel_id=1, source_target_pairs={{0,6},{1,5},{2,4},{3,7},{4,2},{5,1},{6,0},{7,3},{8,14},{9,13},{10,... | collective-permute-start | bytes 147464 | tf_op jit(solution)/shard_map/ppermute | solution.py:214
  23.7 1.5 %collective-permute-start.11 = (bf16[48,512]{1,0:T(8,128)(2,1)S(1)}, bf16[48,512]{1,0:T(8,128)(2,1)S(1)}, u32[]{:S(2)}, u32[]{:S(2)}) collective-permute-start(bf16[48,512]{1,0:T(8,128)(2,1)S(1)} %get-tuple-element.40), channel_id=1, source_target_pairs={{0,2},{1,3},{2,0},{3,1},{4,6},{5,7},{6,4},{7,5},{8,10},{9,11},{10,... | collective-permute-start | bytes 147464 | tf_op jit(solution)/shard_map/ppermute | solution.py:214
  25.3 0.7 %collective-permute-done.8.refs_1_ = bf16[48,512]{1,0:T(8,128)(2,1)S(1)} collective-permute-done((bf16[48,512]{1,0:T(8,128)(2,1)S(1)}, bf16[48,512]{1,0:T(8,128)(2,1)S(1)}, u32[]{:S(2)}, u32[]{:S(2)}) %collective-permute-start.8) | collective-permute-done | bytes 49184 | tf_op jit(solution)/shard_map/ppermute | solution.py:214
  26.0 0.0 collective-permute-start.12
  26.0 0.4 %collective-permute-done.9.refs_2_ = bf16[48,512]{1,0:T(8,128)(2,1)S(1)} collective-permute-done((bf16[48,512]{1,0:T(8,128)(2,1)S(1)}, bf16[48,512]{1,0:T(8,128)(2,1)S(1)}, u32[]{:S(2)}, u32[]{:S(2)}) %collective-permute-start.9) | collective-permute-done | bytes 49184 | tf_op jit(solution)/shard_map/ppermute | solution.py:214
  26.4 0.1 collective-permute-start.13
  26.5 0.3 %collective-permute-done.10.refs_3_ = bf16[48,512]{1,0:T(8,128)(2,1)S(1)} collective-permute-done((bf16[48,512]{1,0:T(8,128)(2,1)S(1)}, bf16[48,512]{1,0:T(8,128)(2,1)S(1)}, u32[]{:S(2)}, u32[]{:S(2)}) %collective-permute-start.10) | collective-permute-done | bytes 49184 | tf_op jit(solution)/shard_map/ppermute | solution.py:214
  26.8 0.1 collective-permute-start.14
  26.9 0.0 copy-done
  26.9 0.0 copy-done.2
  26.9 0.8 %fusion.base_ref = f32[128,2048]{1,0:T(8,128)S(1)} fusion(bf16[128,512]{1,0:T(8,128)(2,1)S(1)} %copy-done.2, bf16[2048,512]{1,0:T(8,128)(2,1)S(1)} %copy-done), kind=kOutput, calls=%fused_computation | convolution fusion | flops 268435456 | bytes 3276800 | tf_op jit(solution)/shard_map/dot_general | solution.py:20
  27.7 1.0 %shard_map.115 = bf16[128,2048]{1,0:T(8,128)(2,1)} custom-call(bf16[256,512]{1,0:T(8,128)(2,1)S(1)} %get-tuple-element.33.kept_ref, f32[128,2048]{1,0:T(8,128)S(1)} %fusion.base_ref, bf16[128,32]{1,0:T(8,128)(2,1)S(1)} %get-tuple-element.34.dlow_ref, bf16[4,32,512]{2,1,0:T(8,128)(2,1)S(1)} %get-tuple-element.35.a_ref), custom_call_target="tpu_custom_call" | custom-call | flops 16777216 | bytes 1572864 | tf_op jit(solution)/shard_map/pallas_call | solution.py:314
  28.7 0.0 collective-permute-done.11.refs_4_
  28.7 0.0 collective-permute-done.12.refs_5_
  28.7 0.0 collective-permute-done.13.refs_6_
  28.7 0.0 collective-permute-done.14.refs_7_
  28.7 1.0 %shard_map.116 = (f32[512,128]{1,0:T(8,128)}, f32[16,256]{1,0:T(8,128)}) custom-call(bf16[256,512]{1,0:T(8,128)(2,1)S(1)} %get-tuple-element.33.kept_ref, bf16[48,512]{1,0:T(8,128)(2,1)S(1)} %get-tuple-element.36.refs_0_, bf16[48,512]{1,0:T(8,128)(2,1)S(1)} %collective-permute-done.8.refs_1_, bf16[48,512]{1,0:T(8,128)(2,1)S(1)} %collective-permute-done.9.refs_2_, ...), custom_call_target="tpu_custom_call" | custom-call | tf_op jit(solution)/shard_map/pallas_call | solution.py:328
Async XLA Ops:
  0.6 26.3 %copy-start = (bf16[2048,512]{1,0:T(8,128)(2,1)S(1)}, bf16[2048,512]{1,0:T(8,128)(2,1)}, u32[]{:S(2)}) copy-start(bf16[2048,512]{1,0:T(8,128)(2,1)} %param.11) | copy-start | bytes 6291460
  0.6 26.3 %copy-start.2 = (bf16[128,512]{1,0:T(8,128)(2,1)S(1)}, bf16[128,512]{1,0:T(8,128)(2,1)}, u32[]{:S(2)}) copy-start(bf16[128,512]{1,0:T(8,128)(2,1)} %g_hbm.1) | copy-start | bytes 393220
  3.1 14.1 %collective-permute-start = (bf16[64,4096]{1,0:T(8,128)(2,1)}, bf16[64,4096]{1,0:T(8,128)(2,1)S(1)}, u32[]{:S(2)}, u32[]{:S(2)}) collective-permute-start(bf16[64,4096]{1,0:T(8,128)(2,1)} %x_hbm.1), channel_id=1, source_target_pairs={{0,1},{1,0},{2,3},{3,2},{4,5},{5,4},{6,7},{7,6},{8,9},{9,8},{10,11... | collective-permute-start | bytes 1572872 | tf_op jit(solution)/shard_map/ppermute | solution.py:284
  3.6 8.4 %collective-permute-start.1 = (bf16[48,512]{1,0:T(8,128)(2,1)}, bf16[48,512]{1,0:T(8,128)(2,1)S(1)}, u32[]{:S(2)}, u32[]{:S(2)}) collective-permute-start(bf16[48,512]{1,0:T(8,128)(2,1)} %get-tuple-element.29), channel_id=1, source_target_pairs={{0,14},{1,13},{2,12},{3,15},{4,10},{5,9},{6,8},{7,11},{8,6},{9,5},... | collective-permute-start | bytes 147464 | tf_op jit(solution)/shard_map/ppermute | solution.py:214
  9.2 6.2 %collective-permute-start.2 = (bf16[48,512]{1,0:T(8,128)(2,1)}, bf16[48,512]{1,0:T(8,128)(2,1)S(1)}, u32[]{:S(2)}, u32[]{:S(2)}) collective-permute-start(bf16[48,512]{1,0:T(8,128)(2,1)} %get-tuple-element.30), channel_id=1, source_target_pairs={{0,10},{1,9},{2,8},{3,11},{4,14},{5,13},{6,12},{7,15},{8,2},{9,1},... | collective-permute-start | bytes 147464 | tf_op jit(solution)/shard_map/ppermute | solution.py:214
  9.2 6.2 %collective-permute-start.3 = (bf16[48,512]{1,0:T(8,128)(2,1)}, bf16[48,512]{1,0:T(8,128)(2,1)S(1)}, u32[]{:S(2)}, u32[]{:S(2)}) collective-permute-start(bf16[48,512]{1,0:T(8,128)(2,1)} %get-tuple-element.31), channel_id=1, source_target_pairs={{0,6},{1,5},{2,4},{3,7},{4,2},{5,1},{6,0},{7,3},{8,14},{9,13},{10,... | collective-permute-start | bytes 147464 | tf_op jit(solution)/shard_map/ppermute | solution.py:214
  10.9 6.3 %collective-permute-start.4 = (bf16[48,512]{1,0:T(8,128)(2,1)}, bf16[48,512]{1,0:T(8,128)(2,1)S(1)}, u32[]{:S(2)}, u32[]{:S(2)}) collective-permute-start(bf16[48,512]{1,0:T(8,128)(2,1)} %get-tuple-element.32), channel_id=1, source_target_pairs={{0,2},{1,3},{2,0},{3,1},{4,6},{5,7},{6,4},{7,5},{8,10},{9,11},{10,... | collective-permute-start | bytes 147464 | tf_op jit(solution)/shard_map/ppermute | solution.py:214
  12.0 5.2 %collective-permute-start.5 = (bf16[48,512]{1,0:T(8,128)(2,1)S(1)}, bf16[48,512]{1,0:T(8,128)(2,1)S(1)}, u32[]{:S(2)}, u32[]{:S(2)}) collective-permute-start(bf16[48,512]{1,0:T(8,128)(2,1)S(1)} %collective-permute-done.1.refs_0_), channel_id=1, source_target_pairs={{0,1},{1,0},{2,3},{3,2},{4,5},{5,4},{6,7},{7,6},{8,9},{9,8},{10,11... | collective-permute-start | bytes 147464 | tf_op jit(solution)/shard_map/ppermute | solution.py:221
  15.4 1.7 %collective-permute-start.6 = (bf16[48,512]{1,0:T(8,128)(2,1)S(1)}, bf16[48,512]{1,0:T(8,128)(2,1)S(1)}, u32[]{:S(2)}, u32[]{:S(2)}) collective-permute-start(bf16[48,512]{1,0:T(8,128)(2,1)S(1)} %collective-permute-done.2.refs_1_), channel_id=1, source_target_pairs={{0,1},{1,0},{2,3},{3,2},{4,5},{5,4},{6,7},{7,6},{8,9},{9,8},{10,11... | collective-permute-start | bytes 147464 | tf_op jit(solution)/shard_map/ppermute | solution.py:221
  15.4 1.8 %collective-permute-start.7 = (bf16[48,512]{1,0:T(8,128)(2,1)S(1)}, bf16[48,512]{1,0:T(8,128)(2,1)S(1)}, u32[]{:S(2)}, u32[]{:S(2)}) collective-permute-start(bf16[48,512]{1,0:T(8,128)(2,1)S(1)} %collective-permute-done.3.refs_2_), channel_id=1, source_target_pairs={{0,1},{1,0},{2,3},{3,2},{4,5},{5,4},{6,7},{7,6},{8,9},{9,8},{10,11... | collective-permute-start | bytes 147464 | tf_op jit(solution)/shard_map/ppermute | solution.py:221
  15.9 1.1 %copy-start.1 = (bf16[816,512]{1,0:T(8,128)(2,1)S(1)}, bf16[816,512]{1,0:T(8,128)(2,1)}, u32[]{:S(2)}) copy-start(bf16[816,512]{1,0:T(8,128)(2,1)} %get-tuple-element.23.stage) | copy-start | bytes 2506756
  18.5 7.5 %collective-permute-start.8 = (bf16[48,512]{1,0:T(8,128)(2,1)S(1)}, bf16[48,512]{1,0:T(8,128)(2,1)S(1)}, u32[]{:S(2)}, u32[]{:S(2)}) collective-permute-start(bf16[48,512]{1,0:T(8,128)(2,1)S(1)} %get-tuple-element.37), channel_id=1, source_target_pairs={{0,14},{1,13},{2,12},{3,15},{4,10},{5,9},{6,8},{7,11},{8,6},{9,5},... | collective-permute-start | bytes 147464 | tf_op jit(solution)/shard_map/ppermute | solution.py:214
  20.3 6.1 %collective-permute-start.9 = (bf16[48,512]{1,0:T(8,128)(2,1)S(1)}, bf16[48,512]{1,0:T(8,128)(2,1)S(1)}, u32[]{:S(2)}, u32[]{:S(2)}) collective-permute-start(bf16[48,512]{1,0:T(8,128)(2,1)S(1)} %get-tuple-element.38), channel_id=1, source_target_pairs={{0,10},{1,9},{2,8},{3,11},{4,14},{5,13},{6,12},{7,15},{8,2},{9,1},... | collective-permute-start | bytes 147464 | tf_op jit(solution)/shard_map/ppermute | solution.py:214
  20.9 5.9 %collective-permute-start.10 = (bf16[48,512]{1,0:T(8,128)(2,1)S(1)}, bf16[48,512]{1,0:T(8,128)(2,1)S(1)}, u32[]{:S(2)}, u32[]{:S(2)}) collective-permute-start(bf16[48,512]{1,0:T(8,128)(2,1)S(1)} %get-tuple-element.39), channel_id=1, source_target_pairs={{0,6},{1,5},{2,4},{3,7},{4,2},{5,1},{6,0},{7,3},{8,14},{9,13},{10,... | collective-permute-start | bytes 147464 | tf_op jit(solution)/shard_map/ppermute | solution.py:214
  23.7 5.0 %collective-permute-start.11 = (bf16[48,512]{1,0:T(8,128)(2,1)S(1)}, bf16[48,512]{1,0:T(8,128)(2,1)S(1)}, u32[]{:S(2)}, u32[]{:S(2)}) collective-permute-start(bf16[48,512]{1,0:T(8,128)(2,1)S(1)} %get-tuple-element.40), channel_id=1, source_target_pairs={{0,2},{1,3},{2,0},{3,1},{4,6},{5,7},{6,4},{7,5},{8,10},{9,11},{10,... | collective-permute-start | bytes 147464 | tf_op jit(solution)/shard_map/ppermute | solution.py:214
  26.0 2.8 %collective-permute-start.12 = (bf16[48,512]{1,0:T(8,128)(2,1)S(1)}, bf16[48,512]{1,0:T(8,128)(2,1)S(1)}, u32[]{:S(2)}, u32[]{:S(2)}) collective-permute-start(bf16[48,512]{1,0:T(8,128)(2,1)S(1)} %collective-permute-done.8.refs_1_), channel_id=1, source_target_pairs={{0,1},{1,0},{2,3},{3,2},{4,5},{5,4},{6,7},{7,6},{8,9},{9,8},{10,11... | collective-permute-start | bytes 147464 | tf_op jit(solution)/shard_map/ppermute | solution.py:221
  26.4 2.3 %collective-permute-start.13 = (bf16[48,512]{1,0:T(8,128)(2,1)S(1)}, bf16[48,512]{1,0:T(8,128)(2,1)S(1)}, u32[]{:S(2)}, u32[]{:S(2)}) collective-permute-start(bf16[48,512]{1,0:T(8,128)(2,1)S(1)} %collective-permute-done.9.refs_2_), channel_id=1, source_target_pairs={{0,1},{1,0},{2,3},{3,2},{4,5},{5,4},{6,7},{7,6},{8,9},{9,8},{10,11... | collective-permute-start | bytes 147464 | tf_op jit(solution)/shard_map/ppermute | solution.py:221
  26.8 2.0 %collective-permute-start.14 = (bf16[48,512]{1,0:T(8,128)(2,1)S(1)}, bf16[48,512]{1,0:T(8,128)(2,1)S(1)}, u32[]{:S(2)}, u32[]{:S(2)}) collective-permute-start(bf16[48,512]{1,0:T(8,128)(2,1)S(1)} %collective-permute-done.10.refs_3_), channel_id=1, source_target_pairs={{0,1},{1,0},{2,3},{3,2},{4,5},{5,4},{6,7},{7,6},{8,9},{9,8},{10,11... | collective-permute-start | bytes 147464 | tf_op jit(solution)/shard_map/ppermute | solution.py:221

commit v6 on v5

--- a/solution.py
+++ b/solution.py
@@ -51,7 +51,7 @@
 
 
 def pairs(n, core):
-    return [n - 1 - 2 * j - core for j in range(n // 2 - 1)]
+    return [n - 1 - 2 * j - (core if j == 0 else 1 - core) for j in range(n // 2 - 1)]
 
 
 def partners(n, me, core):
@@ -182,14 +182,16 @@
         message[picked:, :] = up_ref[target]
 
 
-def grad_x_kernel(kept_ref, base_ref, dlow_ref, a_ref, out_hbm, out_ref, sems):
+def base_kernel(kept_ref, w_ref, after_ref, out_ref):
+    out_ref[...] = dot(kept_ref[: out_ref.shape[0], :], w_ref[...], 1, 1)
+
+
+def grad_x_kernel(base_ref, dlow_ref, a_ref, out_hbm, out_ref, sems):
     steps, picked, width = a_ref.shape
-    rows = out_ref.shape[0]
-    live = kept_ref[rows:, picked : picked + 1].astype(f32) > 0.0
     done = []
     for j in range(steps):
         at = pl.ds(j * width, width)
-        total = jnp.where(live, base_ref[:, at], 0.0) + dot(dlow_ref[...], a_ref[j], 1, 0)
+        total = base_ref[:, at] + dot(dlow_ref[...], a_ref[j], 1, 0)
         out_ref[:, at] = total.astype(bf16)
         done += start_all([out_ref.at[:, at]], [out_hbm.at[:, at]], sems, j)
     wait_all(done)
@@ -207,7 +209,7 @@
     up_ref[...] = jnp.sum(rows_ref[:, picked:, at].astype(f32), axis=0)
 
 
-def exchange(messages):
+def exchange(messages, beside=None):
     n = 2 * len(messages)
     steps = list(zip(pairs(n, 0), pairs(n, 1))) + [(1, 1)]
     got = [
@@ -218,8 +220,12 @@
         )
         for message, step in zip(messages, steps)
     ]
+    made = None
+    if beside is not None:
+        made = beside(got[0])
+        got[1], made = lax.optimization_barrier((got[1], made))
     passed = [lax.ppermute(message, "tensor", [(0, 1), (1, 0)]) for message in got[:-1]]
-    return got + passed
+    return got + passed, made
 
 
 def local_kernels(
@@ -280,7 +286,7 @@
         up_maps,
     )
     sent, x_late = lax.optimization_barrier((sent, inputs))
-    got = exchange(sent)
+    got, _ = exchange(sent)
     x_other = lax.ppermute(x_late, "tensor", [(0, 1), (1, 0)])
     stage = pl.pallas_call(
         hand_on_kernel,
@@ -290,7 +296,6 @@
         compiler_params=params(8),
         cost_estimate=pl.CostEstimate(flops=0, bytes_accessed=1 << 21, transcendentals=0),
     )(stage)
-    base = dot(output_gradient, frozen_weight, 1, 1)
 
     dlow, a_half, kept, own, *sent = pl.pallas_call(
         functools.partial(middle_kernel, n, lay),
@@ -309,12 +314,24 @@
         ],
         compiler_params=params(8),
     )(stage, x_other, *got)
-    got = exchange(sent)
+    frozen = pl.pallas_call(
+        base_kernel,
+        out_shape=shape((tok_rows, half), f32),
+        in_specs=[VMEM, VMEM, pl.BlockSpec(memory_space=pl.ANY)],
+        out_specs=VMEM,
+        compiler_params=params(8),
+        cost_estimate=pl.CostEstimate(
+            flops=2 * tok_rows * half * out_width,
+            bytes_accessed=4 * half * tok_rows + 2 * half * out_width,
+            transcendentals=0,
+        ),
+    )
+    got, base = exchange(sent, functools.partial(frozen, kept, frozen_weight))
 
     grad_x = pl.pallas_call(
         grad_x_kernel,
         out_shape=shape((tok_rows, half), bf16),
-        in_specs=[VMEM] * 4,
+        in_specs=[VMEM] * 3,
         out_specs=HBM,
         scratch_shapes=[pltpu.VMEM((tok_rows, half), bf16), dma((n // 2,))],
         compiler_params=params(8),
@@ -323,7 +340,7 @@
             bytes_accessed=6 * half * tok_rows,
             transcendentals=0,
         ),
-    )(kept, base, dlow, a_half)
+    )(base, dlow, a_half)
 
     grad_a, up_map_gradient = pl.pallas_call(
         functools.partial(final_kernel, n, lay),

time: 30 us -> 28.8 us (0.960)
  starting transfers between devices: 15.8 us -> 14.6 us
  Pallas kernels: 5.75 us -> 6.56 us
  matrix products: 0.8 us -> 0 us
    ppermute x8, starting transfers between devices: 14.5 us -> 12.7 us  [exchange(): lax.ppermute(message, ('dp', 'tensor'), [(2 * i + c, 2 * (i ^ step[c]) +...]
    pallas_call x0 -> x1, Pallas kernels: none -> 0.8 us  [exchange(): made = beside(got[0])]
    dot_general x1 -> x0, matrix products: 0.8 us -> none  [dot(): lax.dot_general(a, b, (((ca,), (cb,)), ((), ())), preferred_element_type=...]
    ppermute x6, starting transfers between devices: 0.72 us -> 1.35 us  [exchange(): lax.ppermute(message, 'tensor', [(0, 1), (1, 0)])]
    unnamed x6 -> x4, local copies, waits for them, and re-layouts: 1.16 us -> 1.15 us
  transfers between devices with their start and end apart: 15 -> 15, of which waited for: 5 -> 3; matrix products, arithmetic and copies ran while one was open for 3% -> 0% of each run, Pallas kernels for 3% -> 6%
where the time goes in v6:
time: 28.8 us; the launch traced here: 28.6 us
  starting transfers between devices  14.6 us (51%)
  Pallas kernels  6.56 us (23%)
  waiting for transfers between devices  5.53 us (19%)
  local copies, waits for them, and re-layouts  1.15 us (4%)
  between operations  0.77 us (3%)
    ppermute x8, starting transfers between devices, exchange(): lax.ppermute(message, ('dp', 'tensor'), [(2 * i + c, 2 * (i ^ step[c]) +...  12.7 us
    ppermute x8, waiting for transfers between devices, exchange(): lax.ppermute(message, ('dp', 'tensor'), [(2 * i + c, 2 * (i ^ step[c]) +...  5.51 us
    pallas_call x1, Pallas kernels, local_kernels(): pl.pallas_call(functools.partial(pack_kernel, n, lay), out_shape=[message...  2.43 us
    ppermute x6, starting transfers between devices, exchange(): lax.ppermute(message, 'tensor', [(0, 1), (1, 0)])  1.35 us
    pallas_call x1, Pallas kernels, local_kernels(): pl.pallas_call(functools.partial(middle_kernel, n, lay), out_shape=[shape...  1.26 us
    unnamed x4, local copies, waits for them, and re-layouts  1.15 us
    pallas_call x1, Pallas kernels, local_kernels(): pl.pallas_call(functools.partial(final_kernel, n, lay), out_shape=[shape(...  1.02 us
    pallas_call x1, Pallas kernels, local_kernels(): pl.pallas_call(grad_x_kernel, out_shape=shape((tok_rows, half), bf16), in...  0.99 us
  transfers between devices with their start and end apart: 15, of which 3 were waited for; matrix products, arithmetic and copies ran while one was open for 0% of the time, Pallas kernels for 6%

profile of v6, /device:TPU:0, one launch (start us, length us, event | category | flops | bytes accessed | tf_op | source)
XLA Modules:
  0.0 28.6 jit_solution(6035377377556039396)
XLA Ops:
  0.6 0.0 copy-start
  0.6 2.4 %shard_map.112 = (bf16[48,512]{1,0:T(8,128)(2,1)}, bf16[48,512]{1,0:T(8,128)(2,1)}, bf16[48,512]{1,0:T(8,128)(2,1)}, bf16[48,512]{1,0:T(8,128)(2,1)}, bf16[816,512]{1,0:T(8,128)(2,1)}) custom-call(s32[2,8]{1,0:T(2,128)} %bitcast.2, s32[2,8]{1,0:T(2,128)} %bitcast.3, s32[8]{0:T(128)} %slot_hbm.1, s32[8]{0:T(128)} %count_hbm.1, bf16[128,512]{1,0:T(8,128)(2,1)} %g_hbm.1, ...), custom_call_target="tpu_custom_call" | custom-call | tf_op jit(solution)/shard_map/pallas_call | solution.py:264
  3.1 0.5 %collective-permute-start = (bf16[64,4096]{1,0:T(8,128)(2,1)}, bf16[64,4096]{1,0:T(8,128)(2,1)S(1)}, u32[]{:S(2)}, u32[]{:S(2)}) collective-permute-start(bf16[64,4096]{1,0:T(8,128)(2,1)} %x_hbm.1), channel_id=1, source_target_pairs={{0,1},{1,0},{2,3},{3,2},{4,5},{5,4},{6,7},{7,6},{8,9},{9,8},{10,11... | collective-permute-start | bytes 1572872 | tf_op jit(solution)/shard_map/ppermute | solution.py:290
  3.6 5.6 %collective-permute-start.1 = (bf16[48,512]{1,0:T(8,128)(2,1)}, bf16[48,512]{1,0:T(8,128)(2,1)S(1)}, u32[]{:S(2)}, u32[]{:S(2)}) collective-permute-start(bf16[48,512]{1,0:T(8,128)(2,1)} %get-tuple-element.31), channel_id=1, source_target_pairs={{0,14},{1,13},{2,12},{3,15},{4,10},{5,9},{6,8},{7,11},{8,6},{9,5},... | collective-permute-start | bytes 147464 | tf_op jit(solution)/shard_map/ppermute | solution.py:216
  9.2 0.0 collective-permute-start.2
  9.2 0.8 %collective-permute-start.3 = (bf16[48,512]{1,0:T(8,128)(2,1)}, bf16[48,512]{1,0:T(8,128)(2,1)S(1)}, u32[]{:S(2)}, u32[]{:S(2)}) collective-permute-start(bf16[48,512]{1,0:T(8,128)(2,1)} %get-tuple-element.33), channel_id=1, source_target_pairs={{0,4},{1,7},{2,6},{3,5},{4,0},{5,3},{6,2},{7,1},{8,12},{9,15},{10,... | collective-permute-start | bytes 147464 | tf_op jit(solution)/shard_map/ppermute | solution.py:216
  10.0 0.4 %collective-permute-start.4 = (bf16[48,512]{1,0:T(8,128)(2,1)}, bf16[48,512]{1,0:T(8,128)(2,1)S(1)}, u32[]{:S(2)}, u32[]{:S(2)}) collective-permute-start(bf16[48,512]{1,0:T(8,128)(2,1)} %get-tuple-element.34), channel_id=1, source_target_pairs={{0,2},{1,3},{2,0},{3,1},{4,6},{5,7},{6,4},{7,5},{8,10},{9,11},{10,... | collective-permute-start | bytes 147464 | tf_op jit(solution)/shard_map/ppermute | solution.py:216
  10.4 1.4 %collective-permute-done.1.refs_0_ = bf16[48,512]{1,0:T(8,128)(2,1)S(1)} collective-permute-done((bf16[48,512]{1,0:T(8,128)(2,1)}, bf16[48,512]{1,0:T(8,128)(2,1)S(1)}, u32[]{:S(2)}, u32[]{:S(2)}) %collective-permute-start.1) | collective-permute-done | bytes 49184 | tf_op jit(solution)/shard_map/ppermute | solution.py:216
  11.8 0.0 collective-permute-start.5
  11.9 2.7 %collective-permute-done.2.refs_1_ = bf16[48,512]{1,0:T(8,128)(2,1)S(1)} collective-permute-done((bf16[48,512]{1,0:T(8,128)(2,1)}, bf16[48,512]{1,0:T(8,128)(2,1)S(1)}, u32[]{:S(2)}, u32[]{:S(2)}) %collective-permute-start.2) | collective-permute-done | bytes 49184 | tf_op jit(solution)/shard_map/ppermute | solution.py:216
  14.5 0.0 collective-permute-start.6
  14.6 0.0 collective-permute-done.3.refs_2_
  14.6 0.5 %collective-permute-start.7 = (bf16[48,512]{1,0:T(8,128)(2,1)S(1)}, bf16[48,512]{1,0:T(8,128)(2,1)S(1)}, u32[]{:S(2)}, u32[]{:S(2)}) collective-permute-start(bf16[48,512]{1,0:T(8,128)(2,1)S(1)} %collective-permute-done.3.refs_2_), channel_id=1, source_target_pairs={{0,1},{1,0},{2,3},{3,2},{4,5},{5,4},{6,7},{7,6},{8,9},{9,8},{10,11... | collective-permute-start | bytes 147464 | tf_op jit(solution)/shard_map/ppermute | solution.py:227
  15.1 0.0 copy-start.1
  15.1 1.1 %copy-done.1 = bf16[816,512]{1,0:T(8,128)(2,1)S(1)} copy-done((bf16[816,512]{1,0:T(8,128)(2,1)S(1)}, bf16[816,512]{1,0:T(8,128)(2,1)}, u32[]{:S(2)}) %copy-start.1) | copy-done | bytes 835608
  16.2 0.1 shard_map.113.stage
  16.3 0.0 collective-permute-done.4.refs_3_
  16.3 0.0 collective-permute-done.5.refs_4_
  16.3 0.0 collective-permute-done.6.refs_5_
  16.3 0.0 collective-permute-done.7.refs_6_
  16.3 0.0 collective-permute-done.x_other
  16.3 1.3 %shard_map.114 = (bf16[128,32]{1,0:T(8,128)(2,1)S(1)}, bf16[4,32,512]{2,1,0:T(8,128)(2,1)S(1)}, bf16[256,512]{1,0:T(8,128)(2,1)S(1)}, bf16[48,512]{1,0:T(8,128)(...) custom-call(bf16[816,512]{1,0:T(8,128)(2,1)S(1)} %shard_map.113.stag, ...), custom_call_target="tpu_custom_call" | custom-call | tf_op jit(solution)/shard_map/pallas_call | solution.py:300
  17.6 2.6 %collective-permute-start.9 = (bf16[48,512]{1,0:T(8,128)(2,1)S(1)}, bf16[48,512]{1,0:T(8,128)(2,1)S(1)}, u32[]{:S(2)}, u32[]{:S(2)}) collective-permute-start(bf16[48,512]{1,0:T(8,128)(2,1)S(1)} %get-tuple-element.37), channel_id=1, source_target_pairs={{0,14},{1,13},{2,12},{3,15},{4,10},{5,9},{6,8},{7,11},{8,6},{9,5},... | collective-permute-start | bytes 147464 | tf_op jit(solution)/shard_map/ppermute | solution.py:216
  20.2 0.0 collective-permute-start.8
  20.2 1.8 %collective-permute-start.10 = (bf16[48,512]{1,0:T(8,128)(2,1)S(1)}, bf16[48,512]{1,0:T(8,128)(2,1)S(1)}, u32[]{:S(2)}, u32[]{:S(2)}) collective-permute-start(bf16[48,512]{1,0:T(8,128)(2,1)S(1)} %get-tuple-element.43), channel_id=1, source_target_pairs={{0,4},{1,7},{2,6},{3,5},{4,0},{5,3},{6,2},{7,1},{8,12},{9,15},{10,... | collective-permute-start | bytes 147464 | tf_op jit(solution)/shard_map/ppermute | solution.py:216
  22.0 1.5 %collective-permute-start.11 = (bf16[48,512]{1,0:T(8,128)(2,1)S(1)}, bf16[48,512]{1,0:T(8,128)(2,1)S(1)}, u32[]{:S(2)}, u32[]{:S(2)}) collective-permute-start(bf16[48,512]{1,0:T(8,128)(2,1)S(1)} %get-tuple-element.44), channel_id=1, source_target_pairs={{0,2},{1,3},{2,0},{3,1},{4,6},{5,7},{6,4},{7,5},{8,10},{9,11},{10,... | collective-permute-start | bytes 147464 | tf_op jit(solution)/shard_map/ppermute | solution.py:216
  23.5 1.4 %collective-permute-done.9.after_ref.refs_1_ = bf16[48,512]{1,0:T(8,128)(2,1)S(1)} collective-permute-done((bf16[48,512]{1,0:T(8,128)(2,1)S(1)}, bf16[48,512]{1,0:T(8,128)(2,1)S(1)}, u32[]{:S(2)}, u32[]{:S(2)}) %collective-permute-start.9) | collective-permute-done | bytes 49184 | tf_op jit(solution)/shard_map/ppermute | solution.py:216
  24.9 0.0 copy-done
  24.9 0.8 %shard_map.115.base_ref = f32[128,2048]{1,0:T(8,128)S(1)} custom-call(bf16[256,512]{1,0:T(8,128)(2,1)S(1)} %get-tuple-element.36.kept_ref, bf16[2048,512]{1,0:T(8,128)(2,1)S(1)} %copy-done, bf16[48,512]{1,0:T(8,128)(2,1)S(1)} %collective-permute-done.9.after_ref.refs_1_), custom_call_target="tpu_custom_call" | custom-call | flops 268435456 | bytes 3145728 | tf_op jit(solution)/shard_map/pallas_call | solution.py:225
  25.7 0.0 collective-permute-done.8.refs_2_
  25.7 0.3 %collective-permute-start.12 = (bf16[48,512]{1,0:T(8,128)(2,1)S(1)}, bf16[48,512]{1,0:T(8,128)(2,1)S(1)}, u32[]{:S(2)}, u32[]{:S(2)}) collective-permute-start(bf16[48,512]{1,0:T(8,128)(2,1)S(1)} %collective-permute-done.9.after_ref.refs_1_), channel_id=1, source_target_pairs={{0,1},{1,0},{2,3},{3,2},{4,5},{5,4},{6,7},{7,6},{8,9},{9,8},{10,11... | collective-permute-start | bytes 147464 | tf_op jit(solution)/shard_map/ppermute | solution.py:227
  26.0 0.0 collective-permute-done.10.refs_3_
  26.0 0.2 collective-permute-start.14
  26.3 0.3 collective-permute-start.13
  26.5 1.0 %shard_map.116 = bf16[128,2048]{1,0:T(8,128)(2,1)} custom-call(f32[128,2048]{1,0:T(8,128)S(1)} %shard_map.115.base_ref, bf16[128,32]{1,0:T(8,128)(2,1)S(1)} %get-tuple-element.39.dlow_ref, bf16[4,32,512]{2,1,0:T(8,128)(2,1)S(1)} %get-tuple-element.40.a_ref), custom_call_target="tpu_custom_call" | custom-call | flops 16777216 | bytes 1572864 | tf_op jit(solution)/shard_map/pallas_call | solution.py:331
  27.5 0.0 collective-permute-done.11.refs_4_
  27.5 0.0 collective-permute-done.12.refs_5_
  27.6 0.0 collective-permute-done.14.refs_7_
  27.6 0.0 collective-permute-done.13.refs_6_
  27.6 1.0 %shard_map.117 = (f32[512,128]{1,0:T(8,128)}, f32[16,256]{1,0:T(8,128)}) custom-call(bf16[256,512]{1,0:T(8,128)(2,1)S(1)} %get-tuple-element.36.kept_ref, bf16[48,512]{1,0:T(8,128)(2,1)S(1)} %get-tuple-element.41.refs_0_, bf16[48,512]{1,0:T(8,128)(2,1)S(1)} %collective-permute-done.9.after_ref.refs_1_, bf16[48,512]{1,0:T(8,128)(2,1)S(1)} %collective-permute-done.8.refs_2_, ...), custom_call_target="tpu_custom_call" | custom-call | tf_op jit(solution)/shard_map/pallas_call | solution.py:345
Async XLA Ops:
  0.6 24.2 %copy-start = (bf16[2048,512]{1,0:T(8,128)(2,1)S(1)}, bf16[2048,512]{1,0:T(8,128)(2,1)}, u32[]{:S(2)}) copy-start(bf16[2048,512]{1,0:T(8,128)(2,1)} %w_ref.1) | copy-start | bytes 6291460
  3.1 13.2 %collective-permute-start = (bf16[64,4096]{1,0:T(8,128)(2,1)}, bf16[64,4096]{1,0:T(8,128)(2,1)S(1)}, u32[]{:S(2)}, u32[]{:S(2)}) collective-permute-start(bf16[64,4096]{1,0:T(8,128)(2,1)} %x_hbm.1), channel_id=1, source_target_pairs={{0,1},{1,0},{2,3},{3,2},{4,5},{5,4},{6,7},{7,6},{8,9},{9,8},{10,11... | collective-permute-start | bytes 1572872 | tf_op jit(solution)/shard_map/ppermute | solution.py:290
  3.6 8.3 %collective-permute-start.1 = (bf16[48,512]{1,0:T(8,128)(2,1)}, bf16[48,512]{1,0:T(8,128)(2,1)S(1)}, u32[]{:S(2)}, u32[]{:S(2)}) collective-permute-start(bf16[48,512]{1,0:T(8,128)(2,1)} %get-tuple-element.31), channel_id=1, source_target_pairs={{0,14},{1,13},{2,12},{3,15},{4,10},{5,9},{6,8},{7,11},{8,6},{9,5},... | collective-permute-start | bytes 147464 | tf_op jit(solution)/shard_map/ppermute | solution.py:216
  9.2 5.3 %collective-permute-start.2 = (bf16[48,512]{1,0:T(8,128)(2,1)}, bf16[48,512]{1,0:T(8,128)(2,1)S(1)}, u32[]{:S(2)}, u32[]{:S(2)}) collective-permute-start(bf16[48,512]{1,0:T(8,128)(2,1)} %get-tuple-element.32), channel_id=1, source_target_pairs={{0,8},{1,11},{2,10},{3,9},{4,12},{5,15},{6,14},{7,13},{8,0},{9,3},... | collective-permute-start | bytes 147464 | tf_op jit(solution)/shard_map/ppermute | solution.py:216
  9.2 5.4 %collective-permute-start.3 = (bf16[48,512]{1,0:T(8,128)(2,1)}, bf16[48,512]{1,0:T(8,128)(2,1)S(1)}, u32[]{:S(2)}, u32[]{:S(2)}) collective-permute-start(bf16[48,512]{1,0:T(8,128)(2,1)} %get-tuple-element.33), channel_id=1, source_target_pairs={{0,4},{1,7},{2,6},{3,5},{4,0},{5,3},{6,2},{7,1},{8,12},{9,15},{10,... | collective-permute-start | bytes 147464 | tf_op jit(solution)/shard_map/ppermute | solution.py:216
  10.0 6.3 %collective-permute-start.4 = (bf16[48,512]{1,0:T(8,128)(2,1)}, bf16[48,512]{1,0:T(8,128)(2,1)S(1)}, u32[]{:S(2)}, u32[]{:S(2)}) collective-permute-start(bf16[48,512]{1,0:T(8,128)(2,1)} %get-tuple-element.34), channel_id=1, source_target_pairs={{0,2},{1,3},{2,0},{3,1},{4,6},{5,7},{6,4},{7,5},{8,10},{9,11},{10,... | collective-permute-start | bytes 147464 | tf_op jit(solution)/shard_map/ppermute | solution.py:216
  11.8 4.4 %collective-permute-start.5 = (bf16[48,512]{1,0:T(8,128)(2,1)S(1)}, bf16[48,512]{1,0:T(8,128)(2,1)S(1)}, u32[]{:S(2)}, u32[]{:S(2)}) collective-permute-start(bf16[48,512]{1,0:T(8,128)(2,1)S(1)} %collective-permute-done.1.refs_0_), channel_id=1, source_target_pairs={{0,1},{1,0},{2,3},{3,2},{4,5},{5,4},{6,7},{7,6},{8,9},{9,8},{10,11... | collective-permute-start | bytes 147464 | tf_op jit(solution)/shard_map/ppermute | solution.py:227
  14.5 1.7 %collective-permute-start.6 = (bf16[48,512]{1,0:T(8,128)(2,1)S(1)}, bf16[48,512]{1,0:T(8,128)(2,1)S(1)}, u32[]{:S(2)}, u32[]{:S(2)}) collective-permute-start(bf16[48,512]{1,0:T(8,128)(2,1)S(1)} %collective-permute-done.2.refs_1_), channel_id=1, source_target_pairs={{0,1},{1,0},{2,3},{3,2},{4,5},{5,4},{6,7},{7,6},{8,9},{9,8},{10,11... | collective-permute-start | bytes 147464 | tf_op jit(solution)/shard_map/ppermute | solution.py:227
  14.6 1.7 %collective-permute-start.7 = (bf16[48,512]{1,0:T(8,128)(2,1)S(1)}, bf16[48,512]{1,0:T(8,128)(2,1)S(1)}, u32[]{:S(2)}, u32[]{:S(2)}) collective-permute-start(bf16[48,512]{1,0:T(8,128)(2,1)S(1)} %collective-permute-done.3.refs_2_), channel_id=1, source_target_pairs={{0,1},{1,0},{2,3},{3,2},{4,5},{5,4},{6,7},{7,6},{8,9},{9,8},{10,11... | collective-permute-start | bytes 147464 | tf_op jit(solution)/shard_map/ppermute | solution.py:227
  15.1 1.1 %copy-start.1 = (bf16[816,512]{1,0:T(8,128)(2,1)S(1)}, bf16[816,512]{1,0:T(8,128)(2,1)}, u32[]{:S(2)}) copy-start(bf16[816,512]{1,0:T(8,128)(2,1)} %get-tuple-element.25.stage) | copy-start | bytes 2506756
  17.6 7.3 %collective-permute-start.9 = (bf16[48,512]{1,0:T(8,128)(2,1)S(1)}, bf16[48,512]{1,0:T(8,128)(2,1)S(1)}, u32[]{:S(2)}, u32[]{:S(2)}) collective-permute-start(bf16[48,512]{1,0:T(8,128)(2,1)S(1)} %get-tuple-element.37), channel_id=1, source_target_pairs={{0,14},{1,13},{2,12},{3,15},{4,10},{5,9},{6,8},{7,11},{8,6},{9,5},... | collective-permute-start | bytes 147464 | tf_op jit(solution)/shard_map/ppermute | solution.py:216
  20.2 5.4 %collective-permute-start.8 = (bf16[48,512]{1,0:T(8,128)(2,1)S(1)}, bf16[48,512]{1,0:T(8,128)(2,1)S(1)}, u32[]{:S(2)}, u32[]{:S(2)}) collective-permute-start(bf16[48,512]{1,0:T(8,128)(2,1)S(1)} %get-tuple-element.35), channel_id=1, source_target_pairs={{0,8},{1,11},{2,10},{3,9},{4,12},{5,15},{6,14},{7,13},{8,0},{9,3},... | collective-permute-start | bytes 147464 | tf_op jit(solution)/shard_map/ppermute | solution.py:216
  20.2 5.8 %collective-permute-start.10 = (bf16[48,512]{1,0:T(8,128)(2,1)S(1)}, bf16[48,512]{1,0:T(8,128)(2,1)S(1)}, u32[]{:S(2)}, u32[]{:S(2)}) collective-permute-start(bf16[48,512]{1,0:T(8,128)(2,1)S(1)} %get-tuple-element.43), channel_id=1, source_target_pairs={{0,4},{1,7},{2,6},{3,5},{4,0},{5,3},{6,2},{7,1},{8,12},{9,15},{10,... | collective-permute-start | bytes 147464 | tf_op jit(solution)/shard_map/ppermute | solution.py:216
  22.0 5.5 %collective-permute-start.11 = (bf16[48,512]{1,0:T(8,128)(2,1)S(1)}, bf16[48,512]{1,0:T(8,128)(2,1)S(1)}, u32[]{:S(2)}, u32[]{:S(2)}) collective-permute-start(bf16[48,512]{1,0:T(8,128)(2,1)S(1)} %get-tuple-element.44), channel_id=1, source_target_pairs={{0,2},{1,3},{2,0},{3,1},{4,6},{5,7},{6,4},{7,5},{8,10},{9,11},{10,... | collective-permute-start | bytes 147464 | tf_op jit(solution)/shard_map/ppermute | solution.py:216
  25.7 1.9 %collective-permute-start.12 = (bf16[48,512]{1,0:T(8,128)(2,1)S(1)}, bf16[48,512]{1,0:T(8,128)(2,1)S(1)}, u32[]{:S(2)}, u32[]{:S(2)}) collective-permute-start(bf16[48,512]{1,0:T(8,128)(2,1)S(1)} %collective-permute-done.9.after_ref.refs_1_), channel_id=1, source_target_pairs={{0,1},{1,0},{2,3},{3,2},{4,5},{5,4},{6,7},{7,6},{8,9},{9,8},{10,11... | collective-permute-start | bytes 147464 | tf_op jit(solution)/shard_map/ppermute | solution.py:227
  26.0 1.5 %collective-permute-start.14 = (bf16[48,512]{1,0:T(8,128)(2,1)S(1)}, bf16[48,512]{1,0:T(8,128)(2,1)S(1)}, u32[]{:S(2)}, u32[]{:S(2)}) collective-permute-start(bf16[48,512]{1,0:T(8,128)(2,1)S(1)} %collective-permute-done.10.refs_3_), channel_id=1, source_target_pairs={{0,1},{1,0},{2,3},{3,2},{4,5},{5,4},{6,7},{7,6},{8,9},{9,8},{10,11... | collective-permute-start | bytes 147464 | tf_op jit(solution)/shard_map/ppermute | solution.py:227
  26.3 1.3 %collective-permute-start.13 = (bf16[48,512]{1,0:T(8,128)(2,1)S(1)}, bf16[48,512]{1,0:T(8,128)(2,1)S(1)}, u32[]{:S(2)}, u32[]{:S(2)}) collective-permute-start(bf16[48,512]{1,0:T(8,128)(2,1)S(1)} %collective-permute-done.8.refs_2_), channel_id=1, source_target_pairs={{0,1},{1,0},{2,3},{3,2},{4,5},{5,4},{6,7},{7,6},{8,9},{9,8},{10,11... | collective-permute-start | bytes 147464 | tf_op jit(solution)/shard_map/ppermute | solution.py:227

commit v7 on v6

--- a/solution.py
+++ b/solution.py
@@ -50,17 +50,17 @@
         copy.wait()
 
 
-def pairs(n, core):
-    return [n - 1 - 2 * j - (core if j == 0 else 1 - core) for j in range(n // 2 - 1)]
+def steps(n):
+    return [(n // 2, n // 2 + 1), (n - 1, n - 2), (2, 3), (1, 1)]
 
 
 def partners(n, me, core):
-    steps = [jnp.where(core == 0, a, b) for a, b in zip(pairs(n, 0), pairs(n, 1))]
-    return [me] + [me ^ d for d in steps] + [me ^ 1]
+    return [me] + [me ^ jnp.where(core == 0, a, b) for a, b in steps(n)]
 
 
 def senders(n, me, core):
-    return partners(n, me, core) + partners(n, me, 1 - core)[1:-1]
+    passed = [me ^ jnp.where(core == 0, b, a) for a, b in steps(n) if a != b]
+    return partners(n, me, core) + passed
 
 
 class Staged:
@@ -83,45 +83,49 @@
         return jnp.concatenate([kept[self.rows :, k] for k in at], axis=0)
 
 
-def pack_kernel(n, lay, start_hbm, chosen_hbm, slot_hbm, count_hbm, g_hbm, x_hbm, down_hbm, up_hbm, *refs):
+def pack_kernel(n, chosen_hbm, slot_hbm, down_hbm, up_hbm, *refs):
     count = n // 2 + 1
-    send, stage_hbm = refs[: count - 1], refs[count - 1]
-    start_ref, chosen_ref, slot_ref, count_ref, down_ref, up_ref, out_ref, stage, sems = refs[count:]
-    width = down_hbm.shape[0]
+    send, (chosen_ref, slot_ref, down_ref, up_ref, out_ref, sems) = refs[:count], refs[count:]
+    tables = start_all([chosen_hbm, slot_hbm], [chosen_ref, slot_ref], sems)
+    maps = start_all([down_hbm, up_hbm], [down_ref, up_ref], sems, 2)
+    ranks = partners(n, lax.axis_index("dp"), lax.axis_index("tensor"))
+    wait_all(tables)
+    onehot = slot_rows(chosen_ref, slot_ref, ranks, down_ref.shape[1])
+    picked = onehot.shape[0] // count
+    wait_all(maps)
+    columns = dot(onehot, down_ref[...], 1, 1).astype(bf16)
+    for k in range(count):
+        out_ref[k, :picked, :] = columns[k * picked : (k + 1) * picked]
+        out_ref[k, picked:, :] = up_ref[...]
+    wait_all(start_all([out_ref.at[k] for k in range(count)], send, sems, 4))
+
+
+def stage_kernel(
+    n, lay, start_hbm, chosen_hbm, slot_hbm, count_hbm, g_hbm, x_hbm, own_hbm,
+    stage_hbm, start_ref, chosen_ref, slot_ref, count_ref, stage, sems,
+):
     rows, picked, slots = lay.rows, lay.picked, lay.slots
+    width = stage.shape[1]
     tables = start_all(
         [chosen_hbm, slot_hbm, start_hbm, count_hbm], [chosen_ref, slot_ref, start_ref, count_ref], sems
     )
-    maps = start_all([down_hbm, up_hbm], [down_ref, up_ref], sems, 4)
-    gradient = start_all([g_hbm], [stage.at[pl.ds(lay.g, rows)]], sems, 6)
-    tokens = start_all(
-        [x_hbm.at[:, pl.ds(q * width, width)] for q in range(n)],
-        [stage.at[lay.x(q)] for q in range(n)],
+    gradient = start_all([g_hbm], [stage.at[pl.ds(lay.g, rows)]], sems, 4)
+    other = start_all(
+        [own_hbm] + [x_hbm.at[:, pl.ds(q * width, width)] for q in range(n)],
+        [stage.at[pl.ds(lay.message, picked + ADAPTER_RANK)]] + [stage.at[lay.x(q)] for q in range(n)],
         sems,
-        7,
+        5,
     )
     me = lax.axis_index("dp")
-    ranks = partners(n, me, lax.axis_index("tensor"))
     wait_all(tables)
-    onehot = slot_rows(chosen_ref, slot_ref, ranks, slots)
-    wait_all(maps)
-    columns = dot(onehot, down_ref[...], 1, 1).astype(bf16)
-    for k in range(1, count):
-        out_ref[k - 1, :picked, :] = columns[k * picked : (k + 1) * picked]
-        out_ref[k - 1, picked:, :] = up_ref[...]
-    done = start_all([out_ref.at[k] for k in range(count - 1)], send, sems, 7 + n)
-    stage[lay.message : lay.message + picked, :] = columns[:picked]
-    stage[lay.message + picked :, :] = up_ref[...]
-
     position = lax.broadcasted_iota(i32, (rows, slots), 0)
     group = lax.broadcasted_iota(i32, (rows, slots), 1) // ADAPTER_RANK
     segment = jnp.full((rows, slots), -1, i32)
-    segs = start_ref.shape[0]
-    for k in range(segs):
+    for k in range(start_ref.shape[0]):
         segment += jnp.where(position >= start_ref[k, me], 1, 0)
-    flag = (segment == group) | ((group == segs) & (position < count_ref[me]))
-    stage[lay.mask : lay.mask + rows, :slots] = jnp.where(flag, 1.0, 0.0).astype(bf16)
-    stage[lay.mask : lay.mask + picked, slots : 2 * slots] = onehot[:picked]
+    stage[lay.mask : lay.mask + rows, :slots] = jnp.where(segment == group, 1.0, 0.0).astype(bf16)
+    mine = slot_rows(chosen_ref, slot_ref, [me], slots)
+    stage[lay.mask : lay.mask + picked, slots : 2 * slots] = mine
     every = slot_rows(chosen_ref, slot_ref, range(n), slots)
     for k in range(n * picked // rows):
         at = pl.ds((2 + k) * slots, slots)
@@ -130,9 +134,8 @@
     live = lax.broadcasted_iota(i32, (rows, width), 0) < count_ref[me]
     g = stage[lay.g : lay.g + rows, :]
     stage[lay.g : lay.g + rows, :] = jnp.where(live, g, jnp.zeros_like(g))
-    wait_all(tokens)
-    done += start_all([stage], [stage_hbm], sems, 6 + n + count)
-    wait_all(done)
+    wait_all(other)
+    wait_all(start_all([stage], [stage_hbm], sems, 6 + n))
 
 
 def hand_on_kernel(stage, out_ref):
@@ -182,7 +185,7 @@
         message[picked:, :] = up_ref[target]
 
 
-def base_kernel(kept_ref, w_ref, after_ref, out_ref):
+def base_kernel(kept_ref, w_ref, out_ref):
     out_ref[...] = dot(kept_ref[: out_ref.shape[0], :], w_ref[...], 1, 1)
 
 
@@ -209,23 +212,23 @@
     up_ref[...] = jnp.sum(rows_ref[:, picked:, at].astype(f32), axis=0)
 
 
-def exchange(messages, beside=None):
+def exchange(messages, beside):
     n = 2 * len(messages)
-    steps = list(zip(pairs(n, 0), pairs(n, 1))) + [(1, 1)]
     got = [
         lax.ppermute(
             message,
             ("dp", "tensor"),
             [(2 * i + c, 2 * (i ^ step[c]) + c) for i in range(n) for c in range(2)],
         )
-        for message, step in zip(messages, steps)
+        for message, step in zip(messages, steps(n))
     ]
-    made = None
-    if beside is not None:
-        made = beside(got[0])
-        got[1], made = lax.optimization_barrier((got[1], made))
-    passed = [lax.ppermute(message, "tensor", [(0, 1), (1, 0)]) for message in got[:-1]]
-    return got + passed, made
+    got[0], beside = lax.optimization_barrier((got[0], beside))
+    passed = [
+        lax.ppermute(message, "tensor", [(0, 1), (1, 0)])
+        for message, (a, b) in zip(got, steps(n))
+        if a != b
+    ]
+    return got + passed, beside
 
 
 def local_kernels(
@@ -261,33 +264,32 @@
     dma = pltpu.SemaphoreType.DMA
 
     lay = Staged(n, tok_half, tok_rows, picked, column_total, slot_width)
-    *sent, stage = pl.pallas_call(
-        functools.partial(pack_kernel, n, lay),
-        out_shape=[message] * (count - 1) + [shape(lay.shape, bf16)],
-        in_specs=[HBM] * 8,
+    own, *sent = pl.pallas_call(
+        functools.partial(pack_kernel, n),
+        out_shape=[message] * count,
+        in_specs=[HBM] * 4,
         out_specs=[HBM] * count,
-        scratch_shapes=tables
+        scratch_shapes=tables[1:3]
         + [
             pltpu.VMEM(down_maps.shape, bf16),
             pltpu.VMEM(up_maps.shape, bf16),
-            pltpu.VMEM((count - 1,) + message.shape, bf16),
-            pltpu.VMEM(lay.shape, bf16),
-            dma((7 + n + count,)),
+            pltpu.VMEM((count,) + message.shape, bf16),
+            dma((4 + count,)),
         ],
         compiler_params=params(56),
-    )(
-        starts,
-        chosen,
-        adapter_slot,
-        token_count,
-        output_gradient,
-        inputs,
-        down_maps,
-        up_maps,
-    )
+    )(chosen, adapter_slot, down_maps, up_maps)
     sent, x_late = lax.optimization_barrier((sent, inputs))
-    got, _ = exchange(sent)
     x_other = lax.ppermute(x_late, "tensor", [(0, 1), (1, 0)])
+    stage = pl.pallas_call(
+        functools.partial(stage_kernel, n, lay),
+        out_shape=shape(lay.shape, bf16),
+        in_specs=[HBM] * 7,
+        out_specs=HBM,
+        scratch_shapes=tables + [pltpu.VMEM(lay.shape, bf16), dma((7 + n,))],
+        compiler_params=params(56),
+        cost_estimate=pl.CostEstimate(flops=0, bytes_accessed=1 << 21, transcendentals=0),
+    )(starts, chosen, adapter_slot, token_count, output_gradient, inputs, own)
+    got, stage = exchange(sent, stage)
     stage = pl.pallas_call(
         hand_on_kernel,
         out_shape=shape(lay.shape, bf16),
@@ -314,10 +316,10 @@
         ],
         compiler_params=params(8),
     )(stage, x_other, *got)
-    frozen = pl.pallas_call(
+    base = pl.pallas_call(
         base_kernel,
         out_shape=shape((tok_rows, half), f32),
-        in_specs=[VMEM, VMEM, pl.BlockSpec(memory_space=pl.ANY)],
+        in_specs=[VMEM, VMEM],
         out_specs=VMEM,
         compiler_params=params(8),
         cost_estimate=pl.CostEstimate(
@@ -325,8 +327,8 @@
             bytes_accessed=4 * half * tok_rows + 2 * half * out_width,
             transcendentals=0,
         ),
-    )
-    got, base = exchange(sent, functools.partial(frozen, kept, frozen_weight))
+    )(kept, frozen_weight)
+    got, base = exchange(sent, base)
 
     grad_x = pl.pallas_call(
         grad_x_kernel,

time: 28.8 us -> 28.7 us (level)
  Pallas kernels: 6.56 us -> 8.18 us
  starting transfers between devices: 14.6 us -> 13.7 us
  waiting for transfers between devices: 5.53 us -> 4.73 us
    pallas_call x2 -> x3, Pallas kernels: 3.23 us -> 4.85 us  [the longest x1 2.17 us: local_kernels(): pl.pallas_call(functools.partial(stage_kernel, n, lay), out_shape=shape(l...]
    ppermute x8, starting transfers between devices: 12.7 us -> 11.7 us  [exchange(): lax.ppermute(message, ('dp', 'tensor'), [(2 * i + c, 2 * (i ^ step[c]) +...]
    ppermute x8, waiting for transfers between devices: 5.51 us -> 4.71 us  [exchange(): lax.ppermute(message, ('dp', 'tensor'), [(2 * i + c, 2 * (i ^ step[c]) +...]
  transfers between devices with their start and end apart: 15 -> 15, of which waited for: 3 -> 4; matrix products, arithmetic and copies ran while one was open for 0% -> 0% of each run, Pallas kernels for 6% -> 14%
where the time goes in v7:
time: 28.7 us; the launch traced here: 28.5 us
  starting transfers between devices  13.7 us (48%)
  Pallas kernels  8.18 us (29%)
  waiting for transfers between devices  4.73 us (16%)
  local copies, waits for them, and re-layouts  1.15 us (4%)
  between operations  0.76 us (3%)
    ppermute x8, starting transfers between devices, exchange(): lax.ppermute(message, ('dp', 'tensor'), [(2 * i + c, 2 * (i ^ step[c]) +...  11.7 us
    ppermute x8, waiting for transfers between devices, exchange(): lax.ppermute(message, ('dp', 'tensor'), [(2 * i + c, 2 * (i ^ step[c]) +...  4.71 us
    pallas_call x1, Pallas kernels, local_kernels(): pl.pallas_call(functools.partial(stage_kernel, n, lay), out_shape=shape(l...  2.17 us
    pallas_call x1, Pallas kernels, local_kernels(): pl.pallas_call(functools.partial(pack_kernel, n), out_shape=[message] * c...  1.88 us
    ppermute x6, starting transfers between devices, exchange(): lax.ppermute(message, 'tensor', [(0, 1), (1, 0)])  1.43 us
    pallas_call x1, Pallas kernels, local_kernels(): pl.pallas_call(functools.partial(middle_kernel, n, lay), out_shape=[shape...  1.27 us
    unnamed x4, local copies, waits for them, and re-layouts  1.15 us
    pallas_call x1, Pallas kernels, local_kernels(): pl.pallas_call(functools.partial(final_kernel, n, lay), out_shape=[shape(...  1.02 us
  transfers between devices with their start and end apart: 15, of which 4 were waited for; matrix products, arithmetic and copies ran while one was open for 0% of the time, Pallas kernels for 14%

profile of v7, /device:TPU:0, one launch (start us, length us, event | category | flops | bytes accessed | tf_op | source)
XLA Modules:
  0.0 28.5 jit_solution(10227920084756858421)
XLA Ops:
  0.6 1.9 %shard_map.112 = (bf16[48,512]{1,0:T(8,128)(2,1)}, bf16[48,512]{1,0:T(8,128)(2,1)}, bf16[48,512]{1,0:T(8,128)(2,1)}, bf16[48,512]{1,0:T(8,128)(2,1)}, bf16[48,512]{1,0:T(8,128)(2,1)}) custom-call(s32[2,8]{1,0:T(2,128)} %bitcast.2, s32[8]{0:T(128)} %slot_hbm.3, bf16[512,128]{1,0:T(8,128)(2,1)} %down_hbm.1, bf16[16,512]{1,0:T(8,128)(2,1)} %up_hbm.1), custom_call_target="tpu_custom_call" | custom-call | tf_op jit(solution)/shard_map/pallas_call | solution.py:267
  2.5 0.5 %collective-permute-start.1 = (bf16[64,4096]{1,0:T(8,128)(2,1)}, bf16[64,4096]{1,0:T(8,128)(2,1)S(1)}, u32[]{:S(2)}, u32[]{:S(2)}) collective-permute-start(bf16[64,4096]{1,0:T(8,128)(2,1)} %x_hbm.1), channel_id=1, source_target_pairs={{0,1},{1,0},{2,3},{3,2},{4,5},{5,4},{6,7},{7,6},{8,9},{9,8},{10,11... | collective-permute-start | bytes 1572872 | tf_op jit(solution)/shard_map/ppermute | solution.py:282
  3.0 3.7 %collective-permute-start = (bf16[48,512]{1,0:T(8,128)(2,1)}, bf16[48,512]{1,0:T(8,128)(2,1)S(1)}, u32[]{:S(2)}, u32[]{:S(2)}) collective-permute-start(bf16[48,512]{1,0:T(8,128)(2,1)} %get-tuple-element.31), channel_id=1, source_target_pairs={{0,8},{1,11},{2,10},{3,9},{4,12},{5,15},{6,14},{7,13},{8,0},{9,3},... | collective-permute-start | bytes 147464 | tf_op jit(solution)/shard_map/ppermute | solution.py:218
  6.7 2.3 %collective-permute-start.2 = (bf16[48,512]{1,0:T(8,128)(2,1)}, bf16[48,512]{1,0:T(8,128)(2,1)S(1)}, u32[]{:S(2)}, u32[]{:S(2)}) collective-permute-start(bf16[48,512]{1,0:T(8,128)(2,1)} %get-tuple-element.36), channel_id=1, source_target_pairs={{0,14},{1,13},{2,12},{3,15},{4,10},{5,9},{6,8},{7,11},{8,6},{9,5},... | collective-permute-start | bytes 147464 | tf_op jit(solution)/shard_map/ppermute | solution.py:218
  9.0 0.0 collective-permute-start.3
  9.0 0.8 %collective-permute-start.4 = (bf16[48,512]{1,0:T(8,128)(2,1)}, bf16[48,512]{1,0:T(8,128)(2,1)S(1)}, u32[]{:S(2)}, u32[]{:S(2)}) collective-permute-start(bf16[48,512]{1,0:T(8,128)(2,1)} %get-tuple-element.38), channel_id=1, source_target_pairs={{0,2},{1,3},{2,0},{3,1},{4,6},{5,7},{6,4},{7,5},{8,10},{9,11},{10,... | collective-permute-start | bytes 147464 | tf_op jit(solution)/shard_map/ppermute | solution.py:218
  9.8 2.2 %shard_map.113.stage = bf16[816,512]{1,0:T(8,128)(2,1)} custom-call(s32[2,8]{1,0:T(2,128)} %bitcast.4, s32[2,8]{1,0:T(2,128)} %bitcast.3, s32[8]{0:T(128)} %slot_hbm.3, s32[8]{0:T(128)} %count_hbm.1, bf16[128,512]{1,0:T(8,128)(2,1)} %g_hbm.1, bf16[64,4096]{1,0:T(8,128)(2,1)} %x_hbm.1, bf16[48,512]{1,0:T(8,128)(2,1)} %get-tuple-element.32.own_hbm), custom_call_target="tpu_custom_call" | custom-call | bytes 2097152 | tf_op jit(solution)/shard_map/pallas_call | solution.py:283
  11.9 0.0 collective-permute-done.refs_0_
  12.0 0.6 %collective-permute-start.5 = (bf16[48,512]{1,0:T(8,128)(2,1)S(1)}, bf16[48,512]{1,0:T(8,128)(2,1)S(1)}, u32[]{:S(2)}, u32[]{:S(2)}) collective-permute-start(bf16[48,512]{1,0:T(8,128)(2,1)S(1)} %collective-permute-done.refs_0_), channel_id=1, source_target_pairs={{0,1},{1,0},{2,3},{3,2},{4,5},{5,4},{6,7},{7,6},{8,9},{9,8},{10,11... | collective-permute-start | bytes 147464 | tf_op jit(solution)/shard_map/ppermute | solution.py:227
  12.5 1.3 %collective-permute-done.2.refs_1_ = bf16[48,512]{1,0:T(8,128)(2,1)S(1)} collective-permute-done((bf16[48,512]{1,0:T(8,128)(2,1)}, bf16[48,512]{1,0:T(8,128)(2,1)S(1)}, u32[]{:S(2)}, u32[]{:S(2)}) %collective-permute-start.2) | collective-permute-done | bytes 49184 | tf_op jit(solution)/shard_map/ppermute | solution.py:218
  13.8 0.0 collective-permute-start.6
  13.8 0.1 collective-permute-done.3.refs_2_
  14.0 0.4 %collective-permute-start.7 = (bf16[48,512]{1,0:T(8,128)(2,1)S(1)}, bf16[48,512]{1,0:T(8,128)(2,1)S(1)}, u32[]{:S(2)}, u32[]{:S(2)}) collective-permute-start(bf16[48,512]{1,0:T(8,128)(2,1)S(1)} %collective-permute-done.3.refs_2_), channel_id=1, source_target_pairs={{0,1},{1,0},{2,3},{3,2},{4,5},{5,4},{6,7},{7,6},{8,9},{9,8},{10,11... | collective-permute-start | bytes 147464 | tf_op jit(solution)/shard_map/ppermute | solution.py:227
  14.4 0.0 copy-start
  14.4 1.1 %copy-done = bf16[816,512]{1,0:T(8,128)(2,1)S(1)} copy-done((bf16[816,512]{1,0:T(8,128)(2,1)S(1)}, bf16[816,512]{1,0:T(8,128)(2,1)}, u32[]{:S(2)}) %copy-start) | copy-done | bytes 835608
  15.5 0.0 copy-start.1
  15.5 0.1 shard_map.114.stage
  15.6 0.0 collective-permute-done.4.refs_3_
  15.6 0.0 collective-permute-done.5.refs_4_
  15.6 0.0 collective-permute-done.6.refs_5_
  15.6 0.0 collective-permute-done.7.refs_6_
  15.6 0.0 collective-permute-done.1.x_other
  15.6 1.3 %shard_map.115 = (bf16[128,32]{1,0:T(8,128)(2,1)S(1)}, bf16[4,32,512]{2,1,0:T(8,128)(2,1)S(1)}, bf16[256,512]{1,0:T(8,128)(2,1)S(1)}, bf16[48,512]{1,0:T(8,128)(...) custom-call(bf16[816,512]{1,0:T(8,128)(2,1)S(1)} %shard_map.114.stag, ...), custom_call_target="tpu_custom_call" | custom-call | tf_op jit(solution)/shard_map/pallas_call | solution.py:302
  16.9 2.2 %collective-permute-start.8 = (bf16[48,512]{1,0:T(8,128)(2,1)S(1)}, bf16[48,512]{1,0:T(8,128)(2,1)S(1)}, u32[]{:S(2)}, u32[]{:S(2)}) collective-permute-start(bf16[48,512]{1,0:T(8,128)(2,1)S(1)} %get-tuple-element.39), channel_id=1, source_target_pairs={{0,8},{1,11},{2,10},{3,9},{4,12},{5,15},{6,14},{7,13},{8,0},{9,3},... | collective-permute-start | bytes 147464 | tf_op jit(solution)/shard_map/ppermute | solution.py:218
  19.1 1.6 %collective-permute-start.9 = (bf16[48,512]{1,0:T(8,128)(2,1)S(1)}, bf16[48,512]{1,0:T(8,128)(2,1)S(1)}, u32[]{:S(2)}, u32[]{:S(2)}) collective-permute-start(bf16[48,512]{1,0:T(8,128)(2,1)S(1)} %get-tuple-element.46), channel_id=1, source_target_pairs={{0,14},{1,13},{2,12},{3,15},{4,10},{5,9},{6,8},{7,11},{8,6},{9,5},... | collective-permute-start | bytes 147464 | tf_op jit(solution)/shard_map/ppermute | solution.py:218
  20.6 0.9 %collective-permute-start.10 = (bf16[48,512]{1,0:T(8,128)(2,1)S(1)}, bf16[48,512]{1,0:T(8,128)(2,1)S(1)}, u32[]{:S(2)}, u32[]{:S(2)}) collective-permute-start(bf16[48,512]{1,0:T(8,128)(2,1)S(1)} %get-tuple-element.47), channel_id=1, source_target_pairs={{0,4},{1,7},{2,6},{3,5},{4,0},{5,3},{6,2},{7,1},{8,12},{9,15},{10,... | collective-permute-start | bytes 147464 | tf_op jit(solution)/shard_map/ppermute | solution.py:218
  21.5 0.4 %collective-permute-start.11 = (bf16[48,512]{1,0:T(8,128)(2,1)S(1)}, bf16[48,512]{1,0:T(8,128)(2,1)S(1)}, u32[]{:S(2)}, u32[]{:S(2)}) collective-permute-start(bf16[48,512]{1,0:T(8,128)(2,1)S(1)} %get-tuple-element.48), channel_id=1, source_target_pairs={{0,2},{1,3},{2,0},{3,1},{4,6},{5,7},{6,4},{7,5},{8,10},{9,11},{10,... | collective-permute-start | bytes 147464 | tf_op jit(solution)/shard_map/ppermute | solution.py:218
  21.9 0.0 copy-done.1
  21.9 0.8 %shard_map.116.base_ref = f32[128,2048]{1,0:T(8,128)S(1)} custom-call(bf16[256,512]{1,0:T(8,128)(2,1)S(1)} %get-tuple-element.40.kept_ref, bf16[2048,512]{1,0:T(8,128)(2,1)S(1)} %copy-done.1), custom_call_target="tpu_custom_call" | custom-call | flops 268435456 | bytes 3145728 | tf_op jit(solution)/shard_map/pallas_call | solution.py:319
  22.7 0.7 %collective-permute-done.8.refs_1_ = bf16[48,512]{1,0:T(8,128)(2,1)S(1)} collective-permute-done((bf16[48,512]{1,0:T(8,128)(2,1)S(1)}, bf16[48,512]{1,0:T(8,128)(2,1)S(1)}, u32[]{:S(2)}, u32[]{:S(2)}) %collective-permute-start.8) | collective-permute-done | bytes 49184 | tf_op jit(solution)/shard_map/ppermute | solution.py:218
  23.4 0.0 collective-permute-start.12
  23.4 2.5 %collective-permute-done.9.refs_2_ = bf16[48,512]{1,0:T(8,128)(2,1)S(1)} collective-permute-done((bf16[48,512]{1,0:T(8,128)(2,1)S(1)}, bf16[48,512]{1,0:T(8,128)(2,1)S(1)}, u32[]{:S(2)}, u32[]{:S(2)}) %collective-permute-start.9) | collective-permute-done | bytes 49184 | tf_op jit(solution)/shard_map/ppermute | solution.py:218
  26.0 0.0 collective-permute-start.13
  26.0 0.0 collective-permute-done.10.refs_3_
  26.0 0.5 %collective-permute-start.14 = (bf16[48,512]{1,0:T(8,128)(2,1)S(1)}, bf16[48,512]{1,0:T(8,128)(2,1)S(1)}, u32[]{:S(2)}, u32[]{:S(2)}) collective-permute-start(bf16[48,512]{1,0:T(8,128)(2,1)S(1)} %collective-permute-done.10.refs_3_), channel_id=1, source_target_pairs={{0,1},{1,0},{2,3},{3,2},{4,5},{5,4},{6,7},{7,6},{8,9},{9,8},{10,11... | collective-permute-start | bytes 147464 | tf_op jit(solution)/shard_map/ppermute | solution.py:227
  26.5 1.0 %shard_map.117 = bf16[128,2048]{1,0:T(8,128)(2,1)} custom-call(f32[128,2048]{1,0:T(8,128)S(1)} %shard_map.116.base_ref, bf16[128,32]{1,0:T(8,128)(2,1)S(1)} %get-tuple-element.42.dlow_ref, bf16[4,32,512]{2,1,0:T(8,128)(2,1)S(1)} %get-tuple-element.43.a_ref), custom_call_target="tpu_custom_call" | custom-call | flops 16777216 | bytes 1572864 | tf_op jit(solution)/shard_map/pallas_call | solution.py:333
  27.5 0.0 collective-permute-done.11.refs_4_
  27.5 0.0 collective-permute-done.12.refs_5_
  27.5 0.0 collective-permute-done.13.refs_6_
  27.5 0.0 collective-permute-done.14.refs_7_
  27.5 1.0 %shard_map.118 = (f32[512,128]{1,0:T(8,128)}, f32[16,256]{1,0:T(8,128)}) custom-call(bf16[256,512]{1,0:T(8,128)(2,1)S(1)} %get-tuple-element.40.kept_ref, bf16[48,512]{1,0:T(8,128)(2,1)S(1)} %get-tuple-element.44.refs_0_, bf16[48,512]{1,0:T(8,128)(2,1)S(1)} %collective-permute-done.8.refs_1_, bf16[48,512]{1,0:T(8,128)(2,1)S(1)} %collective-permute-done.9.refs_2_, ...), custom_call_target="tpu_custom_call" | custom-call | tf_op jit(solution)/shard_map/pallas_call | solution.py:347
Async XLA Ops:
  2.5 13.1 %collective-permute-start.1 = (bf16[64,4096]{1,0:T(8,128)(2,1)}, bf16[64,4096]{1,0:T(8,128)(2,1)S(1)}, u32[]{:S(2)}, u32[]{:S(2)}) collective-permute-start(bf16[64,4096]{1,0:T(8,128)(2,1)} %x_hbm.1), channel_id=1, source_target_pairs={{0,1},{1,0},{2,3},{3,2},{4,5},{5,4},{6,7},{7,6},{8,9},{9,8},{10,11... | collective-permute-start | bytes 1572872 | tf_op jit(solution)/shard_map/ppermute | solution.py:282
  3.0 8.9 %collective-permute-start = (bf16[48,512]{1,0:T(8,128)(2,1)}, bf16[48,512]{1,0:T(8,128)(2,1)S(1)}, u32[]{:S(2)}, u32[]{:S(2)}) collective-permute-start(bf16[48,512]{1,0:T(8,128)(2,1)} %get-tuple-element.31), channel_id=1, source_target_pairs={{0,8},{1,11},{2,10},{3,9},{4,12},{5,15},{6,14},{7,13},{8,0},{9,3},... | collective-permute-start | bytes 147464 | tf_op jit(solution)/shard_map/ppermute | solution.py:218
  6.7 7.1 %collective-permute-start.2 = (bf16[48,512]{1,0:T(8,128)(2,1)}, bf16[48,512]{1,0:T(8,128)(2,1)S(1)}, u32[]{:S(2)}, u32[]{:S(2)}) collective-permute-start(bf16[48,512]{1,0:T(8,128)(2,1)} %get-tuple-element.36), channel_id=1, source_target_pairs={{0,14},{1,13},{2,12},{3,15},{4,10},{5,9},{6,8},{7,11},{8,6},{9,5},... | collective-permute-start | bytes 147464 | tf_op jit(solution)/shard_map/ppermute | solution.py:218
  9.0 5.0 %collective-permute-start.3 = (bf16[48,512]{1,0:T(8,128)(2,1)}, bf16[48,512]{1,0:T(8,128)(2,1)S(1)}, u32[]{:S(2)}, u32[]{:S(2)}) collective-permute-start(bf16[48,512]{1,0:T(8,128)(2,1)} %get-tuple-element.37), channel_id=1, source_target_pairs={{0,4},{1,7},{2,6},{3,5},{4,0},{5,3},{6,2},{7,1},{8,12},{9,15},{10,... | collective-permute-start | bytes 147464 | tf_op jit(solution)/shard_map/ppermute | solution.py:218
  9.0 6.6 %collective-permute-start.4 = (bf16[48,512]{1,0:T(8,128)(2,1)}, bf16[48,512]{1,0:T(8,128)(2,1)S(1)}, u32[]{:S(2)}, u32[]{:S(2)}) collective-permute-start(bf16[48,512]{1,0:T(8,128)(2,1)} %get-tuple-element.38), channel_id=1, source_target_pairs={{0,2},{1,3},{2,0},{3,1},{4,6},{5,7},{6,4},{7,5},{8,10},{9,11},{10,... | collective-permute-start | bytes 147464 | tf_op jit(solution)/shard_map/ppermute | solution.py:218
  12.0 3.6 %collective-permute-start.5 = (bf16[48,512]{1,0:T(8,128)(2,1)S(1)}, bf16[48,512]{1,0:T(8,128)(2,1)S(1)}, u32[]{:S(2)}, u32[]{:S(2)}) collective-permute-start(bf16[48,512]{1,0:T(8,128)(2,1)S(1)} %collective-permute-done.refs_0_), channel_id=1, source_target_pairs={{0,1},{1,0},{2,3},{3,2},{4,5},{5,4},{6,7},{7,6},{8,9},{9,8},{10,11... | collective-permute-start | bytes 147464 | tf_op jit(solution)/shard_map/ppermute | solution.py:227
  13.8 1.7 %collective-permute-start.6 = (bf16[48,512]{1,0:T(8,128)(2,1)S(1)}, bf16[48,512]{1,0:T(8,128)(2,1)S(1)}, u32[]{:S(2)}, u32[]{:S(2)}) collective-permute-start(bf16[48,512]{1,0:T(8,128)(2,1)S(1)} %collective-permute-done.2.refs_1_), channel_id=1, source_target_pairs={{0,1},{1,0},{2,3},{3,2},{4,5},{5,4},{6,7},{7,6},{8,9},{9,8},{10,11... | collective-permute-start | bytes 147464 | tf_op jit(solution)/shard_map/ppermute | solution.py:227
  14.0 1.6 %collective-permute-start.7 = (bf16[48,512]{1,0:T(8,128)(2,1)S(1)}, bf16[48,512]{1,0:T(8,128)(2,1)S(1)}, u32[]{:S(2)}, u32[]{:S(2)}) collective-permute-start(bf16[48,512]{1,0:T(8,128)(2,1)S(1)} %collective-permute-done.3.refs_2_), channel_id=1, source_target_pairs={{0,1},{1,0},{2,3},{3,2},{4,5},{5,4},{6,7},{7,6},{8,9},{9,8},{10,11... | collective-permute-start | bytes 147464 | tf_op jit(solution)/shard_map/ppermute | solution.py:227
  14.4 1.1 %copy-start = (bf16[816,512]{1,0:T(8,128)(2,1)S(1)}, bf16[816,512]{1,0:T(8,128)(2,1)}, u32[]{:S(2)}) copy-start(bf16[816,512]{1,0:T(8,128)(2,1)} %shard_map.113.stage) | copy-start | bytes 2506756
  15.5 6.4 %copy-start.1 = (bf16[2048,512]{1,0:T(8,128)(2,1)S(1)}, bf16[2048,512]{1,0:T(8,128)(2,1)}, u32[]{:S(2)}) copy-start(bf16[2048,512]{1,0:T(8,128)(2,1)} %w_ref.1) | copy-start | bytes 6291460
  16.9 6.5 %collective-permute-start.8 = (bf16[48,512]{1,0:T(8,128)(2,1)S(1)}, bf16[48,512]{1,0:T(8,128)(2,1)S(1)}, u32[]{:S(2)}, u32[]{:S(2)}) collective-permute-start(bf16[48,512]{1,0:T(8,128)(2,1)S(1)} %get-tuple-element.39), channel_id=1, source_target_pairs={{0,8},{1,11},{2,10},{3,9},{4,12},{5,15},{6,14},{7,13},{8,0},{9,3},... | collective-permute-start | bytes 147464 | tf_op jit(solution)/shard_map/ppermute | solution.py:218
  19.1 6.9 %collective-permute-start.9 = (bf16[48,512]{1,0:T(8,128)(2,1)S(1)}, bf16[48,512]{1,0:T(8,128)(2,1)S(1)}, u32[]{:S(2)}, u32[]{:S(2)}) collective-permute-start(bf16[48,512]{1,0:T(8,128)(2,1)S(1)} %get-tuple-element.46), channel_id=1, source_target_pairs={{0,14},{1,13},{2,12},{3,15},{4,10},{5,9},{6,8},{7,11},{8,6},{9,5},... | collective-permute-start | bytes 147464 | tf_op jit(solution)/shard_map/ppermute | solution.py:218
  20.6 5.3 %collective-permute-start.10 = (bf16[48,512]{1,0:T(8,128)(2,1)S(1)}, bf16[48,512]{1,0:T(8,128)(2,1)S(1)}, u32[]{:S(2)}, u32[]{:S(2)}) collective-permute-start(bf16[48,512]{1,0:T(8,128)(2,1)S(1)} %get-tuple-element.47), channel_id=1, source_target_pairs={{0,4},{1,7},{2,6},{3,5},{4,0},{5,3},{6,2},{7,1},{8,12},{9,15},{10,... | collective-permute-start | bytes 147464 | tf_op jit(solution)/shard_map/ppermute | solution.py:218
  21.5 6.0 %collective-permute-start.11 = (bf16[48,512]{1,0:T(8,128)(2,1)S(1)}, bf16[48,512]{1,0:T(8,128)(2,1)S(1)}, u32[]{:S(2)}, u32[]{:S(2)}) collective-permute-start(bf16[48,512]{1,0:T(8,128)(2,1)S(1)} %get-tuple-element.48), channel_id=1, source_target_pairs={{0,2},{1,3},{2,0},{3,1},{4,6},{5,7},{6,4},{7,5},{8,10},{9,11},{10,... | collective-permute-start | bytes 147464 | tf_op jit(solution)/shard_map/ppermute | solution.py:218
  23.4 4.1 %collective-permute-start.12 = (bf16[48,512]{1,0:T(8,128)(2,1)S(1)}, bf16[48,512]{1,0:T(8,128)(2,1)S(1)}, u32[]{:S(2)}, u32[]{:S(2)}) collective-permute-start(bf16[48,512]{1,0:T(8,128)(2,1)S(1)} %collective-permute-done.8.refs_1_), channel_id=1, source_target_pairs={{0,1},{1,0},{2,3},{3,2},{4,5},{5,4},{6,7},{7,6},{8,9},{9,8},{10,11... | collective-permute-start | bytes 147464 | tf_op jit(solution)/shard_map/ppermute | solution.py:227
  26.0 1.5 %collective-permute-start.13 = (bf16[48,512]{1,0:T(8,128)(2,1)S(1)}, bf16[48,512]{1,0:T(8,128)(2,1)S(1)}, u32[]{:S(2)}, u32[]{:S(2)}) collective-permute-start(bf16[48,512]{1,0:T(8,128)(2,1)S(1)} %collective-permute-done.9.refs_2_), channel_id=1, source_target_pairs={{0,1},{1,0},{2,3},{3,2},{4,5},{5,4},{6,7},{7,6},{8,9},{9,8},{10,11... | collective-permute-start | bytes 147464 | tf_op jit(solution)/shard_map/ppermute | solution.py:227
  26.0 1.5 %collective-permute-start.14 = (bf16[48,512]{1,0:T(8,128)(2,1)S(1)}, bf16[48,512]{1,0:T(8,128)(2,1)S(1)}, u32[]{:S(2)}, u32[]{:S(2)}) collective-permute-start(bf16[48,512]{1,0:T(8,128)(2,1)S(1)} %collective-permute-done.10.refs_3_), channel_id=1, source_target_pairs={{0,1},{1,0},{2,3},{3,2},{4,5},{5,4},{6,7},{7,6},{8,9},{9,8},{10,11... | collective-permute-start | bytes 147464 | tf_op jit(solution)/shard_map/ppermute | solution.py:227

commit v8 on v7

--- a/solution.py
+++ b/solution.py
@@ -51,7 +51,7 @@
 
 
 def steps(n):
-    return [(n // 2, n // 2 + 1), (n - 1, n - 2), (2, 3), (1, 1)]
+    return [(n - 1, n - 2), (n // 2, n // 2 + 1), (2, 3), (1, 1)]
 
 
 def partners(n, me, core):

time: 28.7 us -> 27.9 us (0.972)
  waiting for transfers between devices: 4.73 us -> 2.88 us
  starting transfers between devices: 13.7 us -> 14.7 us
    ppermute x8, waiting for transfers between devices: 4.71 us -> 2.86 us  [exchange(): lax.ppermute(message, ('dp', 'tensor'), [(2 * i + c, 2 * (i ^ step[c]) +...]
    ppermute x8, starting transfers between devices: 11.7 us -> 12.7 us  [exchange(): lax.ppermute(message, ('dp', 'tensor'), [(2 * i + c, 2 * (i ^ step[c]) +...]
  transfers between devices with their start and end apart: 15 -> 15, of which waited for: 4 -> 3; matrix products, arithmetic and copies ran while one was open for 0% -> 0% of each run, Pallas kernels for 14% -> 15%
where the time goes in v8:
time: 27.9 us; the launch traced here: 27.7 us
  starting transfers between devices  14.7 us (53%)
  Pallas kernels  8.18 us (29%)
  waiting for transfers between devices  2.88 us (10%)
  local copies, waits for them, and re-layouts  1.15 us (4%)
  between operations  0.76 us (3%)
    ppermute x8, starting transfers between devices, exchange(): lax.ppermute(message, ('dp', 'tensor'), [(2 * i + c, 2 * (i ^ step[c]) +...  12.7 us
    ppermute x8, waiting for transfers between devices, exchange(): lax.ppermute(message, ('dp', 'tensor'), [(2 * i + c, 2 * (i ^ step[c]) +...  2.86 us
    pallas_call x1, Pallas kernels, local_kernels(): pl.pallas_call(functools.partial(stage_kernel, n, lay), out_shape=shape(l...  2.17 us
    pallas_call x1, Pallas kernels, local_kernels(): pl.pallas_call(functools.partial(pack_kernel, n), out_shape=[message] * c...  1.88 us
    ppermute x6, starting transfers between devices, exchange(): lax.ppermute(message, 'tensor', [(0, 1), (1, 0)])  1.5 us
    pallas_call x1, Pallas kernels, local_kernels(): pl.pallas_call(functools.partial(middle_kernel, n, lay), out_shape=[shape...  1.27 us
    unnamed x4, local copies, waits for them, and re-layouts  1.15 us
    pallas_call x1, Pallas kernels, local_kernels(): pl.pallas_call(functools.partial(final_kernel, n, lay), out_shape=[shape(...  1.02 us
  transfers between devices with their start and end apart: 15, of which 3 were waited for; matrix products, arithmetic and copies ran while one was open for 0% of the time, Pallas kernels for 15%

profile of v8, /device:TPU:0, one launch (start us, length us, event | category | flops | bytes accessed | tf_op | source)
XLA Modules:
  0.0 27.7 jit_solution(6095160307471546754)
XLA Ops:
  0.6 1.9 %shard_map.112 = (bf16[48,512]{1,0:T(8,128)(2,1)}, bf16[48,512]{1,0:T(8,128)(2,1)}, bf16[48,512]{1,0:T(8,128)(2,1)}, bf16[48,512]{1,0:T(8,128)(2,1)}, bf16[48,512]{1,0:T(8,128)(2,1)}) custom-call(s32[2,8]{1,0:T(2,128)} %bitcast.2, s32[8]{0:T(128)} %slot_hbm.3, bf16[512,128]{1,0:T(8,128)(2,1)} %down_hbm.1, bf16[16,512]{1,0:T(8,128)(2,1)} %up_hbm.1), custom_call_target="tpu_custom_call" | custom-call | tf_op jit(solution)/shard_map/pallas_call | solution.py:267
  2.5 0.5 %collective-permute-start.1 = (bf16[64,4096]{1,0:T(8,128)(2,1)}, bf16[64,4096]{1,0:T(8,128)(2,1)S(1)}, u32[]{:S(2)}, u32[]{:S(2)}) collective-permute-start(bf16[64,4096]{1,0:T(8,128)(2,1)} %x_hbm.1), channel_id=1, source_target_pairs={{0,1},{1,0},{2,3},{3,2},{4,5},{5,4},{6,7},{7,6},{8,9},{9,8},{10,11... | collective-permute-start | bytes 1572872 | tf_op jit(solution)/shard_map/ppermute | solution.py:282
  3.0 5.6 %collective-permute-start = (bf16[48,512]{1,0:T(8,128)(2,1)}, bf16[48,512]{1,0:T(8,128)(2,1)S(1)}, u32[]{:S(2)}, u32[]{:S(2)}) collective-permute-start(bf16[48,512]{1,0:T(8,128)(2,1)} %get-tuple-element.31), channel_id=1, source_target_pairs={{0,14},{1,13},{2,12},{3,15},{4,10},{5,9},{6,8},{7,11},{8,6},{9,5},... | collective-permute-start | bytes 147464 | tf_op jit(solution)/shard_map/ppermute | solution.py:218
  8.6 0.0 collective-permute-start.2
  8.6 0.8 %collective-permute-start.3 = (bf16[48,512]{1,0:T(8,128)(2,1)}, bf16[48,512]{1,0:T(8,128)(2,1)S(1)}, u32[]{:S(2)}, u32[]{:S(2)}) collective-permute-start(bf16[48,512]{1,0:T(8,128)(2,1)} %get-tuple-element.37), channel_id=1, source_target_pairs={{0,4},{1,7},{2,6},{3,5},{4,0},{5,3},{6,2},{7,1},{8,12},{9,15},{10,... | collective-permute-start | bytes 147464 | tf_op jit(solution)/shard_map/ppermute | solution.py:218
  9.4 0.4 %collective-permute-start.4 = (bf16[48,512]{1,0:T(8,128)(2,1)}, bf16[48,512]{1,0:T(8,128)(2,1)S(1)}, u32[]{:S(2)}, u32[]{:S(2)}) collective-permute-start(bf16[48,512]{1,0:T(8,128)(2,1)} %get-tuple-element.38), channel_id=1, source_target_pairs={{0,2},{1,3},{2,0},{3,1},{4,6},{5,7},{6,4},{7,5},{8,10},{9,11},{10,... | collective-permute-start | bytes 147464 | tf_op jit(solution)/shard_map/ppermute | solution.py:218
  9.8 2.2 %shard_map.113.stage = bf16[816,512]{1,0:T(8,128)(2,1)} custom-call(s32[2,8]{1,0:T(2,128)} %bitcast.4, s32[2,8]{1,0:T(2,128)} %bitcast.3, s32[8]{0:T(128)} %slot_hbm.3, s32[8]{0:T(128)} %count_hbm.1, bf16[128,512]{1,0:T(8,128)(2,1)} %g_hbm.1, bf16[64,4096]{1,0:T(8,128)(2,1)} %x_hbm.1, bf16[48,512]{1,0:T(8,128)(2,1)} %get-tuple-element.32.own_hbm), custom_call_target="tpu_custom_call" | custom-call | bytes 2097152 | tf_op jit(solution)/shard_map/pallas_call | solution.py:283
  12.0 0.0 collective-permute-done.refs_0_
  12.0 0.5 %collective-permute-start.5 = (bf16[48,512]{1,0:T(8,128)(2,1)S(1)}, bf16[48,512]{1,0:T(8,128)(2,1)S(1)}, u32[]{:S(2)}, u32[]{:S(2)}) collective-permute-start(bf16[48,512]{1,0:T(8,128)(2,1)S(1)} %collective-permute-done.refs_0_), channel_id=1, source_target_pairs={{0,1},{1,0},{2,3},{3,2},{4,5},{5,4},{6,7},{7,6},{8,9},{9,8},{10,11... | collective-permute-start | bytes 147464 | tf_op jit(solution)/shard_map/ppermute | solution.py:227
  12.5 1.5 %collective-permute-done.2.refs_1_ = bf16[48,512]{1,0:T(8,128)(2,1)S(1)} collective-permute-done((bf16[48,512]{1,0:T(8,128)(2,1)}, bf16[48,512]{1,0:T(8,128)(2,1)S(1)}, u32[]{:S(2)}, u32[]{:S(2)}) %collective-permute-start.2) | collective-permute-done | bytes 49184 | tf_op jit(solution)/shard_map/ppermute | solution.py:218
  14.0 0.0 collective-permute-start.6
  14.0 0.0 collective-permute-done.3.refs_2_
  14.0 0.5 %collective-permute-start.7 = (bf16[48,512]{1,0:T(8,128)(2,1)S(1)}, bf16[48,512]{1,0:T(8,128)(2,1)S(1)}, u32[]{:S(2)}, u32[]{:S(2)}) collective-permute-start(bf16[48,512]{1,0:T(8,128)(2,1)S(1)} %collective-permute-done.3.refs_2_), channel_id=1, source_target_pairs={{0,1},{1,0},{2,3},{3,2},{4,5},{5,4},{6,7},{7,6},{8,9},{9,8},{10,11... | collective-permute-start | bytes 147464 | tf_op jit(solution)/shard_map/ppermute | solution.py:227
  14.5 0.0 copy-start
  14.5 1.1 %copy-done = bf16[816,512]{1,0:T(8,128)(2,1)S(1)} copy-done((bf16[816,512]{1,0:T(8,128)(2,1)S(1)}, bf16[816,512]{1,0:T(8,128)(2,1)}, u32[]{:S(2)}) %copy-start) | copy-done | bytes 835608
  15.7 0.0 copy-start.1
  15.7 0.1 shard_map.114.stage
  15.7 0.0 collective-permute-done.4.refs_3_
  15.7 0.0 collective-permute-done.5.refs_4_
  15.7 0.0 collective-permute-done.6.refs_5_
  15.7 0.0 collective-permute-done.7.refs_6_
  15.8 0.0 collective-permute-done.1.x_other
  15.8 1.3 %shard_map.115 = (bf16[128,32]{1,0:T(8,128)(2,1)S(1)}, bf16[4,32,512]{2,1,0:T(8,128)(2,1)S(1)}, bf16[256,512]{1,0:T(8,128)(2,1)S(1)}, bf16[48,512]{1,0:T(8,128)(...) custom-call(bf16[816,512]{1,0:T(8,128)(2,1)S(1)} %shard_map.114.stag, ...), custom_call_target="tpu_custom_call" | custom-call | tf_op jit(solution)/shard_map/pallas_call | solution.py:302
  17.0 2.9 %collective-permute-start.8 = (bf16[48,512]{1,0:T(8,128)(2,1)S(1)}, bf16[48,512]{1,0:T(8,128)(2,1)S(1)}, u32[]{:S(2)}, u32[]{:S(2)}) collective-permute-start(bf16[48,512]{1,0:T(8,128)(2,1)S(1)} %get-tuple-element.39), channel_id=1, source_target_pairs={{0,14},{1,13},{2,12},{3,15},{4,10},{5,9},{6,8},{7,11},{8,6},{9,5},... | collective-permute-start | bytes 147464 | tf_op jit(solution)/shard_map/ppermute | solution.py:218
  19.9 0.0 collective-permute-start.9
  19.9 1.5 %collective-permute-start.10 = (bf16[48,512]{1,0:T(8,128)(2,1)S(1)}, bf16[48,512]{1,0:T(8,128)(2,1)S(1)}, u32[]{:S(2)}, u32[]{:S(2)}) collective-permute-start(bf16[48,512]{1,0:T(8,128)(2,1)S(1)} %get-tuple-element.47), channel_id=1, source_target_pairs={{0,4},{1,7},{2,6},{3,5},{4,0},{5,3},{6,2},{7,1},{8,12},{9,15},{10,... | collective-permute-start | bytes 147464 | tf_op jit(solution)/shard_map/ppermute | solution.py:218
  21.5 1.5 %collective-permute-start.11 = (bf16[48,512]{1,0:T(8,128)(2,1)S(1)}, bf16[48,512]{1,0:T(8,128)(2,1)S(1)}, u32[]{:S(2)}, u32[]{:S(2)}) collective-permute-start(bf16[48,512]{1,0:T(8,128)(2,1)S(1)} %get-tuple-element.48), channel_id=1, source_target_pairs={{0,2},{1,3},{2,0},{3,1},{4,6},{5,7},{6,4},{7,5},{8,10},{9,11},{10,... | collective-permute-start | bytes 147464 | tf_op jit(solution)/shard_map/ppermute | solution.py:218
  23.0 0.0 copy-done.1
  23.0 0.8 %shard_map.116.base_ref = f32[128,2048]{1,0:T(8,128)S(1)} custom-call(bf16[256,512]{1,0:T(8,128)(2,1)S(1)} %get-tuple-element.40.kept_ref, bf16[2048,512]{1,0:T(8,128)(2,1)S(1)} %copy-done.1), custom_call_target="tpu_custom_call" | custom-call | flops 268435456 | bytes 3145728 | tf_op jit(solution)/shard_map/pallas_call | solution.py:319
  23.8 0.5 %collective-permute-done.8.refs_1_ = bf16[48,512]{1,0:T(8,128)(2,1)S(1)} collective-permute-done((bf16[48,512]{1,0:T(8,128)(2,1)S(1)}, bf16[48,512]{1,0:T(8,128)(2,1)S(1)}, u32[]{:S(2)}, u32[]{:S(2)}) %collective-permute-start.8) | collective-permute-done | bytes 49184 | tf_op jit(solution)/shard_map/ppermute | solution.py:218
  24.3 0.0 collective-permute-start.12
  24.3 0.8 %collective-permute-done.9.refs_2_ = bf16[48,512]{1,0:T(8,128)(2,1)S(1)} collective-permute-done((bf16[48,512]{1,0:T(8,128)(2,1)S(1)}, bf16[48,512]{1,0:T(8,128)(2,1)S(1)}, u32[]{:S(2)}, u32[]{:S(2)}) %collective-permute-start.9) | collective-permute-done | bytes 49184 | tf_op jit(solution)/shard_map/ppermute | solution.py:218
  25.1 0.3 %collective-permute-start.13 = (bf16[48,512]{1,0:T(8,128)(2,1)S(1)}, bf16[48,512]{1,0:T(8,128)(2,1)S(1)}, u32[]{:S(2)}, u32[]{:S(2)}) collective-permute-start(bf16[48,512]{1,0:T(8,128)(2,1)S(1)} %collective-permute-done.9.refs_2_), channel_id=1, source_target_pairs={{0,1},{1,0},{2,3},{3,2},{4,5},{5,4},{6,7},{7,6},{8,9},{9,8},{10,11... | collective-permute-start | bytes 147464 | tf_op jit(solution)/shard_map/ppermute | solution.py:227
  25.5 0.0 collective-permute-done.10.refs_3_
  25.5 0.2 collective-permute-start.14
  25.7 1.0 %shard_map.117 = bf16[128,2048]{1,0:T(8,128)(2,1)} custom-call(f32[128,2048]{1,0:T(8,128)S(1)} %shard_map.116.base_ref, bf16[128,32]{1,0:T(8,128)(2,1)S(1)} %get-tuple-element.42.dlow_ref, bf16[4,32,512]{2,1,0:T(8,128)(2,1)S(1)} %get-tuple-element.43.a_ref), custom_call_target="tpu_custom_call" | custom-call | flops 16777216 | bytes 1572864 | tf_op jit(solution)/shard_map/pallas_call | solution.py:333
  26.7 0.0 collective-permute-done.11.refs_4_
  26.7 0.0 collective-permute-done.12.refs_5_
  26.7 0.0 collective-permute-done.13.refs_6_
  26.7 0.0 collective-permute-done.14.refs_7_
  26.7 1.0 %shard_map.118 = (f32[512,128]{1,0:T(8,128)}, f32[16,256]{1,0:T(8,128)}) custom-call(bf16[256,512]{1,0:T(8,128)(2,1)S(1)} %get-tuple-element.40.kept_ref, bf16[48,512]{1,0:T(8,128)(2,1)S(1)} %get-tuple-element.44.refs_0_, bf16[48,512]{1,0:T(8,128)(2,1)S(1)} %collective-permute-done.8.refs_1_, bf16[48,512]{1,0:T(8,128)(2,1)S(1)} %collective-permute-done.9.refs_2_, ...), custom_call_target="tpu_custom_call" | custom-call | tf_op jit(solution)/shard_map/pallas_call | solution.py:347
Async XLA Ops:
  2.5 13.2 %collective-permute-start.1 = (bf16[64,4096]{1,0:T(8,128)(2,1)}, bf16[64,4096]{1,0:T(8,128)(2,1)S(1)}, u32[]{:S(2)}, u32[]{:S(2)}) collective-permute-start(bf16[64,4096]{1,0:T(8,128)(2,1)} %x_hbm.1), channel_id=1, source_target_pairs={{0,1},{1,0},{2,3},{3,2},{4,5},{5,4},{6,7},{7,6},{8,9},{9,8},{10,11... | collective-permute-start | bytes 1572872 | tf_op jit(solution)/shard_map/ppermute | solution.py:282
  3.0 9.0 %collective-permute-start = (bf16[48,512]{1,0:T(8,128)(2,1)}, bf16[48,512]{1,0:T(8,128)(2,1)S(1)}, u32[]{:S(2)}, u32[]{:S(2)}) collective-permute-start(bf16[48,512]{1,0:T(8,128)(2,1)} %get-tuple-element.31), channel_id=1, source_target_pairs={{0,14},{1,13},{2,12},{3,15},{4,10},{5,9},{6,8},{7,11},{8,6},{9,5},... | collective-permute-start | bytes 147464 | tf_op jit(solution)/shard_map/ppermute | solution.py:218
  8.6 5.4 %collective-permute-start.2 = (bf16[48,512]{1,0:T(8,128)(2,1)}, bf16[48,512]{1,0:T(8,128)(2,1)S(1)}, u32[]{:S(2)}, u32[]{:S(2)}) collective-permute-start(bf16[48,512]{1,0:T(8,128)(2,1)} %get-tuple-element.36), channel_id=1, source_target_pairs={{0,8},{1,11},{2,10},{3,9},{4,12},{5,15},{6,14},{7,13},{8,0},{9,3},... | collective-permute-start | bytes 147464 | tf_op jit(solution)/shard_map/ppermute | solution.py:218
  8.6 5.4 %collective-permute-start.3 = (bf16[48,512]{1,0:T(8,128)(2,1)}, bf16[48,512]{1,0:T(8,128)(2,1)S(1)}, u32[]{:S(2)}, u32[]{:S(2)}) collective-permute-start(bf16[48,512]{1,0:T(8,128)(2,1)} %get-tuple-element.37), channel_id=1, source_target_pairs={{0,4},{1,7},{2,6},{3,5},{4,0},{5,3},{6,2},{7,1},{8,12},{9,15},{10,... | collective-permute-start | bytes 147464 | tf_op jit(solution)/shard_map/ppermute | solution.py:218
  9.4 6.3 %collective-permute-start.4 = (bf16[48,512]{1,0:T(8,128)(2,1)}, bf16[48,512]{1,0:T(8,128)(2,1)S(1)}, u32[]{:S(2)}, u32[]{:S(2)}) collective-permute-start(bf16[48,512]{1,0:T(8,128)(2,1)} %get-tuple-element.38), channel_id=1, source_target_pairs={{0,2},{1,3},{2,0},{3,1},{4,6},{5,7},{6,4},{7,5},{8,10},{9,11},{10,... | collective-permute-start | bytes 147464 | tf_op jit(solution)/shard_map/ppermute | solution.py:218
  12.0 3.7 %collective-permute-start.5 = (bf16[48,512]{1,0:T(8,128)(2,1)S(1)}, bf16[48,512]{1,0:T(8,128)(2,1)S(1)}, u32[]{:S(2)}, u32[]{:S(2)}) collective-permute-start(bf16[48,512]{1,0:T(8,128)(2,1)S(1)} %collective-permute-done.refs_0_), channel_id=1, source_target_pairs={{0,1},{1,0},{2,3},{3,2},{4,5},{5,4},{6,7},{7,6},{8,9},{9,8},{10,11... | collective-permute-start | bytes 147464 | tf_op jit(solution)/shard_map/ppermute | solution.py:227
  14.0 1.7 %collective-permute-start.6 = (bf16[48,512]{1,0:T(8,128)(2,1)S(1)}, bf16[48,512]{1,0:T(8,128)(2,1)S(1)}, u32[]{:S(2)}, u32[]{:S(2)}) collective-permute-start(bf16[48,512]{1,0:T(8,128)(2,1)S(1)} %collective-permute-done.2.refs_1_), channel_id=1, source_target_pairs={{0,1},{1,0},{2,3},{3,2},{4,5},{5,4},{6,7},{7,6},{8,9},{9,8},{10,11... | collective-permute-start | bytes 147464 | tf_op jit(solution)/shard_map/ppermute | solution.py:227
  14.0 1.8 %collective-permute-start.7 = (bf16[48,512]{1,0:T(8,128)(2,1)S(1)}, bf16[48,512]{1,0:T(8,128)(2,1)S(1)}, u32[]{:S(2)}, u32[]{:S(2)}) collective-permute-start(bf16[48,512]{1,0:T(8,128)(2,1)S(1)} %collective-permute-done.3.refs_2_), channel_id=1, source_target_pairs={{0,1},{1,0},{2,3},{3,2},{4,5},{5,4},{6,7},{7,6},{8,9},{9,8},{10,11... | collective-permute-start | bytes 147464 | tf_op jit(solution)/shard_map/ppermute | solution.py:227
  14.5 1.1 %copy-start = (bf16[816,512]{1,0:T(8,128)(2,1)S(1)}, bf16[816,512]{1,0:T(8,128)(2,1)}, u32[]{:S(2)}) copy-start(bf16[816,512]{1,0:T(8,128)(2,1)} %shard_map.113.stage) | copy-start | bytes 2506756
  15.7 7.3 %copy-start.1 = (bf16[2048,512]{1,0:T(8,128)(2,1)S(1)}, bf16[2048,512]{1,0:T(8,128)(2,1)}, u32[]{:S(2)}) copy-start(bf16[2048,512]{1,0:T(8,128)(2,1)} %w_ref.1) | copy-start | bytes 6291460
  17.0 7.3 %collective-permute-start.8 = (bf16[48,512]{1,0:T(8,128)(2,1)S(1)}, bf16[48,512]{1,0:T(8,128)(2,1)S(1)}, u32[]{:S(2)}, u32[]{:S(2)}) collective-permute-start(bf16[48,512]{1,0:T(8,128)(2,1)S(1)} %get-tuple-element.39), channel_id=1, source_target_pairs={{0,14},{1,13},{2,12},{3,15},{4,10},{5,9},{6,8},{7,11},{8,6},{9,5},... | collective-permute-start | bytes 147464 | tf_op jit(solution)/shard_map/ppermute | solution.py:218
  19.9 5.2 %collective-permute-start.9 = (bf16[48,512]{1,0:T(8,128)(2,1)S(1)}, bf16[48,512]{1,0:T(8,128)(2,1)S(1)}, u32[]{:S(2)}, u32[]{:S(2)}) collective-permute-start(bf16[48,512]{1,0:T(8,128)(2,1)S(1)} %get-tuple-element.46), channel_id=1, source_target_pairs={{0,8},{1,11},{2,10},{3,9},{4,12},{5,15},{6,14},{7,13},{8,0},{9,3},... | collective-permute-start | bytes 147464 | tf_op jit(solution)/shard_map/ppermute | solution.py:218
  19.9 5.5 %collective-permute-start.10 = (bf16[48,512]{1,0:T(8,128)(2,1)S(1)}, bf16[48,512]{1,0:T(8,128)(2,1)S(1)}, u32[]{:S(2)}, u32[]{:S(2)}) collective-permute-start(bf16[48,512]{1,0:T(8,128)(2,1)S(1)} %get-tuple-element.47), channel_id=1, source_target_pairs={{0,4},{1,7},{2,6},{3,5},{4,0},{5,3},{6,2},{7,1},{8,12},{9,15},{10,... | collective-permute-start | bytes 147464 | tf_op jit(solution)/shard_map/ppermute | solution.py:218
  21.5 5.2 %collective-permute-start.11 = (bf16[48,512]{1,0:T(8,128)(2,1)S(1)}, bf16[48,512]{1,0:T(8,128)(2,1)S(1)}, u32[]{:S(2)}, u32[]{:S(2)}) collective-permute-start(bf16[48,512]{1,0:T(8,128)(2,1)S(1)} %get-tuple-element.48), channel_id=1, source_target_pairs={{0,2},{1,3},{2,0},{3,1},{4,6},{5,7},{6,4},{7,5},{8,10},{9,11},{10,... | collective-permute-start | bytes 147464 | tf_op jit(solution)/shard_map/ppermute | solution.py:218
  24.3 2.4 %collective-permute-start.12 = (bf16[48,512]{1,0:T(8,128)(2,1)S(1)}, bf16[48,512]{1,0:T(8,128)(2,1)S(1)}, u32[]{:S(2)}, u32[]{:S(2)}) collective-permute-start(bf16[48,512]{1,0:T(8,128)(2,1)S(1)} %collective-permute-done.8.refs_1_), channel_id=1, source_target_pairs={{0,1},{1,0},{2,3},{3,2},{4,5},{5,4},{6,7},{7,6},{8,9},{9,8},{10,11... | collective-permute-start | bytes 147464 | tf_op jit(solution)/shard_map/ppermute | solution.py:227
  25.1 1.5 %collective-permute-start.13 = (bf16[48,512]{1,0:T(8,128)(2,1)S(1)}, bf16[48,512]{1,0:T(8,128)(2,1)S(1)}, u32[]{:S(2)}, u32[]{:S(2)}) collective-permute-start(bf16[48,512]{1,0:T(8,128)(2,1)S(1)} %collective-permute-done.9.refs_2_), channel_id=1, source_target_pairs={{0,1},{1,0},{2,3},{3,2},{4,5},{5,4},{6,7},{7,6},{8,9},{9,8},{10,11... | collective-permute-start | bytes 147464 | tf_op jit(solution)/shard_map/ppermute | solution.py:227
  25.5 1.2 %collective-permute-start.14 = (bf16[48,512]{1,0:T(8,128)(2,1)S(1)}, bf16[48,512]{1,0:T(8,128)(2,1)S(1)}, u32[]{:S(2)}, u32[]{:S(2)}) collective-permute-start(bf16[48,512]{1,0:T(8,128)(2,1)S(1)} %collective-permute-done.10.refs_3_), channel_id=1, source_target_pairs={{0,1},{1,0},{2,3},{3,2},{4,5},{5,4},{6,7},{7,6},{8,9},{9,8},{10,11... | collective-permute-start | bytes 147464 | tf_op jit(solution)/shard_map/ppermute | solution.py:227

commit v9 on v8

--- a/solution.py
+++ b/solution.py
@@ -51,7 +51,7 @@
 
 
 def steps(n):
-    return [(n - 1, n - 2), (n // 2, n // 2 + 1), (2, 3), (1, 1)]
+    return [(n - 1, n // 2 + 1), (3, n - 2), (2, n // 2), (1, 1)]
 
 
 def partners(n, me, core):
@@ -328,8 +328,6 @@
             transcendentals=0,
         ),
     )(kept, frozen_weight)
-    got, base = exchange(sent, base)
-
     grad_x = pl.pallas_call(
         grad_x_kernel,
         out_shape=shape((tok_rows, half), bf16),
@@ -343,6 +341,8 @@
             transcendentals=0,
         ),
     )(base, dlow, a_half)
+
+    got, grad_x = exchange(sent, grad_x)
 
     grad_a, up_map_gradient = pl.pallas_call(
         functools.partial(final_kernel, n, lay),

time: 27.9 us -> 27.6 us (0.989)
  waiting for transfers between devices: 2.88 us -> 1.59 us
  starting transfers between devices: 14.7 us -> 15.7 us
    ppermute x8, waiting for transfers between devices: 2.86 us -> 1.15 us  [exchange(): lax.ppermute(message, ('dp', 'tensor'), [(2 * i + c, 2 * (i ^ step[c]) +...]
    ppermute x8, starting transfers between devices: 12.7 us -> 14 us  [exchange(): lax.ppermute(message, ('dp', 'tensor'), [(2 * i + c, 2 * (i ^ step[c]) +...]
    ppermute x6, waiting for transfers between devices: 0.02 us -> 0.44 us  [exchange(): lax.ppermute(message, 'tensor', [(0, 1), (1, 0)])]
    ppermute x6, starting transfers between devices: 1.5 us -> 1.22 us  [exchange(): lax.ppermute(message, 'tensor', [(0, 1), (1, 0)])]
  transfers between devices with their start and end apart: 15 -> 15, of which waited for: 3 -> 5; matrix products, arithmetic and copies ran while one was open for 0% -> 0% of each run, Pallas kernels for 15% -> 15%
where the time goes in v9:
time: 27.6 us; the launch traced here: 27.4 us
  starting transfers between devices  15.7 us (57%)
  Pallas kernels  8.17 us (30%)
  waiting for transfers between devices  1.59 us (6%)
  local copies, waits for them, and re-layouts  1.15 us (4%)
  between operations  0.75 us (3%)
    ppermute x8, starting transfers between devices, exchange(): lax.ppermute(message, ('dp', 'tensor'), [(2 * i + c, 2 * (i ^ step[c]) +...  14 us
    pallas_call x1, Pallas kernels, local_kernels(): pl.pallas_call(functools.partial(stage_kernel, n, lay), out_shape=shape(l...  2.17 us
    pallas_call x1, Pallas kernels, local_kernels(): pl.pallas_call(functools.partial(pack_kernel, n), out_shape=[message] * c...  1.88 us
    pallas_call x1, Pallas kernels, local_kernels(): pl.pallas_call(functools.partial(middle_kernel, n, lay), out_shape=[shape...  1.27 us
    ppermute x6, starting transfers between devices, exchange(): lax.ppermute(message, 'tensor', [(0, 1), (1, 0)])  1.22 us
    unnamed x4, local copies, waits for them, and re-layouts  1.15 us
    ppermute x8, waiting for transfers between devices, exchange(): lax.ppermute(message, ('dp', 'tensor'), [(2 * i + c, 2 * (i ^ step[c]) +...  1.15 us
    pallas_call x1, Pallas kernels, local_kernels(): pl.pallas_call(functools.partial(final_kernel, n, lay), out_shape=[shape(...  1.01 us
  transfers between devices with their start and end apart: 15, of which 5 were waited for; matrix products, arithmetic and copies ran while one was open for 0% of the time, Pallas kernels for 15%

profile of v9, /device:TPU:0, one launch (start us, length us, event | category | flops | bytes accessed | tf_op | source)
XLA Modules:
  0.0 27.4 jit_solution(8729304598784731499)
XLA Ops:
  0.6 1.9 %shard_map.112 = (bf16[48,512]{1,0:T(8,128)(2,1)}, bf16[48,512]{1,0:T(8,128)(2,1)}, bf16[48,512]{1,0:T(8,128)(2,1)}, bf16[48,512]{1,0:T(8,128)(2,1)}, bf16[48,512]{1,0:T(8,128)(2,1)}) custom-call(s32[2,8]{1,0:T(2,128)} %bitcast.2, s32[8]{0:T(128)} %slot_hbm.3, bf16[512,128]{1,0:T(8,128)(2,1)} %down_hbm.1, bf16[16,512]{1,0:T(8,128)(2,1)} %up_hbm.1), custom_call_target="tpu_custom_call" | custom-call | tf_op jit(solution)/shard_map/pallas_call | solution.py:267
  2.5 0.5 %collective-permute-start.1 = (bf16[64,4096]{1,0:T(8,128)(2,1)}, bf16[64,4096]{1,0:T(8,128)(2,1)S(1)}, u32[]{:S(2)}, u32[]{:S(2)}) collective-permute-start(bf16[64,4096]{1,0:T(8,128)(2,1)} %x_hbm.1), channel_id=1, source_target_pairs={{0,1},{1,0},{2,3},{3,2},{4,5},{5,4},{6,7},{7,6},{8,9},{9,8},{10,11... | collective-permute-start | bytes 1572872 | tf_op jit(solution)/shard_map/ppermute | solution.py:282
  3.0 5.6 %collective-permute-start = (bf16[48,512]{1,0:T(8,128)(2,1)}, bf16[48,512]{1,0:T(8,128)(2,1)S(1)}, u32[]{:S(2)}, u32[]{:S(2)}) collective-permute-start(bf16[48,512]{1,0:T(8,128)(2,1)} %get-tuple-element.31), channel_id=1, source_target_pairs={{0,14},{1,11},{2,12},{3,9},{4,10},{5,15},{6,8},{7,13},{8,6},{9,3},... | collective-permute-start | bytes 147464 | tf_op jit(solution)/shard_map/ppermute | solution.py:218
  8.6 0.0 collective-permute-start.2
  8.6 2.0 %collective-permute-start.3 = (bf16[48,512]{1,0:T(8,128)(2,1)}, bf16[48,512]{1,0:T(8,128)(2,1)S(1)}, u32[]{:S(2)}, u32[]{:S(2)}) collective-permute-start(bf16[48,512]{1,0:T(8,128)(2,1)} %get-tuple-element.37), channel_id=1, source_target_pairs={{0,4},{1,9},{2,6},{3,11},{4,0},{5,13},{6,2},{7,15},{8,12},{9,1},{1... | collective-permute-start | bytes 147464 | tf_op jit(solution)/shard_map/ppermute | solution.py:218
  10.6 1.5 %collective-permute-start.4 = (bf16[48,512]{1,0:T(8,128)(2,1)}, bf16[48,512]{1,0:T(8,128)(2,1)S(1)}, u32[]{:S(2)}, u32[]{:S(2)}) collective-permute-start(bf16[48,512]{1,0:T(8,128)(2,1)} %get-tuple-element.38), channel_id=1, source_target_pairs={{0,2},{1,3},{2,0},{3,1},{4,6},{5,7},{6,4},{7,5},{8,10},{9,11},{10,... | collective-permute-start | bytes 147464 | tf_op jit(solution)/shard_map/ppermute | solution.py:218
  12.1 2.2 %shard_map.113.stage = bf16[816,512]{1,0:T(8,128)(2,1)} custom-call(s32[2,8]{1,0:T(2,128)} %bitcast.4, s32[2,8]{1,0:T(2,128)} %bitcast.3, s32[8]{0:T(128)} %slot_hbm.3, s32[8]{0:T(128)} %count_hbm.1, bf16[128,512]{1,0:T(8,128)(2,1)} %g_hbm.1, bf16[64,4096]{1,0:T(8,128)(2,1)} %x_hbm.1, bf16[48,512]{1,0:T(8,128)(2,1)} %get-tuple-element.32.own_hbm), custom_call_target="tpu_custom_call" | custom-call | bytes 2097152 | tf_op jit(solution)/shard_map/pallas_call | solution.py:283
  14.3 0.0 collective-permute-done.refs_0_
  14.3 0.1 collective-permute-start.5
  14.4 0.0 collective-permute-done.2.refs_1_
  14.4 0.5 %collective-permute-start.6 = (bf16[48,512]{1,0:T(8,128)(2,1)S(1)}, bf16[48,512]{1,0:T(8,128)(2,1)S(1)}, u32[]{:S(2)}, u32[]{:S(2)}) collective-permute-start(bf16[48,512]{1,0:T(8,128)(2,1)S(1)} %collective-permute-done.2.refs_1_), channel_id=1, source_target_pairs={{0,1},{1,0},{2,3},{3,2},{4,5},{5,4},{6,7},{7,6},{8,9},{9,8},{10,11... | collective-permute-start | bytes 147464 | tf_op jit(solution)/shard_map/ppermute | solution.py:227
  14.9 0.0 collective-permute-done.3.refs_2_
  14.9 0.1 collective-permute-start.7
  15.0 0.0 copy-start
  15.0 1.1 %copy-done = bf16[816,512]{1,0:T(8,128)(2,1)S(1)} copy-done((bf16[816,512]{1,0:T(8,128)(2,1)S(1)}, bf16[816,512]{1,0:T(8,128)(2,1)}, u32[]{:S(2)}) %copy-start) | copy-done | bytes 835608
  16.1 0.0 copy-start.1
  16.1 0.1 shard_map.114.stage
  16.2 0.0 collective-permute-done.4.refs_3_
  16.2 0.0 collective-permute-done.5.refs_4_
  16.2 0.0 collective-permute-done.6.refs_5_
  16.2 0.0 collective-permute-done.7.refs_6_
  16.2 0.0 collective-permute-done.1.x_other
  16.2 1.3 %shard_map.115 = (bf16[128,32]{1,0:T(8,128)(2,1)S(1)}, bf16[4,32,512]{2,1,0:T(8,128)(2,1)S(1)}, bf16[256,512]{1,0:T(8,128)(2,1)S(1)}, bf16[48,512]{1,0:T(8,128)(...) custom-call(bf16[816,512]{1,0:T(8,128)(2,1)S(1)} %shard_map.114.stag, ...), custom_call_target="tpu_custom_call" | custom-call | tf_op jit(solution)/shard_map/pallas_call | solution.py:302
  17.5 1.4 %collective-permute-start.8 = (bf16[48,512]{1,0:T(8,128)(2,1)S(1)}, bf16[48,512]{1,0:T(8,128)(2,1)S(1)}, u32[]{:S(2)}, u32[]{:S(2)}) collective-permute-start(bf16[48,512]{1,0:T(8,128)(2,1)S(1)} %get-tuple-element.39), channel_id=1, source_target_pairs={{0,14},{1,11},{2,12},{3,9},{4,10},{5,15},{6,8},{7,13},{8,6},{9,3},... | collective-permute-start | bytes 147464 | tf_op jit(solution)/shard_map/ppermute | solution.py:218
  18.9 0.0 collective-permute-start.9
  19.0 2.9 %collective-permute-start.10 = (bf16[48,512]{1,0:T(8,128)(2,1)S(1)}, bf16[48,512]{1,0:T(8,128)(2,1)S(1)}, u32[]{:S(2)}, u32[]{:S(2)}) collective-permute-start(bf16[48,512]{1,0:T(8,128)(2,1)S(1)} %get-tuple-element.47), channel_id=1, source_target_pairs={{0,4},{1,9},{2,6},{3,11},{4,0},{5,13},{6,2},{7,15},{8,12},{9,1},{1... | collective-permute-start | bytes 147464 | tf_op jit(solution)/shard_map/ppermute | solution.py:218
  21.9 0.6 %collective-permute-start.11 = (bf16[48,512]{1,0:T(8,128)(2,1)S(1)}, bf16[48,512]{1,0:T(8,128)(2,1)S(1)}, u32[]{:S(2)}, u32[]{:S(2)}) collective-permute-start(bf16[48,512]{1,0:T(8,128)(2,1)S(1)} %get-tuple-element.48), channel_id=1, source_target_pairs={{0,2},{1,3},{2,0},{3,1},{4,6},{5,7},{6,4},{7,5},{8,10},{9,11},{10,... | collective-permute-start | bytes 147464 | tf_op jit(solution)/shard_map/ppermute | solution.py:218
  22.4 0.0 copy-done.1
  22.4 0.8 %shard_map.116.base_ref = f32[128,2048]{1,0:T(8,128)S(1)} custom-call(bf16[256,512]{1,0:T(8,128)(2,1)S(1)} %get-tuple-element.40.kept_ref, bf16[2048,512]{1,0:T(8,128)(2,1)S(1)} %copy-done.1), custom_call_target="tpu_custom_call" | custom-call | flops 268435456 | bytes 3145728 | tf_op jit(solution)/shard_map/pallas_call | solution.py:319
  23.2 1.0 %shard_map.117 = bf16[128,2048]{1,0:T(8,128)(2,1)} custom-call(f32[128,2048]{1,0:T(8,128)S(1)} %shard_map.116.base_ref, bf16[128,32]{1,0:T(8,128)(2,1)S(1)} %get-tuple-element.41.dlow_ref, bf16[4,32,512]{2,1,0:T(8,128)(2,1)S(1)} %get-tuple-element.42.a_ref), custom_call_target="tpu_custom_call" | custom-call | flops 16777216 | bytes 1572864 | tf_op jit(solution)/shard_map/pallas_call | solution.py:331
  24.2 0.3 %collective-permute-done.8.refs_1_ = bf16[48,512]{1,0:T(8,128)(2,1)S(1)} collective-permute-done((bf16[48,512]{1,0:T(8,128)(2,1)S(1)}, bf16[48,512]{1,0:T(8,128)(2,1)S(1)}, u32[]{:S(2)}, u32[]{:S(2)}) %collective-permute-start.8) | collective-permute-done | bytes 49184 | tf_op jit(solution)/shard_map/ppermute | solution.py:218
  24.5 0.0 collective-permute-start.12
  24.5 0.4 %collective-permute-done.9.refs_2_ = bf16[48,512]{1,0:T(8,128)(2,1)S(1)} collective-permute-done((bf16[48,512]{1,0:T(8,128)(2,1)S(1)}, bf16[48,512]{1,0:T(8,128)(2,1)S(1)}, u32[]{:S(2)}, u32[]{:S(2)}) %collective-permute-start.9) | collective-permute-done | bytes 49184 | tf_op jit(solution)/shard_map/ppermute | solution.py:218
  24.9 0.2 collective-permute-start.13
  25.0 0.0 collective-permute-done.10.refs_3_
  25.1 0.4 %collective-permute-start.14 = (bf16[48,512]{1,0:T(8,128)(2,1)S(1)}, bf16[48,512]{1,0:T(8,128)(2,1)S(1)}, u32[]{:S(2)}, u32[]{:S(2)}) collective-permute-start(bf16[48,512]{1,0:T(8,128)(2,1)S(1)} %collective-permute-done.10.refs_3_), channel_id=1, source_target_pairs={{0,1},{1,0},{2,3},{3,2},{4,5},{5,4},{6,7},{7,6},{8,9},{9,8},{10,11... | collective-permute-start | bytes 147464 | tf_op jit(solution)/shard_map/ppermute | solution.py:227
  25.5 0.5 %collective-permute-done.11.refs_4_ = bf16[48,512]{1,0:T(8,128)(2,1)S(1)} collective-permute-done((bf16[48,512]{1,0:T(8,128)(2,1)S(1)}, bf16[48,512]{1,0:T(8,128)(2,1)S(1)}, u32[]{:S(2)}, u32[]{:S(2)}) %collective-permute-start.11) | collective-permute-done | bytes 49184 | tf_op jit(solution)/shard_map/ppermute | solution.py:218
  26.0 0.0 collective-permute-done.12.refs_5_
  26.0 0.2 collective-permute-done.13.refs_6_
  26.1 0.3 collective-permute-done.14.refs_7_
  26.4 1.0 %shard_map.118 = (f32[512,128]{1,0:T(8,128)}, f32[16,256]{1,0:T(8,128)}) custom-call(bf16[256,512]{1,0:T(8,128)(2,1)S(1)} %get-tuple-element.40.kept_ref, bf16[48,512]{1,0:T(8,128)(2,1)S(1)} %get-tuple-element.44.refs_0_, bf16[48,512]{1,0:T(8,128)(2,1)S(1)} %collective-permute-done.8.refs_1_, bf16[48,512]{1,0:T(8,128)(2,1)S(1)} %collective-permute-done.9.refs_2_, ...), custom_call_target="tpu_custom_call" | custom-call | tf_op jit(solution)/shard_map/pallas_call | solution.py:347
Async XLA Ops:
  2.5 13.7 %collective-permute-start.1 = (bf16[64,4096]{1,0:T(8,128)(2,1)}, bf16[64,4096]{1,0:T(8,128)(2,1)S(1)}, u32[]{:S(2)}, u32[]{:S(2)}) collective-permute-start(bf16[64,4096]{1,0:T(8,128)(2,1)} %x_hbm.1), channel_id=1, source_target_pairs={{0,1},{1,0},{2,3},{3,2},{4,5},{5,4},{6,7},{7,6},{8,9},{9,8},{10,11... | collective-permute-start | bytes 1572872 | tf_op jit(solution)/shard_map/ppermute | solution.py:282
  3.0 11.3 %collective-permute-start = (bf16[48,512]{1,0:T(8,128)(2,1)}, bf16[48,512]{1,0:T(8,128)(2,1)S(1)}, u32[]{:S(2)}, u32[]{:S(2)}) collective-permute-start(bf16[48,512]{1,0:T(8,128)(2,1)} %get-tuple-element.31), channel_id=1, source_target_pairs={{0,14},{1,11},{2,12},{3,9},{4,10},{5,15},{6,8},{7,13},{8,6},{9,3},... | collective-permute-start | bytes 147464 | tf_op jit(solution)/shard_map/ppermute | solution.py:218
  8.6 5.8 %collective-permute-start.2 = (bf16[48,512]{1,0:T(8,128)(2,1)}, bf16[48,512]{1,0:T(8,128)(2,1)S(1)}, u32[]{:S(2)}, u32[]{:S(2)}) collective-permute-start(bf16[48,512]{1,0:T(8,128)(2,1)} %get-tuple-element.36), channel_id=1, source_target_pairs={{0,6},{1,13},{2,4},{3,15},{4,2},{5,9},{6,0},{7,11},{8,14},{9,5},{1... | collective-permute-start | bytes 147464 | tf_op jit(solution)/shard_map/ppermute | solution.py:218
  8.6 6.3 %collective-permute-start.3 = (bf16[48,512]{1,0:T(8,128)(2,1)}, bf16[48,512]{1,0:T(8,128)(2,1)S(1)}, u32[]{:S(2)}, u32[]{:S(2)}) collective-permute-start(bf16[48,512]{1,0:T(8,128)(2,1)} %get-tuple-element.37), channel_id=1, source_target_pairs={{0,4},{1,9},{2,6},{3,11},{4,0},{5,13},{6,2},{7,15},{8,12},{9,1},{1... | collective-permute-start | bytes 147464 | tf_op jit(solution)/shard_map/ppermute | solution.py:218
  10.6 5.6 %collective-permute-start.4 = (bf16[48,512]{1,0:T(8,128)(2,1)}, bf16[48,512]{1,0:T(8,128)(2,1)S(1)}, u32[]{:S(2)}, u32[]{:S(2)}) collective-permute-start(bf16[48,512]{1,0:T(8,128)(2,1)} %get-tuple-element.38), channel_id=1, source_target_pairs={{0,2},{1,3},{2,0},{3,1},{4,6},{5,7},{6,4},{7,5},{8,10},{9,11},{10,... | collective-permute-start | bytes 147464 | tf_op jit(solution)/shard_map/ppermute | solution.py:218
  14.3 1.9 %collective-permute-start.5 = (bf16[48,512]{1,0:T(8,128)(2,1)S(1)}, bf16[48,512]{1,0:T(8,128)(2,1)S(1)}, u32[]{:S(2)}, u32[]{:S(2)}) collective-permute-start(bf16[48,512]{1,0:T(8,128)(2,1)S(1)} %collective-permute-done.refs_0_), channel_id=1, source_target_pairs={{0,1},{1,0},{2,3},{3,2},{4,5},{5,4},{6,7},{7,6},{8,9},{9,8},{10,11... | collective-permute-start | bytes 147464 | tf_op jit(solution)/shard_map/ppermute | solution.py:227
  14.4 1.8 %collective-permute-start.6 = (bf16[48,512]{1,0:T(8,128)(2,1)S(1)}, bf16[48,512]{1,0:T(8,128)(2,1)S(1)}, u32[]{:S(2)}, u32[]{:S(2)}) collective-permute-start(bf16[48,512]{1,0:T(8,128)(2,1)S(1)} %collective-permute-done.2.refs_1_), channel_id=1, source_target_pairs={{0,1},{1,0},{2,3},{3,2},{4,5},{5,4},{6,7},{7,6},{8,9},{9,8},{10,11... | collective-permute-start | bytes 147464 | tf_op jit(solution)/shard_map/ppermute | solution.py:227
  14.9 1.3 %collective-permute-start.7 = (bf16[48,512]{1,0:T(8,128)(2,1)S(1)}, bf16[48,512]{1,0:T(8,128)(2,1)S(1)}, u32[]{:S(2)}, u32[]{:S(2)}) collective-permute-start(bf16[48,512]{1,0:T(8,128)(2,1)S(1)} %collective-permute-done.3.refs_2_), channel_id=1, source_target_pairs={{0,1},{1,0},{2,3},{3,2},{4,5},{5,4},{6,7},{7,6},{8,9},{9,8},{10,11... | collective-permute-start | bytes 147464 | tf_op jit(solution)/shard_map/ppermute | solution.py:227
  15.0 1.1 %copy-start = (bf16[816,512]{1,0:T(8,128)(2,1)S(1)}, bf16[816,512]{1,0:T(8,128)(2,1)}, u32[]{:S(2)}) copy-start(bf16[816,512]{1,0:T(8,128)(2,1)} %shard_map.113.stage) | copy-start | bytes 2506756
  16.1 6.3 %copy-start.1 = (bf16[2048,512]{1,0:T(8,128)(2,1)S(1)}, bf16[2048,512]{1,0:T(8,128)(2,1)}, u32[]{:S(2)}) copy-start(bf16[2048,512]{1,0:T(8,128)(2,1)} %w_ref.1) | copy-start | bytes 6291460
  17.5 7.0 %collective-permute-start.8 = (bf16[48,512]{1,0:T(8,128)(2,1)S(1)}, bf16[48,512]{1,0:T(8,128)(2,1)S(1)}, u32[]{:S(2)}, u32[]{:S(2)}) collective-permute-start(bf16[48,512]{1,0:T(8,128)(2,1)S(1)} %get-tuple-element.39), channel_id=1, source_target_pairs={{0,14},{1,11},{2,12},{3,9},{4,10},{5,15},{6,8},{7,13},{8,6},{9,3},... | collective-permute-start | bytes 147464 | tf_op jit(solution)/shard_map/ppermute | solution.py:218
  18.9 6.0 %collective-permute-start.9 = (bf16[48,512]{1,0:T(8,128)(2,1)S(1)}, bf16[48,512]{1,0:T(8,128)(2,1)S(1)}, u32[]{:S(2)}, u32[]{:S(2)}) collective-permute-start(bf16[48,512]{1,0:T(8,128)(2,1)S(1)} %get-tuple-element.46), channel_id=1, source_target_pairs={{0,6},{1,13},{2,4},{3,15},{4,2},{5,9},{6,0},{7,11},{8,14},{9,5},{1... | collective-permute-start | bytes 147464 | tf_op jit(solution)/shard_map/ppermute | solution.py:218
  19.0 6.1 %collective-permute-start.10 = (bf16[48,512]{1,0:T(8,128)(2,1)S(1)}, bf16[48,512]{1,0:T(8,128)(2,1)S(1)}, u32[]{:S(2)}, u32[]{:S(2)}) collective-permute-start(bf16[48,512]{1,0:T(8,128)(2,1)S(1)} %get-tuple-element.47), channel_id=1, source_target_pairs={{0,4},{1,9},{2,6},{3,11},{4,0},{5,13},{6,2},{7,15},{8,12},{9,1},{1... | collective-permute-start | bytes 147464 | tf_op jit(solution)/shard_map/ppermute | solution.py:218
  21.9 4.1 %collective-permute-start.11 = (bf16[48,512]{1,0:T(8,128)(2,1)S(1)}, bf16[48,512]{1,0:T(8,128)(2,1)S(1)}, u32[]{:S(2)}, u32[]{:S(2)}) collective-permute-start(bf16[48,512]{1,0:T(8,128)(2,1)S(1)} %get-tuple-element.48), channel_id=1, source_target_pairs={{0,2},{1,3},{2,0},{3,1},{4,6},{5,7},{6,4},{7,5},{8,10},{9,11},{10,... | collective-permute-start | bytes 147464 | tf_op jit(solution)/shard_map/ppermute | solution.py:218
  24.5 1.4 %collective-permute-start.12 = (bf16[48,512]{1,0:T(8,128)(2,1)S(1)}, bf16[48,512]{1,0:T(8,128)(2,1)S(1)}, u32[]{:S(2)}, u32[]{:S(2)}) collective-permute-start(bf16[48,512]{1,0:T(8,128)(2,1)S(1)} %collective-permute-done.8.refs_1_), channel_id=1, source_target_pairs={{0,1},{1,0},{2,3},{3,2},{4,5},{5,4},{6,7},{7,6},{8,9},{9,8},{10,11... | collective-permute-start | bytes 147464 | tf_op jit(solution)/shard_map/ppermute | solution.py:227
  24.9 1.2 %collective-permute-start.13 = (bf16[48,512]{1,0:T(8,128)(2,1)S(1)}, bf16[48,512]{1,0:T(8,128)(2,1)S(1)}, u32[]{:S(2)}, u32[]{:S(2)}) collective-permute-start(bf16[48,512]{1,0:T(8,128)(2,1)S(1)} %collective-permute-done.9.refs_2_), channel_id=1, source_target_pairs={{0,1},{1,0},{2,3},{3,2},{4,5},{5,4},{6,7},{7,6},{8,9},{9,8},{10,11... | collective-permute-start | bytes 147464 | tf_op jit(solution)/shard_map/ppermute | solution.py:227
  25.1 1.3 %collective-permute-start.14 = (bf16[48,512]{1,0:T(8,128)(2,1)S(1)}, bf16[48,512]{1,0:T(8,128)(2,1)S(1)}, u32[]{:S(2)}, u32[]{:S(2)}) collective-permute-start(bf16[48,512]{1,0:T(8,128)(2,1)S(1)} %collective-permute-done.10.refs_3_), channel_id=1, source_target_pairs={{0,1},{1,0},{2,3},{3,2},{4,5},{5,4},{6,7},{7,6},{8,9},{9,8},{10,11... | collective-permute-start | bytes 147464 | tf_op jit(solution)/shard_map/ppermute | solution.py:227

commit v10 on v9

--- a/solution.py
+++ b/solution.py
@@ -50,17 +50,20 @@
         copy.wait()
 
 
-def steps(n):
-    return [(n - 1, n // 2 + 1), (3, n - 2), (2, n // 2), (1, 1)]
-
-
-def partners(n, me, core):
-    return [me] + [me ^ jnp.where(core == 0, a, b) for a, b in steps(n)]
-
-
-def senders(n, me, core):
-    passed = [me ^ jnp.where(core == 0, b, a) for a, b in steps(n) if a != b]
-    return partners(n, me, core) + passed
+def steps(n, turn):
+    half = n // 2
+    if turn == 0:
+        return [(half, half + 1), (n - 1, n - 2), (2, 3), (1, 1)]
+    return [(n - 1, half + 1), (2, half), (n - 2, 3), (1, 1)]
+
+
+def partners(n, turn, me, core):
+    return [me] + [me ^ jnp.where(core == 0, a, b) for a, b in steps(n, turn)]
+
+
+def senders(n, turn, me, core):
+    passed = [me ^ jnp.where(core == 0, b, a) for a, b in steps(n, turn) if a != b]
+    return partners(n, turn, me, core) + passed
 
 
 class Staged:
@@ -88,7 +91,7 @@
     send, (chosen_ref, slot_ref, down_ref, up_ref, out_ref, sems) = refs[:count], refs[count:]
     tables = start_all([chosen_hbm, slot_hbm], [chosen_ref, slot_ref], sems)
     maps = start_all([down_hbm, up_hbm], [down_ref, up_ref], sems, 2)
-    ranks = partners(n, lax.axis_index("dp"), lax.axis_index("tensor"))
+    ranks = partners(n, 0, lax.axis_index("dp"), lax.axis_index("tensor"))
     wait_all(tables)
     onehot = slot_rows(chosen_ref, slot_ref, ranks, down_ref.shape[1])
     picked = onehot.shape[0] // count
@@ -154,7 +157,7 @@
     for q in range(n):
         x_ref[mine, q * width : (q + 1) * width] = stage[lay.x(q), :]
     x_ref[other, :] = x_other[...]
-    ranks = senders(n, me, core)
+    ranks = senders(n, 0, me, core)
     got_ref[me] = stage[lay.message :, :]
     for sender, message in zip(ranks[1:], got):
         got_ref[sender] = message[...]
@@ -169,7 +172,7 @@
     parts = n // 2
     a_ref[...] = got_ref[pl.ds(pl.multiple_of(core * parts, parts), parts), :picked, :]
     kept_ref[...] = stage[lay.g : lay.message, :]
-    targets = partners(n, me, core)
+    targets = partners(n, 1, me, core)
     for target, message in zip(targets, send):
         at = pl.ds(pl.multiple_of(target * width, width), width)
         message[:picked, :] = dot(dlow, x_ref[:, at], 0, 0).astype(bf16)
@@ -204,7 +207,7 @@
     got, (a_ref, up_ref, rows_ref) = refs[:n], refs[n:]
     me, core = lax.axis_index("dp"), lax.axis_index("tensor")
     piece, picked = up_ref.shape[1], lay.picked
-    for sender, message in zip(senders(n, me, core), got):
+    for sender, message in zip(senders(n, 1, me, core), got):
         rows_ref[sender] = message[...]
     rows = rows_ref[:, :picked, :].reshape(n * picked, rows_ref.shape[2])
     a_ref[...] = dot(rows, lay.all_rows(kept_ref), 0, 0)
@@ -212,7 +215,7 @@
     up_ref[...] = jnp.sum(rows_ref[:, picked:, at].astype(f32), axis=0)
 
 
-def exchange(messages, beside):
+def exchange(messages, turn, beside):
     n = 2 * len(messages)
     got = [
         lax.ppermute(
@@ -220,12 +223,12 @@
             ("dp", "tensor"),
             [(2 * i + c, 2 * (i ^ step[c]) + c) for i in range(n) for c in range(2)],
         )
-        for message, step in zip(messages, steps(n))
+        for message, step in zip(messages, steps(n, turn))
     ]
     got[0], beside = lax.optimization_barrier((got[0], beside))
     passed = [
         lax.ppermute(message, "tensor", [(0, 1), (1, 0)])
-        for message, (a, b) in zip(got, steps(n))
+        for message, (a, b) in zip(got, steps(n, turn))
         if a != b
     ]
     return got + passed, beside
@@ -289,7 +292,7 @@
         compiler_params=params(56),
         cost_estimate=pl.CostEstimate(flops=0, bytes_accessed=1 << 21, transcendentals=0),
     )(starts, chosen, adapter_slot, token_count, output_gradient, inputs, own)
-    got, stage = exchange(sent, stage)
+    got, stage = exchange(sent, 0, stage)
     stage = pl.pallas_call(
         hand_on_kernel,
         out_shape=shape(lay.shape, bf16),
@@ -342,7 +345,7 @@
         ),
     )(base, dlow, a_half)
 
-    got, grad_x = exchange(sent, grad_x)
+    got, grad_x = exchange(sent, 1, grad_x)
 
     grad_a, up_map_gradient = pl.pallas_call(
         functools.partial(final_kernel, n, lay),

time: 27.6 us -> 28.5 us (1.033)
  waiting for transfers between devices: 1.59 us -> 4.57 us
  starting transfers between devices: 15.7 us -> 13.6 us
    ppermute x8, waiting for transfers between devices: 1.15 us -> 3.34 us  [exchange(): lax.ppermute(message, ('dp', 'tensor'), [(2 * i + c, 2 * (i ^ step[c]) +...]
    ppermute x8, starting transfers between devices: 14 us -> 12.1 us  [exchange(): lax.ppermute(message, ('dp', 'tensor'), [(2 * i + c, 2 * (i ^ step[c]) +...]
    ppermute x6, waiting for transfers between devices: 0.44 us -> 1.23 us  [exchange(): lax.ppermute(message, 'tensor', [(0, 1), (1, 0)])]
  transfers between devices with their start and end apart: 15 -> 15, of which waited for: 5 -> 6; matrix products, arithmetic and copies ran while one was open for 0% -> 0% of each run, Pallas kernels for 15% -> 14%
where the time goes in v10:
time: 28.5 us; the launch traced here: 28.2 us
  starting transfers between devices  13.6 us (48%)
  Pallas kernels  8.17 us (29%)
  waiting for transfers between devices  4.57 us (16%)
  local copies, waits for them, and re-layouts  1.15 us (4%)
  between operations  0.75 us (3%)
    ppermute x8, starting transfers between devices, exchange(): lax.ppermute(message, ('dp', 'tensor'), [(2 * i + c, 2 * (i ^ step[c]) +...  12.1 us
    ppermute x8, waiting for transfers between devices, exchange(): lax.ppermute(message, ('dp', 'tensor'), [(2 * i + c, 2 * (i ^ step[c]) +...  3.34 us
    pallas_call x1, Pallas kernels, local_kernels(): pl.pallas_call(functools.partial(stage_kernel, n, lay), out_shape=shape(l...  2.17 us
    pallas_call x1, Pallas kernels, local_kernels(): pl.pallas_call(functools.partial(pack_kernel, n), out_shape=[message] * c...  1.88 us
    pallas_call x1, Pallas kernels, local_kernels(): pl.pallas_call(functools.partial(middle_kernel, n, lay), out_shape=[shape...  1.26 us
    ppermute x6, waiting for transfers between devices, exchange(): lax.ppermute(message, 'tensor', [(0, 1), (1, 0)])  1.23 us
    unnamed x4, local copies, waits for them, and re-layouts  1.15 us
    pallas_call x1, Pallas kernels, local_kernels(): pl.pallas_call(functools.partial(final_kernel, n, lay), out_shape=[shape(...  1.01 us
  transfers between devices with their start and end apart: 15, of which 6 were waited for; matrix products, arithmetic and copies ran while one was open for 0% of the time, Pallas kernels for 14%

profile of v10, /device:TPU:0, one launch (start us, length us, event | category | flops | bytes accessed | tf_op | source)
XLA Modules:
  0.0 28.2 jit_solution(15092809763526293813)
XLA Ops:
  0.6 1.9 %shard_map.112 = (bf16[48,512]{1,0:T(8,128)(2,1)}, bf16[48,512]{1,0:T(8,128)(2,1)}, bf16[48,512]{1,0:T(8,128)(2,1)}, bf16[48,512]{1,0:T(8,128)(2,1)}, bf16[48,512]{1,0:T(8,128)(2,1)}) custom-call(s32[2,8]{1,0:T(2,128)} %bitcast.2, s32[8]{0:T(128)} %slot_hbm.3, bf16[512,128]{1,0:T(8,128)(2,1)} %down_hbm.1, bf16[16,512]{1,0:T(8,128)(2,1)} %up_hbm.1), custom_call_target="tpu_custom_call" | custom-call | tf_op jit(solution)/shard_map/pallas_call | solution.py:270
  2.5 0.5 %collective-permute-start.1 = (bf16[64,4096]{1,0:T(8,128)(2,1)}, bf16[64,4096]{1,0:T(8,128)(2,1)S(1)}, u32[]{:S(2)}, u32[]{:S(2)}) collective-permute-start(bf16[64,4096]{1,0:T(8,128)(2,1)} %x_hbm.1), channel_id=1, source_target_pairs={{0,1},{1,0},{2,3},{3,2},{4,5},{5,4},{6,7},{7,6},{8,9},{9,8},{10,11... | collective-permute-start | bytes 1572872 | tf_op jit(solution)/shard_map/ppermute | solution.py:285
  3.0 3.7 %collective-permute-start = (bf16[48,512]{1,0:T(8,128)(2,1)}, bf16[48,512]{1,0:T(8,128)(2,1)S(1)}, u32[]{:S(2)}, u32[]{:S(2)}) collective-permute-start(bf16[48,512]{1,0:T(8,128)(2,1)} %get-tuple-element.31), channel_id=1, source_target_pairs={{0,8},{1,11},{2,10},{3,9},{4,12},{5,15},{6,14},{7,13},{8,0},{9,3},... | collective-permute-start | bytes 147464 | tf_op jit(solution)/shard_map/ppermute | solution.py:221
  6.7 2.3 %collective-permute-start.2 = (bf16[48,512]{1,0:T(8,128)(2,1)}, bf16[48,512]{1,0:T(8,128)(2,1)S(1)}, u32[]{:S(2)}, u32[]{:S(2)}) collective-permute-start(bf16[48,512]{1,0:T(8,128)(2,1)} %get-tuple-element.36), channel_id=1, source_target_pairs={{0,14},{1,13},{2,12},{3,15},{4,10},{5,9},{6,8},{7,11},{8,6},{9,5},... | collective-permute-start | bytes 147464 | tf_op jit(solution)/shard_map/ppermute | solution.py:221
  9.0 0.0 collective-permute-start.3
  9.0 0.8 %collective-permute-start.4 = (bf16[48,512]{1,0:T(8,128)(2,1)}, bf16[48,512]{1,0:T(8,128)(2,1)S(1)}, u32[]{:S(2)}, u32[]{:S(2)}) collective-permute-start(bf16[48,512]{1,0:T(8,128)(2,1)} %get-tuple-element.38), channel_id=1, source_target_pairs={{0,2},{1,3},{2,0},{3,1},{4,6},{5,7},{6,4},{7,5},{8,10},{9,11},{10,... | collective-permute-start | bytes 147464 | tf_op jit(solution)/shard_map/ppermute | solution.py:221
  9.8 2.2 %shard_map.113.stage = bf16[816,512]{1,0:T(8,128)(2,1)} custom-call(s32[2,8]{1,0:T(2,128)} %bitcast.4, s32[2,8]{1,0:T(2,128)} %bitcast.3, s32[8]{0:T(128)} %slot_hbm.3, s32[8]{0:T(128)} %count_hbm.1, bf16[128,512]{1,0:T(8,128)(2,1)} %g_hbm.1, bf16[64,4096]{1,0:T(8,128)(2,1)} %x_hbm.1, bf16[48,512]{1,0:T(8,128)(2,1)} %get-tuple-element.32.own_hbm), custom_call_target="tpu_custom_call" | custom-call | bytes 2097152 | tf_op jit(solution)/shard_map/pallas_call | solution.py:286
  11.9 0.0 collective-permute-done.refs_0_
  12.0 0.6 %collective-permute-start.5 = (bf16[48,512]{1,0:T(8,128)(2,1)S(1)}, bf16[48,512]{1,0:T(8,128)(2,1)S(1)}, u32[]{:S(2)}, u32[]{:S(2)}) collective-permute-start(bf16[48,512]{1,0:T(8,128)(2,1)S(1)} %collective-permute-done.refs_0_), channel_id=1, source_target_pairs={{0,1},{1,0},{2,3},{3,2},{4,5},{5,4},{6,7},{7,6},{8,9},{9,8},{10,11... | collective-permute-start | bytes 147464 | tf_op jit(solution)/shard_map/ppermute | solution.py:230
  12.5 1.3 %collective-permute-done.2.refs_1_ = bf16[48,512]{1,0:T(8,128)(2,1)S(1)} collective-permute-done((bf16[48,512]{1,0:T(8,128)(2,1)}, bf16[48,512]{1,0:T(8,128)(2,1)S(1)}, u32[]{:S(2)}, u32[]{:S(2)}) %collective-permute-start.2) | collective-permute-done | bytes 49184 | tf_op jit(solution)/shard_map/ppermute | solution.py:221
  13.8 0.0 collective-permute-start.6
  13.8 0.1 collective-permute-done.3.refs_2_
  14.0 0.4 %collective-permute-start.7 = (bf16[48,512]{1,0:T(8,128)(2,1)S(1)}, bf16[48,512]{1,0:T(8,128)(2,1)S(1)}, u32[]{:S(2)}, u32[]{:S(2)}) collective-permute-start(bf16[48,512]{1,0:T(8,128)(2,1)S(1)} %collective-permute-done.3.refs_2_), channel_id=1, source_target_pairs={{0,1},{1,0},{2,3},{3,2},{4,5},{5,4},{6,7},{7,6},{8,9},{9,8},{10,11... | collective-permute-start | bytes 147464 | tf_op jit(solution)/shard_map/ppermute | solution.py:230
  14.4 0.0 copy-start
  14.4 1.1 %copy-done = bf16[816,512]{1,0:T(8,128)(2,1)S(1)} copy-done((bf16[816,512]{1,0:T(8,128)(2,1)S(1)}, bf16[816,512]{1,0:T(8,128)(2,1)}, u32[]{:S(2)}) %copy-start) | copy-done | bytes 835608
  15.5 0.0 copy-start.1
  15.5 0.1 shard_map.114.stage
  15.6 0.0 collective-permute-done.4.refs_3_
  15.6 0.0 collective-permute-done.5.refs_4_
  15.6 0.0 collective-permute-done.6.refs_5_
  15.6 0.0 collective-permute-done.7.refs_6_
  15.6 0.0 collective-permute-done.1.x_other
  15.6 1.3 %shard_map.115 = (bf16[128,32]{1,0:T(8,128)(2,1)S(1)}, bf16[4,32,512]{2,1,0:T(8,128)(2,1)S(1)}, bf16[256,512]{1,0:T(8,128)(2,1)S(1)}, bf16[48,512]{1,0:T(8,128)(...) custom-call(bf16[816,512]{1,0:T(8,128)(2,1)S(1)} %shard_map.114.stag, ...), custom_call_target="tpu_custom_call" | custom-call | tf_op jit(solution)/shard_map/pallas_call | solution.py:305
  16.9 2.8 %collective-permute-start.8 = (bf16[48,512]{1,0:T(8,128)(2,1)S(1)}, bf16[48,512]{1,0:T(8,128)(2,1)S(1)}, u32[]{:S(2)}, u32[]{:S(2)}) collective-permute-start(bf16[48,512]{1,0:T(8,128)(2,1)S(1)} %get-tuple-element.39), channel_id=1, source_target_pairs={{0,14},{1,11},{2,12},{3,9},{4,10},{5,15},{6,8},{7,13},{8,6},{9,3},... | collective-permute-start | bytes 147464 | tf_op jit(solution)/shard_map/ppermute | solution.py:221
  19.7 0.4 %collective-permute-start.9 = (bf16[48,512]{1,0:T(8,128)(2,1)S(1)}, bf16[48,512]{1,0:T(8,128)(2,1)S(1)}, u32[]{:S(2)}, u32[]{:S(2)}) collective-permute-start(bf16[48,512]{1,0:T(8,128)(2,1)S(1)} %get-tuple-element.46), channel_id=1, source_target_pairs={{0,4},{1,9},{2,6},{3,11},{4,0},{5,13},{6,2},{7,15},{8,12},{9,1},{1... | collective-permute-start | bytes 147464 | tf_op jit(solution)/shard_map/ppermute | solution.py:221
  20.1 1.7 %collective-permute-start.10 = (bf16[48,512]{1,0:T(8,128)(2,1)S(1)}, bf16[48,512]{1,0:T(8,128)(2,1)S(1)}, u32[]{:S(2)}, u32[]{:S(2)}) collective-permute-start(bf16[48,512]{1,0:T(8,128)(2,1)S(1)} %get-tuple-element.47), channel_id=1, source_target_pairs={{0,12},{1,7},{2,14},{3,5},{4,8},{5,3},{6,10},{7,1},{8,4},{9,15},{1... | collective-permute-start | bytes 147464 | tf_op jit(solution)/shard_map/ppermute | solution.py:221
  21.8 0.4 %collective-permute-start.11 = (bf16[48,512]{1,0:T(8,128)(2,1)S(1)}, bf16[48,512]{1,0:T(8,128)(2,1)S(1)}, u32[]{:S(2)}, u32[]{:S(2)}) collective-permute-start(bf16[48,512]{1,0:T(8,128)(2,1)S(1)} %get-tuple-element.48), channel_id=1, source_target_pairs={{0,2},{1,3},{2,0},{3,1},{4,6},{5,7},{6,4},{7,5},{8,10},{9,11},{10,... | collective-permute-start | bytes 147464 | tf_op jit(solution)/shard_map/ppermute | solution.py:221
  22.2 0.0 copy-done.1
  22.2 0.8 %shard_map.116.base_ref = f32[128,2048]{1,0:T(8,128)S(1)} custom-call(bf16[256,512]{1,0:T(8,128)(2,1)S(1)} %get-tuple-element.40.kept_ref, bf16[2048,512]{1,0:T(8,128)(2,1)S(1)} %copy-done.1), custom_call_target="tpu_custom_call" | custom-call | flops 268435456 | bytes 3145728 | tf_op jit(solution)/shard_map/pallas_call | solution.py:322
  23.1 1.0 %shard_map.117 = bf16[128,2048]{1,0:T(8,128)(2,1)} custom-call(f32[128,2048]{1,0:T(8,128)S(1)} %shard_map.116.base_ref, bf16[128,32]{1,0:T(8,128)(2,1)S(1)} %get-tuple-element.41.dlow_ref, bf16[4,32,512]{2,1,0:T(8,128)(2,1)S(1)} %get-tuple-element.42.a_ref), custom_call_target="tpu_custom_call" | custom-call | flops 16777216 | bytes 1572864 | tf_op jit(solution)/shard_map/pallas_call | solution.py:334
  24.1 0.0 collective-permute-done.8.refs_1_
  24.1 0.1 collective-permute-start.12
  24.1 0.8 %collective-permute-done.9.refs_2_ = bf16[48,512]{1,0:T(8,128)(2,1)S(1)} collective-permute-done((bf16[48,512]{1,0:T(8,128)(2,1)S(1)}, bf16[48,512]{1,0:T(8,128)(2,1)S(1)}, u32[]{:S(2)}, u32[]{:S(2)}) %collective-permute-start.9) | collective-permute-done | bytes 49184 | tf_op jit(solution)/shard_map/ppermute | solution.py:221
  25.0 0.0 collective-permute-start.13
  25.0 1.0 %collective-permute-done.10.refs_3_ = bf16[48,512]{1,0:T(8,128)(2,1)S(1)} collective-permute-done((bf16[48,512]{1,0:T(8,128)(2,1)S(1)}, bf16[48,512]{1,0:T(8,128)(2,1)S(1)}, u32[]{:S(2)}, u32[]{:S(2)}) %collective-permute-start.10) | collective-permute-done | bytes 49184 | tf_op jit(solution)/shard_map/ppermute | solution.py:221
  26.0 0.0 collective-permute-start.14
  26.0 0.0 collective-permute-done.11.refs_4_
  26.0 0.0 collective-permute-done.12.refs_5_
  26.0 0.2 collective-permute-done.13.refs_6_
  26.2 1.0 %collective-permute-done.14.refs_7_ = bf16[48,512]{1,0:T(8,128)(2,1)S(1)} collective-permute-done((bf16[48,512]{1,0:T(8,128)(2,1)S(1)}, bf16[48,512]{1,0:T(8,128)(2,1)S(1)}, u32[]{:S(2)}, u32[]{:S(2)}) %collective-permute-start.14) | collective-permute-done | bytes 49184 | tf_op jit(solution)/shard_map/ppermute | solution.py:230
  27.2 1.0 %shard_map.118 = (f32[512,128]{1,0:T(8,128)}, f32[16,256]{1,0:T(8,128)}) custom-call(bf16[256,512]{1,0:T(8,128)(2,1)S(1)} %get-tuple-element.40.kept_ref, bf16[48,512]{1,0:T(8,128)(2,1)S(1)} %get-tuple-element.44.refs_0_, bf16[48,512]{1,0:T(8,128)(2,1)S(1)} %collective-permute-done.8.refs_1_, bf16[48,512]{1,0:T(8,128)(2,1)S(1)} %collective-permute-done.9.refs_2_, ...), custom_call_target="tpu_custom_call" | custom-call | tf_op jit(solution)/shard_map/pallas_call | solution.py:350
Async XLA Ops:
  2.5 13.1 %collective-permute-start.1 = (bf16[64,4096]{1,0:T(8,128)(2,1)}, bf16[64,4096]{1,0:T(8,128)(2,1)S(1)}, u32[]{:S(2)}, u32[]{:S(2)}) collective-permute-start(bf16[64,4096]{1,0:T(8,128)(2,1)} %x_hbm.1), channel_id=1, source_target_pairs={{0,1},{1,0},{2,3},{3,2},{4,5},{5,4},{6,7},{7,6},{8,9},{9,8},{10,11... | collective-permute-start | bytes 1572872 | tf_op jit(solution)/shard_map/ppermute | solution.py:285
  3.0 8.9 %collective-permute-start = (bf16[48,512]{1,0:T(8,128)(2,1)}, bf16[48,512]{1,0:T(8,128)(2,1)S(1)}, u32[]{:S(2)}, u32[]{:S(2)}) collective-permute-start(bf16[48,512]{1,0:T(8,128)(2,1)} %get-tuple-element.31), channel_id=1, source_target_pairs={{0,8},{1,11},{2,10},{3,9},{4,12},{5,15},{6,14},{7,13},{8,0},{9,3},... | collective-permute-start | bytes 147464 | tf_op jit(solution)/shard_map/ppermute | solution.py:221
  6.7 7.1 %collective-permute-start.2 = (bf16[48,512]{1,0:T(8,128)(2,1)}, bf16[48,512]{1,0:T(8,128)(2,1)S(1)}, u32[]{:S(2)}, u32[]{:S(2)}) collective-permute-start(bf16[48,512]{1,0:T(8,128)(2,1)} %get-tuple-element.36), channel_id=1, source_target_pairs={{0,14},{1,13},{2,12},{3,15},{4,10},{5,9},{6,8},{7,11},{8,6},{9,5},... | collective-permute-start | bytes 147464 | tf_op jit(solution)/shard_map/ppermute | solution.py:221
  9.0 5.0 %collective-permute-start.3 = (bf16[48,512]{1,0:T(8,128)(2,1)}, bf16[48,512]{1,0:T(8,128)(2,1)S(1)}, u32[]{:S(2)}, u32[]{:S(2)}) collective-permute-start(bf16[48,512]{1,0:T(8,128)(2,1)} %get-tuple-element.37), channel_id=1, source_target_pairs={{0,4},{1,7},{2,6},{3,5},{4,0},{5,3},{6,2},{7,1},{8,12},{9,15},{10,... | collective-permute-start | bytes 147464 | tf_op jit(solution)/shard_map/ppermute | solution.py:221
  9.0 6.6 %collective-permute-start.4 = (bf16[48,512]{1,0:T(8,128)(2,1)}, bf16[48,512]{1,0:T(8,128)(2,1)S(1)}, u32[]{:S(2)}, u32[]{:S(2)}) collective-permute-start(bf16[48,512]{1,0:T(8,128)(2,1)} %get-tuple-element.38), channel_id=1, source_target_pairs={{0,2},{1,3},{2,0},{3,1},{4,6},{5,7},{6,4},{7,5},{8,10},{9,11},{10,... | collective-permute-start | bytes 147464 | tf_op jit(solution)/shard_map/ppermute | solution.py:221
  12.0 3.6 %collective-permute-start.5 = (bf16[48,512]{1,0:T(8,128)(2,1)S(1)}, bf16[48,512]{1,0:T(8,128)(2,1)S(1)}, u32[]{:S(2)}, u32[]{:S(2)}) collective-permute-start(bf16[48,512]{1,0:T(8,128)(2,1)S(1)} %collective-permute-done.refs_0_), channel_id=1, source_target_pairs={{0,1},{1,0},{2,3},{3,2},{4,5},{5,4},{6,7},{7,6},{8,9},{9,8},{10,11... | collective-permute-start | bytes 147464 | tf_op jit(solution)/shard_map/ppermute | solution.py:230
  13.8 1.7 %collective-permute-start.6 = (bf16[48,512]{1,0:T(8,128)(2,1)S(1)}, bf16[48,512]{1,0:T(8,128)(2,1)S(1)}, u32[]{:S(2)}, u32[]{:S(2)}) collective-permute-start(bf16[48,512]{1,0:T(8,128)(2,1)S(1)} %collective-permute-done.2.refs_1_), channel_id=1, source_target_pairs={{0,1},{1,0},{2,3},{3,2},{4,5},{5,4},{6,7},{7,6},{8,9},{9,8},{10,11... | collective-permute-start | bytes 147464 | tf_op jit(solution)/shard_map/ppermute | solution.py:230
  14.0 1.6 %collective-permute-start.7 = (bf16[48,512]{1,0:T(8,128)(2,1)S(1)}, bf16[48,512]{1,0:T(8,128)(2,1)S(1)}, u32[]{:S(2)}, u32[]{:S(2)}) collective-permute-start(bf16[48,512]{1,0:T(8,128)(2,1)S(1)} %collective-permute-done.3.refs_2_), channel_id=1, source_target_pairs={{0,1},{1,0},{2,3},{3,2},{4,5},{5,4},{6,7},{7,6},{8,9},{9,8},{10,11... | collective-permute-start | bytes 147464 | tf_op jit(solution)/shard_map/ppermute | solution.py:230
  14.4 1.1 %copy-start = (bf16[816,512]{1,0:T(8,128)(2,1)S(1)}, bf16[816,512]{1,0:T(8,128)(2,1)}, u32[]{:S(2)}) copy-start(bf16[816,512]{1,0:T(8,128)(2,1)} %shard_map.113.stage) | copy-start | bytes 2506756
  15.5 6.7 %copy-start.1 = (bf16[2048,512]{1,0:T(8,128)(2,1)S(1)}, bf16[2048,512]{1,0:T(8,128)(2,1)}, u32[]{:S(2)}) copy-start(bf16[2048,512]{1,0:T(8,128)(2,1)} %w_ref.1) | copy-start | bytes 6291460
  16.9 7.2 %collective-permute-start.8 = (bf16[48,512]{1,0:T(8,128)(2,1)S(1)}, bf16[48,512]{1,0:T(8,128)(2,1)S(1)}, u32[]{:S(2)}, u32[]{:S(2)}) collective-permute-start(bf16[48,512]{1,0:T(8,128)(2,1)S(1)} %get-tuple-element.39), channel_id=1, source_target_pairs={{0,14},{1,11},{2,12},{3,9},{4,10},{5,15},{6,8},{7,13},{8,6},{9,3},... | collective-permute-start | bytes 147464 | tf_op jit(solution)/shard_map/ppermute | solution.py:221
  19.7 5.3 %collective-permute-start.9 = (bf16[48,512]{1,0:T(8,128)(2,1)S(1)}, bf16[48,512]{1,0:T(8,128)(2,1)S(1)}, u32[]{:S(2)}, u32[]{:S(2)}) collective-permute-start(bf16[48,512]{1,0:T(8,128)(2,1)S(1)} %get-tuple-element.46), channel_id=1, source_target_pairs={{0,4},{1,9},{2,6},{3,11},{4,0},{5,13},{6,2},{7,15},{8,12},{9,1},{1... | collective-permute-start | bytes 147464 | tf_op jit(solution)/shard_map/ppermute | solution.py:221
  20.1 5.9 %collective-permute-start.10 = (bf16[48,512]{1,0:T(8,128)(2,1)S(1)}, bf16[48,512]{1,0:T(8,128)(2,1)S(1)}, u32[]{:S(2)}, u32[]{:S(2)}) collective-permute-start(bf16[48,512]{1,0:T(8,128)(2,1)S(1)} %get-tuple-element.47), channel_id=1, source_target_pairs={{0,12},{1,7},{2,14},{3,5},{4,8},{5,3},{6,10},{7,1},{8,4},{9,15},{1... | collective-permute-start | bytes 147464 | tf_op jit(solution)/shard_map/ppermute | solution.py:221
  21.8 4.2 %collective-permute-start.11 = (bf16[48,512]{1,0:T(8,128)(2,1)S(1)}, bf16[48,512]{1,0:T(8,128)(2,1)S(1)}, u32[]{:S(2)}, u32[]{:S(2)}) collective-permute-start(bf16[48,512]{1,0:T(8,128)(2,1)S(1)} %get-tuple-element.48), channel_id=1, source_target_pairs={{0,2},{1,3},{2,0},{3,1},{4,6},{5,7},{6,4},{7,5},{8,10},{9,11},{10,... | collective-permute-start | bytes 147464 | tf_op jit(solution)/shard_map/ppermute | solution.py:221
  24.1 1.9 %collective-permute-start.12 = (bf16[48,512]{1,0:T(8,128)(2,1)S(1)}, bf16[48,512]{1,0:T(8,128)(2,1)S(1)}, u32[]{:S(2)}, u32[]{:S(2)}) collective-permute-start(bf16[48,512]{1,0:T(8,128)(2,1)S(1)} %collective-permute-done.8.refs_1_), channel_id=1, source_target_pairs={{0,1},{1,0},{2,3},{3,2},{4,5},{5,4},{6,7},{7,6},{8,9},{9,8},{10,11... | collective-permute-start | bytes 147464 | tf_op jit(solution)/shard_map/ppermute | solution.py:230
  25.0 1.2 %collective-permute-start.13 = (bf16[48,512]{1,0:T(8,128)(2,1)S(1)}, bf16[48,512]{1,0:T(8,128)(2,1)S(1)}, u32[]{:S(2)}, u32[]{:S(2)}) collective-permute-start(bf16[48,512]{1,0:T(8,128)(2,1)S(1)} %collective-permute-done.9.refs_2_), channel_id=1, source_target_pairs={{0,1},{1,0},{2,3},{3,2},{4,5},{5,4},{6,7},{7,6},{8,9},{9,8},{10,11... | collective-permute-start | bytes 147464 | tf_op jit(solution)/shard_map/ppermute | solution.py:230
  26.0 1.2 %collective-permute-start.14 = (bf16[48,512]{1,0:T(8,128)(2,1)S(1)}, bf16[48,512]{1,0:T(8,128)(2,1)S(1)}, u32[]{:S(2)}, u32[]{:S(2)}) collective-permute-start(bf16[48,512]{1,0:T(8,128)(2,1)S(1)} %collective-permute-done.10.refs_3_), channel_id=1, source_target_pairs={{0,1},{1,0},{2,3},{3,2},{4,5},{5,4},{6,7},{7,6},{8,9},{9,8},{10,11... | collective-permute-start | bytes 147464 | tf_op jit(solution)/shard_map/ppermute | solution.py:230

commit v11 on v10

--- a/solution.py
+++ b/solution.py
@@ -54,7 +54,7 @@
     half = n // 2
     if turn == 0:
         return [(half, half + 1), (n - 1, n - 2), (2, 3), (1, 1)]
-    return [(n - 1, half + 1), (2, half), (n - 2, 3), (1, 1)]
+    return [(n - 1, half + 1), (3, n - 2), (2, half), (1, 1)]
 
 
 def partners(n, turn, me, core):

time: 28.5 us -> 28.5 us (level)
  starting transfers between devices: 13.6 us -> 14.8 us
  waiting for transfers between devices: 4.57 us -> 3.38 us
    ppermute x8, waiting for transfers between devices: 3.34 us -> 2.39 us  [exchange(): lax.ppermute(message, ('dp', 'tensor'), [(2 * i + c, 2 * (i ^ step[c]) +...]
    ppermute x8, starting transfers between devices: 12.1 us -> 13 us  [exchange(): lax.ppermute(message, ('dp', 'tensor'), [(2 * i + c, 2 * (i ^ step[c]) +...]
  transfers between devices with their start and end apart: 15 -> 15, of which waited for: 6 -> 7; matrix products, arithmetic and copies ran while one was open for 0% -> 0% of each run, Pallas kernels for 14% -> 14%
where the time goes in v11:
time: 28.5 us; the launch traced here: 28.3 us
  starting transfers between devices  14.8 us (52%)
  Pallas kernels  8.17 us (29%)
  waiting for transfers between devices  3.38 us (12%)
  local copies, waits for them, and re-layouts  1.15 us (4%)
  between operations  0.75 us (3%)
    ppermute x8, starting transfers between devices, exchange(): lax.ppermute(message, ('dp', 'tensor'), [(2 * i + c, 2 * (i ^ step[c]) +...  13 us
    ppermute x8, waiting for transfers between devices, exchange(): lax.ppermute(message, ('dp', 'tensor'), [(2 * i + c, 2 * (i ^ step[c]) +...  2.39 us
    pallas_call x1, Pallas kernels, local_kernels(): pl.pallas_call(functools.partial(stage_kernel, n, lay), out_shape=shape(l...  2.17 us
    pallas_call x1, Pallas kernels, local_kernels(): pl.pallas_call(functools.partial(pack_kernel, n), out_shape=[message] * c...  1.88 us
    pallas_call x1, Pallas kernels, local_kernels(): pl.pallas_call(functools.partial(middle_kernel, n, lay), out_shape=[shape...  1.26 us
    ppermute x6, starting transfers between devices, exchange(): lax.ppermute(message, 'tensor', [(0, 1), (1, 0)])  1.26 us
    unnamed x4, local copies, waits for them, and re-layouts  1.15 us
    pallas_call x1, Pallas kernels, local_kernels(): pl.pallas_call(functools.partial(final_kernel, n, lay), out_shape=[shape(...  1.01 us
  transfers between devices with their start and end apart: 15, of which 7 were waited for; matrix products, arithmetic and copies ran while one was open for 0% of the time, Pallas kernels for 14%

profile of v11, /device:TPU:0, one launch (start us, length us, event | category | flops | bytes accessed | tf_op | source)
XLA Modules:
  0.0 28.3 jit_solution(12850754268639930873)
XLA Ops:
  0.6 1.9 %shard_map.112 = (bf16[48,512]{1,0:T(8,128)(2,1)}, bf16[48,512]{1,0:T(8,128)(2,1)}, bf16[48,512]{1,0:T(8,128)(2,1)}, bf16[48,512]{1,0:T(8,128)(2,1)}, bf16[48,512]{1,0:T(8,128)(2,1)}) custom-call(s32[2,8]{1,0:T(2,128)} %bitcast.2, s32[8]{0:T(128)} %slot_hbm.3, bf16[512,128]{1,0:T(8,128)(2,1)} %down_hbm.1, bf16[16,512]{1,0:T(8,128)(2,1)} %up_hbm.1), custom_call_target="tpu_custom_call" | custom-call | tf_op jit(solution)/shard_map/pallas_call | solution.py:270
  2.5 0.5 %collective-permute-start.1 = (bf16[64,4096]{1,0:T(8,128)(2,1)}, bf16[64,4096]{1,0:T(8,128)(2,1)S(1)}, u32[]{:S(2)}, u32[]{:S(2)}) collective-permute-start(bf16[64,4096]{1,0:T(8,128)(2,1)} %x_hbm.1), channel_id=1, source_target_pairs={{0,1},{1,0},{2,3},{3,2},{4,5},{5,4},{6,7},{7,6},{8,9},{9,8},{10,11... | collective-permute-start | bytes 1572872 | tf_op jit(solution)/shard_map/ppermute | solution.py:285
  3.0 3.7 %collective-permute-start = (bf16[48,512]{1,0:T(8,128)(2,1)}, bf16[48,512]{1,0:T(8,128)(2,1)S(1)}, u32[]{:S(2)}, u32[]{:S(2)}) collective-permute-start(bf16[48,512]{1,0:T(8,128)(2,1)} %get-tuple-element.31), channel_id=1, source_target_pairs={{0,8},{1,11},{2,10},{3,9},{4,12},{5,15},{6,14},{7,13},{8,0},{9,3},... | collective-permute-start | bytes 147464 | tf_op jit(solution)/shard_map/ppermute | solution.py:221
  6.7 2.3 %collective-permute-start.2 = (bf16[48,512]{1,0:T(8,128)(2,1)}, bf16[48,512]{1,0:T(8,128)(2,1)S(1)}, u32[]{:S(2)}, u32[]{:S(2)}) collective-permute-start(bf16[48,512]{1,0:T(8,128)(2,1)} %get-tuple-element.36), channel_id=1, source_target_pairs={{0,14},{1,13},{2,12},{3,15},{4,10},{5,9},{6,8},{7,11},{8,6},{9,5},... | collective-permute-start | bytes 147464 | tf_op jit(solution)/shard_map/ppermute | solution.py:221
  9.0 0.0 collective-permute-start.3
  9.0 0.8 %collective-permute-start.4 = (bf16[48,512]{1,0:T(8,128)(2,1)}, bf16[48,512]{1,0:T(8,128)(2,1)S(1)}, u32[]{:S(2)}, u32[]{:S(2)}) collective-permute-start(bf16[48,512]{1,0:T(8,128)(2,1)} %get-tuple-element.38), channel_id=1, source_target_pairs={{0,2},{1,3},{2,0},{3,1},{4,6},{5,7},{6,4},{7,5},{8,10},{9,11},{10,... | collective-permute-start | bytes 147464 | tf_op jit(solution)/shard_map/ppermute | solution.py:221
  9.8 2.2 %shard_map.113.stage = bf16[816,512]{1,0:T(8,128)(2,1)} custom-call(s32[2,8]{1,0:T(2,128)} %bitcast.4, s32[2,8]{1,0:T(2,128)} %bitcast.3, s32[8]{0:T(128)} %slot_hbm.3, s32[8]{0:T(128)} %count_hbm.1, bf16[128,512]{1,0:T(8,128)(2,1)} %g_hbm.1, bf16[64,4096]{1,0:T(8,128)(2,1)} %x_hbm.1, bf16[48,512]{1,0:T(8,128)(2,1)} %get-tuple-element.32.own_hbm), custom_call_target="tpu_custom_call" | custom-call | bytes 2097152 | tf_op jit(solution)/shard_map/pallas_call | solution.py:286
  11.9 0.0 collective-permute-done.refs_0_
  12.0 0.6 %collective-permute-start.5 = (bf16[48,512]{1,0:T(8,128)(2,1)S(1)}, bf16[48,512]{1,0:T(8,128)(2,1)S(1)}, u32[]{:S(2)}, u32[]{:S(2)}) collective-permute-start(bf16[48,512]{1,0:T(8,128)(2,1)S(1)} %collective-permute-done.refs_0_), channel_id=1, source_target_pairs={{0,1},{1,0},{2,3},{3,2},{4,5},{5,4},{6,7},{7,6},{8,9},{9,8},{10,11... | collective-permute-start | bytes 147464 | tf_op jit(solution)/shard_map/ppermute | solution.py:230
  12.5 1.3 %collective-permute-done.2.refs_1_ = bf16[48,512]{1,0:T(8,128)(2,1)S(1)} collective-permute-done((bf16[48,512]{1,0:T(8,128)(2,1)}, bf16[48,512]{1,0:T(8,128)(2,1)S(1)}, u32[]{:S(2)}, u32[]{:S(2)}) %collective-permute-start.2) | collective-permute-done | bytes 49184 | tf_op jit(solution)/shard_map/ppermute | solution.py:221
  13.8 0.0 collective-permute-start.6
  13.8 0.1 collective-permute-done.3.refs_2_
  14.0 0.4 %collective-permute-start.7 = (bf16[48,512]{1,0:T(8,128)(2,1)S(1)}, bf16[48,512]{1,0:T(8,128)(2,1)S(1)}, u32[]{:S(2)}, u32[]{:S(2)}) collective-permute-start(bf16[48,512]{1,0:T(8,128)(2,1)S(1)} %collective-permute-done.3.refs_2_), channel_id=1, source_target_pairs={{0,1},{1,0},{2,3},{3,2},{4,5},{5,4},{6,7},{7,6},{8,9},{9,8},{10,11... | collective-permute-start | bytes 147464 | tf_op jit(solution)/shard_map/ppermute | solution.py:230
  14.4 0.0 copy-start
  14.4 1.1 %copy-done = bf16[816,512]{1,0:T(8,128)(2,1)S(1)} copy-done((bf16[816,512]{1,0:T(8,128)(2,1)S(1)}, bf16[816,512]{1,0:T(8,128)(2,1)}, u32[]{:S(2)}) %copy-start) | copy-done | bytes 835608
  15.5 0.0 copy-start.1
  15.5 0.1 shard_map.114.stage
  15.6 0.0 collective-permute-done.4.refs_3_
  15.6 0.0 collective-permute-done.5.refs_4_
  15.6 0.0 collective-permute-done.6.refs_5_
  15.6 0.0 collective-permute-done.7.refs_6_
  15.6 0.0 collective-permute-done.1.x_other
  15.6 1.3 %shard_map.115 = (bf16[128,32]{1,0:T(8,128)(2,1)S(1)}, bf16[4,32,512]{2,1,0:T(8,128)(2,1)S(1)}, bf16[256,512]{1,0:T(8,128)(2,1)S(1)}, bf16[48,512]{1,0:T(8,128)(...) custom-call(bf16[816,512]{1,0:T(8,128)(2,1)S(1)} %shard_map.114.stag, ...), custom_call_target="tpu_custom_call" | custom-call | tf_op jit(solution)/shard_map/pallas_call | solution.py:305
  16.9 2.8 %collective-permute-start.8 = (bf16[48,512]{1,0:T(8,128)(2,1)S(1)}, bf16[48,512]{1,0:T(8,128)(2,1)S(1)}, u32[]{:S(2)}, u32[]{:S(2)}) collective-permute-start(bf16[48,512]{1,0:T(8,128)(2,1)S(1)} %get-tuple-element.39), channel_id=1, source_target_pairs={{0,14},{1,11},{2,12},{3,9},{4,10},{5,15},{6,8},{7,13},{8,6},{9,3},... | collective-permute-start | bytes 147464 | tf_op jit(solution)/shard_map/ppermute | solution.py:221
  19.7 0.8 %collective-permute-start.9 = (bf16[48,512]{1,0:T(8,128)(2,1)S(1)}, bf16[48,512]{1,0:T(8,128)(2,1)S(1)}, u32[]{:S(2)}, u32[]{:S(2)}) collective-permute-start(bf16[48,512]{1,0:T(8,128)(2,1)S(1)} %get-tuple-element.46), channel_id=1, source_target_pairs={{0,6},{1,13},{2,4},{3,15},{4,2},{5,9},{6,0},{7,11},{8,14},{9,5},{1... | collective-permute-start | bytes 147464 | tf_op jit(solution)/shard_map/ppermute | solution.py:221
  20.5 1.7 %collective-permute-start.10 = (bf16[48,512]{1,0:T(8,128)(2,1)S(1)}, bf16[48,512]{1,0:T(8,128)(2,1)S(1)}, u32[]{:S(2)}, u32[]{:S(2)}) collective-permute-start(bf16[48,512]{1,0:T(8,128)(2,1)S(1)} %get-tuple-element.47), channel_id=1, source_target_pairs={{0,4},{1,9},{2,6},{3,11},{4,0},{5,13},{6,2},{7,15},{8,12},{9,1},{1... | collective-permute-start | bytes 147464 | tf_op jit(solution)/shard_map/ppermute | solution.py:221
  22.2 1.0 %collective-permute-start.11 = (bf16[48,512]{1,0:T(8,128)(2,1)S(1)}, bf16[48,512]{1,0:T(8,128)(2,1)S(1)}, u32[]{:S(2)}, u32[]{:S(2)}) collective-permute-start(bf16[48,512]{1,0:T(8,128)(2,1)S(1)} %get-tuple-element.48), channel_id=1, source_target_pairs={{0,2},{1,3},{2,0},{3,1},{4,6},{5,7},{6,4},{7,5},{8,10},{9,11},{10,... | collective-permute-start | bytes 147464 | tf_op jit(solution)/shard_map/ppermute | solution.py:221
  23.2 0.0 copy-done.1
  23.2 0.8 %shard_map.116.base_ref = f32[128,2048]{1,0:T(8,128)S(1)} custom-call(bf16[256,512]{1,0:T(8,128)(2,1)S(1)} %get-tuple-element.40.kept_ref, bf16[2048,512]{1,0:T(8,128)(2,1)S(1)} %copy-done.1), custom_call_target="tpu_custom_call" | custom-call | flops 268435456 | bytes 3145728 | tf_op jit(solution)/shard_map/pallas_call | solution.py:322
  24.0 1.0 %shard_map.117 = bf16[128,2048]{1,0:T(8,128)(2,1)} custom-call(f32[128,2048]{1,0:T(8,128)S(1)} %shard_map.116.base_ref, bf16[128,32]{1,0:T(8,128)(2,1)S(1)} %get-tuple-element.41.dlow_ref, bf16[4,32,512]{2,1,0:T(8,128)(2,1)S(1)} %get-tuple-element.42.a_ref), custom_call_target="tpu_custom_call" | custom-call | flops 16777216 | bytes 1572864 | tf_op jit(solution)/shard_map/pallas_call | solution.py:334
  25.0 0.0 collective-permute-done.8.refs_1_
  25.0 0.1 collective-permute-start.12
  25.1 0.2 collective-permute-done.9.refs_2_
  25.3 0.3 collective-permute-start.13
  25.6 0.4 %collective-permute-done.10.refs_3_ = bf16[48,512]{1,0:T(8,128)(2,1)S(1)} collective-permute-done((bf16[48,512]{1,0:T(8,128)(2,1)S(1)}, bf16[48,512]{1,0:T(8,128)(2,1)S(1)}, u32[]{:S(2)}, u32[]{:S(2)}) %collective-permute-start.10) | collective-permute-done | bytes 49184 | tf_op jit(solution)/shard_map/ppermute | solution.py:221
  26.0 0.0 collective-permute-start.14
  26.0 0.2 collective-permute-done.11.refs_4_
  26.3 0.0 collective-permute-done.12.refs_5_
  26.3 0.3 collective-permute-done.13.refs_6_
  26.6 0.7 %collective-permute-done.14.refs_7_ = bf16[48,512]{1,0:T(8,128)(2,1)S(1)} collective-permute-done((bf16[48,512]{1,0:T(8,128)(2,1)S(1)}, bf16[48,512]{1,0:T(8,128)(2,1)S(1)}, u32[]{:S(2)}, u32[]{:S(2)}) %collective-permute-start.14) | collective-permute-done | bytes 49184 | tf_op jit(solution)/shard_map/ppermute | solution.py:230
  27.2 1.0 %shard_map.118 = (f32[512,128]{1,0:T(8,128)}, f32[16,256]{1,0:T(8,128)}) custom-call(bf16[256,512]{1,0:T(8,128)(2,1)S(1)} %get-tuple-element.40.kept_ref, bf16[48,512]{1,0:T(8,128)(2,1)S(1)} %get-tuple-element.44.refs_0_, bf16[48,512]{1,0:T(8,128)(2,1)S(1)} %collective-permute-done.8.refs_1_, bf16[48,512]{1,0:T(8,128)(2,1)S(1)} %collective-permute-done.9.refs_2_, ...), custom_call_target="tpu_custom_call" | custom-call | tf_op jit(solution)/shard_map/pallas_call | solution.py:350
Async XLA Ops:
  2.5 13.1 %collective-permute-start.1 = (bf16[64,4096]{1,0:T(8,128)(2,1)}, bf16[64,4096]{1,0:T(8,128)(2,1)S(1)}, u32[]{:S(2)}, u32[]{:S(2)}) collective-permute-start(bf16[64,4096]{1,0:T(8,128)(2,1)} %x_hbm.1), channel_id=1, source_target_pairs={{0,1},{1,0},{2,3},{3,2},{4,5},{5,4},{6,7},{7,6},{8,9},{9,8},{10,11... | collective-permute-start | bytes 1572872 | tf_op jit(solution)/shard_map/ppermute | solution.py:285
  3.0 8.9 %collective-permute-start = (bf16[48,512]{1,0:T(8,128)(2,1)}, bf16[48,512]{1,0:T(8,128)(2,1)S(1)}, u32[]{:S(2)}, u32[]{:S(2)}) collective-permute-start(bf16[48,512]{1,0:T(8,128)(2,1)} %get-tuple-element.31), channel_id=1, source_target_pairs={{0,8},{1,11},{2,10},{3,9},{4,12},{5,15},{6,14},{7,13},{8,0},{9,3},... | collective-permute-start | bytes 147464 | tf_op jit(solution)/shard_map/ppermute | solution.py:221
  6.7 7.1 %collective-permute-start.2 = (bf16[48,512]{1,0:T(8,128)(2,1)}, bf16[48,512]{1,0:T(8,128)(2,1)S(1)}, u32[]{:S(2)}, u32[]{:S(2)}) collective-permute-start(bf16[48,512]{1,0:T(8,128)(2,1)} %get-tuple-element.36), channel_id=1, source_target_pairs={{0,14},{1,13},{2,12},{3,15},{4,10},{5,9},{6,8},{7,11},{8,6},{9,5},... | collective-permute-start | bytes 147464 | tf_op jit(solution)/shard_map/ppermute | solution.py:221
  9.0 5.0 %collective-permute-start.3 = (bf16[48,512]{1,0:T(8,128)(2,1)}, bf16[48,512]{1,0:T(8,128)(2,1)S(1)}, u32[]{:S(2)}, u32[]{:S(2)}) collective-permute-start(bf16[48,512]{1,0:T(8,128)(2,1)} %get-tuple-element.37), channel_id=1, source_target_pairs={{0,4},{1,7},{2,6},{3,5},{4,0},{5,3},{6,2},{7,1},{8,12},{9,15},{10,... | collective-permute-start | bytes 147464 | tf_op jit(solution)/shard_map/ppermute | solution.py:221
  9.0 6.6 %collective-permute-start.4 = (bf16[48,512]{1,0:T(8,128)(2,1)}, bf16[48,512]{1,0:T(8,128)(2,1)S(1)}, u32[]{:S(2)}, u32[]{:S(2)}) collective-permute-start(bf16[48,512]{1,0:T(8,128)(2,1)} %get-tuple-element.38), channel_id=1, source_target_pairs={{0,2},{1,3},{2,0},{3,1},{4,6},{5,7},{6,4},{7,5},{8,10},{9,11},{10,... | collective-permute-start | bytes 147464 | tf_op jit(solution)/shard_map/ppermute | solution.py:221
  12.0 3.6 %collective-permute-start.5 = (bf16[48,512]{1,0:T(8,128)(2,1)S(1)}, bf16[48,512]{1,0:T(8,128)(2,1)S(1)}, u32[]{:S(2)}, u32[]{:S(2)}) collective-permute-start(bf16[48,512]{1,0:T(8,128)(2,1)S(1)} %collective-permute-done.refs_0_), channel_id=1, source_target_pairs={{0,1},{1,0},{2,3},{3,2},{4,5},{5,4},{6,7},{7,6},{8,9},{9,8},{10,11... | collective-permute-start | bytes 147464 | tf_op jit(solution)/shard_map/ppermute | solution.py:230
  13.8 1.7 %collective-permute-start.6 = (bf16[48,512]{1,0:T(8,128)(2,1)S(1)}, bf16[48,512]{1,0:T(8,128)(2,1)S(1)}, u32[]{:S(2)}, u32[]{:S(2)}) collective-permute-start(bf16[48,512]{1,0:T(8,128)(2,1)S(1)} %collective-permute-done.2.refs_1_), channel_id=1, source_target_pairs={{0,1},{1,0},{2,3},{3,2},{4,5},{5,4},{6,7},{7,6},{8,9},{9,8},{10,11... | collective-permute-start | bytes 147464 | tf_op jit(solution)/shard_map/ppermute | solution.py:230
  14.0 1.6 %collective-permute-start.7 = (bf16[48,512]{1,0:T(8,128)(2,1)S(1)}, bf16[48,512]{1,0:T(8,128)(2,1)S(1)}, u32[]{:S(2)}, u32[]{:S(2)}) collective-permute-start(bf16[48,512]{1,0:T(8,128)(2,1)S(1)} %collective-permute-done.3.refs_2_), channel_id=1, source_target_pairs={{0,1},{1,0},{2,3},{3,2},{4,5},{5,4},{6,7},{7,6},{8,9},{9,8},{10,11... | collective-permute-start | bytes 147464 | tf_op jit(solution)/shard_map/ppermute | solution.py:230
  14.4 1.1 %copy-start = (bf16[816,512]{1,0:T(8,128)(2,1)S(1)}, bf16[816,512]{1,0:T(8,128)(2,1)}, u32[]{:S(2)}) copy-start(bf16[816,512]{1,0:T(8,128)(2,1)} %shard_map.113.stage) | copy-start | bytes 2506756
  15.5 7.7 %copy-start.1 = (bf16[2048,512]{1,0:T(8,128)(2,1)S(1)}, bf16[2048,512]{1,0:T(8,128)(2,1)}, u32[]{:S(2)}) copy-start(bf16[2048,512]{1,0:T(8,128)(2,1)} %w_ref.1) | copy-start | bytes 6291460
  16.9 8.1 %collective-permute-start.8 = (bf16[48,512]{1,0:T(8,128)(2,1)S(1)}, bf16[48,512]{1,0:T(8,128)(2,1)S(1)}, u32[]{:S(2)}, u32[]{:S(2)}) collective-permute-start(bf16[48,512]{1,0:T(8,128)(2,1)S(1)} %get-tuple-element.39), channel_id=1, source_target_pairs={{0,14},{1,11},{2,12},{3,9},{4,10},{5,15},{6,8},{7,13},{8,6},{9,3},... | collective-permute-start | bytes 147464 | tf_op jit(solution)/shard_map/ppermute | solution.py:221
  19.7 5.6 %collective-permute-start.9 = (bf16[48,512]{1,0:T(8,128)(2,1)S(1)}, bf16[48,512]{1,0:T(8,128)(2,1)S(1)}, u32[]{:S(2)}, u32[]{:S(2)}) collective-permute-start(bf16[48,512]{1,0:T(8,128)(2,1)S(1)} %get-tuple-element.46), channel_id=1, source_target_pairs={{0,6},{1,13},{2,4},{3,15},{4,2},{5,9},{6,0},{7,11},{8,14},{9,5},{1... | collective-permute-start | bytes 147464 | tf_op jit(solution)/shard_map/ppermute | solution.py:221
  20.5 5.5 %collective-permute-start.10 = (bf16[48,512]{1,0:T(8,128)(2,1)S(1)}, bf16[48,512]{1,0:T(8,128)(2,1)S(1)}, u32[]{:S(2)}, u32[]{:S(2)}) collective-permute-start(bf16[48,512]{1,0:T(8,128)(2,1)S(1)} %get-tuple-element.47), channel_id=1, source_target_pairs={{0,4},{1,9},{2,6},{3,11},{4,0},{5,13},{6,2},{7,15},{8,12},{9,1},{1... | collective-permute-start | bytes 147464 | tf_op jit(solution)/shard_map/ppermute | solution.py:221
  22.2 4.1 %collective-permute-start.11 = (bf16[48,512]{1,0:T(8,128)(2,1)S(1)}, bf16[48,512]{1,0:T(8,128)(2,1)S(1)}, u32[]{:S(2)}, u32[]{:S(2)}) collective-permute-start(bf16[48,512]{1,0:T(8,128)(2,1)S(1)} %get-tuple-element.48), channel_id=1, source_target_pairs={{0,2},{1,3},{2,0},{3,1},{4,6},{5,7},{6,4},{7,5},{8,10},{9,11},{10,... | collective-permute-start | bytes 147464 | tf_op jit(solution)/shard_map/ppermute | solution.py:221
  25.0 1.3 %collective-permute-start.12 = (bf16[48,512]{1,0:T(8,128)(2,1)S(1)}, bf16[48,512]{1,0:T(8,128)(2,1)S(1)}, u32[]{:S(2)}, u32[]{:S(2)}) collective-permute-start(bf16[48,512]{1,0:T(8,128)(2,1)S(1)} %collective-permute-done.8.refs_1_), channel_id=1, source_target_pairs={{0,1},{1,0},{2,3},{3,2},{4,5},{5,4},{6,7},{7,6},{8,9},{9,8},{10,11... | collective-permute-start | bytes 147464 | tf_op jit(solution)/shard_map/ppermute | solution.py:230
  25.3 1.2 %collective-permute-start.13 = (bf16[48,512]{1,0:T(8,128)(2,1)S(1)}, bf16[48,512]{1,0:T(8,128)(2,1)S(1)}, u32[]{:S(2)}, u32[]{:S(2)}) collective-permute-start(bf16[48,512]{1,0:T(8,128)(2,1)S(1)} %collective-permute-done.9.refs_2_), channel_id=1, source_target_pairs={{0,1},{1,0},{2,3},{3,2},{4,5},{5,4},{6,7},{7,6},{8,9},{9,8},{10,11... | collective-permute-start | bytes 147464 | tf_op jit(solution)/shard_map/ppermute | solution.py:230
  26.0 1.2 %collective-permute-start.14 = (bf16[48,512]{1,0:T(8,128)(2,1)S(1)}, bf16[48,512]{1,0:T(8,128)(2,1)S(1)}, u32[]{:S(2)}, u32[]{:S(2)}) collective-permute-start(bf16[48,512]{1,0:T(8,128)(2,1)S(1)} %collective-permute-done.10.refs_3_), channel_id=1, source_target_pairs={{0,1},{1,0},{2,3},{3,2},{4,5},{5,4},{6,7},{7,6},{8,9},{9,8},{10,11... | collective-permute-start | bytes 147464 | tf_op jit(solution)/shard_map/ppermute | solution.py:230

commit v12 on v11

--- a/solution.py
+++ b/solution.py
@@ -53,7 +53,7 @@
 def steps(n, turn):
     half = n // 2
     if turn == 0:
-        return [(half, half + 1), (n - 1, n - 2), (2, 3), (1, 1)]
+        return [(n - 1, half + 1), (3, n - 2), (2, half), (1, 1)]
     return [(n - 1, half + 1), (3, n - 2), (2, half), (1, 1)]
 
 
@@ -64,26 +64,6 @@
 def senders(n, turn, me, core):
     passed = [me ^ jnp.where(core == 0, b, a) for a, b in steps(n, turn) if a != b]
     return partners(n, turn, me, core) + passed
-
-
-class Staged:
-    def __init__(self, n, half, rows, picked, width, slots):
-        self.n, self.half, self.rows, self.picked, self.slots = n, half, rows, picked, slots
-        self.g = n * half
-        self.mask = self.g + rows
-        self.message = self.mask + rows
-        self.shape = (self.message + picked + ADAPTER_RANK, width)
-
-    def x(self, q):
-        return pl.ds(q * self.half, self.half)
-
-    def own_rows(self, ref):
-        return ref[self.mask : self.mask + self.picked, self.slots : 2 * self.slots]
-
-    def all_rows(self, kept):
-        parts = self.n * self.picked // self.rows
-        at = [pl.ds((2 + k) * self.slots, self.slots) for k in range(parts)]
-        return jnp.concatenate([kept[self.rows :, k] for k in at], axis=0)
 
 
 def pack_kernel(n, chosen_hbm, slot_hbm, down_hbm, up_hbm, *refs):
@@ -103,75 +83,63 @@
     wait_all(start_all([out_ref.at[k] for k in range(count)], send, sems, 4))
 
 
-def stage_kernel(
-    n, lay, start_hbm, chosen_hbm, slot_hbm, count_hbm, g_hbm, x_hbm, own_hbm,
-    stage_hbm, start_ref, chosen_ref, slot_ref, count_ref, stage, sems,
+def table_kernel(
+    n, picked, start_hbm, chosen_hbm, slot_hbm, count_hbm, out_hbm, start_ref, chosen_ref, slot_ref, count_ref, out_ref, sems,
 ):
-    rows, picked, slots = lay.rows, lay.picked, lay.slots
-    width = stage.shape[1]
-    tables = start_all(
-        [chosen_hbm, slot_hbm, start_hbm, count_hbm], [chosen_ref, slot_ref, start_ref, count_ref], sems
-    )
-    gradient = start_all([g_hbm], [stage.at[pl.ds(lay.g, rows)]], sems, 4)
-    other = start_all(
-        [own_hbm] + [x_hbm.at[:, pl.ds(q * width, width)] for q in range(n)],
-        [stage.at[pl.ds(lay.message, picked + ADAPTER_RANK)]] + [stage.at[lay.x(q)] for q in range(n)],
-        sems,
-        5,
+    rows, width = out_ref.shape
+    slots = width // 4
+    wait_all(
+        start_all(
+            [start_hbm, chosen_hbm, slot_hbm, count_hbm], [start_ref, chosen_ref, slot_ref, count_ref], sems
+        )
     )
     me = lax.axis_index("dp")
-    wait_all(tables)
     position = lax.broadcasted_iota(i32, (rows, slots), 0)
     group = lax.broadcasted_iota(i32, (rows, slots), 1) // ADAPTER_RANK
+    segs = start_ref.shape[0]
     segment = jnp.full((rows, slots), -1, i32)
-    for k in range(start_ref.shape[0]):
+    for k in range(segs):
         segment += jnp.where(position >= start_ref[k, me], 1, 0)
-    stage[lay.mask : lay.mask + rows, :slots] = jnp.where(segment == group, 1.0, 0.0).astype(bf16)
-    mine = slot_rows(chosen_ref, slot_ref, [me], slots)
-    stage[lay.mask : lay.mask + picked, slots : 2 * slots] = mine
+    flag = (segment == group) | ((group == segs) & (position < count_ref[me]))
+    out_ref[:, :slots] = jnp.where(flag, 1.0, 0.0).astype(bf16)
+    out_ref[:picked, slots : 2 * slots] = slot_rows(chosen_ref, slot_ref, [me], slots)
     every = slot_rows(chosen_ref, slot_ref, range(n), slots)
-    for k in range(n * picked // rows):
-        at = pl.ds((2 + k) * slots, slots)
-        stage[lay.mask : lay.mask + rows, at] = every[k * rows : (k + 1) * rows]
-    wait_all(gradient)
-    live = lax.broadcasted_iota(i32, (rows, width), 0) < count_ref[me]
-    g = stage[lay.g : lay.g + rows, :]
-    stage[lay.g : lay.g + rows, :] = jnp.where(live, g, jnp.zeros_like(g))
-    wait_all(other)
-    wait_all(start_all([stage], [stage_hbm], sems, 6 + n))
-
-
-def hand_on_kernel(stage, out_ref):
-    out_ref[...] = stage[...]
-
-
-def middle_kernel(n, lay, stage, x_other, *refs):
+    out_ref[:, 2 * slots : 3 * slots] = every[:rows]
+    out_ref[:, 3 * slots :] = every[rows:]
+    wait_all(start_all([out_ref], [out_hbm], sems, 4))
+
+
+def hand_on_kernel(in_ref, out_ref):
+    out_ref[...] = in_ref[...]
+
+
+def middle_kernel(n, table_ref, g_ref, x_mine, x_other, own_ref, *refs):
     count = n // 2 + 1
     got, (dlow_ref, a_ref, kept_ref) = refs[: n - 1], refs[n - 1 : n + 2]
     send, (x_ref, got_ref, up_ref) = refs[n + 2 : n + 2 + count], refs[n + 2 + count :]
     me, core = lax.axis_index("dp"), lax.axis_index("tensor")
-    half, rows, picked = lay.half, lay.rows, lay.picked
-    width = stage.shape[1]
-    mine = pl.ds(pl.multiple_of(core * half, half), half)
-    other = pl.ds(pl.multiple_of((1 - core) * half, half), half)
-    for q in range(n):
-        x_ref[mine, q * width : (q + 1) * width] = stage[lay.x(q), :]
-    x_ref[other, :] = x_other[...]
-    ranks = senders(n, 0, me, core)
-    got_ref[me] = stage[lay.message :, :]
-    for sender, message in zip(ranks[1:], got):
+    half = x_mine.shape[0]
+    rows, picked = dlow_ref.shape
+    width = g_ref.shape[1]
+    slots = width // 4
+    x_ref[pl.ds(pl.multiple_of(core * half, half), half), :] = x_mine[...]
+    x_ref[pl.ds(pl.multiple_of((1 - core) * half, half), half), :] = x_other[...]
+    for sender, message in zip(senders(n, 0, me, core), (own_ref,) + got):
         got_ref[sender] = message[...]
 
-    in_seg = stage[lay.mask : lay.mask + rows, :picked].astype(f32) > 0.0
-    g = stage[lay.g : lay.g + rows, :]
-    onehot = lay.own_rows(stage)
+    flags = table_ref[:, :slots].astype(f32)
+    in_seg = flags[:, :picked] > 0.0
+    live = flags[:, picked : picked + 1] > 0.0
+    g = jnp.where(live, g_ref[...], jnp.zeros(g_ref.shape, bf16))
+    onehot = table_ref[:picked, slots : 2 * slots]
     up_maps = got_ref[:, picked:, :].reshape(-1, width)
     b_sel = dot(onehot, up_maps, 1, 0).astype(bf16)
     dlow = jnp.where(in_seg, adapter_scale * dot(g, b_sel, 1, 1), 0.0).astype(bf16)
     dlow_ref[...] = dlow
     parts = n // 2
     a_ref[...] = got_ref[pl.ds(pl.multiple_of(core * parts, parts), parts), :picked, :]
-    kept_ref[...] = stage[lay.g : lay.message, :]
+    kept_ref[:rows, :] = g
+    kept_ref[rows:, :] = table_ref[...]
     targets = partners(n, 1, me, core)
     for target, message in zip(targets, send):
         at = pl.ds(pl.multiple_of(target * width, width), width)
@@ -203,16 +171,24 @@
     wait_all(done)
 
 
-def final_kernel(n, lay, kept_ref, *refs):
+def final_kernel(n, kept_ref, *refs):
     got, (a_ref, up_ref, rows_ref) = refs[:n], refs[n:]
     me, core = lax.axis_index("dp"), lax.axis_index("tensor")
-    piece, picked = up_ref.shape[1], lay.picked
+    piece, picked = up_ref.shape[1], rows_ref.shape[1] - ADAPTER_RANK
+    rows, slots = kept_ref.shape[0] // 2, kept_ref.shape[1] // 4
     for sender, message in zip(senders(n, 1, me, core), got):
         rows_ref[sender] = message[...]
-    rows = rows_ref[:, :picked, :].reshape(n * picked, rows_ref.shape[2])
-    a_ref[...] = dot(rows, lay.all_rows(kept_ref), 0, 0)
+    sums = rows_ref[:, :picked, :].reshape(n * picked, rows_ref.shape[2])
+    onehot = jnp.concatenate(
+        [kept_ref[rows:, 2 * slots : 3 * slots], kept_ref[rows:, 3 * slots :]], axis=0
+    )
+    a_ref[...] = dot(sums, onehot, 0, 0)
     at = pl.ds(pl.multiple_of(core * piece, piece), piece)
     up_ref[...] = jnp.sum(rows_ref[:, picked:, at].astype(f32), axis=0)
+
+
+def swap(array):
+    return lax.ppermute(array, "tensor", [(0, 1), (1, 0)])
 
 
 def exchange(messages, turn, beside):
@@ -227,7 +203,7 @@
     ]
     got[0], beside = lax.optimization_barrier((got[0], beside))
     passed = [
-        lax.ppermute(message, "tensor", [(0, 1), (1, 0)])
+        swap(message)
         for message, (a, b) in zip(got, steps(n, turn))
         if a != b
     ]
@@ -245,7 +221,7 @@
     adapter_slot,
     token_count,
 ):
-    tok_half, model_width = inputs.shape
+    model_width = inputs.shape[1]
     tok_rows, out_width = output_gradient.shape
     column_total, slot_width = down_maps.shape
     half = frozen_weight.shape[0]
@@ -266,7 +242,6 @@
     ]
     dma = pltpu.SemaphoreType.DMA
 
-    lay = Staged(n, tok_half, tok_rows, picked, column_total, slot_width)
     own, *sent = pl.pallas_call(
         functools.partial(pack_kernel, n),
         out_shape=[message] * count,
@@ -281,36 +256,39 @@
         ],
         compiler_params=params(56),
     )(chosen, adapter_slot, down_maps, up_maps)
-    sent, x_late = lax.optimization_barrier((sent, inputs))
-    x_other = lax.ppermute(x_late, "tensor", [(0, 1), (1, 0)])
-    stage = pl.pallas_call(
-        functools.partial(stage_kernel, n, lay),
-        out_shape=shape(lay.shape, bf16),
-        in_specs=[HBM] * 7,
+    table = pl.pallas_call(
+        functools.partial(table_kernel, n, picked),
+        out_shape=shape((tok_rows, 4 * slot_width), bf16),
+        in_specs=[HBM] * 4,
         out_specs=HBM,
-        scratch_shapes=tables + [pltpu.VMEM(lay.shape, bf16), dma((7 + n,))],
+        scratch_shapes=tables + [pltpu.VMEM((tok_rows, 4 * slot_width), bf16), dma((5,))],
         compiler_params=params(56),
         cost_estimate=pl.CostEstimate(flops=0, bytes_accessed=1 << 21, transcendentals=0),
-    )(starts, chosen, adapter_slot, token_count, output_gradient, inputs, own)
-    got, stage = exchange(sent, 0, stage)
-    stage = pl.pallas_call(
+    )(starts, chosen, adapter_slot, token_count)
+    sent, x_late, g_late = lax.optimization_barrier((sent, inputs, output_gradient))
+    x_other = swap(x_late)
+    g = swap(g_late)
+    own = swap(own)
+    got, table = exchange(sent, 0, table)
+    table = swap(table)
+    x_mine = pl.pallas_call(
         hand_on_kernel,
-        out_shape=shape(lay.shape, bf16),
+        out_shape=shape(inputs.shape, bf16),
         in_specs=[VMEM],
         out_specs=VMEM,
         compiler_params=params(8),
         cost_estimate=pl.CostEstimate(flops=0, bytes_accessed=1 << 21, transcendentals=0),
-    )(stage)
+    )(inputs)
 
     dlow, a_half, kept, own, *sent = pl.pallas_call(
-        functools.partial(middle_kernel, n, lay),
+        functools.partial(middle_kernel, n),
         out_shape=[
             shape((tok_rows, picked), bf16),
             shape((n // 2, picked, column_total), bf16),
             shape((2 * tok_rows, out_width), bf16),
         ]
         + [message] * count,
-        in_specs=[VMEM] * (1 + n),
+        in_specs=[VMEM] * (4 + n),
         out_specs=[VMEM] * (3 + count),
         scratch_shapes=[
             pltpu.VMEM((tok_rows, model_width), bf16),
@@ -318,7 +296,12 @@
             pltpu.VMEM((n, ADAPTER_RANK, out_width), bf16),
         ],
         compiler_params=params(8),
-    )(stage, x_other, *got)
+        cost_estimate=pl.CostEstimate(
+            flops=6 * tok_rows * model_width * picked,
+            bytes_accessed=4 * tok_rows * model_width,
+            transcendentals=0,
+        ),
+    )(table, g, x_mine, x_other, own, *got)
     base = pl.pallas_call(
         base_kernel,
         out_shape=shape((tok_rows, half), f32),
@@ -348,7 +331,7 @@
     got, grad_x = exchange(sent, 1, grad_x)
 
     grad_a, up_map_gradient = pl.pallas_call(
-        functools.partial(final_kernel, n, lay),
+        functools.partial(final_kernel, n),
         out_shape=[shape((column_total, slot_width), f32), shape((ADAPTER_RANK, piece), f32)],
         in_specs=[VMEM] * (1 + n),
         out_specs=[VMEM, VMEM],
@@ -439,7 +422,7 @@
         and down_maps.shape[0] == out_width
         and down_maps.shape[1] == n * up_maps.shape[0]
         and out_width % (128 * tp) == 0
-        and out_width >= 4 * down_maps.shape[1]
+        and out_width == 4 * down_maps.shape[1]
         and args[1].shape[0] == 2 * args[0].shape[0] == down_maps.shape[1]
         and args[5].shape[1] * ADAPTER_RANK * n == 2 * down_maps.shape[1]
     )

time: 28.5 us -> 29.9 us (1.049)
  starting transfers between devices: 14.8 us -> 16.3 us
  waiting for transfers between devices: 3.38 us -> 3.97 us
  Pallas kernels: 8.17 us -> 7.61 us
    ppermute x8, starting transfers between devices: 13 us -> 14.5 us  [exchange(): lax.ppermute(message, ('dp', 'tensor'), [(2 * i + c, 2 * (i ^ step[c]) +...]
    ppermute x7 -> x10, waiting for transfers between devices: 0.99 us -> 2.15 us  [swap(): return lax.ppermute(array, 'tensor', [(0, 1), (1, 0)])]
    pallas_call x4, Pallas kernels: 4.51 us -> 3.8 us  [the longest x1 1.47 us: local_kernels(): pl.pallas_call(functools.partial(table_kernel, n, picked), out_shape=shap...]
    ppermute x8, waiting for transfers between devices: 2.39 us -> 1.81 us  [exchange(): lax.ppermute(message, ('dp', 'tensor'), [(2 * i + c, 2 * (i ^ step[c]) +...]
    ppermute x7 -> x10, starting transfers between devices: 1.77 us -> 1.81 us  [swap(): return lax.ppermute(array, 'tensor', [(0, 1), (1, 0)])]
  transfers between devices with their start and end apart: 15 -> 18, of which waited for: 7 -> 11; matrix products, arithmetic and copies ran while one was open for 0% -> 0% of each run, Pallas kernels for 14% -> 11%
where the time goes in v12:
time: 29.9 us; the launch traced here: 29.7 us
  starting transfers between devices  16.3 us (55%)
  Pallas kernels  7.61 us (25%)
  waiting for transfers between devices  3.97 us (13%)
  local copies, waits for them, and re-layouts  1.05 us (4%)
  between operations  0.76 us (3%)
    ppermute x8, starting transfers between devices, exchange(): lax.ppermute(message, ('dp', 'tensor'), [(2 * i + c, 2 * (i ^ step[c]) +...  14.5 us
    ppermute x10, waiting for transfers between devices, swap(): return lax.ppermute(array, 'tensor', [(0, 1), (1, 0)])  2.15 us
    pallas_call x1, Pallas kernels, local_kernels(): pl.pallas_call(functools.partial(pack_kernel, n), out_shape=[message] * c...  2.02 us
    ppermute x8, waiting for transfers between devices, exchange(): lax.ppermute(message, ('dp', 'tensor'), [(2 * i + c, 2 * (i ^ step[c]) +...  1.81 us
    ppermute x10, starting transfers between devices, swap(): return lax.ppermute(array, 'tensor', [(0, 1), (1, 0)])  1.81 us
    pallas_call x1, Pallas kernels, local_kernels(): pl.pallas_call(functools.partial(table_kernel, n, picked), out_shape=shap...  1.47 us
    pallas_call x1, Pallas kernels, local_kernels(): pl.pallas_call(functools.partial(middle_kernel, n), out_shape=[shape((tok...  1.28 us
    unnamed x4, local copies, waits for them, and re-layouts  1.05 us
  transfers between devices with their start and end apart: 18, of which 11 were waited for; matrix products, arithmetic and copies ran while one was open for 0% of the time, Pallas kernels for 11%

profile of v12, /device:TPU:0, one launch (start us, length us, event | category | flops | bytes accessed | tf_op | source)
XLA Modules:
  0.0 29.7 jit_solution(17556473838172018734)
XLA Ops:
  0.6 0.0 copy-start
  0.6 2.0 %shard_map.112 = (bf16[48,512]{1,0:T(8,128)(2,1)}, bf16[48,512]{1,0:T(8,128)(2,1)}, bf16[48,512]{1,0:T(8,128)(2,1)}, bf16[48,512]{1,0:T(8,128)(2,1)}, bf16[48,512]{1,0:T(8,128)(2,1)}) custom-call(s32[2,8]{1,0:T(2,128)} %bitcast.2, s32[8]{0:T(128)} %slot_hbm.3, bf16[512,128]{1,0:T(8,128)(2,1)} %down_hbm.1, bf16[16,512]{1,0:T(8,128)(2,1)} %up_hbm.1), custom_call_target="tpu_custom_call" | custom-call | tf_op jit(solution)/shard_map/pallas_call | solution.py:245
  2.7 0.5 %collective-permute-start.3 = (bf16[64,4096]{1,0:T(8,128)(2,1)}, bf16[64,4096]{1,0:T(8,128)(2,1)S(1)}, u32[]{:S(2)}, u32[]{:S(2)}) collective-permute-start(bf16[64,4096]{1,0:T(8,128)(2,1)} %in_ref.1), channel_id=1, source_target_pairs={{0,1},{1,0},{2,3},{3,2},{4,5},{5,4},{6,7},{7,6},{8,9},{9,8},{10,11... | collective-permute-start | bytes 1572872 | tf_op jit(solution)/shard_map/ppermute | solution.py:191
  3.2 5.6 %collective-permute-start = (bf16[48,512]{1,0:T(8,128)(2,1)}, bf16[48,512]{1,0:T(8,128)(2,1)S(1)}, u32[]{:S(2)}, u32[]{:S(2)}) collective-permute-start(bf16[48,512]{1,0:T(8,128)(2,1)} %get-tuple-element.32), channel_id=1, source_target_pairs={{0,14},{1,11},{2,12},{3,9},{4,10},{5,15},{6,8},{7,13},{8,6},{9,3},... | collective-permute-start | bytes 147464 | tf_op jit(solution)/shard_map/ppermute | solution.py:197
  8.8 0.0 collective-permute-start.5
  8.8 2.0 %collective-permute-start.6 = (bf16[48,512]{1,0:T(8,128)(2,1)}, bf16[48,512]{1,0:T(8,128)(2,1)S(1)}, u32[]{:S(2)}, u32[]{:S(2)}) collective-permute-start(bf16[48,512]{1,0:T(8,128)(2,1)} %get-tuple-element.39), channel_id=1, source_target_pairs={{0,4},{1,9},{2,6},{3,11},{4,0},{5,13},{6,2},{7,15},{8,12},{9,1},{1... | collective-permute-start | bytes 147464 | tf_op jit(solution)/shard_map/ppermute | solution.py:197
  10.8 1.5 %collective-permute-start.7 = (bf16[48,512]{1,0:T(8,128)(2,1)}, bf16[48,512]{1,0:T(8,128)(2,1)S(1)}, u32[]{:S(2)}, u32[]{:S(2)}) collective-permute-start(bf16[48,512]{1,0:T(8,128)(2,1)} %get-tuple-element.40), channel_id=1, source_target_pairs={{0,2},{1,3},{2,0},{3,1},{4,6},{5,7},{6,4},{7,5},{8,10},{9,11},{10,... | collective-permute-start | bytes 147464 | tf_op jit(solution)/shard_map/ppermute | solution.py:197
  12.3 1.5 %shard_map.113 = bf16[128,512]{1,0:T(8,128)(2,1)} custom-call(s32[2,8]{1,0:T(2,128)} %bitcast.4, s32[2,8]{1,0:T(2,128)} %bitcast.3, s32[8]{0:T(128)} %slot_hbm.3, s32[8]{0:T(128)} %count_hbm.1), custom_call_target="tpu_custom_call" | custom-call | bytes 2097152 | tf_op jit(solution)/shard_map/pallas_call | solution.py:259
  13.8 0.0 collective-permute-done.refs_0_
  13.8 0.1 collective-permute-start.2
  13.8 0.3 collective-permute-done.5.refs_1_
  14.1 0.2 collective-permute-start.1
  14.3 0.3 collective-permute-done.6.refs_2_
  14.6 0.0 collective-permute-start.4
  14.6 0.4 %collective-permute-done.7.refs_3_ = bf16[48,512]{1,0:T(8,128)(2,1)S(1)} collective-permute-done((bf16[48,512]{1,0:T(8,128)(2,1)}, bf16[48,512]{1,0:T(8,128)(2,1)S(1)}, u32[]{:S(2)}, u32[]{:S(2)}) %collective-permute-start.7) | collective-permute-done | bytes 49184 | tf_op jit(solution)/shard_map/ppermute | solution.py:197
  15.1 0.1 collective-permute-start.8
  15.1 0.9 %collective-permute-done.4.own_ref = bf16[48,512]{1,0:T(8,128)(2,1)S(1)} collective-permute-done((bf16[48,512]{1,0:T(8,128)(2,1)}, bf16[48,512]{1,0:T(8,128)(2,1)S(1)}, u32[]{:S(2)}, u32[]{:S(2)}) %collective-permute-start.4) | collective-permute-done | bytes 49184 | tf_op jit(solution)/shard_map/ppermute | solution.py:191
  16.1 0.2 collective-permute-start.9
  16.2 0.1 collective-permute-done.8.refs_4_
  16.3 0.3 collective-permute-start.10
  16.6 0.0 copy-start.1
  16.6 1.0 %copy-done.1 = bf16[64,4096]{1,0:T(8,128)(2,1)S(1)} copy-done((bf16[64,4096]{1,0:T(8,128)(2,1)S(1)}, bf16[64,4096]{1,0:T(8,128)(2,1)}, u32[]{:S(2)}) %copy-start.1) | copy-done | bytes 524312
  17.7 0.0 collective-permute-done.9.refs_5_
  17.7 0.0 collective-permute-done.10.refs_6_
  17.7 0.0 collective-permute-done.2.g_ref
  17.7 0.0 collective-permute-done.1.table_ref
  17.7 0.0 collective-permute-done.3.x_other
  17.7 1.3 %shard_map.115 = (bf16[128,32]{1,0:T(8,128)(2,1)S(1)}, bf16[4,32,512]{2,1,0:T(8,128)(2,1)S(1)}, bf16[256,512]{1,0:T(8,128)(2,1)S(1)}, bf16[48,512]{1,0:T(8,128)(...) custom-call(bf16[128,512]{1,0:T(8,128)(2,1)S(1)} %collective-permute, ...), custom_call_target="tpu_custom_call" | custom-call | flops 100663296 | bytes 2097152 | tf_op jit(solution)/shard_map/pallas_call | solution.py:283
  19.0 2.0 %collective-permute-start.11 = (bf16[48,512]{1,0:T(8,128)(2,1)S(1)}, bf16[48,512]{1,0:T(8,128)(2,1)S(1)}, u32[]{:S(2)}, u32[]{:S(2)}) collective-permute-start(bf16[48,512]{1,0:T(8,128)(2,1)S(1)} %get-tuple-element.41), channel_id=1, source_target_pairs={{0,14},{1,11},{2,12},{3,9},{4,10},{5,15},{6,8},{7,13},{8,6},{9,3},... | collective-permute-start | bytes 147464 | tf_op jit(solution)/shard_map/ppermute | solution.py:197
  21.0 0.0 collective-permute-start.12
  21.0 2.5 %collective-permute-start.13 = (bf16[48,512]{1,0:T(8,128)(2,1)S(1)}, bf16[48,512]{1,0:T(8,128)(2,1)S(1)}, u32[]{:S(2)}, u32[]{:S(2)}) collective-permute-start(bf16[48,512]{1,0:T(8,128)(2,1)S(1)} %get-tuple-element.49), channel_id=1, source_target_pairs={{0,4},{1,9},{2,6},{3,11},{4,0},{5,13},{6,2},{7,15},{8,12},{9,1},{1... | collective-permute-start | bytes 147464 | tf_op jit(solution)/shard_map/ppermute | solution.py:197
  23.5 1.0 %collective-permute-start.14 = (bf16[48,512]{1,0:T(8,128)(2,1)S(1)}, bf16[48,512]{1,0:T(8,128)(2,1)S(1)}, u32[]{:S(2)}, u32[]{:S(2)}) collective-permute-start(bf16[48,512]{1,0:T(8,128)(2,1)S(1)} %get-tuple-element.50), channel_id=1, source_target_pairs={{0,2},{1,3},{2,0},{3,1},{4,6},{5,7},{6,4},{7,5},{8,10},{9,11},{10,... | collective-permute-start | bytes 147464 | tf_op jit(solution)/shard_map/ppermute | solution.py:197
  24.5 0.0 copy-done
  24.5 0.8 %shard_map.116.base_ref = f32[128,2048]{1,0:T(8,128)S(1)} custom-call(bf16[256,512]{1,0:T(8,128)(2,1)S(1)} %get-tuple-element.42.kept_ref, bf16[2048,512]{1,0:T(8,128)(2,1)S(1)} %copy-done), custom_call_target="tpu_custom_call" | custom-call | flops 268435456 | bytes 3145728 | tf_op jit(solution)/shard_map/pallas_call | solution.py:305
  25.3 1.0 %shard_map.117 = bf16[128,2048]{1,0:T(8,128)(2,1)} custom-call(f32[128,2048]{1,0:T(8,128)S(1)} %shard_map.116.base_ref, bf16[128,32]{1,0:T(8,128)(2,1)S(1)} %get-tuple-element.43.dlow_ref, bf16[4,32,512]{2,1,0:T(8,128)(2,1)S(1)} %get-tuple-element.44.a_ref), custom_call_target="tpu_custom_call" | custom-call | flops 16777216 | bytes 1572864 | tf_op jit(solution)/shard_map/pallas_call | solution.py:317
  26.3 0.0 collective-permute-done.11.refs_1_
  26.3 0.4 %collective-permute-done.12.refs_2_ = bf16[48,512]{1,0:T(8,128)(2,1)S(1)} collective-permute-done((bf16[48,512]{1,0:T(8,128)(2,1)S(1)}, bf16[48,512]{1,0:T(8,128)(2,1)S(1)}, u32[]{:S(2)}, u32[]{:S(2)}) %collective-permute-start.12) | collective-permute-done | bytes 49184 | tf_op jit(solution)/shard_map/ppermute | solution.py:197
  26.7 0.0 collective-permute-start.16
  26.7 0.3 %collective-permute-done.13.refs_3_ = bf16[48,512]{1,0:T(8,128)(2,1)S(1)} collective-permute-done((bf16[48,512]{1,0:T(8,128)(2,1)S(1)}, bf16[48,512]{1,0:T(8,128)(2,1)S(1)}, u32[]{:S(2)}, u32[]{:S(2)}) %collective-permute-start.13) | collective-permute-done | bytes 49184 | tf_op jit(solution)/shard_map/ppermute | solution.py:197
  27.0 0.5 %collective-permute-start.17 = (bf16[48,512]{1,0:T(8,128)(2,1)S(1)}, bf16[48,512]{1,0:T(8,128)(2,1)S(1)}, u32[]{:S(2)}, u32[]{:S(2)}) collective-permute-start(bf16[48,512]{1,0:T(8,128)(2,1)S(1)} %collective-permute-done.13.refs_3_), channel_id=1, source_target_pairs={{0,1},{1,0},{2,3},{3,2},{4,5},{5,4},{6,7},{7,6},{8,9},{9,8},{10,11... | collective-permute-start | bytes 147464 | tf_op jit(solution)/shard_map/ppermute | solution.py:191
  27.5 0.0 collective-permute-start.15
  27.5 0.1 collective-permute-done.14.refs_4_
  27.6 0.3 %collective-permute-done.16.refs_6_ = bf16[48,512]{1,0:T(8,128)(2,1)S(1)} collective-permute-done((bf16[48,512]{1,0:T(8,128)(2,1)S(1)}, bf16[48,512]{1,0:T(8,128)(2,1)S(1)}, u32[]{:S(2)}, u32[]{:S(2)}) %collective-permute-start.16) | collective-permute-done | bytes 49184 | tf_op jit(solution)/shard_map/ppermute | solution.py:191
  27.9 0.4 %collective-permute-done.17.refs_7_ = bf16[48,512]{1,0:T(8,128)(2,1)S(1)} collective-permute-done((bf16[48,512]{1,0:T(8,128)(2,1)S(1)}, bf16[48,512]{1,0:T(8,128)(2,1)S(1)}, u32[]{:S(2)}, u32[]{:S(2)}) %collective-permute-start.17) | collective-permute-done | bytes 49184 | tf_op jit(solution)/shard_map/ppermute | solution.py:191
  28.4 0.3 %collective-permute-done.15.refs_5_ = bf16[48,512]{1,0:T(8,128)(2,1)S(1)} collective-permute-done((bf16[48,512]{1,0:T(8,128)(2,1)S(1)}, bf16[48,512]{1,0:T(8,128)(2,1)S(1)}, u32[]{:S(2)}, u32[]{:S(2)}) %collective-permute-start.15) | collective-permute-done | bytes 49184 | tf_op jit(solution)/shard_map/ppermute | solution.py:191
  28.7 1.0 %shard_map.118 = (f32[512,128]{1,0:T(8,128)}, f32[16,256]{1,0:T(8,128)}) custom-call(bf16[256,512]{1,0:T(8,128)(2,1)S(1)} %get-tuple-element.42.kept_ref, bf16[48,512]{1,0:T(8,128)(2,1)S(1)} %get-tuple-element.46.refs_0_, bf16[48,512]{1,0:T(8,128)(2,1)S(1)} %collective-permute-done.11.refs_1_, bf16[48,512]{1,0:T(8,128)(2,1)S(1)} %collective-permute-done.12.refs_2_, ...), custom_call_target="tpu_custom_call" | custom-call | tf_op jit(solution)/shard_map/pallas_call | solution.py:333
  (1 shorter events, 0.0 us)
Async XLA Ops:
  0.6 23.8 %copy-start = (bf16[2048,512]{1,0:T(8,128)(2,1)S(1)}, bf16[2048,512]{1,0:T(8,128)(2,1)}, u32[]{:S(2)}) copy-start(bf16[2048,512]{1,0:T(8,128)(2,1)} %w_ref.1) | copy-start | bytes 6291460
  2.7 15.0 %collective-permute-start.3 = (bf16[64,4096]{1,0:T(8,128)(2,1)}, bf16[64,4096]{1,0:T(8,128)(2,1)S(1)}, u32[]{:S(2)}, u32[]{:S(2)}) collective-permute-start(bf16[64,4096]{1,0:T(8,128)(2,1)} %in_ref.1), channel_id=1, source_target_pairs={{0,1},{1,0},{2,3},{3,2},{4,5},{5,4},{6,7},{7,6},{8,9},{9,8},{10,11... | collective-permute-start | bytes 1572872 | tf_op jit(solution)/shard_map/ppermute | solution.py:191
  3.2 10.6 %collective-permute-start = (bf16[48,512]{1,0:T(8,128)(2,1)}, bf16[48,512]{1,0:T(8,128)(2,1)S(1)}, u32[]{:S(2)}, u32[]{:S(2)}) collective-permute-start(bf16[48,512]{1,0:T(8,128)(2,1)} %get-tuple-element.32), channel_id=1, source_target_pairs={{0,14},{1,11},{2,12},{3,9},{4,10},{5,15},{6,8},{7,13},{8,6},{9,3},... | collective-permute-start | bytes 147464 | tf_op jit(solution)/shard_map/ppermute | solution.py:197
  8.8 5.3 %collective-permute-start.5 = (bf16[48,512]{1,0:T(8,128)(2,1)}, bf16[48,512]{1,0:T(8,128)(2,1)S(1)}, u32[]{:S(2)}, u32[]{:S(2)}) collective-permute-start(bf16[48,512]{1,0:T(8,128)(2,1)} %get-tuple-element.38), channel_id=1, source_target_pairs={{0,6},{1,13},{2,4},{3,15},{4,2},{5,9},{6,0},{7,11},{8,14},{9,5},{1... | collective-permute-start | bytes 147464 | tf_op jit(solution)/shard_map/ppermute | solution.py:197
  8.8 5.8 %collective-permute-start.6 = (bf16[48,512]{1,0:T(8,128)(2,1)}, bf16[48,512]{1,0:T(8,128)(2,1)S(1)}, u32[]{:S(2)}, u32[]{:S(2)}) collective-permute-start(bf16[48,512]{1,0:T(8,128)(2,1)} %get-tuple-element.39), channel_id=1, source_target_pairs={{0,4},{1,9},{2,6},{3,11},{4,0},{5,13},{6,2},{7,15},{8,12},{9,1},{1... | collective-permute-start | bytes 147464 | tf_op jit(solution)/shard_map/ppermute | solution.py:197
  10.8 4.3 %collective-permute-start.7 = (bf16[48,512]{1,0:T(8,128)(2,1)}, bf16[48,512]{1,0:T(8,128)(2,1)S(1)}, u32[]{:S(2)}, u32[]{:S(2)}) collective-permute-start(bf16[48,512]{1,0:T(8,128)(2,1)} %get-tuple-element.40), channel_id=1, source_target_pairs={{0,2},{1,3},{2,0},{3,1},{4,6},{5,7},{6,4},{7,5},{8,10},{9,11},{10,... | collective-permute-start | bytes 147464 | tf_op jit(solution)/shard_map/ppermute | solution.py:197
  13.8 3.9 %collective-permute-start.2 = (bf16[128,512]{1,0:T(8,128)(2,1)}, bf16[128,512]{1,0:T(8,128)(2,1)S(1)}, u32[]{:S(2)}, u32[]{:S(2)}) collective-permute-start(bf16[128,512]{1,0:T(8,128)(2,1)} %param.10), channel_id=1, source_target_pairs={{0,1},{1,0},{2,3},{3,2},{4,5},{5,4},{6,7},{7,6},{8,9},{9,8},{10,11... | collective-permute-start | bytes 393224 | tf_op jit(solution)/shard_map/ppermute | solution.py:191
  14.1 3.6 %collective-permute-start.1 = (bf16[128,512]{1,0:T(8,128)(2,1)}, bf16[128,512]{1,0:T(8,128)(2,1)S(1)}, u32[]{:S(2)}, u32[]{:S(2)}) collective-permute-start(bf16[128,512]{1,0:T(8,128)(2,1)} %shard_map.113), channel_id=1, source_target_pairs={{0,1},{1,0},{2,3},{3,2},{4,5},{5,4},{6,7},{7,6},{8,9},{9,8},{10,11... | collective-permute-start | bytes 393224 | tf_op jit(solution)/shard_map/ppermute | solution.py:191
  14.6 1.4 %collective-permute-start.4 = (bf16[48,512]{1,0:T(8,128)(2,1)}, bf16[48,512]{1,0:T(8,128)(2,1)S(1)}, u32[]{:S(2)}, u32[]{:S(2)}) collective-permute-start(bf16[48,512]{1,0:T(8,128)(2,1)} %get-tuple-element.36), channel_id=1, source_target_pairs={{0,1},{1,0},{2,3},{3,2},{4,5},{5,4},{6,7},{7,6},{8,9},{9,8},{10,11... | collective-permute-start | bytes 147464 | tf_op jit(solution)/shard_map/ppermute | solution.py:191
  15.1 1.2 %collective-permute-start.8 = (bf16[48,512]{1,0:T(8,128)(2,1)S(1)}, bf16[48,512]{1,0:T(8,128)(2,1)S(1)}, u32[]{:S(2)}, u32[]{:S(2)}) collective-permute-start(bf16[48,512]{1,0:T(8,128)(2,1)S(1)} %collective-permute-done.refs_0_), channel_id=1, source_target_pairs={{0,1},{1,0},{2,3},{3,2},{4,5},{5,4},{6,7},{7,6},{8,9},{9,8},{10,11... | collective-permute-start | bytes 147464 | tf_op jit(solution)/shard_map/ppermute | solution.py:191
  16.1 1.6 %collective-permute-start.9 = (bf16[48,512]{1,0:T(8,128)(2,1)S(1)}, bf16[48,512]{1,0:T(8,128)(2,1)S(1)}, u32[]{:S(2)}, u32[]{:S(2)}) collective-permute-start(bf16[48,512]{1,0:T(8,128)(2,1)S(1)} %collective-permute-done.5.refs_1_), channel_id=1, source_target_pairs={{0,1},{1,0},{2,3},{3,2},{4,5},{5,4},{6,7},{7,6},{8,9},{9,8},{10,11... | collective-permute-start | bytes 147464 | tf_op jit(solution)/shard_map/ppermute | solution.py:191
  16.3 1.4 %collective-permute-start.10 = (bf16[48,512]{1,0:T(8,128)(2,1)S(1)}, bf16[48,512]{1,0:T(8,128)(2,1)S(1)}, u32[]{:S(2)}, u32[]{:S(2)}) collective-permute-start(bf16[48,512]{1,0:T(8,128)(2,1)S(1)} %collective-permute-done.6.refs_2_), channel_id=1, source_target_pairs={{0,1},{1,0},{2,3},{3,2},{4,5},{5,4},{6,7},{7,6},{8,9},{9,8},{10,11... | collective-permute-start | bytes 147464 | tf_op jit(solution)/shard_map/ppermute | solution.py:191
  16.6 1.0 %copy-start.1 = (bf16[64,4096]{1,0:T(8,128)(2,1)S(1)}, bf16[64,4096]{1,0:T(8,128)(2,1)}, u32[]{:S(2)}) copy-start(bf16[64,4096]{1,0:T(8,128)(2,1)} %in_ref.1) | copy-start | bytes 1572868
  19.0 7.3 %collective-permute-start.11 = (bf16[48,512]{1,0:T(8,128)(2,1)S(1)}, bf16[48,512]{1,0:T(8,128)(2,1)S(1)}, u32[]{:S(2)}, u32[]{:S(2)}) collective-permute-start(bf16[48,512]{1,0:T(8,128)(2,1)S(1)} %get-tuple-element.41), channel_id=1, source_target_pairs={{0,14},{1,11},{2,12},{3,9},{4,10},{5,15},{6,8},{7,13},{8,6},{9,3},... | collective-permute-start | bytes 147464 | tf_op jit(solution)/shard_map/ppermute | solution.py:197
  21.0 5.7 %collective-permute-start.12 = (bf16[48,512]{1,0:T(8,128)(2,1)S(1)}, bf16[48,512]{1,0:T(8,128)(2,1)S(1)}, u32[]{:S(2)}, u32[]{:S(2)}) collective-permute-start(bf16[48,512]{1,0:T(8,128)(2,1)S(1)} %get-tuple-element.48), channel_id=1, source_target_pairs={{0,6},{1,13},{2,4},{3,15},{4,2},{5,9},{6,0},{7,11},{8,14},{9,5},{1... | collective-permute-start | bytes 147464 | tf_op jit(solution)/shard_map/ppermute | solution.py:197
  21.0 6.0 %collective-permute-start.13 = (bf16[48,512]{1,0:T(8,128)(2,1)S(1)}, bf16[48,512]{1,0:T(8,128)(2,1)S(1)}, u32[]{:S(2)}, u32[]{:S(2)}) collective-permute-start(bf16[48,512]{1,0:T(8,128)(2,1)S(1)} %get-tuple-element.49), channel_id=1, source_target_pairs={{0,4},{1,9},{2,6},{3,11},{4,0},{5,13},{6,2},{7,15},{8,12},{9,1},{1... | collective-permute-start | bytes 147464 | tf_op jit(solution)/shard_map/ppermute | solution.py:197
  23.5 4.1 %collective-permute-start.14 = (bf16[48,512]{1,0:T(8,128)(2,1)S(1)}, bf16[48,512]{1,0:T(8,128)(2,1)S(1)}, u32[]{:S(2)}, u32[]{:S(2)}) collective-permute-start(bf16[48,512]{1,0:T(8,128)(2,1)S(1)} %get-tuple-element.50), channel_id=1, source_target_pairs={{0,2},{1,3},{2,0},{3,1},{4,6},{5,7},{6,4},{7,5},{8,10},{9,11},{10,... | collective-permute-start | bytes 147464 | tf_op jit(solution)/shard_map/ppermute | solution.py:197
  26.7 1.2 %collective-permute-start.16 = (bf16[48,512]{1,0:T(8,128)(2,1)S(1)}, bf16[48,512]{1,0:T(8,128)(2,1)S(1)}, u32[]{:S(2)}, u32[]{:S(2)}) collective-permute-start(bf16[48,512]{1,0:T(8,128)(2,1)S(1)} %collective-permute-done.12.refs_2_), channel_id=1, source_target_pairs={{0,1},{1,0},{2,3},{3,2},{4,5},{5,4},{6,7},{7,6},{8,9},{9,8},{10,11... | collective-permute-start | bytes 147464 | tf_op jit(solution)/shard_map/ppermute | solution.py:191
  27.0 1.3 %collective-permute-start.17 = (bf16[48,512]{1,0:T(8,128)(2,1)S(1)}, bf16[48,512]{1,0:T(8,128)(2,1)S(1)}, u32[]{:S(2)}, u32[]{:S(2)}) collective-permute-start(bf16[48,512]{1,0:T(8,128)(2,1)S(1)} %collective-permute-done.13.refs_3_), channel_id=1, source_target_pairs={{0,1},{1,0},{2,3},{3,2},{4,5},{5,4},{6,7},{7,6},{8,9},{9,8},{10,11... | collective-permute-start | bytes 147464 | tf_op jit(solution)/shard_map/ppermute | solution.py:191
  27.5 1.2 %collective-permute-start.15 = (bf16[48,512]{1,0:T(8,128)(2,1)S(1)}, bf16[48,512]{1,0:T(8,128)(2,1)S(1)}, u32[]{:S(2)}, u32[]{:S(2)}) collective-permute-start(bf16[48,512]{1,0:T(8,128)(2,1)S(1)} %collective-permute-done.11.refs_1_), channel_id=1, source_target_pairs={{0,1},{1,0},{2,3},{3,2},{4,5},{5,4},{6,7},{7,6},{8,9},{9,8},{10,11... | collective-permute-start | bytes 147464 | tf_op jit(solution)/shard_map/ppermute | solution.py:191

commit v13 on v9

--- a/solution.py
+++ b/solution.py
@@ -117,6 +117,9 @@
         5,
     )
     me = lax.axis_index("dp")
+    wait_all(other)
+    parts = [pl.ds(0, lay.g), pl.ds(lay.message, picked + ADAPTER_RANK), pl.ds(lay.g, 2 * rows)]
+    done = start_all([stage.at[at] for at in parts[:2]], [stage_hbm.at[at] for at in parts[:2]], sems, 6 + n)
     wait_all(tables)
     position = lax.broadcasted_iota(i32, (rows, slots), 0)
     group = lax.broadcasted_iota(i32, (rows, slots), 1) // ADAPTER_RANK
@@ -134,8 +137,8 @@
     live = lax.broadcasted_iota(i32, (rows, width), 0) < count_ref[me]
     g = stage[lay.g : lay.g + rows, :]
     stage[lay.g : lay.g + rows, :] = jnp.where(live, g, jnp.zeros_like(g))
-    wait_all(other)
-    wait_all(start_all([stage], [stage_hbm], sems, 6 + n))
+    done += start_all([stage.at[parts[2]]], [stage_hbm.at[parts[2]]], sems, 8 + n)
+    wait_all(done)
 
 
 def hand_on_kernel(stage, out_ref):
@@ -201,15 +204,22 @@
 
 
 def final_kernel(n, lay, kept_ref, *refs):
-    got, (a_ref, up_ref, rows_ref) = refs[:n], refs[n:]
+    got, (a_hbm, up_ref, rows_ref, a_ref, sems) = refs[:n], refs[n:]
     me, core = lax.axis_index("dp"), lax.axis_index("tensor")
     piece, picked = up_ref.shape[1], lay.picked
     for sender, message in zip(senders(n, me, core), got):
         rows_ref[sender] = message[...]
-    rows = rows_ref[:, :picked, :].reshape(n * picked, rows_ref.shape[2])
-    a_ref[...] = dot(rows, lay.all_rows(kept_ref), 0, 0)
+    onehot = lay.all_rows(kept_ref)
+    done = []
+    part = a_ref.shape[0] // 2
+    for k in range(2):
+        at = pl.ds(k * part, part)
+        rows = rows_ref[:, :picked, at].reshape(n * picked, part)
+        a_ref[at, :] = dot(rows, onehot, 0, 0)
+        done += start_all([a_ref.at[at]], [a_hbm.at[at]], sems, k)
     at = pl.ds(pl.multiple_of(core * piece, piece), piece)
     up_ref[...] = jnp.sum(rows_ref[:, picked:, at].astype(f32), axis=0)
+    wait_all(done)
 
 
 def exchange(messages, beside):
@@ -285,7 +295,7 @@
         out_shape=shape(lay.shape, bf16),
         in_specs=[HBM] * 7,
         out_specs=HBM,
-        scratch_shapes=tables + [pltpu.VMEM(lay.shape, bf16), dma((7 + n,))],
+        scratch_shapes=tables + [pltpu.VMEM(lay.shape, bf16), dma((9 + n,))],
         compiler_params=params(56),
         cost_estimate=pl.CostEstimate(flops=0, bytes_accessed=1 << 21, transcendentals=0),
     )(starts, chosen, adapter_slot, token_count, output_gradient, inputs, own)
@@ -348,8 +358,12 @@
         functools.partial(final_kernel, n, lay),
         out_shape=[shape((column_total, slot_width), f32), shape((ADAPTER_RANK, piece), f32)],
         in_specs=[VMEM] * (1 + n),
-        out_specs=[VMEM, VMEM],
-        scratch_shapes=[pltpu.VMEM((n,) + message.shape, bf16)],
+        out_specs=[HBM, VMEM],
+        scratch_shapes=[
+            pltpu.VMEM((n,) + message.shape, bf16),
+            pltpu.VMEM((column_total, slot_width), f32),
+            dma((2,)),
+        ],
         compiler_params=params(8),
     )(kept, own, *got)
     return grad_x, grad_a, up_map_gradient

time: 27.6 us -> 28.2 us (1.022)
  Pallas kernels: 8.17 us -> 8.79 us
    pallas_call x1, Pallas kernels: 1.01 us -> 1.61 us  [local_kernels(): pl.pallas_call(functools.partial(final_kernel, n, lay), out_shape=[shape(...]
  transfers between devices with their start and end apart: 15 -> 15, of which waited for: 5 -> 5; matrix products, arithmetic and copies ran while one was open for 0% -> 0% of each run, Pallas kernels for 15% -> 14%
where the time goes in v13:
time: 28.2 us; the launch traced here: 28 us
  starting transfers between devices  15.7 us (56%)
  Pallas kernels  8.79 us (31%)
  waiting for transfers between devices  1.59 us (6%)
  local copies, waits for them, and re-layouts  1.15 us (4%)
  between operations  0.75 us (3%)
    ppermute x8, starting transfers between devices, exchange(): lax.ppermute(message, ('dp', 'tensor'), [(2 * i + c, 2 * (i ^ step[c]) +...  14 us
    pallas_call x1, Pallas kernels, local_kernels(): pl.pallas_call(functools.partial(stage_kernel, n, lay), out_shape=shape(l...  2.19 us
    pallas_call x1, Pallas kernels, local_kernels(): pl.pallas_call(functools.partial(pack_kernel, n), out_shape=[message] * c...  1.88 us
    pallas_call x1, Pallas kernels, local_kernels(): pl.pallas_call(functools.partial(final_kernel, n, lay), out_shape=[shape(...  1.61 us
    pallas_call x1, Pallas kernels, local_kernels(): pl.pallas_call(functools.partial(middle_kernel, n, lay), out_shape=[shape...  1.27 us
    ppermute x6, starting transfers between devices, exchange(): lax.ppermute(message, 'tensor', [(0, 1), (1, 0)])  1.21 us
    ppermute x8, waiting for transfers between devices, exchange(): lax.ppermute(message, ('dp', 'tensor'), [(2 * i + c, 2 * (i ^ step[c]) +...  1.16 us
    unnamed x4, local copies, waits for them, and re-layouts  1.15 us
  transfers between devices with their start and end apart: 15, of which 5 were waited for; matrix products, arithmetic and copies ran while one was open for 0% of the time, Pallas kernels for 14%

profile of v13, /device:TPU:0, one launch (start us, length us, event | category | flops | bytes accessed | tf_op | source)
XLA Modules:
  0.0 28.0 jit_solution(3094662511343742880)
XLA Ops:
  0.6 1.9 %shard_map.112 = (bf16[48,512]{1,0:T(8,128)(2,1)}, bf16[48,512]{1,0:T(8,128)(2,1)}, bf16[48,512]{1,0:T(8,128)(2,1)}, bf16[48,512]{1,0:T(8,128)(2,1)}, bf16[48,512]{1,0:T(8,128)(2,1)}) custom-call(s32[2,8]{1,0:T(2,128)} %bitcast.2, s32[8]{0:T(128)} %slot_hbm.3, bf16[512,128]{1,0:T(8,128)(2,1)} %down_hbm.1, bf16[16,512]{1,0:T(8,128)(2,1)} %up_hbm.1), custom_call_target="tpu_custom_call" | custom-call | tf_op jit(solution)/shard_map/pallas_call | solution.py:277
  2.5 0.5 %collective-permute-start.1 = (bf16[64,4096]{1,0:T(8,128)(2,1)}, bf16[64,4096]{1,0:T(8,128)(2,1)S(1)}, u32[]{:S(2)}, u32[]{:S(2)}) collective-permute-start(bf16[64,4096]{1,0:T(8,128)(2,1)} %x_hbm.1), channel_id=1, source_target_pairs={{0,1},{1,0},{2,3},{3,2},{4,5},{5,4},{6,7},{7,6},{8,9},{9,8},{10,11... | collective-permute-start | bytes 1572872 | tf_op jit(solution)/shard_map/ppermute | solution.py:292
  3.0 5.6 %collective-permute-start = (bf16[48,512]{1,0:T(8,128)(2,1)}, bf16[48,512]{1,0:T(8,128)(2,1)S(1)}, u32[]{:S(2)}, u32[]{:S(2)}) collective-permute-start(bf16[48,512]{1,0:T(8,128)(2,1)} %get-tuple-element.31), channel_id=1, source_target_pairs={{0,14},{1,11},{2,12},{3,9},{4,10},{5,15},{6,8},{7,13},{8,6},{9,3},... | collective-permute-start | bytes 147464 | tf_op jit(solution)/shard_map/ppermute | solution.py:228
  8.6 0.0 collective-permute-start.2
  8.6 2.0 %collective-permute-start.3 = (bf16[48,512]{1,0:T(8,128)(2,1)}, bf16[48,512]{1,0:T(8,128)(2,1)S(1)}, u32[]{:S(2)}, u32[]{:S(2)}) collective-permute-start(bf16[48,512]{1,0:T(8,128)(2,1)} %get-tuple-element.37), channel_id=1, source_target_pairs={{0,4},{1,9},{2,6},{3,11},{4,0},{5,13},{6,2},{7,15},{8,12},{9,1},{1... | collective-permute-start | bytes 147464 | tf_op jit(solution)/shard_map/ppermute | solution.py:228
  10.6 1.5 %collective-permute-start.4 = (bf16[48,512]{1,0:T(8,128)(2,1)}, bf16[48,512]{1,0:T(8,128)(2,1)S(1)}, u32[]{:S(2)}, u32[]{:S(2)}) collective-permute-start(bf16[48,512]{1,0:T(8,128)(2,1)} %get-tuple-element.38), channel_id=1, source_target_pairs={{0,2},{1,3},{2,0},{3,1},{4,6},{5,7},{6,4},{7,5},{8,10},{9,11},{10,... | collective-permute-start | bytes 147464 | tf_op jit(solution)/shard_map/ppermute | solution.py:228
  12.1 2.2 %shard_map.113.stage = bf16[816,512]{1,0:T(8,128)(2,1)} custom-call(s32[2,8]{1,0:T(2,128)} %bitcast.4, s32[2,8]{1,0:T(2,128)} %bitcast.3, s32[8]{0:T(128)} %slot_hbm.3, s32[8]{0:T(128)} %count_hbm.1, bf16[128,512]{1,0:T(8,128)(2,1)} %g_hbm.1, bf16[64,4096]{1,0:T(8,128)(2,1)} %x_hbm.1, bf16[48,512]{1,0:T(8,128)(2,1)} %get-tuple-element.32.own_hbm), custom_call_target="tpu_custom_call" | custom-call | bytes 2097152 | tf_op jit(solution)/shard_map/pallas_call | solution.py:293
  14.3 0.0 collective-permute-done.refs_0_
  14.3 0.1 collective-permute-start.5
  14.4 0.0 collective-permute-done.2.refs_1_
  14.4 0.5 %collective-permute-start.6 = (bf16[48,512]{1,0:T(8,128)(2,1)S(1)}, bf16[48,512]{1,0:T(8,128)(2,1)S(1)}, u32[]{:S(2)}, u32[]{:S(2)}) collective-permute-start(bf16[48,512]{1,0:T(8,128)(2,1)S(1)} %collective-permute-done.2.refs_1_), channel_id=1, source_target_pairs={{0,1},{1,0},{2,3},{3,2},{4,5},{5,4},{6,7},{7,6},{8,9},{9,8},{10,11... | collective-permute-start | bytes 147464 | tf_op jit(solution)/shard_map/ppermute | solution.py:237
  14.9 0.0 collective-permute-done.3.refs_2_
  14.9 0.1 collective-permute-start.7
  15.0 0.0 copy-start
  15.0 1.1 %copy-done = bf16[816,512]{1,0:T(8,128)(2,1)S(1)} copy-done((bf16[816,512]{1,0:T(8,128)(2,1)S(1)}, bf16[816,512]{1,0:T(8,128)(2,1)}, u32[]{:S(2)}) %copy-start) | copy-done | bytes 835608
  16.2 0.0 copy-start.1
  16.2 0.1 shard_map.114.stage
  16.2 0.0 collective-permute-done.4.refs_3_
  16.2 0.0 collective-permute-done.5.refs_4_
  16.2 0.0 collective-permute-done.6.refs_5_
  16.2 0.0 collective-permute-done.7.refs_6_
  16.3 0.0 collective-permute-done.1.x_other
  16.3 1.3 %shard_map.115 = (bf16[128,32]{1,0:T(8,128)(2,1)S(1)}, bf16[4,32,512]{2,1,0:T(8,128)(2,1)S(1)}, bf16[256,512]{1,0:T(8,128)(2,1)S(1)}, bf16[48,512]{1,0:T(8,128)(...) custom-call(bf16[816,512]{1,0:T(8,128)(2,1)S(1)} %shard_map.114.stag, ...), custom_call_target="tpu_custom_call" | custom-call | tf_op jit(solution)/shard_map/pallas_call | solution.py:312
  17.5 1.4 %collective-permute-start.8 = (bf16[48,512]{1,0:T(8,128)(2,1)S(1)}, bf16[48,512]{1,0:T(8,128)(2,1)S(1)}, u32[]{:S(2)}, u32[]{:S(2)}) collective-permute-start(bf16[48,512]{1,0:T(8,128)(2,1)S(1)} %get-tuple-element.39), channel_id=1, source_target_pairs={{0,14},{1,11},{2,12},{3,9},{4,10},{5,15},{6,8},{7,13},{8,6},{9,3},... | collective-permute-start | bytes 147464 | tf_op jit(solution)/shard_map/ppermute | solution.py:228
  18.9 0.0 collective-permute-start.9
  19.0 2.9 %collective-permute-start.10 = (bf16[48,512]{1,0:T(8,128)(2,1)S(1)}, bf16[48,512]{1,0:T(8,128)(2,1)S(1)}, u32[]{:S(2)}, u32[]{:S(2)}) collective-permute-start(bf16[48,512]{1,0:T(8,128)(2,1)S(1)} %get-tuple-element.47), channel_id=1, source_target_pairs={{0,4},{1,9},{2,6},{3,11},{4,0},{5,13},{6,2},{7,15},{8,12},{9,1},{1... | collective-permute-start | bytes 147464 | tf_op jit(solution)/shard_map/ppermute | solution.py:228
  21.9 0.6 %collective-permute-start.11 = (bf16[48,512]{1,0:T(8,128)(2,1)S(1)}, bf16[48,512]{1,0:T(8,128)(2,1)S(1)}, u32[]{:S(2)}, u32[]{:S(2)}) collective-permute-start(bf16[48,512]{1,0:T(8,128)(2,1)S(1)} %get-tuple-element.48), channel_id=1, source_target_pairs={{0,2},{1,3},{2,0},{3,1},{4,6},{5,7},{6,4},{7,5},{8,10},{9,11},{10,... | collective-permute-start | bytes 147464 | tf_op jit(solution)/shard_map/ppermute | solution.py:228
  22.4 0.0 copy-done.1
  22.4 0.8 %shard_map.116.base_ref = f32[128,2048]{1,0:T(8,128)S(1)} custom-call(bf16[256,512]{1,0:T(8,128)(2,1)S(1)} %get-tuple-element.40.kept_ref, bf16[2048,512]{1,0:T(8,128)(2,1)S(1)} %copy-done.1), custom_call_target="tpu_custom_call" | custom-call | flops 268435456 | bytes 3145728 | tf_op jit(solution)/shard_map/pallas_call | solution.py:329
  23.2 1.0 %shard_map.117 = bf16[128,2048]{1,0:T(8,128)(2,1)} custom-call(f32[128,2048]{1,0:T(8,128)S(1)} %shard_map.116.base_ref, bf16[128,32]{1,0:T(8,128)(2,1)S(1)} %get-tuple-element.41.dlow_ref, bf16[4,32,512]{2,1,0:T(8,128)(2,1)S(1)} %get-tuple-element.42.a_ref), custom_call_target="tpu_custom_call" | custom-call | flops 16777216 | bytes 1572864 | tf_op jit(solution)/shard_map/pallas_call | solution.py:341
  24.2 0.3 %collective-permute-done.8.refs_1_ = bf16[48,512]{1,0:T(8,128)(2,1)S(1)} collective-permute-done((bf16[48,512]{1,0:T(8,128)(2,1)S(1)}, bf16[48,512]{1,0:T(8,128)(2,1)S(1)}, u32[]{:S(2)}, u32[]{:S(2)}) %collective-permute-start.8) | collective-permute-done | bytes 49184 | tf_op jit(solution)/shard_map/ppermute | solution.py:228
  24.6 0.0 collective-permute-start.12
  24.6 0.4 %collective-permute-done.9.refs_2_ = bf16[48,512]{1,0:T(8,128)(2,1)S(1)} collective-permute-done((bf16[48,512]{1,0:T(8,128)(2,1)S(1)}, bf16[48,512]{1,0:T(8,128)(2,1)S(1)}, u32[]{:S(2)}, u32[]{:S(2)}) %collective-permute-start.9) | collective-permute-done | bytes 49184 | tf_op jit(solution)/shard_map/ppermute | solution.py:228
  24.9 0.2 collective-permute-start.13
  25.1 0.0 collective-permute-done.10.refs_3_
  25.1 0.4 %collective-permute-start.14 = (bf16[48,512]{1,0:T(8,128)(2,1)S(1)}, bf16[48,512]{1,0:T(8,128)(2,1)S(1)}, u32[]{:S(2)}, u32[]{:S(2)}) collective-permute-start(bf16[48,512]{1,0:T(8,128)(2,1)S(1)} %collective-permute-done.10.refs_3_), channel_id=1, source_target_pairs={{0,1},{1,0},{2,3},{3,2},{4,5},{5,4},{6,7},{7,6},{8,9},{9,8},{10,11... | collective-permute-start | bytes 147464 | tf_op jit(solution)/shard_map/ppermute | solution.py:237
  25.5 0.5 %collective-permute-done.11.refs_4_ = bf16[48,512]{1,0:T(8,128)(2,1)S(1)} collective-permute-done((bf16[48,512]{1,0:T(8,128)(2,1)S(1)}, bf16[48,512]{1,0:T(8,128)(2,1)S(1)}, u32[]{:S(2)}, u32[]{:S(2)}) %collective-permute-start.11) | collective-permute-done | bytes 49184 | tf_op jit(solution)/shard_map/ppermute | solution.py:228
  26.0 0.0 collective-permute-done.12.refs_5_
  26.0 0.2 collective-permute-done.13.refs_6_
  26.1 0.2 collective-permute-done.14.refs_7_
  26.4 1.6 %shard_map.118 = (f32[512,128]{1,0:T(8,128)}, f32[16,256]{1,0:T(8,128)}) custom-call(bf16[256,512]{1,0:T(8,128)(2,1)S(1)} %get-tuple-element.40.kept_ref, bf16[48,512]{1,0:T(8,128)(2,1)S(1)} %get-tuple-element.44.refs_0_, bf16[48,512]{1,0:T(8,128)(2,1)S(1)} %collective-permute-done.8.refs_1_, bf16[48,512]{1,0:T(8,128)(2,1)S(1)} %collective-permute-done.9.refs_2_, ...), custom_call_target="tpu_custom_call" | custom-call | tf_op jit(solution)/shard_map/pallas_call | solution.py:357
Async XLA Ops:
  2.5 13.7 %collective-permute-start.1 = (bf16[64,4096]{1,0:T(8,128)(2,1)}, bf16[64,4096]{1,0:T(8,128)(2,1)S(1)}, u32[]{:S(2)}, u32[]{:S(2)}) collective-permute-start(bf16[64,4096]{1,0:T(8,128)(2,1)} %x_hbm.1), channel_id=1, source_target_pairs={{0,1},{1,0},{2,3},{3,2},{4,5},{5,4},{6,7},{7,6},{8,9},{9,8},{10,11... | collective-permute-start | bytes 1572872 | tf_op jit(solution)/shard_map/ppermute | solution.py:292
  3.0 11.3 %collective-permute-start = (bf16[48,512]{1,0:T(8,128)(2,1)}, bf16[48,512]{1,0:T(8,128)(2,1)S(1)}, u32[]{:S(2)}, u32[]{:S(2)}) collective-permute-start(bf16[48,512]{1,0:T(8,128)(2,1)} %get-tuple-element.31), channel_id=1, source_target_pairs={{0,14},{1,11},{2,12},{3,9},{4,10},{5,15},{6,8},{7,13},{8,6},{9,3},... | collective-permute-start | bytes 147464 | tf_op jit(solution)/shard_map/ppermute | solution.py:228
  8.6 5.8 %collective-permute-start.2 = (bf16[48,512]{1,0:T(8,128)(2,1)}, bf16[48,512]{1,0:T(8,128)(2,1)S(1)}, u32[]{:S(2)}, u32[]{:S(2)}) collective-permute-start(bf16[48,512]{1,0:T(8,128)(2,1)} %get-tuple-element.36), channel_id=1, source_target_pairs={{0,6},{1,13},{2,4},{3,15},{4,2},{5,9},{6,0},{7,11},{8,14},{9,5},{1... | collective-permute-start | bytes 147464 | tf_op jit(solution)/shard_map/ppermute | solution.py:228
  8.6 6.3 %collective-permute-start.3 = (bf16[48,512]{1,0:T(8,128)(2,1)}, bf16[48,512]{1,0:T(8,128)(2,1)S(1)}, u32[]{:S(2)}, u32[]{:S(2)}) collective-permute-start(bf16[48,512]{1,0:T(8,128)(2,1)} %get-tuple-element.37), channel_id=1, source_target_pairs={{0,4},{1,9},{2,6},{3,11},{4,0},{5,13},{6,2},{7,15},{8,12},{9,1},{1... | collective-permute-start | bytes 147464 | tf_op jit(solution)/shard_map/ppermute | solution.py:228
  10.6 5.6 %collective-permute-start.4 = (bf16[48,512]{1,0:T(8,128)(2,1)}, bf16[48,512]{1,0:T(8,128)(2,1)S(1)}, u32[]{:S(2)}, u32[]{:S(2)}) collective-permute-start(bf16[48,512]{1,0:T(8,128)(2,1)} %get-tuple-element.38), channel_id=1, source_target_pairs={{0,2},{1,3},{2,0},{3,1},{4,6},{5,7},{6,4},{7,5},{8,10},{9,11},{10,... | collective-permute-start | bytes 147464 | tf_op jit(solution)/shard_map/ppermute | solution.py:228
  14.3 1.9 %collective-permute-start.5 = (bf16[48,512]{1,0:T(8,128)(2,1)S(1)}, bf16[48,512]{1,0:T(8,128)(2,1)S(1)}, u32[]{:S(2)}, u32[]{:S(2)}) collective-permute-start(bf16[48,512]{1,0:T(8,128)(2,1)S(1)} %collective-permute-done.refs_0_), channel_id=1, source_target_pairs={{0,1},{1,0},{2,3},{3,2},{4,5},{5,4},{6,7},{7,6},{8,9},{9,8},{10,11... | collective-permute-start | bytes 147464 | tf_op jit(solution)/shard_map/ppermute | solution.py:237
  14.4 1.8 %collective-permute-start.6 = (bf16[48,512]{1,0:T(8,128)(2,1)S(1)}, bf16[48,512]{1,0:T(8,128)(2,1)S(1)}, u32[]{:S(2)}, u32[]{:S(2)}) collective-permute-start(bf16[48,512]{1,0:T(8,128)(2,1)S(1)} %collective-permute-done.2.refs_1_), channel_id=1, source_target_pairs={{0,1},{1,0},{2,3},{3,2},{4,5},{5,4},{6,7},{7,6},{8,9},{9,8},{10,11... | collective-permute-start | bytes 147464 | tf_op jit(solution)/shard_map/ppermute | solution.py:237
  14.9 1.3 %collective-permute-start.7 = (bf16[48,512]{1,0:T(8,128)(2,1)S(1)}, bf16[48,512]{1,0:T(8,128)(2,1)S(1)}, u32[]{:S(2)}, u32[]{:S(2)}) collective-permute-start(bf16[48,512]{1,0:T(8,128)(2,1)S(1)} %collective-permute-done.3.refs_2_), channel_id=1, source_target_pairs={{0,1},{1,0},{2,3},{3,2},{4,5},{5,4},{6,7},{7,6},{8,9},{9,8},{10,11... | collective-permute-start | bytes 147464 | tf_op jit(solution)/shard_map/ppermute | solution.py:237
  15.0 1.1 %copy-start = (bf16[816,512]{1,0:T(8,128)(2,1)S(1)}, bf16[816,512]{1,0:T(8,128)(2,1)}, u32[]{:S(2)}) copy-start(bf16[816,512]{1,0:T(8,128)(2,1)} %shard_map.113.stage) | copy-start | bytes 2506756
  16.2 6.3 %copy-start.1 = (bf16[2048,512]{1,0:T(8,128)(2,1)S(1)}, bf16[2048,512]{1,0:T(8,128)(2,1)}, u32[]{:S(2)}) copy-start(bf16[2048,512]{1,0:T(8,128)(2,1)} %w_ref.1) | copy-start | bytes 6291460
  17.5 7.0 %collective-permute-start.8 = (bf16[48,512]{1,0:T(8,128)(2,1)S(1)}, bf16[48,512]{1,0:T(8,128)(2,1)S(1)}, u32[]{:S(2)}, u32[]{:S(2)}) collective-permute-start(bf16[48,512]{1,0:T(8,128)(2,1)S(1)} %get-tuple-element.39), channel_id=1, source_target_pairs={{0,14},{1,11},{2,12},{3,9},{4,10},{5,15},{6,8},{7,13},{8,6},{9,3},... | collective-permute-start | bytes 147464 | tf_op jit(solution)/shard_map/ppermute | solution.py:228
  18.9 6.0 %collective-permute-start.9 = (bf16[48,512]{1,0:T(8,128)(2,1)S(1)}, bf16[48,512]{1,0:T(8,128)(2,1)S(1)}, u32[]{:S(2)}, u32[]{:S(2)}) collective-permute-start(bf16[48,512]{1,0:T(8,128)(2,1)S(1)} %get-tuple-element.46), channel_id=1, source_target_pairs={{0,6},{1,13},{2,4},{3,15},{4,2},{5,9},{6,0},{7,11},{8,14},{9,5},{1... | collective-permute-start | bytes 147464 | tf_op jit(solution)/shard_map/ppermute | solution.py:228
  19.0 6.1 %collective-permute-start.10 = (bf16[48,512]{1,0:T(8,128)(2,1)S(1)}, bf16[48,512]{1,0:T(8,128)(2,1)S(1)}, u32[]{:S(2)}, u32[]{:S(2)}) collective-permute-start(bf16[48,512]{1,0:T(8,128)(2,1)S(1)} %get-tuple-element.47), channel_id=1, source_target_pairs={{0,4},{1,9},{2,6},{3,11},{4,0},{5,13},{6,2},{7,15},{8,12},{9,1},{1... | collective-permute-start | bytes 147464 | tf_op jit(solution)/shard_map/ppermute | solution.py:228
  21.9 4.1 %collective-permute-start.11 = (bf16[48,512]{1,0:T(8,128)(2,1)S(1)}, bf16[48,512]{1,0:T(8,128)(2,1)S(1)}, u32[]{:S(2)}, u32[]{:S(2)}) collective-permute-start(bf16[48,512]{1,0:T(8,128)(2,1)S(1)} %get-tuple-element.48), channel_id=1, source_target_pairs={{0,2},{1,3},{2,0},{3,1},{4,6},{5,7},{6,4},{7,5},{8,10},{9,11},{10,... | collective-permute-start | bytes 147464 | tf_op jit(solution)/shard_map/ppermute | solution.py:228
  24.6 1.4 %collective-permute-start.12 = (bf16[48,512]{1,0:T(8,128)(2,1)S(1)}, bf16[48,512]{1,0:T(8,128)(2,1)S(1)}, u32[]{:S(2)}, u32[]{:S(2)}) collective-permute-start(bf16[48,512]{1,0:T(8,128)(2,1)S(1)} %collective-permute-done.8.refs_1_), channel_id=1, source_target_pairs={{0,1},{1,0},{2,3},{3,2},{4,5},{5,4},{6,7},{7,6},{8,9},{9,8},{10,11... | collective-permute-start | bytes 147464 | tf_op jit(solution)/shard_map/ppermute | solution.py:237
  24.9 1.2 %collective-permute-start.13 = (bf16[48,512]{1,0:T(8,128)(2,1)S(1)}, bf16[48,512]{1,0:T(8,128)(2,1)S(1)}, u32[]{:S(2)}, u32[]{:S(2)}) collective-permute-start(bf16[48,512]{1,0:T(8,128)(2,1)S(1)} %collective-permute-done.9.refs_2_), channel_id=1, source_target_pairs={{0,1},{1,0},{2,3},{3,2},{4,5},{5,4},{6,7},{7,6},{8,9},{9,8},{10,11... | collective-permute-start | bytes 147464 | tf_op jit(solution)/shard_map/ppermute | solution.py:237
  25.1 1.3 %collective-permute-start.14 = (bf16[48,512]{1,0:T(8,128)(2,1)S(1)}, bf16[48,512]{1,0:T(8,128)(2,1)S(1)}, u32[]{:S(2)}, u32[]{:S(2)}) collective-permute-start(bf16[48,512]{1,0:T(8,128)(2,1)S(1)} %collective-permute-done.10.refs_3_), channel_id=1, source_target_pairs={{0,1},{1,0},{2,3},{3,2},{4,5},{5,4},{6,7},{7,6},{8,9},{9,8},{10,11... | collective-permute-start | bytes 147464 | tf_op jit(solution)/shard_map/ppermute | solution.py:237

commit v14 on v11

--- a/solution.py
+++ b/solution.py
@@ -53,8 +53,8 @@
 def steps(n, turn):
     half = n // 2
     if turn == 0:
-        return [(half, half + 1), (n - 1, n - 2), (2, 3), (1, 1)]
-    return [(n - 1, half + 1), (3, n - 2), (2, half), (1, 1)]
+        return [(n - 1, half), (3, half + 1), (n - 2, 2), (1, 1)]
+    return [(n - 1, half + 1), (2, n - 2), (half, 3), (1, 1)]
 
 
 def partners(n, turn, me, core):

time: 28.5 us -> 28.5 us (level)
    ppermute x8, starting transfers between devices: 13 us -> 13.9 us  [exchange(): lax.ppermute(message, ('dp', 'tensor'), [(2 * i + c, 2 * (i ^ step[c]) +...]
    ppermute x6, starting transfers between devices: 1.26 us -> 0.46 us  [exchange(): lax.ppermute(message, 'tensor', [(0, 1), (1, 0)])]
    ppermute x6, waiting for transfers between devices: 0.99 us -> 0.58 us  [exchange(): lax.ppermute(message, 'tensor', [(0, 1), (1, 0)])]
    ppermute x8, waiting for transfers between devices: 2.39 us -> 2.77 us  [exchange(): lax.ppermute(message, ('dp', 'tensor'), [(2 * i + c, 2 * (i ^ step[c]) +...]
  transfers between devices with their start and end apart: 15 -> 15, of which waited for: 7 -> 6; matrix products, arithmetic and copies ran while one was open for 0% -> 0% of each run, Pallas kernels for 14% -> 14%
where the time goes in v14:
time: 28.5 us; the launch traced here: 28.3 us
  starting transfers between devices  14.9 us (52%)
  Pallas kernels  8.16 us (29%)
  waiting for transfers between devices  3.36 us (12%)
  local copies, waits for them, and re-layouts  1.15 us (4%)
  between operations  0.76 us (3%)
    ppermute x8, starting transfers between devices, exchange(): lax.ppermute(message, ('dp', 'tensor'), [(2 * i + c, 2 * (i ^ step[c]) +...  13.9 us
    ppermute x8, waiting for transfers between devices, exchange(): lax.ppermute(message, ('dp', 'tensor'), [(2 * i + c, 2 * (i ^ step[c]) +...  2.77 us
    pallas_call x1, Pallas kernels, local_kernels(): pl.pallas_call(functools.partial(stage_kernel, n, lay), out_shape=shape(l...  2.17 us
    pallas_call x1, Pallas kernels, local_kernels(): pl.pallas_call(functools.partial(pack_kernel, n), out_shape=[message] * c...  1.88 us
    pallas_call x1, Pallas kernels, local_kernels(): pl.pallas_call(functools.partial(middle_kernel, n, lay), out_shape=[shape...  1.26 us
    unnamed x4, local copies, waits for them, and re-layouts  1.15 us
    pallas_call x1, Pallas kernels, local_kernels(): pl.pallas_call(functools.partial(final_kernel, n, lay), out_shape=[shape(...  1.01 us
    pallas_call x1, Pallas kernels, local_kernels(): pl.pallas_call(grad_x_kernel, out_shape=shape((tok_rows, half), bf16), in...  0.98 us
  transfers between devices with their start and end apart: 15, of which 6 were waited for; matrix products, arithmetic and copies ran while one was open for 0% of the time, Pallas kernels for 14%

profile of v14, /device:TPU:0, one launch (start us, length us, event | category | flops | bytes accessed | tf_op | source)
XLA Modules:
  0.0 28.3 jit_solution(2006785328877090409)
XLA Ops:
  0.6 1.9 %shard_map.112 = (bf16[48,512]{1,0:T(8,128)(2,1)}, bf16[48,512]{1,0:T(8,128)(2,1)}, bf16[48,512]{1,0:T(8,128)(2,1)}, bf16[48,512]{1,0:T(8,128)(2,1)}, bf16[48,512]{1,0:T(8,128)(2,1)}) custom-call(s32[2,8]{1,0:T(2,128)} %bitcast.2, s32[8]{0:T(128)} %slot_hbm.3, bf16[512,128]{1,0:T(8,128)(2,1)} %down_hbm.1, bf16[16,512]{1,0:T(8,128)(2,1)} %up_hbm.1), custom_call_target="tpu_custom_call" | custom-call | tf_op jit(solution)/shard_map/pallas_call | solution.py:270
  2.5 0.5 %collective-permute-start.1 = (bf16[64,4096]{1,0:T(8,128)(2,1)}, bf16[64,4096]{1,0:T(8,128)(2,1)S(1)}, u32[]{:S(2)}, u32[]{:S(2)}) collective-permute-start(bf16[64,4096]{1,0:T(8,128)(2,1)} %x_hbm.1), channel_id=1, source_target_pairs={{0,1},{1,0},{2,3},{3,2},{4,5},{5,4},{6,7},{7,6},{8,9},{9,8},{10,11... | collective-permute-start | bytes 1572872 | tf_op jit(solution)/shard_map/ppermute | solution.py:285
  3.0 5.6 %collective-permute-start = (bf16[48,512]{1,0:T(8,128)(2,1)}, bf16[48,512]{1,0:T(8,128)(2,1)S(1)}, u32[]{:S(2)}, u32[]{:S(2)}) collective-permute-start(bf16[48,512]{1,0:T(8,128)(2,1)} %get-tuple-element.31), channel_id=1, source_target_pairs={{0,14},{1,9},{2,12},{3,11},{4,10},{5,13},{6,8},{7,15},{8,6},{9,1},... | collective-permute-start | bytes 147464 | tf_op jit(solution)/shard_map/ppermute | solution.py:221
  8.6 0.0 collective-permute-start.2
  8.6 0.9 %collective-permute-start.3 = (bf16[48,512]{1,0:T(8,128)(2,1)}, bf16[48,512]{1,0:T(8,128)(2,1)S(1)}, u32[]{:S(2)}, u32[]{:S(2)}) collective-permute-start(bf16[48,512]{1,0:T(8,128)(2,1)} %get-tuple-element.37), channel_id=1, source_target_pairs={{0,12},{1,5},{2,14},{3,7},{4,8},{5,1},{6,10},{7,3},{8,4},{9,13},{1... | collective-permute-start | bytes 147464 | tf_op jit(solution)/shard_map/ppermute | solution.py:221
  9.5 1.5 %collective-permute-start.4 = (bf16[48,512]{1,0:T(8,128)(2,1)}, bf16[48,512]{1,0:T(8,128)(2,1)S(1)}, u32[]{:S(2)}, u32[]{:S(2)}) collective-permute-start(bf16[48,512]{1,0:T(8,128)(2,1)} %get-tuple-element.38), channel_id=1, source_target_pairs={{0,2},{1,3},{2,0},{3,1},{4,6},{5,7},{6,4},{7,5},{8,10},{9,11},{10,... | collective-permute-start | bytes 147464 | tf_op jit(solution)/shard_map/ppermute | solution.py:221
  11.0 2.2 %shard_map.113.stage = bf16[816,512]{1,0:T(8,128)(2,1)} custom-call(s32[2,8]{1,0:T(2,128)} %bitcast.4, s32[2,8]{1,0:T(2,128)} %bitcast.3, s32[8]{0:T(128)} %slot_hbm.3, s32[8]{0:T(128)} %count_hbm.1, bf16[128,512]{1,0:T(8,128)(2,1)} %g_hbm.1, bf16[64,4096]{1,0:T(8,128)(2,1)} %x_hbm.1, bf16[48,512]{1,0:T(8,128)(2,1)} %get-tuple-element.32.own_hbm), custom_call_target="tpu_custom_call" | custom-call | bytes 2097152 | tf_op jit(solution)/shard_map/pallas_call | solution.py:286
  13.2 0.0 collective-permute-done.refs_0_
  13.2 0.1 collective-permute-start.5
  13.3 0.7 %collective-permute-done.2.refs_1_ = bf16[48,512]{1,0:T(8,128)(2,1)S(1)} collective-permute-done((bf16[48,512]{1,0:T(8,128)(2,1)}, bf16[48,512]{1,0:T(8,128)(2,1)S(1)}, u32[]{:S(2)}, u32[]{:S(2)}) %collective-permute-start.2) | collective-permute-done | bytes 49184 | tf_op jit(solution)/shard_map/ppermute | solution.py:221
  13.9 0.0 collective-permute-start.6
  13.9 0.9 %collective-permute-done.3.refs_2_ = bf16[48,512]{1,0:T(8,128)(2,1)S(1)} collective-permute-done((bf16[48,512]{1,0:T(8,128)(2,1)}, bf16[48,512]{1,0:T(8,128)(2,1)S(1)}, u32[]{:S(2)}, u32[]{:S(2)}) %collective-permute-start.3) | collective-permute-done | bytes 49184 | tf_op jit(solution)/shard_map/ppermute | solution.py:221
  14.8 0.0 collective-permute-start.7
  14.8 0.0 copy-start
  14.8 1.1 %copy-done = bf16[816,512]{1,0:T(8,128)(2,1)S(1)} copy-done((bf16[816,512]{1,0:T(8,128)(2,1)S(1)}, bf16[816,512]{1,0:T(8,128)(2,1)}, u32[]{:S(2)}) %copy-start) | copy-done | bytes 835608
  16.0 0.0 copy-start.1
  16.0 0.1 shard_map.114.stage
  16.1 0.0 collective-permute-done.4.refs_3_
  16.1 0.0 collective-permute-done.5.refs_4_
  16.1 0.0 collective-permute-done.6.refs_5_
  16.1 0.0 collective-permute-done.7.refs_6_
  16.1 0.0 collective-permute-done.1.x_other
  16.1 1.3 %shard_map.115 = (bf16[128,32]{1,0:T(8,128)(2,1)S(1)}, bf16[4,32,512]{2,1,0:T(8,128)(2,1)S(1)}, bf16[256,512]{1,0:T(8,128)(2,1)S(1)}, bf16[48,512]{1,0:T(8,128)(...) custom-call(bf16[816,512]{1,0:T(8,128)(2,1)S(1)} %shard_map.114.stag, ...), custom_call_target="tpu_custom_call" | custom-call | tf_op jit(solution)/shard_map/pallas_call | solution.py:305
  17.4 2.0 %collective-permute-start.8 = (bf16[48,512]{1,0:T(8,128)(2,1)S(1)}, bf16[48,512]{1,0:T(8,128)(2,1)S(1)}, u32[]{:S(2)}, u32[]{:S(2)}) collective-permute-start(bf16[48,512]{1,0:T(8,128)(2,1)S(1)} %get-tuple-element.39), channel_id=1, source_target_pairs={{0,14},{1,11},{2,12},{3,9},{4,10},{5,15},{6,8},{7,13},{8,6},{9,3},... | collective-permute-start | bytes 147464 | tf_op jit(solution)/shard_map/ppermute | solution.py:221
  19.4 0.2 collective-permute-start.9
  19.6 2.6 %collective-permute-start.10 = (bf16[48,512]{1,0:T(8,128)(2,1)S(1)}, bf16[48,512]{1,0:T(8,128)(2,1)S(1)}, u32[]{:S(2)}, u32[]{:S(2)}) collective-permute-start(bf16[48,512]{1,0:T(8,128)(2,1)S(1)} %get-tuple-element.47), channel_id=1, source_target_pairs={{0,8},{1,7},{2,10},{3,5},{4,12},{5,3},{6,14},{7,1},{8,0},{9,15},{1... | collective-permute-start | bytes 147464 | tf_op jit(solution)/shard_map/ppermute | solution.py:221
  22.2 1.1 %collective-permute-start.11 = (bf16[48,512]{1,0:T(8,128)(2,1)S(1)}, bf16[48,512]{1,0:T(8,128)(2,1)S(1)}, u32[]{:S(2)}, u32[]{:S(2)}) collective-permute-start(bf16[48,512]{1,0:T(8,128)(2,1)S(1)} %get-tuple-element.48), channel_id=1, source_target_pairs={{0,2},{1,3},{2,0},{3,1},{4,6},{5,7},{6,4},{7,5},{8,10},{9,11},{10,... | collective-permute-start | bytes 147464 | tf_op jit(solution)/shard_map/ppermute | solution.py:221
  23.3 0.0 copy-done.1
  23.3 0.8 %shard_map.116.base_ref = f32[128,2048]{1,0:T(8,128)S(1)} custom-call(bf16[256,512]{1,0:T(8,128)(2,1)S(1)} %get-tuple-element.40.kept_ref, bf16[2048,512]{1,0:T(8,128)(2,1)S(1)} %copy-done.1), custom_call_target="tpu_custom_call" | custom-call | flops 268435456 | bytes 3145728 | tf_op jit(solution)/shard_map/pallas_call | solution.py:322
  24.1 1.0 %shard_map.117 = bf16[128,2048]{1,0:T(8,128)(2,1)} custom-call(f32[128,2048]{1,0:T(8,128)S(1)} %shard_map.116.base_ref, bf16[128,32]{1,0:T(8,128)(2,1)S(1)} %get-tuple-element.41.dlow_ref, bf16[4,32,512]{2,1,0:T(8,128)(2,1)S(1)} %get-tuple-element.42.a_ref), custom_call_target="tpu_custom_call" | custom-call | flops 16777216 | bytes 1572864 | tf_op jit(solution)/shard_map/pallas_call | solution.py:334
  25.1 0.0 collective-permute-done.8.refs_1_
  25.1 0.1 collective-permute-start.12
  25.2 0.3 %collective-permute-done.9.refs_2_ = bf16[48,512]{1,0:T(8,128)(2,1)S(1)} collective-permute-done((bf16[48,512]{1,0:T(8,128)(2,1)S(1)}, bf16[48,512]{1,0:T(8,128)(2,1)S(1)}, u32[]{:S(2)}, u32[]{:S(2)}) %collective-permute-start.9) | collective-permute-done | bytes 49184 | tf_op jit(solution)/shard_map/ppermute | solution.py:221
  25.5 0.2 collective-permute-start.13
  25.7 0.4 %collective-permute-done.10.refs_3_ = bf16[48,512]{1,0:T(8,128)(2,1)S(1)} collective-permute-done((bf16[48,512]{1,0:T(8,128)(2,1)S(1)}, bf16[48,512]{1,0:T(8,128)(2,1)S(1)}, u32[]{:S(2)}, u32[]{:S(2)}) %collective-permute-start.10) | collective-permute-done | bytes 49184 | tf_op jit(solution)/shard_map/ppermute | solution.py:221
  26.0 0.1 collective-permute-start.14
  26.2 0.5 %collective-permute-done.11.refs_4_ = bf16[48,512]{1,0:T(8,128)(2,1)S(1)} collective-permute-done((bf16[48,512]{1,0:T(8,128)(2,1)S(1)}, bf16[48,512]{1,0:T(8,128)(2,1)S(1)}, u32[]{:S(2)}, u32[]{:S(2)}) %collective-permute-start.11) | collective-permute-done | bytes 49184 | tf_op jit(solution)/shard_map/ppermute | solution.py:221
  26.7 0.0 collective-permute-done.12.refs_5_
  26.7 0.0 collective-permute-done.13.refs_6_
  26.7 0.6 %collective-permute-done.14.refs_7_ = bf16[48,512]{1,0:T(8,128)(2,1)S(1)} collective-permute-done((bf16[48,512]{1,0:T(8,128)(2,1)S(1)}, bf16[48,512]{1,0:T(8,128)(2,1)S(1)}, u32[]{:S(2)}, u32[]{:S(2)}) %collective-permute-start.14) | collective-permute-done | bytes 49184 | tf_op jit(solution)/shard_map/ppermute | solution.py:230
  27.3 1.0 %shard_map.118 = (f32[512,128]{1,0:T(8,128)}, f32[16,256]{1,0:T(8,128)}) custom-call(bf16[256,512]{1,0:T(8,128)(2,1)S(1)} %get-tuple-element.40.kept_ref, bf16[48,512]{1,0:T(8,128)(2,1)S(1)} %get-tuple-element.44.refs_0_, bf16[48,512]{1,0:T(8,128)(2,1)S(1)} %collective-permute-done.8.refs_1_, bf16[48,512]{1,0:T(8,128)(2,1)S(1)} %collective-permute-done.9.refs_2_, ...), custom_call_target="tpu_custom_call" | custom-call | tf_op jit(solution)/shard_map/pallas_call | solution.py:350
Async XLA Ops:
  2.5 13.6 %collective-permute-start.1 = (bf16[64,4096]{1,0:T(8,128)(2,1)}, bf16[64,4096]{1,0:T(8,128)(2,1)S(1)}, u32[]{:S(2)}, u32[]{:S(2)}) collective-permute-start(bf16[64,4096]{1,0:T(8,128)(2,1)} %x_hbm.1), channel_id=1, source_target_pairs={{0,1},{1,0},{2,3},{3,2},{4,5},{5,4},{6,7},{7,6},{8,9},{9,8},{10,11... | collective-permute-start | bytes 1572872 | tf_op jit(solution)/shard_map/ppermute | solution.py:285
  3.0 10.2 %collective-permute-start = (bf16[48,512]{1,0:T(8,128)(2,1)}, bf16[48,512]{1,0:T(8,128)(2,1)S(1)}, u32[]{:S(2)}, u32[]{:S(2)}) collective-permute-start(bf16[48,512]{1,0:T(8,128)(2,1)} %get-tuple-element.31), channel_id=1, source_target_pairs={{0,14},{1,9},{2,12},{3,11},{4,10},{5,13},{6,8},{7,15},{8,6},{9,1},... | collective-permute-start | bytes 147464 | tf_op jit(solution)/shard_map/ppermute | solution.py:221
  8.6 5.3 %collective-permute-start.2 = (bf16[48,512]{1,0:T(8,128)(2,1)}, bf16[48,512]{1,0:T(8,128)(2,1)S(1)}, u32[]{:S(2)}, u32[]{:S(2)}) collective-permute-start(bf16[48,512]{1,0:T(8,128)(2,1)} %get-tuple-element.36), channel_id=1, source_target_pairs={{0,6},{1,11},{2,4},{3,9},{4,2},{5,15},{6,0},{7,13},{8,14},{9,3},{1... | collective-permute-start | bytes 147464 | tf_op jit(solution)/shard_map/ppermute | solution.py:221
  8.6 6.2 %collective-permute-start.3 = (bf16[48,512]{1,0:T(8,128)(2,1)}, bf16[48,512]{1,0:T(8,128)(2,1)S(1)}, u32[]{:S(2)}, u32[]{:S(2)}) collective-permute-start(bf16[48,512]{1,0:T(8,128)(2,1)} %get-tuple-element.37), channel_id=1, source_target_pairs={{0,12},{1,5},{2,14},{3,7},{4,8},{5,1},{6,10},{7,3},{8,4},{9,13},{1... | collective-permute-start | bytes 147464 | tf_op jit(solution)/shard_map/ppermute | solution.py:221
  9.5 6.6 %collective-permute-start.4 = (bf16[48,512]{1,0:T(8,128)(2,1)}, bf16[48,512]{1,0:T(8,128)(2,1)S(1)}, u32[]{:S(2)}, u32[]{:S(2)}) collective-permute-start(bf16[48,512]{1,0:T(8,128)(2,1)} %get-tuple-element.38), channel_id=1, source_target_pairs={{0,2},{1,3},{2,0},{3,1},{4,6},{5,7},{6,4},{7,5},{8,10},{9,11},{10,... | collective-permute-start | bytes 147464 | tf_op jit(solution)/shard_map/ppermute | solution.py:221
  13.2 2.9 %collective-permute-start.5 = (bf16[48,512]{1,0:T(8,128)(2,1)S(1)}, bf16[48,512]{1,0:T(8,128)(2,1)S(1)}, u32[]{:S(2)}, u32[]{:S(2)}) collective-permute-start(bf16[48,512]{1,0:T(8,128)(2,1)S(1)} %collective-permute-done.refs_0_), channel_id=1, source_target_pairs={{0,1},{1,0},{2,3},{3,2},{4,5},{5,4},{6,7},{7,6},{8,9},{9,8},{10,11... | collective-permute-start | bytes 147464 | tf_op jit(solution)/shard_map/ppermute | solution.py:230
  13.9 2.1 %collective-permute-start.6 = (bf16[48,512]{1,0:T(8,128)(2,1)S(1)}, bf16[48,512]{1,0:T(8,128)(2,1)S(1)}, u32[]{:S(2)}, u32[]{:S(2)}) collective-permute-start(bf16[48,512]{1,0:T(8,128)(2,1)S(1)} %collective-permute-done.2.refs_1_), channel_id=1, source_target_pairs={{0,1},{1,0},{2,3},{3,2},{4,5},{5,4},{6,7},{7,6},{8,9},{9,8},{10,11... | collective-permute-start | bytes 147464 | tf_op jit(solution)/shard_map/ppermute | solution.py:230
  14.8 1.2 %collective-permute-start.7 = (bf16[48,512]{1,0:T(8,128)(2,1)S(1)}, bf16[48,512]{1,0:T(8,128)(2,1)S(1)}, u32[]{:S(2)}, u32[]{:S(2)}) collective-permute-start(bf16[48,512]{1,0:T(8,128)(2,1)S(1)} %collective-permute-done.3.refs_2_), channel_id=1, source_target_pairs={{0,1},{1,0},{2,3},{3,2},{4,5},{5,4},{6,7},{7,6},{8,9},{9,8},{10,11... | collective-permute-start | bytes 147464 | tf_op jit(solution)/shard_map/ppermute | solution.py:230
  14.8 1.2 %copy-start = (bf16[816,512]{1,0:T(8,128)(2,1)S(1)}, bf16[816,512]{1,0:T(8,128)(2,1)}, u32[]{:S(2)}) copy-start(bf16[816,512]{1,0:T(8,128)(2,1)} %shard_map.113.stage) | copy-start | bytes 2506756
  16.0 7.3 %copy-start.1 = (bf16[2048,512]{1,0:T(8,128)(2,1)S(1)}, bf16[2048,512]{1,0:T(8,128)(2,1)}, u32[]{:S(2)}) copy-start(bf16[2048,512]{1,0:T(8,128)(2,1)} %w_ref.1) | copy-start | bytes 6291460
  17.4 7.7 %collective-permute-start.8 = (bf16[48,512]{1,0:T(8,128)(2,1)S(1)}, bf16[48,512]{1,0:T(8,128)(2,1)S(1)}, u32[]{:S(2)}, u32[]{:S(2)}) collective-permute-start(bf16[48,512]{1,0:T(8,128)(2,1)S(1)} %get-tuple-element.39), channel_id=1, source_target_pairs={{0,14},{1,11},{2,12},{3,9},{4,10},{5,15},{6,8},{7,13},{8,6},{9,3},... | collective-permute-start | bytes 147464 | tf_op jit(solution)/shard_map/ppermute | solution.py:221
  19.4 6.1 %collective-permute-start.9 = (bf16[48,512]{1,0:T(8,128)(2,1)S(1)}, bf16[48,512]{1,0:T(8,128)(2,1)S(1)}, u32[]{:S(2)}, u32[]{:S(2)}) collective-permute-start(bf16[48,512]{1,0:T(8,128)(2,1)S(1)} %get-tuple-element.46), channel_id=1, source_target_pairs={{0,4},{1,13},{2,6},{3,15},{4,0},{5,9},{6,2},{7,11},{8,12},{9,5},{1... | collective-permute-start | bytes 147464 | tf_op jit(solution)/shard_map/ppermute | solution.py:221
  19.6 6.5 %collective-permute-start.10 = (bf16[48,512]{1,0:T(8,128)(2,1)S(1)}, bf16[48,512]{1,0:T(8,128)(2,1)S(1)}, u32[]{:S(2)}, u32[]{:S(2)}) collective-permute-start(bf16[48,512]{1,0:T(8,128)(2,1)S(1)} %get-tuple-element.47), channel_id=1, source_target_pairs={{0,8},{1,7},{2,10},{3,5},{4,12},{5,3},{6,14},{7,1},{8,0},{9,15},{1... | collective-permute-start | bytes 147464 | tf_op jit(solution)/shard_map/ppermute | solution.py:221
  22.2 4.5 %collective-permute-start.11 = (bf16[48,512]{1,0:T(8,128)(2,1)S(1)}, bf16[48,512]{1,0:T(8,128)(2,1)S(1)}, u32[]{:S(2)}, u32[]{:S(2)}) collective-permute-start(bf16[48,512]{1,0:T(8,128)(2,1)S(1)} %get-tuple-element.48), channel_id=1, source_target_pairs={{0,2},{1,3},{2,0},{3,1},{4,6},{5,7},{6,4},{7,5},{8,10},{9,11},{10,... | collective-permute-start | bytes 147464 | tf_op jit(solution)/shard_map/ppermute | solution.py:221
  25.1 1.6 %collective-permute-start.12 = (bf16[48,512]{1,0:T(8,128)(2,1)S(1)}, bf16[48,512]{1,0:T(8,128)(2,1)S(1)}, u32[]{:S(2)}, u32[]{:S(2)}) collective-permute-start(bf16[48,512]{1,0:T(8,128)(2,1)S(1)} %collective-permute-done.8.refs_1_), channel_id=1, source_target_pairs={{0,1},{1,0},{2,3},{3,2},{4,5},{5,4},{6,7},{7,6},{8,9},{9,8},{10,11... | collective-permute-start | bytes 147464 | tf_op jit(solution)/shard_map/ppermute | solution.py:230
  25.5 1.2 %collective-permute-start.13 = (bf16[48,512]{1,0:T(8,128)(2,1)S(1)}, bf16[48,512]{1,0:T(8,128)(2,1)S(1)}, u32[]{:S(2)}, u32[]{:S(2)}) collective-permute-start(bf16[48,512]{1,0:T(8,128)(2,1)S(1)} %collective-permute-done.9.refs_2_), channel_id=1, source_target_pairs={{0,1},{1,0},{2,3},{3,2},{4,5},{5,4},{6,7},{7,6},{8,9},{9,8},{10,11... | collective-permute-start | bytes 147464 | tf_op jit(solution)/shard_map/ppermute | solution.py:230
  26.0 1.2 %collective-permute-start.14 = (bf16[48,512]{1,0:T(8,128)(2,1)S(1)}, bf16[48,512]{1,0:T(8,128)(2,1)S(1)}, u32[]{:S(2)}, u32[]{:S(2)}) collective-permute-start(bf16[48,512]{1,0:T(8,128)(2,1)S(1)} %collective-permute-done.10.refs_3_), channel_id=1, source_target_pairs={{0,1},{1,0},{2,3},{3,2},{4,5},{5,4},{6,7},{7,6},{8,9},{9,8},{10,11... | collective-permute-start | bytes 147464 | tf_op jit(solution)/shard_map/ppermute | solution.py:230

commit v15 on v11

--- a/solution.py
+++ b/solution.py
@@ -53,7 +53,7 @@
 def steps(n, turn):
     half = n // 2
     if turn == 0:
-        return [(half, half + 1), (n - 1, n - 2), (2, 3), (1, 1)]
+        return [(half + 1, 3), (n - 1, n - 2), (1, 1), (2, half)]
     return [(n - 1, half + 1), (3, n - 2), (2, half), (1, 1)]
 
 

time: 28.5 us -> 28.9 us (1.014)
  starting transfers between devices: 14.8 us -> 15.3 us
    ppermute x8, starting transfers between devices: 13 us -> 13.7 us  [exchange(): lax.ppermute(message, ('dp', 'tensor'), [(2 * i + c, 2 * (i ^ step[c]) +...]
  transfers between devices with their start and end apart: 15 -> 15, of which waited for: 7 -> 5; matrix products, arithmetic and copies ran while one was open for 0% -> 0% of each run, Pallas kernels for 14% -> 14%
where the time goes in v15:
time: 28.9 us; the launch traced here: 28.7 us
  starting transfers between devices  15.3 us (53%)
  Pallas kernels  8.17 us (28%)
  waiting for transfers between devices  3.31 us (11%)
  local copies, waits for them, and re-layouts  1.15 us (4%)
  between operations  0.76 us (3%)
    ppermute x8, starting transfers between devices, exchange(): lax.ppermute(message, ('dp', 'tensor'), [(2 * i + c, 2 * (i ^ step[c]) +...  13.7 us
    ppermute x8, waiting for transfers between devices, exchange(): lax.ppermute(message, ('dp', 'tensor'), [(2 * i + c, 2 * (i ^ step[c]) +...  2.29 us
    pallas_call x1, Pallas kernels, local_kernels(): pl.pallas_call(functools.partial(stage_kernel, n, lay), out_shape=shape(l...  2.17 us
    pallas_call x1, Pallas kernels, local_kernels(): pl.pallas_call(functools.partial(pack_kernel, n), out_shape=[message] * c...  1.87 us
    pallas_call x1, Pallas kernels, local_kernels(): pl.pallas_call(functools.partial(middle_kernel, n, lay), out_shape=[shape...  1.26 us
    ppermute x6, starting transfers between devices, exchange(): lax.ppermute(message, 'tensor', [(0, 1), (1, 0)])  1.16 us
    unnamed x4, local copies, waits for them, and re-layouts  1.15 us
    ppermute x6, waiting for transfers between devices, exchange(): lax.ppermute(message, 'tensor', [(0, 1), (1, 0)])  1.02 us
  transfers between devices with their start and end apart: 15, of which 5 were waited for; matrix products, arithmetic and copies ran while one was open for 0% of the time, Pallas kernels for 14%

profile of v15, /device:TPU:0, one launch (start us, length us, event | category | flops | bytes accessed | tf_op | source)
XLA Modules:
  0.0 28.7 jit_solution(5825153317500955653)
XLA Ops:
  0.6 1.9 %shard_map.112 = (bf16[48,512]{1,0:T(8,128)(2,1)}, bf16[48,512]{1,0:T(8,128)(2,1)}, bf16[48,512]{1,0:T(8,128)(2,1)}, bf16[48,512]{1,0:T(8,128)(2,1)}, bf16[48,512]{1,0:T(8,128)(2,1)}) custom-call(s32[2,8]{1,0:T(2,128)} %bitcast.2, s32[8]{0:T(128)} %slot_hbm.3, bf16[512,128]{1,0:T(8,128)(2,1)} %down_hbm.1, bf16[16,512]{1,0:T(8,128)(2,1)} %up_hbm.1), custom_call_target="tpu_custom_call" | custom-call | tf_op jit(solution)/shard_map/pallas_call | solution.py:270
  2.5 0.5 %collective-permute-start.1 = (bf16[64,4096]{1,0:T(8,128)(2,1)}, bf16[64,4096]{1,0:T(8,128)(2,1)S(1)}, u32[]{:S(2)}, u32[]{:S(2)}) collective-permute-start(bf16[64,4096]{1,0:T(8,128)(2,1)} %x_hbm.1), channel_id=1, source_target_pairs={{0,1},{1,0},{2,3},{3,2},{4,5},{5,4},{6,7},{7,6},{8,9},{9,8},{10,11... | collective-permute-start | bytes 1572872 | tf_op jit(solution)/shard_map/ppermute | solution.py:285
  3.0 4.6 %collective-permute-start = (bf16[48,512]{1,0:T(8,128)(2,1)}, bf16[48,512]{1,0:T(8,128)(2,1)S(1)}, u32[]{:S(2)}, u32[]{:S(2)}) collective-permute-start(bf16[48,512]{1,0:T(8,128)(2,1)} %get-tuple-element.31), channel_id=1, source_target_pairs={{0,10},{1,7},{2,8},{3,5},{4,14},{5,3},{6,12},{7,1},{8,2},{9,15},{1... | collective-permute-start | bytes 147464 | tf_op jit(solution)/shard_map/ppermute | solution.py:221
  7.6 1.3 %collective-permute-start.2 = (bf16[48,512]{1,0:T(8,128)(2,1)}, bf16[48,512]{1,0:T(8,128)(2,1)S(1)}, u32[]{:S(2)}, u32[]{:S(2)}) collective-permute-start(bf16[48,512]{1,0:T(8,128)(2,1)} %get-tuple-element.36), channel_id=1, source_target_pairs={{0,14},{1,13},{2,12},{3,15},{4,10},{5,9},{6,8},{7,11},{8,6},{9,5},... | collective-permute-start | bytes 147464 | tf_op jit(solution)/shard_map/ppermute | solution.py:221
  8.9 0.3 collective-permute-start.4
  9.2 1.2 %collective-permute-start.3 = (bf16[48,512]{1,0:T(8,128)(2,1)}, bf16[48,512]{1,0:T(8,128)(2,1)S(1)}, u32[]{:S(2)}, u32[]{:S(2)}) collective-permute-start(bf16[48,512]{1,0:T(8,128)(2,1)} %get-tuple-element.37), channel_id=1, source_target_pairs={{0,2},{1,3},{2,0},{3,1},{4,6},{5,7},{6,4},{7,5},{8,10},{9,11},{10,... | collective-permute-start | bytes 147464 | tf_op jit(solution)/shard_map/ppermute | solution.py:221
  10.4 2.2 %shard_map.113.stage = bf16[816,512]{1,0:T(8,128)(2,1)} custom-call(s32[2,8]{1,0:T(2,128)} %bitcast.4, s32[2,8]{1,0:T(2,128)} %bitcast.3, s32[8]{0:T(128)} %slot_hbm.3, s32[8]{0:T(128)} %count_hbm.1, bf16[128,512]{1,0:T(8,128)(2,1)} %g_hbm.1, bf16[64,4096]{1,0:T(8,128)(2,1)} %x_hbm.1, bf16[48,512]{1,0:T(8,128)(2,1)} %get-tuple-element.32.own_hbm), custom_call_target="tpu_custom_call" | custom-call | bytes 2097152 | tf_op jit(solution)/shard_map/pallas_call | solution.py:286
  12.6 0.0 collective-permute-done.refs_0_
  12.6 0.1 collective-permute-start.5
  12.7 2.1 %collective-permute-done.2.refs_1_ = bf16[48,512]{1,0:T(8,128)(2,1)S(1)} collective-permute-done((bf16[48,512]{1,0:T(8,128)(2,1)}, bf16[48,512]{1,0:T(8,128)(2,1)S(1)}, u32[]{:S(2)}, u32[]{:S(2)}) %collective-permute-start.2) | collective-permute-done | bytes 49184 | tf_op jit(solution)/shard_map/ppermute | solution.py:221
  14.8 0.0 collective-permute-start.6
  14.8 0.0 collective-permute-done.4.refs_3_
  14.8 0.5 %collective-permute-start.7 = (bf16[48,512]{1,0:T(8,128)(2,1)S(1)}, bf16[48,512]{1,0:T(8,128)(2,1)S(1)}, u32[]{:S(2)}, u32[]{:S(2)}) collective-permute-start(bf16[48,512]{1,0:T(8,128)(2,1)S(1)} %collective-permute-done.4.refs_3_), channel_id=1, source_target_pairs={{0,1},{1,0},{2,3},{3,2},{4,5},{5,4},{6,7},{7,6},{8,9},{9,8},{10,11... | collective-permute-start | bytes 147464 | tf_op jit(solution)/shard_map/ppermute | solution.py:230
  15.3 0.0 copy-start
  15.3 1.1 %copy-done = bf16[816,512]{1,0:T(8,128)(2,1)S(1)} copy-done((bf16[816,512]{1,0:T(8,128)(2,1)S(1)}, bf16[816,512]{1,0:T(8,128)(2,1)}, u32[]{:S(2)}) %copy-start) | copy-done | bytes 835608
  16.4 0.0 copy-start.1
  16.4 0.1 shard_map.114.stage
  16.5 0.0 collective-permute-done.3.refs_2_
  16.5 0.0 collective-permute-done.5.refs_4_
  16.5 0.0 collective-permute-done.6.refs_5_
  16.5 0.0 collective-permute-done.7.refs_6_
  16.5 0.0 collective-permute-done.1.x_other
  16.6 1.3 %shard_map.115 = (bf16[128,32]{1,0:T(8,128)(2,1)S(1)}, bf16[4,32,512]{2,1,0:T(8,128)(2,1)S(1)}, bf16[256,512]{1,0:T(8,128)(2,1)S(1)}, bf16[48,512]{1,0:T(8,128)(...) custom-call(bf16[816,512]{1,0:T(8,128)(2,1)S(1)} %shard_map.114.stag, ...), custom_call_target="tpu_custom_call" | custom-call | tf_op jit(solution)/shard_map/pallas_call | solution.py:305
  17.8 2.8 %collective-permute-start.8 = (bf16[48,512]{1,0:T(8,128)(2,1)S(1)}, bf16[48,512]{1,0:T(8,128)(2,1)S(1)}, u32[]{:S(2)}, u32[]{:S(2)}) collective-permute-start(bf16[48,512]{1,0:T(8,128)(2,1)S(1)} %get-tuple-element.39), channel_id=1, source_target_pairs={{0,14},{1,11},{2,12},{3,9},{4,10},{5,15},{6,8},{7,13},{8,6},{9,3},... | collective-permute-start | bytes 147464 | tf_op jit(solution)/shard_map/ppermute | solution.py:221
  20.6 0.4 %collective-permute-start.9 = (bf16[48,512]{1,0:T(8,128)(2,1)S(1)}, bf16[48,512]{1,0:T(8,128)(2,1)S(1)}, u32[]{:S(2)}, u32[]{:S(2)}) collective-permute-start(bf16[48,512]{1,0:T(8,128)(2,1)S(1)} %get-tuple-element.46), channel_id=1, source_target_pairs={{0,6},{1,13},{2,4},{3,15},{4,2},{5,9},{6,0},{7,11},{8,14},{9,5},{1... | collective-permute-start | bytes 147464 | tf_op jit(solution)/shard_map/ppermute | solution.py:221
  21.0 1.5 %collective-permute-start.10 = (bf16[48,512]{1,0:T(8,128)(2,1)S(1)}, bf16[48,512]{1,0:T(8,128)(2,1)S(1)}, u32[]{:S(2)}, u32[]{:S(2)}) collective-permute-start(bf16[48,512]{1,0:T(8,128)(2,1)S(1)} %get-tuple-element.47), channel_id=1, source_target_pairs={{0,4},{1,9},{2,6},{3,11},{4,0},{5,13},{6,2},{7,15},{8,12},{9,1},{1... | collective-permute-start | bytes 147464 | tf_op jit(solution)/shard_map/ppermute | solution.py:221
  22.6 1.5 %collective-permute-start.11 = (bf16[48,512]{1,0:T(8,128)(2,1)S(1)}, bf16[48,512]{1,0:T(8,128)(2,1)S(1)}, u32[]{:S(2)}, u32[]{:S(2)}) collective-permute-start(bf16[48,512]{1,0:T(8,128)(2,1)S(1)} %get-tuple-element.48), channel_id=1, source_target_pairs={{0,2},{1,3},{2,0},{3,1},{4,6},{5,7},{6,4},{7,5},{8,10},{9,11},{10,... | collective-permute-start | bytes 147464 | tf_op jit(solution)/shard_map/ppermute | solution.py:221
  24.1 0.0 copy-done.1
  24.1 0.8 %shard_map.116.base_ref = f32[128,2048]{1,0:T(8,128)S(1)} custom-call(bf16[256,512]{1,0:T(8,128)(2,1)S(1)} %get-tuple-element.40.kept_ref, bf16[2048,512]{1,0:T(8,128)(2,1)S(1)} %copy-done.1), custom_call_target="tpu_custom_call" | custom-call | flops 268435456 | bytes 3145728 | tf_op jit(solution)/shard_map/pallas_call | solution.py:322
  24.9 1.0 %shard_map.117 = bf16[128,2048]{1,0:T(8,128)(2,1)} custom-call(f32[128,2048]{1,0:T(8,128)S(1)} %shard_map.116.base_ref, bf16[128,32]{1,0:T(8,128)(2,1)S(1)} %get-tuple-element.41.dlow_ref, bf16[4,32,512]{2,1,0:T(8,128)(2,1)S(1)} %get-tuple-element.42.a_ref), custom_call_target="tpu_custom_call" | custom-call | flops 16777216 | bytes 1572864 | tf_op jit(solution)/shard_map/pallas_call | solution.py:334
  25.9 0.0 collective-permute-done.8.refs_1_
  25.9 0.1 collective-permute-start.12
  26.0 0.2 collective-permute-done.9.refs_2_
  26.2 0.3 %collective-permute-start.13 = (bf16[48,512]{1,0:T(8,128)(2,1)S(1)}, bf16[48,512]{1,0:T(8,128)(2,1)S(1)}, u32[]{:S(2)}, u32[]{:S(2)}) collective-permute-start(bf16[48,512]{1,0:T(8,128)(2,1)S(1)} %collective-permute-done.9.refs_2_), channel_id=1, source_target_pairs={{0,1},{1,0},{2,3},{3,2},{4,5},{5,4},{6,7},{7,6},{8,9},{9,8},{10,11... | collective-permute-start | bytes 147464 | tf_op jit(solution)/shard_map/ppermute | solution.py:230
  26.5 0.0 collective-permute-done.10.refs_3_
  26.5 0.2 collective-permute-start.14
  26.7 0.0 collective-permute-done.11.refs_4_
  26.7 0.5 %collective-permute-done.12.refs_5_ = bf16[48,512]{1,0:T(8,128)(2,1)S(1)} collective-permute-done((bf16[48,512]{1,0:T(8,128)(2,1)S(1)}, bf16[48,512]{1,0:T(8,128)(2,1)S(1)}, u32[]{:S(2)}, u32[]{:S(2)}) %collective-permute-start.12) | collective-permute-done | bytes 49184 | tf_op jit(solution)/shard_map/ppermute | solution.py:230
  27.2 0.2 collective-permute-done.13.refs_6_
  27.4 0.3 %collective-permute-done.14.refs_7_ = bf16[48,512]{1,0:T(8,128)(2,1)S(1)} collective-permute-done((bf16[48,512]{1,0:T(8,128)(2,1)S(1)}, bf16[48,512]{1,0:T(8,128)(2,1)S(1)}, u32[]{:S(2)}, u32[]{:S(2)}) %collective-permute-start.14) | collective-permute-done | bytes 49184 | tf_op jit(solution)/shard_map/ppermute | solution.py:230
  27.7 1.0 %shard_map.118 = (f32[512,128]{1,0:T(8,128)}, f32[16,256]{1,0:T(8,128)}) custom-call(bf16[256,512]{1,0:T(8,128)(2,1)S(1)} %get-tuple-element.40.kept_ref, bf16[48,512]{1,0:T(8,128)(2,1)S(1)} %get-tuple-element.44.refs_0_, bf16[48,512]{1,0:T(8,128)(2,1)S(1)} %collective-permute-done.8.refs_1_, bf16[48,512]{1,0:T(8,128)(2,1)S(1)} %collective-permute-done.9.refs_2_, ...), custom_call_target="tpu_custom_call" | custom-call | tf_op jit(solution)/shard_map/pallas_call | solution.py:350
Async XLA Ops:
  2.5 14.0 %collective-permute-start.1 = (bf16[64,4096]{1,0:T(8,128)(2,1)}, bf16[64,4096]{1,0:T(8,128)(2,1)S(1)}, u32[]{:S(2)}, u32[]{:S(2)}) collective-permute-start(bf16[64,4096]{1,0:T(8,128)(2,1)} %x_hbm.1), channel_id=1, source_target_pairs={{0,1},{1,0},{2,3},{3,2},{4,5},{5,4},{6,7},{7,6},{8,9},{9,8},{10,11... | collective-permute-start | bytes 1572872 | tf_op jit(solution)/shard_map/ppermute | solution.py:285
  3.0 9.6 %collective-permute-start = (bf16[48,512]{1,0:T(8,128)(2,1)}, bf16[48,512]{1,0:T(8,128)(2,1)S(1)}, u32[]{:S(2)}, u32[]{:S(2)}) collective-permute-start(bf16[48,512]{1,0:T(8,128)(2,1)} %get-tuple-element.31), channel_id=1, source_target_pairs={{0,10},{1,7},{2,8},{3,5},{4,14},{5,3},{6,12},{7,1},{8,2},{9,15},{1... | collective-permute-start | bytes 147464 | tf_op jit(solution)/shard_map/ppermute | solution.py:221
  7.6 7.2 %collective-permute-start.2 = (bf16[48,512]{1,0:T(8,128)(2,1)}, bf16[48,512]{1,0:T(8,128)(2,1)S(1)}, u32[]{:S(2)}, u32[]{:S(2)}) collective-permute-start(bf16[48,512]{1,0:T(8,128)(2,1)} %get-tuple-element.36), channel_id=1, source_target_pairs={{0,14},{1,13},{2,12},{3,15},{4,10},{5,9},{6,8},{7,11},{8,6},{9,5},... | collective-permute-start | bytes 147464 | tf_op jit(solution)/shard_map/ppermute | solution.py:221
  8.9 5.8 %collective-permute-start.4 = (bf16[48,512]{1,0:T(8,128)(2,1)}, bf16[48,512]{1,0:T(8,128)(2,1)S(1)}, u32[]{:S(2)}, u32[]{:S(2)}) collective-permute-start(bf16[48,512]{1,0:T(8,128)(2,1)} %get-tuple-element.38), channel_id=1, source_target_pairs={{0,4},{1,9},{2,6},{3,11},{4,0},{5,13},{6,2},{7,15},{8,12},{9,1},{1... | collective-permute-start | bytes 147464 | tf_op jit(solution)/shard_map/ppermute | solution.py:221
  9.2 7.3 %collective-permute-start.3 = (bf16[48,512]{1,0:T(8,128)(2,1)}, bf16[48,512]{1,0:T(8,128)(2,1)S(1)}, u32[]{:S(2)}, u32[]{:S(2)}) collective-permute-start(bf16[48,512]{1,0:T(8,128)(2,1)} %get-tuple-element.37), channel_id=1, source_target_pairs={{0,2},{1,3},{2,0},{3,1},{4,6},{5,7},{6,4},{7,5},{8,10},{9,11},{10,... | collective-permute-start | bytes 147464 | tf_op jit(solution)/shard_map/ppermute | solution.py:221
  12.6 3.9 %collective-permute-start.5 = (bf16[48,512]{1,0:T(8,128)(2,1)S(1)}, bf16[48,512]{1,0:T(8,128)(2,1)S(1)}, u32[]{:S(2)}, u32[]{:S(2)}) collective-permute-start(bf16[48,512]{1,0:T(8,128)(2,1)S(1)} %collective-permute-done.refs_0_), channel_id=1, source_target_pairs={{0,1},{1,0},{2,3},{3,2},{4,5},{5,4},{6,7},{7,6},{8,9},{9,8},{10,11... | collective-permute-start | bytes 147464 | tf_op jit(solution)/shard_map/ppermute | solution.py:230
  14.8 1.7 %collective-permute-start.6 = (bf16[48,512]{1,0:T(8,128)(2,1)S(1)}, bf16[48,512]{1,0:T(8,128)(2,1)S(1)}, u32[]{:S(2)}, u32[]{:S(2)}) collective-permute-start(bf16[48,512]{1,0:T(8,128)(2,1)S(1)} %collective-permute-done.2.refs_1_), channel_id=1, source_target_pairs={{0,1},{1,0},{2,3},{3,2},{4,5},{5,4},{6,7},{7,6},{8,9},{9,8},{10,11... | collective-permute-start | bytes 147464 | tf_op jit(solution)/shard_map/ppermute | solution.py:230
  14.8 1.8 %collective-permute-start.7 = (bf16[48,512]{1,0:T(8,128)(2,1)S(1)}, bf16[48,512]{1,0:T(8,128)(2,1)S(1)}, u32[]{:S(2)}, u32[]{:S(2)}) collective-permute-start(bf16[48,512]{1,0:T(8,128)(2,1)S(1)} %collective-permute-done.4.refs_3_), channel_id=1, source_target_pairs={{0,1},{1,0},{2,3},{3,2},{4,5},{5,4},{6,7},{7,6},{8,9},{9,8},{10,11... | collective-permute-start | bytes 147464 | tf_op jit(solution)/shard_map/ppermute | solution.py:230
  15.3 1.1 %copy-start = (bf16[816,512]{1,0:T(8,128)(2,1)S(1)}, bf16[816,512]{1,0:T(8,128)(2,1)}, u32[]{:S(2)}) copy-start(bf16[816,512]{1,0:T(8,128)(2,1)} %shard_map.113.stage) | copy-start | bytes 2506756
  16.4 7.6 %copy-start.1 = (bf16[2048,512]{1,0:T(8,128)(2,1)S(1)}, bf16[2048,512]{1,0:T(8,128)(2,1)}, u32[]{:S(2)}) copy-start(bf16[2048,512]{1,0:T(8,128)(2,1)} %w_ref.1) | copy-start | bytes 6291460
  17.8 8.1 %collective-permute-start.8 = (bf16[48,512]{1,0:T(8,128)(2,1)S(1)}, bf16[48,512]{1,0:T(8,128)(2,1)S(1)}, u32[]{:S(2)}, u32[]{:S(2)}) collective-permute-start(bf16[48,512]{1,0:T(8,128)(2,1)S(1)} %get-tuple-element.39), channel_id=1, source_target_pairs={{0,14},{1,11},{2,12},{3,9},{4,10},{5,15},{6,8},{7,13},{8,6},{9,3},... | collective-permute-start | bytes 147464 | tf_op jit(solution)/shard_map/ppermute | solution.py:221
  20.6 5.6 %collective-permute-start.9 = (bf16[48,512]{1,0:T(8,128)(2,1)S(1)}, bf16[48,512]{1,0:T(8,128)(2,1)S(1)}, u32[]{:S(2)}, u32[]{:S(2)}) collective-permute-start(bf16[48,512]{1,0:T(8,128)(2,1)S(1)} %get-tuple-element.46), channel_id=1, source_target_pairs={{0,6},{1,13},{2,4},{3,15},{4,2},{5,9},{6,0},{7,11},{8,14},{9,5},{1... | collective-permute-start | bytes 147464 | tf_op jit(solution)/shard_map/ppermute | solution.py:221
  21.0 5.5 %collective-permute-start.10 = (bf16[48,512]{1,0:T(8,128)(2,1)S(1)}, bf16[48,512]{1,0:T(8,128)(2,1)S(1)}, u32[]{:S(2)}, u32[]{:S(2)}) collective-permute-start(bf16[48,512]{1,0:T(8,128)(2,1)S(1)} %get-tuple-element.47), channel_id=1, source_target_pairs={{0,4},{1,9},{2,6},{3,11},{4,0},{5,13},{6,2},{7,15},{8,12},{9,1},{1... | collective-permute-start | bytes 147464 | tf_op jit(solution)/shard_map/ppermute | solution.py:221
  22.6 4.1 %collective-permute-start.11 = (bf16[48,512]{1,0:T(8,128)(2,1)S(1)}, bf16[48,512]{1,0:T(8,128)(2,1)S(1)}, u32[]{:S(2)}, u32[]{:S(2)}) collective-permute-start(bf16[48,512]{1,0:T(8,128)(2,1)S(1)} %get-tuple-element.48), channel_id=1, source_target_pairs={{0,2},{1,3},{2,0},{3,1},{4,6},{5,7},{6,4},{7,5},{8,10},{9,11},{10,... | collective-permute-start | bytes 147464 | tf_op jit(solution)/shard_map/ppermute | solution.py:221
  25.9 1.3 %collective-permute-start.12 = (bf16[48,512]{1,0:T(8,128)(2,1)S(1)}, bf16[48,512]{1,0:T(8,128)(2,1)S(1)}, u32[]{:S(2)}, u32[]{:S(2)}) collective-permute-start(bf16[48,512]{1,0:T(8,128)(2,1)S(1)} %collective-permute-done.8.refs_1_), channel_id=1, source_target_pairs={{0,1},{1,0},{2,3},{3,2},{4,5},{5,4},{6,7},{7,6},{8,9},{9,8},{10,11... | collective-permute-start | bytes 147464 | tf_op jit(solution)/shard_map/ppermute | solution.py:230
  26.2 1.2 %collective-permute-start.13 = (bf16[48,512]{1,0:T(8,128)(2,1)S(1)}, bf16[48,512]{1,0:T(8,128)(2,1)S(1)}, u32[]{:S(2)}, u32[]{:S(2)}) collective-permute-start(bf16[48,512]{1,0:T(8,128)(2,1)S(1)} %collective-permute-done.9.refs_2_), channel_id=1, source_target_pairs={{0,1},{1,0},{2,3},{3,2},{4,5},{5,4},{6,7},{7,6},{8,9},{9,8},{10,11... | collective-permute-start | bytes 147464 | tf_op jit(solution)/shard_map/ppermute | solution.py:230
  26.5 1.2 %collective-permute-start.14 = (bf16[48,512]{1,0:T(8,128)(2,1)S(1)}, bf16[48,512]{1,0:T(8,128)(2,1)S(1)}, u32[]{:S(2)}, u32[]{:S(2)}) collective-permute-start(bf16[48,512]{1,0:T(8,128)(2,1)S(1)} %collective-permute-done.10.refs_3_), channel_id=1, source_target_pairs={{0,1},{1,0},{2,3},{3,2},{4,5},{5,4},{6,7},{7,6},{8,9},{9,8},{10,11... | collective-permute-start | bytes 147464 | tf_op jit(solution)/shard_map/ppermute | solution.py:230

commit v16 on v11

--- a/solution.py
+++ b/solution.py
@@ -292,7 +292,6 @@
         compiler_params=params(56),
         cost_estimate=pl.CostEstimate(flops=0, bytes_accessed=1 << 21, transcendentals=0),
     )(starts, chosen, adapter_slot, token_count, output_gradient, inputs, own)
-    got, stage = exchange(sent, 0, stage)
     stage = pl.pallas_call(
         hand_on_kernel,
         out_shape=shape(lay.shape, bf16),
@@ -301,6 +300,7 @@
         compiler_params=params(8),
         cost_estimate=pl.CostEstimate(flops=0, bytes_accessed=1 << 21, transcendentals=0),
     )(stage)
+    got, stage = exchange(sent, 0, stage)
 
     dlow, a_half, kept, own, *sent = pl.pallas_call(
         functools.partial(middle_kernel, n, lay),

time: 28.5 us -> 28.6 us (level)
  starting transfers between devices: 14.8 us -> 15.9 us
  waiting for transfers between devices: 3.38 us -> 2.54 us
    ppermute x8, waiting for transfers between devices: 2.39 us -> 0.78 us  [exchange(): lax.ppermute(message, ('dp', 'tensor'), [(2 * i + c, 2 * (i ^ step[c]) +...]
    ppermute x8, starting transfers between devices: 13 us -> 13.9 us  [exchange(): lax.ppermute(message, ('dp', 'tensor'), [(2 * i + c, 2 * (i ^ step[c]) +...]
    ppermute x6, waiting for transfers between devices: 0.99 us -> 1.75 us  [exchange(): lax.ppermute(message, 'tensor', [(0, 1), (1, 0)])]
  transfers between devices with their start and end apart: 15 -> 15, of which waited for: 7 -> 9; matrix products, arithmetic and copies ran while one was open for 0% -> 0% of each run, Pallas kernels for 14% -> 14%
where the time goes in v16:
time: 28.6 us; the launch traced here: 28.4 us
  starting transfers between devices  15.9 us (56%)
  Pallas kernels  8.16 us (29%)
  waiting for transfers between devices  2.54 us (9%)
  local copies, waits for them, and re-layouts  1.15 us (4%)
  between operations  0.72 us (3%)
    ppermute x8, starting transfers between devices, exchange(): lax.ppermute(message, ('dp', 'tensor'), [(2 * i + c, 2 * (i ^ step[c]) +...  13.9 us
    pallas_call x1, Pallas kernels, local_kernels(): pl.pallas_call(functools.partial(stage_kernel, n, lay), out_shape=shape(l...  2.17 us
    pallas_call x1, Pallas kernels, local_kernels(): pl.pallas_call(functools.partial(pack_kernel, n), out_shape=[message] * c...  1.87 us
    ppermute x6, waiting for transfers between devices, exchange(): lax.ppermute(message, 'tensor', [(0, 1), (1, 0)])  1.75 us
    ppermute x6, starting transfers between devices, exchange(): lax.ppermute(message, 'tensor', [(0, 1), (1, 0)])  1.5 us
    pallas_call x1, Pallas kernels, local_kernels(): pl.pallas_call(functools.partial(middle_kernel, n, lay), out_shape=[shape...  1.26 us
    unnamed x4, local copies, waits for them, and re-layouts  1.15 us
    pallas_call x1, Pallas kernels, local_kernels(): pl.pallas_call(functools.partial(final_kernel, n, lay), out_shape=[shape(...  1.01 us
  transfers between devices with their start and end apart: 15, of which 9 were waited for; matrix products, arithmetic and copies ran while one was open for 0% of the time, Pallas kernels for 14%

profile of v16, /device:TPU:0, one launch (start us, length us, event | category | flops | bytes accessed | tf_op | source)
XLA Modules:
  0.0 28.4 jit_solution(11161916275765408145)
XLA Ops:
  0.6 1.9 %shard_map.112 = (bf16[48,512]{1,0:T(8,128)(2,1)}, bf16[48,512]{1,0:T(8,128)(2,1)}, bf16[48,512]{1,0:T(8,128)(2,1)}, bf16[48,512]{1,0:T(8,128)(2,1)}, bf16[48,512]{1,0:T(8,128)(2,1)}) custom-call(s32[2,8]{1,0:T(2,128)} %bitcast.2, s32[8]{0:T(128)} %slot_hbm.3, bf16[512,128]{1,0:T(8,128)(2,1)} %down_hbm.1, bf16[16,512]{1,0:T(8,128)(2,1)} %up_hbm.1), custom_call_target="tpu_custom_call" | custom-call | tf_op jit(solution)/shard_map/pallas_call | solution.py:270
  2.5 0.5 %collective-permute-start.1 = (bf16[64,4096]{1,0:T(8,128)(2,1)}, bf16[64,4096]{1,0:T(8,128)(2,1)S(1)}, u32[]{:S(2)}, u32[]{:S(2)}) collective-permute-start(bf16[64,4096]{1,0:T(8,128)(2,1)} %x_hbm.1), channel_id=1, source_target_pairs={{0,1},{1,0},{2,3},{3,2},{4,5},{5,4},{6,7},{7,6},{8,9},{9,8},{10,11... | collective-permute-start | bytes 1572872 | tf_op jit(solution)/shard_map/ppermute | solution.py:285
  3.0 3.7 %collective-permute-start = (bf16[48,512]{1,0:T(8,128)(2,1)}, bf16[48,512]{1,0:T(8,128)(2,1)S(1)}, u32[]{:S(2)}, u32[]{:S(2)}) collective-permute-start(bf16[48,512]{1,0:T(8,128)(2,1)} %get-tuple-element.31), channel_id=1, source_target_pairs={{0,8},{1,11},{2,10},{3,9},{4,12},{5,15},{6,14},{7,13},{8,0},{9,3},... | collective-permute-start | bytes 147464 | tf_op jit(solution)/shard_map/ppermute | solution.py:221
  6.7 2.3 %collective-permute-start.2 = (bf16[48,512]{1,0:T(8,128)(2,1)}, bf16[48,512]{1,0:T(8,128)(2,1)S(1)}, u32[]{:S(2)}, u32[]{:S(2)}) collective-permute-start(bf16[48,512]{1,0:T(8,128)(2,1)} %get-tuple-element.36), channel_id=1, source_target_pairs={{0,14},{1,13},{2,12},{3,15},{4,10},{5,9},{6,8},{7,11},{8,6},{9,5},... | collective-permute-start | bytes 147464 | tf_op jit(solution)/shard_map/ppermute | solution.py:221
  9.0 0.0 collective-permute-start.3
  9.0 0.8 %collective-permute-start.4 = (bf16[48,512]{1,0:T(8,128)(2,1)}, bf16[48,512]{1,0:T(8,128)(2,1)S(1)}, u32[]{:S(2)}, u32[]{:S(2)}) collective-permute-start(bf16[48,512]{1,0:T(8,128)(2,1)} %get-tuple-element.38), channel_id=1, source_target_pairs={{0,2},{1,3},{2,0},{3,1},{4,6},{5,7},{6,4},{7,5},{8,10},{9,11},{10,... | collective-permute-start | bytes 147464 | tf_op jit(solution)/shard_map/ppermute | solution.py:221
  9.8 2.2 %shard_map.113.stage = bf16[816,512]{1,0:T(8,128)(2,1)} custom-call(s32[2,8]{1,0:T(2,128)} %bitcast.4, s32[2,8]{1,0:T(2,128)} %bitcast.3, s32[8]{0:T(128)} %slot_hbm.3, s32[8]{0:T(128)} %count_hbm.1, bf16[128,512]{1,0:T(8,128)(2,1)} %g_hbm.1, bf16[64,4096]{1,0:T(8,128)(2,1)} %x_hbm.1, bf16[48,512]{1,0:T(8,128)(2,1)} %get-tuple-element.32.own_hbm), custom_call_target="tpu_custom_call" | custom-call | bytes 2097152 | tf_op jit(solution)/shard_map/pallas_call | solution.py:286
  11.9 0.0 copy-start
  12.0 1.1 %copy-done = bf16[816,512]{1,0:T(8,128)(2,1)S(1)} copy-done((bf16[816,512]{1,0:T(8,128)(2,1)S(1)}, bf16[816,512]{1,0:T(8,128)(2,1)}, u32[]{:S(2)}) %copy-start) | copy-done | bytes 835608
  13.1 0.0 copy-start.1
  13.1 0.1 shard_map.114.stage
  13.2 0.0 collective-permute-done.refs_0_
  13.2 0.6 %collective-permute-start.5 = (bf16[48,512]{1,0:T(8,128)(2,1)S(1)}, bf16[48,512]{1,0:T(8,128)(2,1)S(1)}, u32[]{:S(2)}, u32[]{:S(2)}) collective-permute-start(bf16[48,512]{1,0:T(8,128)(2,1)S(1)} %collective-permute-done.refs_0_), channel_id=1, source_target_pairs={{0,1},{1,0},{2,3},{3,2},{4,5},{5,4},{6,7},{7,6},{8,9},{9,8},{10,11... | collective-permute-start | bytes 147464 | tf_op jit(solution)/shard_map/ppermute | solution.py:230
  13.7 0.1 collective-permute-done.2.refs_1_
  13.8 0.0 collective-permute-start.6
  13.8 0.1 collective-permute-done.3.refs_2_
  14.0 0.4 %collective-permute-start.7 = (bf16[48,512]{1,0:T(8,128)(2,1)S(1)}, bf16[48,512]{1,0:T(8,128)(2,1)S(1)}, u32[]{:S(2)}, u32[]{:S(2)}) collective-permute-start(bf16[48,512]{1,0:T(8,128)(2,1)S(1)} %collective-permute-done.3.refs_2_), channel_id=1, source_target_pairs={{0,1},{1,0},{2,3},{3,2},{4,5},{5,4},{6,7},{7,6},{8,9},{9,8},{10,11... | collective-permute-start | bytes 147464 | tf_op jit(solution)/shard_map/ppermute | solution.py:230
  14.3 0.0 collective-permute-done.4.refs_3_
  14.3 0.3 collective-permute-done.5.refs_4_
  14.6 0.5 %collective-permute-done.6.refs_5_ = bf16[48,512]{1,0:T(8,128)(2,1)S(1)} collective-permute-done((bf16[48,512]{1,0:T(8,128)(2,1)S(1)}, bf16[48,512]{1,0:T(8,128)(2,1)S(1)}, u32[]{:S(2)}, u32[]{:S(2)}) %collective-permute-start.6) | collective-permute-done | bytes 49184 | tf_op jit(solution)/shard_map/ppermute | solution.py:230
  15.1 0.2 collective-permute-done.7.refs_6_
  15.2 0.0 collective-permute-done.1.x_other
  15.2 1.3 %shard_map.115 = (bf16[128,32]{1,0:T(8,128)(2,1)S(1)}, bf16[4,32,512]{2,1,0:T(8,128)(2,1)S(1)}, bf16[256,512]{1,0:T(8,128)(2,1)S(1)}, bf16[48,512]{1,0:T(8,128)(...) custom-call(bf16[816,512]{1,0:T(8,128)(2,1)S(1)} %shard_map.114.stag, ...), custom_call_target="tpu_custom_call" | custom-call | tf_op jit(solution)/shard_map/pallas_call | solution.py:305
  16.5 3.6 %collective-permute-start.8 = (bf16[48,512]{1,0:T(8,128)(2,1)S(1)}, bf16[48,512]{1,0:T(8,128)(2,1)S(1)}, u32[]{:S(2)}, u32[]{:S(2)}) collective-permute-start(bf16[48,512]{1,0:T(8,128)(2,1)S(1)} %get-tuple-element.39), channel_id=1, source_target_pairs={{0,14},{1,11},{2,12},{3,9},{4,10},{5,15},{6,8},{7,13},{8,6},{9,3},... | collective-permute-start | bytes 147464 | tf_op jit(solution)/shard_map/ppermute | solution.py:221
  20.1 0.4 %collective-permute-start.9 = (bf16[48,512]{1,0:T(8,128)(2,1)S(1)}, bf16[48,512]{1,0:T(8,128)(2,1)S(1)}, u32[]{:S(2)}, u32[]{:S(2)}) collective-permute-start(bf16[48,512]{1,0:T(8,128)(2,1)S(1)} %get-tuple-element.46), channel_id=1, source_target_pairs={{0,6},{1,13},{2,4},{3,15},{4,2},{5,9},{6,0},{7,11},{8,14},{9,5},{1... | collective-permute-start | bytes 147464 | tf_op jit(solution)/shard_map/ppermute | solution.py:221
  20.6 1.6 %collective-permute-start.10 = (bf16[48,512]{1,0:T(8,128)(2,1)S(1)}, bf16[48,512]{1,0:T(8,128)(2,1)S(1)}, u32[]{:S(2)}, u32[]{:S(2)}) collective-permute-start(bf16[48,512]{1,0:T(8,128)(2,1)S(1)} %get-tuple-element.47), channel_id=1, source_target_pairs={{0,4},{1,9},{2,6},{3,11},{4,0},{5,13},{6,2},{7,15},{8,12},{9,1},{1... | collective-permute-start | bytes 147464 | tf_op jit(solution)/shard_map/ppermute | solution.py:221
  22.1 1.5 %collective-permute-start.11 = (bf16[48,512]{1,0:T(8,128)(2,1)S(1)}, bf16[48,512]{1,0:T(8,128)(2,1)S(1)}, u32[]{:S(2)}, u32[]{:S(2)}) collective-permute-start(bf16[48,512]{1,0:T(8,128)(2,1)S(1)} %get-tuple-element.48), channel_id=1, source_target_pairs={{0,2},{1,3},{2,0},{3,1},{4,6},{5,7},{6,4},{7,5},{8,10},{9,11},{10,... | collective-permute-start | bytes 147464 | tf_op jit(solution)/shard_map/ppermute | solution.py:221
  23.6 0.0 copy-done.1
  23.6 0.8 %shard_map.116.base_ref = f32[128,2048]{1,0:T(8,128)S(1)} custom-call(bf16[256,512]{1,0:T(8,128)(2,1)S(1)} %get-tuple-element.40.kept_ref, bf16[2048,512]{1,0:T(8,128)(2,1)S(1)} %copy-done.1), custom_call_target="tpu_custom_call" | custom-call | flops 268435456 | bytes 3145728 | tf_op jit(solution)/shard_map/pallas_call | solution.py:322
  24.4 1.0 %shard_map.117 = bf16[128,2048]{1,0:T(8,128)(2,1)} custom-call(f32[128,2048]{1,0:T(8,128)S(1)} %shard_map.116.base_ref, bf16[128,32]{1,0:T(8,128)(2,1)S(1)} %get-tuple-element.41.dlow_ref, bf16[4,32,512]{2,1,0:T(8,128)(2,1)S(1)} %get-tuple-element.42.a_ref), custom_call_target="tpu_custom_call" | custom-call | flops 16777216 | bytes 1572864 | tf_op jit(solution)/shard_map/pallas_call | solution.py:334
  25.4 0.0 collective-permute-done.8.refs_1_
  25.4 0.1 collective-permute-start.12
  25.5 0.5 %collective-permute-done.9.refs_2_ = bf16[48,512]{1,0:T(8,128)(2,1)S(1)} collective-permute-done((bf16[48,512]{1,0:T(8,128)(2,1)S(1)}, bf16[48,512]{1,0:T(8,128)(2,1)S(1)}, u32[]{:S(2)}, u32[]{:S(2)}) %collective-permute-start.9) | collective-permute-done | bytes 49184 | tf_op jit(solution)/shard_map/ppermute | solution.py:221
  26.0 0.0 collective-permute-start.13
  26.0 0.0 collective-permute-done.10.refs_3_
  26.0 0.5 %collective-permute-start.14 = (bf16[48,512]{1,0:T(8,128)(2,1)S(1)}, bf16[48,512]{1,0:T(8,128)(2,1)S(1)}, u32[]{:S(2)}, u32[]{:S(2)}) collective-permute-start(bf16[48,512]{1,0:T(8,128)(2,1)S(1)} %collective-permute-done.10.refs_3_), channel_id=1, source_target_pairs={{0,1},{1,0},{2,3},{3,2},{4,5},{5,4},{6,7},{7,6},{8,9},{9,8},{10,11... | collective-permute-start | bytes 147464 | tf_op jit(solution)/shard_map/ppermute | solution.py:230
  26.5 0.0 collective-permute-done.11.refs_4_
  26.5 0.2 collective-permute-done.12.refs_5_
  26.7 0.5 %collective-permute-done.13.refs_6_ = bf16[48,512]{1,0:T(8,128)(2,1)S(1)} collective-permute-done((bf16[48,512]{1,0:T(8,128)(2,1)S(1)}, bf16[48,512]{1,0:T(8,128)(2,1)S(1)}, u32[]{:S(2)}, u32[]{:S(2)}) %collective-permute-start.13) | collective-permute-done | bytes 49184 | tf_op jit(solution)/shard_map/ppermute | solution.py:230
  27.3 0.2 collective-permute-done.14.refs_7_
  27.4 1.0 %shard_map.118 = (f32[512,128]{1,0:T(8,128)}, f32[16,256]{1,0:T(8,128)}) custom-call(bf16[256,512]{1,0:T(8,128)(2,1)S(1)} %get-tuple-element.40.kept_ref, bf16[48,512]{1,0:T(8,128)(2,1)S(1)} %get-tuple-element.44.refs_0_, bf16[48,512]{1,0:T(8,128)(2,1)S(1)} %collective-permute-done.8.refs_1_, bf16[48,512]{1,0:T(8,128)(2,1)S(1)} %collective-permute-done.9.refs_2_, ...), custom_call_target="tpu_custom_call" | custom-call | tf_op jit(solution)/shard_map/pallas_call | solution.py:350
Async XLA Ops:
  2.5 12.7 %collective-permute-start.1 = (bf16[64,4096]{1,0:T(8,128)(2,1)}, bf16[64,4096]{1,0:T(8,128)(2,1)S(1)}, u32[]{:S(2)}, u32[]{:S(2)}) collective-permute-start(bf16[64,4096]{1,0:T(8,128)(2,1)} %x_hbm.1), channel_id=1, source_target_pairs={{0,1},{1,0},{2,3},{3,2},{4,5},{5,4},{6,7},{7,6},{8,9},{9,8},{10,11... | collective-permute-start | bytes 1572872 | tf_op jit(solution)/shard_map/ppermute | solution.py:285
  3.0 10.1 %collective-permute-start = (bf16[48,512]{1,0:T(8,128)(2,1)}, bf16[48,512]{1,0:T(8,128)(2,1)S(1)}, u32[]{:S(2)}, u32[]{:S(2)}) collective-permute-start(bf16[48,512]{1,0:T(8,128)(2,1)} %get-tuple-element.31), channel_id=1, source_target_pairs={{0,8},{1,11},{2,10},{3,9},{4,12},{5,15},{6,14},{7,13},{8,0},{9,3},... | collective-permute-start | bytes 147464 | tf_op jit(solution)/shard_map/ppermute | solution.py:221
  6.7 7.1 %collective-permute-start.2 = (bf16[48,512]{1,0:T(8,128)(2,1)}, bf16[48,512]{1,0:T(8,128)(2,1)S(1)}, u32[]{:S(2)}, u32[]{:S(2)}) collective-permute-start(bf16[48,512]{1,0:T(8,128)(2,1)} %get-tuple-element.36), channel_id=1, source_target_pairs={{0,14},{1,13},{2,12},{3,15},{4,10},{5,9},{6,8},{7,11},{8,6},{9,5},... | collective-permute-start | bytes 147464 | tf_op jit(solution)/shard_map/ppermute | solution.py:221
  9.0 5.0 %collective-permute-start.3 = (bf16[48,512]{1,0:T(8,128)(2,1)}, bf16[48,512]{1,0:T(8,128)(2,1)S(1)}, u32[]{:S(2)}, u32[]{:S(2)}) collective-permute-start(bf16[48,512]{1,0:T(8,128)(2,1)} %get-tuple-element.37), channel_id=1, source_target_pairs={{0,4},{1,7},{2,6},{3,5},{4,0},{5,3},{6,2},{7,1},{8,12},{9,15},{10,... | collective-permute-start | bytes 147464 | tf_op jit(solution)/shard_map/ppermute | solution.py:221
  9.0 5.4 %collective-permute-start.4 = (bf16[48,512]{1,0:T(8,128)(2,1)}, bf16[48,512]{1,0:T(8,128)(2,1)S(1)}, u32[]{:S(2)}, u32[]{:S(2)}) collective-permute-start(bf16[48,512]{1,0:T(8,128)(2,1)} %get-tuple-element.38), channel_id=1, source_target_pairs={{0,2},{1,3},{2,0},{3,1},{4,6},{5,7},{6,4},{7,5},{8,10},{9,11},{10,... | collective-permute-start | bytes 147464 | tf_op jit(solution)/shard_map/ppermute | solution.py:221
  11.9 1.2 %copy-start = (bf16[816,512]{1,0:T(8,128)(2,1)S(1)}, bf16[816,512]{1,0:T(8,128)(2,1)}, u32[]{:S(2)}) copy-start(bf16[816,512]{1,0:T(8,128)(2,1)} %shard_map.113.stage) | copy-start | bytes 2506756
  13.1 10.5 %copy-start.1 = (bf16[2048,512]{1,0:T(8,128)(2,1)S(1)}, bf16[2048,512]{1,0:T(8,128)(2,1)}, u32[]{:S(2)}) copy-start(bf16[2048,512]{1,0:T(8,128)(2,1)} %w_ref.1) | copy-start | bytes 6291460
  13.2 1.4 %collective-permute-start.5 = (bf16[48,512]{1,0:T(8,128)(2,1)S(1)}, bf16[48,512]{1,0:T(8,128)(2,1)S(1)}, u32[]{:S(2)}, u32[]{:S(2)}) collective-permute-start(bf16[48,512]{1,0:T(8,128)(2,1)S(1)} %collective-permute-done.refs_0_), channel_id=1, source_target_pairs={{0,1},{1,0},{2,3},{3,2},{4,5},{5,4},{6,7},{7,6},{8,9},{9,8},{10,11... | collective-permute-start | bytes 147464 | tf_op jit(solution)/shard_map/ppermute | solution.py:230
  13.8 1.2 %collective-permute-start.6 = (bf16[48,512]{1,0:T(8,128)(2,1)S(1)}, bf16[48,512]{1,0:T(8,128)(2,1)S(1)}, u32[]{:S(2)}, u32[]{:S(2)}) collective-permute-start(bf16[48,512]{1,0:T(8,128)(2,1)S(1)} %collective-permute-done.2.refs_1_), channel_id=1, source_target_pairs={{0,1},{1,0},{2,3},{3,2},{4,5},{5,4},{6,7},{7,6},{8,9},{9,8},{10,11... | collective-permute-start | bytes 147464 | tf_op jit(solution)/shard_map/ppermute | solution.py:230
  14.0 1.2 %collective-permute-start.7 = (bf16[48,512]{1,0:T(8,128)(2,1)S(1)}, bf16[48,512]{1,0:T(8,128)(2,1)S(1)}, u32[]{:S(2)}, u32[]{:S(2)}) collective-permute-start(bf16[48,512]{1,0:T(8,128)(2,1)S(1)} %collective-permute-done.3.refs_2_), channel_id=1, source_target_pairs={{0,1},{1,0},{2,3},{3,2},{4,5},{5,4},{6,7},{7,6},{8,9},{9,8},{10,11... | collective-permute-start | bytes 147464 | tf_op jit(solution)/shard_map/ppermute | solution.py:230
  16.5 8.9 %collective-permute-start.8 = (bf16[48,512]{1,0:T(8,128)(2,1)S(1)}, bf16[48,512]{1,0:T(8,128)(2,1)S(1)}, u32[]{:S(2)}, u32[]{:S(2)}) collective-permute-start(bf16[48,512]{1,0:T(8,128)(2,1)S(1)} %get-tuple-element.39), channel_id=1, source_target_pairs={{0,14},{1,11},{2,12},{3,9},{4,10},{5,15},{6,8},{7,13},{8,6},{9,3},... | collective-permute-start | bytes 147464 | tf_op jit(solution)/shard_map/ppermute | solution.py:221
  20.1 5.9 %collective-permute-start.9 = (bf16[48,512]{1,0:T(8,128)(2,1)S(1)}, bf16[48,512]{1,0:T(8,128)(2,1)S(1)}, u32[]{:S(2)}, u32[]{:S(2)}) collective-permute-start(bf16[48,512]{1,0:T(8,128)(2,1)S(1)} %get-tuple-element.46), channel_id=1, source_target_pairs={{0,6},{1,13},{2,4},{3,15},{4,2},{5,9},{6,0},{7,11},{8,14},{9,5},{1... | collective-permute-start | bytes 147464 | tf_op jit(solution)/shard_map/ppermute | solution.py:221
  20.6 5.5 %collective-permute-start.10 = (bf16[48,512]{1,0:T(8,128)(2,1)S(1)}, bf16[48,512]{1,0:T(8,128)(2,1)S(1)}, u32[]{:S(2)}, u32[]{:S(2)}) collective-permute-start(bf16[48,512]{1,0:T(8,128)(2,1)S(1)} %get-tuple-element.47), channel_id=1, source_target_pairs={{0,4},{1,9},{2,6},{3,11},{4,0},{5,13},{6,2},{7,15},{8,12},{9,1},{1... | collective-permute-start | bytes 147464 | tf_op jit(solution)/shard_map/ppermute | solution.py:221
  22.1 4.4 %collective-permute-start.11 = (bf16[48,512]{1,0:T(8,128)(2,1)S(1)}, bf16[48,512]{1,0:T(8,128)(2,1)S(1)}, u32[]{:S(2)}, u32[]{:S(2)}) collective-permute-start(bf16[48,512]{1,0:T(8,128)(2,1)S(1)} %get-tuple-element.48), channel_id=1, source_target_pairs={{0,2},{1,3},{2,0},{3,1},{4,6},{5,7},{6,4},{7,5},{8,10},{9,11},{10,... | collective-permute-start | bytes 147464 | tf_op jit(solution)/shard_map/ppermute | solution.py:221
  25.4 1.3 %collective-permute-start.12 = (bf16[48,512]{1,0:T(8,128)(2,1)S(1)}, bf16[48,512]{1,0:T(8,128)(2,1)S(1)}, u32[]{:S(2)}, u32[]{:S(2)}) collective-permute-start(bf16[48,512]{1,0:T(8,128)(2,1)S(1)} %collective-permute-done.8.refs_1_), channel_id=1, source_target_pairs={{0,1},{1,0},{2,3},{3,2},{4,5},{5,4},{6,7},{7,6},{8,9},{9,8},{10,11... | collective-permute-start | bytes 147464 | tf_op jit(solution)/shard_map/ppermute | solution.py:230
  26.0 1.2 %collective-permute-start.13 = (bf16[48,512]{1,0:T(8,128)(2,1)S(1)}, bf16[48,512]{1,0:T(8,128)(2,1)S(1)}, u32[]{:S(2)}, u32[]{:S(2)}) collective-permute-start(bf16[48,512]{1,0:T(8,128)(2,1)S(1)} %collective-permute-done.9.refs_2_), channel_id=1, source_target_pairs={{0,1},{1,0},{2,3},{3,2},{4,5},{5,4},{6,7},{7,6},{8,9},{9,8},{10,11... | collective-permute-start | bytes 147464 | tf_op jit(solution)/shard_map/ppermute | solution.py:230
  26.0 1.4 %collective-permute-start.14 = (bf16[48,512]{1,0:T(8,128)(2,1)S(1)}, bf16[48,512]{1,0:T(8,128)(2,1)S(1)}, u32[]{:S(2)}, u32[]{:S(2)}) collective-permute-start(bf16[48,512]{1,0:T(8,128)(2,1)S(1)} %collective-permute-done.10.refs_3_), channel_id=1, source_target_pairs={{0,1},{1,0},{2,3},{3,2},{4,5},{5,4},{6,7},{7,6},{8,9},{9,8},{10,11... | collective-permute-start | bytes 147464 | tf_op jit(solution)/shard_map/ppermute | solution.py:230

commit v17 on v9

--- a/solution.py
+++ b/solution.py
@@ -63,29 +63,13 @@
     return partners(n, me, core) + passed
 
 
-class Staged:
-    def __init__(self, n, half, rows, picked, width, slots):
-        self.n, self.half, self.rows, self.picked, self.slots = n, half, rows, picked, slots
-        self.g = n * half
-        self.mask = self.g + rows
-        self.message = self.mask + rows
-        self.shape = (self.message + picked + ADAPTER_RANK, width)
-
-    def x(self, q):
-        return pl.ds(q * self.half, self.half)
-
-    def own_rows(self, ref):
-        return ref[self.mask : self.mask + self.picked, self.slots : 2 * self.slots]
-
-    def all_rows(self, kept):
-        parts = self.n * self.picked // self.rows
-        at = [pl.ds((2 + k) * self.slots, self.slots) for k in range(parts)]
-        return jnp.concatenate([kept[self.rows :, k] for k in at], axis=0)
+def in_hbm(*arrays):
+    return [pltpu.with_memory_space_constraint(array, pltpu.HBM) for array in arrays]
 
 
 def pack_kernel(n, chosen_hbm, slot_hbm, down_hbm, up_hbm, *refs):
     count = n // 2 + 1
-    send, (chosen_ref, slot_ref, down_ref, up_ref, out_ref, sems) = refs[:count], refs[count:]
+    send, (chosen_ref, slot_ref, down_ref, up_ref, sems) = refs[:count], refs[count:]
     tables = start_all([chosen_hbm, slot_hbm], [chosen_ref, slot_ref], sems)
     maps = start_all([down_hbm, up_hbm], [down_ref, up_ref], sems, 2)
     ranks = partners(n, lax.axis_index("dp"), lax.axis_index("tensor"))
@@ -95,80 +79,63 @@
     wait_all(maps)
     columns = dot(onehot, down_ref[...], 1, 1).astype(bf16)
     for k in range(count):
-        out_ref[k, :picked, :] = columns[k * picked : (k + 1) * picked]
-        out_ref[k, picked:, :] = up_ref[...]
-    wait_all(start_all([out_ref.at[k] for k in range(count)], send, sems, 4))
+        send[k][:picked, :] = columns[k * picked : (k + 1) * picked]
+        send[k][picked:, :] = up_ref[...]
 
 
 def stage_kernel(
-    n, lay, start_hbm, chosen_hbm, slot_hbm, count_hbm, g_hbm, x_hbm, own_hbm,
-    stage_hbm, start_ref, chosen_ref, slot_ref, count_ref, stage, sems,
+    n, picked, start_hbm, chosen_hbm, slot_hbm, count_hbm, g_hbm, x_mine, x_other,
+    x_ref, kept_ref, start_ref, chosen_ref, slot_ref, count_ref, sems,
 ):
-    rows, picked, slots = lay.rows, lay.picked, lay.slots
-    width = stage.shape[1]
+    rows, width = g_hbm.shape
+    half = x_mine.shape[0]
+    slots = width // 4
+    me, core = lax.axis_index("dp"), lax.axis_index("tensor")
     tables = start_all(
         [chosen_hbm, slot_hbm, start_hbm, count_hbm], [chosen_ref, slot_ref, start_ref, count_ref], sems
     )
-    gradient = start_all([g_hbm], [stage.at[pl.ds(lay.g, rows)]], sems, 4)
-    other = start_all(
-        [own_hbm] + [x_hbm.at[:, pl.ds(q * width, width)] for q in range(n)],
-        [stage.at[pl.ds(lay.message, picked + ADAPTER_RANK)]] + [stage.at[lay.x(q)] for q in range(n)],
-        sems,
-        5,
-    )
-    me = lax.axis_index("dp")
+    gradient = start_all([g_hbm], [kept_ref.at[pl.ds(0, rows)]], sems, 4)
+    mine = pl.ds(pl.multiple_of(core * half, half), half)
+    tokens = start_all([x_mine], [x_ref.at[mine]], sems, 5)
+    x_ref[pl.ds(pl.multiple_of((1 - core) * half, half), half), :] = x_other[...]
     wait_all(tables)
     position = lax.broadcasted_iota(i32, (rows, slots), 0)
     group = lax.broadcasted_iota(i32, (rows, slots), 1) // ADAPTER_RANK
     segment = jnp.full((rows, slots), -1, i32)
     for k in range(start_ref.shape[0]):
         segment += jnp.where(position >= start_ref[k, me], 1, 0)
-    stage[lay.mask : lay.mask + rows, :slots] = jnp.where(segment == group, 1.0, 0.0).astype(bf16)
-    mine = slot_rows(chosen_ref, slot_ref, [me], slots)
-    stage[lay.mask : lay.mask + picked, slots : 2 * slots] = mine
+    kept_ref[rows:, :slots] = jnp.where(segment == group, 1.0, 0.0).astype(bf16)
+    kept_ref[rows : rows + picked, slots : 2 * slots] = slot_rows(chosen_ref, slot_ref, [me], slots)
     every = slot_rows(chosen_ref, slot_ref, range(n), slots)
-    for k in range(n * picked // rows):
-        at = pl.ds((2 + k) * slots, slots)
-        stage[lay.mask : lay.mask + rows, at] = every[k * rows : (k + 1) * rows]
+    kept_ref[rows:, 2 * slots : 3 * slots] = every[:rows]
+    kept_ref[rows:, 3 * slots :] = every[rows:]
     wait_all(gradient)
     live = lax.broadcasted_iota(i32, (rows, width), 0) < count_ref[me]
-    g = stage[lay.g : lay.g + rows, :]
-    stage[lay.g : lay.g + rows, :] = jnp.where(live, g, jnp.zeros_like(g))
-    wait_all(other)
-    wait_all(start_all([stage], [stage_hbm], sems, 6 + n))
-
-
-def hand_on_kernel(stage, out_ref):
-    out_ref[...] = stage[...]
-
-
-def middle_kernel(n, lay, stage, x_other, *refs):
+    g = kept_ref[:rows, :]
+    kept_ref[:rows, :] = jnp.where(live, g, jnp.zeros_like(g))
+    wait_all(tokens)
+
+
+def middle_kernel(n, kept_ref, x_ref, *refs):
     count = n // 2 + 1
-    got, (dlow_ref, a_ref, kept_ref) = refs[: n - 1], refs[n - 1 : n + 2]
-    send, (x_ref, got_ref, up_ref) = refs[n + 2 : n + 2 + count], refs[n + 2 + count :]
+    got, (dlow_ref, a_ref), send = refs[:n], refs[n : n + 2], refs[n + 2 : n + 2 + count]
+    got_ref, up_ref = refs[n + 2 + count :]
     me, core = lax.axis_index("dp"), lax.axis_index("tensor")
-    half, rows, picked = lay.half, lay.rows, lay.picked
-    width = stage.shape[1]
-    mine = pl.ds(pl.multiple_of(core * half, half), half)
-    other = pl.ds(pl.multiple_of((1 - core) * half, half), half)
-    for q in range(n):
-        x_ref[mine, q * width : (q + 1) * width] = stage[lay.x(q), :]
-    x_ref[other, :] = x_other[...]
-    ranks = senders(n, me, core)
-    got_ref[me] = stage[lay.message :, :]
-    for sender, message in zip(ranks[1:], got):
+    rows, picked = dlow_ref.shape
+    width = kept_ref.shape[1]
+    slots = width // 4
+    for sender, message in zip(senders(n, me, core), got):
         got_ref[sender] = message[...]
 
-    in_seg = stage[lay.mask : lay.mask + rows, :picked].astype(f32) > 0.0
-    g = stage[lay.g : lay.g + rows, :]
-    onehot = lay.own_rows(stage)
+    in_seg = kept_ref[rows:, :picked].astype(f32) > 0.0
+    g = kept_ref[:rows, :]
+    onehot = kept_ref[rows : rows + picked, slots : 2 * slots]
     up_maps = got_ref[:, picked:, :].reshape(-1, width)
     b_sel = dot(onehot, up_maps, 1, 0).astype(bf16)
     dlow = jnp.where(in_seg, adapter_scale * dot(g, b_sel, 1, 1), 0.0).astype(bf16)
     dlow_ref[...] = dlow
     parts = n // 2
     a_ref[...] = got_ref[pl.ds(pl.multiple_of(core * parts, parts), parts), :picked, :]
-    kept_ref[...] = stage[lay.g : lay.message, :]
     targets = partners(n, me, core)
     for target, message in zip(targets, send):
         at = pl.ds(pl.multiple_of(target * width, width), width)
@@ -185,29 +152,30 @@
         message[picked:, :] = up_ref[target]
 
 
-def base_kernel(kept_ref, w_ref, out_ref):
-    out_ref[...] = dot(kept_ref[: out_ref.shape[0], :], w_ref[...], 1, 1)
-
-
-def grad_x_kernel(base_ref, dlow_ref, a_ref, out_hbm, out_ref, sems):
+def grad_x_kernel(kept_ref, w_ref, dlow_ref, a_ref, out_hbm, out_ref, sems):
     steps, picked, width = a_ref.shape
+    g = kept_ref[: out_ref.shape[0], :]
     done = []
     for j in range(steps):
         at = pl.ds(j * width, width)
-        total = base_ref[:, at] + dot(dlow_ref[...], a_ref[j], 1, 0)
+        total = dot(g, w_ref[at, :], 1, 1) + dot(dlow_ref[...], a_ref[j], 1, 0)
         out_ref[:, at] = total.astype(bf16)
         done += start_all([out_ref.at[:, at]], [out_hbm.at[:, at]], sems, j)
     wait_all(done)
 
 
-def final_kernel(n, lay, kept_ref, *refs):
+def final_kernel(n, kept_ref, *refs):
     got, (a_ref, up_ref, rows_ref) = refs[:n], refs[n:]
     me, core = lax.axis_index("dp"), lax.axis_index("tensor")
-    piece, picked = up_ref.shape[1], lay.picked
+    piece, picked = up_ref.shape[1], rows_ref.shape[1] - ADAPTER_RANK
+    half, slots = kept_ref.shape[0] // 2, kept_ref.shape[1] // 4
     for sender, message in zip(senders(n, me, core), got):
         rows_ref[sender] = message[...]
     rows = rows_ref[:, :picked, :].reshape(n * picked, rows_ref.shape[2])
-    a_ref[...] = dot(rows, lay.all_rows(kept_ref), 0, 0)
+    onehot = jnp.concatenate(
+        [kept_ref[half:, 2 * slots : 3 * slots], kept_ref[half:, 3 * slots :]], axis=0
+    )
+    a_ref[...] = dot(rows, onehot, 0, 0)
     at = pl.ds(pl.multiple_of(core * piece, piece), piece)
     up_ref[...] = jnp.sum(rows_ref[:, picked:, at].astype(f32), axis=0)
 
@@ -222,7 +190,9 @@
         )
         for message, step in zip(messages, steps(n))
     ]
-    got[0], beside = lax.optimization_barrier((got[0], beside))
+    for k, (a, b) in enumerate(steps(n)):
+        if a != b:
+            got[k], beside = lax.optimization_barrier((got[k], beside))
     passed = [
         lax.ppermute(message, "tensor", [(0, 1), (1, 0)])
         for message, (a, b) in zip(got, steps(n))
@@ -242,7 +212,7 @@
     adapter_slot,
     token_count,
 ):
-    tok_half, model_width = inputs.shape
+    model_width = inputs.shape[1]
     tok_rows, out_width = output_gradient.shape
     column_total, slot_width = down_maps.shape
     half = frozen_weight.shape[0]
@@ -263,89 +233,60 @@
     ]
     dma = pltpu.SemaphoreType.DMA
 
-    lay = Staged(n, tok_half, tok_rows, picked, column_total, slot_width)
     own, *sent = pl.pallas_call(
         functools.partial(pack_kernel, n),
         out_shape=[message] * count,
         in_specs=[HBM] * 4,
-        out_specs=[HBM] * count,
+        out_specs=[VMEM] * count,
         scratch_shapes=tables[1:3]
-        + [
-            pltpu.VMEM(down_maps.shape, bf16),
-            pltpu.VMEM(up_maps.shape, bf16),
-            pltpu.VMEM((count,) + message.shape, bf16),
-            dma((4 + count,)),
-        ],
-        compiler_params=params(56),
-    )(chosen, adapter_slot, down_maps, up_maps)
+        + [pltpu.VMEM(down_maps.shape, bf16), pltpu.VMEM(up_maps.shape, bf16), dma((4,))],
+        compiler_params=params(8),
+    )(*in_hbm(chosen, adapter_slot, down_maps, up_maps))
     sent, x_late = lax.optimization_barrier((sent, inputs))
     x_other = lax.ppermute(x_late, "tensor", [(0, 1), (1, 0)])
-    stage = pl.pallas_call(
-        functools.partial(stage_kernel, n, lay),
-        out_shape=shape(lay.shape, bf16),
-        in_specs=[HBM] * 7,
-        out_specs=HBM,
-        scratch_shapes=tables + [pltpu.VMEM(lay.shape, bf16), dma((7 + n,))],
-        compiler_params=params(56),
-        cost_estimate=pl.CostEstimate(flops=0, bytes_accessed=1 << 21, transcendentals=0),
-    )(starts, chosen, adapter_slot, token_count, output_gradient, inputs, own)
-    got, stage = exchange(sent, stage)
-    stage = pl.pallas_call(
-        hand_on_kernel,
-        out_shape=shape(lay.shape, bf16),
-        in_specs=[VMEM],
-        out_specs=VMEM,
+    x, kept = pl.pallas_call(
+        functools.partial(stage_kernel, n, picked),
+        out_shape=[shape((tok_rows, model_width), bf16), shape((2 * tok_rows, out_width), bf16)],
+        in_specs=[HBM] * 6 + [VMEM],
+        out_specs=[VMEM] * 2,
+        scratch_shapes=tables + [dma((6,))],
         compiler_params=params(8),
         cost_estimate=pl.CostEstimate(flops=0, bytes_accessed=1 << 21, transcendentals=0),
-    )(stage)
-
-    dlow, a_half, kept, own, *sent = pl.pallas_call(
-        functools.partial(middle_kernel, n, lay),
-        out_shape=[
-            shape((tok_rows, picked), bf16),
-            shape((n // 2, picked, column_total), bf16),
-            shape((2 * tok_rows, out_width), bf16),
-        ]
+    )(*in_hbm(starts, chosen, adapter_slot, token_count, output_gradient, inputs), x_other)
+    got, kept = exchange(sent, kept)
+
+    dlow, a_half, *sent = pl.pallas_call(
+        functools.partial(middle_kernel, n),
+        out_shape=[shape((tok_rows, picked), bf16), shape((n // 2, picked, column_total), bf16)]
         + [message] * count,
-        in_specs=[VMEM] * (1 + n),
-        out_specs=[VMEM] * (3 + count),
+        in_specs=[VMEM] * (2 + n),
+        out_specs=[VMEM] * (2 + count),
         scratch_shapes=[
-            pltpu.VMEM((tok_rows, model_width), bf16),
             pltpu.VMEM((n,) + message.shape, bf16),
             pltpu.VMEM((n, ADAPTER_RANK, out_width), bf16),
         ],
         compiler_params=params(8),
-    )(stage, x_other, *got)
-    base = pl.pallas_call(
-        base_kernel,
-        out_shape=shape((tok_rows, half), f32),
-        in_specs=[VMEM, VMEM],
-        out_specs=VMEM,
-        compiler_params=params(8),
-        cost_estimate=pl.CostEstimate(
-            flops=2 * tok_rows * half * out_width,
-            bytes_accessed=4 * half * tok_rows + 2 * half * out_width,
-            transcendentals=0,
-        ),
-    )(kept, frozen_weight)
+    )(kept, x, own, *got)
+    own, *sent = sent
+
     grad_x = pl.pallas_call(
         grad_x_kernel,
         out_shape=shape((tok_rows, half), bf16),
-        in_specs=[VMEM] * 3,
+        in_specs=[VMEM] * 4,
         out_specs=HBM,
         scratch_shapes=[pltpu.VMEM((tok_rows, half), bf16), dma((n // 2,))],
         compiler_params=params(8),
         cost_estimate=pl.CostEstimate(
-            flops=2 * tok_rows * half * picked,
-            bytes_accessed=6 * half * tok_rows,
+            flops=2 * tok_rows * half * (out_width + picked),
+            bytes_accessed=2 * half * (out_width + tok_rows),
             transcendentals=0,
         ),
-    )(base, dlow, a_half)
+    )(kept, frozen_weight, dlow, a_half)
 
     got, grad_x = exchange(sent, grad_x)
 
     grad_a, up_map_gradient = pl.pallas_call(
-        functools.partial(final_kernel, n, lay),
+        functools.partial(final_kernel, n),
         out_shape=[shape((column_total, slot_width), f32), shape((ADAPTER_RANK, piece), f32)],
         in_specs=[VMEM] * (1 + n),
         out_specs=[VMEM, VMEM],
@@ -436,7 +377,7 @@
         and down_maps.shape[0] == out_width
         and down_maps.shape[1] == n * up_maps.shape[0]
         and out_width % (128 * tp) == 0
-        and out_width >= 4 * down_maps.shape[1]
+        and out_width == 4 * down_maps.shape[1]
         and args[1].shape[0] == 2 * args[0].shape[0] == down_maps.shape[1]
         and args[5].shape[1] * ADAPTER_RANK * n == 2 * down_maps.shape[1]
     )

time: 27.6 us -> 27.4 us (level)
  waiting for transfers between devices: 1.59 us -> 3.91 us
  Pallas kernels: 8.17 us -> 6.38 us
  local copies, waits for them, and re-layouts: 1.15 us -> 0.01 us
  starting transfers between devices: 15.7 us -> 16.3 us
    pallas_call x5 -> x3, Pallas kernels: 5.31 us -> 3.44 us  [the longest x1 1.25 us: local_kernels(): pl.pallas_call(functools.partial(middle_kernel, n), out_shape=[shape((tok...]
    ppermute x6, waiting for transfers between devices: 0.44 us -> 2.1 us  [exchange(): lax.ppermute(message, 'tensor', [(0, 1), (1, 0)])]
    unnamed x4 -> x2, local copies, waits for them, and re-layouts: 1.15 us -> 0.01 us
    ppermute x8, waiting for transfers between devices: 1.15 us -> 1.8 us  [exchange(): lax.ppermute(message, ('dp', 'tensor'), [(2 * i + c, 2 * (i ^ step[c]) +...]
    pallas_call x1, Pallas kernels: 0.99 us -> 1.64 us  [local_kernels(): pl.pallas_call(grad_x_kernel, out_shape=shape((tok_rows, half), bf16), in...]
    pallas_call x1, Pallas kernels: 1.88 us -> 1.3 us  [local_kernels(): pl.pallas_call(functools.partial(pack_kernel, n), out_shape=[message] * c...]
    ppermute x6, starting transfers between devices: 1.22 us -> 1.61 us  [exchange(): lax.ppermute(message, 'tensor', [(0, 1), (1, 0)])]
  transfers between devices with their start and end apart: 15 -> 15, of which waited for: 5 -> 10; matrix products, arithmetic and copies ran while one was open for 0% -> 0% of each run, Pallas kernels for 15% -> 10%
where the time goes in v17:
time: 27.4 us; the launch traced here: 27.2 us
  starting transfers between devices  16.3 us (59%)
  Pallas kernels  6.38 us (23%)
  waiting for transfers between devices  3.91 us (14%)
  between operations  0.69 us (3%)
    ppermute x8, starting transfers between devices, exchange(): lax.ppermute(message, ('dp', 'tensor'), [(2 * i + c, 2 * (i ^ step[c]) +...  14.1 us
    ppermute x6, waiting for transfers between devices, exchange(): lax.ppermute(message, 'tensor', [(0, 1), (1, 0)])  2.1 us
    ppermute x8, waiting for transfers between devices, exchange(): lax.ppermute(message, ('dp', 'tensor'), [(2 * i + c, 2 * (i ^ step[c]) +...  1.8 us
    pallas_call x1, Pallas kernels, local_kernels(): pl.pallas_call(grad_x_kernel, out_shape=shape((tok_rows, half), bf16), in...  1.64 us
    ppermute x6, starting transfers between devices, exchange(): lax.ppermute(message, 'tensor', [(0, 1), (1, 0)])  1.61 us
    pallas_call x1, Pallas kernels, local_kernels(): pl.pallas_call(functools.partial(pack_kernel, n), out_shape=[message] * c...  1.3 us
    pallas_call x1, Pallas kernels, local_kernels(): pl.pallas_call(functools.partial(middle_kernel, n), out_shape=[shape((tok...  1.25 us
    pallas_call x1, Pallas kernels, local_kernels(): pl.pallas_call(functools.partial(stage_kernel, n, picked), out_shape=[sha...  1.17 us
  transfers between devices with their start and end apart: 15, of which 10 were waited for; matrix products, arithmetic and copies ran while one was open for 0% of the time, Pallas kernels for 10%

profile of v17, /device:TPU:0, one launch (start us, length us, event | category | flops | bytes accessed | tf_op | source)
XLA Modules:
  0.0 27.2 jit_solution(5875493279835874296)
XLA Ops:
  0.6 0.0 copy-start
  0.6 1.3 %shard_map.112 = (bf16[48,512]{1,0:T(8,128)(2,1)S(1)}, bf16[48,512]{1,0:T(8,128)(2,1)S(1)}, bf16[48,512]{1,0:T(8,128)(2,1)S(1)}, bf16[48,512]{1,0:T(8,128)(2,1)S(1)}, bf16[48,512]{1,0:T(8,128)(2,1)S(1)}) custom-call(s32[2,8]{1,0:T(2,128)} %bitcast.2, s32[8]{0:T(128)} %slot_hbm.3, bf16[512,128]{1,0:T(8,128)(2,1)} %down_hbm.1, bf16[16,512]{1,0:T(8,128)(2,1)} %up_hbm.1), custom_call_target="tpu_custom_call" | custom-call | tf_op jit(solution)/shard_map/pallas_call | solution.py:236
  2.0 0.5 %collective-permute-start.3 = (bf16[64,4096]{1,0:T(8,128)(2,1)}, bf16[64,4096]{1,0:T(8,128)(2,1)S(1)}, u32[]{:S(2)}, u32[]{:S(2)}) collective-permute-start(bf16[64,4096]{1,0:T(8,128)(2,1)} %x_mine.1), channel_id=1, source_target_pairs={{0,1},{1,0},{2,3},{3,2},{4,5},{5,4},{6,7},{7,6},{8,9},{9,8},{10,11... | collective-permute-start | bytes 1572872 | tf_op jit(solution)/shard_map/ppermute | solution.py:246
  2.5 5.6 %collective-permute-start.2 = (bf16[48,512]{1,0:T(8,128)(2,1)S(1)}, bf16[48,512]{1,0:T(8,128)(2,1)S(1)}, u32[]{:S(2)}, u32[]{:S(2)}) collective-permute-start(bf16[48,512]{1,0:T(8,128)(2,1)S(1)} %get-tuple-element.42), channel_id=1, source_target_pairs={{0,14},{1,11},{2,12},{3,9},{4,10},{5,15},{6,8},{7,13},{8,6},{9,3},... | collective-permute-start | bytes 147464 | tf_op jit(solution)/shard_map/ppermute | solution.py:186
  8.1 0.0 collective-permute-start.1
  8.1 2.0 %collective-permute-start = (bf16[48,512]{1,0:T(8,128)(2,1)S(1)}, bf16[48,512]{1,0:T(8,128)(2,1)S(1)}, u32[]{:S(2)}, u32[]{:S(2)}) collective-permute-start(bf16[48,512]{1,0:T(8,128)(2,1)S(1)} %get-tuple-element.40), channel_id=1, source_target_pairs={{0,4},{1,9},{2,6},{3,11},{4,0},{5,13},{6,2},{7,15},{8,12},{9,1},{1... | collective-permute-start | bytes 147464 | tf_op jit(solution)/shard_map/ppermute | solution.py:186
  10.1 1.5 %collective-permute-start.4 = (bf16[48,512]{1,0:T(8,128)(2,1)S(1)}, bf16[48,512]{1,0:T(8,128)(2,1)S(1)}, u32[]{:S(2)}, u32[]{:S(2)}) collective-permute-start(bf16[48,512]{1,0:T(8,128)(2,1)S(1)} %get-tuple-element.53), channel_id=1, source_target_pairs={{0,2},{1,3},{2,0},{3,1},{4,6},{5,7},{6,4},{7,5},{8,10},{9,11},{10,... | collective-permute-start | bytes 147464 | tf_op jit(solution)/shard_map/ppermute | solution.py:186
  11.6 0.0 collective-permute-done.3.x_other
  11.6 1.2 %shard_map.113 = (bf16[128,4096]{1,0:T(8,128)(2,1)S(1)}, bf16[256,512]{1,0:T(8,128)(2,1)S(1)}) custom-call(s32[2,8]{1,0:T(2,128)} %bitcast.4, s32[2,8]{1,0:T(2,128)} %bitcast.3, s32[8]{0:T(128)} %slot_hbm.3, s32[8]{0:T(128)} %count_hbm.1, bf16[128,512]{1,0:T(8,128)(2,1)} %g_hbm.1, bf16[64,4096]{1,0:T(8,128)(2,1)} %x_mine.1, ...), custom_call_target="tpu_custom_call" | custom-call | bytes 2097152 | tf_op jit(solution)/shard_map/pallas_call | solution.py:247
  12.7 0.0 collective-permute-done.2.refs_1_
  12.8 0.5 %collective-permute-done.1.refs_2_ = bf16[48,512]{1,0:T(8,128)(2,1)S(1)} collective-permute-done((bf16[48,512]{1,0:T(8,128)(2,1)S(1)}, bf16[48,512]{1,0:T(8,128)(2,1)S(1)}, u32[]{:S(2)}, u32[]{:S(2)}) %collective-permute-start.1) | collective-permute-done | bytes 49184 | tf_op jit(solution)/shard_map/ppermute | solution.py:186
  13.2 0.5 %collective-permute-done.refs_3_ = bf16[48,512]{1,0:T(8,128)(2,1)S(1)} collective-permute-done((bf16[48,512]{1,0:T(8,128)(2,1)S(1)}, bf16[48,512]{1,0:T(8,128)(2,1)S(1)}, u32[]{:S(2)}, u32[]{:S(2)}) %collective-permute-start) | collective-permute-done | bytes 49184 | tf_op jit(solution)/shard_map/ppermute | solution.py:186
  13.7 0.0 collective-permute-start.7
  13.7 0.5 %collective-permute-start.6 = (bf16[48,512]{1,0:T(8,128)(2,1)S(1)}, bf16[48,512]{1,0:T(8,128)(2,1)S(1)}, u32[]{:S(2)}, u32[]{:S(2)}) collective-permute-start(bf16[48,512]{1,0:T(8,128)(2,1)S(1)} %collective-permute-done.1.refs_2_), channel_id=1, source_target_pairs={{0,1},{1,0},{2,3},{3,2},{4,5},{5,4},{6,7},{7,6},{8,9},{9,8},{10,11... | collective-permute-start | bytes 147464 | tf_op jit(solution)/shard_map/ppermute | solution.py:197
  14.2 0.0 collective-permute-start.5
  14.2 0.0 collective-permute-done.4.refs_4_
  14.2 0.7 %collective-permute-done.7.refs_7_ = bf16[48,512]{1,0:T(8,128)(2,1)S(1)} collective-permute-done((bf16[48,512]{1,0:T(8,128)(2,1)S(1)}, bf16[48,512]{1,0:T(8,128)(2,1)S(1)}, u32[]{:S(2)}, u32[]{:S(2)}) %collective-permute-start.7) | collective-permute-done | bytes 49184 | tf_op jit(solution)/shard_map/ppermute | solution.py:197
  14.9 0.2 collective-permute-done.6.refs_6_
  15.1 0.3 %collective-permute-done.5.refs_5_ = bf16[48,512]{1,0:T(8,128)(2,1)S(1)} collective-permute-done((bf16[48,512]{1,0:T(8,128)(2,1)S(1)}, bf16[48,512]{1,0:T(8,128)(2,1)S(1)}, u32[]{:S(2)}, u32[]{:S(2)}) %collective-permute-start.5) | collective-permute-done | bytes 49184 | tf_op jit(solution)/shard_map/ppermute | solution.py:197
  15.4 1.3 %shard_map.114 = (bf16[128,32]{1,0:T(8,128)(2,1)S(1)}, bf16[4,32,512]{2,1,0:T(8,128)(2,1)S(1)}, bf16[48,512]{1,0:T(8,128)(2,1)S(1)}, bf16[48,512]{1,0:T(8,128)(2...) custom-call(bf16[256,512]{1,0:T(8,128)(2,1)S(1)} %get-tuple-element.47.kept_ref, ...), custom_call_target="tpu_custom_call" | custom-call | tf_op jit(solution)/shard_map/pallas_call | solution.py:258
  16.7 1.6 %collective-permute-start.10 = (bf16[48,512]{1,0:T(8,128)(2,1)S(1)}, bf16[48,512]{1,0:T(8,128)(2,1)S(1)}, u32[]{:S(2)}, u32[]{:S(2)}) collective-permute-start(bf16[48,512]{1,0:T(8,128)(2,1)S(1)} %get-tuple-element.56), channel_id=1, source_target_pairs={{0,14},{1,11},{2,12},{3,9},{4,10},{5,15},{6,8},{7,13},{8,6},{9,3},... | collective-permute-start | bytes 147464 | tf_op jit(solution)/shard_map/ppermute | solution.py:186
  18.3 0.1 collective-permute-start.9
  18.3 2.9 %collective-permute-start.8 = (bf16[48,512]{1,0:T(8,128)(2,1)S(1)}, bf16[48,512]{1,0:T(8,128)(2,1)S(1)}, u32[]{:S(2)}, u32[]{:S(2)}) collective-permute-start(bf16[48,512]{1,0:T(8,128)(2,1)S(1)} %get-tuple-element.54), channel_id=1, source_target_pairs={{0,4},{1,9},{2,6},{3,11},{4,0},{5,13},{6,2},{7,15},{8,12},{9,1},{1... | collective-permute-start | bytes 147464 | tf_op jit(solution)/shard_map/ppermute | solution.py:186
  21.2 0.6 %collective-permute-start.11 = (bf16[48,512]{1,0:T(8,128)(2,1)S(1)}, bf16[48,512]{1,0:T(8,128)(2,1)S(1)}, u32[]{:S(2)}, u32[]{:S(2)}) collective-permute-start(bf16[48,512]{1,0:T(8,128)(2,1)S(1)} %get-tuple-element.66), channel_id=1, source_target_pairs={{0,2},{1,3},{2,0},{3,1},{4,6},{5,7},{6,4},{7,5},{8,10},{9,11},{10,... | collective-permute-start | bytes 147464 | tf_op jit(solution)/shard_map/ppermute | solution.py:186
  21.8 0.0 copy-done
  21.8 1.6 %shard_map.115 = bf16[128,2048]{1,0:T(8,128)(2,1)} custom-call(bf16[256,512]{1,0:T(8,128)(2,1)S(1)} %get-tuple-element.47.kept_ref, bf16[2048,512]{1,0:T(8,128)(2,1)S(1)} %copy-done, bf16[128,32]{1,0:T(8,128)(2,1)S(1)} %get-tuple-element.57.dlow_ref, bf16[4,32,512]{2,1,0:T(8,128)(2,1)S(1)} %get-tuple-element.58.a_ref), custom_call_target="tpu_custom_call" | custom-call | flops 285212672 | bytes 2621440 | tf_op jit(solution)/shard_map/pallas_call | solution.py:272
  23.4 0.3 collective-permute-done.10.refs_1_
  23.7 0.6 %collective-permute-done.9.refs_2_ = bf16[48,512]{1,0:T(8,128)(2,1)S(1)} collective-permute-done((bf16[48,512]{1,0:T(8,128)(2,1)S(1)}, bf16[48,512]{1,0:T(8,128)(2,1)S(1)}, u32[]{:S(2)}, u32[]{:S(2)}) %collective-permute-start.9) | collective-permute-done | bytes 49184 | tf_op jit(solution)/shard_map/ppermute | solution.py:186
  24.2 0.0 collective-permute-done.8.refs_3_
  24.2 0.6 %collective-permute-start.14 = (bf16[48,512]{1,0:T(8,128)(2,1)S(1)}, bf16[48,512]{1,0:T(8,128)(2,1)S(1)}, u32[]{:S(2)}, u32[]{:S(2)}) collective-permute-start(bf16[48,512]{1,0:T(8,128)(2,1)S(1)} %collective-permute-done.8.refs_3_), channel_id=1, source_target_pairs={{0,1},{1,0},{2,3},{3,2},{4,5},{5,4},{6,7},{7,6},{8,9},{9,8},{10,11... | collective-permute-start | bytes 147464 | tf_op jit(solution)/shard_map/ppermute | solution.py:197
  24.8 0.0 collective-permute-start.13
  24.8 0.5 %collective-permute-start.12 = (bf16[48,512]{1,0:T(8,128)(2,1)S(1)}, bf16[48,512]{1,0:T(8,128)(2,1)S(1)}, u32[]{:S(2)}, u32[]{:S(2)}) collective-permute-start(bf16[48,512]{1,0:T(8,128)(2,1)S(1)} %collective-permute-done.10.refs_1_), channel_id=1, source_target_pairs={{0,1},{1,0},{2,3},{3,2},{4,5},{5,4},{6,7},{7,6},{8,9},{9,8},{10,11... | collective-permute-start | bytes 147464 | tf_op jit(solution)/shard_map/ppermute | solution.py:197
  25.4 0.0 collective-permute-done.11.refs_4_
  25.4 0.4 %collective-permute-done.14.refs_7_ = bf16[48,512]{1,0:T(8,128)(2,1)S(1)} collective-permute-done((bf16[48,512]{1,0:T(8,128)(2,1)S(1)}, bf16[48,512]{1,0:T(8,128)(2,1)S(1)}, u32[]{:S(2)}, u32[]{:S(2)}) %collective-permute-start.14) | collective-permute-done | bytes 49184 | tf_op jit(solution)/shard_map/ppermute | solution.py:197
  25.7 0.3 %collective-permute-done.13.refs_6_ = bf16[48,512]{1,0:T(8,128)(2,1)S(1)} collective-permute-done((bf16[48,512]{1,0:T(8,128)(2,1)S(1)}, bf16[48,512]{1,0:T(8,128)(2,1)S(1)}, u32[]{:S(2)}, u32[]{:S(2)}) %collective-permute-start.13) | collective-permute-done | bytes 49184 | tf_op jit(solution)/shard_map/ppermute | solution.py:197
  26.1 0.2 collective-permute-done.12.refs_5_
  26.2 1.0 %shard_map.116 = (f32[512,128]{1,0:T(8,128)}, f32[16,256]{1,0:T(8,128)}) custom-call(bf16[256,512]{1,0:T(8,128)(2,1)S(1)} %get-tuple-element.47.kept_ref, bf16[48,512]{1,0:T(8,128)(2,1)S(1)} %get-tuple-element.62.refs_0_, bf16[48,512]{1,0:T(8,128)(2,1)S(1)} %collective-permute-done.10.refs_1_, bf16[48,512]{1,0:T(8,128)(2,1)S(1)} %collective-permute-done.9.refs_2_, ...), custom_call_target="tpu_custom_call" | custom-call | tf_op jit(solution)/shard_map/pallas_call | solution.py:288
Async XLA Ops:
  0.6 21.1 %copy-start = (bf16[2048,512]{1,0:T(8,128)(2,1)S(1)}, bf16[2048,512]{1,0:T(8,128)(2,1)}, u32[]{:S(2)}) copy-start(bf16[2048,512]{1,0:T(8,128)(2,1)} %w_ref.1) | copy-start | bytes 6291460
  2.0 9.6 %collective-permute-start.3 = (bf16[64,4096]{1,0:T(8,128)(2,1)}, bf16[64,4096]{1,0:T(8,128)(2,1)S(1)}, u32[]{:S(2)}, u32[]{:S(2)}) collective-permute-start(bf16[64,4096]{1,0:T(8,128)(2,1)} %x_mine.1), channel_id=1, source_target_pairs={{0,1},{1,0},{2,3},{3,2},{4,5},{5,4},{6,7},{7,6},{8,9},{9,8},{10,11... | collective-permute-start | bytes 1572872 | tf_op jit(solution)/shard_map/ppermute | solution.py:246
  2.5 10.3 %collective-permute-start.2 = (bf16[48,512]{1,0:T(8,128)(2,1)S(1)}, bf16[48,512]{1,0:T(8,128)(2,1)S(1)}, u32[]{:S(2)}, u32[]{:S(2)}) collective-permute-start(bf16[48,512]{1,0:T(8,128)(2,1)S(1)} %get-tuple-element.42), channel_id=1, source_target_pairs={{0,14},{1,11},{2,12},{3,9},{4,10},{5,15},{6,8},{7,13},{8,6},{9,3},... | collective-permute-start | bytes 147464 | tf_op jit(solution)/shard_map/ppermute | solution.py:186
  8.1 5.1 %collective-permute-start.1 = (bf16[48,512]{1,0:T(8,128)(2,1)S(1)}, bf16[48,512]{1,0:T(8,128)(2,1)S(1)}, u32[]{:S(2)}, u32[]{:S(2)}) collective-permute-start(bf16[48,512]{1,0:T(8,128)(2,1)S(1)} %get-tuple-element.41), channel_id=1, source_target_pairs={{0,6},{1,13},{2,4},{3,15},{4,2},{5,9},{6,0},{7,11},{8,14},{9,5},{1... | collective-permute-start | bytes 147464 | tf_op jit(solution)/shard_map/ppermute | solution.py:186
  8.1 5.6 %collective-permute-start = (bf16[48,512]{1,0:T(8,128)(2,1)S(1)}, bf16[48,512]{1,0:T(8,128)(2,1)S(1)}, u32[]{:S(2)}, u32[]{:S(2)}) collective-permute-start(bf16[48,512]{1,0:T(8,128)(2,1)S(1)} %get-tuple-element.40), channel_id=1, source_target_pairs={{0,4},{1,9},{2,6},{3,11},{4,0},{5,13},{6,2},{7,15},{8,12},{9,1},{1... | collective-permute-start | bytes 147464 | tf_op jit(solution)/shard_map/ppermute | solution.py:186
  10.1 4.2 %collective-permute-start.4 = (bf16[48,512]{1,0:T(8,128)(2,1)S(1)}, bf16[48,512]{1,0:T(8,128)(2,1)S(1)}, u32[]{:S(2)}, u32[]{:S(2)}) collective-permute-start(bf16[48,512]{1,0:T(8,128)(2,1)S(1)} %get-tuple-element.53), channel_id=1, source_target_pairs={{0,2},{1,3},{2,0},{3,1},{4,6},{5,7},{6,4},{7,5},{8,10},{9,11},{10,... | collective-permute-start | bytes 147464 | tf_op jit(solution)/shard_map/ppermute | solution.py:186
  13.7 1.2 %collective-permute-start.7 = (bf16[48,512]{1,0:T(8,128)(2,1)S(1)}, bf16[48,512]{1,0:T(8,128)(2,1)S(1)}, u32[]{:S(2)}, u32[]{:S(2)}) collective-permute-start(bf16[48,512]{1,0:T(8,128)(2,1)S(1)} %collective-permute-done.refs_3_), channel_id=1, source_target_pairs={{0,1},{1,0},{2,3},{3,2},{4,5},{5,4},{6,7},{7,6},{8,9},{9,8},{10,11... | collective-permute-start | bytes 147464 | tf_op jit(solution)/shard_map/ppermute | solution.py:197
  13.7 1.4 %collective-permute-start.6 = (bf16[48,512]{1,0:T(8,128)(2,1)S(1)}, bf16[48,512]{1,0:T(8,128)(2,1)S(1)}, u32[]{:S(2)}, u32[]{:S(2)}) collective-permute-start(bf16[48,512]{1,0:T(8,128)(2,1)S(1)} %collective-permute-done.1.refs_2_), channel_id=1, source_target_pairs={{0,1},{1,0},{2,3},{3,2},{4,5},{5,4},{6,7},{7,6},{8,9},{9,8},{10,11... | collective-permute-start | bytes 147464 | tf_op jit(solution)/shard_map/ppermute | solution.py:197
  14.2 1.2 %collective-permute-start.5 = (bf16[48,512]{1,0:T(8,128)(2,1)S(1)}, bf16[48,512]{1,0:T(8,128)(2,1)S(1)}, u32[]{:S(2)}, u32[]{:S(2)}) collective-permute-start(bf16[48,512]{1,0:T(8,128)(2,1)S(1)} %collective-permute-done.2.refs_1_), channel_id=1, source_target_pairs={{0,1},{1,0},{2,3},{3,2},{4,5},{5,4},{6,7},{7,6},{8,9},{9,8},{10,11... | collective-permute-start | bytes 147464 | tf_op jit(solution)/shard_map/ppermute | solution.py:197
  16.7 7.0 %collective-permute-start.10 = (bf16[48,512]{1,0:T(8,128)(2,1)S(1)}, bf16[48,512]{1,0:T(8,128)(2,1)S(1)}, u32[]{:S(2)}, u32[]{:S(2)}) collective-permute-start(bf16[48,512]{1,0:T(8,128)(2,1)S(1)} %get-tuple-element.56), channel_id=1, source_target_pairs={{0,14},{1,11},{2,12},{3,9},{4,10},{5,15},{6,8},{7,13},{8,6},{9,3},... | collective-permute-start | bytes 147464 | tf_op jit(solution)/shard_map/ppermute | solution.py:186
  18.3 6.0 %collective-permute-start.9 = (bf16[48,512]{1,0:T(8,128)(2,1)S(1)}, bf16[48,512]{1,0:T(8,128)(2,1)S(1)}, u32[]{:S(2)}, u32[]{:S(2)}) collective-permute-start(bf16[48,512]{1,0:T(8,128)(2,1)S(1)} %get-tuple-element.55), channel_id=1, source_target_pairs={{0,6},{1,13},{2,4},{3,15},{4,2},{5,9},{6,0},{7,11},{8,14},{9,5},{1... | collective-permute-start | bytes 147464 | tf_op jit(solution)/shard_map/ppermute | solution.py:186
  18.3 5.9 %collective-permute-start.8 = (bf16[48,512]{1,0:T(8,128)(2,1)S(1)}, bf16[48,512]{1,0:T(8,128)(2,1)S(1)}, u32[]{:S(2)}, u32[]{:S(2)}) collective-permute-start(bf16[48,512]{1,0:T(8,128)(2,1)S(1)} %get-tuple-element.54), channel_id=1, source_target_pairs={{0,4},{1,9},{2,6},{3,11},{4,0},{5,13},{6,2},{7,15},{8,12},{9,1},{1... | collective-permute-start | bytes 147464 | tf_op jit(solution)/shard_map/ppermute | solution.py:186
  21.2 4.2 %collective-permute-start.11 = (bf16[48,512]{1,0:T(8,128)(2,1)S(1)}, bf16[48,512]{1,0:T(8,128)(2,1)S(1)}, u32[]{:S(2)}, u32[]{:S(2)}) collective-permute-start(bf16[48,512]{1,0:T(8,128)(2,1)S(1)} %get-tuple-element.66), channel_id=1, source_target_pairs={{0,2},{1,3},{2,0},{3,1},{4,6},{5,7},{6,4},{7,5},{8,10},{9,11},{10,... | collective-permute-start | bytes 147464 | tf_op jit(solution)/shard_map/ppermute | solution.py:186
  24.2 1.5 %collective-permute-start.14 = (bf16[48,512]{1,0:T(8,128)(2,1)S(1)}, bf16[48,512]{1,0:T(8,128)(2,1)S(1)}, u32[]{:S(2)}, u32[]{:S(2)}) collective-permute-start(bf16[48,512]{1,0:T(8,128)(2,1)S(1)} %collective-permute-done.8.refs_3_), channel_id=1, source_target_pairs={{0,1},{1,0},{2,3},{3,2},{4,5},{5,4},{6,7},{7,6},{8,9},{9,8},{10,11... | collective-permute-start | bytes 147464 | tf_op jit(solution)/shard_map/ppermute | solution.py:197
  24.8 1.2 %collective-permute-start.13 = (bf16[48,512]{1,0:T(8,128)(2,1)S(1)}, bf16[48,512]{1,0:T(8,128)(2,1)S(1)}, u32[]{:S(2)}, u32[]{:S(2)}) collective-permute-start(bf16[48,512]{1,0:T(8,128)(2,1)S(1)} %collective-permute-done.9.refs_2_), channel_id=1, source_target_pairs={{0,1},{1,0},{2,3},{3,2},{4,5},{5,4},{6,7},{7,6},{8,9},{9,8},{10,11... | collective-permute-start | bytes 147464 | tf_op jit(solution)/shard_map/ppermute | solution.py:197
  24.8 1.4 %collective-permute-start.12 = (bf16[48,512]{1,0:T(8,128)(2,1)S(1)}, bf16[48,512]{1,0:T(8,128)(2,1)S(1)}, u32[]{:S(2)}, u32[]{:S(2)}) collective-permute-start(bf16[48,512]{1,0:T(8,128)(2,1)S(1)} %collective-permute-done.10.refs_1_), channel_id=1, source_target_pairs={{0,1},{1,0},{2,3},{3,2},{4,5},{5,4},{6,7},{7,6},{8,9},{9,8},{10,11... | collective-permute-start | bytes 147464 | tf_op jit(solution)/shard_map/ppermute | solution.py:197

commit v18 on v17

--- a/solution.py
+++ b/solution.py
@@ -84,20 +84,17 @@
 
 
 def stage_kernel(
-    n, picked, start_hbm, chosen_hbm, slot_hbm, count_hbm, g_hbm, x_mine, x_other,
+    n, picked, start_hbm, chosen_hbm, slot_hbm, count_hbm, g_hbm, x_hbm,
     x_ref, kept_ref, start_ref, chosen_ref, slot_ref, count_ref, sems,
 ):
     rows, width = g_hbm.shape
-    half = x_mine.shape[0]
     slots = width // 4
-    me, core = lax.axis_index("dp"), lax.axis_index("tensor")
+    me = lax.axis_index("dp")
     tables = start_all(
         [chosen_hbm, slot_hbm, start_hbm, count_hbm], [chosen_ref, slot_ref, start_ref, count_ref], sems
     )
     gradient = start_all([g_hbm], [kept_ref.at[pl.ds(0, rows)]], sems, 4)
-    mine = pl.ds(pl.multiple_of(core * half, half), half)
-    tokens = start_all([x_mine], [x_ref.at[mine]], sems, 5)
-    x_ref[pl.ds(pl.multiple_of((1 - core) * half, half), half), :] = x_other[...]
+    tokens = start_all([x_hbm], [x_ref], sems, 5)
     wait_all(tables)
     position = lax.broadcasted_iota(i32, (rows, slots), 0)
     group = lax.broadcasted_iota(i32, (rows, slots), 1) // ADAPTER_RANK
@@ -116,6 +113,12 @@
     wait_all(tokens)
 
 
+def join_kernel(x_mine, x_other, x_ref):
+    core, half = lax.axis_index("tensor"), x_mine.shape[0]
+    x_ref[pl.ds(pl.multiple_of(core * half, half), half), :] = x_mine[...]
+    x_ref[pl.ds(pl.multiple_of((1 - core) * half, half), half), :] = x_other[...]
+
+
 def middle_kernel(n, kept_ref, x_ref, *refs):
     count = n // 2 + 1
     got, (dlow_ref, a_ref), send = refs[:n], refs[n : n + 2], refs[n + 2 : n + 2 + count]
@@ -180,7 +183,7 @@
     up_ref[...] = jnp.sum(rows_ref[:, picked:, at].astype(f32), axis=0)
 
 
-def exchange(messages, beside):
+def exchange(messages, tied, beside):
     n = 2 * len(messages)
     got = [
         lax.ppermute(
@@ -190,9 +193,8 @@
         )
         for message, step in zip(messages, steps(n))
     ]
-    for k, (a, b) in enumerate(steps(n)):
-        if a != b:
-            got[k], beside = lax.optimization_barrier((got[k], beside))
+    for k in tied:
+        got[k], beside = lax.optimization_barrier((got[k], beside))
     passed = [
         lax.ppermute(message, "tensor", [(0, 1), (1, 0)])
         for message, (a, b) in zip(got, steps(n))
@@ -244,16 +246,24 @@
     )(*in_hbm(chosen, adapter_slot, down_maps, up_maps))
     sent, x_late = lax.optimization_barrier((sent, inputs))
     x_other = lax.ppermute(x_late, "tensor", [(0, 1), (1, 0)])
-    x, kept = pl.pallas_call(
+    x_mine, kept = pl.pallas_call(
         functools.partial(stage_kernel, n, picked),
-        out_shape=[shape((tok_rows, model_width), bf16), shape((2 * tok_rows, out_width), bf16)],
-        in_specs=[HBM] * 6 + [VMEM],
+        out_shape=[shape(inputs.shape, bf16), shape((2 * tok_rows, out_width), bf16)],
+        in_specs=[HBM] * 6,
         out_specs=[VMEM] * 2,
         scratch_shapes=tables + [dma((6,))],
         compiler_params=params(8),
         cost_estimate=pl.CostEstimate(flops=0, bytes_accessed=1 << 21, transcendentals=0),
-    )(*in_hbm(starts, chosen, adapter_slot, token_count, output_gradient, inputs), x_other)
-    got, kept = exchange(sent, kept)
+    )(*in_hbm(starts, chosen, adapter_slot, token_count, output_gradient, inputs))
+    got, x_mine = exchange(sent, (0,), x_mine)
+    x = pl.pallas_call(
+        join_kernel,
+        out_shape=shape((tok_rows, model_width), bf16),
+        in_specs=[VMEM] * 2,
+        out_specs=VMEM,
+        compiler_params=params(8),
+        cost_estimate=pl.CostEstimate(flops=0, bytes_accessed=1 << 21, transcendentals=0),
+    )(x_mine, x_other)
 
     dlow, a_half, *sent = pl.pallas_call(
         functools.partial(middle_kernel, n),
@@ -283,7 +293,7 @@
         ),
     )(kept, frozen_weight, dlow, a_half)
 
-    got, grad_x = exchange(sent, grad_x)
+    got, grad_x = exchange(sent, (0,), grad_x)
 
     grad_a, up_map_gradient = pl.pallas_call(
         functools.partial(final_kernel, n),

time: 27.4 us -> 26.6 us (0.971)
  waiting for transfers between devices: 3.91 us -> 3.35 us
  starting transfers between devices: 16.3 us -> 15.9 us
    ppermute x6, starting transfers between devices: 1.61 us -> 0.97 us  [exchange(): lax.ppermute(message, 'tensor', [(0, 1), (1, 0)])]
    ppermute x6, waiting for transfers between devices: 2.1 us -> 1.56 us  [exchange(): lax.ppermute(message, 'tensor', [(0, 1), (1, 0)])]
    ppermute x8, starting transfers between devices: 14.1 us -> 14.4 us  [exchange(): lax.ppermute(message, ('dp', 'tensor'), [(2 * i + c, 2 * (i ^ step[c]) +...]
  transfers between devices with their start and end apart: 15 -> 15, of which waited for: 10 -> 11; matrix products, arithmetic and copies ran while one was open for 0% -> 0% of each run, Pallas kernels for 10% -> 11%
where the time goes in v18:
time: 26.6 us; the launch traced here: 26.4 us
  starting transfers between devices  15.9 us (60%)
  Pallas kernels  6.45 us (24%)
  waiting for transfers between devices  3.35 us (13%)
  between operations  0.7 us (3%)
    ppermute x8, starting transfers between devices, exchange(): lax.ppermute(message, ('dp', 'tensor'), [(2 * i + c, 2 * (i ^ step[c]) +...  14.4 us
    ppermute x8, waiting for transfers between devices, exchange(): lax.ppermute(message, ('dp', 'tensor'), [(2 * i + c, 2 * (i ^ step[c]) +...  1.79 us
    pallas_call x1, Pallas kernels, local_kernels(): pl.pallas_call(grad_x_kernel, out_shape=shape((tok_rows, half), bf16), in...  1.64 us
    ppermute x6, waiting for transfers between devices, exchange(): lax.ppermute(message, 'tensor', [(0, 1), (1, 0)])  1.56 us
    pallas_call x1, Pallas kernels, local_kernels(): pl.pallas_call(functools.partial(stage_kernel, n, picked), out_shape=[sha...  1.31 us
    pallas_call x1, Pallas kernels, local_kernels(): pl.pallas_call(functools.partial(middle_kernel, n), out_shape=[shape((tok...  1.25 us
    pallas_call x1, Pallas kernels, local_kernels(): pl.pallas_call(functools.partial(pack_kernel, n), out_shape=[message] * c...  1.15 us
    pallas_call x1, Pallas kernels, local_kernels(): pl.pallas_call(functools.partial(final_kernel, n), out_shape=[shape((colu...  1.01 us
  transfers between devices with their start and end apart: 15, of which 11 were waited for; matrix products, arithmetic and copies ran while one was open for 0% of the time, Pallas kernels for 11%

profile of v18, /device:TPU:0, one launch (start us, length us, event | category | flops | bytes accessed | tf_op | source)
XLA Modules:
  0.0 26.4 jit_solution(14188148942535806234)
XLA Ops:
  0.6 1.2 %shard_map.113 = (bf16[48,512]{1,0:T(8,128)(2,1)S(1)}, bf16[48,512]{1,0:T(8,128)(2,1)S(1)}, bf16[48,512]{1,0:T(8,128)(2,1)S(1)}, bf16[48,512]{1,0:T(8,128)(2,1)S(1)}, bf16[48,512]{1,0:T(8,128)(2,1)S(1)}) custom-call(s32[2,8]{1,0:T(2,128)} %bitcast.2, s32[8]{0:T(128)} %slot_hbm.3, bf16[512,128]{1,0:T(8,128)(2,1)} %down_hbm.1, bf16[16,512]{1,0:T(8,128)(2,1)} %up_hbm.1), custom_call_target="tpu_custom_call" | custom-call | tf_op jit(solution)/shard_map/pallas_call | solution.py:238
  1.8 0.5 %collective-permute-start.1 = (bf16[64,4096]{1,0:T(8,128)(2,1)}, bf16[64,4096]{1,0:T(8,128)(2,1)S(1)}, u32[]{:S(2)}, u32[]{:S(2)}) collective-permute-start(bf16[64,4096]{1,0:T(8,128)(2,1)} %x_hbm.1), channel_id=1, source_target_pairs={{0,1},{1,0},{2,3},{3,2},{4,5},{5,4},{6,7},{7,6},{8,9},{9,8},{10,11... | collective-permute-start | bytes 1572872 | tf_op jit(solution)/shard_map/ppermute | solution.py:248
  2.3 5.6 %collective-permute-start = (bf16[48,512]{1,0:T(8,128)(2,1)S(1)}, bf16[48,512]{1,0:T(8,128)(2,1)S(1)}, u32[]{:S(2)}, u32[]{:S(2)}) collective-permute-start(bf16[48,512]{1,0:T(8,128)(2,1)S(1)} %get-tuple-element.33), channel_id=1, source_target_pairs={{0,14},{1,11},{2,12},{3,9},{4,10},{5,15},{6,8},{7,13},{8,6},{9,3},... | collective-permute-start | bytes 147464 | tf_op jit(solution)/shard_map/ppermute | solution.py:189
  7.9 0.0 collective-permute-start.2
  7.9 2.0 %collective-permute-start.3 = (bf16[48,512]{1,0:T(8,128)(2,1)S(1)}, bf16[48,512]{1,0:T(8,128)(2,1)S(1)}, u32[]{:S(2)}, u32[]{:S(2)}) collective-permute-start(bf16[48,512]{1,0:T(8,128)(2,1)S(1)} %get-tuple-element.40), channel_id=1, source_target_pairs={{0,4},{1,9},{2,6},{3,11},{4,0},{5,13},{6,2},{7,15},{8,12},{9,1},{1... | collective-permute-start | bytes 147464 | tf_op jit(solution)/shard_map/ppermute | solution.py:189
  9.9 1.5 %collective-permute-start.4 = (bf16[48,512]{1,0:T(8,128)(2,1)S(1)}, bf16[48,512]{1,0:T(8,128)(2,1)S(1)}, u32[]{:S(2)}, u32[]{:S(2)}) collective-permute-start(bf16[48,512]{1,0:T(8,128)(2,1)S(1)} %get-tuple-element.41), channel_id=1, source_target_pairs={{0,2},{1,3},{2,0},{3,1},{4,6},{5,7},{6,4},{7,5},{8,10},{9,11},{10,... | collective-permute-start | bytes 147464 | tf_op jit(solution)/shard_map/ppermute | solution.py:189
  11.4 0.0 copy-start
  11.4 1.3 %shard_map.112 = (bf16[64,4096]{1,0:T(8,128)(2,1)S(1)}, bf16[256,512]{1,0:T(8,128)(2,1)S(1)}) custom-call(s32[2,8]{1,0:T(2,128)} %bitcast.4, s32[2,8]{1,0:T(2,128)} %bitcast.3, s32[8]{0:T(128)} %slot_hbm.3, s32[8]{0:T(128)} %count_hbm.1, bf16[128,512]{1,0:T(8,128)(2,1)} %g_hbm.1, bf16[64,4096]{1,0:T(8,128)(2,1)} %x_hbm.1), custom_call_target="tpu_custom_call" | custom-call | bytes 2097152 | tf_op jit(solution)/shard_map/pallas_call | solution.py:249
  12.7 0.0 collective-permute-done.refs_1_
  12.7 0.1 collective-permute-start.5
  12.8 0.2 collective-permute-done.2.refs_2_
  13.0 0.3 %collective-permute-start.6 = (bf16[48,512]{1,0:T(8,128)(2,1)S(1)}, bf16[48,512]{1,0:T(8,128)(2,1)S(1)}, u32[]{:S(2)}, u32[]{:S(2)}) collective-permute-start(bf16[48,512]{1,0:T(8,128)(2,1)S(1)} %collective-permute-done.2.refs_2_), channel_id=1, source_target_pairs={{0,1},{1,0},{2,3},{3,2},{4,5},{5,4},{6,7},{7,6},{8,9},{9,8},{10,11... | collective-permute-start | bytes 147464 | tf_op jit(solution)/shard_map/ppermute | solution.py:199
  13.3 0.2 collective-permute-done.3.refs_3_
  13.6 0.0 collective-permute-start.7
  13.6 0.0 collective-permute-done.1.x_other
  13.6 0.1 shard_map.114.x_ref
  13.6 0.4 %collective-permute-done.4.refs_4_ = bf16[48,512]{1,0:T(8,128)(2,1)S(1)} collective-permute-done((bf16[48,512]{1,0:T(8,128)(2,1)S(1)}, bf16[48,512]{1,0:T(8,128)(2,1)S(1)}, u32[]{:S(2)}, u32[]{:S(2)}) %collective-permute-start.4) | collective-permute-done | bytes 49184 | tf_op jit(solution)/shard_map/ppermute | solution.py:189
  14.0 0.0 collective-permute-done.5.refs_5_
  14.0 0.2 collective-permute-done.6.refs_6_
  14.3 0.5 %collective-permute-done.7.refs_7_ = bf16[48,512]{1,0:T(8,128)(2,1)S(1)} collective-permute-done((bf16[48,512]{1,0:T(8,128)(2,1)S(1)}, bf16[48,512]{1,0:T(8,128)(2,1)S(1)}, u32[]{:S(2)}, u32[]{:S(2)}) %collective-permute-start.7) | collective-permute-done | bytes 49184 | tf_op jit(solution)/shard_map/ppermute | solution.py:199
  14.8 1.3 %shard_map.115 = (bf16[128,32]{1,0:T(8,128)(2,1)S(1)}, bf16[4,32,512]{2,1,0:T(8,128)(2,1)S(1)}, bf16[48,512]{1,0:T(8,128)(2,1)S(1)}, bf16[48,512]{1,0:T(8,128)(2...) custom-call(bf16[256,512]{1,0:T(8,128)(2,1)S(1)} %get-tuple-element.28.kept_ref, ...), custom_call_target="tpu_custom_call" | custom-call | tf_op jit(solution)/shard_map/pallas_call | solution.py:268
  16.0 1.8 %collective-permute-start.8 = (bf16[48,512]{1,0:T(8,128)(2,1)S(1)}, bf16[48,512]{1,0:T(8,128)(2,1)S(1)}, u32[]{:S(2)}, u32[]{:S(2)}) collective-permute-start(bf16[48,512]{1,0:T(8,128)(2,1)S(1)} %get-tuple-element.42), channel_id=1, source_target_pairs={{0,14},{1,11},{2,12},{3,9},{4,10},{5,15},{6,8},{7,13},{8,6},{9,3},... | collective-permute-start | bytes 147464 | tf_op jit(solution)/shard_map/ppermute | solution.py:189
  17.9 0.1 collective-permute-start.9
  18.0 2.5 %collective-permute-start.10 = (bf16[48,512]{1,0:T(8,128)(2,1)S(1)}, bf16[48,512]{1,0:T(8,128)(2,1)S(1)}, u32[]{:S(2)}, u32[]{:S(2)}) collective-permute-start(bf16[48,512]{1,0:T(8,128)(2,1)S(1)} %get-tuple-element.49), channel_id=1, source_target_pairs={{0,4},{1,9},{2,6},{3,11},{4,0},{5,13},{6,2},{7,15},{8,12},{9,1},{1... | collective-permute-start | bytes 147464 | tf_op jit(solution)/shard_map/ppermute | solution.py:189
  20.5 0.8 %collective-permute-start.11 = (bf16[48,512]{1,0:T(8,128)(2,1)S(1)}, bf16[48,512]{1,0:T(8,128)(2,1)S(1)}, u32[]{:S(2)}, u32[]{:S(2)}) collective-permute-start(bf16[48,512]{1,0:T(8,128)(2,1)S(1)} %get-tuple-element.50), channel_id=1, source_target_pairs={{0,2},{1,3},{2,0},{3,1},{4,6},{5,7},{6,4},{7,5},{8,10},{9,11},{10,... | collective-permute-start | bytes 147464 | tf_op jit(solution)/shard_map/ppermute | solution.py:189
  21.4 0.0 copy-done
  21.4 1.6 %shard_map.116 = bf16[128,2048]{1,0:T(8,128)(2,1)} custom-call(bf16[256,512]{1,0:T(8,128)(2,1)S(1)} %get-tuple-element.28.kept_ref, bf16[2048,512]{1,0:T(8,128)(2,1)S(1)} %copy-done, bf16[128,32]{1,0:T(8,128)(2,1)S(1)} %get-tuple-element.43.dlow_ref, bf16[4,32,512]{2,1,0:T(8,128)(2,1)S(1)} %get-tuple-element.44.a_ref), custom_call_target="tpu_custom_call" | custom-call | flops 285212672 | bytes 2621440 | tf_op jit(solution)/shard_map/pallas_call | solution.py:282
  23.0 0.1 collective-permute-done.8.refs_1_
  23.1 0.0 collective-permute-start.12
  23.1 0.6 %collective-permute-done.9.refs_2_ = bf16[48,512]{1,0:T(8,128)(2,1)S(1)} collective-permute-done((bf16[48,512]{1,0:T(8,128)(2,1)S(1)}, bf16[48,512]{1,0:T(8,128)(2,1)S(1)}, u32[]{:S(2)}, u32[]{:S(2)}) %collective-permute-start.9) | collective-permute-done | bytes 49184 | tf_op jit(solution)/shard_map/ppermute | solution.py:189
  23.7 0.0 collective-permute-start.13
  23.7 0.2 collective-permute-done.10.refs_3_
  23.9 0.6 %collective-permute-start.14 = (bf16[48,512]{1,0:T(8,128)(2,1)S(1)}, bf16[48,512]{1,0:T(8,128)(2,1)S(1)}, u32[]{:S(2)}, u32[]{:S(2)}) collective-permute-start(bf16[48,512]{1,0:T(8,128)(2,1)S(1)} %collective-permute-done.10.refs_3_), channel_id=1, source_target_pairs={{0,1},{1,0},{2,3},{3,2},{4,5},{5,4},{6,7},{7,6},{8,9},{9,8},{10,11... | collective-permute-start | bytes 147464 | tf_op jit(solution)/shard_map/ppermute | solution.py:199
  24.5 0.1 collective-permute-done.11.refs_4_
  24.6 0.0 collective-permute-done.12.refs_5_
  24.6 0.3 %collective-permute-done.13.refs_6_ = bf16[48,512]{1,0:T(8,128)(2,1)S(1)} collective-permute-done((bf16[48,512]{1,0:T(8,128)(2,1)S(1)}, bf16[48,512]{1,0:T(8,128)(2,1)S(1)}, u32[]{:S(2)}, u32[]{:S(2)}) %collective-permute-start.13) | collective-permute-done | bytes 49184 | tf_op jit(solution)/shard_map/ppermute | solution.py:199
  24.9 0.5 %collective-permute-done.14.refs_7_ = bf16[48,512]{1,0:T(8,128)(2,1)S(1)} collective-permute-done((bf16[48,512]{1,0:T(8,128)(2,1)S(1)}, bf16[48,512]{1,0:T(8,128)(2,1)S(1)}, u32[]{:S(2)}, u32[]{:S(2)}) %collective-permute-start.14) | collective-permute-done | bytes 49184 | tf_op jit(solution)/shard_map/ppermute | solution.py:199
  25.4 1.0 %shard_map.117 = (f32[512,128]{1,0:T(8,128)}, f32[16,256]{1,0:T(8,128)}) custom-call(bf16[256,512]{1,0:T(8,128)(2,1)S(1)} %get-tuple-element.28.kept_ref, bf16[48,512]{1,0:T(8,128)(2,1)S(1)} %get-tuple-element.46.refs_0_, bf16[48,512]{1,0:T(8,128)(2,1)S(1)} %collective-permute-done.8.refs_1_, bf16[48,512]{1,0:T(8,128)(2,1)S(1)} %collective-permute-done.9.refs_2_, ...), custom_call_target="tpu_custom_call" | custom-call | tf_op jit(solution)/shard_map/pallas_call | solution.py:298
Async XLA Ops:
  1.8 11.8 %collective-permute-start.1 = (bf16[64,4096]{1,0:T(8,128)(2,1)}, bf16[64,4096]{1,0:T(8,128)(2,1)S(1)}, u32[]{:S(2)}, u32[]{:S(2)}) collective-permute-start(bf16[64,4096]{1,0:T(8,128)(2,1)} %x_hbm.1), channel_id=1, source_target_pairs={{0,1},{1,0},{2,3},{3,2},{4,5},{5,4},{6,7},{7,6},{8,9},{9,8},{10,11... | collective-permute-start | bytes 1572872 | tf_op jit(solution)/shard_map/ppermute | solution.py:248
  2.3 10.4 %collective-permute-start = (bf16[48,512]{1,0:T(8,128)(2,1)S(1)}, bf16[48,512]{1,0:T(8,128)(2,1)S(1)}, u32[]{:S(2)}, u32[]{:S(2)}) collective-permute-start(bf16[48,512]{1,0:T(8,128)(2,1)S(1)} %get-tuple-element.33), channel_id=1, source_target_pairs={{0,14},{1,11},{2,12},{3,9},{4,10},{5,15},{6,8},{7,13},{8,6},{9,3},... | collective-permute-start | bytes 147464 | tf_op jit(solution)/shard_map/ppermute | solution.py:189
  7.9 5.1 %collective-permute-start.2 = (bf16[48,512]{1,0:T(8,128)(2,1)S(1)}, bf16[48,512]{1,0:T(8,128)(2,1)S(1)}, u32[]{:S(2)}, u32[]{:S(2)}) collective-permute-start(bf16[48,512]{1,0:T(8,128)(2,1)S(1)} %get-tuple-element.39), channel_id=1, source_target_pairs={{0,6},{1,13},{2,4},{3,15},{4,2},{5,9},{6,0},{7,11},{8,14},{9,5},{1... | collective-permute-start | bytes 147464 | tf_op jit(solution)/shard_map/ppermute | solution.py:189
  7.9 5.6 %collective-permute-start.3 = (bf16[48,512]{1,0:T(8,128)(2,1)S(1)}, bf16[48,512]{1,0:T(8,128)(2,1)S(1)}, u32[]{:S(2)}, u32[]{:S(2)}) collective-permute-start(bf16[48,512]{1,0:T(8,128)(2,1)S(1)} %get-tuple-element.40), channel_id=1, source_target_pairs={{0,4},{1,9},{2,6},{3,11},{4,0},{5,13},{6,2},{7,15},{8,12},{9,1},{1... | collective-permute-start | bytes 147464 | tf_op jit(solution)/shard_map/ppermute | solution.py:189
  9.9 4.1 %collective-permute-start.4 = (bf16[48,512]{1,0:T(8,128)(2,1)S(1)}, bf16[48,512]{1,0:T(8,128)(2,1)S(1)}, u32[]{:S(2)}, u32[]{:S(2)}) collective-permute-start(bf16[48,512]{1,0:T(8,128)(2,1)S(1)} %get-tuple-element.41), channel_id=1, source_target_pairs={{0,2},{1,3},{2,0},{3,1},{4,6},{5,7},{6,4},{7,5},{8,10},{9,11},{10,... | collective-permute-start | bytes 147464 | tf_op jit(solution)/shard_map/ppermute | solution.py:189
  11.4 10.0 %copy-start = (bf16[2048,512]{1,0:T(8,128)(2,1)S(1)}, bf16[2048,512]{1,0:T(8,128)(2,1)}, u32[]{:S(2)}) copy-start(bf16[2048,512]{1,0:T(8,128)(2,1)} %w_ref.1) | copy-start | bytes 6291460
  12.7 1.3 %collective-permute-start.5 = (bf16[48,512]{1,0:T(8,128)(2,1)S(1)}, bf16[48,512]{1,0:T(8,128)(2,1)S(1)}, u32[]{:S(2)}, u32[]{:S(2)}) collective-permute-start(bf16[48,512]{1,0:T(8,128)(2,1)S(1)} %collective-permute-done.refs_1_), channel_id=1, source_target_pairs={{0,1},{1,0},{2,3},{3,2},{4,5},{5,4},{6,7},{7,6},{8,9},{9,8},{10,11... | collective-permute-start | bytes 147464 | tf_op jit(solution)/shard_map/ppermute | solution.py:199
  13.0 1.2 %collective-permute-start.6 = (bf16[48,512]{1,0:T(8,128)(2,1)S(1)}, bf16[48,512]{1,0:T(8,128)(2,1)S(1)}, u32[]{:S(2)}, u32[]{:S(2)}) collective-permute-start(bf16[48,512]{1,0:T(8,128)(2,1)S(1)} %collective-permute-done.2.refs_2_), channel_id=1, source_target_pairs={{0,1},{1,0},{2,3},{3,2},{4,5},{5,4},{6,7},{7,6},{8,9},{9,8},{10,11... | collective-permute-start | bytes 147464 | tf_op jit(solution)/shard_map/ppermute | solution.py:199
  13.6 1.2 %collective-permute-start.7 = (bf16[48,512]{1,0:T(8,128)(2,1)S(1)}, bf16[48,512]{1,0:T(8,128)(2,1)S(1)}, u32[]{:S(2)}, u32[]{:S(2)}) collective-permute-start(bf16[48,512]{1,0:T(8,128)(2,1)S(1)} %collective-permute-done.3.refs_3_), channel_id=1, source_target_pairs={{0,1},{1,0},{2,3},{3,2},{4,5},{5,4},{6,7},{7,6},{8,9},{9,8},{10,11... | collective-permute-start | bytes 147464 | tf_op jit(solution)/shard_map/ppermute | solution.py:199
  16.0 7.1 %collective-permute-start.8 = (bf16[48,512]{1,0:T(8,128)(2,1)S(1)}, bf16[48,512]{1,0:T(8,128)(2,1)S(1)}, u32[]{:S(2)}, u32[]{:S(2)}) collective-permute-start(bf16[48,512]{1,0:T(8,128)(2,1)S(1)} %get-tuple-element.42), channel_id=1, source_target_pairs={{0,14},{1,11},{2,12},{3,9},{4,10},{5,15},{6,8},{7,13},{8,6},{9,3},... | collective-permute-start | bytes 147464 | tf_op jit(solution)/shard_map/ppermute | solution.py:189
  17.9 5.8 %collective-permute-start.9 = (bf16[48,512]{1,0:T(8,128)(2,1)S(1)}, bf16[48,512]{1,0:T(8,128)(2,1)S(1)}, u32[]{:S(2)}, u32[]{:S(2)}) collective-permute-start(bf16[48,512]{1,0:T(8,128)(2,1)S(1)} %get-tuple-element.48), channel_id=1, source_target_pairs={{0,6},{1,13},{2,4},{3,15},{4,2},{5,9},{6,0},{7,11},{8,14},{9,5},{1... | collective-permute-start | bytes 147464 | tf_op jit(solution)/shard_map/ppermute | solution.py:189
  18.0 5.9 %collective-permute-start.10 = (bf16[48,512]{1,0:T(8,128)(2,1)S(1)}, bf16[48,512]{1,0:T(8,128)(2,1)S(1)}, u32[]{:S(2)}, u32[]{:S(2)}) collective-permute-start(bf16[48,512]{1,0:T(8,128)(2,1)S(1)} %get-tuple-element.49), channel_id=1, source_target_pairs={{0,4},{1,9},{2,6},{3,11},{4,0},{5,13},{6,2},{7,15},{8,12},{9,1},{1... | collective-permute-start | bytes 147464 | tf_op jit(solution)/shard_map/ppermute | solution.py:189
  20.5 4.1 %collective-permute-start.11 = (bf16[48,512]{1,0:T(8,128)(2,1)S(1)}, bf16[48,512]{1,0:T(8,128)(2,1)S(1)}, u32[]{:S(2)}, u32[]{:S(2)}) collective-permute-start(bf16[48,512]{1,0:T(8,128)(2,1)S(1)} %get-tuple-element.50), channel_id=1, source_target_pairs={{0,2},{1,3},{2,0},{3,1},{4,6},{5,7},{6,4},{7,5},{8,10},{9,11},{10,... | collective-permute-start | bytes 147464 | tf_op jit(solution)/shard_map/ppermute | solution.py:189
  23.1 1.5 %collective-permute-start.12 = (bf16[48,512]{1,0:T(8,128)(2,1)S(1)}, bf16[48,512]{1,0:T(8,128)(2,1)S(1)}, u32[]{:S(2)}, u32[]{:S(2)}) collective-permute-start(bf16[48,512]{1,0:T(8,128)(2,1)S(1)} %collective-permute-done.8.refs_1_), channel_id=1, source_target_pairs={{0,1},{1,0},{2,3},{3,2},{4,5},{5,4},{6,7},{7,6},{8,9},{9,8},{10,11... | collective-permute-start | bytes 147464 | tf_op jit(solution)/shard_map/ppermute | solution.py:199
  23.7 1.2 %collective-permute-start.13 = (bf16[48,512]{1,0:T(8,128)(2,1)S(1)}, bf16[48,512]{1,0:T(8,128)(2,1)S(1)}, u32[]{:S(2)}, u32[]{:S(2)}) collective-permute-start(bf16[48,512]{1,0:T(8,128)(2,1)S(1)} %collective-permute-done.9.refs_2_), channel_id=1, source_target_pairs={{0,1},{1,0},{2,3},{3,2},{4,5},{5,4},{6,7},{7,6},{8,9},{9,8},{10,11... | collective-permute-start | bytes 147464 | tf_op jit(solution)/shard_map/ppermute | solution.py:199
  23.9 1.5 %collective-permute-start.14 = (bf16[48,512]{1,0:T(8,128)(2,1)S(1)}, bf16[48,512]{1,0:T(8,128)(2,1)S(1)}, u32[]{:S(2)}, u32[]{:S(2)}) collective-permute-start(bf16[48,512]{1,0:T(8,128)(2,1)S(1)} %collective-permute-done.10.refs_3_), channel_id=1, source_target_pairs={{0,1},{1,0},{2,3},{3,2},{4,5},{5,4},{6,7},{7,6},{8,9},{9,8},{10,11... | collective-permute-start | bytes 147464 | tf_op jit(solution)/shard_map/ppermute | solution.py:199

commit v19 on v18

--- a/solution.py
+++ b/solution.py
@@ -113,40 +113,58 @@
     wait_all(tokens)
 
 
-def join_kernel(x_mine, x_other, x_ref):
-    core, half = lax.axis_index("tensor"), x_mine.shape[0]
+def picked_maps(kept_ref, b_ref, picked, ranks, messages):
+    rows, slots = kept_ref.shape[0] // 2, kept_ref.shape[1] // 4
+    b_ref[...] = jnp.zeros(b_ref.shape, bf16)
+    for rank, message in zip(ranks, messages):
+        b_ref[rank] = message[picked:, :]
+    onehot = kept_ref[rows : rows + picked, slots : 2 * slots]
+    return dot(onehot, b_ref[...].reshape(-1, b_ref.shape[2]), 1, 0).astype(bf16)
+
+
+def low_terms(x_ref, picked, ranks, messages):
+    total = jnp.zeros((x_ref.shape[0], picked), f32)
+    for rank, message in zip(ranks, messages):
+        width = message.shape[1]
+        at = pl.ds(pl.multiple_of(rank * width, width), width)
+        total += dot(x_ref[:, at], message[:picked, :], 1, 1)
+    return total
+
+
+def early_kernel(n, picked, kept_ref, x_mine, x_other, *refs):
+    count = n // 2 + 1
+    here, (x_ref, low_ref, dlow_ref, b_ref) = refs[:count], refs[count:]
+    me, core, half = lax.axis_index("dp"), lax.axis_index("tensor"), x_mine.shape[0]
+    ranks = senders(n, me, core)[:count]
     x_ref[pl.ds(pl.multiple_of(core * half, half), half), :] = x_mine[...]
     x_ref[pl.ds(pl.multiple_of((1 - core) * half, half), half), :] = x_other[...]
-
-
-def middle_kernel(n, kept_ref, x_ref, *refs):
+    b_sel = picked_maps(kept_ref, b_ref, picked, ranks, here)
+    dlow_ref[...] = dot(kept_ref[: 2 * half, :], b_sel, 1, 1)
+    low_ref[...] = low_terms(x_ref, picked, ranks, here)
+
+
+def middle_kernel(n, kept_ref, x_ref, low_ref, dlow_part, *refs):
     count = n // 2 + 1
-    got, (dlow_ref, a_ref), send = refs[:n], refs[n : n + 2], refs[n + 2 : n + 2 + count]
-    got_ref, up_ref = refs[n + 2 + count :]
+    got, dlow_ref, send = refs[: n - count], refs[n - count], refs[n - count + 1 : n + 1]
+    b_ref, up_ref = refs[n + 1 :]
     me, core = lax.axis_index("dp"), lax.axis_index("tensor")
     rows, picked = dlow_ref.shape
     width = kept_ref.shape[1]
     slots = width // 4
-    for sender, message in zip(senders(n, me, core), got):
-        got_ref[sender] = message[...]
-
+    ranks = senders(n, me, core)[count:]
     in_seg = kept_ref[rows:, :picked].astype(f32) > 0.0
     g = kept_ref[:rows, :]
     onehot = kept_ref[rows : rows + picked, slots : 2 * slots]
-    up_maps = got_ref[:, picked:, :].reshape(-1, width)
-    b_sel = dot(onehot, up_maps, 1, 0).astype(bf16)
-    dlow = jnp.where(in_seg, adapter_scale * dot(g, b_sel, 1, 1), 0.0).astype(bf16)
+    b_sel = picked_maps(kept_ref, b_ref, picked, ranks, got)
+    dlow = dlow_part[...] + dot(g, b_sel, 1, 1)
+    dlow = jnp.where(in_seg, adapter_scale * dlow, 0.0).astype(bf16)
     dlow_ref[...] = dlow
-    parts = n // 2
-    a_ref[...] = got_ref[pl.ds(pl.multiple_of(core * parts, parts), parts), :picked, :]
     targets = partners(n, me, core)
     for target, message in zip(targets, send):
         at = pl.ds(pl.multiple_of(target * width, width), width)
         message[:picked, :] = dot(dlow, x_ref[:, at], 0, 0).astype(bf16)
 
-    low = jnp.zeros((rows, picked), f32)
-    for q in range(n):
-        low += dot(x_ref[:, q * width : (q + 1) * width], got_ref[q, :picked, :], 1, 1)
+    low = low_ref[...] + low_terms(x_ref, picked, ranks, got)
     low = jnp.where(in_seg, low, 0.0).astype(bf16)
     low_wide = dot(low, onehot, 1, 0).astype(bf16)
     up = (adapter_scale * dot(low_wide, g, 0, 0)).astype(bf16)
@@ -155,13 +173,17 @@
         message[picked:, :] = up_ref[target]
 
 
-def grad_x_kernel(kept_ref, w_ref, dlow_ref, a_ref, out_hbm, out_ref, sems):
-    steps, picked, width = a_ref.shape
+def grad_x_kernel(n, kept_ref, w_ref, dlow_ref, *refs):
+    got, (out_hbm, a_ref, out_ref, sems) = refs[:n], refs[n:]
+    me, core = lax.axis_index("dp"), lax.axis_index("tensor")
+    picked, width = a_ref.shape[1:]
+    for sender, message in zip(senders(n, me, core), got):
+        a_ref[sender] = message[:picked, :]
     g = kept_ref[: out_ref.shape[0], :]
     done = []
-    for j in range(steps):
+    for j in range(n // 2):
         at = pl.ds(j * width, width)
-        total = dot(g, w_ref[at, :], 1, 1) + dot(dlow_ref[...], a_ref[j], 1, 0)
+        total = dot(g, w_ref[at, :], 1, 1) + dot(dlow_ref[...], a_ref[core * (n // 2) + j], 1, 0)
         out_ref[:, at] = total.astype(bf16)
         done += start_all([out_ref.at[:, at]], [out_hbm.at[:, at]], sems, j)
     wait_all(done)
@@ -256,42 +278,46 @@
         cost_estimate=pl.CostEstimate(flops=0, bytes_accessed=1 << 21, transcendentals=0),
     )(*in_hbm(starts, chosen, adapter_slot, token_count, output_gradient, inputs))
     got, x_mine = exchange(sent, (0,), x_mine)
-    x = pl.pallas_call(
-        join_kernel,
-        out_shape=shape((tok_rows, model_width), bf16),
-        in_specs=[VMEM] * 2,
-        out_specs=VMEM,
+    low = shape((tok_rows, picked), f32)
+    maps = pltpu.VMEM((n, ADAPTER_RANK, out_width), bf16)
+    got = [own] + got
+    x, low, dlow = pl.pallas_call(
+        functools.partial(early_kernel, n, picked),
+        out_shape=[shape((tok_rows, model_width), bf16), low, low],
+        in_specs=[VMEM] * (3 + count),
+        out_specs=[VMEM] * 3,
+        scratch_shapes=[maps],
         compiler_params=params(8),
         cost_estimate=pl.CostEstimate(flops=0, bytes_accessed=1 << 21, transcendentals=0),
-    )(x_mine, x_other)
-
-    dlow, a_half, *sent = pl.pallas_call(
+    )(kept, x_mine, x_other, *got[:count])
+
+    dlow, *sent = pl.pallas_call(
         functools.partial(middle_kernel, n),
-        out_shape=[shape((tok_rows, picked), bf16), shape((n // 2, picked, column_total), bf16)]
-        + [message] * count,
-        in_specs=[VMEM] * (2 + n),
-        out_specs=[VMEM] * (2 + count),
+        out_shape=[shape((tok_rows, picked), bf16)] + [message] * count,
+        in_specs=[VMEM] * (4 + n - count),
+        out_specs=[VMEM] * (1 + count),
+        scratch_shapes=[maps, maps],
+        compiler_params=params(8),
+    )(kept, x, low, dlow, *got[count:])
+    own, *sent = sent
+
+    grad_x = pl.pallas_call(
+        functools.partial(grad_x_kernel, n),
+        out_shape=shape((tok_rows, half), bf16),
+        in_specs=[VMEM] * (3 + n),
+        out_specs=HBM,
         scratch_shapes=[
-            pltpu.VMEM((n,) + message.shape, bf16),
-            pltpu.VMEM((n, ADAPTER_RANK, out_width), bf16),
+            pltpu.VMEM((n, picked, column_total), bf16),
+            pltpu.VMEM((tok_rows, half), bf16),
+            dma((n // 2,)),
         ],
-        compiler_params=params(8),
-    )(kept, x, own, *got)
-    own, *sent = sent
-
-    grad_x = pl.pallas_call(
-        grad_x_kernel,
-        out_shape=shape((tok_rows, half), bf16),
-        in_specs=[VMEM] * 4,
-        out_specs=HBM,
-        scratch_shapes=[pltpu.VMEM((tok_rows, half), bf16), dma((n // 2,))],
         compiler_params=params(8),
         cost_estimate=pl.CostEstimate(
             flops=2 * tok_rows * half * (out_width + picked),
             bytes_accessed=2 * half * (out_width + tok_rows),
             transcendentals=0,
         ),
-    )(kept, frozen_weight, dlow, a_half)
+    )(kept, frozen_weight, dlow, *got)
 
     got, grad_x = exchange(sent, (0,), grad_x)
 

time: 26.6 us -> 26.5 us (level)
    ppermute x6, waiting for transfers between devices: 1.56 us -> 1.03 us  [exchange(): lax.ppermute(message, 'tensor', [(0, 1), (1, 0)])]
    pallas_call x2, Pallas kernels: 1.72 us -> 2.17 us  [the longest x1 1.67 us: local_kernels(): pl.pallas_call(functools.partial(grad_x_kernel, n), out_shape=shape((tok_...]
    ppermute x8, waiting for transfers between devices: 1.79 us -> 2.15 us  [exchange(): lax.ppermute(message, ('dp', 'tensor'), [(2 * i + c, 2 * (i ^ step[c]) +...]
  transfers between devices with their start and end apart: 15 -> 15, of which waited for: 11 -> 9; matrix products, arithmetic and copies ran while one was open for 0% -> 0% of each run, Pallas kernels for 11% -> 13%
where the time goes in v19:
time: 26.5 us; the launch traced here: 26.3 us
  starting transfers between devices  15.7 us (59%)
  Pallas kernels  6.65 us (25%)
  waiting for transfers between devices  3.18 us (12%)
  between operations  0.73 us (3%)
    ppermute x8, starting transfers between devices, exchange(): lax.ppermute(message, ('dp', 'tensor'), [(2 * i + c, 2 * (i ^ step[c]) +...  14.4 us
    ppermute x8, waiting for transfers between devices, exchange(): lax.ppermute(message, ('dp', 'tensor'), [(2 * i + c, 2 * (i ^ step[c]) +...  2.15 us
    pallas_call x1, Pallas kernels, local_kernels(): pl.pallas_call(functools.partial(grad_x_kernel, n), out_shape=shape((tok_...  1.67 us
    pallas_call x1, Pallas kernels, local_kernels(): pl.pallas_call(functools.partial(pack_kernel, n), out_shape=[message] * c...  1.3 us
    pallas_call x1, Pallas kernels, local_kernels(): pl.pallas_call(functools.partial(stage_kernel, n, picked), out_shape=[sha...  1.17 us
    ppermute x6, waiting for transfers between devices, exchange(): lax.ppermute(message, 'tensor', [(0, 1), (1, 0)])  1.03 us
    pallas_call x1, Pallas kernels, local_kernels(): pl.pallas_call(functools.partial(final_kernel, n), out_shape=[shape((colu...  1.01 us
    pallas_call x1, Pallas kernels, local_kernels(): pl.pallas_call(functools.partial(middle_kernel, n), out_shape=[shape((tok...  1 us
  transfers between devices with their start and end apart: 15, of which 9 were waited for; matrix products, arithmetic and copies ran while one was open for 0% of the time, Pallas kernels for 13%

profile of v19, /device:TPU:0, one launch (start us, length us, event | category | flops | bytes accessed | tf_op | source)
XLA Modules:
  0.0 26.3 jit_solution(10065758658202424967)
XLA Ops:
  0.6 0.0 copy-start
  0.6 1.3 %shard_map.113 = (bf16[48,512]{1,0:T(8,128)(2,1)S(1)}, bf16[48,512]{1,0:T(8,128)(2,1)S(1)}, bf16[48,512]{1,0:T(8,128)(2,1)S(1)}, bf16[48,512]{1,0:T(8,128)(2,1)S(1)}, bf16[48,512]{1,0:T(8,128)(2,1)S(1)}) custom-call(s32[2,8]{1,0:T(2,128)} %bitcast.2, s32[8]{0:T(128)} %slot_hbm.3, bf16[512,128]{1,0:T(8,128)(2,1)} %down_hbm.1, bf16[16,512]{1,0:T(8,128)(2,1)} %up_hbm.1), custom_call_target="tpu_custom_call" | custom-call | tf_op jit(solution)/shard_map/pallas_call | solution.py:260
  2.0 0.5 %collective-permute-start.1 = (bf16[64,4096]{1,0:T(8,128)(2,1)}, bf16[64,4096]{1,0:T(8,128)(2,1)S(1)}, u32[]{:S(2)}, u32[]{:S(2)}) collective-permute-start(bf16[64,4096]{1,0:T(8,128)(2,1)} %x_hbm.1), channel_id=1, source_target_pairs={{0,1},{1,0},{2,3},{3,2},{4,5},{5,4},{6,7},{7,6},{8,9},{9,8},{10,11... | collective-permute-start | bytes 1572872 | tf_op jit(solution)/shard_map/ppermute | solution.py:270
  2.5 5.6 %collective-permute-start = (bf16[48,512]{1,0:T(8,128)(2,1)S(1)}, bf16[48,512]{1,0:T(8,128)(2,1)S(1)}, u32[]{:S(2)}, u32[]{:S(2)}) collective-permute-start(bf16[48,512]{1,0:T(8,128)(2,1)S(1)} %get-tuple-element.35), channel_id=1, source_target_pairs={{0,14},{1,11},{2,12},{3,9},{4,10},{5,15},{6,8},{7,13},{8,6},{9,3},... | collective-permute-start | bytes 147464 | tf_op jit(solution)/shard_map/ppermute | solution.py:211
  8.1 0.0 collective-permute-start.2
  8.1 2.0 %collective-permute-start.3 = (bf16[48,512]{1,0:T(8,128)(2,1)S(1)}, bf16[48,512]{1,0:T(8,128)(2,1)S(1)}, u32[]{:S(2)}, u32[]{:S(2)}) collective-permute-start(bf16[48,512]{1,0:T(8,128)(2,1)S(1)} %get-tuple-element.42), channel_id=1, source_target_pairs={{0,4},{1,9},{2,6},{3,11},{4,0},{5,13},{6,2},{7,15},{8,12},{9,1},{1... | collective-permute-start | bytes 147464 | tf_op jit(solution)/shard_map/ppermute | solution.py:211
  10.1 1.5 %collective-permute-start.4 = (bf16[48,512]{1,0:T(8,128)(2,1)S(1)}, bf16[48,512]{1,0:T(8,128)(2,1)S(1)}, u32[]{:S(2)}, u32[]{:S(2)}) collective-permute-start(bf16[48,512]{1,0:T(8,128)(2,1)S(1)} %get-tuple-element.43), channel_id=1, source_target_pairs={{0,2},{1,3},{2,0},{3,1},{4,6},{5,7},{6,4},{7,5},{8,10},{9,11},{10,... | collective-permute-start | bytes 147464 | tf_op jit(solution)/shard_map/ppermute | solution.py:211
  11.6 1.2 %shard_map.112 = (bf16[64,4096]{1,0:T(8,128)(2,1)S(1)}, bf16[256,512]{1,0:T(8,128)(2,1)S(1)}) custom-call(s32[2,8]{1,0:T(2,128)} %bitcast.4, s32[2,8]{1,0:T(2,128)} %bitcast.3, s32[8]{0:T(128)} %slot_hbm.3, s32[8]{0:T(128)} %count_hbm.1, bf16[128,512]{1,0:T(8,128)(2,1)} %g_hbm.1, bf16[64,4096]{1,0:T(8,128)(2,1)} %x_hbm.1), custom_call_target="tpu_custom_call" | custom-call | bytes 2097152 | tf_op jit(solution)/shard_map/pallas_call | solution.py:271
  12.7 0.0 collective-permute-done.refs_1_
  12.7 0.1 collective-permute-start.5
  12.8 0.4 %collective-permute-done.2.refs_2_ = bf16[48,512]{1,0:T(8,128)(2,1)S(1)} collective-permute-done((bf16[48,512]{1,0:T(8,128)(2,1)S(1)}, bf16[48,512]{1,0:T(8,128)(2,1)S(1)}, u32[]{:S(2)}, u32[]{:S(2)}) %collective-permute-start.2) | collective-permute-done | bytes 49184 | tf_op jit(solution)/shard_map/ppermute | solution.py:211
  13.2 0.1 collective-permute-start.6
  13.3 0.4 %collective-permute-done.3.refs_3_ = bf16[48,512]{1,0:T(8,128)(2,1)S(1)} collective-permute-done((bf16[48,512]{1,0:T(8,128)(2,1)S(1)}, bf16[48,512]{1,0:T(8,128)(2,1)S(1)}, u32[]{:S(2)}, u32[]{:S(2)}) %collective-permute-start.3) | collective-permute-done | bytes 49184 | tf_op jit(solution)/shard_map/ppermute | solution.py:211
  13.7 0.0 collective-permute-start.7
  13.7 0.4 %collective-permute-done.4.refs_4_ = bf16[48,512]{1,0:T(8,128)(2,1)S(1)} collective-permute-done((bf16[48,512]{1,0:T(8,128)(2,1)S(1)}, bf16[48,512]{1,0:T(8,128)(2,1)S(1)}, u32[]{:S(2)}, u32[]{:S(2)}) %collective-permute-start.4) | collective-permute-done | bytes 49184 | tf_op jit(solution)/shard_map/ppermute | solution.py:211
  14.2 0.0 collective-permute-done.1.x_other
  14.2 0.5 %shard_map.114 = (bf16[128,4096]{1,0:T(8,128)(2,1)S(1)}, f32[128,32]{1,0:T(8,128)S(1)}, f32[128,32]{1,0:T(8,128)S(1)}) custom-call(bf16[256,512]{1,0:T(8,128)(2,1)S(1)} %get-tuple-element.30.kept_ref, bf16[64,4096]{1,0:T(8,128)(2,1)S(1)} %get-tuple-element.37.x_mine, bf16[64,4096]{1,0:T(8,128)(2,1)S(1)} %collective-permute-done.1.x_other, ...), custom_call_target="tpu_custom_call" | custom-call | bytes 2097152 | tf_op jit(solution)/shard_map/pallas_call | solution.py:284
  14.7 0.0 collective-permute-done.5.refs_0_.refs_5_
  14.7 0.0 collective-permute-done.6.refs_1_.refs_6_
  14.7 0.2 collective-permute-done.7.refs_2_.refs_7_
  14.9 1.0 %shard_map.115 = (bf16[128,32]{1,0:T(8,128)(2,1)S(1)}, bf16[48,512]{1,0:T(8,128)(2,1)S(1)}, bf16[48,512]{1,0:T(8,128)(2,1)S(1)}, bf16[48,512]{1,0:T(8,128)(2,1)S...) custom-call(bf16[256,512]{1,0:T(8,128)(2,1)S(1)} %get-tuple-element.30.kept_ref, ...), custom_call_target="tpu_custom_call" | custom-call | tf_op jit(solution)/shard_map/pallas_call | solution.py:294
  15.9 1.9 %collective-permute-start.8 = (bf16[48,512]{1,0:T(8,128)(2,1)S(1)}, bf16[48,512]{1,0:T(8,128)(2,1)S(1)}, u32[]{:S(2)}, u32[]{:S(2)}) collective-permute-start(bf16[48,512]{1,0:T(8,128)(2,1)S(1)} %get-tuple-element.47), channel_id=1, source_target_pairs={{0,14},{1,11},{2,12},{3,9},{4,10},{5,15},{6,8},{7,13},{8,6},{9,3},... | collective-permute-start | bytes 147464 | tf_op jit(solution)/shard_map/ppermute | solution.py:211
  17.8 0.1 collective-permute-start.9
  17.9 2.5 %collective-permute-start.10 = (bf16[48,512]{1,0:T(8,128)(2,1)S(1)}, bf16[48,512]{1,0:T(8,128)(2,1)S(1)}, u32[]{:S(2)}, u32[]{:S(2)}) collective-permute-start(bf16[48,512]{1,0:T(8,128)(2,1)S(1)} %get-tuple-element.53), channel_id=1, source_target_pairs={{0,4},{1,9},{2,6},{3,11},{4,0},{5,13},{6,2},{7,15},{8,12},{9,1},{1... | collective-permute-start | bytes 147464 | tf_op jit(solution)/shard_map/ppermute | solution.py:211
  20.4 0.8 %collective-permute-start.11 = (bf16[48,512]{1,0:T(8,128)(2,1)S(1)}, bf16[48,512]{1,0:T(8,128)(2,1)S(1)}, u32[]{:S(2)}, u32[]{:S(2)}) collective-permute-start(bf16[48,512]{1,0:T(8,128)(2,1)S(1)} %get-tuple-element.54), channel_id=1, source_target_pairs={{0,2},{1,3},{2,0},{3,1},{4,6},{5,7},{6,4},{7,5},{8,10},{9,11},{10,... | collective-permute-start | bytes 147464 | tf_op jit(solution)/shard_map/ppermute | solution.py:211
  21.3 0.0 copy-done
  21.3 1.7 %shard_map.116 = bf16[128,2048]{1,0:T(8,128)(2,1)} custom-call(bf16[256,512]{1,0:T(8,128)(2,1)S(1)} %get-tuple-element.30.kept_ref, bf16[2048,512]{1,0:T(8,128)(2,1)S(1)} %copy-done, bf16[128,32]{1,0:T(8,128)(2,1)S(1)} %get-tuple-element.48.dlow_ref, bf16[48,512]{1,0:T(8,128)(2,1)S(1)} %get-tuple-element.39.refs_0_, ...), custom_call_target="tpu_custom_call" | custom-call | flops 285212672 | bytes 2621440 | tf_op jit(solution)/shard_map/pallas_call | solution.py:304
  23.0 0.0 collective-permute-done.8.refs_1_
  23.0 0.0 collective-permute-start.12
  23.1 0.6 %collective-permute-done.9.refs_2_ = bf16[48,512]{1,0:T(8,128)(2,1)S(1)} collective-permute-done((bf16[48,512]{1,0:T(8,128)(2,1)S(1)}, bf16[48,512]{1,0:T(8,128)(2,1)S(1)}, u32[]{:S(2)}, u32[]{:S(2)}) %collective-permute-start.9) | collective-permute-done | bytes 49184 | tf_op jit(solution)/shard_map/ppermute | solution.py:211
  23.6 0.0 collective-permute-start.13
  23.6 0.2 collective-permute-done.10.refs_3_
  23.9 0.6 %collective-permute-start.14 = (bf16[48,512]{1,0:T(8,128)(2,1)S(1)}, bf16[48,512]{1,0:T(8,128)(2,1)S(1)}, u32[]{:S(2)}, u32[]{:S(2)}) collective-permute-start(bf16[48,512]{1,0:T(8,128)(2,1)S(1)} %collective-permute-done.10.refs_3_), channel_id=1, source_target_pairs={{0,1},{1,0},{2,3},{3,2},{4,5},{5,4},{6,7},{7,6},{8,9},{9,8},{10,11... | collective-permute-start | bytes 147464 | tf_op jit(solution)/shard_map/ppermute | solution.py:221
  24.4 0.1 collective-permute-done.11.refs_4_
  24.5 0.0 collective-permute-done.12.refs_5_
  24.5 0.3 %collective-permute-done.13.refs_6_ = bf16[48,512]{1,0:T(8,128)(2,1)S(1)} collective-permute-done((bf16[48,512]{1,0:T(8,128)(2,1)S(1)}, bf16[48,512]{1,0:T(8,128)(2,1)S(1)}, u32[]{:S(2)}, u32[]{:S(2)}) %collective-permute-start.13) | collective-permute-done | bytes 49184 | tf_op jit(solution)/shard_map/ppermute | solution.py:221
  24.9 0.4 %collective-permute-done.14.refs_7_ = bf16[48,512]{1,0:T(8,128)(2,1)S(1)} collective-permute-done((bf16[48,512]{1,0:T(8,128)(2,1)S(1)}, bf16[48,512]{1,0:T(8,128)(2,1)S(1)}, u32[]{:S(2)}, u32[]{:S(2)}) %collective-permute-start.14) | collective-permute-done | bytes 49184 | tf_op jit(solution)/shard_map/ppermute | solution.py:221
  25.3 1.0 %shard_map.117 = (f32[512,128]{1,0:T(8,128)}, f32[16,256]{1,0:T(8,128)}) custom-call(bf16[256,512]{1,0:T(8,128)(2,1)S(1)} %get-tuple-element.30.kept_ref, bf16[48,512]{1,0:T(8,128)(2,1)S(1)} %get-tuple-element.50.refs_0_, bf16[48,512]{1,0:T(8,128)(2,1)S(1)} %collective-permute-done.8.refs_1_, bf16[48,512]{1,0:T(8,128)(2,1)S(1)} %collective-permute-done.9.refs_2_, ...), custom_call_target="tpu_custom_call" | custom-call | tf_op jit(solution)/shard_map/pallas_call | solution.py:324
Async XLA Ops:
  0.6 20.7 %copy-start = (bf16[2048,512]{1,0:T(8,128)(2,1)S(1)}, bf16[2048,512]{1,0:T(8,128)(2,1)}, u32[]{:S(2)}) copy-start(bf16[2048,512]{1,0:T(8,128)(2,1)} %w_ref.1) | copy-start | bytes 6291460
  2.0 12.2 %collective-permute-start.1 = (bf16[64,4096]{1,0:T(8,128)(2,1)}, bf16[64,4096]{1,0:T(8,128)(2,1)S(1)}, u32[]{:S(2)}, u32[]{:S(2)}) collective-permute-start(bf16[64,4096]{1,0:T(8,128)(2,1)} %x_hbm.1), channel_id=1, source_target_pairs={{0,1},{1,0},{2,3},{3,2},{4,5},{5,4},{6,7},{7,6},{8,9},{9,8},{10,11... | collective-permute-start | bytes 1572872 | tf_op jit(solution)/shard_map/ppermute | solution.py:270
  2.5 10.3 %collective-permute-start = (bf16[48,512]{1,0:T(8,128)(2,1)S(1)}, bf16[48,512]{1,0:T(8,128)(2,1)S(1)}, u32[]{:S(2)}, u32[]{:S(2)}) collective-permute-start(bf16[48,512]{1,0:T(8,128)(2,1)S(1)} %get-tuple-element.35), channel_id=1, source_target_pairs={{0,14},{1,11},{2,12},{3,9},{4,10},{5,15},{6,8},{7,13},{8,6},{9,3},... | collective-permute-start | bytes 147464 | tf_op jit(solution)/shard_map/ppermute | solution.py:211
  8.1 5.1 %collective-permute-start.2 = (bf16[48,512]{1,0:T(8,128)(2,1)S(1)}, bf16[48,512]{1,0:T(8,128)(2,1)S(1)}, u32[]{:S(2)}, u32[]{:S(2)}) collective-permute-start(bf16[48,512]{1,0:T(8,128)(2,1)S(1)} %get-tuple-element.41), channel_id=1, source_target_pairs={{0,6},{1,13},{2,4},{3,15},{4,2},{5,9},{6,0},{7,11},{8,14},{9,5},{1... | collective-permute-start | bytes 147464 | tf_op jit(solution)/shard_map/ppermute | solution.py:211
  8.1 5.6 %collective-permute-start.3 = (bf16[48,512]{1,0:T(8,128)(2,1)S(1)}, bf16[48,512]{1,0:T(8,128)(2,1)S(1)}, u32[]{:S(2)}, u32[]{:S(2)}) collective-permute-start(bf16[48,512]{1,0:T(8,128)(2,1)S(1)} %get-tuple-element.42), channel_id=1, source_target_pairs={{0,4},{1,9},{2,6},{3,11},{4,0},{5,13},{6,2},{7,15},{8,12},{9,1},{1... | collective-permute-start | bytes 147464 | tf_op jit(solution)/shard_map/ppermute | solution.py:211
  10.1 4.1 %collective-permute-start.4 = (bf16[48,512]{1,0:T(8,128)(2,1)S(1)}, bf16[48,512]{1,0:T(8,128)(2,1)S(1)}, u32[]{:S(2)}, u32[]{:S(2)}) collective-permute-start(bf16[48,512]{1,0:T(8,128)(2,1)S(1)} %get-tuple-element.43), channel_id=1, source_target_pairs={{0,2},{1,3},{2,0},{3,1},{4,6},{5,7},{6,4},{7,5},{8,10},{9,11},{10,... | collective-permute-start | bytes 147464 | tf_op jit(solution)/shard_map/ppermute | solution.py:211
  12.7 1.9 %collective-permute-start.5 = (bf16[48,512]{1,0:T(8,128)(2,1)S(1)}, bf16[48,512]{1,0:T(8,128)(2,1)S(1)}, u32[]{:S(2)}, u32[]{:S(2)}) collective-permute-start(bf16[48,512]{1,0:T(8,128)(2,1)S(1)} %collective-permute-done.refs_1_), channel_id=1, source_target_pairs={{0,1},{1,0},{2,3},{3,2},{4,5},{5,4},{6,7},{7,6},{8,9},{9,8},{10,11... | collective-permute-start | bytes 147464 | tf_op jit(solution)/shard_map/ppermute | solution.py:221
  13.2 1.5 %collective-permute-start.6 = (bf16[48,512]{1,0:T(8,128)(2,1)S(1)}, bf16[48,512]{1,0:T(8,128)(2,1)S(1)}, u32[]{:S(2)}, u32[]{:S(2)}) collective-permute-start(bf16[48,512]{1,0:T(8,128)(2,1)S(1)} %collective-permute-done.2.refs_2_), channel_id=1, source_target_pairs={{0,1},{1,0},{2,3},{3,2},{4,5},{5,4},{6,7},{7,6},{8,9},{9,8},{10,11... | collective-permute-start | bytes 147464 | tf_op jit(solution)/shard_map/ppermute | solution.py:221
  13.7 1.2 %collective-permute-start.7 = (bf16[48,512]{1,0:T(8,128)(2,1)S(1)}, bf16[48,512]{1,0:T(8,128)(2,1)S(1)}, u32[]{:S(2)}, u32[]{:S(2)}) collective-permute-start(bf16[48,512]{1,0:T(8,128)(2,1)S(1)} %collective-permute-done.3.refs_3_), channel_id=1, source_target_pairs={{0,1},{1,0},{2,3},{3,2},{4,5},{5,4},{6,7},{7,6},{8,9},{9,8},{10,11... | collective-permute-start | bytes 147464 | tf_op jit(solution)/shard_map/ppermute | solution.py:221
  15.9 7.1 %collective-permute-start.8 = (bf16[48,512]{1,0:T(8,128)(2,1)S(1)}, bf16[48,512]{1,0:T(8,128)(2,1)S(1)}, u32[]{:S(2)}, u32[]{:S(2)}) collective-permute-start(bf16[48,512]{1,0:T(8,128)(2,1)S(1)} %get-tuple-element.47), channel_id=1, source_target_pairs={{0,14},{1,11},{2,12},{3,9},{4,10},{5,15},{6,8},{7,13},{8,6},{9,3},... | collective-permute-start | bytes 147464 | tf_op jit(solution)/shard_map/ppermute | solution.py:211
  17.8 5.8 %collective-permute-start.9 = (bf16[48,512]{1,0:T(8,128)(2,1)S(1)}, bf16[48,512]{1,0:T(8,128)(2,1)S(1)}, u32[]{:S(2)}, u32[]{:S(2)}) collective-permute-start(bf16[48,512]{1,0:T(8,128)(2,1)S(1)} %get-tuple-element.52), channel_id=1, source_target_pairs={{0,6},{1,13},{2,4},{3,15},{4,2},{5,9},{6,0},{7,11},{8,14},{9,5},{1... | collective-permute-start | bytes 147464 | tf_op jit(solution)/shard_map/ppermute | solution.py:211
  17.9 6.0 %collective-permute-start.10 = (bf16[48,512]{1,0:T(8,128)(2,1)S(1)}, bf16[48,512]{1,0:T(8,128)(2,1)S(1)}, u32[]{:S(2)}, u32[]{:S(2)}) collective-permute-start(bf16[48,512]{1,0:T(8,128)(2,1)S(1)} %get-tuple-element.53), channel_id=1, source_target_pairs={{0,4},{1,9},{2,6},{3,11},{4,0},{5,13},{6,2},{7,15},{8,12},{9,1},{1... | collective-permute-start | bytes 147464 | tf_op jit(solution)/shard_map/ppermute | solution.py:211
  20.4 4.1 %collective-permute-start.11 = (bf16[48,512]{1,0:T(8,128)(2,1)S(1)}, bf16[48,512]{1,0:T(8,128)(2,1)S(1)}, u32[]{:S(2)}, u32[]{:S(2)}) collective-permute-start(bf16[48,512]{1,0:T(8,128)(2,1)S(1)} %get-tuple-element.54), channel_id=1, source_target_pairs={{0,2},{1,3},{2,0},{3,1},{4,6},{5,7},{6,4},{7,5},{8,10},{9,11},{10,... | collective-permute-start | bytes 147464 | tf_op jit(solution)/shard_map/ppermute | solution.py:211
  23.0 1.5 %collective-permute-start.12 = (bf16[48,512]{1,0:T(8,128)(2,1)S(1)}, bf16[48,512]{1,0:T(8,128)(2,1)S(1)}, u32[]{:S(2)}, u32[]{:S(2)}) collective-permute-start(bf16[48,512]{1,0:T(8,128)(2,1)S(1)} %collective-permute-done.8.refs_1_), channel_id=1, source_target_pairs={{0,1},{1,0},{2,3},{3,2},{4,5},{5,4},{6,7},{7,6},{8,9},{9,8},{10,11... | collective-permute-start | bytes 147464 | tf_op jit(solution)/shard_map/ppermute | solution.py:221
  23.6 1.2 %collective-permute-start.13 = (bf16[48,512]{1,0:T(8,128)(2,1)S(1)}, bf16[48,512]{1,0:T(8,128)(2,1)S(1)}, u32[]{:S(2)}, u32[]{:S(2)}) collective-permute-start(bf16[48,512]{1,0:T(8,128)(2,1)S(1)} %collective-permute-done.9.refs_2_), channel_id=1, source_target_pairs={{0,1},{1,0},{2,3},{3,2},{4,5},{5,4},{6,7},{7,6},{8,9},{9,8},{10,11... | collective-permute-start | bytes 147464 | tf_op jit(solution)/shard_map/ppermute | solution.py:221
  23.9 1.4 %collective-permute-start.14 = (bf16[48,512]{1,0:T(8,128)(2,1)S(1)}, bf16[48,512]{1,0:T(8,128)(2,1)S(1)}, u32[]{:S(2)}, u32[]{:S(2)}) collective-permute-start(bf16[48,512]{1,0:T(8,128)(2,1)S(1)} %collective-permute-done.10.refs_3_), channel_id=1, source_target_pairs={{0,1},{1,0},{2,3},{3,2},{4,5},{5,4},{6,7},{7,6},{8,9},{9,8},{10,11... | collective-permute-start | bytes 147464 | tf_op jit(solution)/shard_map/ppermute | solution.py:221

commit v20 on v19

--- a/solution.py
+++ b/solution.py
@@ -84,7 +84,7 @@
 
 
 def stage_kernel(
-    n, picked, start_hbm, chosen_hbm, slot_hbm, count_hbm, g_hbm, x_hbm,
+    n, picked, start_hbm, chosen_hbm, slot_hbm, count_hbm, g_hbm, x_hbm, w_hbm,
     x_ref, kept_ref, start_ref, chosen_ref, slot_ref, count_ref, sems,
 ):
     rows, width = g_hbm.shape
@@ -271,12 +271,12 @@
     x_mine, kept = pl.pallas_call(
         functools.partial(stage_kernel, n, picked),
         out_shape=[shape(inputs.shape, bf16), shape((2 * tok_rows, out_width), bf16)],
-        in_specs=[HBM] * 6,
+        in_specs=[HBM] * 7,
         out_specs=[VMEM] * 2,
         scratch_shapes=tables + [dma((6,))],
         compiler_params=params(8),
         cost_estimate=pl.CostEstimate(flops=0, bytes_accessed=1 << 21, transcendentals=0),
-    )(*in_hbm(starts, chosen, adapter_slot, token_count, output_gradient, inputs))
+    )(*in_hbm(starts, chosen, adapter_slot, token_count, output_gradient, inputs, frozen_weight))
     got, x_mine = exchange(sent, (0,), x_mine)
     low = shape((tok_rows, picked), f32)
     maps = pltpu.VMEM((n, ADAPTER_RANK, out_width), bf16)

time: 26.5 us -> 26.4 us (level)
  no operation moved by 1% of the time
where the time goes in v20:
time: 26.4 us; the launch traced here: 26.2 us
  starting transfers between devices  15.8 us (60%)
  Pallas kernels  6.51 us (25%)
  waiting for transfers between devices  3.16 us (12%)
  between operations  0.73 us (3%)
    ppermute x8, starting transfers between devices, exchange(): lax.ppermute(message, ('dp', 'tensor'), [(2 * i + c, 2 * (i ^ step[c]) +...  14.4 us
    ppermute x8, waiting for transfers between devices, exchange(): lax.ppermute(message, ('dp', 'tensor'), [(2 * i + c, 2 * (i ^ step[c]) +...  2.12 us
    pallas_call x1, Pallas kernels, local_kernels(): pl.pallas_call(functools.partial(grad_x_kernel, n), out_shape=shape((tok_...  1.67 us
    pallas_call x1, Pallas kernels, local_kernels(): pl.pallas_call(functools.partial(stage_kernel, n, picked), out_shape=[sha...  1.17 us
    pallas_call x1, Pallas kernels, local_kernels(): pl.pallas_call(functools.partial(pack_kernel, n), out_shape=[message] * c...  1.15 us
    ppermute x6, waiting for transfers between devices, exchange(): lax.ppermute(message, 'tensor', [(0, 1), (1, 0)])  1.03 us
    pallas_call x1, Pallas kernels, local_kernels(): pl.pallas_call(functools.partial(final_kernel, n), out_shape=[shape((colu...  1.01 us
    pallas_call x1, Pallas kernels, local_kernels(): pl.pallas_call(functools.partial(middle_kernel, n), out_shape=[shape((tok...  1 us
  transfers between devices with their start and end apart: 15, of which 9 were waited for; matrix products, arithmetic and copies ran while one was open for 0% of the time, Pallas kernels for 13%

profile of v20, /device:TPU:0, one launch (start us, length us, event | category | flops | bytes accessed | tf_op | source)
XLA Modules:
  0.0 26.2 jit_solution(6903340284528261876)
XLA Ops:
  0.6 1.2 %shard_map.113 = (bf16[48,512]{1,0:T(8,128)(2,1)S(1)}, bf16[48,512]{1,0:T(8,128)(2,1)S(1)}, bf16[48,512]{1,0:T(8,128)(2,1)S(1)}, bf16[48,512]{1,0:T(8,128)(2,1)S(1)}, bf16[48,512]{1,0:T(8,128)(2,1)S(1)}) custom-call(s32[2,8]{1,0:T(2,128)} %bitcast.2, s32[8]{0:T(128)} %slot_hbm.3, bf16[512,128]{1,0:T(8,128)(2,1)} %down_hbm.1, bf16[16,512]{1,0:T(8,128)(2,1)} %up_hbm.1), custom_call_target="tpu_custom_call" | custom-call | tf_op jit(solution)/shard_map/pallas_call | solution.py:260
  1.8 0.5 %collective-permute-start.1 = (bf16[64,4096]{1,0:T(8,128)(2,1)}, bf16[64,4096]{1,0:T(8,128)(2,1)S(1)}, u32[]{:S(2)}, u32[]{:S(2)}) collective-permute-start(bf16[64,4096]{1,0:T(8,128)(2,1)} %x_hbm.1), channel_id=1, source_target_pairs={{0,1},{1,0},{2,3},{3,2},{4,5},{5,4},{6,7},{7,6},{8,9},{9,8},{10,11... | collective-permute-start | bytes 1572872 | tf_op jit(solution)/shard_map/ppermute | solution.py:270
  2.3 5.6 %collective-permute-start = (bf16[48,512]{1,0:T(8,128)(2,1)S(1)}, bf16[48,512]{1,0:T(8,128)(2,1)S(1)}, u32[]{:S(2)}, u32[]{:S(2)}) collective-permute-start(bf16[48,512]{1,0:T(8,128)(2,1)S(1)} %get-tuple-element.35), channel_id=1, source_target_pairs={{0,14},{1,11},{2,12},{3,9},{4,10},{5,15},{6,8},{7,13},{8,6},{9,3},... | collective-permute-start | bytes 147464 | tf_op jit(solution)/shard_map/ppermute | solution.py:211
  7.9 0.0 collective-permute-start.2
  7.9 2.0 %collective-permute-start.3 = (bf16[48,512]{1,0:T(8,128)(2,1)S(1)}, bf16[48,512]{1,0:T(8,128)(2,1)S(1)}, u32[]{:S(2)}, u32[]{:S(2)}) collective-permute-start(bf16[48,512]{1,0:T(8,128)(2,1)S(1)} %get-tuple-element.42), channel_id=1, source_target_pairs={{0,4},{1,9},{2,6},{3,11},{4,0},{5,13},{6,2},{7,15},{8,12},{9,1},{1... | collective-permute-start | bytes 147464 | tf_op jit(solution)/shard_map/ppermute | solution.py:211
  9.9 1.5 %collective-permute-start.4 = (bf16[48,512]{1,0:T(8,128)(2,1)S(1)}, bf16[48,512]{1,0:T(8,128)(2,1)S(1)}, u32[]{:S(2)}, u32[]{:S(2)}) collective-permute-start(bf16[48,512]{1,0:T(8,128)(2,1)S(1)} %get-tuple-element.43), channel_id=1, source_target_pairs={{0,2},{1,3},{2,0},{3,1},{4,6},{5,7},{6,4},{7,5},{8,10},{9,11},{10,... | collective-permute-start | bytes 147464 | tf_op jit(solution)/shard_map/ppermute | solution.py:211
  11.4 1.2 %shard_map.112 = (bf16[64,4096]{1,0:T(8,128)(2,1)S(1)}, bf16[256,512]{1,0:T(8,128)(2,1)S(1)}) custom-call(s32[2,8]{1,0:T(2,128)} %bitcast.4, s32[2,8]{1,0:T(2,128)} %bitcast.3, s32[8]{0:T(128)} %slot_hbm.3, s32[8]{0:T(128)} %count_hbm.1, bf16[128,512]{1,0:T(8,128)(2,1)} %g_hbm.1, bf16[64,4096]{1,0:T(8,128)(2,1)} %x_hbm.1, bf16[2048,512]{1,0:T(8,128)(2,1)} %w_ref.1), custom_call_target="tpu_custom_call" | custom-call | bytes 2097152 | tf_op jit(solution)/shard_map/pallas_call | solution.py:271
  12.6 0.0 copy-start
  12.6 0.0 collective-permute-done.refs_1_
  12.6 0.1 collective-permute-start.5
  12.7 0.4 %collective-permute-done.2.refs_2_ = bf16[48,512]{1,0:T(8,128)(2,1)S(1)} collective-permute-done((bf16[48,512]{1,0:T(8,128)(2,1)S(1)}, bf16[48,512]{1,0:T(8,128)(2,1)S(1)}, u32[]{:S(2)}, u32[]{:S(2)}) %collective-permute-start.2) | collective-permute-done | bytes 49184 | tf_op jit(solution)/shard_map/ppermute | solution.py:211
  13.0 0.1 collective-permute-start.6
  13.2 0.4 %collective-permute-done.3.refs_3_ = bf16[48,512]{1,0:T(8,128)(2,1)S(1)} collective-permute-done((bf16[48,512]{1,0:T(8,128)(2,1)S(1)}, bf16[48,512]{1,0:T(8,128)(2,1)S(1)}, u32[]{:S(2)}, u32[]{:S(2)}) %collective-permute-start.3) | collective-permute-done | bytes 49184 | tf_op jit(solution)/shard_map/ppermute | solution.py:211
  13.6 0.0 collective-permute-start.7
  13.6 0.4 %collective-permute-done.4.refs_4_ = bf16[48,512]{1,0:T(8,128)(2,1)S(1)} collective-permute-done((bf16[48,512]{1,0:T(8,128)(2,1)S(1)}, bf16[48,512]{1,0:T(8,128)(2,1)S(1)}, u32[]{:S(2)}, u32[]{:S(2)}) %collective-permute-start.4) | collective-permute-done | bytes 49184 | tf_op jit(solution)/shard_map/ppermute | solution.py:211
  14.0 0.0 collective-permute-done.1.x_other
  14.0 0.5 %shard_map.114 = (bf16[128,4096]{1,0:T(8,128)(2,1)S(1)}, f32[128,32]{1,0:T(8,128)S(1)}, f32[128,32]{1,0:T(8,128)S(1)}) custom-call(bf16[256,512]{1,0:T(8,128)(2,1)S(1)} %get-tuple-element.30.kept_ref, bf16[64,4096]{1,0:T(8,128)(2,1)S(1)} %get-tuple-element.37.x_mine, bf16[64,4096]{1,0:T(8,128)(2,1)S(1)} %collective-permute-done.1.x_other, ...), custom_call_target="tpu_custom_call" | custom-call | bytes 2097152 | tf_op jit(solution)/shard_map/pallas_call | solution.py:284
  14.5 0.0 collective-permute-done.5.refs_0_.refs_5_
  14.5 0.0 collective-permute-done.6.refs_1_.refs_6_
  14.5 0.3 collective-permute-done.7.refs_2_.refs_7_
  14.8 1.0 %shard_map.115 = (bf16[128,32]{1,0:T(8,128)(2,1)S(1)}, bf16[48,512]{1,0:T(8,128)(2,1)S(1)}, bf16[48,512]{1,0:T(8,128)(2,1)S(1)}, bf16[48,512]{1,0:T(8,128)(2,1)S...) custom-call(bf16[256,512]{1,0:T(8,128)(2,1)S(1)} %get-tuple-element.30.kept_ref, ...), custom_call_target="tpu_custom_call" | custom-call | tf_op jit(solution)/shard_map/pallas_call | solution.py:294
  15.8 1.8 %collective-permute-start.8 = (bf16[48,512]{1,0:T(8,128)(2,1)S(1)}, bf16[48,512]{1,0:T(8,128)(2,1)S(1)}, u32[]{:S(2)}, u32[]{:S(2)}) collective-permute-start(bf16[48,512]{1,0:T(8,128)(2,1)S(1)} %get-tuple-element.47), channel_id=1, source_target_pairs={{0,14},{1,11},{2,12},{3,9},{4,10},{5,15},{6,8},{7,13},{8,6},{9,3},... | collective-permute-start | bytes 147464 | tf_op jit(solution)/shard_map/ppermute | solution.py:211
  17.6 0.1 collective-permute-start.9
  17.7 2.5 %collective-permute-start.10 = (bf16[48,512]{1,0:T(8,128)(2,1)S(1)}, bf16[48,512]{1,0:T(8,128)(2,1)S(1)}, u32[]{:S(2)}, u32[]{:S(2)}) collective-permute-start(bf16[48,512]{1,0:T(8,128)(2,1)S(1)} %get-tuple-element.53), channel_id=1, source_target_pairs={{0,4},{1,9},{2,6},{3,11},{4,0},{5,13},{6,2},{7,15},{8,12},{9,1},{1... | collective-permute-start | bytes 147464 | tf_op jit(solution)/shard_map/ppermute | solution.py:211
  20.3 0.8 %collective-permute-start.11 = (bf16[48,512]{1,0:T(8,128)(2,1)S(1)}, bf16[48,512]{1,0:T(8,128)(2,1)S(1)}, u32[]{:S(2)}, u32[]{:S(2)}) collective-permute-start(bf16[48,512]{1,0:T(8,128)(2,1)S(1)} %get-tuple-element.54), channel_id=1, source_target_pairs={{0,2},{1,3},{2,0},{3,1},{4,6},{5,7},{6,4},{7,5},{8,10},{9,11},{10,... | collective-permute-start | bytes 147464 | tf_op jit(solution)/shard_map/ppermute | solution.py:211
  21.1 0.0 copy-done
  21.1 1.7 %shard_map.116 = bf16[128,2048]{1,0:T(8,128)(2,1)} custom-call(bf16[256,512]{1,0:T(8,128)(2,1)S(1)} %get-tuple-element.30.kept_ref, bf16[2048,512]{1,0:T(8,128)(2,1)S(1)} %copy-done, bf16[128,32]{1,0:T(8,128)(2,1)S(1)} %get-tuple-element.48.dlow_ref, bf16[48,512]{1,0:T(8,128)(2,1)S(1)} %get-tuple-element.39.refs_0_, ...), custom_call_target="tpu_custom_call" | custom-call | flops 285212672 | bytes 2621440 | tf_op jit(solution)/shard_map/pallas_call | solution.py:304
  22.8 0.0 collective-permute-done.8.refs_1_
  22.8 0.0 collective-permute-start.12
  22.9 0.6 %collective-permute-done.9.refs_2_ = bf16[48,512]{1,0:T(8,128)(2,1)S(1)} collective-permute-done((bf16[48,512]{1,0:T(8,128)(2,1)S(1)}, bf16[48,512]{1,0:T(8,128)(2,1)S(1)}, u32[]{:S(2)}, u32[]{:S(2)}) %collective-permute-start.9) | collective-permute-done | bytes 49184 | tf_op jit(solution)/shard_map/ppermute | solution.py:211
  23.5 0.0 collective-permute-start.13
  23.5 0.2 collective-permute-done.10.refs_3_
  23.7 0.6 %collective-permute-start.14 = (bf16[48,512]{1,0:T(8,128)(2,1)S(1)}, bf16[48,512]{1,0:T(8,128)(2,1)S(1)}, u32[]{:S(2)}, u32[]{:S(2)}) collective-permute-start(bf16[48,512]{1,0:T(8,128)(2,1)S(1)} %collective-permute-done.10.refs_3_), channel_id=1, source_target_pairs={{0,1},{1,0},{2,3},{3,2},{4,5},{5,4},{6,7},{7,6},{8,9},{9,8},{10,11... | collective-permute-start | bytes 147464 | tf_op jit(solution)/shard_map/ppermute | solution.py:221
  24.3 0.1 collective-permute-done.11.refs_4_
  24.4 0.0 collective-permute-done.12.refs_5_
  24.4 0.3 %collective-permute-done.13.refs_6_ = bf16[48,512]{1,0:T(8,128)(2,1)S(1)} collective-permute-done((bf16[48,512]{1,0:T(8,128)(2,1)S(1)}, bf16[48,512]{1,0:T(8,128)(2,1)S(1)}, u32[]{:S(2)}, u32[]{:S(2)}) %collective-permute-start.13) | collective-permute-done | bytes 49184 | tf_op jit(solution)/shard_map/ppermute | solution.py:221
  24.7 0.5 %collective-permute-done.14.refs_7_ = bf16[48,512]{1,0:T(8,128)(2,1)S(1)} collective-permute-done((bf16[48,512]{1,0:T(8,128)(2,1)S(1)}, bf16[48,512]{1,0:T(8,128)(2,1)S(1)}, u32[]{:S(2)}, u32[]{:S(2)}) %collective-permute-start.14) | collective-permute-done | bytes 49184 | tf_op jit(solution)/shard_map/ppermute | solution.py:221
  25.1 1.0 %shard_map.117 = (f32[512,128]{1,0:T(8,128)}, f32[16,256]{1,0:T(8,128)}) custom-call(bf16[256,512]{1,0:T(8,128)(2,1)S(1)} %get-tuple-element.30.kept_ref, bf16[48,512]{1,0:T(8,128)(2,1)S(1)} %get-tuple-element.50.refs_0_, bf16[48,512]{1,0:T(8,128)(2,1)S(1)} %collective-permute-done.8.refs_1_, bf16[48,512]{1,0:T(8,128)(2,1)S(1)} %collective-permute-done.9.refs_2_, ...), custom_call_target="tpu_custom_call" | custom-call | tf_op jit(solution)/shard_map/pallas_call | solution.py:324
Async XLA Ops:
  1.8 12.2 %collective-permute-start.1 = (bf16[64,4096]{1,0:T(8,128)(2,1)}, bf16[64,4096]{1,0:T(8,128)(2,1)S(1)}, u32[]{:S(2)}, u32[]{:S(2)}) collective-permute-start(bf16[64,4096]{1,0:T(8,128)(2,1)} %x_hbm.1), channel_id=1, source_target_pairs={{0,1},{1,0},{2,3},{3,2},{4,5},{5,4},{6,7},{7,6},{8,9},{9,8},{10,11... | collective-permute-start | bytes 1572872 | tf_op jit(solution)/shard_map/ppermute | solution.py:270
  2.3 10.3 %collective-permute-start = (bf16[48,512]{1,0:T(8,128)(2,1)S(1)}, bf16[48,512]{1,0:T(8,128)(2,1)S(1)}, u32[]{:S(2)}, u32[]{:S(2)}) collective-permute-start(bf16[48,512]{1,0:T(8,128)(2,1)S(1)} %get-tuple-element.35), channel_id=1, source_target_pairs={{0,14},{1,11},{2,12},{3,9},{4,10},{5,15},{6,8},{7,13},{8,6},{9,3},... | collective-permute-start | bytes 147464 | tf_op jit(solution)/shard_map/ppermute | solution.py:211
  7.9 5.1 %collective-permute-start.2 = (bf16[48,512]{1,0:T(8,128)(2,1)S(1)}, bf16[48,512]{1,0:T(8,128)(2,1)S(1)}, u32[]{:S(2)}, u32[]{:S(2)}) collective-permute-start(bf16[48,512]{1,0:T(8,128)(2,1)S(1)} %get-tuple-element.41), channel_id=1, source_target_pairs={{0,6},{1,13},{2,4},{3,15},{4,2},{5,9},{6,0},{7,11},{8,14},{9,5},{1... | collective-permute-start | bytes 147464 | tf_op jit(solution)/shard_map/ppermute | solution.py:211
  7.9 5.6 %collective-permute-start.3 = (bf16[48,512]{1,0:T(8,128)(2,1)S(1)}, bf16[48,512]{1,0:T(8,128)(2,1)S(1)}, u32[]{:S(2)}, u32[]{:S(2)}) collective-permute-start(bf16[48,512]{1,0:T(8,128)(2,1)S(1)} %get-tuple-element.42), channel_id=1, source_target_pairs={{0,4},{1,9},{2,6},{3,11},{4,0},{5,13},{6,2},{7,15},{8,12},{9,1},{1... | collective-permute-start | bytes 147464 | tf_op jit(solution)/shard_map/ppermute | solution.py:211
  9.9 4.1 %collective-permute-start.4 = (bf16[48,512]{1,0:T(8,128)(2,1)S(1)}, bf16[48,512]{1,0:T(8,128)(2,1)S(1)}, u32[]{:S(2)}, u32[]{:S(2)}) collective-permute-start(bf16[48,512]{1,0:T(8,128)(2,1)S(1)} %get-tuple-element.43), channel_id=1, source_target_pairs={{0,2},{1,3},{2,0},{3,1},{4,6},{5,7},{6,4},{7,5},{8,10},{9,11},{10,... | collective-permute-start | bytes 147464 | tf_op jit(solution)/shard_map/ppermute | solution.py:211
  12.6 8.5 %copy-start = (bf16[2048,512]{1,0:T(8,128)(2,1)S(1)}, bf16[2048,512]{1,0:T(8,128)(2,1)}, u32[]{:S(2)}) copy-start(bf16[2048,512]{1,0:T(8,128)(2,1)} %w_ref.1) | copy-start | bytes 6291460
  12.6 1.9 %collective-permute-start.5 = (bf16[48,512]{1,0:T(8,128)(2,1)S(1)}, bf16[48,512]{1,0:T(8,128)(2,1)S(1)}, u32[]{:S(2)}, u32[]{:S(2)}) collective-permute-start(bf16[48,512]{1,0:T(8,128)(2,1)S(1)} %collective-permute-done.refs_1_), channel_id=1, source_target_pairs={{0,1},{1,0},{2,3},{3,2},{4,5},{5,4},{6,7},{7,6},{8,9},{9,8},{10,11... | collective-permute-start | bytes 147464 | tf_op jit(solution)/shard_map/ppermute | solution.py:221
  13.0 1.5 %collective-permute-start.6 = (bf16[48,512]{1,0:T(8,128)(2,1)S(1)}, bf16[48,512]{1,0:T(8,128)(2,1)S(1)}, u32[]{:S(2)}, u32[]{:S(2)}) collective-permute-start(bf16[48,512]{1,0:T(8,128)(2,1)S(1)} %collective-permute-done.2.refs_2_), channel_id=1, source_target_pairs={{0,1},{1,0},{2,3},{3,2},{4,5},{5,4},{6,7},{7,6},{8,9},{9,8},{10,11... | collective-permute-start | bytes 147464 | tf_op jit(solution)/shard_map/ppermute | solution.py:221
  13.6 1.2 %collective-permute-start.7 = (bf16[48,512]{1,0:T(8,128)(2,1)S(1)}, bf16[48,512]{1,0:T(8,128)(2,1)S(1)}, u32[]{:S(2)}, u32[]{:S(2)}) collective-permute-start(bf16[48,512]{1,0:T(8,128)(2,1)S(1)} %collective-permute-done.3.refs_3_), channel_id=1, source_target_pairs={{0,1},{1,0},{2,3},{3,2},{4,5},{5,4},{6,7},{7,6},{8,9},{9,8},{10,11... | collective-permute-start | bytes 147464 | tf_op jit(solution)/shard_map/ppermute | solution.py:221
  15.8 7.1 %collective-permute-start.8 = (bf16[48,512]{1,0:T(8,128)(2,1)S(1)}, bf16[48,512]{1,0:T(8,128)(2,1)S(1)}, u32[]{:S(2)}, u32[]{:S(2)}) collective-permute-start(bf16[48,512]{1,0:T(8,128)(2,1)S(1)} %get-tuple-element.47), channel_id=1, source_target_pairs={{0,14},{1,11},{2,12},{3,9},{4,10},{5,15},{6,8},{7,13},{8,6},{9,3},... | collective-permute-start | bytes 147464 | tf_op jit(solution)/shard_map/ppermute | solution.py:211
  17.6 5.8 %collective-permute-start.9 = (bf16[48,512]{1,0:T(8,128)(2,1)S(1)}, bf16[48,512]{1,0:T(8,128)(2,1)S(1)}, u32[]{:S(2)}, u32[]{:S(2)}) collective-permute-start(bf16[48,512]{1,0:T(8,128)(2,1)S(1)} %get-tuple-element.52), channel_id=1, source_target_pairs={{0,6},{1,13},{2,4},{3,15},{4,2},{5,9},{6,0},{7,11},{8,14},{9,5},{1... | collective-permute-start | bytes 147464 | tf_op jit(solution)/shard_map/ppermute | solution.py:211
  17.7 6.0 %collective-permute-start.10 = (bf16[48,512]{1,0:T(8,128)(2,1)S(1)}, bf16[48,512]{1,0:T(8,128)(2,1)S(1)}, u32[]{:S(2)}, u32[]{:S(2)}) collective-permute-start(bf16[48,512]{1,0:T(8,128)(2,1)S(1)} %get-tuple-element.53), channel_id=1, source_target_pairs={{0,4},{1,9},{2,6},{3,11},{4,0},{5,13},{6,2},{7,15},{8,12},{9,1},{1... | collective-permute-start | bytes 147464 | tf_op jit(solution)/shard_map/ppermute | solution.py:211
  20.3 4.1 %collective-permute-start.11 = (bf16[48,512]{1,0:T(8,128)(2,1)S(1)}, bf16[48,512]{1,0:T(8,128)(2,1)S(1)}, u32[]{:S(2)}, u32[]{:S(2)}) collective-permute-start(bf16[48,512]{1,0:T(8,128)(2,1)S(1)} %get-tuple-element.54), channel_id=1, source_target_pairs={{0,2},{1,3},{2,0},{3,1},{4,6},{5,7},{6,4},{7,5},{8,10},{9,11},{10,... | collective-permute-start | bytes 147464 | tf_op jit(solution)/shard_map/ppermute | solution.py:211
  22.8 1.5 %collective-permute-start.12 = (bf16[48,512]{1,0:T(8,128)(2,1)S(1)}, bf16[48,512]{1,0:T(8,128)(2,1)S(1)}, u32[]{:S(2)}, u32[]{:S(2)}) collective-permute-start(bf16[48,512]{1,0:T(8,128)(2,1)S(1)} %collective-permute-done.8.refs_1_), channel_id=1, source_target_pairs={{0,1},{1,0},{2,3},{3,2},{4,5},{5,4},{6,7},{7,6},{8,9},{9,8},{10,11... | collective-permute-start | bytes 147464 | tf_op jit(solution)/shard_map/ppermute | solution.py:221
  23.5 1.2 %collective-permute-start.13 = (bf16[48,512]{1,0:T(8,128)(2,1)S(1)}, bf16[48,512]{1,0:T(8,128)(2,1)S(1)}, u32[]{:S(2)}, u32[]{:S(2)}) collective-permute-start(bf16[48,512]{1,0:T(8,128)(2,1)S(1)} %collective-permute-done.9.refs_2_), channel_id=1, source_target_pairs={{0,1},{1,0},{2,3},{3,2},{4,5},{5,4},{6,7},{7,6},{8,9},{9,8},{10,11... | collective-permute-start | bytes 147464 | tf_op jit(solution)/shard_map/ppermute | solution.py:221
  23.7 1.4 %collective-permute-start.14 = (bf16[48,512]{1,0:T(8,128)(2,1)S(1)}, bf16[48,512]{1,0:T(8,128)(2,1)S(1)}, u32[]{:S(2)}, u32[]{:S(2)}) collective-permute-start(bf16[48,512]{1,0:T(8,128)(2,1)S(1)} %collective-permute-done.10.refs_3_), channel_id=1, source_target_pairs={{0,1},{1,0},{2,3},{3,2},{4,5},{5,4},{6,7},{7,6},{8,9},{9,8},{10,11... | collective-permute-start | bytes 147464 | tf_op jit(solution)/shard_map/ppermute | solution.py:221

commit v21 on v20

--- a/solution.py
+++ b/solution.py
@@ -50,17 +50,20 @@
         copy.wait()
 
 
-def steps(n):
-    return [(n - 1, n // 2 + 1), (3, n - 2), (2, n // 2), (1, 1)]
-
-
-def partners(n, me, core):
-    return [me] + [me ^ jnp.where(core == 0, a, b) for a, b in steps(n)]
-
-
-def senders(n, me, core):
-    passed = [me ^ jnp.where(core == 0, b, a) for a, b in steps(n) if a != b]
-    return partners(n, me, core) + passed
+def steps(n, turn):
+    half = n // 2
+    if turn == 0:
+        return [(n - 1, half), (3, half + 1), (n - 2, 2), (1, 1)]
+    return [(n - 1, half + 1), (3, n - 2), (2, half), (1, 1)]
+
+
+def partners(n, turn, me, core):
+    return [me] + [me ^ jnp.where(core == 0, a, b) for a, b in steps(n, turn)]
+
+
+def senders(n, turn, me, core):
+    passed = [me ^ jnp.where(core == 0, b, a) for a, b in steps(n, turn) if a != b]
+    return partners(n, turn, me, core) + passed
 
 
 def in_hbm(*arrays):
@@ -72,7 +75,7 @@
     send, (chosen_ref, slot_ref, down_ref, up_ref, sems) = refs[:count], refs[count:]
     tables = start_all([chosen_hbm, slot_hbm], [chosen_ref, slot_ref], sems)
     maps = start_all([down_hbm, up_hbm], [down_ref, up_ref], sems, 2)
-    ranks = partners(n, lax.axis_index("dp"), lax.axis_index("tensor"))
+    ranks = partners(n, 0, lax.axis_index("dp"), lax.axis_index("tensor"))
     wait_all(tables)
     onehot = slot_rows(chosen_ref, slot_ref, ranks, down_ref.shape[1])
     picked = onehot.shape[0] // count
@@ -135,7 +138,7 @@
     count = n // 2 + 1
     here, (x_ref, low_ref, dlow_ref, b_ref) = refs[:count], refs[count:]
     me, core, half = lax.axis_index("dp"), lax.axis_index("tensor"), x_mine.shape[0]
-    ranks = senders(n, me, core)[:count]
+    ranks = senders(n, 0, me, core)[:count]
     x_ref[pl.ds(pl.multiple_of(core * half, half), half), :] = x_mine[...]
     x_ref[pl.ds(pl.multiple_of((1 - core) * half, half), half), :] = x_other[...]
     b_sel = picked_maps(kept_ref, b_ref, picked, ranks, here)
@@ -151,7 +154,7 @@
     rows, picked = dlow_ref.shape
     width = kept_ref.shape[1]
     slots = width // 4
-    ranks = senders(n, me, core)[count:]
+    ranks = senders(n, 0, me, core)[count:]
     in_seg = kept_ref[rows:, :picked].astype(f32) > 0.0
     g = kept_ref[:rows, :]
     onehot = kept_ref[rows : rows + picked, slots : 2 * slots]
@@ -159,7 +162,7 @@
     dlow = dlow_part[...] + dot(g, b_sel, 1, 1)
     dlow = jnp.where(in_seg, adapter_scale * dlow, 0.0).astype(bf16)
     dlow_ref[...] = dlow
-    targets = partners(n, me, core)
+    targets = partners(n, 1, me, core)
     for target, message in zip(targets, send):
         at = pl.ds(pl.multiple_of(target * width, width), width)
         message[:picked, :] = dot(dlow, x_ref[:, at], 0, 0).astype(bf16)
@@ -177,7 +180,7 @@
     got, (out_hbm, a_ref, out_ref, sems) = refs[:n], refs[n:]
     me, core = lax.axis_index("dp"), lax.axis_index("tensor")
     picked, width = a_ref.shape[1:]
-    for sender, message in zip(senders(n, me, core), got):
+    for sender, message in zip(senders(n, 0, me, core), got):
         a_ref[sender] = message[:picked, :]
     g = kept_ref[: out_ref.shape[0], :]
     done = []
@@ -194,7 +197,7 @@
     me, core = lax.axis_index("dp"), lax.axis_index("tensor")
     piece, picked = up_ref.shape[1], rows_ref.shape[1] - ADAPTER_RANK
     half, slots = kept_ref.shape[0] // 2, kept_ref.shape[1] // 4
-    for sender, message in zip(senders(n, me, core), got):
+    for sender, message in zip(senders(n, 1, me, core), got):
         rows_ref[sender] = message[...]
     rows = rows_ref[:, :picked, :].reshape(n * picked, rows_ref.shape[2])
     onehot = jnp.concatenate(
@@ -205,7 +208,7 @@
     up_ref[...] = jnp.sum(rows_ref[:, picked:, at].astype(f32), axis=0)
 
 
-def exchange(messages, tied, beside):
+def exchange(messages, turn, tied, beside):
     n = 2 * len(messages)
     got = [
         lax.ppermute(
@@ -213,13 +216,13 @@
             ("dp", "tensor"),
             [(2 * i + c, 2 * (i ^ step[c]) + c) for i in range(n) for c in range(2)],
         )
-        for message, step in zip(messages, steps(n))
+        for message, step in zip(messages, steps(n, turn))
     ]
     for k in tied:
         got[k], beside = lax.optimization_barrier((got[k], beside))
     passed = [
         lax.ppermute(message, "tensor", [(0, 1), (1, 0)])
-        for message, (a, b) in zip(got, steps(n))
+        for message, (a, b) in zip(got, steps(n, turn))
         if a != b
     ]
     return got + passed, beside
@@ -277,7 +280,7 @@
         compiler_params=params(8),
         cost_estimate=pl.CostEstimate(flops=0, bytes_accessed=1 << 21, transcendentals=0),
     )(*in_hbm(starts, chosen, adapter_slot, token_count, output_gradient, inputs, frozen_weight))
-    got, x_mine = exchange(sent, (0,), x_mine)
+    got, x_mine = exchange(sent, 0, (0,), x_mine)
     low = shape((tok_rows, picked), f32)
     maps = pltpu.VMEM((n, ADAPTER_RANK, out_width), bf16)
     got = [own] + got
@@ -319,7 +322,7 @@
         ),
     )(kept, frozen_weight, dlow, *got)
 
-    got, grad_x = exchange(sent, (0,), grad_x)
+    got, grad_x = exchange(sent, 1, (0,), grad_x)
 
     grad_a, up_map_gradient = pl.pallas_call(
         functools.partial(final_kernel, n),

time: 26.4 us -> 26.5 us (level)
  waiting for transfers between devices: 3.16 us -> 4.51 us
  starting transfers between devices: 15.8 us -> 14.5 us
    ppermute x8, starting transfers between devices: 14.4 us -> 13.4 us  [exchange(): lax.ppermute(message, ('dp', 'tensor'), [(2 * i + c, 2 * (i ^ step[c]) +...]
    ppermute x8, waiting for transfers between devices: 2.12 us -> 3.05 us  [exchange(): lax.ppermute(message, ('dp', 'tensor'), [(2 * i + c, 2 * (i ^ step[c]) +...]
    ppermute x6, waiting for transfers between devices: 1.03 us -> 1.46 us  [exchange(): lax.ppermute(message, 'tensor', [(0, 1), (1, 0)])]
where the time goes in v21:
time: 26.5 us; the launch traced here: 26.3 us
  starting transfers between devices  14.5 us (55%)
  Pallas kernels  6.5 us (25%)
  waiting for transfers between devices  4.51 us (17%)
  between operations  0.72 us (3%)
    ppermute x8, starting transfers between devices, exchange(): lax.ppermute(message, ('dp', 'tensor'), [(2 * i + c, 2 * (i ^ step[c]) +...  13.4 us
    ppermute x8, waiting for transfers between devices, exchange(): lax.ppermute(message, ('dp', 'tensor'), [(2 * i + c, 2 * (i ^ step[c]) +...  3.05 us
    pallas_call x1, Pallas kernels, local_kernels(): pl.pallas_call(functools.partial(grad_x_kernel, n), out_shape=shape((tok_...  1.67 us
    ppermute x6, waiting for transfers between devices, exchange(): lax.ppermute(message, 'tensor', [(0, 1), (1, 0)])  1.46 us
    pallas_call x1, Pallas kernels, local_kernels(): pl.pallas_call(functools.partial(stage_kernel, n, picked), out_shape=[sha...  1.17 us
    pallas_call x1, Pallas kernels, local_kernels(): pl.pallas_call(functools.partial(pack_kernel, n), out_shape=[message] * c...  1.15 us
    pallas_call x1, Pallas kernels, local_kernels(): pl.pallas_call(functools.partial(final_kernel, n), out_shape=[shape((colu...  1.01 us
    pallas_call x1, Pallas kernels, local_kernels(): pl.pallas_call(functools.partial(middle_kernel, n), out_shape=[shape((tok...  1 us
  transfers between devices with their start and end apart: 15, of which 9 were waited for; matrix products, arithmetic and copies ran while one was open for 0% of the time, Pallas kernels for 13%

profile of v21, /device:TPU:0, one launch (start us, length us, event | category | flops | bytes accessed | tf_op | source)
XLA Modules:
  0.0 26.3 jit_solution(7794341676080394081)
XLA Ops:
  0.6 1.2 %shard_map.113 = (bf16[48,512]{1,0:T(8,128)(2,1)S(1)}, bf16[48,512]{1,0:T(8,128)(2,1)S(1)}, bf16[48,512]{1,0:T(8,128)(2,1)S(1)}, bf16[48,512]{1,0:T(8,128)(2,1)S(1)}, bf16[48,512]{1,0:T(8,128)(2,1)S(1)}) custom-call(s32[2,8]{1,0:T(2,128)} %bitcast.2, s32[8]{0:T(128)} %slot_hbm.3, bf16[512,128]{1,0:T(8,128)(2,1)} %down_hbm.1, bf16[16,512]{1,0:T(8,128)(2,1)} %up_hbm.1), custom_call_target="tpu_custom_call" | custom-call | tf_op jit(solution)/shard_map/pallas_call | solution.py:263
  1.8 0.5 %collective-permute-start.1 = (bf16[64,4096]{1,0:T(8,128)(2,1)}, bf16[64,4096]{1,0:T(8,128)(2,1)S(1)}, u32[]{:S(2)}, u32[]{:S(2)}) collective-permute-start(bf16[64,4096]{1,0:T(8,128)(2,1)} %x_hbm.1), channel_id=1, source_target_pairs={{0,1},{1,0},{2,3},{3,2},{4,5},{5,4},{6,7},{7,6},{8,9},{9,8},{10,11... | collective-permute-start | bytes 1572872 | tf_op jit(solution)/shard_map/ppermute | solution.py:273
  2.3 5.6 %collective-permute-start = (bf16[48,512]{1,0:T(8,128)(2,1)S(1)}, bf16[48,512]{1,0:T(8,128)(2,1)S(1)}, u32[]{:S(2)}, u32[]{:S(2)}) collective-permute-start(bf16[48,512]{1,0:T(8,128)(2,1)S(1)} %get-tuple-element.35), channel_id=1, source_target_pairs={{0,14},{1,9},{2,12},{3,11},{4,10},{5,13},{6,8},{7,15},{8,6},{9,1},... | collective-permute-start | bytes 147464 | tf_op jit(solution)/shard_map/ppermute | solution.py:214
  7.9 0.0 collective-permute-start.2
  7.9 0.9 %collective-permute-start.3 = (bf16[48,512]{1,0:T(8,128)(2,1)S(1)}, bf16[48,512]{1,0:T(8,128)(2,1)S(1)}, u32[]{:S(2)}, u32[]{:S(2)}) collective-permute-start(bf16[48,512]{1,0:T(8,128)(2,1)S(1)} %get-tuple-element.42), channel_id=1, source_target_pairs={{0,12},{1,5},{2,14},{3,7},{4,8},{5,1},{6,10},{7,3},{8,4},{9,13},{1... | collective-permute-start | bytes 147464 | tf_op jit(solution)/shard_map/ppermute | solution.py:214
  8.8 1.5 %collective-permute-start.4 = (bf16[48,512]{1,0:T(8,128)(2,1)S(1)}, bf16[48,512]{1,0:T(8,128)(2,1)S(1)}, u32[]{:S(2)}, u32[]{:S(2)}) collective-permute-start(bf16[48,512]{1,0:T(8,128)(2,1)S(1)} %get-tuple-element.43), channel_id=1, source_target_pairs={{0,2},{1,3},{2,0},{3,1},{4,6},{5,7},{6,4},{7,5},{8,10},{9,11},{10,... | collective-permute-start | bytes 147464 | tf_op jit(solution)/shard_map/ppermute | solution.py:214
  10.3 1.2 %shard_map.112 = (bf16[64,4096]{1,0:T(8,128)(2,1)S(1)}, bf16[256,512]{1,0:T(8,128)(2,1)S(1)}) custom-call(s32[2,8]{1,0:T(2,128)} %bitcast.4, s32[2,8]{1,0:T(2,128)} %bitcast.3, s32[8]{0:T(128)} %slot_hbm.3, s32[8]{0:T(128)} %count_hbm.1, bf16[128,512]{1,0:T(8,128)(2,1)} %g_hbm.1, bf16[64,4096]{1,0:T(8,128)(2,1)} %x_hbm.1, bf16[2048,512]{1,0:T(8,128)(2,1)} %w_ref.1), custom_call_target="tpu_custom_call" | custom-call | bytes 2097152 | tf_op jit(solution)/shard_map/pallas_call | solution.py:274
  11.5 0.0 copy-start
  11.5 0.0 collective-permute-done.refs_1_
  11.5 0.1 collective-permute-start.5
  11.6 1.5 %collective-permute-done.2.refs_2_ = bf16[48,512]{1,0:T(8,128)(2,1)S(1)} collective-permute-done((bf16[48,512]{1,0:T(8,128)(2,1)S(1)}, bf16[48,512]{1,0:T(8,128)(2,1)S(1)}, u32[]{:S(2)}, u32[]{:S(2)}) %collective-permute-start.2) | collective-permute-done | bytes 49184 | tf_op jit(solution)/shard_map/ppermute | solution.py:214
  13.0 0.0 collective-permute-start.6
  13.0 0.9 %collective-permute-done.3.refs_3_ = bf16[48,512]{1,0:T(8,128)(2,1)S(1)} collective-permute-done((bf16[48,512]{1,0:T(8,128)(2,1)S(1)}, bf16[48,512]{1,0:T(8,128)(2,1)S(1)}, u32[]{:S(2)}, u32[]{:S(2)}) %collective-permute-start.3) | collective-permute-done | bytes 49184 | tf_op jit(solution)/shard_map/ppermute | solution.py:214
  13.9 0.0 collective-permute-start.7
  13.9 0.0 collective-permute-done.4.refs_4_
  13.9 0.0 collective-permute-done.1.x_other
  13.9 0.5 %shard_map.114 = (bf16[128,4096]{1,0:T(8,128)(2,1)S(1)}, f32[128,32]{1,0:T(8,128)S(1)}, f32[128,32]{1,0:T(8,128)S(1)}) custom-call(bf16[256,512]{1,0:T(8,128)(2,1)S(1)} %get-tuple-element.30.kept_ref, bf16[64,4096]{1,0:T(8,128)(2,1)S(1)} %get-tuple-element.37.x_mine, bf16[64,4096]{1,0:T(8,128)(2,1)S(1)} %collective-permute-done.1.x_other, ...), custom_call_target="tpu_custom_call" | custom-call | bytes 2097152 | tf_op jit(solution)/shard_map/pallas_call | solution.py:287
  14.4 0.0 collective-permute-done.5.refs_0_.refs_5_
  14.4 0.0 collective-permute-done.6.refs_1_.refs_6_
  14.5 0.7 %collective-permute-done.7.refs_2_.refs_7_ = bf16[48,512]{1,0:T(8,128)(2,1)S(1)} collective-permute-done((bf16[48,512]{1,0:T(8,128)(2,1)S(1)}, bf16[48,512]{1,0:T(8,128)(2,1)S(1)}, u32[]{:S(2)}, u32[]{:S(2)}) %collective-permute-start.7) | collective-permute-done | bytes 49184 | tf_op jit(solution)/shard_map/ppermute | solution.py:224
  15.1 1.0 %shard_map.115 = (bf16[128,32]{1,0:T(8,128)(2,1)S(1)}, bf16[48,512]{1,0:T(8,128)(2,1)S(1)}, bf16[48,512]{1,0:T(8,128)(2,1)S(1)}, bf16[48,512]{1,0:T(8,128)(2,1)S...) custom-call(bf16[256,512]{1,0:T(8,128)(2,1)S(1)} %get-tuple-element.30.kept_ref, ...), custom_call_target="tpu_custom_call" | custom-call | tf_op jit(solution)/shard_map/pallas_call | solution.py:297
  16.2 1.9 %collective-permute-start.8 = (bf16[48,512]{1,0:T(8,128)(2,1)S(1)}, bf16[48,512]{1,0:T(8,128)(2,1)S(1)}, u32[]{:S(2)}, u32[]{:S(2)}) collective-permute-start(bf16[48,512]{1,0:T(8,128)(2,1)S(1)} %get-tuple-element.47), channel_id=1, source_target_pairs={{0,14},{1,11},{2,12},{3,9},{4,10},{5,15},{6,8},{7,13},{8,6},{9,3},... | collective-permute-start | bytes 147464 | tf_op jit(solution)/shard_map/ppermute | solution.py:214
  18.1 0.5 %collective-permute-start.9 = (bf16[48,512]{1,0:T(8,128)(2,1)S(1)}, bf16[48,512]{1,0:T(8,128)(2,1)S(1)}, u32[]{:S(2)}, u32[]{:S(2)}) collective-permute-start(bf16[48,512]{1,0:T(8,128)(2,1)S(1)} %get-tuple-element.52), channel_id=1, source_target_pairs={{0,6},{1,13},{2,4},{3,15},{4,2},{5,9},{6,0},{7,11},{8,14},{9,5},{1... | collective-permute-start | bytes 147464 | tf_op jit(solution)/shard_map/ppermute | solution.py:214
  18.5 1.9 %collective-permute-start.10 = (bf16[48,512]{1,0:T(8,128)(2,1)S(1)}, bf16[48,512]{1,0:T(8,128)(2,1)S(1)}, u32[]{:S(2)}, u32[]{:S(2)}) collective-permute-start(bf16[48,512]{1,0:T(8,128)(2,1)S(1)} %get-tuple-element.53), channel_id=1, source_target_pairs={{0,4},{1,9},{2,6},{3,11},{4,0},{5,13},{6,2},{7,15},{8,12},{9,1},{1... | collective-permute-start | bytes 147464 | tf_op jit(solution)/shard_map/ppermute | solution.py:214
  20.4 1.1 %collective-permute-start.11 = (bf16[48,512]{1,0:T(8,128)(2,1)S(1)}, bf16[48,512]{1,0:T(8,128)(2,1)S(1)}, u32[]{:S(2)}, u32[]{:S(2)}) collective-permute-start(bf16[48,512]{1,0:T(8,128)(2,1)S(1)} %get-tuple-element.54), channel_id=1, source_target_pairs={{0,2},{1,3},{2,0},{3,1},{4,6},{5,7},{6,4},{7,5},{8,10},{9,11},{10,... | collective-permute-start | bytes 147464 | tf_op jit(solution)/shard_map/ppermute | solution.py:214
  21.6 0.0 copy-done
  21.6 1.7 %shard_map.116 = bf16[128,2048]{1,0:T(8,128)(2,1)} custom-call(bf16[256,512]{1,0:T(8,128)(2,1)S(1)} %get-tuple-element.30.kept_ref, bf16[2048,512]{1,0:T(8,128)(2,1)S(1)} %copy-done, bf16[128,32]{1,0:T(8,128)(2,1)S(1)} %get-tuple-element.48.dlow_ref, bf16[48,512]{1,0:T(8,128)(2,1)S(1)} %get-tuple-element.39.refs_0_, ...), custom_call_target="tpu_custom_call" | custom-call | flops 285212672 | bytes 2621440 | tf_op jit(solution)/shard_map/pallas_call | solution.py:307
  23.2 0.2 collective-permute-done.8.refs_1_
  23.4 0.1 collective-permute-start.12
  23.5 0.4 %collective-permute-done.9.refs_2_ = bf16[48,512]{1,0:T(8,128)(2,1)S(1)} collective-permute-done((bf16[48,512]{1,0:T(8,128)(2,1)S(1)}, bf16[48,512]{1,0:T(8,128)(2,1)S(1)}, u32[]{:S(2)}, u32[]{:S(2)}) %collective-permute-start.9) | collective-permute-done | bytes 49184 | tf_op jit(solution)/shard_map/ppermute | solution.py:214
  23.9 0.1 collective-permute-start.13
  23.9 0.0 collective-permute-done.10.refs_3_
  23.9 0.4 %collective-permute-start.14 = (bf16[48,512]{1,0:T(8,128)(2,1)S(1)}, bf16[48,512]{1,0:T(8,128)(2,1)S(1)}, u32[]{:S(2)}, u32[]{:S(2)}) collective-permute-start(bf16[48,512]{1,0:T(8,128)(2,1)S(1)} %collective-permute-done.10.refs_3_), channel_id=1, source_target_pairs={{0,1},{1,0},{2,3},{3,2},{4,5},{5,4},{6,7},{7,6},{8,9},{9,8},{10,11... | collective-permute-start | bytes 147464 | tf_op jit(solution)/shard_map/ppermute | solution.py:224
  24.4 0.1 collective-permute-done.11.refs_4_
  24.5 0.1 collective-permute-done.12.refs_5_
  24.6 0.4 %collective-permute-done.13.refs_6_ = bf16[48,512]{1,0:T(8,128)(2,1)S(1)} collective-permute-done((bf16[48,512]{1,0:T(8,128)(2,1)S(1)}, bf16[48,512]{1,0:T(8,128)(2,1)S(1)}, u32[]{:S(2)}, u32[]{:S(2)}) %collective-permute-start.13) | collective-permute-done | bytes 49184 | tf_op jit(solution)/shard_map/ppermute | solution.py:224
  25.1 0.2 collective-permute-done.14.refs_7_
  25.3 1.0 %shard_map.117 = (f32[512,128]{1,0:T(8,128)}, f32[16,256]{1,0:T(8,128)}) custom-call(bf16[256,512]{1,0:T(8,128)(2,1)S(1)} %get-tuple-element.30.kept_ref, bf16[48,512]{1,0:T(8,128)(2,1)S(1)} %get-tuple-element.50.refs_0_, bf16[48,512]{1,0:T(8,128)(2,1)S(1)} %collective-permute-done.8.refs_1_, bf16[48,512]{1,0:T(8,128)(2,1)S(1)} %collective-permute-done.9.refs_2_, ...), custom_call_target="tpu_custom_call" | custom-call | tf_op jit(solution)/shard_map/pallas_call | solution.py:327
Async XLA Ops:
  1.8 12.1 %collective-permute-start.1 = (bf16[64,4096]{1,0:T(8,128)(2,1)}, bf16[64,4096]{1,0:T(8,128)(2,1)S(1)}, u32[]{:S(2)}, u32[]{:S(2)}) collective-permute-start(bf16[64,4096]{1,0:T(8,128)(2,1)} %x_hbm.1), channel_id=1, source_target_pairs={{0,1},{1,0},{2,3},{3,2},{4,5},{5,4},{6,7},{7,6},{8,9},{9,8},{10,11... | collective-permute-start | bytes 1572872 | tf_op jit(solution)/shard_map/ppermute | solution.py:273
  2.3 9.2 %collective-permute-start = (bf16[48,512]{1,0:T(8,128)(2,1)S(1)}, bf16[48,512]{1,0:T(8,128)(2,1)S(1)}, u32[]{:S(2)}, u32[]{:S(2)}) collective-permute-start(bf16[48,512]{1,0:T(8,128)(2,1)S(1)} %get-tuple-element.35), channel_id=1, source_target_pairs={{0,14},{1,9},{2,12},{3,11},{4,10},{5,13},{6,8},{7,15},{8,6},{9,1},... | collective-permute-start | bytes 147464 | tf_op jit(solution)/shard_map/ppermute | solution.py:214
  7.9 5.1 %collective-permute-start.2 = (bf16[48,512]{1,0:T(8,128)(2,1)S(1)}, bf16[48,512]{1,0:T(8,128)(2,1)S(1)}, u32[]{:S(2)}, u32[]{:S(2)}) collective-permute-start(bf16[48,512]{1,0:T(8,128)(2,1)S(1)} %get-tuple-element.41), channel_id=1, source_target_pairs={{0,6},{1,11},{2,4},{3,9},{4,2},{5,15},{6,0},{7,13},{8,14},{9,3},{1... | collective-permute-start | bytes 147464 | tf_op jit(solution)/shard_map/ppermute | solution.py:214
  7.9 6.0 %collective-permute-start.3 = (bf16[48,512]{1,0:T(8,128)(2,1)S(1)}, bf16[48,512]{1,0:T(8,128)(2,1)S(1)}, u32[]{:S(2)}, u32[]{:S(2)}) collective-permute-start(bf16[48,512]{1,0:T(8,128)(2,1)S(1)} %get-tuple-element.42), channel_id=1, source_target_pairs={{0,12},{1,5},{2,14},{3,7},{4,8},{5,1},{6,10},{7,3},{8,4},{9,13},{1... | collective-permute-start | bytes 147464 | tf_op jit(solution)/shard_map/ppermute | solution.py:214
  8.8 5.1 %collective-permute-start.4 = (bf16[48,512]{1,0:T(8,128)(2,1)S(1)}, bf16[48,512]{1,0:T(8,128)(2,1)S(1)}, u32[]{:S(2)}, u32[]{:S(2)}) collective-permute-start(bf16[48,512]{1,0:T(8,128)(2,1)S(1)} %get-tuple-element.43), channel_id=1, source_target_pairs={{0,2},{1,3},{2,0},{3,1},{4,6},{5,7},{6,4},{7,5},{8,10},{9,11},{10,... | collective-permute-start | bytes 147464 | tf_op jit(solution)/shard_map/ppermute | solution.py:214
  11.5 10.1 %copy-start = (bf16[2048,512]{1,0:T(8,128)(2,1)S(1)}, bf16[2048,512]{1,0:T(8,128)(2,1)}, u32[]{:S(2)}) copy-start(bf16[2048,512]{1,0:T(8,128)(2,1)} %w_ref.1) | copy-start | bytes 6291460
  11.5 3.0 %collective-permute-start.5 = (bf16[48,512]{1,0:T(8,128)(2,1)S(1)}, bf16[48,512]{1,0:T(8,128)(2,1)S(1)}, u32[]{:S(2)}, u32[]{:S(2)}) collective-permute-start(bf16[48,512]{1,0:T(8,128)(2,1)S(1)} %collective-permute-done.refs_1_), channel_id=1, source_target_pairs={{0,1},{1,0},{2,3},{3,2},{4,5},{5,4},{6,7},{7,6},{8,9},{9,8},{10,11... | collective-permute-start | bytes 147464 | tf_op jit(solution)/shard_map/ppermute | solution.py:224
  13.0 1.4 %collective-permute-start.6 = (bf16[48,512]{1,0:T(8,128)(2,1)S(1)}, bf16[48,512]{1,0:T(8,128)(2,1)S(1)}, u32[]{:S(2)}, u32[]{:S(2)}) collective-permute-start(bf16[48,512]{1,0:T(8,128)(2,1)S(1)} %collective-permute-done.2.refs_2_), channel_id=1, source_target_pairs={{0,1},{1,0},{2,3},{3,2},{4,5},{5,4},{6,7},{7,6},{8,9},{9,8},{10,11... | collective-permute-start | bytes 147464 | tf_op jit(solution)/shard_map/ppermute | solution.py:224
  13.9 1.2 %collective-permute-start.7 = (bf16[48,512]{1,0:T(8,128)(2,1)S(1)}, bf16[48,512]{1,0:T(8,128)(2,1)S(1)}, u32[]{:S(2)}, u32[]{:S(2)}) collective-permute-start(bf16[48,512]{1,0:T(8,128)(2,1)S(1)} %collective-permute-done.3.refs_3_), channel_id=1, source_target_pairs={{0,1},{1,0},{2,3},{3,2},{4,5},{5,4},{6,7},{7,6},{8,9},{9,8},{10,11... | collective-permute-start | bytes 147464 | tf_op jit(solution)/shard_map/ppermute | solution.py:224
  16.2 7.3 %collective-permute-start.8 = (bf16[48,512]{1,0:T(8,128)(2,1)S(1)}, bf16[48,512]{1,0:T(8,128)(2,1)S(1)}, u32[]{:S(2)}, u32[]{:S(2)}) collective-permute-start(bf16[48,512]{1,0:T(8,128)(2,1)S(1)} %get-tuple-element.47), channel_id=1, source_target_pairs={{0,14},{1,11},{2,12},{3,9},{4,10},{5,15},{6,8},{7,13},{8,6},{9,3},... | collective-permute-start | bytes 147464 | tf_op jit(solution)/shard_map/ppermute | solution.py:214
  18.1 5.8 %collective-permute-start.9 = (bf16[48,512]{1,0:T(8,128)(2,1)S(1)}, bf16[48,512]{1,0:T(8,128)(2,1)S(1)}, u32[]{:S(2)}, u32[]{:S(2)}) collective-permute-start(bf16[48,512]{1,0:T(8,128)(2,1)S(1)} %get-tuple-element.52), channel_id=1, source_target_pairs={{0,6},{1,13},{2,4},{3,15},{4,2},{5,9},{6,0},{7,11},{8,14},{9,5},{1... | collective-permute-start | bytes 147464 | tf_op jit(solution)/shard_map/ppermute | solution.py:214
  18.5 5.4 %collective-permute-start.10 = (bf16[48,512]{1,0:T(8,128)(2,1)S(1)}, bf16[48,512]{1,0:T(8,128)(2,1)S(1)}, u32[]{:S(2)}, u32[]{:S(2)}) collective-permute-start(bf16[48,512]{1,0:T(8,128)(2,1)S(1)} %get-tuple-element.53), channel_id=1, source_target_pairs={{0,4},{1,9},{2,6},{3,11},{4,0},{5,13},{6,2},{7,15},{8,12},{9,1},{1... | collective-permute-start | bytes 147464 | tf_op jit(solution)/shard_map/ppermute | solution.py:214
  20.4 4.1 %collective-permute-start.11 = (bf16[48,512]{1,0:T(8,128)(2,1)S(1)}, bf16[48,512]{1,0:T(8,128)(2,1)S(1)}, u32[]{:S(2)}, u32[]{:S(2)}) collective-permute-start(bf16[48,512]{1,0:T(8,128)(2,1)S(1)} %get-tuple-element.54), channel_id=1, source_target_pairs={{0,2},{1,3},{2,0},{3,1},{4,6},{5,7},{6,4},{7,5},{8,10},{9,11},{10,... | collective-permute-start | bytes 147464 | tf_op jit(solution)/shard_map/ppermute | solution.py:214
  23.4 1.2 %collective-permute-start.12 = (bf16[48,512]{1,0:T(8,128)(2,1)S(1)}, bf16[48,512]{1,0:T(8,128)(2,1)S(1)}, u32[]{:S(2)}, u32[]{:S(2)}) collective-permute-start(bf16[48,512]{1,0:T(8,128)(2,1)S(1)} %collective-permute-done.8.refs_1_), channel_id=1, source_target_pairs={{0,1},{1,0},{2,3},{3,2},{4,5},{5,4},{6,7},{7,6},{8,9},{9,8},{10,11... | collective-permute-start | bytes 147464 | tf_op jit(solution)/shard_map/ppermute | solution.py:224
  23.9 1.2 %collective-permute-start.13 = (bf16[48,512]{1,0:T(8,128)(2,1)S(1)}, bf16[48,512]{1,0:T(8,128)(2,1)S(1)}, u32[]{:S(2)}, u32[]{:S(2)}) collective-permute-start(bf16[48,512]{1,0:T(8,128)(2,1)S(1)} %collective-permute-done.9.refs_2_), channel_id=1, source_target_pairs={{0,1},{1,0},{2,3},{3,2},{4,5},{5,4},{6,7},{7,6},{8,9},{9,8},{10,11... | collective-permute-start | bytes 147464 | tf_op jit(solution)/shard_map/ppermute | solution.py:224
  23.9 1.3 %collective-permute-start.14 = (bf16[48,512]{1,0:T(8,128)(2,1)S(1)}, bf16[48,512]{1,0:T(8,128)(2,1)S(1)}, u32[]{:S(2)}, u32[]{:S(2)}) collective-permute-start(bf16[48,512]{1,0:T(8,128)(2,1)S(1)} %collective-permute-done.10.refs_3_), channel_id=1, source_target_pairs={{0,1},{1,0},{2,3},{3,2},{4,5},{5,4},{6,7},{7,6},{8,9},{9,8},{10,11... | collective-permute-start | bytes 147464 | tf_op jit(solution)/shard_map/ppermute | solution.py:224

commit v22 on v20

--- a/solution.py
+++ b/solution.py
@@ -61,6 +61,10 @@
 def senders(n, me, core):
     passed = [me ^ jnp.where(core == 0, b, a) for a, b in steps(n) if a != b]
     return partners(n, me, core) + passed
+
+
+def both_orders(n, me):
+    return [me] + [me ^ d for step in steps(n) for d in sorted(set(step), key=step.index)]
 
 
 def in_hbm(*arrays):
@@ -103,7 +107,7 @@
         segment += jnp.where(position >= start_ref[k, me], 1, 0)
     kept_ref[rows:, :slots] = jnp.where(segment == group, 1.0, 0.0).astype(bf16)
     kept_ref[rows : rows + picked, slots : 2 * slots] = slot_rows(chosen_ref, slot_ref, [me], slots)
-    every = slot_rows(chosen_ref, slot_ref, range(n), slots)
+    every = slot_rows(chosen_ref, slot_ref, both_orders(n, me), slots)
     kept_ref[rows:, 2 * slots : 3 * slots] = every[:rows]
     kept_ref[rows:, 3 * slots :] = every[rows:]
     wait_all(gradient)
@@ -190,19 +194,24 @@
 
 
 def final_kernel(n, kept_ref, *refs):
-    got, (a_ref, up_ref, rows_ref) = refs[:n], refs[n:]
-    me, core = lax.axis_index("dp"), lax.axis_index("tensor")
-    piece, picked = up_ref.shape[1], rows_ref.shape[1] - ADAPTER_RANK
+    got, (a_ref, up_ref) = refs[:n], refs[n:]
+    core = lax.axis_index("tensor")
+    piece, picked = up_ref.shape[1], got[0].shape[0] - ADAPTER_RANK
     half, slots = kept_ref.shape[0] // 2, kept_ref.shape[1] // 4
-    for sender, message in zip(senders(n, me, core), got):
-        rows_ref[sender] = message[...]
-    rows = rows_ref[:, :picked, :].reshape(n * picked, rows_ref.shape[2])
+    blocks, passed = [got[0][:picked, :]], iter(got[n // 2 + 1 :])
+    for (a, b), message in zip(steps(n), got[1:]):
+        mine = message[:picked, :]
+        if a == b:
+            blocks.append(mine)
+        else:
+            other = next(passed)[:picked, :]
+            blocks += [jnp.where(core == 0, mine, other), jnp.where(core == 0, other, mine)]
     onehot = jnp.concatenate(
         [kept_ref[half:, 2 * slots : 3 * slots], kept_ref[half:, 3 * slots :]], axis=0
     )
-    a_ref[...] = dot(rows, onehot, 0, 0)
+    a_ref[...] = dot(jnp.concatenate(blocks, axis=0), onehot, 0, 0)
     at = pl.ds(pl.multiple_of(core * piece, piece), piece)
-    up_ref[...] = jnp.sum(rows_ref[:, picked:, at].astype(f32), axis=0)
+    up_ref[...] = sum(message[picked:, at].astype(f32) for message in got)
 
 
 def exchange(messages, tied, beside):
@@ -326,7 +335,6 @@
         out_shape=[shape((column_total, slot_width), f32), shape((ADAPTER_RANK, piece), f32)],
         in_specs=[VMEM] * (1 + n),
         out_specs=[VMEM, VMEM],
-        scratch_shapes=[pltpu.VMEM((n,) + message.shape, bf16)],
         compiler_params=params(8),
     )(kept, own, *got)
     return grad_x, grad_a, up_map_gradient

time: 26.4 us -> 26.3 us (level)
  no operation moved by 1% of the time
where the time goes in v22:
time: 26.3 us; the launch traced here: 26.1 us
  starting transfers between devices  15.8 us (60%)
  Pallas kernels  6.48 us (25%)
  waiting for transfers between devices  3.16 us (12%)
  between operations  0.73 us (3%)
    ppermute x8, starting transfers between devices, exchange(): lax.ppermute(message, ('dp', 'tensor'), [(2 * i + c, 2 * (i ^ step[c]) +...  14.4 us
    ppermute x8, waiting for transfers between devices, exchange(): lax.ppermute(message, ('dp', 'tensor'), [(2 * i + c, 2 * (i ^ step[c]) +...  2.12 us
    pallas_call x1, Pallas kernels, local_kernels(): pl.pallas_call(functools.partial(grad_x_kernel, n), out_shape=shape((tok_...  1.67 us
    pallas_call x1, Pallas kernels, local_kernels(): pl.pallas_call(functools.partial(stage_kernel, n, picked), out_shape=[sha...  1.17 us
    pallas_call x1, Pallas kernels, local_kernels(): pl.pallas_call(functools.partial(pack_kernel, n), out_shape=[message] * c...  1.15 us
    ppermute x6, waiting for transfers between devices, exchange(): lax.ppermute(message, 'tensor', [(0, 1), (1, 0)])  1.03 us
    pallas_call x1, Pallas kernels, local_kernels(): pl.pallas_call(functools.partial(middle_kernel, n), out_shape=[shape((tok...  1 us
    pallas_call x1, Pallas kernels, local_kernels(): pl.pallas_call(functools.partial(final_kernel, n), out_shape=[shape((colu...  0.98 us
  transfers between devices with their start and end apart: 15, of which 9 were waited for; matrix products, arithmetic and copies ran while one was open for 0% of the time, Pallas kernels for 13%

profile of v22, /device:TPU:0, one launch (start us, length us, event | category | flops | bytes accessed | tf_op | source)
XLA Modules:
  0.0 26.1 jit_solution(2911755781926453241)
XLA Ops:
  0.6 1.2 %shard_map.113 = (bf16[48,512]{1,0:T(8,128)(2,1)S(1)}, bf16[48,512]{1,0:T(8,128)(2,1)S(1)}, bf16[48,512]{1,0:T(8,128)(2,1)S(1)}, bf16[48,512]{1,0:T(8,128)(2,1)S(1)}, bf16[48,512]{1,0:T(8,128)(2,1)S(1)}) custom-call(s32[2,8]{1,0:T(2,128)} %bitcast.2, s32[8]{0:T(128)} %slot_hbm.3, bf16[512,128]{1,0:T(8,128)(2,1)} %down_hbm.1, bf16[16,512]{1,0:T(8,128)(2,1)} %up_hbm.1), custom_call_target="tpu_custom_call" | custom-call | tf_op jit(solution)/shard_map/pallas_call | solution.py:269
  1.8 0.5 %collective-permute-start.1 = (bf16[64,4096]{1,0:T(8,128)(2,1)}, bf16[64,4096]{1,0:T(8,128)(2,1)S(1)}, u32[]{:S(2)}, u32[]{:S(2)}) collective-permute-start(bf16[64,4096]{1,0:T(8,128)(2,1)} %x_hbm.1), channel_id=1, source_target_pairs={{0,1},{1,0},{2,3},{3,2},{4,5},{5,4},{6,7},{7,6},{8,9},{9,8},{10,11... | collective-permute-start | bytes 1572872 | tf_op jit(solution)/shard_map/ppermute | solution.py:279
  2.3 5.6 %collective-permute-start = (bf16[48,512]{1,0:T(8,128)(2,1)S(1)}, bf16[48,512]{1,0:T(8,128)(2,1)S(1)}, u32[]{:S(2)}, u32[]{:S(2)}) collective-permute-start(bf16[48,512]{1,0:T(8,128)(2,1)S(1)} %get-tuple-element.35), channel_id=1, source_target_pairs={{0,14},{1,11},{2,12},{3,9},{4,10},{5,15},{6,8},{7,13},{8,6},{9,3},... | collective-permute-start | bytes 147464 | tf_op jit(solution)/shard_map/ppermute | solution.py:220
  7.9 0.0 collective-permute-start.2
  7.9 2.0 %collective-permute-start.3 = (bf16[48,512]{1,0:T(8,128)(2,1)S(1)}, bf16[48,512]{1,0:T(8,128)(2,1)S(1)}, u32[]{:S(2)}, u32[]{:S(2)}) collective-permute-start(bf16[48,512]{1,0:T(8,128)(2,1)S(1)} %get-tuple-element.42), channel_id=1, source_target_pairs={{0,4},{1,9},{2,6},{3,11},{4,0},{5,13},{6,2},{7,15},{8,12},{9,1},{1... | collective-permute-start | bytes 147464 | tf_op jit(solution)/shard_map/ppermute | solution.py:220
  9.9 1.5 %collective-permute-start.4 = (bf16[48,512]{1,0:T(8,128)(2,1)S(1)}, bf16[48,512]{1,0:T(8,128)(2,1)S(1)}, u32[]{:S(2)}, u32[]{:S(2)}) collective-permute-start(bf16[48,512]{1,0:T(8,128)(2,1)S(1)} %get-tuple-element.43), channel_id=1, source_target_pairs={{0,2},{1,3},{2,0},{3,1},{4,6},{5,7},{6,4},{7,5},{8,10},{9,11},{10,... | collective-permute-start | bytes 147464 | tf_op jit(solution)/shard_map/ppermute | solution.py:220
  11.4 1.2 %shard_map.112 = (bf16[64,4096]{1,0:T(8,128)(2,1)S(1)}, bf16[256,512]{1,0:T(8,128)(2,1)S(1)}) custom-call(s32[2,8]{1,0:T(2,128)} %bitcast.4, s32[2,8]{1,0:T(2,128)} %bitcast.3, s32[8]{0:T(128)} %slot_hbm.3, s32[8]{0:T(128)} %count_hbm.1, bf16[128,512]{1,0:T(8,128)(2,1)} %g_hbm.1, bf16[64,4096]{1,0:T(8,128)(2,1)} %x_hbm.1, bf16[2048,512]{1,0:T(8,128)(2,1)} %w_ref.1), custom_call_target="tpu_custom_call" | custom-call | bytes 2097152 | tf_op jit(solution)/shard_map/pallas_call | solution.py:280
  12.6 0.0 copy-start
  12.6 0.0 collective-permute-done.refs_1_
  12.6 0.1 collective-permute-start.5
  12.7 0.4 %collective-permute-done.2.refs_2_ = bf16[48,512]{1,0:T(8,128)(2,1)S(1)} collective-permute-done((bf16[48,512]{1,0:T(8,128)(2,1)S(1)}, bf16[48,512]{1,0:T(8,128)(2,1)S(1)}, u32[]{:S(2)}, u32[]{:S(2)}) %collective-permute-start.2) | collective-permute-done | bytes 49184 | tf_op jit(solution)/shard_map/ppermute | solution.py:220
  13.0 0.1 collective-permute-start.6
  13.2 0.4 %collective-permute-done.3.refs_3_ = bf16[48,512]{1,0:T(8,128)(2,1)S(1)} collective-permute-done((bf16[48,512]{1,0:T(8,128)(2,1)S(1)}, bf16[48,512]{1,0:T(8,128)(2,1)S(1)}, u32[]{:S(2)}, u32[]{:S(2)}) %collective-permute-start.3) | collective-permute-done | bytes 49184 | tf_op jit(solution)/shard_map/ppermute | solution.py:220
  13.6 0.0 collective-permute-start.7
  13.6 0.4 %collective-permute-done.4.refs_4_ = bf16[48,512]{1,0:T(8,128)(2,1)S(1)} collective-permute-done((bf16[48,512]{1,0:T(8,128)(2,1)S(1)}, bf16[48,512]{1,0:T(8,128)(2,1)S(1)}, u32[]{:S(2)}, u32[]{:S(2)}) %collective-permute-start.4) | collective-permute-done | bytes 49184 | tf_op jit(solution)/shard_map/ppermute | solution.py:220
  14.0 0.0 collective-permute-done.1.x_other
  14.0 0.5 %shard_map.114 = (bf16[128,4096]{1,0:T(8,128)(2,1)S(1)}, f32[128,32]{1,0:T(8,128)S(1)}, f32[128,32]{1,0:T(8,128)S(1)}) custom-call(bf16[256,512]{1,0:T(8,128)(2,1)S(1)} %get-tuple-element.30.kept_ref, bf16[64,4096]{1,0:T(8,128)(2,1)S(1)} %get-tuple-element.37.x_mine, bf16[64,4096]{1,0:T(8,128)(2,1)S(1)} %collective-permute-done.1.x_other, ...), custom_call_target="tpu_custom_call" | custom-call | bytes 2097152 | tf_op jit(solution)/shard_map/pallas_call | solution.py:293
  14.5 0.0 collective-permute-done.5.refs_0_.refs_5_
  14.5 0.0 collective-permute-done.6.refs_1_.refs_6_
  14.5 0.3 collective-permute-done.7.refs_2_.refs_7_
  14.8 1.0 %shard_map.115 = (bf16[128,32]{1,0:T(8,128)(2,1)S(1)}, bf16[48,512]{1,0:T(8,128)(2,1)S(1)}, bf16[48,512]{1,0:T(8,128)(2,1)S(1)}, bf16[48,512]{1,0:T(8,128)(2,1)S...) custom-call(bf16[256,512]{1,0:T(8,128)(2,1)S(1)} %get-tuple-element.30.kept_ref, ...), custom_call_target="tpu_custom_call" | custom-call | tf_op jit(solution)/shard_map/pallas_call | solution.py:303
  15.8 1.8 %collective-permute-start.8 = (bf16[48,512]{1,0:T(8,128)(2,1)S(1)}, bf16[48,512]{1,0:T(8,128)(2,1)S(1)}, u32[]{:S(2)}, u32[]{:S(2)}) collective-permute-start(bf16[48,512]{1,0:T(8,128)(2,1)S(1)} %get-tuple-element.47), channel_id=1, source_target_pairs={{0,14},{1,11},{2,12},{3,9},{4,10},{5,15},{6,8},{7,13},{8,6},{9,3},... | collective-permute-start | bytes 147464 | tf_op jit(solution)/shard_map/ppermute | solution.py:220
  17.6 0.1 collective-permute-start.9
  17.7 2.5 %collective-permute-start.10 = (bf16[48,512]{1,0:T(8,128)(2,1)S(1)}, bf16[48,512]{1,0:T(8,128)(2,1)S(1)}, u32[]{:S(2)}, u32[]{:S(2)}) collective-permute-start(bf16[48,512]{1,0:T(8,128)(2,1)S(1)} %get-tuple-element.53), channel_id=1, source_target_pairs={{0,4},{1,9},{2,6},{3,11},{4,0},{5,13},{6,2},{7,15},{8,12},{9,1},{1... | collective-permute-start | bytes 147464 | tf_op jit(solution)/shard_map/ppermute | solution.py:220
  20.3 0.8 %collective-permute-start.11 = (bf16[48,512]{1,0:T(8,128)(2,1)S(1)}, bf16[48,512]{1,0:T(8,128)(2,1)S(1)}, u32[]{:S(2)}, u32[]{:S(2)}) collective-permute-start(bf16[48,512]{1,0:T(8,128)(2,1)S(1)} %get-tuple-element.54), channel_id=1, source_target_pairs={{0,2},{1,3},{2,0},{3,1},{4,6},{5,7},{6,4},{7,5},{8,10},{9,11},{10,... | collective-permute-start | bytes 147464 | tf_op jit(solution)/shard_map/ppermute | solution.py:220
  21.1 0.0 copy-done
  21.1 1.7 %shard_map.116 = bf16[128,2048]{1,0:T(8,128)(2,1)} custom-call(bf16[256,512]{1,0:T(8,128)(2,1)S(1)} %get-tuple-element.30.kept_ref, bf16[2048,512]{1,0:T(8,128)(2,1)S(1)} %copy-done, bf16[128,32]{1,0:T(8,128)(2,1)S(1)} %get-tuple-element.48.dlow_ref, bf16[48,512]{1,0:T(8,128)(2,1)S(1)} %get-tuple-element.39.refs_0_, ...), custom_call_target="tpu_custom_call" | custom-call | flops 285212672 | bytes 2621440 | tf_op jit(solution)/shard_map/pallas_call | solution.py:313
  22.8 0.0 collective-permute-done.8.refs_1_
  22.8 0.0 collective-permute-start.12
  22.9 0.6 %collective-permute-done.9.refs_2_ = bf16[48,512]{1,0:T(8,128)(2,1)S(1)} collective-permute-done((bf16[48,512]{1,0:T(8,128)(2,1)S(1)}, bf16[48,512]{1,0:T(8,128)(2,1)S(1)}, u32[]{:S(2)}, u32[]{:S(2)}) %collective-permute-start.9) | collective-permute-done | bytes 49184 | tf_op jit(solution)/shard_map/ppermute | solution.py:220
  23.5 0.0 collective-permute-start.13
  23.5 0.2 collective-permute-done.10.refs_3_
  23.7 0.6 %collective-permute-start.14 = (bf16[48,512]{1,0:T(8,128)(2,1)S(1)}, bf16[48,512]{1,0:T(8,128)(2,1)S(1)}, u32[]{:S(2)}, u32[]{:S(2)}) collective-permute-start(bf16[48,512]{1,0:T(8,128)(2,1)S(1)} %collective-permute-done.10.refs_3_), channel_id=1, source_target_pairs={{0,1},{1,0},{2,3},{3,2},{4,5},{5,4},{6,7},{7,6},{8,9},{9,8},{10,11... | collective-permute-start | bytes 147464 | tf_op jit(solution)/shard_map/ppermute | solution.py:230
  24.3 0.1 collective-permute-done.11.refs_4_
  24.4 0.0 collective-permute-done.12.refs_5_
  24.4 0.3 %collective-permute-done.13.refs_6_ = bf16[48,512]{1,0:T(8,128)(2,1)S(1)} collective-permute-done((bf16[48,512]{1,0:T(8,128)(2,1)S(1)}, bf16[48,512]{1,0:T(8,128)(2,1)S(1)}, u32[]{:S(2)}, u32[]{:S(2)}) %collective-permute-start.13) | collective-permute-done | bytes 49184 | tf_op jit(solution)/shard_map/ppermute | solution.py:230
  24.7 0.5 %collective-permute-done.14.refs_7_ = bf16[48,512]{1,0:T(8,128)(2,1)S(1)} collective-permute-done((bf16[48,512]{1,0:T(8,128)(2,1)S(1)}, bf16[48,512]{1,0:T(8,128)(2,1)S(1)}, u32[]{:S(2)}, u32[]{:S(2)}) %collective-permute-start.14) | collective-permute-done | bytes 49184 | tf_op jit(solution)/shard_map/ppermute | solution.py:230
  25.1 1.0 %shard_map.117 = (f32[512,128]{1,0:T(8,128)}, f32[16,256]{1,0:T(8,128)}) custom-call(bf16[256,512]{1,0:T(8,128)(2,1)S(1)} %get-tuple-element.30.kept_ref, bf16[48,512]{1,0:T(8,128)(2,1)S(1)} %get-tuple-element.50.refs_0_, bf16[48,512]{1,0:T(8,128)(2,1)S(1)} %collective-permute-done.8.refs_1_, bf16[48,512]{1,0:T(8,128)(2,1)S(1)} %collective-permute-done.9.refs_2_, ...), custom_call_target="tpu_custom_call" | custom-call | tf_op jit(solution)/shard_map/pallas_call | solution.py:333
Async XLA Ops:
  1.8 12.2 %collective-permute-start.1 = (bf16[64,4096]{1,0:T(8,128)(2,1)}, bf16[64,4096]{1,0:T(8,128)(2,1)S(1)}, u32[]{:S(2)}, u32[]{:S(2)}) collective-permute-start(bf16[64,4096]{1,0:T(8,128)(2,1)} %x_hbm.1), channel_id=1, source_target_pairs={{0,1},{1,0},{2,3},{3,2},{4,5},{5,4},{6,7},{7,6},{8,9},{9,8},{10,11... | collective-permute-start | bytes 1572872 | tf_op jit(solution)/shard_map/ppermute | solution.py:279
  2.3 10.3 %collective-permute-start = (bf16[48,512]{1,0:T(8,128)(2,1)S(1)}, bf16[48,512]{1,0:T(8,128)(2,1)S(1)}, u32[]{:S(2)}, u32[]{:S(2)}) collective-permute-start(bf16[48,512]{1,0:T(8,128)(2,1)S(1)} %get-tuple-element.35), channel_id=1, source_target_pairs={{0,14},{1,11},{2,12},{3,9},{4,10},{5,15},{6,8},{7,13},{8,6},{9,3},... | collective-permute-start | bytes 147464 | tf_op jit(solution)/shard_map/ppermute | solution.py:220
  7.9 5.1 %collective-permute-start.2 = (bf16[48,512]{1,0:T(8,128)(2,1)S(1)}, bf16[48,512]{1,0:T(8,128)(2,1)S(1)}, u32[]{:S(2)}, u32[]{:S(2)}) collective-permute-start(bf16[48,512]{1,0:T(8,128)(2,1)S(1)} %get-tuple-element.41), channel_id=1, source_target_pairs={{0,6},{1,13},{2,4},{3,15},{4,2},{5,9},{6,0},{7,11},{8,14},{9,5},{1... | collective-permute-start | bytes 147464 | tf_op jit(solution)/shard_map/ppermute | solution.py:220
  7.9 5.6 %collective-permute-start.3 = (bf16[48,512]{1,0:T(8,128)(2,1)S(1)}, bf16[48,512]{1,0:T(8,128)(2,1)S(1)}, u32[]{:S(2)}, u32[]{:S(2)}) collective-permute-start(bf16[48,512]{1,0:T(8,128)(2,1)S(1)} %get-tuple-element.42), channel_id=1, source_target_pairs={{0,4},{1,9},{2,6},{3,11},{4,0},{5,13},{6,2},{7,15},{8,12},{9,1},{1... | collective-permute-start | bytes 147464 | tf_op jit(solution)/shard_map/ppermute | solution.py:220
  9.9 4.1 %collective-permute-start.4 = (bf16[48,512]{1,0:T(8,128)(2,1)S(1)}, bf16[48,512]{1,0:T(8,128)(2,1)S(1)}, u32[]{:S(2)}, u32[]{:S(2)}) collective-permute-start(bf16[48,512]{1,0:T(8,128)(2,1)S(1)} %get-tuple-element.43), channel_id=1, source_target_pairs={{0,2},{1,3},{2,0},{3,1},{4,6},{5,7},{6,4},{7,5},{8,10},{9,11},{10,... | collective-permute-start | bytes 147464 | tf_op jit(solution)/shard_map/ppermute | solution.py:220
  12.6 8.5 %copy-start = (bf16[2048,512]{1,0:T(8,128)(2,1)S(1)}, bf16[2048,512]{1,0:T(8,128)(2,1)}, u32[]{:S(2)}) copy-start(bf16[2048,512]{1,0:T(8,128)(2,1)} %w_ref.1) | copy-start | bytes 6291460
  12.6 1.9 %collective-permute-start.5 = (bf16[48,512]{1,0:T(8,128)(2,1)S(1)}, bf16[48,512]{1,0:T(8,128)(2,1)S(1)}, u32[]{:S(2)}, u32[]{:S(2)}) collective-permute-start(bf16[48,512]{1,0:T(8,128)(2,1)S(1)} %collective-permute-done.refs_1_), channel_id=1, source_target_pairs={{0,1},{1,0},{2,3},{3,2},{4,5},{5,4},{6,7},{7,6},{8,9},{9,8},{10,11... | collective-permute-start | bytes 147464 | tf_op jit(solution)/shard_map/ppermute | solution.py:230
  13.0 1.5 %collective-permute-start.6 = (bf16[48,512]{1,0:T(8,128)(2,1)S(1)}, bf16[48,512]{1,0:T(8,128)(2,1)S(1)}, u32[]{:S(2)}, u32[]{:S(2)}) collective-permute-start(bf16[48,512]{1,0:T(8,128)(2,1)S(1)} %collective-permute-done.2.refs_2_), channel_id=1, source_target_pairs={{0,1},{1,0},{2,3},{3,2},{4,5},{5,4},{6,7},{7,6},{8,9},{9,8},{10,11... | collective-permute-start | bytes 147464 | tf_op jit(solution)/shard_map/ppermute | solution.py:230
  13.6 1.2 %collective-permute-start.7 = (bf16[48,512]{1,0:T(8,128)(2,1)S(1)}, bf16[48,512]{1,0:T(8,128)(2,1)S(1)}, u32[]{:S(2)}, u32[]{:S(2)}) collective-permute-start(bf16[48,512]{1,0:T(8,128)(2,1)S(1)} %collective-permute-done.3.refs_3_), channel_id=1, source_target_pairs={{0,1},{1,0},{2,3},{3,2},{4,5},{5,4},{6,7},{7,6},{8,9},{9,8},{10,11... | collective-permute-start | bytes 147464 | tf_op jit(solution)/shard_map/ppermute | solution.py:230
  15.8 7.1 %collective-permute-start.8 = (bf16[48,512]{1,0:T(8,128)(2,1)S(1)}, bf16[48,512]{1,0:T(8,128)(2,1)S(1)}, u32[]{:S(2)}, u32[]{:S(2)}) collective-permute-start(bf16[48,512]{1,0:T(8,128)(2,1)S(1)} %get-tuple-element.47), channel_id=1, source_target_pairs={{0,14},{1,11},{2,12},{3,9},{4,10},{5,15},{6,8},{7,13},{8,6},{9,3},... | collective-permute-start | bytes 147464 | tf_op jit(solution)/shard_map/ppermute | solution.py:220
  17.6 5.8 %collective-permute-start.9 = (bf16[48,512]{1,0:T(8,128)(2,1)S(1)}, bf16[48,512]{1,0:T(8,128)(2,1)S(1)}, u32[]{:S(2)}, u32[]{:S(2)}) collective-permute-start(bf16[48,512]{1,0:T(8,128)(2,1)S(1)} %get-tuple-element.52), channel_id=1, source_target_pairs={{0,6},{1,13},{2,4},{3,15},{4,2},{5,9},{6,0},{7,11},{8,14},{9,5},{1... | collective-permute-start | bytes 147464 | tf_op jit(solution)/shard_map/ppermute | solution.py:220
  17.7 6.0 %collective-permute-start.10 = (bf16[48,512]{1,0:T(8,128)(2,1)S(1)}, bf16[48,512]{1,0:T(8,128)(2,1)S(1)}, u32[]{:S(2)}, u32[]{:S(2)}) collective-permute-start(bf16[48,512]{1,0:T(8,128)(2,1)S(1)} %get-tuple-element.53), channel_id=1, source_target_pairs={{0,4},{1,9},{2,6},{3,11},{4,0},{5,13},{6,2},{7,15},{8,12},{9,1},{1... | collective-permute-start | bytes 147464 | tf_op jit(solution)/shard_map/ppermute | solution.py:220
  20.3 4.1 %collective-permute-start.11 = (bf16[48,512]{1,0:T(8,128)(2,1)S(1)}, bf16[48,512]{1,0:T(8,128)(2,1)S(1)}, u32[]{:S(2)}, u32[]{:S(2)}) collective-permute-start(bf16[48,512]{1,0:T(8,128)(2,1)S(1)} %get-tuple-element.54), channel_id=1, source_target_pairs={{0,2},{1,3},{2,0},{3,1},{4,6},{5,7},{6,4},{7,5},{8,10},{9,11},{10,... | collective-permute-start | bytes 147464 | tf_op jit(solution)/shard_map/ppermute | solution.py:220
  22.8 1.5 %collective-permute-start.12 = (bf16[48,512]{1,0:T(8,128)(2,1)S(1)}, bf16[48,512]{1,0:T(8,128)(2,1)S(1)}, u32[]{:S(2)}, u32[]{:S(2)}) collective-permute-start(bf16[48,512]{1,0:T(8,128)(2,1)S(1)} %collective-permute-done.8.refs_1_), channel_id=1, source_target_pairs={{0,1},{1,0},{2,3},{3,2},{4,5},{5,4},{6,7},{7,6},{8,9},{9,8},{10,11... | collective-permute-start | bytes 147464 | tf_op jit(solution)/shard_map/ppermute | solution.py:230
  23.5 1.2 %collective-permute-start.13 = (bf16[48,512]{1,0:T(8,128)(2,1)S(1)}, bf16[48,512]{1,0:T(8,128)(2,1)S(1)}, u32[]{:S(2)}, u32[]{:S(2)}) collective-permute-start(bf16[48,512]{1,0:T(8,128)(2,1)S(1)} %collective-permute-done.9.refs_2_), channel_id=1, source_target_pairs={{0,1},{1,0},{2,3},{3,2},{4,5},{5,4},{6,7},{7,6},{8,9},{9,8},{10,11... | collective-permute-start | bytes 147464 | tf_op jit(solution)/shard_map/ppermute | solution.py:230
  23.7 1.4 %collective-permute-start.14 = (bf16[48,512]{1,0:T(8,128)(2,1)S(1)}, bf16[48,512]{1,0:T(8,128)(2,1)S(1)}, u32[]{:S(2)}, u32[]{:S(2)}) collective-permute-start(bf16[48,512]{1,0:T(8,128)(2,1)S(1)} %collective-permute-done.10.refs_3_), channel_id=1, source_target_pairs={{0,1},{1,0},{2,3},{3,2},{4,5},{5,4},{6,7},{7,6},{8,9},{9,8},{10,11... | collective-permute-start | bytes 147464 | tf_op jit(solution)/shard_map/ppermute | solution.py:230

commit v23 on v20

--- a/solution.py
+++ b/solution.py
@@ -51,7 +51,7 @@
 
 
 def steps(n):
-    return [(n - 1, n // 2 + 1), (3, n - 2), (2, n // 2), (1, 1)]
+    return [(n - 1, n // 2 + 1), (2, n - 2), (3, n // 2), (1, 1)]
 
 
 def partners(n, me, core):

time: 26.4 us -> 26.5 us (level)
  no operation moved by 1% of the time
where the time goes in v23:
time: 26.5 us; the launch traced here: 26.3 us
  starting transfers between devices  16 us (60%)
  Pallas kernels  6.5 us (25%)
  waiting for transfers between devices  3.07 us (12%)
  between operations  0.72 us (3%)
    ppermute x8, starting transfers between devices, exchange(): lax.ppermute(message, ('dp', 'tensor'), [(2 * i + c, 2 * (i ^ step[c]) +...  14.5 us
    ppermute x8, waiting for transfers between devices, exchange(): lax.ppermute(message, ('dp', 'tensor'), [(2 * i + c, 2 * (i ^ step[c]) +...  2.07 us
    pallas_call x1, Pallas kernels, local_kernels(): pl.pallas_call(functools.partial(grad_x_kernel, n), out_shape=shape((tok_...  1.67 us
    pallas_call x1, Pallas kernels, local_kernels(): pl.pallas_call(functools.partial(stage_kernel, n, picked), out_shape=[sha...  1.17 us
    pallas_call x1, Pallas kernels, local_kernels(): pl.pallas_call(functools.partial(pack_kernel, n), out_shape=[message] * c...  1.15 us
    pallas_call x1, Pallas kernels, local_kernels(): pl.pallas_call(functools.partial(final_kernel, n), out_shape=[shape((colu...  1.01 us
    pallas_call x1, Pallas kernels, local_kernels(): pl.pallas_call(functools.partial(middle_kernel, n), out_shape=[shape((tok...  1 us
    ppermute x6, waiting for transfers between devices, exchange(): lax.ppermute(message, 'tensor', [(0, 1), (1, 0)])  1 us
  transfers between devices with their start and end apart: 15, of which 9 were waited for; matrix products, arithmetic and copies ran while one was open for 0% of the time, Pallas kernels for 13%

profile of v23, /device:TPU:0, one launch (start us, length us, event | category | flops | bytes accessed | tf_op | source)
XLA Modules:
  0.0 26.3 jit_solution(17385418570353782498)
XLA Ops:
  0.6 1.2 %shard_map.113 = (bf16[48,512]{1,0:T(8,128)(2,1)S(1)}, bf16[48,512]{1,0:T(8,128)(2,1)S(1)}, bf16[48,512]{1,0:T(8,128)(2,1)S(1)}, bf16[48,512]{1,0:T(8,128)(2,1)S(1)}, bf16[48,512]{1,0:T(8,128)(2,1)S(1)}) custom-call(s32[2,8]{1,0:T(2,128)} %bitcast.2, s32[8]{0:T(128)} %slot_hbm.3, bf16[512,128]{1,0:T(8,128)(2,1)} %down_hbm.1, bf16[16,512]{1,0:T(8,128)(2,1)} %up_hbm.1), custom_call_target="tpu_custom_call" | custom-call | tf_op jit(solution)/shard_map/pallas_call | solution.py:260
  1.8 0.5 %collective-permute-start.1 = (bf16[64,4096]{1,0:T(8,128)(2,1)}, bf16[64,4096]{1,0:T(8,128)(2,1)S(1)}, u32[]{:S(2)}, u32[]{:S(2)}) collective-permute-start(bf16[64,4096]{1,0:T(8,128)(2,1)} %x_hbm.1), channel_id=1, source_target_pairs={{0,1},{1,0},{2,3},{3,2},{4,5},{5,4},{6,7},{7,6},{8,9},{9,8},{10,11... | collective-permute-start | bytes 1572872 | tf_op jit(solution)/shard_map/ppermute | solution.py:270
  2.3 5.6 %collective-permute-start = (bf16[48,512]{1,0:T(8,128)(2,1)S(1)}, bf16[48,512]{1,0:T(8,128)(2,1)S(1)}, u32[]{:S(2)}, u32[]{:S(2)}) collective-permute-start(bf16[48,512]{1,0:T(8,128)(2,1)S(1)} %get-tuple-element.35), channel_id=1, source_target_pairs={{0,14},{1,11},{2,12},{3,9},{4,10},{5,15},{6,8},{7,13},{8,6},{9,3},... | collective-permute-start | bytes 147464 | tf_op jit(solution)/shard_map/ppermute | solution.py:211
  7.9 0.0 collective-permute-start.2
  7.9 2.0 %collective-permute-start.3 = (bf16[48,512]{1,0:T(8,128)(2,1)S(1)}, bf16[48,512]{1,0:T(8,128)(2,1)S(1)}, u32[]{:S(2)}, u32[]{:S(2)}) collective-permute-start(bf16[48,512]{1,0:T(8,128)(2,1)S(1)} %get-tuple-element.42), channel_id=1, source_target_pairs={{0,6},{1,9},{2,4},{3,11},{4,2},{5,13},{6,0},{7,15},{8,14},{9,1},{1... | collective-permute-start | bytes 147464 | tf_op jit(solution)/shard_map/ppermute | solution.py:211
  9.9 1.5 %collective-permute-start.4 = (bf16[48,512]{1,0:T(8,128)(2,1)S(1)}, bf16[48,512]{1,0:T(8,128)(2,1)S(1)}, u32[]{:S(2)}, u32[]{:S(2)}) collective-permute-start(bf16[48,512]{1,0:T(8,128)(2,1)S(1)} %get-tuple-element.43), channel_id=1, source_target_pairs={{0,2},{1,3},{2,0},{3,1},{4,6},{5,7},{6,4},{7,5},{8,10},{9,11},{10,... | collective-permute-start | bytes 147464 | tf_op jit(solution)/shard_map/ppermute | solution.py:211
  11.4 1.2 %shard_map.112 = (bf16[64,4096]{1,0:T(8,128)(2,1)S(1)}, bf16[256,512]{1,0:T(8,128)(2,1)S(1)}) custom-call(s32[2,8]{1,0:T(2,128)} %bitcast.4, s32[2,8]{1,0:T(2,128)} %bitcast.3, s32[8]{0:T(128)} %slot_hbm.3, s32[8]{0:T(128)} %count_hbm.1, bf16[128,512]{1,0:T(8,128)(2,1)} %g_hbm.1, bf16[64,4096]{1,0:T(8,128)(2,1)} %x_hbm.1, bf16[2048,512]{1,0:T(8,128)(2,1)} %w_ref.1), custom_call_target="tpu_custom_call" | custom-call | bytes 2097152 | tf_op jit(solution)/shard_map/pallas_call | solution.py:271
  12.6 0.0 copy-start
  12.6 0.0 collective-permute-done.refs_1_
  12.6 0.1 collective-permute-start.5
  12.7 0.3 %collective-permute-done.2.refs_2_ = bf16[48,512]{1,0:T(8,128)(2,1)S(1)} collective-permute-done((bf16[48,512]{1,0:T(8,128)(2,1)S(1)}, bf16[48,512]{1,0:T(8,128)(2,1)S(1)}, u32[]{:S(2)}, u32[]{:S(2)}) %collective-permute-start.2) | collective-permute-done | bytes 49184 | tf_op jit(solution)/shard_map/ppermute | solution.py:211
  13.0 0.2 collective-permute-start.6
  13.2 0.3 %collective-permute-done.3.refs_3_ = bf16[48,512]{1,0:T(8,128)(2,1)S(1)} collective-permute-done((bf16[48,512]{1,0:T(8,128)(2,1)S(1)}, bf16[48,512]{1,0:T(8,128)(2,1)S(1)}, u32[]{:S(2)}, u32[]{:S(2)}) %collective-permute-start.3) | collective-permute-done | bytes 49184 | tf_op jit(solution)/shard_map/ppermute | solution.py:211
  13.5 0.0 collective-permute-start.7
  13.5 0.5 %collective-permute-done.4.refs_4_ = bf16[48,512]{1,0:T(8,128)(2,1)S(1)} collective-permute-done((bf16[48,512]{1,0:T(8,128)(2,1)S(1)}, bf16[48,512]{1,0:T(8,128)(2,1)S(1)}, u32[]{:S(2)}, u32[]{:S(2)}) %collective-permute-start.4) | collective-permute-done | bytes 49184 | tf_op jit(solution)/shard_map/ppermute | solution.py:211
  14.0 0.0 collective-permute-done.1.x_other
  14.1 0.5 %shard_map.114 = (bf16[128,4096]{1,0:T(8,128)(2,1)S(1)}, f32[128,32]{1,0:T(8,128)S(1)}, f32[128,32]{1,0:T(8,128)S(1)}) custom-call(bf16[256,512]{1,0:T(8,128)(2,1)S(1)} %get-tuple-element.30.kept_ref, bf16[64,4096]{1,0:T(8,128)(2,1)S(1)} %get-tuple-element.37.x_mine, bf16[64,4096]{1,0:T(8,128)(2,1)S(1)} %collective-permute-done.1.x_other, ...), custom_call_target="tpu_custom_call" | custom-call | bytes 2097152 | tf_op jit(solution)/shard_map/pallas_call | solution.py:284
  14.6 0.0 collective-permute-done.5.refs_0_.refs_5_
  14.6 0.0 collective-permute-done.6.refs_1_.refs_6_
  14.6 0.2 collective-permute-done.7.refs_2_.refs_7_
  14.8 1.0 %shard_map.115 = (bf16[128,32]{1,0:T(8,128)(2,1)S(1)}, bf16[48,512]{1,0:T(8,128)(2,1)S(1)}, bf16[48,512]{1,0:T(8,128)(2,1)S(1)}, bf16[48,512]{1,0:T(8,128)(2,1)S...) custom-call(bf16[256,512]{1,0:T(8,128)(2,1)S(1)} %get-tuple-element.30.kept_ref, ...), custom_call_target="tpu_custom_call" | custom-call | tf_op jit(solution)/shard_map/pallas_call | solution.py:294
  15.8 2.0 %collective-permute-start.8 = (bf16[48,512]{1,0:T(8,128)(2,1)S(1)}, bf16[48,512]{1,0:T(8,128)(2,1)S(1)}, u32[]{:S(2)}, u32[]{:S(2)}) collective-permute-start(bf16[48,512]{1,0:T(8,128)(2,1)S(1)} %get-tuple-element.47), channel_id=1, source_target_pairs={{0,14},{1,11},{2,12},{3,9},{4,10},{5,15},{6,8},{7,13},{8,6},{9,3},... | collective-permute-start | bytes 147464 | tf_op jit(solution)/shard_map/ppermute | solution.py:211
  17.7 0.0 collective-permute-start.9
  17.7 2.6 %collective-permute-start.10 = (bf16[48,512]{1,0:T(8,128)(2,1)S(1)}, bf16[48,512]{1,0:T(8,128)(2,1)S(1)}, u32[]{:S(2)}, u32[]{:S(2)}) collective-permute-start(bf16[48,512]{1,0:T(8,128)(2,1)S(1)} %get-tuple-element.53), channel_id=1, source_target_pairs={{0,6},{1,9},{2,4},{3,11},{4,2},{5,13},{6,0},{7,15},{8,14},{9,1},{1... | collective-permute-start | bytes 147464 | tf_op jit(solution)/shard_map/ppermute | solution.py:211
  20.3 0.9 %collective-permute-start.11 = (bf16[48,512]{1,0:T(8,128)(2,1)S(1)}, bf16[48,512]{1,0:T(8,128)(2,1)S(1)}, u32[]{:S(2)}, u32[]{:S(2)}) collective-permute-start(bf16[48,512]{1,0:T(8,128)(2,1)S(1)} %get-tuple-element.54), channel_id=1, source_target_pairs={{0,2},{1,3},{2,0},{3,1},{4,6},{5,7},{6,4},{7,5},{8,10},{9,11},{10,... | collective-permute-start | bytes 147464 | tf_op jit(solution)/shard_map/ppermute | solution.py:211
  21.2 0.0 copy-done
  21.2 1.7 %shard_map.116 = bf16[128,2048]{1,0:T(8,128)(2,1)} custom-call(bf16[256,512]{1,0:T(8,128)(2,1)S(1)} %get-tuple-element.30.kept_ref, bf16[2048,512]{1,0:T(8,128)(2,1)S(1)} %copy-done, bf16[128,32]{1,0:T(8,128)(2,1)S(1)} %get-tuple-element.48.dlow_ref, bf16[48,512]{1,0:T(8,128)(2,1)S(1)} %get-tuple-element.39.refs_0_, ...), custom_call_target="tpu_custom_call" | custom-call | flops 285212672 | bytes 2621440 | tf_op jit(solution)/shard_map/pallas_call | solution.py:304
  22.9 0.3 %collective-permute-done.8.refs_1_ = bf16[48,512]{1,0:T(8,128)(2,1)S(1)} collective-permute-done((bf16[48,512]{1,0:T(8,128)(2,1)S(1)}, bf16[48,512]{1,0:T(8,128)(2,1)S(1)}, u32[]{:S(2)}, u32[]{:S(2)}) %collective-permute-start.8) | collective-permute-done | bytes 49184 | tf_op jit(solution)/shard_map/ppermute | solution.py:211
  23.2 0.0 collective-permute-start.12
  23.2 0.0 collective-permute-done.9.refs_2_
  23.2 0.5 %collective-permute-start.13 = (bf16[48,512]{1,0:T(8,128)(2,1)S(1)}, bf16[48,512]{1,0:T(8,128)(2,1)S(1)}, u32[]{:S(2)}, u32[]{:S(2)}) collective-permute-start(bf16[48,512]{1,0:T(8,128)(2,1)S(1)} %collective-permute-done.9.refs_2_), channel_id=1, source_target_pairs={{0,1},{1,0},{2,3},{3,2},{4,5},{5,4},{6,7},{7,6},{8,9},{9,8},{10,11... | collective-permute-start | bytes 147464 | tf_op jit(solution)/shard_map/ppermute | solution.py:221
  23.7 0.4 %collective-permute-done.10.refs_3_ = bf16[48,512]{1,0:T(8,128)(2,1)S(1)} collective-permute-done((bf16[48,512]{1,0:T(8,128)(2,1)S(1)}, bf16[48,512]{1,0:T(8,128)(2,1)S(1)}, u32[]{:S(2)}, u32[]{:S(2)}) %collective-permute-start.10) | collective-permute-done | bytes 49184 | tf_op jit(solution)/shard_map/ppermute | solution.py:211
  24.1 0.2 collective-permute-start.14
  24.3 0.2 collective-permute-done.11.refs_4_
  24.5 0.0 collective-permute-done.12.refs_5_
  24.5 0.1 collective-permute-done.13.refs_6_
  24.6 0.7 %collective-permute-done.14.refs_7_ = bf16[48,512]{1,0:T(8,128)(2,1)S(1)} collective-permute-done((bf16[48,512]{1,0:T(8,128)(2,1)S(1)}, bf16[48,512]{1,0:T(8,128)(2,1)S(1)}, u32[]{:S(2)}, u32[]{:S(2)}) %collective-permute-start.14) | collective-permute-done | bytes 49184 | tf_op jit(solution)/shard_map/ppermute | solution.py:221
  25.3 1.0 %shard_map.117 = (f32[512,128]{1,0:T(8,128)}, f32[16,256]{1,0:T(8,128)}) custom-call(bf16[256,512]{1,0:T(8,128)(2,1)S(1)} %get-tuple-element.30.kept_ref, bf16[48,512]{1,0:T(8,128)(2,1)S(1)} %get-tuple-element.50.refs_0_, bf16[48,512]{1,0:T(8,128)(2,1)S(1)} %collective-permute-done.8.refs_1_, bf16[48,512]{1,0:T(8,128)(2,1)S(1)} %collective-permute-done.9.refs_2_, ...), custom_call_target="tpu_custom_call" | custom-call | tf_op jit(solution)/shard_map/pallas_call | solution.py:324
Async XLA Ops:
  1.8 12.3 %collective-permute-start.1 = (bf16[64,4096]{1,0:T(8,128)(2,1)}, bf16[64,4096]{1,0:T(8,128)(2,1)S(1)}, u32[]{:S(2)}, u32[]{:S(2)}) collective-permute-start(bf16[64,4096]{1,0:T(8,128)(2,1)} %x_hbm.1), channel_id=1, source_target_pairs={{0,1},{1,0},{2,3},{3,2},{4,5},{5,4},{6,7},{7,6},{8,9},{9,8},{10,11... | collective-permute-start | bytes 1572872 | tf_op jit(solution)/shard_map/ppermute | solution.py:270
  2.3 10.3 %collective-permute-start = (bf16[48,512]{1,0:T(8,128)(2,1)S(1)}, bf16[48,512]{1,0:T(8,128)(2,1)S(1)}, u32[]{:S(2)}, u32[]{:S(2)}) collective-permute-start(bf16[48,512]{1,0:T(8,128)(2,1)S(1)} %get-tuple-element.35), channel_id=1, source_target_pairs={{0,14},{1,11},{2,12},{3,9},{4,10},{5,15},{6,8},{7,13},{8,6},{9,3},... | collective-permute-start | bytes 147464 | tf_op jit(solution)/shard_map/ppermute | solution.py:211
  7.9 5.1 %collective-permute-start.2 = (bf16[48,512]{1,0:T(8,128)(2,1)S(1)}, bf16[48,512]{1,0:T(8,128)(2,1)S(1)}, u32[]{:S(2)}, u32[]{:S(2)}) collective-permute-start(bf16[48,512]{1,0:T(8,128)(2,1)S(1)} %get-tuple-element.41), channel_id=1, source_target_pairs={{0,4},{1,13},{2,6},{3,15},{4,0},{5,9},{6,2},{7,11},{8,12},{9,5},{1... | collective-permute-start | bytes 147464 | tf_op jit(solution)/shard_map/ppermute | solution.py:211
  7.9 5.6 %collective-permute-start.3 = (bf16[48,512]{1,0:T(8,128)(2,1)S(1)}, bf16[48,512]{1,0:T(8,128)(2,1)S(1)}, u32[]{:S(2)}, u32[]{:S(2)}) collective-permute-start(bf16[48,512]{1,0:T(8,128)(2,1)S(1)} %get-tuple-element.42), channel_id=1, source_target_pairs={{0,6},{1,9},{2,4},{3,11},{4,2},{5,13},{6,0},{7,15},{8,14},{9,1},{1... | collective-permute-start | bytes 147464 | tf_op jit(solution)/shard_map/ppermute | solution.py:211
  9.9 4.1 %collective-permute-start.4 = (bf16[48,512]{1,0:T(8,128)(2,1)S(1)}, bf16[48,512]{1,0:T(8,128)(2,1)S(1)}, u32[]{:S(2)}, u32[]{:S(2)}) collective-permute-start(bf16[48,512]{1,0:T(8,128)(2,1)S(1)} %get-tuple-element.43), channel_id=1, source_target_pairs={{0,2},{1,3},{2,0},{3,1},{4,6},{5,7},{6,4},{7,5},{8,10},{9,11},{10,... | collective-permute-start | bytes 147464 | tf_op jit(solution)/shard_map/ppermute | solution.py:211
  12.6 8.6 %copy-start = (bf16[2048,512]{1,0:T(8,128)(2,1)S(1)}, bf16[2048,512]{1,0:T(8,128)(2,1)}, u32[]{:S(2)}) copy-start(bf16[2048,512]{1,0:T(8,128)(2,1)} %w_ref.1) | copy-start | bytes 6291460
  12.6 2.0 %collective-permute-start.5 = (bf16[48,512]{1,0:T(8,128)(2,1)S(1)}, bf16[48,512]{1,0:T(8,128)(2,1)S(1)}, u32[]{:S(2)}, u32[]{:S(2)}) collective-permute-start(bf16[48,512]{1,0:T(8,128)(2,1)S(1)} %collective-permute-done.refs_1_), channel_id=1, source_target_pairs={{0,1},{1,0},{2,3},{3,2},{4,5},{5,4},{6,7},{7,6},{8,9},{9,8},{10,11... | collective-permute-start | bytes 147464 | tf_op jit(solution)/shard_map/ppermute | solution.py:221
  13.0 1.5 %collective-permute-start.6 = (bf16[48,512]{1,0:T(8,128)(2,1)S(1)}, bf16[48,512]{1,0:T(8,128)(2,1)S(1)}, u32[]{:S(2)}, u32[]{:S(2)}) collective-permute-start(bf16[48,512]{1,0:T(8,128)(2,1)S(1)} %collective-permute-done.2.refs_2_), channel_id=1, source_target_pairs={{0,1},{1,0},{2,3},{3,2},{4,5},{5,4},{6,7},{7,6},{8,9},{9,8},{10,11... | collective-permute-start | bytes 147464 | tf_op jit(solution)/shard_map/ppermute | solution.py:221
  13.5 1.2 %collective-permute-start.7 = (bf16[48,512]{1,0:T(8,128)(2,1)S(1)}, bf16[48,512]{1,0:T(8,128)(2,1)S(1)}, u32[]{:S(2)}, u32[]{:S(2)}) collective-permute-start(bf16[48,512]{1,0:T(8,128)(2,1)S(1)} %collective-permute-done.3.refs_3_), channel_id=1, source_target_pairs={{0,1},{1,0},{2,3},{3,2},{4,5},{5,4},{6,7},{7,6},{8,9},{9,8},{10,11... | collective-permute-start | bytes 147464 | tf_op jit(solution)/shard_map/ppermute | solution.py:221
  15.8 7.4 %collective-permute-start.8 = (bf16[48,512]{1,0:T(8,128)(2,1)S(1)}, bf16[48,512]{1,0:T(8,128)(2,1)S(1)}, u32[]{:S(2)}, u32[]{:S(2)}) collective-permute-start(bf16[48,512]{1,0:T(8,128)(2,1)S(1)} %get-tuple-element.47), channel_id=1, source_target_pairs={{0,14},{1,11},{2,12},{3,9},{4,10},{5,15},{6,8},{7,13},{8,6},{9,3},... | collective-permute-start | bytes 147464 | tf_op jit(solution)/shard_map/ppermute | solution.py:211
  17.7 5.5 %collective-permute-start.9 = (bf16[48,512]{1,0:T(8,128)(2,1)S(1)}, bf16[48,512]{1,0:T(8,128)(2,1)S(1)}, u32[]{:S(2)}, u32[]{:S(2)}) collective-permute-start(bf16[48,512]{1,0:T(8,128)(2,1)S(1)} %get-tuple-element.52), channel_id=1, source_target_pairs={{0,4},{1,13},{2,6},{3,15},{4,0},{5,9},{6,2},{7,11},{8,12},{9,5},{1... | collective-permute-start | bytes 147464 | tf_op jit(solution)/shard_map/ppermute | solution.py:211
  17.7 6.4 %collective-permute-start.10 = (bf16[48,512]{1,0:T(8,128)(2,1)S(1)}, bf16[48,512]{1,0:T(8,128)(2,1)S(1)}, u32[]{:S(2)}, u32[]{:S(2)}) collective-permute-start(bf16[48,512]{1,0:T(8,128)(2,1)S(1)} %get-tuple-element.53), channel_id=1, source_target_pairs={{0,6},{1,9},{2,4},{3,11},{4,2},{5,13},{6,0},{7,15},{8,14},{9,1},{1... | collective-permute-start | bytes 147464 | tf_op jit(solution)/shard_map/ppermute | solution.py:211
  20.3 4.2 %collective-permute-start.11 = (bf16[48,512]{1,0:T(8,128)(2,1)S(1)}, bf16[48,512]{1,0:T(8,128)(2,1)S(1)}, u32[]{:S(2)}, u32[]{:S(2)}) collective-permute-start(bf16[48,512]{1,0:T(8,128)(2,1)S(1)} %get-tuple-element.54), channel_id=1, source_target_pairs={{0,2},{1,3},{2,0},{3,1},{4,6},{5,7},{6,4},{7,5},{8,10},{9,11},{10,... | collective-permute-start | bytes 147464 | tf_op jit(solution)/shard_map/ppermute | solution.py:211
  23.2 1.3 %collective-permute-start.12 = (bf16[48,512]{1,0:T(8,128)(2,1)S(1)}, bf16[48,512]{1,0:T(8,128)(2,1)S(1)}, u32[]{:S(2)}, u32[]{:S(2)}) collective-permute-start(bf16[48,512]{1,0:T(8,128)(2,1)S(1)} %collective-permute-done.8.refs_1_), channel_id=1, source_target_pairs={{0,1},{1,0},{2,3},{3,2},{4,5},{5,4},{6,7},{7,6},{8,9},{9,8},{10,11... | collective-permute-start | bytes 147464 | tf_op jit(solution)/shard_map/ppermute | solution.py:221
  23.2 1.4 %collective-permute-start.13 = (bf16[48,512]{1,0:T(8,128)(2,1)S(1)}, bf16[48,512]{1,0:T(8,128)(2,1)S(1)}, u32[]{:S(2)}, u32[]{:S(2)}) collective-permute-start(bf16[48,512]{1,0:T(8,128)(2,1)S(1)} %collective-permute-done.9.refs_2_), channel_id=1, source_target_pairs={{0,1},{1,0},{2,3},{3,2},{4,5},{5,4},{6,7},{7,6},{8,9},{9,8},{10,11... | collective-permute-start | bytes 147464 | tf_op jit(solution)/shard_map/ppermute | solution.py:221
  24.1 1.2 %collective-permute-start.14 = (bf16[48,512]{1,0:T(8,128)(2,1)S(1)}, bf16[48,512]{1,0:T(8,128)(2,1)S(1)}, u32[]{:S(2)}, u32[]{:S(2)}) collective-permute-start(bf16[48,512]{1,0:T(8,128)(2,1)S(1)} %collective-permute-done.10.refs_3_), channel_id=1, source_target_pairs={{0,1},{1,0},{2,3},{3,2},{4,5},{5,4},{6,7},{7,6},{8,9},{9,8},{10,11... | collective-permute-start | bytes 147464 | tf_op jit(solution)/shard_map/ppermute | solution.py:221

commit v24 on v20

--- a/solution.py
+++ b/solution.py
@@ -145,7 +145,7 @@
 
 def middle_kernel(n, kept_ref, x_ref, low_ref, dlow_part, *refs):
     count = n // 2 + 1
-    got, dlow_ref, send = refs[: n - count], refs[n - count], refs[n - count + 1 : n + 1]
+    got, (dlow_ref, own_ref), send = refs[: n - count], refs[n - count :][:2], refs[n - count + 2 : n + 1]
     b_ref, up_ref = refs[n + 1 :]
     me, core = lax.axis_index("dp"), lax.axis_index("tensor")
     rows, picked = dlow_ref.shape
@@ -159,7 +159,7 @@
     dlow = dlow_part[...] + dot(g, b_sel, 1, 1)
     dlow = jnp.where(in_seg, adapter_scale * dlow, 0.0).astype(bf16)
     dlow_ref[...] = dlow
-    targets = partners(n, me, core)
+    targets = partners(n, me, core)[1:]
     for target, message in zip(targets, send):
         at = pl.ds(pl.multiple_of(target * width, width), width)
         message[:picked, :] = dot(dlow, x_ref[:, at], 0, 0).astype(bf16)
@@ -169,12 +169,13 @@
     low_wide = dot(low, onehot, 1, 0).astype(bf16)
     up = (adapter_scale * dot(low_wide, g, 0, 0)).astype(bf16)
     up_ref[...] = up.reshape(up_ref.shape)
+    own_ref[...] = up_ref[me]
     for target, message in zip(targets, send):
         message[picked:, :] = up_ref[target]
 
 
-def grad_x_kernel(n, kept_ref, w_ref, dlow_ref, *refs):
-    got, (out_hbm, a_ref, out_ref, sems) = refs[:n], refs[n:]
+def grad_x_kernel(n, kept_ref, w_ref, x_ref, up_ref, dlow_ref, *refs):
+    got, (out_hbm, own_ref, a_ref, out_ref, sems) = refs[:n], refs[n:]
     me, core = lax.axis_index("dp"), lax.axis_index("tensor")
     picked, width = a_ref.shape[1:]
     for sender, message in zip(senders(n, me, core), got):
@@ -186,6 +187,9 @@
         total = dot(g, w_ref[at, :], 1, 1) + dot(dlow_ref[...], a_ref[core * (n // 2) + j], 1, 0)
         out_ref[:, at] = total.astype(bf16)
         done += start_all([out_ref.at[:, at]], [out_hbm.at[:, at]], sems, j)
+    at = pl.ds(pl.multiple_of(me * width, width), width)
+    own_ref[:picked, :] = dot(dlow_ref[...], x_ref[:, at], 0, 0).astype(bf16)
+    own_ref[picked:, :] = up_ref[...]
     wait_all(done)
 
 
@@ -291,21 +295,21 @@
         cost_estimate=pl.CostEstimate(flops=0, bytes_accessed=1 << 21, transcendentals=0),
     )(kept, x_mine, x_other, *got[:count])
 
-    dlow, *sent = pl.pallas_call(
+    dlow, own_up, *sent = pl.pallas_call(
         functools.partial(middle_kernel, n),
-        out_shape=[shape((tok_rows, picked), bf16)] + [message] * count,
+        out_shape=[shape((tok_rows, picked), bf16), shape((ADAPTER_RANK, out_width), bf16)]
+        + [message] * (count - 1),
         in_specs=[VMEM] * (4 + n - count),
         out_specs=[VMEM] * (1 + count),
         scratch_shapes=[maps, maps],
         compiler_params=params(8),
     )(kept, x, low, dlow, *got[count:])
-    own, *sent = sent
-
-    grad_x = pl.pallas_call(
+
+    grad_x, own = pl.pallas_call(
         functools.partial(grad_x_kernel, n),
-        out_shape=shape((tok_rows, half), bf16),
-        in_specs=[VMEM] * (3 + n),
-        out_specs=HBM,
+        out_shape=[shape((tok_rows, half), bf16), message],
+        in_specs=[VMEM] * (5 + n),
+        out_specs=[HBM, VMEM],
         scratch_shapes=[
             pltpu.VMEM((n, picked, column_total), bf16),
             pltpu.VMEM((tok_rows, half), bf16),
@@ -317,7 +321,7 @@
             bytes_accessed=2 * half * (out_width + tok_rows),
             transcendentals=0,
         ),
-    )(kept, frozen_weight, dlow, *got)
+    )(kept, frozen_weight, x, own_up, dlow, *got)
 
     got, grad_x = exchange(sent, (0,), grad_x)
 

time: 26.4 us -> 26.3 us (level)
  no operation moved by 1% of the time
where the time goes in v24:
time: 26.3 us; the launch traced here: 26.1 us
  starting transfers between devices  15.8 us (60%)
  Pallas kernels  6.49 us (25%)
  waiting for transfers between devices  3.16 us (12%)
  between operations  0.73 us (3%)
    ppermute x8, starting transfers between devices, exchange(): lax.ppermute(message, ('dp', 'tensor'), [(2 * i + c, 2 * (i ^ step[c]) +...  14.4 us
    ppermute x8, waiting for transfers between devices, exchange(): lax.ppermute(message, ('dp', 'tensor'), [(2 * i + c, 2 * (i ^ step[c]) +...  2.12 us
    pallas_call x1, Pallas kernels, local_kernels(): pl.pallas_call(functools.partial(grad_x_kernel, n), out_shape=[shape((tok...  1.67 us
    pallas_call x1, Pallas kernels, local_kernels(): pl.pallas_call(functools.partial(stage_kernel, n, picked), out_shape=[sha...  1.17 us
    pallas_call x1, Pallas kernels, local_kernels(): pl.pallas_call(functools.partial(pack_kernel, n), out_shape=[message] * c...  1.15 us
    ppermute x6, waiting for transfers between devices, exchange(): lax.ppermute(message, 'tensor', [(0, 1), (1, 0)])  1.03 us
    pallas_call x1, Pallas kernels, local_kernels(): pl.pallas_call(functools.partial(final_kernel, n), out_shape=[shape((colu...  1.01 us
    pallas_call x1, Pallas kernels, local_kernels(): pl.pallas_call(functools.partial(middle_kernel, n), out_shape=[shape((tok...  0.99 us
  transfers between devices with their start and end apart: 15, of which 9 were waited for; matrix products, arithmetic and copies ran while one was open for 0% of the time, Pallas kernels for 13%

profile of v24, /device:TPU:0, one launch (start us, length us, event | category | flops | bytes accessed | tf_op | source)
XLA Modules:
  0.0 26.1 jit_solution(6059441481808821992)
XLA Ops:
  0.6 1.2 %shard_map.113 = (bf16[48,512]{1,0:T(8,128)(2,1)S(1)}, bf16[48,512]{1,0:T(8,128)(2,1)S(1)}, bf16[48,512]{1,0:T(8,128)(2,1)S(1)}, bf16[48,512]{1,0:T(8,128)(2,1)S(1)}, bf16[48,512]{1,0:T(8,128)(2,1)S(1)}) custom-call(s32[2,8]{1,0:T(2,128)} %bitcast.2, s32[8]{0:T(128)} %slot_hbm.3, bf16[512,128]{1,0:T(8,128)(2,1)} %down_hbm.1, bf16[16,512]{1,0:T(8,128)(2,1)} %up_hbm.1), custom_call_target="tpu_custom_call" | custom-call | tf_op jit(solution)/shard_map/pallas_call | solution.py:264
  1.8 0.5 %collective-permute-start.1 = (bf16[64,4096]{1,0:T(8,128)(2,1)}, bf16[64,4096]{1,0:T(8,128)(2,1)S(1)}, u32[]{:S(2)}, u32[]{:S(2)}) collective-permute-start(bf16[64,4096]{1,0:T(8,128)(2,1)} %x_hbm.1), channel_id=1, source_target_pairs={{0,1},{1,0},{2,3},{3,2},{4,5},{5,4},{6,7},{7,6},{8,9},{9,8},{10,11... | collective-permute-start | bytes 1572872 | tf_op jit(solution)/shard_map/ppermute | solution.py:274
  2.3 5.6 %collective-permute-start = (bf16[48,512]{1,0:T(8,128)(2,1)S(1)}, bf16[48,512]{1,0:T(8,128)(2,1)S(1)}, u32[]{:S(2)}, u32[]{:S(2)}) collective-permute-start(bf16[48,512]{1,0:T(8,128)(2,1)S(1)} %get-tuple-element.37), channel_id=1, source_target_pairs={{0,14},{1,11},{2,12},{3,9},{4,10},{5,15},{6,8},{7,13},{8,6},{9,3},... | collective-permute-start | bytes 147464 | tf_op jit(solution)/shard_map/ppermute | solution.py:215
  7.9 0.0 collective-permute-start.2
  7.9 2.0 %collective-permute-start.3 = (bf16[48,512]{1,0:T(8,128)(2,1)S(1)}, bf16[48,512]{1,0:T(8,128)(2,1)S(1)}, u32[]{:S(2)}, u32[]{:S(2)}) collective-permute-start(bf16[48,512]{1,0:T(8,128)(2,1)S(1)} %get-tuple-element.44), channel_id=1, source_target_pairs={{0,4},{1,9},{2,6},{3,11},{4,0},{5,13},{6,2},{7,15},{8,12},{9,1},{1... | collective-permute-start | bytes 147464 | tf_op jit(solution)/shard_map/ppermute | solution.py:215
  9.9 1.5 %collective-permute-start.4 = (bf16[48,512]{1,0:T(8,128)(2,1)S(1)}, bf16[48,512]{1,0:T(8,128)(2,1)S(1)}, u32[]{:S(2)}, u32[]{:S(2)}) collective-permute-start(bf16[48,512]{1,0:T(8,128)(2,1)S(1)} %get-tuple-element.45), channel_id=1, source_target_pairs={{0,2},{1,3},{2,0},{3,1},{4,6},{5,7},{6,4},{7,5},{8,10},{9,11},{10,... | collective-permute-start | bytes 147464 | tf_op jit(solution)/shard_map/ppermute | solution.py:215
  11.4 1.2 %shard_map.112 = (bf16[64,4096]{1,0:T(8,128)(2,1)S(1)}, bf16[256,512]{1,0:T(8,128)(2,1)S(1)}) custom-call(s32[2,8]{1,0:T(2,128)} %bitcast.4, s32[2,8]{1,0:T(2,128)} %bitcast.3, s32[8]{0:T(128)} %slot_hbm.3, s32[8]{0:T(128)} %count_hbm.1, bf16[128,512]{1,0:T(8,128)(2,1)} %g_hbm.1, bf16[64,4096]{1,0:T(8,128)(2,1)} %x_hbm.1, bf16[2048,512]{1,0:T(8,128)(2,1)} %w_ref.1), custom_call_target="tpu_custom_call" | custom-call | bytes 2097152 | tf_op jit(solution)/shard_map/pallas_call | solution.py:275
  12.6 0.0 copy-start
  12.6 0.0 collective-permute-done.refs_1_
  12.6 0.1 collective-permute-start.5
  12.7 0.4 %collective-permute-done.2.refs_2_ = bf16[48,512]{1,0:T(8,128)(2,1)S(1)} collective-permute-done((bf16[48,512]{1,0:T(8,128)(2,1)S(1)}, bf16[48,512]{1,0:T(8,128)(2,1)S(1)}, u32[]{:S(2)}, u32[]{:S(2)}) %collective-permute-start.2) | collective-permute-done | bytes 49184 | tf_op jit(solution)/shard_map/ppermute | solution.py:215
  13.0 0.1 collective-permute-start.6
  13.2 0.4 %collective-permute-done.3.refs_3_ = bf16[48,512]{1,0:T(8,128)(2,1)S(1)} collective-permute-done((bf16[48,512]{1,0:T(8,128)(2,1)S(1)}, bf16[48,512]{1,0:T(8,128)(2,1)S(1)}, u32[]{:S(2)}, u32[]{:S(2)}) %collective-permute-start.3) | collective-permute-done | bytes 49184 | tf_op jit(solution)/shard_map/ppermute | solution.py:215
  13.6 0.0 collective-permute-start.7
  13.6 0.4 %collective-permute-done.4.refs_4_ = bf16[48,512]{1,0:T(8,128)(2,1)S(1)} collective-permute-done((bf16[48,512]{1,0:T(8,128)(2,1)S(1)}, bf16[48,512]{1,0:T(8,128)(2,1)S(1)}, u32[]{:S(2)}, u32[]{:S(2)}) %collective-permute-start.4) | collective-permute-done | bytes 49184 | tf_op jit(solution)/shard_map/ppermute | solution.py:215
  14.0 0.0 collective-permute-done.1.x_other
  14.0 0.5 %shard_map.114 = (bf16[128,4096]{1,0:T(8,128)(2,1)S(1)}, f32[128,32]{1,0:T(8,128)S(1)}, f32[128,32]{1,0:T(8,128)S(1)}) custom-call(bf16[256,512]{1,0:T(8,128)(2,1)S(1)} %get-tuple-element.32.kept_ref, bf16[64,4096]{1,0:T(8,128)(2,1)S(1)} %get-tuple-element.39.x_mine, bf16[64,4096]{1,0:T(8,128)(2,1)S(1)} %collective-permute-done.1.x_other, ...), custom_call_target="tpu_custom_call" | custom-call | bytes 2097152 | tf_op jit(solution)/shard_map/pallas_call | solution.py:288
  14.5 0.0 collective-permute-done.5.refs_0_.refs_5_
  14.5 0.0 collective-permute-done.6.refs_1_.refs_6_
  14.5 0.3 collective-permute-done.7.refs_2_.refs_7_
  14.8 1.0 %shard_map.115 = (bf16[128,32]{1,0:T(8,128)(2,1)S(1)}, bf16[16,512]{1,0:T(8,128)(2,1)S(1)}, bf16[48,512]{1,0:T(8,128)(2,1)S(1)}, bf16[48,512]{1,0:T(8,128)(2,1)S...) custom-call(bf16[256,512]{1,0:T(8,128)(2,1)S(1)} %get-tuple-element.32.kept_ref, ...), custom_call_target="tpu_custom_call" | custom-call | tf_op jit(solution)/shard_map/pallas_call | solution.py:298
  15.8 1.8 %collective-permute-start.8 = (bf16[48,512]{1,0:T(8,128)(2,1)S(1)}, bf16[48,512]{1,0:T(8,128)(2,1)S(1)}, u32[]{:S(2)}, u32[]{:S(2)}) collective-permute-start(bf16[48,512]{1,0:T(8,128)(2,1)S(1)} %get-tuple-element.49), channel_id=1, source_target_pairs={{0,14},{1,11},{2,12},{3,9},{4,10},{5,15},{6,8},{7,13},{8,6},{9,3},... | collective-permute-start | bytes 147464 | tf_op jit(solution)/shard_map/ppermute | solution.py:215
  17.6 0.1 collective-permute-start.9
  17.7 2.5 %collective-permute-start.10 = (bf16[48,512]{1,0:T(8,128)(2,1)S(1)}, bf16[48,512]{1,0:T(8,128)(2,1)S(1)}, u32[]{:S(2)}, u32[]{:S(2)}) collective-permute-start(bf16[48,512]{1,0:T(8,128)(2,1)S(1)} %get-tuple-element.57), channel_id=1, source_target_pairs={{0,4},{1,9},{2,6},{3,11},{4,0},{5,13},{6,2},{7,15},{8,12},{9,1},{1... | collective-permute-start | bytes 147464 | tf_op jit(solution)/shard_map/ppermute | solution.py:215
  20.3 0.8 %collective-permute-start.11 = (bf16[48,512]{1,0:T(8,128)(2,1)S(1)}, bf16[48,512]{1,0:T(8,128)(2,1)S(1)}, u32[]{:S(2)}, u32[]{:S(2)}) collective-permute-start(bf16[48,512]{1,0:T(8,128)(2,1)S(1)} %get-tuple-element.58), channel_id=1, source_target_pairs={{0,2},{1,3},{2,0},{3,1},{4,6},{5,7},{6,4},{7,5},{8,10},{9,11},{10,... | collective-permute-start | bytes 147464 | tf_op jit(solution)/shard_map/ppermute | solution.py:215
  21.1 0.0 copy-done
  21.1 1.7 %shard_map.116 = (bf16[128,2048]{1,0:T(8,128)(2,1)}, bf16[48,512]{1,0:T(8,128)(2,1)S(1)}) custom-call(bf16[256,512]{1,0:T(8,128)(2,1)S(1)} %get-tuple-element.32.kept_ref, bf16[2048,512]{1,0:T(8,128)(2,1)S(1)} %copy-done, bf16[128,4096]{1,0:T(8,128)(2,1)S(1)} %get-tuple-element.46.x_ref, bf16[16,512]{1,0:T(8,128)(2,1)S(1)} %get-tuple-element.50.up_ref, ...), custom_call_target="tpu_custom_call" | custom-call | flops 285212672 | bytes 2621440 | tf_op jit(solution)/shard_map/pallas_call | solution.py:308
  22.8 0.0 collective-permute-done.8.refs_1_
  22.8 0.0 collective-permute-start.12
  22.9 0.6 %collective-permute-done.9.refs_2_ = bf16[48,512]{1,0:T(8,128)(2,1)S(1)} collective-permute-done((bf16[48,512]{1,0:T(8,128)(2,1)S(1)}, bf16[48,512]{1,0:T(8,128)(2,1)S(1)}, u32[]{:S(2)}, u32[]{:S(2)}) %collective-permute-start.9) | collective-permute-done | bytes 49184 | tf_op jit(solution)/shard_map/ppermute | solution.py:215
  23.4 0.0 collective-permute-start.13
  23.4 0.2 collective-permute-done.10.refs_3_
  23.7 0.6 %collective-permute-start.14 = (bf16[48,512]{1,0:T(8,128)(2,1)S(1)}, bf16[48,512]{1,0:T(8,128)(2,1)S(1)}, u32[]{:S(2)}, u32[]{:S(2)}) collective-permute-start(bf16[48,512]{1,0:T(8,128)(2,1)S(1)} %collective-permute-done.10.refs_3_), channel_id=1, source_target_pairs={{0,1},{1,0},{2,3},{3,2},{4,5},{5,4},{6,7},{7,6},{8,9},{9,8},{10,11... | collective-permute-start | bytes 147464 | tf_op jit(solution)/shard_map/ppermute | solution.py:225
  24.2 0.1 collective-permute-done.11.refs_4_
  24.4 0.0 collective-permute-done.12.refs_5_
  24.4 0.3 %collective-permute-done.13.refs_6_ = bf16[48,512]{1,0:T(8,128)(2,1)S(1)} collective-permute-done((bf16[48,512]{1,0:T(8,128)(2,1)S(1)}, bf16[48,512]{1,0:T(8,128)(2,1)S(1)}, u32[]{:S(2)}, u32[]{:S(2)}) %collective-permute-start.13) | collective-permute-done | bytes 49184 | tf_op jit(solution)/shard_map/ppermute | solution.py:225
  24.7 0.5 %collective-permute-done.14.refs_7_ = bf16[48,512]{1,0:T(8,128)(2,1)S(1)} collective-permute-done((bf16[48,512]{1,0:T(8,128)(2,1)S(1)}, bf16[48,512]{1,0:T(8,128)(2,1)S(1)}, u32[]{:S(2)}, u32[]{:S(2)}) %collective-permute-start.14) | collective-permute-done | bytes 49184 | tf_op jit(solution)/shard_map/ppermute | solution.py:225
  25.1 1.0 %shard_map.117 = (f32[512,128]{1,0:T(8,128)}, f32[16,256]{1,0:T(8,128)}) custom-call(bf16[256,512]{1,0:T(8,128)(2,1)S(1)} %get-tuple-element.32.kept_ref, bf16[48,512]{1,0:T(8,128)(2,1)S(1)} %get-tuple-element.54.refs_0_, bf16[48,512]{1,0:T(8,128)(2,1)S(1)} %collective-permute-done.8.refs_1_, bf16[48,512]{1,0:T(8,128)(2,1)S(1)} %collective-permute-done.9.refs_2_, ...), custom_call_target="tpu_custom_call" | custom-call | tf_op jit(solution)/shard_map/pallas_call | solution.py:328
Async XLA Ops:
  1.8 12.2 %collective-permute-start.1 = (bf16[64,4096]{1,0:T(8,128)(2,1)}, bf16[64,4096]{1,0:T(8,128)(2,1)S(1)}, u32[]{:S(2)}, u32[]{:S(2)}) collective-permute-start(bf16[64,4096]{1,0:T(8,128)(2,1)} %x_hbm.1), channel_id=1, source_target_pairs={{0,1},{1,0},{2,3},{3,2},{4,5},{5,4},{6,7},{7,6},{8,9},{9,8},{10,11... | collective-permute-start | bytes 1572872 | tf_op jit(solution)/shard_map/ppermute | solution.py:274
  2.3 10.3 %collective-permute-start = (bf16[48,512]{1,0:T(8,128)(2,1)S(1)}, bf16[48,512]{1,0:T(8,128)(2,1)S(1)}, u32[]{:S(2)}, u32[]{:S(2)}) collective-permute-start(bf16[48,512]{1,0:T(8,128)(2,1)S(1)} %get-tuple-element.37), channel_id=1, source_target_pairs={{0,14},{1,11},{2,12},{3,9},{4,10},{5,15},{6,8},{7,13},{8,6},{9,3},... | collective-permute-start | bytes 147464 | tf_op jit(solution)/shard_map/ppermute | solution.py:215
  7.9 5.1 %collective-permute-start.2 = (bf16[48,512]{1,0:T(8,128)(2,1)S(1)}, bf16[48,512]{1,0:T(8,128)(2,1)S(1)}, u32[]{:S(2)}, u32[]{:S(2)}) collective-permute-start(bf16[48,512]{1,0:T(8,128)(2,1)S(1)} %get-tuple-element.43), channel_id=1, source_target_pairs={{0,6},{1,13},{2,4},{3,15},{4,2},{5,9},{6,0},{7,11},{8,14},{9,5},{1... | collective-permute-start | bytes 147464 | tf_op jit(solution)/shard_map/ppermute | solution.py:215
  7.9 5.6 %collective-permute-start.3 = (bf16[48,512]{1,0:T(8,128)(2,1)S(1)}, bf16[48,512]{1,0:T(8,128)(2,1)S(1)}, u32[]{:S(2)}, u32[]{:S(2)}) collective-permute-start(bf16[48,512]{1,0:T(8,128)(2,1)S(1)} %get-tuple-element.44), channel_id=1, source_target_pairs={{0,4},{1,9},{2,6},{3,11},{4,0},{5,13},{6,2},{7,15},{8,12},{9,1},{1... | collective-permute-start | bytes 147464 | tf_op jit(solution)/shard_map/ppermute | solution.py:215
  9.9 4.1 %collective-permute-start.4 = (bf16[48,512]{1,0:T(8,128)(2,1)S(1)}, bf16[48,512]{1,0:T(8,128)(2,1)S(1)}, u32[]{:S(2)}, u32[]{:S(2)}) collective-permute-start(bf16[48,512]{1,0:T(8,128)(2,1)S(1)} %get-tuple-element.45), channel_id=1, source_target_pairs={{0,2},{1,3},{2,0},{3,1},{4,6},{5,7},{6,4},{7,5},{8,10},{9,11},{10,... | collective-permute-start | bytes 147464 | tf_op jit(solution)/shard_map/ppermute | solution.py:215
  12.6 8.5 %copy-start = (bf16[2048,512]{1,0:T(8,128)(2,1)S(1)}, bf16[2048,512]{1,0:T(8,128)(2,1)}, u32[]{:S(2)}) copy-start(bf16[2048,512]{1,0:T(8,128)(2,1)} %w_ref.1) | copy-start | bytes 6291460
  12.6 1.9 %collective-permute-start.5 = (bf16[48,512]{1,0:T(8,128)(2,1)S(1)}, bf16[48,512]{1,0:T(8,128)(2,1)S(1)}, u32[]{:S(2)}, u32[]{:S(2)}) collective-permute-start(bf16[48,512]{1,0:T(8,128)(2,1)S(1)} %collective-permute-done.refs_1_), channel_id=1, source_target_pairs={{0,1},{1,0},{2,3},{3,2},{4,5},{5,4},{6,7},{7,6},{8,9},{9,8},{10,11... | collective-permute-start | bytes 147464 | tf_op jit(solution)/shard_map/ppermute | solution.py:225
  13.0 1.5 %collective-permute-start.6 = (bf16[48,512]{1,0:T(8,128)(2,1)S(1)}, bf16[48,512]{1,0:T(8,128)(2,1)S(1)}, u32[]{:S(2)}, u32[]{:S(2)}) collective-permute-start(bf16[48,512]{1,0:T(8,128)(2,1)S(1)} %collective-permute-done.2.refs_2_), channel_id=1, source_target_pairs={{0,1},{1,0},{2,3},{3,2},{4,5},{5,4},{6,7},{7,6},{8,9},{9,8},{10,11... | collective-permute-start | bytes 147464 | tf_op jit(solution)/shard_map/ppermute | solution.py:225
  13.6 1.2 %collective-permute-start.7 = (bf16[48,512]{1,0:T(8,128)(2,1)S(1)}, bf16[48,512]{1,0:T(8,128)(2,1)S(1)}, u32[]{:S(2)}, u32[]{:S(2)}) collective-permute-start(bf16[48,512]{1,0:T(8,128)(2,1)S(1)} %collective-permute-done.3.refs_3_), channel_id=1, source_target_pairs={{0,1},{1,0},{2,3},{3,2},{4,5},{5,4},{6,7},{7,6},{8,9},{9,8},{10,11... | collective-permute-start | bytes 147464 | tf_op jit(solution)/shard_map/ppermute | solution.py:225
  15.8 7.1 %collective-permute-start.8 = (bf16[48,512]{1,0:T(8,128)(2,1)S(1)}, bf16[48,512]{1,0:T(8,128)(2,1)S(1)}, u32[]{:S(2)}, u32[]{:S(2)}) collective-permute-start(bf16[48,512]{1,0:T(8,128)(2,1)S(1)} %get-tuple-element.49), channel_id=1, source_target_pairs={{0,14},{1,11},{2,12},{3,9},{4,10},{5,15},{6,8},{7,13},{8,6},{9,3},... | collective-permute-start | bytes 147464 | tf_op jit(solution)/shard_map/ppermute | solution.py:215
  17.6 5.8 %collective-permute-start.9 = (bf16[48,512]{1,0:T(8,128)(2,1)S(1)}, bf16[48,512]{1,0:T(8,128)(2,1)S(1)}, u32[]{:S(2)}, u32[]{:S(2)}) collective-permute-start(bf16[48,512]{1,0:T(8,128)(2,1)S(1)} %get-tuple-element.56), channel_id=1, source_target_pairs={{0,6},{1,13},{2,4},{3,15},{4,2},{5,9},{6,0},{7,11},{8,14},{9,5},{1... | collective-permute-start | bytes 147464 | tf_op jit(solution)/shard_map/ppermute | solution.py:215
  17.7 6.0 %collective-permute-start.10 = (bf16[48,512]{1,0:T(8,128)(2,1)S(1)}, bf16[48,512]{1,0:T(8,128)(2,1)S(1)}, u32[]{:S(2)}, u32[]{:S(2)}) collective-permute-start(bf16[48,512]{1,0:T(8,128)(2,1)S(1)} %get-tuple-element.57), channel_id=1, source_target_pairs={{0,4},{1,9},{2,6},{3,11},{4,0},{5,13},{6,2},{7,15},{8,12},{9,1},{1... | collective-permute-start | bytes 147464 | tf_op jit(solution)/shard_map/ppermute | solution.py:215
  20.3 4.1 %collective-permute-start.11 = (bf16[48,512]{1,0:T(8,128)(2,1)S(1)}, bf16[48,512]{1,0:T(8,128)(2,1)S(1)}, u32[]{:S(2)}, u32[]{:S(2)}) collective-permute-start(bf16[48,512]{1,0:T(8,128)(2,1)S(1)} %get-tuple-element.58), channel_id=1, source_target_pairs={{0,2},{1,3},{2,0},{3,1},{4,6},{5,7},{6,4},{7,5},{8,10},{9,11},{10,... | collective-permute-start | bytes 147464 | tf_op jit(solution)/shard_map/ppermute | solution.py:215
  22.8 1.5 %collective-permute-start.12 = (bf16[48,512]{1,0:T(8,128)(2,1)S(1)}, bf16[48,512]{1,0:T(8,128)(2,1)S(1)}, u32[]{:S(2)}, u32[]{:S(2)}) collective-permute-start(bf16[48,512]{1,0:T(8,128)(2,1)S(1)} %collective-permute-done.8.refs_1_), channel_id=1, source_target_pairs={{0,1},{1,0},{2,3},{3,2},{4,5},{5,4},{6,7},{7,6},{8,9},{9,8},{10,11... | collective-permute-start | bytes 147464 | tf_op jit(solution)/shard_map/ppermute | solution.py:225
  23.4 1.2 %collective-permute-start.13 = (bf16[48,512]{1,0:T(8,128)(2,1)S(1)}, bf16[48,512]{1,0:T(8,128)(2,1)S(1)}, u32[]{:S(2)}, u32[]{:S(2)}) collective-permute-start(bf16[48,512]{1,0:T(8,128)(2,1)S(1)} %collective-permute-done.9.refs_2_), channel_id=1, source_target_pairs={{0,1},{1,0},{2,3},{3,2},{4,5},{5,4},{6,7},{7,6},{8,9},{9,8},{10,11... | collective-permute-start | bytes 147464 | tf_op jit(solution)/shard_map/ppermute | solution.py:225
  23.7 1.4 %collective-permute-start.14 = (bf16[48,512]{1,0:T(8,128)(2,1)S(1)}, bf16[48,512]{1,0:T(8,128)(2,1)S(1)}, u32[]{:S(2)}, u32[]{:S(2)}) collective-permute-start(bf16[48,512]{1,0:T(8,128)(2,1)S(1)} %collective-permute-done.10.refs_3_), channel_id=1, source_target_pairs={{0,1},{1,0},{2,3},{3,2},{4,5},{5,4},{6,7},{7,6},{8,9},{9,8},{10,11... | collective-permute-start | bytes 147464 | tf_op jit(solution)/shard_map/ppermute | solution.py:225

commit v25 on v20

--- a/solution.py
+++ b/solution.py
@@ -69,18 +69,20 @@
 
 def pack_kernel(n, chosen_hbm, slot_hbm, down_hbm, up_hbm, *refs):
     count = n // 2 + 1
-    send, (chosen_ref, slot_ref, down_ref, up_ref, sems) = refs[:count], refs[count:]
+    send, (chosen_ref, slot_ref, down_ref, sems) = refs[:count], refs[count:]
     tables = start_all([chosen_hbm, slot_hbm], [chosen_ref, slot_ref], sems)
-    maps = start_all([down_hbm, up_hbm], [down_ref, up_ref], sems, 2)
+    maps = start_all([down_hbm], [down_ref], sems, 2)
+    picked = chosen_ref.shape[0] * ADAPTER_RANK
+    tail = pl.ds(picked, ADAPTER_RANK)
+    ups = start_all([up_hbm] * count, [message.at[tail] for message in send], sems, 3)
     ranks = partners(n, lax.axis_index("dp"), lax.axis_index("tensor"))
     wait_all(tables)
     onehot = slot_rows(chosen_ref, slot_ref, ranks, down_ref.shape[1])
-    picked = onehot.shape[0] // count
     wait_all(maps)
     columns = dot(onehot, down_ref[...], 1, 1).astype(bf16)
     for k in range(count):
         send[k][:picked, :] = columns[k * picked : (k + 1) * picked]
-        send[k][picked:, :] = up_ref[...]
+    wait_all(ups)
 
 
 def stage_kernel(
@@ -263,7 +265,7 @@
         in_specs=[HBM] * 4,
         out_specs=[VMEM] * count,
         scratch_shapes=tables[1:3]
-        + [pltpu.VMEM(down_maps.shape, bf16), pltpu.VMEM(up_maps.shape, bf16), dma((4,))],
+        + [pltpu.VMEM(down_maps.shape, bf16), dma((3 + count,))],
         compiler_params=params(8),
     )(*in_hbm(chosen, adapter_slot, down_maps, up_maps))
     sent, x_late = lax.optimization_barrier((sent, inputs))

time: 26.4 us -> 26.4 us (level)
  no operation moved by 1% of the time
where the time goes in v25:
time: 26.4 us; the launch traced here: 26.2 us
  starting transfers between devices  15.8 us (60%)
  Pallas kernels  6.54 us (25%)
  waiting for transfers between devices  3.14 us (12%)
  between operations  0.73 us (3%)
    ppermute x8, starting transfers between devices, exchange(): lax.ppermute(message, ('dp', 'tensor'), [(2 * i + c, 2 * (i ^ step[c]) +...  14.4 us
    ppermute x8, waiting for transfers between devices, exchange(): lax.ppermute(message, ('dp', 'tensor'), [(2 * i + c, 2 * (i ^ step[c]) +...  2.11 us
    pallas_call x1, Pallas kernels, local_kernels(): pl.pallas_call(functools.partial(grad_x_kernel, n), out_shape=shape((tok_...  1.67 us
    pallas_call x1, Pallas kernels, local_kernels(): pl.pallas_call(functools.partial(pack_kernel, n), out_shape=[message] * c...  1.2 us
    pallas_call x1, Pallas kernels, local_kernels(): pl.pallas_call(functools.partial(stage_kernel, n, picked), out_shape=[sha...  1.17 us
    ppermute x6, waiting for transfers between devices, exchange(): lax.ppermute(message, 'tensor', [(0, 1), (1, 0)])  1.03 us
    pallas_call x1, Pallas kernels, local_kernels(): pl.pallas_call(functools.partial(final_kernel, n), out_shape=[shape((colu...  1.01 us
    pallas_call x1, Pallas kernels, local_kernels(): pl.pallas_call(functools.partial(middle_kernel, n), out_shape=[shape((tok...  1 us
  transfers between devices with their start and end apart: 15, of which 9 were waited for; matrix products, arithmetic and copies ran while one was open for 0% of the time, Pallas kernels for 13%

profile of v25, /device:TPU:0, one launch (start us, length us, event | category | flops | bytes accessed | tf_op | source)
XLA Modules:
  0.0 26.2 jit_solution(7682818633371757158)
XLA Ops:
  0.6 1.2 %shard_map.113 = (bf16[48,512]{1,0:T(8,128)(2,1)S(1)}, bf16[48,512]{1,0:T(8,128)(2,1)S(1)}, bf16[48,512]{1,0:T(8,128)(2,1)S(1)}, bf16[48,512]{1,0:T(8,128)(2,1)S(1)}, bf16[48,512]{1,0:T(8,128)(2,1)S(1)}) custom-call(s32[2,8]{1,0:T(2,128)} %bitcast.2, s32[8]{0:T(128)} %slot_hbm.3, bf16[512,128]{1,0:T(8,128)(2,1)} %down_hbm.1, bf16[16,512]{1,0:T(8,128)(2,1)} %up_hbm.1), custom_call_target="tpu_custom_call" | custom-call | tf_op jit(solution)/shard_map/pallas_call | solution.py:262
  1.8 0.5 %collective-permute-start.1 = (bf16[64,4096]{1,0:T(8,128)(2,1)}, bf16[64,4096]{1,0:T(8,128)(2,1)S(1)}, u32[]{:S(2)}, u32[]{:S(2)}) collective-permute-start(bf16[64,4096]{1,0:T(8,128)(2,1)} %x_hbm.1), channel_id=1, source_target_pairs={{0,1},{1,0},{2,3},{3,2},{4,5},{5,4},{6,7},{7,6},{8,9},{9,8},{10,11... | collective-permute-start | bytes 1572872 | tf_op jit(solution)/shard_map/ppermute | solution.py:272
  2.4 5.6 %collective-permute-start = (bf16[48,512]{1,0:T(8,128)(2,1)S(1)}, bf16[48,512]{1,0:T(8,128)(2,1)S(1)}, u32[]{:S(2)}, u32[]{:S(2)}) collective-permute-start(bf16[48,512]{1,0:T(8,128)(2,1)S(1)} %get-tuple-element.35), channel_id=1, source_target_pairs={{0,14},{1,11},{2,12},{3,9},{4,10},{5,15},{6,8},{7,13},{8,6},{9,3},... | collective-permute-start | bytes 147464 | tf_op jit(solution)/shard_map/ppermute | solution.py:213
  7.9 0.0 collective-permute-start.2
  8.0 2.0 %collective-permute-start.3 = (bf16[48,512]{1,0:T(8,128)(2,1)S(1)}, bf16[48,512]{1,0:T(8,128)(2,1)S(1)}, u32[]{:S(2)}, u32[]{:S(2)}) collective-permute-start(bf16[48,512]{1,0:T(8,128)(2,1)S(1)} %get-tuple-element.42), channel_id=1, source_target_pairs={{0,4},{1,9},{2,6},{3,11},{4,0},{5,13},{6,2},{7,15},{8,12},{9,1},{1... | collective-permute-start | bytes 147464 | tf_op jit(solution)/shard_map/ppermute | solution.py:213
  10.0 1.5 %collective-permute-start.4 = (bf16[48,512]{1,0:T(8,128)(2,1)S(1)}, bf16[48,512]{1,0:T(8,128)(2,1)S(1)}, u32[]{:S(2)}, u32[]{:S(2)}) collective-permute-start(bf16[48,512]{1,0:T(8,128)(2,1)S(1)} %get-tuple-element.43), channel_id=1, source_target_pairs={{0,2},{1,3},{2,0},{3,1},{4,6},{5,7},{6,4},{7,5},{8,10},{9,11},{10,... | collective-permute-start | bytes 147464 | tf_op jit(solution)/shard_map/ppermute | solution.py:213
  11.4 1.2 %shard_map.112 = (bf16[64,4096]{1,0:T(8,128)(2,1)S(1)}, bf16[256,512]{1,0:T(8,128)(2,1)S(1)}) custom-call(s32[2,8]{1,0:T(2,128)} %bitcast.4, s32[2,8]{1,0:T(2,128)} %bitcast.3, s32[8]{0:T(128)} %slot_hbm.3, s32[8]{0:T(128)} %count_hbm.1, bf16[128,512]{1,0:T(8,128)(2,1)} %g_hbm.1, bf16[64,4096]{1,0:T(8,128)(2,1)} %x_hbm.1, bf16[2048,512]{1,0:T(8,128)(2,1)} %w_ref.1), custom_call_target="tpu_custom_call" | custom-call | bytes 2097152 | tf_op jit(solution)/shard_map/pallas_call | solution.py:273
  12.6 0.0 copy-start
  12.6 0.0 collective-permute-done.refs_1_
  12.6 0.1 collective-permute-start.5
  12.7 0.4 %collective-permute-done.2.refs_2_ = bf16[48,512]{1,0:T(8,128)(2,1)S(1)} collective-permute-done((bf16[48,512]{1,0:T(8,128)(2,1)S(1)}, bf16[48,512]{1,0:T(8,128)(2,1)S(1)}, u32[]{:S(2)}, u32[]{:S(2)}) %collective-permute-start.2) | collective-permute-done | bytes 49184 | tf_op jit(solution)/shard_map/ppermute | solution.py:213
  13.1 0.1 collective-permute-start.6
  13.2 0.4 %collective-permute-done.3.refs_3_ = bf16[48,512]{1,0:T(8,128)(2,1)S(1)} collective-permute-done((bf16[48,512]{1,0:T(8,128)(2,1)S(1)}, bf16[48,512]{1,0:T(8,128)(2,1)S(1)}, u32[]{:S(2)}, u32[]{:S(2)}) %collective-permute-start.3) | collective-permute-done | bytes 49184 | tf_op jit(solution)/shard_map/ppermute | solution.py:213
  13.6 0.0 collective-permute-start.7
  13.6 0.4 %collective-permute-done.4.refs_4_ = bf16[48,512]{1,0:T(8,128)(2,1)S(1)} collective-permute-done((bf16[48,512]{1,0:T(8,128)(2,1)S(1)}, bf16[48,512]{1,0:T(8,128)(2,1)S(1)}, u32[]{:S(2)}, u32[]{:S(2)}) %collective-permute-start.4) | collective-permute-done | bytes 49184 | tf_op jit(solution)/shard_map/ppermute | solution.py:213
  14.0 0.0 collective-permute-done.1.x_other
  14.0 0.5 %shard_map.114 = (bf16[128,4096]{1,0:T(8,128)(2,1)S(1)}, f32[128,32]{1,0:T(8,128)S(1)}, f32[128,32]{1,0:T(8,128)S(1)}) custom-call(bf16[256,512]{1,0:T(8,128)(2,1)S(1)} %get-tuple-element.30.kept_ref, bf16[64,4096]{1,0:T(8,128)(2,1)S(1)} %get-tuple-element.37.x_mine, bf16[64,4096]{1,0:T(8,128)(2,1)S(1)} %collective-permute-done.1.x_other, ...), custom_call_target="tpu_custom_call" | custom-call | bytes 2097152 | tf_op jit(solution)/shard_map/pallas_call | solution.py:286
  14.6 0.0 collective-permute-done.5.refs_0_.refs_5_
  14.6 0.0 collective-permute-done.6.refs_1_.refs_6_
  14.6 0.2 collective-permute-done.7.refs_2_.refs_7_
  14.8 1.0 %shard_map.115 = (bf16[128,32]{1,0:T(8,128)(2,1)S(1)}, bf16[48,512]{1,0:T(8,128)(2,1)S(1)}, bf16[48,512]{1,0:T(8,128)(2,1)S(1)}, bf16[48,512]{1,0:T(8,128)(2,1)S...) custom-call(bf16[256,512]{1,0:T(8,128)(2,1)S(1)} %get-tuple-element.30.kept_ref, ...), custom_call_target="tpu_custom_call" | custom-call | tf_op jit(solution)/shard_map/pallas_call | solution.py:296
  15.8 1.9 %collective-permute-start.8 = (bf16[48,512]{1,0:T(8,128)(2,1)S(1)}, bf16[48,512]{1,0:T(8,128)(2,1)S(1)}, u32[]{:S(2)}, u32[]{:S(2)}) collective-permute-start(bf16[48,512]{1,0:T(8,128)(2,1)S(1)} %get-tuple-element.47), channel_id=1, source_target_pairs={{0,14},{1,11},{2,12},{3,9},{4,10},{5,15},{6,8},{7,13},{8,6},{9,3},... | collective-permute-start | bytes 147464 | tf_op jit(solution)/shard_map/ppermute | solution.py:213
  17.7 0.1 collective-permute-start.9
  17.8 2.5 %collective-permute-start.10 = (bf16[48,512]{1,0:T(8,128)(2,1)S(1)}, bf16[48,512]{1,0:T(8,128)(2,1)S(1)}, u32[]{:S(2)}, u32[]{:S(2)}) collective-permute-start(bf16[48,512]{1,0:T(8,128)(2,1)S(1)} %get-tuple-element.53), channel_id=1, source_target_pairs={{0,4},{1,9},{2,6},{3,11},{4,0},{5,13},{6,2},{7,15},{8,12},{9,1},{1... | collective-permute-start | bytes 147464 | tf_op jit(solution)/shard_map/ppermute | solution.py:213
  20.3 0.9 %collective-permute-start.11 = (bf16[48,512]{1,0:T(8,128)(2,1)S(1)}, bf16[48,512]{1,0:T(8,128)(2,1)S(1)}, u32[]{:S(2)}, u32[]{:S(2)}) collective-permute-start(bf16[48,512]{1,0:T(8,128)(2,1)S(1)} %get-tuple-element.54), channel_id=1, source_target_pairs={{0,2},{1,3},{2,0},{3,1},{4,6},{5,7},{6,4},{7,5},{8,10},{9,11},{10,... | collective-permute-start | bytes 147464 | tf_op jit(solution)/shard_map/ppermute | solution.py:213
  21.2 0.0 copy-done
  21.2 1.7 %shard_map.116 = bf16[128,2048]{1,0:T(8,128)(2,1)} custom-call(bf16[256,512]{1,0:T(8,128)(2,1)S(1)} %get-tuple-element.30.kept_ref, bf16[2048,512]{1,0:T(8,128)(2,1)S(1)} %copy-done, bf16[128,32]{1,0:T(8,128)(2,1)S(1)} %get-tuple-element.48.dlow_ref, bf16[48,512]{1,0:T(8,128)(2,1)S(1)} %get-tuple-element.39.refs_0_, ...), custom_call_target="tpu_custom_call" | custom-call | flops 285212672 | bytes 2621440 | tf_op jit(solution)/shard_map/pallas_call | solution.py:306
  22.9 0.0 collective-permute-done.8.refs_1_
  22.9 0.1 collective-permute-start.12
  22.9 0.6 %collective-permute-done.9.refs_2_ = bf16[48,512]{1,0:T(8,128)(2,1)S(1)} collective-permute-done((bf16[48,512]{1,0:T(8,128)(2,1)S(1)}, bf16[48,512]{1,0:T(8,128)(2,1)S(1)}, u32[]{:S(2)}, u32[]{:S(2)}) %collective-permute-start.9) | collective-permute-done | bytes 49184 | tf_op jit(solution)/shard_map/ppermute | solution.py:213
  23.5 0.0 collective-permute-start.13
  23.5 0.2 collective-permute-done.10.refs_3_
  23.7 0.6 %collective-permute-start.14 = (bf16[48,512]{1,0:T(8,128)(2,1)S(1)}, bf16[48,512]{1,0:T(8,128)(2,1)S(1)}, u32[]{:S(2)}, u32[]{:S(2)}) collective-permute-start(bf16[48,512]{1,0:T(8,128)(2,1)S(1)} %collective-permute-done.10.refs_3_), channel_id=1, source_target_pairs={{0,1},{1,0},{2,3},{3,2},{4,5},{5,4},{6,7},{7,6},{8,9},{9,8},{10,11... | collective-permute-start | bytes 147464 | tf_op jit(solution)/shard_map/ppermute | solution.py:223
  24.3 0.1 collective-permute-done.11.refs_4_
  24.4 0.0 collective-permute-done.12.refs_5_
  24.4 0.3 %collective-permute-done.13.refs_6_ = bf16[48,512]{1,0:T(8,128)(2,1)S(1)} collective-permute-done((bf16[48,512]{1,0:T(8,128)(2,1)S(1)}, bf16[48,512]{1,0:T(8,128)(2,1)S(1)}, u32[]{:S(2)}, u32[]{:S(2)}) %collective-permute-start.13) | collective-permute-done | bytes 49184 | tf_op jit(solution)/shard_map/ppermute | solution.py:223
  24.7 0.4 %collective-permute-done.14.refs_7_ = bf16[48,512]{1,0:T(8,128)(2,1)S(1)} collective-permute-done((bf16[48,512]{1,0:T(8,128)(2,1)S(1)}, bf16[48,512]{1,0:T(8,128)(2,1)S(1)}, u32[]{:S(2)}, u32[]{:S(2)}) %collective-permute-start.14) | collective-permute-done | bytes 49184 | tf_op jit(solution)/shard_map/ppermute | solution.py:223
  25.2 1.0 %shard_map.117 = (f32[512,128]{1,0:T(8,128)}, f32[16,256]{1,0:T(8,128)}) custom-call(bf16[256,512]{1,0:T(8,128)(2,1)S(1)} %get-tuple-element.30.kept_ref, bf16[48,512]{1,0:T(8,128)(2,1)S(1)} %get-tuple-element.50.refs_0_, bf16[48,512]{1,0:T(8,128)(2,1)S(1)} %collective-permute-done.8.refs_1_, bf16[48,512]{1,0:T(8,128)(2,1)S(1)} %collective-permute-done.9.refs_2_, ...), custom_call_target="tpu_custom_call" | custom-call | tf_op jit(solution)/shard_map/pallas_call | solution.py:326
Async XLA Ops:
  1.8 12.2 %collective-permute-start.1 = (bf16[64,4096]{1,0:T(8,128)(2,1)}, bf16[64,4096]{1,0:T(8,128)(2,1)S(1)}, u32[]{:S(2)}, u32[]{:S(2)}) collective-permute-start(bf16[64,4096]{1,0:T(8,128)(2,1)} %x_hbm.1), channel_id=1, source_target_pairs={{0,1},{1,0},{2,3},{3,2},{4,5},{5,4},{6,7},{7,6},{8,9},{9,8},{10,11... | collective-permute-start | bytes 1572872 | tf_op jit(solution)/shard_map/ppermute | solution.py:272
  2.4 10.3 %collective-permute-start = (bf16[48,512]{1,0:T(8,128)(2,1)S(1)}, bf16[48,512]{1,0:T(8,128)(2,1)S(1)}, u32[]{:S(2)}, u32[]{:S(2)}) collective-permute-start(bf16[48,512]{1,0:T(8,128)(2,1)S(1)} %get-tuple-element.35), channel_id=1, source_target_pairs={{0,14},{1,11},{2,12},{3,9},{4,10},{5,15},{6,8},{7,13},{8,6},{9,3},... | collective-permute-start | bytes 147464 | tf_op jit(solution)/shard_map/ppermute | solution.py:213
  7.9 5.1 %collective-permute-start.2 = (bf16[48,512]{1,0:T(8,128)(2,1)S(1)}, bf16[48,512]{1,0:T(8,128)(2,1)S(1)}, u32[]{:S(2)}, u32[]{:S(2)}) collective-permute-start(bf16[48,512]{1,0:T(8,128)(2,1)S(1)} %get-tuple-element.41), channel_id=1, source_target_pairs={{0,6},{1,13},{2,4},{3,15},{4,2},{5,9},{6,0},{7,11},{8,14},{9,5},{1... | collective-permute-start | bytes 147464 | tf_op jit(solution)/shard_map/ppermute | solution.py:213
  8.0 5.6 %collective-permute-start.3 = (bf16[48,512]{1,0:T(8,128)(2,1)S(1)}, bf16[48,512]{1,0:T(8,128)(2,1)S(1)}, u32[]{:S(2)}, u32[]{:S(2)}) collective-permute-start(bf16[48,512]{1,0:T(8,128)(2,1)S(1)} %get-tuple-element.42), channel_id=1, source_target_pairs={{0,4},{1,9},{2,6},{3,11},{4,0},{5,13},{6,2},{7,15},{8,12},{9,1},{1... | collective-permute-start | bytes 147464 | tf_op jit(solution)/shard_map/ppermute | solution.py:213
  10.0 4.1 %collective-permute-start.4 = (bf16[48,512]{1,0:T(8,128)(2,1)S(1)}, bf16[48,512]{1,0:T(8,128)(2,1)S(1)}, u32[]{:S(2)}, u32[]{:S(2)}) collective-permute-start(bf16[48,512]{1,0:T(8,128)(2,1)S(1)} %get-tuple-element.43), channel_id=1, source_target_pairs={{0,2},{1,3},{2,0},{3,1},{4,6},{5,7},{6,4},{7,5},{8,10},{9,11},{10,... | collective-permute-start | bytes 147464 | tf_op jit(solution)/shard_map/ppermute | solution.py:213
  12.6 8.6 %copy-start = (bf16[2048,512]{1,0:T(8,128)(2,1)S(1)}, bf16[2048,512]{1,0:T(8,128)(2,1)}, u32[]{:S(2)}) copy-start(bf16[2048,512]{1,0:T(8,128)(2,1)} %w_ref.1) | copy-start | bytes 6291460
  12.6 1.9 %collective-permute-start.5 = (bf16[48,512]{1,0:T(8,128)(2,1)S(1)}, bf16[48,512]{1,0:T(8,128)(2,1)S(1)}, u32[]{:S(2)}, u32[]{:S(2)}) collective-permute-start(bf16[48,512]{1,0:T(8,128)(2,1)S(1)} %collective-permute-done.refs_1_), channel_id=1, source_target_pairs={{0,1},{1,0},{2,3},{3,2},{4,5},{5,4},{6,7},{7,6},{8,9},{9,8},{10,11... | collective-permute-start | bytes 147464 | tf_op jit(solution)/shard_map/ppermute | solution.py:223
  13.1 1.5 %collective-permute-start.6 = (bf16[48,512]{1,0:T(8,128)(2,1)S(1)}, bf16[48,512]{1,0:T(8,128)(2,1)S(1)}, u32[]{:S(2)}, u32[]{:S(2)}) collective-permute-start(bf16[48,512]{1,0:T(8,128)(2,1)S(1)} %collective-permute-done.2.refs_2_), channel_id=1, source_target_pairs={{0,1},{1,0},{2,3},{3,2},{4,5},{5,4},{6,7},{7,6},{8,9},{9,8},{10,11... | collective-permute-start | bytes 147464 | tf_op jit(solution)/shard_map/ppermute | solution.py:223
  13.6 1.2 %collective-permute-start.7 = (bf16[48,512]{1,0:T(8,128)(2,1)S(1)}, bf16[48,512]{1,0:T(8,128)(2,1)S(1)}, u32[]{:S(2)}, u32[]{:S(2)}) collective-permute-start(bf16[48,512]{1,0:T(8,128)(2,1)S(1)} %collective-permute-done.3.refs_3_), channel_id=1, source_target_pairs={{0,1},{1,0},{2,3},{3,2},{4,5},{5,4},{6,7},{7,6},{8,9},{9,8},{10,11... | collective-permute-start | bytes 147464 | tf_op jit(solution)/shard_map/ppermute | solution.py:223
  15.8 7.1 %collective-permute-start.8 = (bf16[48,512]{1,0:T(8,128)(2,1)S(1)}, bf16[48,512]{1,0:T(8,128)(2,1)S(1)}, u32[]{:S(2)}, u32[]{:S(2)}) collective-permute-start(bf16[48,512]{1,0:T(8,128)(2,1)S(1)} %get-tuple-element.47), channel_id=1, source_target_pairs={{0,14},{1,11},{2,12},{3,9},{4,10},{5,15},{6,8},{7,13},{8,6},{9,3},... | collective-permute-start | bytes 147464 | tf_op jit(solution)/shard_map/ppermute | solution.py:213
  17.7 5.8 %collective-permute-start.9 = (bf16[48,512]{1,0:T(8,128)(2,1)S(1)}, bf16[48,512]{1,0:T(8,128)(2,1)S(1)}, u32[]{:S(2)}, u32[]{:S(2)}) collective-permute-start(bf16[48,512]{1,0:T(8,128)(2,1)S(1)} %get-tuple-element.52), channel_id=1, source_target_pairs={{0,6},{1,13},{2,4},{3,15},{4,2},{5,9},{6,0},{7,11},{8,14},{9,5},{1... | collective-permute-start | bytes 147464 | tf_op jit(solution)/shard_map/ppermute | solution.py:213
  17.8 6.0 %collective-permute-start.10 = (bf16[48,512]{1,0:T(8,128)(2,1)S(1)}, bf16[48,512]{1,0:T(8,128)(2,1)S(1)}, u32[]{:S(2)}, u32[]{:S(2)}) collective-permute-start(bf16[48,512]{1,0:T(8,128)(2,1)S(1)} %get-tuple-element.53), channel_id=1, source_target_pairs={{0,4},{1,9},{2,6},{3,11},{4,0},{5,13},{6,2},{7,15},{8,12},{9,1},{1... | collective-permute-start | bytes 147464 | tf_op jit(solution)/shard_map/ppermute | solution.py:213
  20.3 4.1 %collective-permute-start.11 = (bf16[48,512]{1,0:T(8,128)(2,1)S(1)}, bf16[48,512]{1,0:T(8,128)(2,1)S(1)}, u32[]{:S(2)}, u32[]{:S(2)}) collective-permute-start(bf16[48,512]{1,0:T(8,128)(2,1)S(1)} %get-tuple-element.54), channel_id=1, source_target_pairs={{0,2},{1,3},{2,0},{3,1},{4,6},{5,7},{6,4},{7,5},{8,10},{9,11},{10,... | collective-permute-start | bytes 147464 | tf_op jit(solution)/shard_map/ppermute | solution.py:213
  22.9 1.5 %collective-permute-start.12 = (bf16[48,512]{1,0:T(8,128)(2,1)S(1)}, bf16[48,512]{1,0:T(8,128)(2,1)S(1)}, u32[]{:S(2)}, u32[]{:S(2)}) collective-permute-start(bf16[48,512]{1,0:T(8,128)(2,1)S(1)} %collective-permute-done.8.refs_1_), channel_id=1, source_target_pairs={{0,1},{1,0},{2,3},{3,2},{4,5},{5,4},{6,7},{7,6},{8,9},{9,8},{10,11... | collective-permute-start | bytes 147464 | tf_op jit(solution)/shard_map/ppermute | solution.py:223
  23.5 1.2 %collective-permute-start.13 = (bf16[48,512]{1,0:T(8,128)(2,1)S(1)}, bf16[48,512]{1,0:T(8,128)(2,1)S(1)}, u32[]{:S(2)}, u32[]{:S(2)}) collective-permute-start(bf16[48,512]{1,0:T(8,128)(2,1)S(1)} %collective-permute-done.9.refs_2_), channel_id=1, source_target_pairs={{0,1},{1,0},{2,3},{3,2},{4,5},{5,4},{6,7},{7,6},{8,9},{9,8},{10,11... | collective-permute-start | bytes 147464 | tf_op jit(solution)/shard_map/ppermute | solution.py:223
  23.7 1.4 %collective-permute-start.14 = (bf16[48,512]{1,0:T(8,128)(2,1)S(1)}, bf16[48,512]{1,0:T(8,128)(2,1)S(1)}, u32[]{:S(2)}, u32[]{:S(2)}) collective-permute-start(bf16[48,512]{1,0:T(8,128)(2,1)S(1)} %collective-permute-done.10.refs_3_), channel_id=1, source_target_pairs={{0,1},{1,0},{2,3},{3,2},{4,5},{5,4},{6,7},{7,6},{8,9},{9,8},{10,11... | collective-permute-start | bytes 147464 | tf_op jit(solution)/shard_map/ppermute | solution.py:223

commit v26 on v20

--- a/solution.py
+++ b/solution.py
@@ -70,8 +70,8 @@
 def pack_kernel(n, chosen_hbm, slot_hbm, down_hbm, up_hbm, *refs):
     count = n // 2 + 1
     send, (chosen_ref, slot_ref, down_ref, up_ref, sems) = refs[:count], refs[count:]
+    maps = start_all([down_hbm, up_hbm], [down_ref, up_ref], sems, 2)
     tables = start_all([chosen_hbm, slot_hbm], [chosen_ref, slot_ref], sems)
-    maps = start_all([down_hbm, up_hbm], [down_ref, up_ref], sems, 2)
     ranks = partners(n, lax.axis_index("dp"), lax.axis_index("tensor"))
     wait_all(tables)
     onehot = slot_rows(chosen_ref, slot_ref, ranks, down_ref.shape[1])

time: 26.4 us -> 26.3 us (level)
  no operation moved by 1% of the time
where the time goes in v26:
time: 26.3 us; the launch traced here: 26.2 us
  starting transfers between devices  16 us (61%)
  Pallas kernels  6.5 us (25%)
  waiting for transfers between devices  2.95 us (11%)
  between operations  0.74 us (3%)
    ppermute x8, starting transfers between devices, exchange(): lax.ppermute(message, ('dp', 'tensor'), [(2 * i + c, 2 * (i ^ step[c]) +...  14.5 us
    ppermute x8, waiting for transfers between devices, exchange(): lax.ppermute(message, ('dp', 'tensor'), [(2 * i + c, 2 * (i ^ step[c]) +...  1.92 us
    pallas_call x1, Pallas kernels, local_kernels(): pl.pallas_call(functools.partial(grad_x_kernel, n), out_shape=shape((tok_...  1.67 us
    pallas_call x1, Pallas kernels, local_kernels(): pl.pallas_call(functools.partial(stage_kernel, n, picked), out_shape=[sha...  1.17 us
    pallas_call x1, Pallas kernels, local_kernels(): pl.pallas_call(functools.partial(pack_kernel, n), out_shape=[message] * c...  1.15 us
    ppermute x6, waiting for transfers between devices, exchange(): lax.ppermute(message, 'tensor', [(0, 1), (1, 0)])  1.03 us
    pallas_call x1, Pallas kernels, local_kernels(): pl.pallas_call(functools.partial(final_kernel, n), out_shape=[shape((colu...  1.01 us
    pallas_call x1, Pallas kernels, local_kernels(): pl.pallas_call(functools.partial(middle_kernel, n), out_shape=[shape((tok...  1 us
  transfers between devices with their start and end apart: 15, of which 9 were waited for; matrix products, arithmetic and copies ran while one was open for 0% of the time, Pallas kernels for 13%

profile of v26, /device:TPU:0, one launch (start us, length us, event | category | flops | bytes accessed | tf_op | source)
XLA Modules:
  0.0 26.2 jit_solution(5401361441442988447)
XLA Ops:
  0.6 1.1 %shard_map.113 = (bf16[48,512]{1,0:T(8,128)(2,1)S(1)}, bf16[48,512]{1,0:T(8,128)(2,1)S(1)}, bf16[48,512]{1,0:T(8,128)(2,1)S(1)}, bf16[48,512]{1,0:T(8,128)(2,1)S(1)}, bf16[48,512]{1,0:T(8,128)(2,1)S(1)}) custom-call(s32[2,8]{1,0:T(2,128)} %bitcast.2, s32[8]{0:T(128)} %slot_hbm.3, bf16[512,128]{1,0:T(8,128)(2,1)} %down_hbm.1, bf16[16,512]{1,0:T(8,128)(2,1)} %up_hbm.1), custom_call_target="tpu_custom_call" | custom-call | tf_op jit(solution)/shard_map/pallas_call | solution.py:260
  1.8 0.5 %collective-permute-start.1 = (bf16[64,4096]{1,0:T(8,128)(2,1)}, bf16[64,4096]{1,0:T(8,128)(2,1)S(1)}, u32[]{:S(2)}, u32[]{:S(2)}) collective-permute-start(bf16[64,4096]{1,0:T(8,128)(2,1)} %x_hbm.1), channel_id=1, source_target_pairs={{0,1},{1,0},{2,3},{3,2},{4,5},{5,4},{6,7},{7,6},{8,9},{9,8},{10,11... | collective-permute-start | bytes 1572872 | tf_op jit(solution)/shard_map/ppermute | solution.py:270
  2.3 5.6 %collective-permute-start = (bf16[48,512]{1,0:T(8,128)(2,1)S(1)}, bf16[48,512]{1,0:T(8,128)(2,1)S(1)}, u32[]{:S(2)}, u32[]{:S(2)}) collective-permute-start(bf16[48,512]{1,0:T(8,128)(2,1)S(1)} %get-tuple-element.35), channel_id=1, source_target_pairs={{0,14},{1,11},{2,12},{3,9},{4,10},{5,15},{6,8},{7,13},{8,6},{9,3},... | collective-permute-start | bytes 147464 | tf_op jit(solution)/shard_map/ppermute | solution.py:211
  7.9 0.0 collective-permute-start.2
  7.9 2.0 %collective-permute-start.3 = (bf16[48,512]{1,0:T(8,128)(2,1)S(1)}, bf16[48,512]{1,0:T(8,128)(2,1)S(1)}, u32[]{:S(2)}, u32[]{:S(2)}) collective-permute-start(bf16[48,512]{1,0:T(8,128)(2,1)S(1)} %get-tuple-element.42), channel_id=1, source_target_pairs={{0,4},{1,9},{2,6},{3,11},{4,0},{5,13},{6,2},{7,15},{8,12},{9,1},{1... | collective-permute-start | bytes 147464 | tf_op jit(solution)/shard_map/ppermute | solution.py:211
  9.9 1.5 %collective-permute-start.4 = (bf16[48,512]{1,0:T(8,128)(2,1)S(1)}, bf16[48,512]{1,0:T(8,128)(2,1)S(1)}, u32[]{:S(2)}, u32[]{:S(2)}) collective-permute-start(bf16[48,512]{1,0:T(8,128)(2,1)S(1)} %get-tuple-element.43), channel_id=1, source_target_pairs={{0,2},{1,3},{2,0},{3,1},{4,6},{5,7},{6,4},{7,5},{8,10},{9,11},{10,... | collective-permute-start | bytes 147464 | tf_op jit(solution)/shard_map/ppermute | solution.py:211
  11.4 1.2 %shard_map.112 = (bf16[64,4096]{1,0:T(8,128)(2,1)S(1)}, bf16[256,512]{1,0:T(8,128)(2,1)S(1)}) custom-call(s32[2,8]{1,0:T(2,128)} %bitcast.4, s32[2,8]{1,0:T(2,128)} %bitcast.3, s32[8]{0:T(128)} %slot_hbm.3, s32[8]{0:T(128)} %count_hbm.1, bf16[128,512]{1,0:T(8,128)(2,1)} %g_hbm.1, bf16[64,4096]{1,0:T(8,128)(2,1)} %x_hbm.1, bf16[2048,512]{1,0:T(8,128)(2,1)} %w_ref.1), custom_call_target="tpu_custom_call" | custom-call | bytes 2097152 | tf_op jit(solution)/shard_map/pallas_call | solution.py:271
  12.6 0.0 copy-start
  12.6 0.0 collective-permute-done.refs_1_
  12.6 0.1 collective-permute-start.5
  12.7 0.4 %collective-permute-done.2.refs_2_ = bf16[48,512]{1,0:T(8,128)(2,1)S(1)} collective-permute-done((bf16[48,512]{1,0:T(8,128)(2,1)S(1)}, bf16[48,512]{1,0:T(8,128)(2,1)S(1)}, u32[]{:S(2)}, u32[]{:S(2)}) %collective-permute-start.2) | collective-permute-done | bytes 49184 | tf_op jit(solution)/shard_map/ppermute | solution.py:211
  13.0 0.1 collective-permute-start.6
  13.2 0.4 %collective-permute-done.3.refs_3_ = bf16[48,512]{1,0:T(8,128)(2,1)S(1)} collective-permute-done((bf16[48,512]{1,0:T(8,128)(2,1)S(1)}, bf16[48,512]{1,0:T(8,128)(2,1)S(1)}, u32[]{:S(2)}, u32[]{:S(2)}) %collective-permute-start.3) | collective-permute-done | bytes 49184 | tf_op jit(solution)/shard_map/ppermute | solution.py:211
  13.5 0.0 collective-permute-start.7
  13.6 0.4 %collective-permute-done.4.refs_4_ = bf16[48,512]{1,0:T(8,128)(2,1)S(1)} collective-permute-done((bf16[48,512]{1,0:T(8,128)(2,1)S(1)}, bf16[48,512]{1,0:T(8,128)(2,1)S(1)}, u32[]{:S(2)}, u32[]{:S(2)}) %collective-permute-start.4) | collective-permute-done | bytes 49184 | tf_op jit(solution)/shard_map/ppermute | solution.py:211
  14.0 0.0 collective-permute-done.1.x_other
  14.0 0.5 %shard_map.114 = (bf16[128,4096]{1,0:T(8,128)(2,1)S(1)}, f32[128,32]{1,0:T(8,128)S(1)}, f32[128,32]{1,0:T(8,128)S(1)}) custom-call(bf16[256,512]{1,0:T(8,128)(2,1)S(1)} %get-tuple-element.30.kept_ref, bf16[64,4096]{1,0:T(8,128)(2,1)S(1)} %get-tuple-element.37.x_mine, bf16[64,4096]{1,0:T(8,128)(2,1)S(1)} %collective-permute-done.1.x_other, ...), custom_call_target="tpu_custom_call" | custom-call | bytes 2097152 | tf_op jit(solution)/shard_map/pallas_call | solution.py:284
  14.5 0.0 collective-permute-done.5.refs_0_.refs_5_
  14.5 0.0 collective-permute-done.6.refs_1_.refs_6_
  14.5 0.2 collective-permute-done.7.refs_2_.refs_7_
  14.8 1.0 %shard_map.115 = (bf16[128,32]{1,0:T(8,128)(2,1)S(1)}, bf16[48,512]{1,0:T(8,128)(2,1)S(1)}, bf16[48,512]{1,0:T(8,128)(2,1)S(1)}, bf16[48,512]{1,0:T(8,128)(2,1)S...) custom-call(bf16[256,512]{1,0:T(8,128)(2,1)S(1)} %get-tuple-element.30.kept_ref, ...), custom_call_target="tpu_custom_call" | custom-call | tf_op jit(solution)/shard_map/pallas_call | solution.py:294
  15.8 2.0 %collective-permute-start.8 = (bf16[48,512]{1,0:T(8,128)(2,1)S(1)}, bf16[48,512]{1,0:T(8,128)(2,1)S(1)}, u32[]{:S(2)}, u32[]{:S(2)}) collective-permute-start(bf16[48,512]{1,0:T(8,128)(2,1)S(1)} %get-tuple-element.47), channel_id=1, source_target_pairs={{0,14},{1,11},{2,12},{3,9},{4,10},{5,15},{6,8},{7,13},{8,6},{9,3},... | collective-permute-start | bytes 147464 | tf_op jit(solution)/shard_map/ppermute | solution.py:211
  17.7 0.0 collective-permute-start.9
  17.7 2.5 %collective-permute-start.10 = (bf16[48,512]{1,0:T(8,128)(2,1)S(1)}, bf16[48,512]{1,0:T(8,128)(2,1)S(1)}, u32[]{:S(2)}, u32[]{:S(2)}) collective-permute-start(bf16[48,512]{1,0:T(8,128)(2,1)S(1)} %get-tuple-element.53), channel_id=1, source_target_pairs={{0,4},{1,9},{2,6},{3,11},{4,0},{5,13},{6,2},{7,15},{8,12},{9,1},{1... | collective-permute-start | bytes 147464 | tf_op jit(solution)/shard_map/ppermute | solution.py:211
  20.3 1.0 %collective-permute-start.11 = (bf16[48,512]{1,0:T(8,128)(2,1)S(1)}, bf16[48,512]{1,0:T(8,128)(2,1)S(1)}, u32[]{:S(2)}, u32[]{:S(2)}) collective-permute-start(bf16[48,512]{1,0:T(8,128)(2,1)S(1)} %get-tuple-element.54), channel_id=1, source_target_pairs={{0,2},{1,3},{2,0},{3,1},{4,6},{5,7},{6,4},{7,5},{8,10},{9,11},{10,... | collective-permute-start | bytes 147464 | tf_op jit(solution)/shard_map/ppermute | solution.py:211
  21.2 0.0 copy-done
  21.2 1.7 %shard_map.116 = bf16[128,2048]{1,0:T(8,128)(2,1)} custom-call(bf16[256,512]{1,0:T(8,128)(2,1)S(1)} %get-tuple-element.30.kept_ref, bf16[2048,512]{1,0:T(8,128)(2,1)S(1)} %copy-done, bf16[128,32]{1,0:T(8,128)(2,1)S(1)} %get-tuple-element.48.dlow_ref, bf16[48,512]{1,0:T(8,128)(2,1)S(1)} %get-tuple-element.39.refs_0_, ...), custom_call_target="tpu_custom_call" | custom-call | flops 285212672 | bytes 2621440 | tf_op jit(solution)/shard_map/pallas_call | solution.py:304
  22.9 0.0 collective-permute-done.8.refs_1_
  22.9 0.1 collective-permute-start.12
  23.0 0.5 %collective-permute-done.9.refs_2_ = bf16[48,512]{1,0:T(8,128)(2,1)S(1)} collective-permute-done((bf16[48,512]{1,0:T(8,128)(2,1)S(1)}, bf16[48,512]{1,0:T(8,128)(2,1)S(1)}, u32[]{:S(2)}, u32[]{:S(2)}) %collective-permute-start.9) | collective-permute-done | bytes 49184 | tf_op jit(solution)/shard_map/ppermute | solution.py:211
  23.5 0.0 collective-permute-start.13
  23.5 0.2 collective-permute-done.10.refs_3_
  23.7 0.6 %collective-permute-start.14 = (bf16[48,512]{1,0:T(8,128)(2,1)S(1)}, bf16[48,512]{1,0:T(8,128)(2,1)S(1)}, u32[]{:S(2)}, u32[]{:S(2)}) collective-permute-start(bf16[48,512]{1,0:T(8,128)(2,1)S(1)} %collective-permute-done.10.refs_3_), channel_id=1, source_target_pairs={{0,1},{1,0},{2,3},{3,2},{4,5},{5,4},{6,7},{7,6},{8,9},{9,8},{10,11... | collective-permute-start | bytes 147464 | tf_op jit(solution)/shard_map/ppermute | solution.py:221
  24.3 0.1 collective-permute-done.11.refs_4_
  24.4 0.0 collective-permute-done.12.refs_5_
  24.4 0.3 %collective-permute-done.13.refs_6_ = bf16[48,512]{1,0:T(8,128)(2,1)S(1)} collective-permute-done((bf16[48,512]{1,0:T(8,128)(2,1)S(1)}, bf16[48,512]{1,0:T(8,128)(2,1)S(1)}, u32[]{:S(2)}, u32[]{:S(2)}) %collective-permute-start.13) | collective-permute-done | bytes 49184 | tf_op jit(solution)/shard_map/ppermute | solution.py:221
  24.7 0.5 %collective-permute-done.14.refs_7_ = bf16[48,512]{1,0:T(8,128)(2,1)S(1)} collective-permute-done((bf16[48,512]{1,0:T(8,128)(2,1)S(1)}, bf16[48,512]{1,0:T(8,128)(2,1)S(1)}, u32[]{:S(2)}, u32[]{:S(2)}) %collective-permute-start.14) | collective-permute-done | bytes 49184 | tf_op jit(solution)/shard_map/ppermute | solution.py:221
  25.1 1.0 %shard_map.117 = (f32[512,128]{1,0:T(8,128)}, f32[16,256]{1,0:T(8,128)}) custom-call(bf16[256,512]{1,0:T(8,128)(2,1)S(1)} %get-tuple-element.30.kept_ref, bf16[48,512]{1,0:T(8,128)(2,1)S(1)} %get-tuple-element.50.refs_0_, bf16[48,512]{1,0:T(8,128)(2,1)S(1)} %collective-permute-done.8.refs_1_, bf16[48,512]{1,0:T(8,128)(2,1)S(1)} %collective-permute-done.9.refs_2_, ...), custom_call_target="tpu_custom_call" | custom-call | tf_op jit(solution)/shard_map/pallas_call | solution.py:324
Async XLA Ops:
  1.8 12.2 %collective-permute-start.1 = (bf16[64,4096]{1,0:T(8,128)(2,1)}, bf16[64,4096]{1,0:T(8,128)(2,1)S(1)}, u32[]{:S(2)}, u32[]{:S(2)}) collective-permute-start(bf16[64,4096]{1,0:T(8,128)(2,1)} %x_hbm.1), channel_id=1, source_target_pairs={{0,1},{1,0},{2,3},{3,2},{4,5},{5,4},{6,7},{7,6},{8,9},{9,8},{10,11... | collective-permute-start | bytes 1572872 | tf_op jit(solution)/shard_map/ppermute | solution.py:270
  2.3 10.3 %collective-permute-start = (bf16[48,512]{1,0:T(8,128)(2,1)S(1)}, bf16[48,512]{1,0:T(8,128)(2,1)S(1)}, u32[]{:S(2)}, u32[]{:S(2)}) collective-permute-start(bf16[48,512]{1,0:T(8,128)(2,1)S(1)} %get-tuple-element.35), channel_id=1, source_target_pairs={{0,14},{1,11},{2,12},{3,9},{4,10},{5,15},{6,8},{7,13},{8,6},{9,3},... | collective-permute-start | bytes 147464 | tf_op jit(solution)/shard_map/ppermute | solution.py:211
  7.9 5.1 %collective-permute-start.2 = (bf16[48,512]{1,0:T(8,128)(2,1)S(1)}, bf16[48,512]{1,0:T(8,128)(2,1)S(1)}, u32[]{:S(2)}, u32[]{:S(2)}) collective-permute-start(bf16[48,512]{1,0:T(8,128)(2,1)S(1)} %get-tuple-element.41), channel_id=1, source_target_pairs={{0,6},{1,13},{2,4},{3,15},{4,2},{5,9},{6,0},{7,11},{8,14},{9,5},{1... | collective-permute-start | bytes 147464 | tf_op jit(solution)/shard_map/ppermute | solution.py:211
  7.9 5.6 %collective-permute-start.3 = (bf16[48,512]{1,0:T(8,128)(2,1)S(1)}, bf16[48,512]{1,0:T(8,128)(2,1)S(1)}, u32[]{:S(2)}, u32[]{:S(2)}) collective-permute-start(bf16[48,512]{1,0:T(8,128)(2,1)S(1)} %get-tuple-element.42), channel_id=1, source_target_pairs={{0,4},{1,9},{2,6},{3,11},{4,0},{5,13},{6,2},{7,15},{8,12},{9,1},{1... | collective-permute-start | bytes 147464 | tf_op jit(solution)/shard_map/ppermute | solution.py:211
  9.9 4.1 %collective-permute-start.4 = (bf16[48,512]{1,0:T(8,128)(2,1)S(1)}, bf16[48,512]{1,0:T(8,128)(2,1)S(1)}, u32[]{:S(2)}, u32[]{:S(2)}) collective-permute-start(bf16[48,512]{1,0:T(8,128)(2,1)S(1)} %get-tuple-element.43), channel_id=1, source_target_pairs={{0,2},{1,3},{2,0},{3,1},{4,6},{5,7},{6,4},{7,5},{8,10},{9,11},{10,... | collective-permute-start | bytes 147464 | tf_op jit(solution)/shard_map/ppermute | solution.py:211
  12.6 8.7 %copy-start = (bf16[2048,512]{1,0:T(8,128)(2,1)S(1)}, bf16[2048,512]{1,0:T(8,128)(2,1)}, u32[]{:S(2)}) copy-start(bf16[2048,512]{1,0:T(8,128)(2,1)} %w_ref.1) | copy-start | bytes 6291460
  12.6 1.9 %collective-permute-start.5 = (bf16[48,512]{1,0:T(8,128)(2,1)S(1)}, bf16[48,512]{1,0:T(8,128)(2,1)S(1)}, u32[]{:S(2)}, u32[]{:S(2)}) collective-permute-start(bf16[48,512]{1,0:T(8,128)(2,1)S(1)} %collective-permute-done.refs_1_), channel_id=1, source_target_pairs={{0,1},{1,0},{2,3},{3,2},{4,5},{5,4},{6,7},{7,6},{8,9},{9,8},{10,11... | collective-permute-start | bytes 147464 | tf_op jit(solution)/shard_map/ppermute | solution.py:221
  13.0 1.5 %collective-permute-start.6 = (bf16[48,512]{1,0:T(8,128)(2,1)S(1)}, bf16[48,512]{1,0:T(8,128)(2,1)S(1)}, u32[]{:S(2)}, u32[]{:S(2)}) collective-permute-start(bf16[48,512]{1,0:T(8,128)(2,1)S(1)} %collective-permute-done.2.refs_2_), channel_id=1, source_target_pairs={{0,1},{1,0},{2,3},{3,2},{4,5},{5,4},{6,7},{7,6},{8,9},{9,8},{10,11... | collective-permute-start | bytes 147464 | tf_op jit(solution)/shard_map/ppermute | solution.py:221
  13.5 1.2 %collective-permute-start.7 = (bf16[48,512]{1,0:T(8,128)(2,1)S(1)}, bf16[48,512]{1,0:T(8,128)(2,1)S(1)}, u32[]{:S(2)}, u32[]{:S(2)}) collective-permute-start(bf16[48,512]{1,0:T(8,128)(2,1)S(1)} %collective-permute-done.3.refs_3_), channel_id=1, source_target_pairs={{0,1},{1,0},{2,3},{3,2},{4,5},{5,4},{6,7},{7,6},{8,9},{9,8},{10,11... | collective-permute-start | bytes 147464 | tf_op jit(solution)/shard_map/ppermute | solution.py:221
  15.8 7.1 %collective-permute-start.8 = (bf16[48,512]{1,0:T(8,128)(2,1)S(1)}, bf16[48,512]{1,0:T(8,128)(2,1)S(1)}, u32[]{:S(2)}, u32[]{:S(2)}) collective-permute-start(bf16[48,512]{1,0:T(8,128)(2,1)S(1)} %get-tuple-element.47), channel_id=1, source_target_pairs={{0,14},{1,11},{2,12},{3,9},{4,10},{5,15},{6,8},{7,13},{8,6},{9,3},... | collective-permute-start | bytes 147464 | tf_op jit(solution)/shard_map/ppermute | solution.py:211
  17.7 5.7 %collective-permute-start.9 = (bf16[48,512]{1,0:T(8,128)(2,1)S(1)}, bf16[48,512]{1,0:T(8,128)(2,1)S(1)}, u32[]{:S(2)}, u32[]{:S(2)}) collective-permute-start(bf16[48,512]{1,0:T(8,128)(2,1)S(1)} %get-tuple-element.52), channel_id=1, source_target_pairs={{0,6},{1,13},{2,4},{3,15},{4,2},{5,9},{6,0},{7,11},{8,14},{9,5},{1... | collective-permute-start | bytes 147464 | tf_op jit(solution)/shard_map/ppermute | solution.py:211
  17.7 5.9 %collective-permute-start.10 = (bf16[48,512]{1,0:T(8,128)(2,1)S(1)}, bf16[48,512]{1,0:T(8,128)(2,1)S(1)}, u32[]{:S(2)}, u32[]{:S(2)}) collective-permute-start(bf16[48,512]{1,0:T(8,128)(2,1)S(1)} %get-tuple-element.53), channel_id=1, source_target_pairs={{0,4},{1,9},{2,6},{3,11},{4,0},{5,13},{6,2},{7,15},{8,12},{9,1},{1... | collective-permute-start | bytes 147464 | tf_op jit(solution)/shard_map/ppermute | solution.py:211
  20.3 4.1 %collective-permute-start.11 = (bf16[48,512]{1,0:T(8,128)(2,1)S(1)}, bf16[48,512]{1,0:T(8,128)(2,1)S(1)}, u32[]{:S(2)}, u32[]{:S(2)}) collective-permute-start(bf16[48,512]{1,0:T(8,128)(2,1)S(1)} %get-tuple-element.54), channel_id=1, source_target_pairs={{0,2},{1,3},{2,0},{3,1},{4,6},{5,7},{6,4},{7,5},{8,10},{9,11},{10,... | collective-permute-start | bytes 147464 | tf_op jit(solution)/shard_map/ppermute | solution.py:211
  22.9 1.4 %collective-permute-start.12 = (bf16[48,512]{1,0:T(8,128)(2,1)S(1)}, bf16[48,512]{1,0:T(8,128)(2,1)S(1)}, u32[]{:S(2)}, u32[]{:S(2)}) collective-permute-start(bf16[48,512]{1,0:T(8,128)(2,1)S(1)} %collective-permute-done.8.refs_1_), channel_id=1, source_target_pairs={{0,1},{1,0},{2,3},{3,2},{4,5},{5,4},{6,7},{7,6},{8,9},{9,8},{10,11... | collective-permute-start | bytes 147464 | tf_op jit(solution)/shard_map/ppermute | solution.py:221
  23.5 1.2 %collective-permute-start.13 = (bf16[48,512]{1,0:T(8,128)(2,1)S(1)}, bf16[48,512]{1,0:T(8,128)(2,1)S(1)}, u32[]{:S(2)}, u32[]{:S(2)}) collective-permute-start(bf16[48,512]{1,0:T(8,128)(2,1)S(1)} %collective-permute-done.9.refs_2_), channel_id=1, source_target_pairs={{0,1},{1,0},{2,3},{3,2},{4,5},{5,4},{6,7},{7,6},{8,9},{9,8},{10,11... | collective-permute-start | bytes 147464 | tf_op jit(solution)/shard_map/ppermute | solution.py:221
  23.7 1.4 %collective-permute-start.14 = (bf16[48,512]{1,0:T(8,128)(2,1)S(1)}, bf16[48,512]{1,0:T(8,128)(2,1)S(1)}, u32[]{:S(2)}, u32[]{:S(2)}) collective-permute-start(bf16[48,512]{1,0:T(8,128)(2,1)S(1)} %collective-permute-done.10.refs_3_), channel_id=1, source_target_pairs={{0,1},{1,0},{2,3},{3,2},{4,5},{5,4},{6,7},{7,6},{8,9},{9,8},{10,11... | collective-permute-start | bytes 147464 | tf_op jit(solution)/shard_map/ppermute | solution.py:221
